TPU v7x, 32 devices: a whole 2x2x4 slice. The times are simulated.
32 devices in a mesh: seq: 16 (over z, y, x), dp: 2 (over core).
Axes of the slice: x: 2, y: 2, z: 4, core: 2. Of those that a mesh axis runs over, the one named last changes fastest.
Arguments:
- tokens: bfloat16 [2, 8192, 1280], P('dp', 'seq'), may hold values from -6 to 6
- cotangent: bfloat16 [2, 8192, 1280], P('dp', 'seq'), may hold values from -1.5 to 1.5
- router: bfloat16 [1280, 2], replicated, may hold values from -0.15625 to 0.15625
- logit_scale: float32 [1], replicated, may hold values from 40 to 60
- expert_in: bfloat16 [1280, 10240], P(None, 'seq'), may hold values from -12 to 12
- expert_out: bfloat16 [10240, 1280], P('seq'), may hold values from -0.078125 to 0.078125
Outputs:
- mixed: bfloat16 [2, 8192, 1280], P('dp', 'seq')
- grad_tokens: bfloat16 [2, 8192, 1280], P('dp', 'seq')
- grad_expert_in: float32 [1280, 10240], P('dp', 'seq')
- grad_expert_out: float32 [10240, 1280], P('seq', 'dp')
- grad_router: float32 [1280, 2], replicated
All inputs are finite; a program needn't handle non-finite values.
Results may differ from a plain program's by a relative error of at most 0.0085.
The roundings to bfloat16 on the way count: a program that leaves them out, or rounds other values in their place, can miss the bound.
Values may be sent and summed in bfloat16 or wider, within the bound.
No kernel may reach another device: no remote copies, remote signals or barrier semaphores. Data moves between devices by JAX's collectives and lax.ppermute only.
A program may use at most 64 MiB of HBM per device.

v0:
```python
import jax
import jax.numpy as jnp
from jax import lax
from jax.sharding import PartitionSpec as P

epsilon = 1e-06


def gelu_slope(pre_act):
    cdf = 0.5 * (1.0 + lax.erf(pre_act * 0.7071067811865476))
    return cdf + pre_act * jnp.exp(-0.5 * pre_act * pre_act) * 0.3989422804014327


def per_device(tokens, cotangent, router, logit_scale, expert_in, expert_out):
    tok_in = tokens[0]
    tok_cot = cotangent[0]
    experts = router.shape[1]
    group_size = lax.axis_size("seq") // experts
    owned = lax.axis_index("seq") // group_size
    slot_ids = jnp.arange(experts)[:, None]
    phi_f32 = router.astype(jnp.float32)
    phi_scale = lax.rsqrt(jnp.sum(phi_f32 * phi_f32, axis=0, keepdims=True) + epsilon)
    phi_unit = phi_f32 * phi_scale
    phi_norm = phi_unit.astype(jnp.bfloat16)
    tok_f32 = tok_in.astype(jnp.float32)
    tok_scale = lax.rsqrt(jnp.sum(tok_f32 * tok_f32, axis=1, keepdims=True) + epsilon)
    tok_unit = tok_f32 * tok_scale
    tok_norm = tok_unit.astype(jnp.bfloat16)
    logits = logit_scale[0] * jnp.dot(tok_norm, phi_norm, preferred_element_type=jnp.float32)
    exp_scores = jnp.exp(logits)
    totals = lax.psum(jnp.sum(exp_scores, axis=0, keepdims=True), "seq")
    dispatch_f = exp_scores / totals
    dispatch = dispatch_f.astype(jnp.bfloat16)
    slot_part = jnp.einsum("ns,nd->sd", dispatch, tok_in, preferred_element_type=jnp.float32)
    slot_in = lax.psum(slot_part, "seq")
    slot_x = slot_in.astype(jnp.bfloat16)
    row_x = lax.dynamic_slice_in_dim(slot_x, owned, 1, 0)
    pre_act = jnp.dot(row_x, expert_in, preferred_element_type=jnp.float32)
    hidden = jax.nn.gelu(pre_act, approximate=False).astype(jnp.bfloat16)
    part_out = jnp.dot(hidden, expert_out, preferred_element_type=jnp.float32)
    placed = jnp.where(slot_ids == owned, part_out, 0.0)
    slot_sum = lax.psum(placed, "seq")
    slot_y = slot_sum.astype(jnp.bfloat16)
    combine_f = exp_scores / jnp.sum(exp_scores, axis=1, keepdims=True)
    combine = combine_f.astype(jnp.bfloat16)
    mixed = jnp.dot(combine, slot_y, preferred_element_type=jnp.float32).astype(jnp.bfloat16)
    cot_part = jnp.einsum("ns,nd->sd", combine, tok_cot, preferred_element_type=jnp.float32)
    slot_cot = lax.psum(cot_part, "seq").astype(jnp.bfloat16)
    comb_dot = jnp.einsum("nd,sd->ns", tok_cot, slot_y, preferred_element_type=jnp.float32)
    grad_comb = combine_f * (comb_dot - jnp.sum(combine_f * comb_dot, axis=1, keepdims=True))
    row_cot = lax.dynamic_slice_in_dim(slot_cot, owned, 1, 0)
    hid_grad = jnp.einsum("od,hd->oh", row_cot, expert_out, preferred_element_type=jnp.float32)
    pre_grad = (hid_grad * gelu_slope(pre_act)).astype(jnp.bfloat16)
    part_dx = jnp.einsum("oh,dh->od", pre_grad, expert_in, preferred_element_type=jnp.float32)
    placed_dx = jnp.where(slot_ids == owned, part_dx, 0.0)
    dx_sum = lax.psum(placed_dx, "seq")
    slot_dx = dx_sum.astype(jnp.bfloat16)
    term_in = jnp.einsum("od,oh->dh", row_x, pre_grad, preferred_element_type=jnp.float32)
    term_out = jnp.einsum("oh,od->hd", hidden, row_cot, preferred_element_type=jnp.float32)
    grad_expert_in, grad_expert_out = (
        lax.psum_scatter(term_in, "dp", scatter_dimension=0, tiled=True),
        lax.psum_scatter(term_out, "dp", scatter_dimension=1, tiled=True),
    )
    disp_dot = jnp.einsum("nd,sd->ns", tok_in, slot_dx, preferred_element_type=jnp.float32)
    local_stat = jnp.sum(dispatch.astype(jnp.float32) * disp_dot, axis=0, keepdims=True)
    column_stat = lax.psum(local_stat, "seq")
    grad_disp = dispatch_f * (disp_dot - column_stat)
    score_grad = (logit_scale[0] * (grad_comb + grad_disp)).astype(jnp.bfloat16)
    norm_grad = jnp.einsum("ns,ds->nd", score_grad, phi_norm, preferred_element_type=jnp.float32)
    phi_part = jnp.einsum("nd,ns->ds", tok_norm, score_grad, preferred_element_type=jnp.float32)
    phi_grad = lax.psum(phi_part, ("seq", "dp"))
    through = jnp.dot(dispatch, slot_dx, preferred_element_type=jnp.float32)
    back_norm = tok_scale * (
        norm_grad - tok_unit * jnp.sum(tok_unit * norm_grad, axis=1, keepdims=True)
    )
    grad_tokens = (through + back_norm).astype(jnp.bfloat16)
    grad_router = phi_scale * (
        phi_grad - phi_unit * jnp.sum(phi_unit * phi_grad, axis=0, keepdims=True)
    )
    return (mixed[None], grad_tokens[None], grad_expert_in, grad_expert_out, grad_router)


def solution(mesh):
    return jax.shard_map(
        per_device,
        mesh=mesh,
        in_specs=(
            P("dp", "seq", None),
            P("dp", "seq", None),
            P(),
            P(),
            P(None, "seq"),
            P("seq", None),
        ),
        out_specs=(P("dp", "seq", None), P("dp", "seq", None), P("dp", "seq"), P("seq", "dp"), P()),
        check_vma=False,
    )
```

profile of v0, /device:TPU:0, one launch (start us, length us, event | category | flops | bytes accessed | tf_op | source)
XLA Modules:
  0.0 298.4 jit_solution(4314532587612037235)
XLA Ops:
  7.2 0.0 copy-start
  7.2 0.0 copy-start.1
  7.2 0.0 reduce-scatter.3.cloned.1.call-start
  7.3 1.8 fusion.9
  9.1 0.8 fusion.34
  10.6 2.0 fusion.68
  12.5 43.5 %psum.49 = f32[2]{0:T(128)S(1)} all-reduce(f32[2]{0:T(128)S(1)} %get-tuple-element.8), channel_id=1, replica_groups=mesh['seq'=16,'dp'=2] {'seq'}, use_global_device_ids=true, to_apply=%region_4.5 | all-reduce | flops 2 | bytes 16 | tf_op jit(solution)/shard_map/psum | solution.py:31
  56.0 0.0 copy-done.1
  56.0 0.3 fusion.16
  56.3 1.6 fusion.12
  57.9 71.8 %all-reduce.1 = (bf16[2,1280]{1,0:T(2,128)(2,1)S(1)}, bf16[2,1280]{1,0:T(2,128)(2,1)S(1)}) all-reduce(f32[2,1280]{1,0:T(2,128)S(1)} %fusion.16, f32[2,1280]{1,0:T(2,128)S(1)} %fusion.12), channel_id=1, replica_groups=mesh['seq'=16,'dp'=2] {'seq'}, use_global_device_ids=true, to_apply=%region_5.6 | all-reduce | flops 5120 | bytes 30720 | tf_op jit(solution)/shard_map/psum | solution.py:35
  129.7 0.0 copy-start.2
  129.7 0.0 copy-done
  129.7 0.3 convolution_reduce_fusion.3
  130.1 1.0 copy-done.2
  131.2 0.5 convolution_reduce_fusion.2
  131.7 2.0 broadcast_multiply_fusion.1
  133.7 0.0 reduce-scatter.3.cloned.1.call-update
  133.7 0.0 reduce-scatter.5.cloned.1.call-start
  133.8 2.0 broadcast_multiply_fusion
  135.8 0.0 reduce-scatter.5.cloned.1.call-update
  135.8 0.0 copy-start.3
  135.9 0.5 convolution_reduce_fusion
  136.4 1.2 copy-done.3
  137.7 0.3 convolution_reduce_fusion.1
  138.0 0.1 broadcast_select_fusion
  138.1 71.8 %all-reduce = (bf16[2,1280]{1,0:T(2,128)(2,1)S(1)}, bf16[2,1280]{1,0:T(2,128)(2,1)S(1)}) all-reduce(f32[2,1280]{1,0:T(2,128)S(1)} %get-tuple-element.20, f32[2,1280]{1,0:T(2,128)S(1)} %get-tuple-element.19), channel_id=1, replica_groups=mesh['seq'=16,'dp'=2] {'seq'}, use_global_device_ids=true, to_apply=%region_6.7 | all-reduce | flops 5120 | bytes 30720 | tf_op jit(solution)/shard_map/psum | solution.py:42
  209.9 0.4 fusion.18
  210.3 0.0 copy-start.4
  210.3 1.9 multiply_reduce_fusion.1
  212.2 36.6 %psum.54 = f32[2]{0:T(128)S(1)} all-reduce(f32[2]{0:T(128)S(1)} %get-tuple-element.6), channel_id=1, replica_groups=mesh['seq'=16,'dp'=2] {'seq'}, use_global_device_ids=true, to_apply=%region_11.12 | all-reduce | flops 2 | bytes 16 | tf_op jit(solution)/shard_map/psum | solution.py:66
  248.8 0.4 fusion.25
  249.2 37.0 %psum.55 = f32[1280,2]{0,1:T(2,128)S(1)} all-reduce(f32[1280,2]{0,1:T(2,128)S(1)} %fusion.25), channel_id=1, replica_groups=mesh['seq'=16,'dp'=2] {'seq','dp'}, use_global_device_ids=true, to_apply=%region_15.16 | all-reduce | flops 2560 | bytes 20480 | tf_op jit(solution)/shard_map/psum | solution.py:71
  286.2 0.0 copy-done.4
  286.2 0.2 fusion.31
  286.4 1.6 fusion.5
  288.0 0.8 fusion.6
  288.8 2.1 fusion.4
  290.8 0.7 fusion.33
  291.5 0.0 reduce-scatter.3.cloned.1.call-done
  291.5 0.0 reduce-scatter.5.cloned.1.call-done
  (9 shorter events, 0.1 us)
Async XLA Ops:
  7.2 122.6 %copy-start = (bf16[1280,640]{1,0:T(8,128)(2,1)S(1)}, bf16[1280,640]{1,0:T(8,128)(2,1)}, u32[]{:S(2)}) copy-start(bf16[1280,640]{1,0:T(8,128)(2,1)} %param.10) | copy-start | bytes 4915204
  7.2 48.8 %copy-start.1 = (bf16[1,512,1280]{2,1,0:T(8,128)(2,1)S(1)}, bf16[1,512,1280]{2,1,0:T(8,128)(2,1)}, u32[]{:S(2)}) copy-start(bf16[1,512,1280]{2,1,0:T(8,128)(2,1)} %param.6) | copy-start | bytes 3932164
  7.2 284.3 %reduce-scatter.3.cloned.1.call-start = ((), (), s32[]{:S(2)}) async-start(), calls=%async_computation.2 | async-start | bytes 4915200 | tf_op jit(solution)/shard_map/reduce_scatter | solution.py:61
  129.7 1.4 copy-start.2
  133.7 157.8 %reduce-scatter.5.cloned.1.call-start = ((), (), s32[]{:S(2)}) async-start(), calls=%async_computation.3 | async-start | bytes 4915200 | tf_op jit(solution)/shard_map/reduce_scatter | solution.py:62
  135.8 1.9 copy-start.3
  210.3 75.9 %copy-start.4 = (bf16[1280,2]{0,1:T(2,128)(2,1)S(1)}, bf16[1280,2]{0,1:T(2,128)(2,1)}, u32[]{:S(2)}) copy-start(bf16[1280,2]{0,1:T(2,128)(2,1)} %param.8) | copy-start | bytes 15364
Sparse Core Ops, SparseCore 0:
  133.9 6.9 reduce-scatter.2
  143.7 12.1 reduce-scatter.4
where the time goes:
time: 300 us; the launch traced here: 298 us
  blocking collectives  261 us (87%)
  between operations  14.8 us (5%)
  matrix products  12.9 us (4%)
  other arithmetic  7.61 us (3%)
    psum x1, blocking collectives, per_device(): slot_in = lax.psum(slot_part, 'seq')  71.8 us
    psum x1, blocking collectives, per_device(): slot_sum = lax.psum(placed, 'seq')  71.8 us
    psum x1, blocking collectives, per_device(): totals = lax.psum(jnp.sum(exp_scores, axis=0, keepdims=True), 'seq')  43.5 us
    psum x1, blocking collectives, per_device(): phi_grad = lax.psum(phi_part, ('seq', 'dp'))  37 us
    psum x1, blocking collectives, per_device(): column_stat = lax.psum(local_stat, 'seq')  36.6 us
  transfers between devices with their start and end apart: 2, of which 0 were waited for; matrix products, arithmetic and copies ran while one was open for 4% of the time, Pallas kernels for 0%

commit v1 on v0

v1 whole, which is shorter than its diff:
```python
import jax
import jax.numpy as jnp
from jax import lax
from jax.sharding import PartitionSpec as P

epsilon = 1e-06


def gelu_slope(pre_act):
    cdf = 0.5 * (1.0 + lax.erf(pre_act * 0.7071067811865476))
    return cdf + pre_act * jnp.exp(-0.5 * pre_act * pre_act) * 0.3989422804014327


def swap(value, axis, mask):
    size = lax.axis_size(axis)
    return lax.ppermute(value, axis, [(i, i ^ mask) for i in range(size)])


def sum_over(value, axis, low, high):
    mask = low
    while mask < high:
        value = value + swap(value, axis, mask)
        mask *= 2
    return value


def scatter_slots(value, axis, group, size):
    mask = size // 2
    while mask >= group:
        half = value.shape[0] // 2
        upper = (lax.axis_index(axis) & mask) != 0
        low, high = value[:half], value[half:]
        keep = jnp.where(upper, high, low)
        give = jnp.where(upper, low, high)
        value = keep + swap(give, axis, mask)
        mask //= 2
    return value


def gather_slots(value, axis, group, size):
    mask = group
    while mask < size:
        upper = (lax.axis_index(axis) & mask) != 0
        other = swap(value, axis, mask)
        value = jnp.where(
            upper, jnp.concatenate([other, value]), jnp.concatenate([value, other])
        )
        mask *= 2
    return value


def per_device(tokens, cotangent, router, logit_scale, expert_in, expert_out):
    f32, bf16 = jnp.float32, jnp.bfloat16
    tok_in = tokens[0]
    tok_cot = cotangent[0]
    experts = router.shape[1]
    width = router.shape[0]
    size = lax.axis_size("seq")
    group = size // experts
    phi_f32 = router.astype(f32)
    phi_scale = lax.rsqrt(jnp.sum(phi_f32 * phi_f32, axis=0, keepdims=True) + epsilon)
    phi_unit = phi_f32 * phi_scale
    phi_norm = phi_unit.astype(bf16)
    tok_f32 = tok_in.astype(f32)
    tok_scale = lax.rsqrt(jnp.sum(tok_f32 * tok_f32, axis=1, keepdims=True) + epsilon)
    tok_unit = tok_f32 * tok_scale
    tok_norm = tok_unit.astype(bf16)
    logits = logit_scale[0] * jnp.dot(tok_norm, phi_norm, preferred_element_type=f32)
    exp_scores = jnp.exp(logits)
    combine_f = exp_scores / jnp.sum(exp_scores, axis=1, keepdims=True)
    combine = combine_f.astype(bf16)
    exp_high = exp_scores.astype(bf16)
    exp_low = (exp_scores - exp_high.astype(f32)).astype(bf16)
    both = jnp.einsum(
        "ns,nd->sd",
        jnp.concatenate([exp_high, exp_low], axis=1),
        tok_in,
        preferred_element_type=f32,
    )
    in_part = both[:experts] + both[experts:]
    cot_part = jnp.einsum("ns,nd->sd", combine, tok_cot, preferred_element_type=f32)
    local_total = jnp.sum(exp_scores, axis=0)
    all_totals = jnp.broadcast_to(local_total[None, :], (experts, experts))
    packed = jnp.concatenate([in_part, cot_part, all_totals], axis=1)
    packed = scatter_slots(packed, "seq", group, size)
    packed = sum_over(packed, "seq", 1, group)
    owned = lax.axis_index("seq") // group
    totals = packed[:, 2 * width :]
    own_total = lax.dynamic_slice_in_dim(totals, owned, 1, 1)
    own_in = packed[:, :width] / own_total
    row_x = own_in.astype(bf16)
    row_cot = packed[:, width : 2 * width].astype(bf16)
    pre_act = jnp.dot(row_x, expert_in, preferred_element_type=f32)
    hidden = jax.nn.gelu(pre_act, approximate=False).astype(bf16)
    part_out = jnp.dot(hidden, expert_out, preferred_element_type=f32)
    hid_grad = jnp.einsum("od,hd->oh", row_cot, expert_out, preferred_element_type=f32)
    pre_grad = (hid_grad * gelu_slope(pre_act)).astype(bf16)
    part_dx = jnp.einsum("oh,dh->od", pre_grad, expert_in, preferred_element_type=f32)
    rows = jnp.concatenate([row_x, row_cot, hidden, pre_grad], axis=1)
    clips = lax.axis_size("dp")
    me = lax.axis_index("dp")
    all_rows = [rows] + [
        lax.ppermute(rows, "dp", [(i, (i + step) % clips) for i in range(clips)])
        for step in range(1, clips)
    ]
    all_rows = jnp.concatenate(all_rows, axis=0)
    units = expert_in.shape[1]
    all_x, all_cot = all_rows[:, :width], all_rows[:, width : 2 * width]
    all_hidden = all_rows[:, 2 * width : 2 * width + units]
    all_grad = all_rows[:, 2 * width + units :]
    share = width // clips
    mine_x = lax.dynamic_slice_in_dim(all_x, me * share, share, 1)
    mine_cot = lax.dynamic_slice_in_dim(all_cot, me * share, share, 1)
    grad_expert_in = jnp.einsum("od,oh->dh", mine_x, all_grad, preferred_element_type=f32)
    grad_expert_out = jnp.einsum("oh,od->hd", all_hidden, mine_cot, preferred_element_type=f32)
    sums = sum_over(jnp.concatenate([part_out, part_dx], axis=1), "seq", 1, group)
    stat = jnp.sum(own_in * sums[:, width:].astype(bf16).astype(f32), axis=1, keepdims=True)
    sums = gather_slots(
        jnp.concatenate([sums, stat], axis=1), "seq", group, size
    )
    slot_y = sums[:, :width].astype(bf16)
    slot_dx = sums[:, width : 2 * width].astype(bf16)
    column_stat = sums[:, 2 * width :].T
    mixed = jnp.dot(combine, slot_y, preferred_element_type=f32).astype(bf16)
    comb_dot = jnp.einsum("nd,sd->ns", tok_cot, slot_y, preferred_element_type=f32)
    grad_comb = combine_f * (comb_dot - jnp.sum(combine_f * comb_dot, axis=1, keepdims=True))
    dispatch_f = exp_scores / totals
    dispatch = dispatch_f.astype(bf16)
    disp_dot = jnp.einsum("nd,sd->ns", tok_in, slot_dx, preferred_element_type=f32)
    grad_disp = dispatch_f * (disp_dot - column_stat)
    score_grad = (logit_scale[0] * (grad_comb + grad_disp)).astype(bf16)
    norm_grad = jnp.einsum("ns,ds->nd", score_grad, phi_norm, preferred_element_type=f32)
    phi_part = jnp.einsum("nd,ns->sd", tok_norm, score_grad, preferred_element_type=f32)
    phi_grad = sum_over(phi_part, "dp", 1, clips)
    phi_grad = sum_over(phi_grad, "seq", 1, size).T
    through = jnp.dot(dispatch, slot_dx, preferred_element_type=f32)
    back_norm = tok_scale * (
        norm_grad - tok_unit * jnp.sum(tok_unit * norm_grad, axis=1, keepdims=True)
    )
    grad_tokens = (through + back_norm).astype(bf16)
    grad_router = phi_scale * (
        phi_grad - phi_unit * jnp.sum(phi_unit * phi_grad, axis=0, keepdims=True)
    )
    return (mixed[None], grad_tokens[None], grad_expert_in, grad_expert_out, grad_router)


def solution(mesh):
    return jax.shard_map(
        per_device,
        mesh=mesh,
        in_specs=(
            P("dp", "seq", None),
            P("dp", "seq", None),
            P(),
            P(),
            P(None, "seq"),
            P("seq", None),
        ),
        out_specs=(P("dp", "seq", None), P("dp", "seq", None), P("dp", "seq"), P("seq", "dp"), P()),
        check_vma=False,
    )
```

time: 300 us -> 67.7 us (0.23)
  blocking collectives: 261 us -> 0 us
  starting transfers between devices: 0.08 us -> 27.3 us
  waiting for transfers between devices: 0.04 us -> 15.6 us
  between operations: 14.8 us -> 1.52 us
  matrix products: 12.9 us -> 15.9 us
    psum x5 -> x0, blocking collectives: 261 us -> none  [the longest x1 71.8 us: per_device(): slot_in = lax.psum(slot_part, 'seq')]
    ppermute x0 -> x14, starting transfers between devices: none -> 27.3 us  [the longest x13 27.2 us: swap(): return lax.ppermute(value, axis, [(i, i ^ mask) for i in range(size)])]
    ppermute x0 -> x14, waiting for transfers between devices: none -> 15.6 us  [the longest x13 15.6 us: swap(): return lax.ppermute(value, axis, [(i, i ^ mask) for i in range(size)])]
    dot_general x2 -> x0, other arithmetic: 3.96 us -> none  [the longest x1 2 us: per_device(): jnp.einsum('oh,od->hd', hidden, row_cot, preferred_element_type=jnp.float32)]
    dot_general x13 -> x15, matrix products: 12.9 us -> 15.9 us  [the longest x1 2.05 us: per_device(): through = jnp.dot(dispatch, slot_dx, preferred_element_type=f32)]
  transfers between devices with their start and end apart: 2 -> 14, of which waited for: 0 -> 11; matrix products, arithmetic and copies ran while one was open for 4% -> 13% of each run, Pallas kernels for 0% -> 0%
where the time goes in v1:
time: 67.7 us; the launch traced here: 67.5 us
  starting transfers between devices  27.3 us (40%)
  matrix products  15.9 us (23%)
  waiting for transfers between devices  15.6 us (23%)
  other arithmetic  6.42 us (9%)
  between operations  1.52 us (2%)
  local copies, waits for them, and re-layouts  0.77 us (1%)
    ppermute x13, starting transfers between devices, swap(): return lax.ppermute(value, axis, [(i, i ^ mask) for i in range(size)])  27.2 us
    ppermute x13, waiting for transfers between devices, swap(): return lax.ppermute(value, axis, [(i, i ^ mask) for i in range(size)])  15.6 us
    dot_general x1, matrix products, per_device(): through = jnp.dot(dispatch, slot_dx, preferred_element_type=f32)  2.05 us
    dot_general x1, matrix products, per_device(): jnp.dot(tok_norm, phi_norm, preferred_element_type=f32)  1.97 us
    reduce_sum x1, other arithmetic, per_device(): jnp.sum(tok_f32 * tok_f32, axis=1, keepdims=True) + epsilon  1.8 us
    dot_general x1, matrix products, per_device(): jnp.einsum('nd,sd->ns', tok_cot, slot_y, preferred_element_type=f32)  1.78 us
    dot_general x1, matrix products, per_device(): jnp.einsum('oh,od->hd', all_hidden, mine_cot, preferred_element_type=f32)  1.64 us
    dot_general x1, matrix products, per_device(): mixed = jnp.dot(combine, slot_y, preferred_element_type=f32).astype(bf16)  1.62 us
  transfers between devices with their start and end apart: 14, of which 11 were waited for; matrix products, arithmetic and copies ran while one was open for 13% of the time, Pallas kernels for 0%

profile of v1, /device:TPU:0, one launch (start us, length us, event | category | flops | bytes accessed | tf_op | source)
XLA Modules:
  0.0 67.5 jit_solution(17667115481102605751)
XLA Ops:
  0.7 1.8 %fusion.9 = f32[512]{0:T(512)S(1)} fusion(bf16[1,512,1280]{2,1,0:T(8,128)(2,1)} %param.6), kind=kLoop, calls=%fused_computation.13 | loop fusion | flops 1965568 | bytes 1312768 | tf_op jit(solution)/shard_map/reduce_sum | solution.py:65
  2.5 0.8 %fusion.50 = f32[2]{0:T(128)S(1)} fusion(bf16[1280,2]{0,1:T(2,128)(2,1)} %param.8), kind=kLoop, calls=%fused_computation.50 | loop fusion | flops 7678 | bytes 5128 | tf_op jit(solution)/shard_map/reduce_sum | solution.py:61
  4.0 2.0 %subtract_convert_fusion = (bf16[512,2]{0,1:T(2,128)(2,1)S(1)}, bf16[512,2]{0,1:T(2,128)(2,1)S(1)}, f32[512]{0:T(512)S(1)}, f32[2]{0:T(128)S(1)}, f32[512,2]{0,1:T(2,128)S(1)}) fusion(bf16[1280,2]{0,1:T(2,128)(2,1)} %param.8, f32[2]{0:T(128)S(1)} %add_rsqrt_fusion.1, bf16[1,512,1280]{2,1,0:T(8,128)(2,1)} %param.6, f32[512]{0:T(512)S(1)} %add_rsqrt_fusion, ...), kind=kOutput, calls=%fused_computation.94 | convolution fusion | flops 4601854 | bytes 1328148 | tf_op jit(solution)/shard_map/dot_general | solution.py:68
  5.9 0.3 fusion.16
  6.3 1.6 %fusion.12 = f32[2,1280]{1,0:T(2,128)S(1)} fusion(bf16[1,512,1280]{2,1,0:T(8,128)(2,1)} %param.7, f32[512,2]{0,1:T(2,128)S(1)} %get-tuple-element.19, f32[512]{0:T(512)S(1)} %get-tuple-element.17), kind=kOutput, calls=%fused_computation.16 | convolution fusion | flops 2623488 | bytes 1327104 | tf_op jit(solution)/shard_map/ns,nd->sd/dot_general | solution.py:81
  7.9 4.1 %collective-permute-start = (f32[1,2562]{1,0:T(1,128)S(1)}, f32[1,2562]{1,0:T(1,128)S(1)}, u32[]{:S(2)}, u32[]{:S(2)}) collective-permute-start(f32[1,2562]{1,0:T(1,128)S(1)} %broadcast_select_fusion), channel_id=1, source_target_pairs={{0,16},{2,18},{4,20},{6,22},{8,24},{10,26},{12,28},{14,30},{16,0},... | collective-permute-start | bytes 30752 | tf_op jit(solution)/shard_map/ppermute | solution.py:16
  12.0 1.7 %collective-permute-done = f32[1,2562]{1,0:T(1,128)S(1)} collective-permute-done((f32[1,2562]{1,0:T(1,128)S(1)}, f32[1,2562]{1,0:T(1,128)S(1)}, u32[]{:S(2)}, u32[]{:S(2)}) %collective-permute-start) | collective-permute-done | bytes 10280 | tf_op jit(solution)/shard_map/ppermute | solution.py:16
  13.7 1.9 %collective-permute-start.1 = (f32[1,2562]{1,0:T(1,128)S(1)}, f32[1,2562]{1,0:T(1,128)S(1)}, u32[]{:S(2)}, u32[]{:S(2)}) collective-permute-start(f32[1,2562]{1,0:T(1,128)S(1)} %fusion.43), channel_id=1, source_target_pairs={{0,2},{2,0},{4,6},{6,4},{8,10},{10,8},{12,14},{14,12},{16,18},{18,... | collective-permute-start | bytes 30752 | tf_op jit(solution)/shard_map/ppermute | solution.py:16
  15.6 1.9 %collective-permute-done.1 = f32[1,2562]{1,0:T(1,128)S(1)} collective-permute-done((f32[1,2562]{1,0:T(1,128)S(1)}, f32[1,2562]{1,0:T(1,128)S(1)}, u32[]{:S(2)}, u32[]{:S(2)}) %collective-permute-start.1) | collective-permute-done | bytes 10280 | tf_op jit(solution)/shard_map/ppermute | solution.py:16
  17.4 1.9 %collective-permute-start.2 = (f32[1,2562]{1,0:T(1,128)S(1)}, f32[1,2562]{1,0:T(1,128)S(1)}, u32[]{:S(2)}, u32[]{:S(2)}) collective-permute-start(f32[1,2562]{1,0:T(1,128)S(1)} %add.85), channel_id=1, source_target_pairs={{0,4},{2,6},{4,0},{6,2},{8,12},{10,14},{12,8},{14,10},{16,20},{18,... | collective-permute-start | bytes 30752 | tf_op jit(solution)/shard_map/ppermute | solution.py:16
  19.4 1.8 %collective-permute-done.2 = f32[1,2562]{1,0:T(1,128)S(1)} collective-permute-done((f32[1,2562]{1,0:T(1,128)S(1)}, f32[1,2562]{1,0:T(1,128)S(1)}, u32[]{:S(2)}, u32[]{:S(2)}) %collective-permute-start.2) | collective-permute-done | bytes 10280 | tf_op jit(solution)/shard_map/ppermute | solution.py:16
  21.2 2.0 %collective-permute-start.3 = (f32[1,2562]{1,0:T(1,128)S(1)}, f32[1,2562]{1,0:T(1,128)S(1)}, u32[]{:S(2)}, u32[]{:S(2)}) collective-permute-start(f32[1,2562]{1,0:T(1,128)S(1)} %add.86), channel_id=1, source_target_pairs={{0,8},{2,10},{4,12},{6,14},{8,0},{10,2},{12,4},{14,6},{16,24},{18,... | collective-permute-start | bytes 30752 | tf_op jit(solution)/shard_map/ppermute | solution.py:16
  23.2 1.8 %collective-permute-done.3 = f32[1,2562]{1,0:T(1,128)S(1)} collective-permute-done((f32[1,2562]{1,0:T(1,128)S(1)}, f32[1,2562]{1,0:T(1,128)S(1)}, u32[]{:S(2)}, u32[]{:S(2)}) %collective-permute-start.3) | collective-permute-done | bytes 10280 | tf_op jit(solution)/shard_map/ppermute | solution.py:16
  25.0 0.6 constant_dynamic-slice_fusion
  25.6 0.7 fusion.122
  26.2 0.5 convolution_reduce_fusion
  26.8 0.3 convolution_reduce_fusion.1
  27.2 0.3 fusion.124
  27.5 0.5 fusion.125
  28.1 1.9 %collective-permute-start.4 = (f32[1,2560]{1,0:T(1,128)S(1)}, f32[1,2560]{1,0:T(1,128)S(1)}, u32[]{:S(2)}, u32[]{:S(2)}) collective-permute-start(f32[1,2560]{1,0:T(1,128)S(1)} %pad_maximum_fusion.3), channel_id=1, source_target_pairs={{0,2},{2,0},{4,6},{6,4},{8,10},{10,8},{12,14},{14,12},{16,18},{18,... | collective-permute-start | bytes 30728 | tf_op jit(solution)/shard_map/ppermute | solution.py:16
  30.0 1.9 %collective-permute-done.4 = f32[1,2560]{1,0:T(1,128)S(1)} collective-permute-done((f32[1,2560]{1,0:T(1,128)S(1)}, f32[1,2560]{1,0:T(1,128)S(1)}, u32[]{:S(2)}, u32[]{:S(2)}) %collective-permute-start.4) | collective-permute-done | bytes 10272 | tf_op jit(solution)/shard_map/ppermute | solution.py:16
  31.9 1.9 %collective-permute-start.5 = (f32[1,2560]{1,0:T(1,128)S(1)}, f32[1,2560]{1,0:T(1,128)S(1)}, u32[]{:S(2)}, u32[]{:S(2)}) collective-permute-start(f32[1,2560]{1,0:T(1,128)S(1)} %fusion.120), channel_id=1, source_target_pairs={{0,4},{2,6},{4,0},{6,2},{8,12},{10,14},{12,8},{14,10},{16,20},{18,... | collective-permute-start | bytes 30728 | tf_op jit(solution)/shard_map/ppermute | solution.py:16
  33.8 1.8 %collective-permute-done.5 = f32[1,2560]{1,0:T(1,128)S(1)} collective-permute-done((f32[1,2560]{1,0:T(1,128)S(1)}, f32[1,2560]{1,0:T(1,128)S(1)}, u32[]{:S(2)}, u32[]{:S(2)}) %collective-permute-start.5) | collective-permute-done | bytes 10272 | tf_op jit(solution)/shard_map/ppermute | solution.py:16
  35.6 2.0 %collective-permute-start.6 = (f32[1,2560]{1,0:T(1,128)S(1)}, f32[1,2560]{1,0:T(1,128)S(1)}, u32[]{:S(2)}, u32[]{:S(2)}) collective-permute-start(f32[1,2560]{1,0:T(1,128)S(1)} %add.92), channel_id=1, source_target_pairs={{0,8},{2,10},{4,12},{6,14},{8,0},{10,2},{12,4},{14,6},{16,24},{18,... | collective-permute-start | bytes 30728 | tf_op jit(solution)/shard_map/ppermute | solution.py:16
  37.7 1.7 %collective-permute-done.6 = f32[1,2560]{1,0:T(1,128)S(1)} collective-permute-done((f32[1,2560]{1,0:T(1,128)S(1)}, f32[1,2560]{1,0:T(1,128)S(1)}, u32[]{:S(2)}, u32[]{:S(2)}) %collective-permute-start.6) | collective-permute-done | bytes 10272 | tf_op jit(solution)/shard_map/ppermute | solution.py:16
  39.4 0.6 fusion.55
  40.0 0.7 pad_maximum_fusion.2
  40.6 3.0 %collective-permute-start.7 = (f32[1,2561]{1,0:T(1,128)S(1)}, f32[1,2561]{1,0:T(1,128)S(1)}, u32[]{:S(2)}, u32[]{:S(2)}) collective-permute-start(f32[1,2561]{1,0:T(1,128)S(1)} %pad_maximum_fusion.2), channel_id=1, source_target_pairs={{0,16},{2,18},{4,20},{6,22},{8,24},{10,26},{12,28},{14,30},{16,0},... | collective-permute-start | bytes 30740 | tf_op jit(solution)/shard_map/ppermute | solution.py:16
  43.7 1.6 %collective-permute-done.7 = f32[1,2561]{1,0:T(1,128)S(1)} collective-permute-done((f32[1,2561]{1,0:T(1,128)S(1)}, f32[1,2561]{1,0:T(1,128)S(1)}, u32[]{:S(2)}, u32[]{:S(2)}) %collective-permute-start.7) | collective-permute-done | bytes 10276 | tf_op jit(solution)/shard_map/ppermute | solution.py:16
  45.3 0.7 %fusion.123 = (bf16[2,2561]{1,0:T(2,128)(2,1)S(1)}, f32[2,2561]{1,0:T(2,128)S(1)}) fusion(f32[1,2561]{1,0:T(1,128)S(1)} %collective-permute-done.7, f32[1,1]{1,0:T(1,128)} %bitcast.4, f32[1,2560]{1,0:T(1,128)S(1)} %add.93, pred[]{:T(512)S(6)} %ne.12), kind=kLoop, calls=%fused_computation.146 | loop fusion | flops 30732 | bytes 51221 | tf_op jit(solution)/shard_map/convert.1
  46.0 1.8 %multiply_reduce_fusion = (f32[512]{0:T(512)S(1)}, f32[512,2]{0,1:T(2,128)S(1)}) fusion(f32[512,2]{0,1:T(2,128)S(1)} %get-tuple-element.19, f32[512]{0:T(512)S(1)} %get-tuple-element.17, bf16[1,512,1280]{2,1,0:T(8,128)(2,1)} %param.7, bf16[2,2561]{1,0:T(2,128)(2,1)S(1)} %get-tuple-element.9), kind=kOutput, calls=%fused_computation.80 | convolution fusion | flops 2624000 | bytes 1328128 | tf_op jit(solution)/shard_map/nd,sd->ns/dot_general | solution.py:125
  47.8 0.1 slice_reduce_fusion
  47.9 0.4 fusion.37
  48.3 0.4 fusion.40
  48.8 1.6 %fusion.83 = f32[640,640]{1,0:T(8,128)} fusion(s32[]{:T(128)S(6)} %select_n.39, bf16[1,3840]{1,0:T(2,128)(2,1)S(1)} %collective-permute-done.8, bf16[1,640]{1,0:T(2,128)(2,1)S(1)} %convert_element_type.75, bf16[1,640]{1,0:T(2,128)(2,1)S(1)} %convert_element_type.74, bf16[1,1280]{1,0:T(2,128)(2,1)S(1)} %slice.104, bf16[1,1280]{1,0:T(2,128)(2,1)S(1)} %get-tuple-element.7), kind=kOutput, calls=%fused_computation.105 | convolution fusion | flops 1664000 | bytes 1699844 | tf_op jit(solution)/shard_map/oh,od->hd/dot_general | solution.py:115
  50.4 1.9 %collective-permute-start.10 = (f32[2,1280]{1,0:T(2,128)S(1)}, f32[2,1280]{1,0:T(2,128)S(1)}, u32[]{:S(2)}, u32[]{:S(2)}) collective-permute-start(f32[2,1280]{1,0:T(2,128)S(1)} %add.97), channel_id=1, source_target_pairs={{0,2},{2,0},{4,6},{6,4},{8,10},{10,8},{12,14},{14,12},{16,18},{18,... | collective-permute-start | bytes 30728 | tf_op jit(solution)/shard_map/ppermute | solution.py:16
  52.3 1.6 %fusion.94 = f32[640,640]{1,0:T(8,128)} fusion(bf16[1,3840]{1,0:T(2,128)(2,1)S(1)} %collective-permute-done.8, bf16[1,640]{1,0:T(2,128)(2,1)S(1)} %convert_element_type.75, bf16[1,640]{1,0:T(2,128)(2,1)S(1)} %convert_element_type.74, bf16[1,1280]{1,0:T(2,128)(2,1)S(1)} %slice.104, bf16[1,1280]{1,0:T(2,128)(2,1)S(1)} %get-tuple-element.7, ...), kind=kOutput, calls=%fused_computation.115 | convolution fusion | flops 1651200 | bytes 1671684 | tf_op jit(solution)/shard_map/od,oh->dh/dot_general | solution.py:114
  53.9 0.3 collective-permute-done.10
  54.2 1.9 %collective-permute-start.11 = (f32[2,1280]{1,0:T(2,128)S(1)}, f32[2,1280]{1,0:T(2,128)S(1)}, u32[]{:S(2)}, u32[]{:S(2)}) collective-permute-start(f32[2,1280]{1,0:T(2,128)S(1)} %add.98), channel_id=1, source_target_pairs={{0,4},{2,6},{4,0},{6,2},{8,12},{10,14},{12,8},{14,10},{16,20},{18,... | collective-permute-start | bytes 30728 | tf_op jit(solution)/shard_map/ppermute | solution.py:16
  56.1 0.7 %fusion.6 = (f32[512]{0:T(512)S(1)}, f32[512,1280]{1,0:T(8,128)S(1)}) fusion(bf16[1,512,1280]{2,1,0:T(8,128)(2,1)S(1)} %copy-done.1, f32[512]{0:T(512)S(1)} %add_rsqrt_fusion, bf16[512,2]{0,1:T(2,128)(2,1)S(1)} %fusion.37, bf16[1280,2]{0,1:T(2,128)(2,1)S(1)} %copy-done.3, f32[2]{0:T(128)S(1)} %add_rsqrt_fusion.1), kind=kOutput, calls=%fused_computation.10 | convolution fusion | flops 5250048 | bytes 3943432 | tf_op jit(solution)/shard_map/ns,ds->nd/dot_general | solution.py:132
  56.8 1.1 %collective-permute-done.11 = f32[2,1280]{1,0:T(2,128)S(1)} collective-permute-done((f32[2,1280]{1,0:T(2,128)S(1)}, f32[2,1280]{1,0:T(2,128)S(1)}, u32[]{:S(2)}, u32[]{:S(2)}) %collective-permute-start.11) | collective-permute-done | bytes 10272 | tf_op jit(solution)/shard_map/ppermute | solution.py:16
  57.9 2.0 %collective-permute-start.12 = (f32[2,1280]{1,0:T(2,128)S(1)}, f32[2,1280]{1,0:T(2,128)S(1)}, u32[]{:S(2)}, u32[]{:S(2)}) collective-permute-start(f32[2,1280]{1,0:T(2,128)S(1)} %add.99), channel_id=1, source_target_pairs={{0,8},{2,10},{4,12},{6,14},{8,0},{10,2},{12,4},{14,6},{16,24},{18,... | collective-permute-start | bytes 30728 | tf_op jit(solution)/shard_map/ppermute | solution.py:16
  59.9 2.1 %fusion.4 = bf16[1,512,1280]{2,1,0:T(8,128)(2,1)} fusion(f32[512,1280]{1,0:T(8,128)S(1)} %get-tuple-element.23, bf16[1,512,1280]{2,1,0:T(8,128)(2,1)S(1)} %copy-done.1, f32[512]{0:T(512)S(1)} %get-tuple-element.22, f32[512]{0:T(512)S(1)} %add_rsqrt_fusion, bf16[2,2561]{1,0:T(2,128)(2,1)S(1)} %get-tuple-element.9, f32[512,2]{0,1:T(2,128)S(1)} %get-tuple-element.19, ...), kind=kOutput, calls=%fused_computation.8 | convolution fusion | flops 7211008 | bytes 5256704 | tf_op jit(solution)/shard_map/dot_general | solution.py:136
  62.0 2.8 %collective-permute-start.13 = (f32[2,1280]{1,0:T(2,128)S(1)}, f32[2,1280]{1,0:T(2,128)S(1)}, u32[]{:S(2)}, u32[]{:S(2)}) collective-permute-start(f32[2,1280]{1,0:T(2,128)S(1)} %add.100), channel_id=1, source_target_pairs={{0,16},{2,18},{4,20},{6,22},{8,24},{10,26},{12,28},{14,30},{16,0},... | collective-permute-start | bytes 30728 | tf_op jit(solution)/shard_map/ppermute | solution.py:16
  64.8 1.6 %fusion.5 = bf16[1,512,1280]{2,1,0:T(8,128)(2,1)} fusion(bf16[2,2561]{1,0:T(2,128)(2,1)S(1)} %get-tuple-element.9, f32[512,2]{0,1:T(2,128)S(1)} %get-tuple-element.19, f32[512]{0:T(512)S(1)} %get-tuple-element.17), kind=kOutput, calls=%fused_computation.9 | convolution fusion | flops 3278848 | bytes 1321984 | tf_op jit(solution)/shard_map/dot_general | solution.py:124
  66.4 0.2 collective-permute-done.13
  66.6 0.2 fusion.47
  66.8 0.7 %fusion.49 = f32[1280,2]{0,1:T(2,128)} fusion(bf16[1280,2]{0,1:T(2,128)(2,1)S(1)} %copy-done.3, f32[2]{0:T(128)S(1)} %fusion.47, f32[2]{0:T(128)S(1)} %add_rsqrt_fusion.1, f32[2,1280]{1,0:T(2,128)S(1)} %add.100, f32[2,1280]{1,0:T(2,128)S(1)} %collective-permute-done.13), kind=kLoop, calls=%fused_computation.49 | loop fusion | flops 15360 | bytes 35856 | tf_op jit(solution)/shard_map/mul | solution.py:141
  (41 shorter events, 0.5 us)
Async XLA Ops:
  0.6 25.6 %copy-start = (bf16[640,1280]{1,0:T(8,128)(2,1)S(1)}, bf16[640,1280]{1,0:T(8,128)(2,1)}, u32[]{:S(2)}) copy-start(bf16[640,1280]{1,0:T(8,128)(2,1)} %param.11) | copy-start | bytes 4915204
  0.6 5.3 %copy-start.1 = (bf16[1,512,1280]{2,1,0:T(8,128)(2,1)S(1)}, bf16[1,512,1280]{2,1,0:T(8,128)(2,1)}, u32[]{:S(2)}) copy-start(bf16[1,512,1280]{2,1,0:T(8,128)(2,1)} %param.6) | copy-start | bytes 3932164
  7.9 5.8 %collective-permute-start = (f32[1,2562]{1,0:T(1,128)S(1)}, f32[1,2562]{1,0:T(1,128)S(1)}, u32[]{:S(2)}, u32[]{:S(2)}) collective-permute-start(f32[1,2562]{1,0:T(1,128)S(1)} %broadcast_select_fusion), channel_id=1, source_target_pairs={{0,16},{2,18},{4,20},{6,22},{8,24},{10,26},{12,28},{14,30},{16,0},... | collective-permute-start | bytes 30752 | tf_op jit(solution)/shard_map/ppermute | solution.py:16
  13.7 3.7 %collective-permute-start.1 = (f32[1,2562]{1,0:T(1,128)S(1)}, f32[1,2562]{1,0:T(1,128)S(1)}, u32[]{:S(2)}, u32[]{:S(2)}) collective-permute-start(f32[1,2562]{1,0:T(1,128)S(1)} %fusion.43), channel_id=1, source_target_pairs={{0,2},{2,0},{4,6},{6,4},{8,10},{10,8},{12,14},{14,12},{16,18},{18,... | collective-permute-start | bytes 30752 | tf_op jit(solution)/shard_map/ppermute | solution.py:16
  17.4 3.7 %collective-permute-start.2 = (f32[1,2562]{1,0:T(1,128)S(1)}, f32[1,2562]{1,0:T(1,128)S(1)}, u32[]{:S(2)}, u32[]{:S(2)}) collective-permute-start(f32[1,2562]{1,0:T(1,128)S(1)} %add.85), channel_id=1, source_target_pairs={{0,4},{2,6},{4,0},{6,2},{8,12},{10,14},{12,8},{14,10},{16,20},{18,... | collective-permute-start | bytes 30752 | tf_op jit(solution)/shard_map/ppermute | solution.py:16
  21.2 3.7 %collective-permute-start.3 = (f32[1,2562]{1,0:T(1,128)S(1)}, f32[1,2562]{1,0:T(1,128)S(1)}, u32[]{:S(2)}, u32[]{:S(2)}) collective-permute-start(f32[1,2562]{1,0:T(1,128)S(1)} %add.86), channel_id=1, source_target_pairs={{0,8},{2,10},{4,12},{6,14},{8,0},{10,2},{12,4},{14,6},{16,24},{18,... | collective-permute-start | bytes 30752 | tf_op jit(solution)/shard_map/ppermute | solution.py:16
  23.2 3.6 %copy-start.2 = (bf16[1280,640]{1,0:T(8,128)(2,1)S(1)}, bf16[1280,640]{1,0:T(8,128)(2,1)}, u32[]{:S(2)}) copy-start(bf16[1280,640]{1,0:T(8,128)(2,1)} %param.10) | copy-start | bytes 4915204
  28.1 3.7 %collective-permute-start.4 = (f32[1,2560]{1,0:T(1,128)S(1)}, f32[1,2560]{1,0:T(1,128)S(1)}, u32[]{:S(2)}, u32[]{:S(2)}) collective-permute-start(f32[1,2560]{1,0:T(1,128)S(1)} %pad_maximum_fusion.3), channel_id=1, source_target_pairs={{0,2},{2,0},{4,6},{6,4},{8,10},{10,8},{12,14},{14,12},{16,18},{18,... | collective-permute-start | bytes 30728 | tf_op jit(solution)/shard_map/ppermute | solution.py:16
  31.9 3.7 %collective-permute-start.5 = (f32[1,2560]{1,0:T(1,128)S(1)}, f32[1,2560]{1,0:T(1,128)S(1)}, u32[]{:S(2)}, u32[]{:S(2)}) collective-permute-start(f32[1,2560]{1,0:T(1,128)S(1)} %fusion.120), channel_id=1, source_target_pairs={{0,4},{2,6},{4,0},{6,2},{8,12},{10,14},{12,8},{14,10},{16,20},{18,... | collective-permute-start | bytes 30728 | tf_op jit(solution)/shard_map/ppermute | solution.py:16
  35.6 3.7 %collective-permute-start.6 = (f32[1,2560]{1,0:T(1,128)S(1)}, f32[1,2560]{1,0:T(1,128)S(1)}, u32[]{:S(2)}, u32[]{:S(2)}) collective-permute-start(f32[1,2560]{1,0:T(1,128)S(1)} %add.92), channel_id=1, source_target_pairs={{0,8},{2,10},{4,12},{6,14},{8,0},{10,2},{12,4},{14,6},{16,24},{18,... | collective-permute-start | bytes 30728 | tf_op jit(solution)/shard_map/ppermute | solution.py:16
  37.6 6.0 %collective-permute-start.8 = (bf16[1,3840]{1,0:T(2,128)(2,1)S(1)}, bf16[1,3840]{1,0:T(2,128)(2,1)S(1)}, u32[]{:S(2)}, u32[]{:S(2)}) collective-permute-start(bf16[1,3840]{1,0:T(2,128)(2,1)S(1)} %pad_maximum_fusion), channel_id=1, source_target_pairs={{0,1},{1,0},{2,3},{3,2},{4,5},{5,4},{6,7},{7,6},{8,9},{9,8},{10,11... | collective-permute-start | bytes 23048 | tf_op jit(solution)/shard_map/ppermute | solution.py:103
  40.6 4.6 %collective-permute-start.7 = (f32[1,2561]{1,0:T(1,128)S(1)}, f32[1,2561]{1,0:T(1,128)S(1)}, u32[]{:S(2)}, u32[]{:S(2)}) collective-permute-start(f32[1,2561]{1,0:T(1,128)S(1)} %pad_maximum_fusion.2), channel_id=1, source_target_pairs={{0,16},{2,18},{4,20},{6,22},{8,24},{10,26},{12,28},{14,30},{16,0},... | collective-permute-start | bytes 30740 | tf_op jit(solution)/shard_map/ppermute | solution.py:16
  48.8 7.3 %copy-start.3 = (bf16[1280,2]{0,1:T(2,128)(2,1)S(1)}, bf16[1280,2]{0,1:T(2,128)(2,1)}, u32[]{:S(2)}) copy-start(bf16[1280,2]{0,1:T(2,128)(2,1)} %param.8) | copy-start | bytes 15364
  48.8 1.7 %collective-permute-start.9 = (f32[2,1280]{1,0:T(2,128)S(1)}, f32[2,1280]{1,0:T(2,128)S(1)}, u32[]{:S(2)}, u32[]{:S(2)}) collective-permute-start(f32[2,1280]{1,0:T(2,128)S(1)} %fusion.40), channel_id=1, source_target_pairs={{0,1},{1,0},{2,3},{3,2},{4,5},{5,4},{6,7},{7,6},{8,9},{9,8},{10,11... | collective-permute-start | bytes 30728 | tf_op jit(solution)/shard_map/ppermute | solution.py:16
  50.4 3.7 %collective-permute-start.10 = (f32[2,1280]{1,0:T(2,128)S(1)}, f32[2,1280]{1,0:T(2,128)S(1)}, u32[]{:S(2)}, u32[]{:S(2)}) collective-permute-start(f32[2,1280]{1,0:T(2,128)S(1)} %add.97), channel_id=1, source_target_pairs={{0,2},{2,0},{4,6},{6,4},{8,10},{10,8},{12,14},{14,12},{16,18},{18,... | collective-permute-start | bytes 30728 | tf_op jit(solution)/shard_map/ppermute | solution.py:16
  54.2 3.7 %collective-permute-start.11 = (f32[2,1280]{1,0:T(2,128)S(1)}, f32[2,1280]{1,0:T(2,128)S(1)}, u32[]{:S(2)}, u32[]{:S(2)}) collective-permute-start(f32[2,1280]{1,0:T(2,128)S(1)} %add.98), channel_id=1, source_target_pairs={{0,4},{2,6},{4,0},{6,2},{8,12},{10,14},{12,8},{14,10},{16,20},{18,... | collective-permute-start | bytes 30728 | tf_op jit(solution)/shard_map/ppermute | solution.py:16
  57.9 4.0 %collective-permute-start.12 = (f32[2,1280]{1,0:T(2,128)S(1)}, f32[2,1280]{1,0:T(2,128)S(1)}, u32[]{:S(2)}, u32[]{:S(2)}) collective-permute-start(f32[2,1280]{1,0:T(2,128)S(1)} %add.99), channel_id=1, source_target_pairs={{0,8},{2,10},{4,12},{6,14},{8,0},{10,2},{12,4},{14,6},{16,24},{18,... | collective-permute-start | bytes 30728 | tf_op jit(solution)/shard_map/ppermute | solution.py:16
  62.0 4.6 %collective-permute-start.13 = (f32[2,1280]{1,0:T(2,128)S(1)}, f32[2,1280]{1,0:T(2,128)S(1)}, u32[]{:S(2)}, u32[]{:S(2)}) collective-permute-start(f32[2,1280]{1,0:T(2,128)S(1)} %add.100), channel_id=1, source_target_pairs={{0,16},{2,18},{4,20},{6,22},{8,24},{10,26},{12,28},{14,30},{16,0},... | collective-permute-start | bytes 30728 | tf_op jit(solution)/shard_map/ppermute | solution.py:16

commit v2 on v1

--- a/solution.py
+++ b/solution.py
@@ -11,42 +11,21 @@
     return cdf + pre_act * jnp.exp(-0.5 * pre_act * pre_act) * 0.3989422804014327
 
 
-def swap(value, axis, mask):
-    size = lax.axis_size(axis)
-    return lax.ppermute(value, axis, [(i, i ^ mask) for i in range(size)])
+LANES = 128
 
 
-def sum_over(value, axis, low, high):
-    mask = low
-    while mask < high:
-        value = value + swap(value, axis, mask)
-        mask *= 2
-    return value
+def packed_rows(parts, rows):
+    flat = jnp.concatenate([part.reshape(part.shape[0], -1) for part in parts], axis=1)
+    flat = jnp.pad(flat, ((0, 0), (0, rows * LANES - flat.shape[1])))
+    return flat.reshape(flat.shape[0], rows, LANES)
 
 
-def scatter_slots(value, axis, group, size):
-    mask = size // 2
-    while mask >= group:
-        half = value.shape[0] // 2
-        upper = (lax.axis_index(axis) & mask) != 0
-        low, high = value[:half], value[half:]
-        keep = jnp.where(upper, high, low)
-        give = jnp.where(upper, low, high)
-        value = keep + swap(give, axis, mask)
-        mask //= 2
-    return value
+def row_count(values):
+    return -(-values // (8 * LANES)) * 8
 
 
-def gather_slots(value, axis, group, size):
-    mask = group
-    while mask < size:
-        upper = (lax.axis_index(axis) & mask) != 0
-        other = swap(value, axis, mask)
-        value = jnp.where(
-            upper, jnp.concatenate([other, value]), jnp.concatenate([value, other])
-        )
-        mask *= 2
-    return value
+def to_each(value, axis):
+    return lax.all_to_all(value, axis, split_axis=0, concat_axis=0)
 
 
 def per_device(tokens, cotangent, router, logit_scale, expert_in, expert_out):
@@ -81,11 +60,12 @@
     cot_part = jnp.einsum("ns,nd->sd", combine, tok_cot, preferred_element_type=f32)
     local_total = jnp.sum(exp_scores, axis=0)
     all_totals = jnp.broadcast_to(local_total[None, :], (experts, experts))
-    packed = jnp.concatenate([in_part, cot_part, all_totals], axis=1)
-    packed = scatter_slots(packed, "seq", group, size)
-    packed = sum_over(packed, "seq", 1, group)
+    rows_a = row_count(2 * width + experts)
+    packed = packed_rows([in_part, cot_part, all_totals], rows_a)
+    packed = jnp.repeat(packed, group, axis=0)
+    packed = jnp.sum(to_each(packed, "seq"), axis=0).reshape(1, -1)
     owned = lax.axis_index("seq") // group
-    totals = packed[:, 2 * width :]
+    totals = packed[:, 2 * width : 2 * width + experts]
     own_total = lax.dynamic_slice_in_dim(totals, owned, 1, 1)
     own_in = packed[:, :width] / own_total
     row_x = own_in.astype(bf16)
@@ -113,14 +93,14 @@
     mine_cot = lax.dynamic_slice_in_dim(all_cot, me * share, share, 1)
     grad_expert_in = jnp.einsum("od,oh->dh", mine_x, all_grad, preferred_element_type=f32)
     grad_expert_out = jnp.einsum("oh,od->hd", all_hidden, mine_cot, preferred_element_type=f32)
-    sums = sum_over(jnp.concatenate([part_out, part_dx], axis=1), "seq", 1, group)
-    stat = jnp.sum(own_in * sums[:, width:].astype(bf16).astype(f32), axis=1, keepdims=True)
-    sums = gather_slots(
-        jnp.concatenate([sums, stat], axis=1), "seq", group, size
-    )
+    dot_part = jnp.sum(own_in * part_dx, axis=1, keepdims=True)
+    rows_b = row_count(2 * width + 1)
+    sums = packed_rows([part_out, part_dx, dot_part], rows_b)
+    sums = to_each(jnp.broadcast_to(sums, (size,) + sums.shape[1:]), "seq")
+    sums = jnp.sum(sums.reshape(experts, group, rows_b * LANES), axis=1)
     slot_y = sums[:, :width].astype(bf16)
     slot_dx = sums[:, width : 2 * width].astype(bf16)
-    column_stat = sums[:, 2 * width :].T
+    column_stat = sums[:, 2 * width : 2 * width + 1].T
     mixed = jnp.dot(combine, slot_y, preferred_element_type=f32).astype(bf16)
     comb_dot = jnp.einsum("nd,sd->ns", tok_cot, slot_y, preferred_element_type=f32)
     grad_comb = combine_f * (comb_dot - jnp.sum(combine_f * comb_dot, axis=1, keepdims=True))
@@ -131,8 +111,13 @@
     score_grad = (logit_scale[0] * (grad_comb + grad_disp)).astype(bf16)
     norm_grad = jnp.einsum("ns,ds->nd", score_grad, phi_norm, preferred_element_type=f32)
     phi_part = jnp.einsum("nd,ns->sd", tok_norm, score_grad, preferred_element_type=f32)
-    phi_grad = sum_over(phi_part, "dp", 1, clips)
-    phi_grad = sum_over(phi_grad, "seq", 1, size).T
+    devices = size * clips
+    share_d = -(-experts * width // (devices * LANES)) * LANES
+    phi_flat = jnp.pad(phi_part.reshape(-1), (0, devices * share_d - experts * width))
+    both_axes = ("seq", "dp")
+    phi_sum = jnp.sum(to_each(phi_flat.reshape(devices, 1, share_d), both_axes), axis=0)
+    phi_all = to_each(jnp.broadcast_to(phi_sum, (devices, 1, share_d)), both_axes)
+    phi_grad = phi_all.reshape(-1)[: experts * width].reshape(experts, width).T
     through = jnp.dot(dispatch, slot_dx, preferred_element_type=f32)
     back_norm = tok_scale * (
         norm_grad - tok_unit * jnp.sum(tok_unit * norm_grad, axis=1, keepdims=True)

time: 67.7 us -> 70.9 us (1.047)
  starting transfers between devices: 27.3 us -> 17.1 us
  waiting for transfers between devices: 15.6 us -> 23.4 us
  matrix products: 15.9 us -> 19.7 us
  local copies, waits for them, and re-layouts: 0.77 us -> 3.5 us
  other arithmetic: 6.42 us -> 5.18 us
    ppermute x13 -> x0, starting transfers between devices: 27.2 us -> none  [swap(): return lax.ppermute(value, axis, [(i, i ^ mask) for i in range(size)])]
    all_to_all x0 -> x4, waiting for transfers between devices: none -> 23.4 us  [to_each(): return lax.all_to_all(value, axis, split_axis=0, concat_axis=0)]
    all_to_all x0 -> x4, starting transfers between devices: none -> 17 us  [to_each(): return lax.all_to_all(value, axis, split_axis=0, concat_axis=0)]
    ppermute x13 -> x0, waiting for transfers between devices: 15.6 us -> none  [swap(): return lax.ppermute(value, axis, [(i, i ^ mask) for i in range(size)])]
    broadcast_in_dim x0 -> x3, local copies, waits for them, and re-layouts: none -> 1.99 us  [the longest x1 0.69 us: per_device(): packed = jnp.repeat(packed, group, axis=0)]
    dot_general x1, matrix products: 2.05 us -> 3.73 us  [per_device(): through = jnp.dot(dispatch, slot_dx, preferred_element_type=f32)]
    dot_general x1, matrix products: 0.53 us -> 1.96 us  [per_device(): jnp.einsum('od,hd->oh', row_cot, expert_out, preferred_element_type=f32)]
    dot_general x1, matrix products: 0.73 us -> 2.14 us  [per_device(): jnp.einsum('ns,ds->nd', score_grad, phi_norm, preferred_element_type=f32)]
  transfers between devices with their start and end apart: 14 -> 5, of which waited for: 11 -> 4; matrix products, arithmetic and copies ran while one was open for 13% -> 16% of each run, Pallas kernels for 0% -> 0%
where the time goes in v2:
time: 70.9 us; the launch traced here: 70.4 us
  waiting for transfers between devices  23.4 us (33%)
  matrix products  19.7 us (28%)
  starting transfers between devices  17.1 us (24%)
  other arithmetic  5.18 us (7%)
  local copies, waits for them, and re-layouts  3.5 us (5%)
  between operations  1.6 us (2%)
    all_to_all x4, waiting for transfers between devices, to_each(): return lax.all_to_all(value, axis, split_axis=0, concat_axis=0)  23.4 us
    all_to_all x4, starting transfers between devices, to_each(): return lax.all_to_all(value, axis, split_axis=0, concat_axis=0)  17 us
    dot_general x1, matrix products, per_device(): through = jnp.dot(dispatch, slot_dx, preferred_element_type=f32)  3.73 us
    dot_general x1, matrix products, per_device(): jnp.einsum('ns,ds->nd', score_grad, phi_norm, preferred_element_type=f32)  2.14 us
    dot_general x1, matrix products, per_device(): jnp.dot(tok_norm, phi_norm, preferred_element_type=f32)  1.97 us
    dot_general x1, matrix products, per_device(): jnp.einsum('od,hd->oh', row_cot, expert_out, preferred_element_type=f32)  1.96 us
    reduce_sum x1, other arithmetic, per_device(): jnp.sum(tok_f32 * tok_f32, axis=1, keepdims=True) + epsilon  1.8 us
    dot_general x1, matrix products, per_device(): jnp.einsum('nd,sd->ns', tok_cot, slot_y, preferred_element_type=f32)  1.78 us
  transfers between devices with their start and end apart: 5, of which 4 were waited for; matrix products, arithmetic and copies ran while one was open for 16% of the time, Pallas kernels for 0%

profile of v2, /device:TPU:0, one launch (start us, length us, event | category | flops | bytes accessed | tf_op | source)
XLA Modules:
  0.0 70.4 jit_solution(2973454630992417179)
XLA Ops:
  0.6 0.0 copy-start
  0.6 0.0 copy-start.1
  0.7 1.8 %fusion.9 = f32[512]{0:T(512)S(1)} fusion(bf16[1,512,1280]{2,1,0:T(8,128)(2,1)} %param.6), kind=kLoop, calls=%fused_computation.13 | loop fusion | flops 1965568 | bytes 1312768 | tf_op jit(solution)/shard_map/reduce_sum | solution.py:44
  2.5 0.0 copy-start.3
  2.5 0.9 %fusion.49 = f32[2]{0:T(128)S(1)} fusion(bf16[1280,2]{0,1:T(2,128)(2,1)} %param.8), kind=kLoop, calls=%fused_computation.50 | loop fusion | flops 7678 | bytes 5128 | tf_op jit(solution)/shard_map/reduce_sum | solution.py:40
  4.1 2.0 %subtract_convert_fusion = (bf16[512,2]{0,1:T(2,128)(2,1)S(1)}, bf16[512,2]{0,1:T(2,128)(2,1)S(1)}, f32[512]{0:T(512)S(1)}, f32[2]{0:T(128)S(1)}, f32[512,2]{0,1:T(2,128)S(1)}) fusion(bf16[1280,2]{0,1:T(2,128)(2,1)} %param.8, f32[2]{0:T(128)S(1)} %add_rsqrt_fusion.1, bf16[1,512,1280]{2,1,0:T(8,128)(2,1)} %param.6, f32[512]{0:T(512)S(1)} %add_rsqrt_fusion, ...), kind=kOutput, calls=%fused_computation.91 | convolution fusion | flops 4601854 | bytes 1328148 | tf_op jit(solution)/shard_map/dot_general | solution.py:47
  6.0 0.0 copy-done.1
  6.0 0.3 fusion.16
  6.3 0.0 copy-done.3
  6.4 0.3 fusion.12
  6.7 0.7 broadcast_in_dim.17
  7.4 8.3 %all-to-all-start = ((f32[16,24,128]{2,1,0:T(8,128)}), f32[16,24,128]{2,1,0:T(8,128)S(1)}, u32[]{:S(2)}, u32[]{:S(2)}) async-start(f32[16,24,128]{2,1,0:T(8,128)} %bitcast.3), calls=%async_computation | async-start | bytes 393216 | tf_op jit(solution)/shard_map/all_to_all | solution.py:28
  15.7 8.6 %all-to-all-done = f32[16,24,128]{2,1,0:T(8,128)S(1)} async-done(((f32[16,24,128]{2,1,0:T(8,128)}), f32[16,24,128]{2,1,0:T(8,128)S(1)}, u32[]{:S(2)}, u32[]{:S(2)}) %all-to-all-start) | async-done | bytes 196640 | tf_op jit(solution)/shard_map/all_to_all | solution.py:28
  24.4 0.6 constant_dynamic-slice_fusion
  25.0 0.7 fusion.117
  25.6 2.0 %convolution_reduce_fusion = f32[640]{0:T(1024)S(1)} fusion(bf16[640,1280]{1,0:T(8,128)(2,1)} %param.11, f32[1,3072]{1,0:T(1,128)S(1)} %bitcast.89), kind=kOutput, calls=%fused_computation.30 | convolution fusion | flops 1638400 | bytes 1646080 | tf_op jit(solution)/shard_map/od,hd->oh/dot_general | solution.py:76
  27.6 0.0 copy-done
  27.6 0.0 copy-start.2
  27.6 0.3 convolution_reduce_fusion.1
  28.1 0.1 collective-permute-start
  28.2 1.2 %multiply_reduce_fusion = (f32[]{:T(128)}, f32[1,1280]{1,0:T(1,128)S(1)}) fusion(f32[1,1280]{1,0:T(1,128)S(1)} %get-tuple-element.8, bf16[640,1]{0,1:T(2,128)(2,1)S(1)} %reshape.168, bf16[1280,640]{1,0:T(8,128)(2,1)S(1)} %copy-done), kind=kOutput, calls=%fused_computation.64 | convolution fusion | flops 1640959 | bytes 1649924 | tf_op jit(solution)/shard_map/oh,dh->od/dot_general | solution.py:78
  29.3 0.0 copy-done.2
  29.3 0.3 fusion.118
  29.7 0.7 select_maximum_fusion
  30.3 0.7 broadcast_in_dim.38
  31.0 3.5 %all-to-all-start.1 = ((f32[16,24,128]{2,1,0:T(8,128)}), f32[16,24,128]{2,1,0:T(8,128)S(1)}, u32[]{:S(2)}, u32[]{:S(2)}) async-start(f32[16,24,128]{2,1,0:T(8,128)} %broadcast_in_dim.38), calls=%async_computation.1 | async-start | bytes 393216 | tf_op jit(solution)/shard_map/all_to_all | solution.py:28
  34.6 0.0 collective-permute-done
  34.6 1.6 %fusion.79 = f32[640,640]{1,0:T(8,128)} fusion(s32[]{:T(128)S(6)} %select_n.14, bf16[1,3840]{1,0:T(2,128)(2,1)S(1)} %collective-permute-done, bf16[1,640]{1,0:T(2,128)(2,1)S(1)} %convert_element_type.76, bf16[1,640]{1,0:T(2,128)(2,1)S(1)} %convert_element_type.75, bf16[1,1280]{1,0:T(2,128)(2,1)S(1)} %slice.84, bf16[1,1280]{1,0:T(2,128)(2,1)S(1)} %get-tuple-element.7), kind=kOutput, calls=%fused_computation.102 | convolution fusion | flops 1664000 | bytes 1699844 | tf_op jit(solution)/shard_map/oh,od->hd/dot_general | solution.py:95
  36.3 1.6 %fusion.90 = f32[640,640]{1,0:T(8,128)} fusion(bf16[1,3840]{1,0:T(2,128)(2,1)S(1)} %collective-permute-done, bf16[1,640]{1,0:T(2,128)(2,1)S(1)} %convert_element_type.76, bf16[1,640]{1,0:T(2,128)(2,1)S(1)} %convert_element_type.75, bf16[1,1280]{1,0:T(2,128)(2,1)S(1)} %slice.84, bf16[1,1280]{1,0:T(2,128)(2,1)S(1)} %get-tuple-element.7, ...), kind=kOutput, calls=%fused_computation.112 | convolution fusion | flops 1651200 | bytes 1671684 | tf_op jit(solution)/shard_map/od,oh->dh/dot_general | solution.py:94
  37.9 0.0 copy-start.4
  37.9 5.9 %all-to-all-done.1 = f32[16,24,128]{2,1,0:T(8,128)S(1)} async-done(((f32[16,24,128]{2,1,0:T(8,128)}), f32[16,24,128]{2,1,0:T(8,128)S(1)}, u32[]{:S(2)}, u32[]{:S(2)}) %all-to-all-start.1) | async-done | bytes 196640 | tf_op jit(solution)/shard_map/all_to_all | solution.py:28
  43.8 0.1 reduce_sum.105
  43.9 0.1 slice_reduce_fusion.1
  44.0 1.8 %multiply_reduce_fusion.1 = (f32[512]{0:T(512)S(1)}, f32[512,2]{0,1:T(2,128)S(1)}) fusion(f32[512,2]{0,1:T(2,128)S(1)} %get-tuple-element.17, f32[512]{0:T(512)S(1)} %get-tuple-element.15, bf16[1,512,1280]{2,1,0:T(8,128)(2,1)} %param.7, bf16[2,3072]{1,0:T(2,128)(2,1)S(1)} %convert.8), kind=kOutput, calls=%fused_computation.77 | convolution fusion | flops 2624000 | bytes 1328128 | tf_op jit(solution)/shard_map/nd,sd->ns/dot_general | solution.py:105
  45.8 0.4 fusion.37
  46.3 0.0 copy-done.4
  46.3 2.1 %fusion.6 = (f32[512]{0:T(512)S(1)}, f32[512,1280]{1,0:T(8,128)}) fusion(bf16[1,512,1280]{2,1,0:T(8,128)(2,1)S(1)} %copy-done.1, f32[512]{0:T(512)S(1)} %add_rsqrt_fusion, bf16[512,2]{0,1:T(2,128)(2,1)S(1)} %fusion.37, bf16[1280,2]{0,1:T(2,128)(2,1)S(1)} %copy-done.4, f32[2]{0:T(128)S(1)} %add_rsqrt_fusion.1), kind=kOutput, calls=%fused_computation.10 | convolution fusion | flops 5250048 | bytes 3943432 | tf_op jit(solution)/shard_map/ns,ds->nd/dot_general | solution.py:112
  48.4 0.4 fusion.40
  48.9 0.6 pad.14
  49.5 2.6 %all-to-all-start.2 = ((f32[32,1,128]{2,1,0:T(1,128)}), f32[32,1,128]{2,1,0:T(1,128)S(1)}, u32[]{:S(2)}, u32[]{:S(2)}) async-start(f32[32,1,128]{2,1,0:T(1,128)} %bitcast.13), calls=%async_computation.2 | async-start | bytes 32768 | tf_op jit(solution)/shard_map/all_to_all | solution.py:28
  52.1 3.7 %fusion.4 = bf16[1,512,1280]{2,1,0:T(8,128)(2,1)} fusion(f32[512,1280]{1,0:T(8,128)} %get-tuple-element.23, bf16[1,512,1280]{2,1,0:T(8,128)(2,1)S(1)} %copy-done.1, f32[512]{0:T(512)S(1)} %get-tuple-element.22, f32[512]{0:T(512)S(1)} %add_rsqrt_fusion, bf16[2,3072]{1,0:T(2,128)(2,1)S(1)} %convert.8, f32[512,2]{0,1:T(2,128)S(1)} %get-tuple-element.17, ...), kind=kOutput, calls=%fused_computation.8 | convolution fusion | flops 7211008 | bytes 5256704 | tf_op jit(solution)/shard_map/dot_general | solution.py:121
  55.8 3.3 %all-to-all-done.2 = f32[32,1,128]{2,1,0:T(1,128)S(1)} async-done(((f32[32,1,128]{2,1,0:T(1,128)}), f32[32,1,128]{2,1,0:T(1,128)S(1)}, u32[]{:S(2)}, u32[]{:S(2)}) %all-to-all-start.2) | async-done | bytes 16416 | tf_op jit(solution)/shard_map/all_to_all | solution.py:28
  59.2 0.6 broadcast_in_dim.41
  59.8 2.6 %all-to-all-start.3 = ((f32[32,1,128]{2,1,0:T(1,128)}), f32[32,1,128]{2,1,0:T(1,128)S(1)}, u32[]{:S(2)}, u32[]{:S(2)}) async-start(f32[32,1,128]{2,1,0:T(1,128)} %broadcast_in_dim.41), calls=%async_computation.3 | async-start | bytes 32768 | tf_op jit(solution)/shard_map/all_to_all | solution.py:28
  62.4 1.6 %fusion.5 = bf16[1,512,1280]{2,1,0:T(8,128)(2,1)} fusion(bf16[2,3072]{1,0:T(2,128)(2,1)S(1)} %convert.8, f32[512,2]{0,1:T(2,128)S(1)} %get-tuple-element.17, f32[512]{0:T(512)S(1)} %get-tuple-element.15), kind=kOutput, calls=%fused_computation.9 | convolution fusion | flops 3278848 | bytes 1321984 | tf_op jit(solution)/shard_map/dot_general | solution.py:104
  64.0 5.5 %all-to-all-done.3 = f32[32,1,128]{2,1,0:T(1,128)S(1)} async-done(((f32[32,1,128]{2,1,0:T(1,128)}), f32[32,1,128]{2,1,0:T(1,128)S(1)}, u32[]{:S(2)}, u32[]{:S(2)}) %all-to-all-start.3) | async-done | bytes 16416 | tf_op jit(solution)/shard_map/all_to_all | solution.py:28
  69.6 0.2 fusion.46
  69.8 0.7 fusion.48
  (24 shorter events, 0.3 us)
Async XLA Ops:
  0.6 27.0 %copy-start = (bf16[1280,640]{1,0:T(8,128)(2,1)S(1)}, bf16[1280,640]{1,0:T(8,128)(2,1)}, u32[]{:S(2)}) copy-start(bf16[1280,640]{1,0:T(8,128)(2,1)} %param.10) | copy-start | bytes 4915204
  0.6 5.4 %copy-start.1 = (bf16[1,512,1280]{2,1,0:T(8,128)(2,1)S(1)}, bf16[1,512,1280]{2,1,0:T(8,128)(2,1)}, u32[]{:S(2)}) copy-start(bf16[1,512,1280]{2,1,0:T(8,128)(2,1)} %param.6) | copy-start | bytes 3932164
  2.5 3.9 %copy-start.3 = (bf16[1,512,1280]{2,1,0:T(8,128)(2,1)S(1)}, bf16[1,512,1280]{2,1,0:T(8,128)(2,1)}, u32[]{:S(2)}) copy-start(bf16[1,512,1280]{2,1,0:T(8,128)(2,1)} %param.7) | copy-start | bytes 3932164
  7.4 17.0 %all-to-all-start = ((f32[16,24,128]{2,1,0:T(8,128)}), f32[16,24,128]{2,1,0:T(8,128)S(1)}, u32[]{:S(2)}, u32[]{:S(2)}) async-start(f32[16,24,128]{2,1,0:T(8,128)} %bitcast.3), calls=%async_computation | async-start | bytes 393216 | tf_op jit(solution)/shard_map/all_to_all | solution.py:28
  27.6 1.7 %copy-start.2 = (bf16[640,1280]{1,0:T(8,128)(2,1)S(1)}, bf16[640,1280]{1,0:T(8,128)(2,1)}, u32[]{:S(2)}) copy-start(bf16[640,1280]{1,0:T(8,128)(2,1)} %param.11) | copy-start | bytes 4915204
  28.1 6.5 %collective-permute-start = (bf16[1,3840]{1,0:T(2,128)(2,1)S(1)}, bf16[1,3840]{1,0:T(2,128)(2,1)S(1)}, u32[]{:S(2)}, u32[]{:S(2)}) collective-permute-start(bf16[1,3840]{1,0:T(2,128)(2,1)S(1)} %pad_maximum_fusion), channel_id=1, source_target_pairs={{0,1},{1,0},{2,3},{3,2},{4,5},{5,4},{6,7},{7,6},{8,9},{9,8},{10,11... | collective-permute-start | bytes 23048 | tf_op jit(solution)/shard_map/ppermute | solution.py:83
  31.0 12.8 %all-to-all-start.1 = ((f32[16,24,128]{2,1,0:T(8,128)}), f32[16,24,128]{2,1,0:T(8,128)S(1)}, u32[]{:S(2)}, u32[]{:S(2)}) async-start(f32[16,24,128]{2,1,0:T(8,128)} %broadcast_in_dim.38), calls=%async_computation.1 | async-start | bytes 393216 | tf_op jit(solution)/shard_map/all_to_all | solution.py:28
  37.9 8.4 %copy-start.4 = (bf16[1280,2]{0,1:T(2,128)(2,1)S(1)}, bf16[1280,2]{0,1:T(2,128)(2,1)}, u32[]{:S(2)}) copy-start(bf16[1280,2]{0,1:T(2,128)(2,1)} %param.8) | copy-start | bytes 15364
  49.5 9.7 %all-to-all-start.2 = ((f32[32,1,128]{2,1,0:T(1,128)}), f32[32,1,128]{2,1,0:T(1,128)S(1)}, u32[]{:S(2)}, u32[]{:S(2)}) async-start(f32[32,1,128]{2,1,0:T(1,128)} %bitcast.13), calls=%async_computation.2 | async-start | bytes 32768 | tf_op jit(solution)/shard_map/all_to_all | solution.py:28
  59.8 9.7 %all-to-all-start.3 = ((f32[32,1,128]{2,1,0:T(1,128)}), f32[32,1,128]{2,1,0:T(1,128)S(1)}, u32[]{:S(2)}, u32[]{:S(2)}) async-start(f32[32,1,128]{2,1,0:T(1,128)} %broadcast_in_dim.41), calls=%async_computation.3 | async-start | bytes 32768 | tf_op jit(solution)/shard_map/all_to_all | solution.py:28

commit v3 on v2

--- a/solution.py
+++ b/solution.py
@@ -59,13 +59,16 @@
     in_part = both[:experts] + both[experts:]
     cot_part = jnp.einsum("ns,nd->sd", combine, tok_cot, preferred_element_type=f32)
     local_total = jnp.sum(exp_scores, axis=0)
-    all_totals = jnp.broadcast_to(local_total[None, :], (experts, experts))
-    rows_a = row_count(2 * width + experts)
-    packed = packed_rows([in_part, cot_part, all_totals], rows_a)
+    total_high = local_total.astype(bf16)
+    total_low = (local_total - total_high.astype(f32)).astype(bf16)
+    all_totals = jnp.tile(jnp.concatenate([total_high, total_low])[None, :], (experts, 1))
+    rows_a = row_count(2 * width + 2 * experts)
+    packed = packed_rows([in_part.astype(bf16), cot_part.astype(bf16), all_totals], rows_a)
     packed = jnp.repeat(packed, group, axis=0)
-    packed = jnp.sum(to_each(packed, "seq"), axis=0).reshape(1, -1)
+    packed = jnp.sum(to_each(packed, "seq").astype(f32), axis=0).reshape(1, -1)
     owned = lax.axis_index("seq") // group
     totals = packed[:, 2 * width : 2 * width + experts]
+    totals = totals + packed[:, 2 * width + experts : 2 * width + 2 * experts]
     own_total = lax.dynamic_slice_in_dim(totals, owned, 1, 1)
     own_in = packed[:, :width] / own_total
     row_x = own_in.astype(bf16)
@@ -95,9 +98,9 @@
     grad_expert_out = jnp.einsum("oh,od->hd", all_hidden, mine_cot, preferred_element_type=f32)
     dot_part = jnp.sum(own_in * part_dx, axis=1, keepdims=True)
     rows_b = row_count(2 * width + 1)
-    sums = packed_rows([part_out, part_dx, dot_part], rows_b)
+    sums = packed_rows([part_out, part_dx, dot_part], rows_b).astype(bf16)
     sums = to_each(jnp.broadcast_to(sums, (size,) + sums.shape[1:]), "seq")
-    sums = jnp.sum(sums.reshape(experts, group, rows_b * LANES), axis=1)
+    sums = jnp.sum(sums.reshape(experts, group, rows_b * LANES).astype(f32), axis=1)
     slot_y = sums[:, :width].astype(bf16)
     slot_dx = sums[:, width : 2 * width].astype(bf16)
     column_stat = sums[:, 2 * width : 2 * width + 1].T
@@ -111,13 +114,26 @@
     score_grad = (logit_scale[0] * (grad_comb + grad_disp)).astype(bf16)
     norm_grad = jnp.einsum("ns,ds->nd", score_grad, phi_norm, preferred_element_type=f32)
     phi_part = jnp.einsum("nd,ns->sd", tok_norm, score_grad, preferred_element_type=f32)
-    devices = size * clips
-    share_d = -(-experts * width // (devices * LANES)) * LANES
-    phi_flat = jnp.pad(phi_part.reshape(-1), (0, devices * share_d - experts * width))
-    both_axes = ("seq", "dp")
-    phi_sum = jnp.sum(to_each(phi_flat.reshape(devices, 1, share_d), both_axes), axis=0)
-    phi_all = to_each(jnp.broadcast_to(phi_sum, (devices, 1, share_d)), both_axes)
-    phi_grad = phi_all.reshape(-1)[: experts * width].reshape(experts, width).T
+    phi_rows = phi_part.reshape(1, -1, LANES)
+    for step in range(1, clips):
+        phi_rows = phi_rows + lax.ppermute(
+            phi_part.reshape(1, -1, LANES), "dp", [(i, (i + step) % clips) for i in range(clips)]
+        )
+    stride = 1
+    while stride < size:
+        radix = min(4, size // stride)
+        groups = [
+            [base + low + stride * i for i in range(radix)]
+            for base in range(0, size, stride * radix)
+            for low in range(stride)
+        ]
+        spread = jnp.broadcast_to(phi_rows, (radix,) + phi_rows.shape[1:])
+        spread = lax.all_to_all(
+            spread, "seq", split_axis=0, concat_axis=0, axis_index_groups=groups
+        )
+        phi_rows = jnp.sum(spread, axis=0, keepdims=True)
+        stride *= radix
+    phi_grad = phi_rows.reshape(experts, width).T
     through = jnp.dot(dispatch, slot_dx, preferred_element_type=f32)
     back_norm = tok_scale * (
         norm_grad - tok_unit * jnp.sum(tok_unit * norm_grad, axis=1, keepdims=True)

time: 70.9 us -> 66.8 us (0.942)
  waiting for transfers between devices: 23.4 us -> 17.4 us
  starting transfers between devices: 17.1 us -> 18.5 us
    all_to_all x4 -> x2, waiting for transfers between devices: 23.4 us -> 12.3 us  [to_each(): return lax.all_to_all(value, axis, split_axis=0, concat_axis=0)]
    all_to_all x0 -> x2, starting transfers between devices: none -> 6.55 us  [per_device(): lax.all_to_all(spread, 'seq', split_axis=0, concat_axis=0, axis_index_gro...]
    all_to_all x4 -> x2, starting transfers between devices: 17 us -> 11.8 us  [to_each(): return lax.all_to_all(value, axis, split_axis=0, concat_axis=0)]
    all_to_all x0 -> x2, waiting for transfers between devices: none -> 5.08 us  [per_device(): lax.all_to_all(spread, 'seq', split_axis=0, concat_axis=0, axis_index_gro...]
  transfers between devices with their start and end apart: 5 -> 6, of which waited for: 4 -> 4; matrix products, arithmetic and copies ran while one was open for 16% -> 18% of each run, Pallas kernels for 0% -> 0%
where the time goes in v3:
time: 66.8 us; the launch traced here: 66.2 us
  matrix products  19.8 us (30%)
  starting transfers between devices  18.5 us (28%)
  waiting for transfers between devices  17.4 us (26%)
  other arithmetic  5.43 us (8%)
  local copies, waits for them, and re-layouts  3.43 us (5%)
  between operations  1.6 us (2%)
    all_to_all x2, waiting for transfers between devices, to_each(): return lax.all_to_all(value, axis, split_axis=0, concat_axis=0)  12.3 us
    all_to_all x2, starting transfers between devices, to_each(): return lax.all_to_all(value, axis, split_axis=0, concat_axis=0)  11.8 us
    all_to_all x2, starting transfers between devices, per_device(): lax.all_to_all(spread, 'seq', split_axis=0, concat_axis=0, axis_index_gro...  6.55 us
    all_to_all x2, waiting for transfers between devices, per_device(): lax.all_to_all(spread, 'seq', split_axis=0, concat_axis=0, axis_index_gro...  5.08 us
    dot_general x1, matrix products, per_device(): through = jnp.dot(dispatch, slot_dx, preferred_element_type=f32)  3.73 us
    dot_general x1, matrix products, per_device(): jnp.einsum('ns,ds->nd', score_grad, phi_norm, preferred_element_type=f32)  2.14 us
    dot_general x1, matrix products, per_device(): jnp.einsum('od,hd->oh', row_cot, expert_out, preferred_element_type=f32)  2.08 us
    dot_general x1, matrix products, per_device(): jnp.dot(tok_norm, phi_norm, preferred_element_type=f32)  1.97 us
  transfers between devices with their start and end apart: 6, of which 4 were waited for; matrix products, arithmetic and copies ran while one was open for 18% of the time, Pallas kernels for 0%

profile of v3, /device:TPU:0, one launch (start us, length us, event | category | flops | bytes accessed | tf_op | source)
XLA Modules:
  0.0 66.2 jit_solution(3999655177498408020)
XLA Ops:
  0.6 0.0 copy-start
  0.6 0.0 copy-start.1
  0.7 1.8 %fusion.9 = f32[512]{0:T(512)S(1)} fusion(bf16[1,512,1280]{2,1,0:T(8,128)(2,1)} %param.6), kind=kLoop, calls=%fused_computation.13 | loop fusion | flops 1965568 | bytes 1312768 | tf_op jit(solution)/shard_map/reduce_sum | solution.py:44
  2.5 0.0 copy-start.3
  2.5 0.9 %fusion.49 = f32[2]{0:T(128)S(1)} fusion(bf16[1280,2]{0,1:T(2,128)(2,1)} %param.8), kind=kLoop, calls=%fused_computation.54 | loop fusion | flops 7678 | bytes 5128 | tf_op jit(solution)/shard_map/reduce_sum | solution.py:40
  4.1 2.0 %subtract_convert_fusion = (bf16[512,2]{0,1:T(2,128)(2,1)S(1)}, bf16[512,2]{0,1:T(2,128)(2,1)S(1)}, f32[512]{0:T(512)S(1)}, f32[2]{0:T(128)S(1)}, f32[512,2]{0,1:T(2,128)S(1)}) fusion(bf16[1280,2]{0,1:T(2,128)(2,1)} %param.8, f32[2]{0:T(128)S(1)} %add_rsqrt_fusion.1, bf16[1,512,1280]{2,1,0:T(8,128)(2,1)} %param.6, f32[512]{0:T(512)S(1)} %add_rsqrt_fusion, ...), kind=kOutput, calls=%fused_computation.96 | convolution fusion | flops 4601854 | bytes 1328148 | tf_op jit(solution)/shard_map/dot_general | solution.py:47
  6.0 0.3 fusion.15
  6.3 0.1 pad_maximum_fusion.2
  6.4 0.3 convolution_convert_fusion.1
  6.8 0.7 broadcast_in_dim.17
  7.4 8.3 %all-to-all-start = ((bf16[16,24,128]{2,1,0:T(8,128)(2,1)}), bf16[16,24,128]{2,1,0:T(8,128)(2,1)S(1)}, u32[]{:S(2)}, u32[]{:S(2)}) async-start(bf16[16,24,128]{2,1,0:T(8,128)(2,1)} %bitcast.3), calls=%async_computation | async-start | bytes 196608 | tf_op jit(solution)/shard_map/all_to_all | solution.py:28
  15.8 7.6 %all-to-all-done = bf16[16,24,128]{2,1,0:T(8,128)(2,1)S(1)} async-done(((bf16[16,24,128]{2,1,0:T(8,128)(2,1)}), bf16[16,24,128]{2,1,0:T(8,128)(2,1)S(1)}, u32[]{:S(2)}, u32[]{:S(2)}) %all-to-all-start) | async-done | bytes 98336 | tf_op jit(solution)/shard_map/all_to_all | solution.py:28
  23.4 0.1 slice_add_fusion.1
  23.5 0.1 fusion.129
  23.6 0.6 constant_dynamic-slice_fusion
  24.2 0.7 fusion.118
  24.8 0.0 copy-start.2
  24.8 2.1 %convolution_reduce_fusion.1 = f32[640]{0:T(1024)S(1)} fusion(bf16[640,1280]{1,0:T(8,128)(2,1)} %param.11, f32[1,3072]{1,0:T(1,128)S(1)} %bitcast.87), kind=kOutput, calls=%fused_computation.31 | convolution fusion | flops 1638400 | bytes 1646080 | tf_op jit(solution)/shard_map/od,hd->oh/dot_general | solution.py:79
  26.9 0.3 convolution_reduce_fusion.2
  27.4 0.3 convolution_reduce_fusion
  27.8 1.2 %fusion.119 = (bf16[1,1280]{1,0:T(2,128)(2,1)S(1)}, bf16[]{:T(256)}) fusion(f32[1,1280]{1,0:T(1,128)S(1)} %get-tuple-element.8, bf16[640,1]{0,1:T(2,128)(2,1)S(1)} %reshape.166, bf16[1280,640]{1,0:T(8,128)(2,1)S(1)} %copy-done), kind=kOutput, calls=%fused_computation.148 | convolution fusion | flops 1642239 | bytes 1647362 | tf_op jit(solution)/shard_map/oh,dh->od/dot_general | solution.py:81
  28.9 0.1 collective-permute-start
  29.0 0.7 %fusion.42 = bf16[3072]{0:T(1024)(128)(2,1)S(1)} fusion(bf16[1,1]{1,0:T(2,128)(2,1)} %bitcast.6, bf16[1,1280]{1,0:T(2,128)(2,1)S(1)} %get-tuple-element.11, bf16[1,1280]{1,0:T(2,128)(2,1)S(1)} %dot_general.56), kind=kLoop, calls=%fused_computation.46 | loop fusion | flops 30720 | bytes 11266 | tf_op jit(solution)/shard_map/jit(_pad)/pad | solution.py:19
  29.7 0.7 broadcast_in_dim.19
  30.4 3.5 %all-to-all-start.1 = ((bf16[16,24,128]{2,1,0:T(8,128)(2,1)}), bf16[16,24,128]{2,1,0:T(8,128)(2,1)S(1)}, u32[]{:S(2)}, u32[]{:S(2)}) async-start(bf16[16,24,128]{2,1,0:T(8,128)(2,1)} %broadcast_in_dim.19), calls=%async_computation.1 | async-start | bytes 196608 | tf_op jit(solution)/shard_map/all_to_all | solution.py:28
  33.9 0.0 collective-permute-done
  34.0 1.6 %fusion.80 = f32[640,640]{1,0:T(8,128)} fusion(s32[]{:T(128)S(6)} %select_n.14, bf16[1,3840]{1,0:T(2,128)(2,1)S(1)} %collective-permute-done, bf16[1,640]{1,0:T(2,128)(2,1)S(1)} %convert_element_type.116, bf16[1,640]{1,0:T(2,128)(2,1)S(1)} %convert_element_type.115, bf16[1,1280]{1,0:T(2,128)(2,1)S(1)} %slice.85, bf16[1,1280]{1,0:T(2,128)(2,1)S(1)} %get-tuple-element.7), kind=kOutput, calls=%fused_computation.107 | convolution fusion | flops 1664000 | bytes 1699844 | tf_op jit(solution)/shard_map/oh,od->hd/dot_general | solution.py:98
  35.6 1.6 %fusion.91 = f32[640,640]{1,0:T(8,128)} fusion(bf16[1,3840]{1,0:T(2,128)(2,1)S(1)} %collective-permute-done, bf16[1,640]{1,0:T(2,128)(2,1)S(1)} %convert_element_type.116, bf16[1,640]{1,0:T(2,128)(2,1)S(1)} %convert_element_type.115, bf16[1,1280]{1,0:T(2,128)(2,1)S(1)} %slice.85, bf16[1,1280]{1,0:T(2,128)(2,1)S(1)} %get-tuple-element.7, ...), kind=kOutput, calls=%fused_computation.117 | convolution fusion | flops 1651200 | bytes 1671684 | tf_op jit(solution)/shard_map/od,oh->dh/dot_general | solution.py:97
  37.2 4.6 %all-to-all-done.1 = bf16[16,24,128]{2,1,0:T(8,128)(2,1)S(1)} async-done(((bf16[16,24,128]{2,1,0:T(8,128)(2,1)}), bf16[16,24,128]{2,1,0:T(8,128)(2,1)S(1)}, u32[]{:S(2)}, u32[]{:S(2)}) %all-to-all-start.1) | async-done | bytes 98336 | tf_op jit(solution)/shard_map/all_to_all | solution.py:28
  41.9 0.1 reduce_sum.114
  42.0 0.1 slice_reduce_fusion
  42.1 1.8 %multiply_reduce_fusion.1 = (f32[512]{0:T(512)S(1)}, f32[512,2]{0,1:T(2,128)S(1)}) fusion(f32[512,2]{0,1:T(2,128)S(1)} %get-tuple-element.19, f32[512]{0:T(512)S(1)} %get-tuple-element.15, bf16[1,512,1280]{2,1,0:T(8,128)(2,1)} %param.7, bf16[2,3072]{1,0:T(2,128)(2,1)S(1)} %convert.25), kind=kOutput, calls=%fused_computation.82 | convolution fusion | flops 2624000 | bytes 1328128 | tf_op jit(solution)/shard_map/nd,sd->ns/dot_general | solution.py:108
  43.9 0.0 copy-start.4
  43.9 0.4 fusion.36
  44.3 0.4 fusion.39
  44.8 0.1 collective-permute-start.1
  44.9 2.1 %fusion.6 = (f32[512]{0:T(512)S(1)}, f32[512,1280]{1,0:T(8,128)}) fusion(bf16[1,512,1280]{2,1,0:T(8,128)(2,1)S(1)} %copy-done.1, f32[512]{0:T(512)S(1)} %add_rsqrt_fusion, bf16[512,2]{0,1:T(2,128)(2,1)S(1)} %fusion.36, bf16[1280,2]{0,1:T(2,128)(2,1)S(1)} %copy-done.4, f32[2]{0:T(128)S(1)} %add_rsqrt_fusion.1), kind=kOutput, calls=%fused_computation.10 | convolution fusion | flops 5250048 | bytes 3943432 | tf_op jit(solution)/shard_map/ns,ds->nd/dot_general | solution.py:115
  47.0 0.0 collective-permute-done.1
  47.0 0.6 broadcast_in_dim.43
  47.6 3.3 %all-to-all-start.2 = ((f32[4,20,128]{2,1,0:T(8,128)}), f32[4,20,128]{2,1,0:T(8,128)S(1)}, u32[]{:S(2)}, u32[]{:S(2)}) async-start(f32[4,20,128]{2,1,0:T(8,128)} %broadcast_in_dim.43), calls=%async_computation.2 | async-start | bytes 98304 | tf_op jit(solution)/shard_map/all_to_all | solution.py:131
  50.9 3.7 %fusion.4 = bf16[1,512,1280]{2,1,0:T(8,128)(2,1)} fusion(f32[512,1280]{1,0:T(8,128)} %get-tuple-element.23, bf16[1,512,1280]{2,1,0:T(8,128)(2,1)S(1)} %copy-done.1, f32[512]{0:T(512)S(1)} %get-tuple-element.22, f32[512]{0:T(512)S(1)} %add_rsqrt_fusion, bf16[2,3072]{1,0:T(2,128)(2,1)S(1)} %convert.25, f32[512,2]{0,1:T(2,128)S(1)} %get-tuple-element.19, ...), kind=kOutput, calls=%fused_computation.8 | convolution fusion | flops 7211008 | bytes 5256704 | tf_op jit(solution)/shard_map/dot_general | solution.py:137
  54.7 1.0 %all-to-all-done.2 = f32[4,20,128]{2,1,0:T(8,128)S(1)} async-done(((f32[4,20,128]{2,1,0:T(8,128)}), f32[4,20,128]{2,1,0:T(8,128)S(1)}, u32[]{:S(2)}, u32[]{:S(2)}) %all-to-all-start.2) | async-done | bytes 40992 | tf_op jit(solution)/shard_map/all_to_all | solution.py:131
  55.7 0.6 broadcast_in_dim.44
  56.3 3.3 %all-to-all-start.3 = ((f32[4,20,128]{2,1,0:T(8,128)}), f32[4,20,128]{2,1,0:T(8,128)S(1)}, u32[]{:S(2)}, u32[]{:S(2)}) async-start(f32[4,20,128]{2,1,0:T(8,128)} %broadcast_in_dim.44), calls=%async_computation.3 | async-start | bytes 98304 | tf_op jit(solution)/shard_map/all_to_all | solution.py:131
  59.6 1.6 %fusion.5 = bf16[1,512,1280]{2,1,0:T(8,128)(2,1)} fusion(bf16[2,3072]{1,0:T(2,128)(2,1)S(1)} %convert.25, f32[512,2]{0,1:T(2,128)S(1)} %get-tuple-element.19, f32[512]{0:T(512)S(1)} %get-tuple-element.15), kind=kOutput, calls=%fused_computation.9 | convolution fusion | flops 3278848 | bytes 1321984 | tf_op jit(solution)/shard_map/dot_general | solution.py:107
  61.2 4.0 %all-to-all-done.3 = f32[4,20,128]{2,1,0:T(8,128)S(1)} async-done(((f32[4,20,128]{2,1,0:T(8,128)}), f32[4,20,128]{2,1,0:T(8,128)S(1)}, u32[]{:S(2)}, u32[]{:S(2)}) %all-to-all-start.3) | async-done | bytes 40992 | tf_op jit(solution)/shard_map/all_to_all | solution.py:131
  65.3 0.2 fusion.46
  65.5 0.7 %fusion.48 = f32[1280,2]{0,1:T(2,128)} fusion(bf16[1280,2]{0,1:T(2,128)(2,1)S(1)} %copy-done.4, f32[2,1280]{1,0:T(2,128)S(1)} %reshape_broadcast_in_dim.3, f32[2]{0:T(128)S(1)} %fusion.46, f32[2]{0:T(128)S(1)} %add_rsqrt_fusion.1), kind=kLoop, calls=%fused_computation.53 | loop fusion | flops 12800 | bytes 25616 | tf_op jit(solution)/shard_map/mul | solution.py:142
  (30 shorter events, 0.4 us)
Async XLA Ops:
  0.6 26.3 %copy-start = (bf16[1280,640]{1,0:T(8,128)(2,1)S(1)}, bf16[1280,640]{1,0:T(8,128)(2,1)}, u32[]{:S(2)}) copy-start(bf16[1280,640]{1,0:T(8,128)(2,1)} %param.10) | copy-start | bytes 4915204
  0.6 5.4 %copy-start.1 = (bf16[1,512,1280]{2,1,0:T(8,128)(2,1)S(1)}, bf16[1,512,1280]{2,1,0:T(8,128)(2,1)}, u32[]{:S(2)}) copy-start(bf16[1,512,1280]{2,1,0:T(8,128)(2,1)} %param.6) | copy-start | bytes 3932164
  2.5 4.0 %copy-start.3 = (bf16[1,512,1280]{2,1,0:T(8,128)(2,1)S(1)}, bf16[1,512,1280]{2,1,0:T(8,128)(2,1)}, u32[]{:S(2)}) copy-start(bf16[1,512,1280]{2,1,0:T(8,128)(2,1)} %param.7) | copy-start | bytes 3932164
  7.4 16.0 %all-to-all-start = ((bf16[16,24,128]{2,1,0:T(8,128)(2,1)}), bf16[16,24,128]{2,1,0:T(8,128)(2,1)S(1)}, u32[]{:S(2)}, u32[]{:S(2)}) async-start(bf16[16,24,128]{2,1,0:T(8,128)(2,1)} %bitcast.3), calls=%async_computation | async-start | bytes 196608 | tf_op jit(solution)/shard_map/all_to_all | solution.py:28
  24.8 2.6 %copy-start.2 = (bf16[640,1280]{1,0:T(8,128)(2,1)S(1)}, bf16[640,1280]{1,0:T(8,128)(2,1)}, u32[]{:S(2)}) copy-start(bf16[640,1280]{1,0:T(8,128)(2,1)} %param.11) | copy-start | bytes 4915204
  28.9 4.9 %collective-permute-start = (bf16[1,3840]{1,0:T(2,128)(2,1)S(1)}, bf16[1,3840]{1,0:T(2,128)(2,1)S(1)}, u32[]{:S(2)}, u32[]{:S(2)}) collective-permute-start(bf16[1,3840]{1,0:T(2,128)(2,1)S(1)} %pad_maximum_fusion), channel_id=1, source_target_pairs={{0,1},{1,0},{2,3},{3,2},{4,5},{5,4},{6,7},{7,6},{8,9},{9,8},{10,11... | collective-permute-start | bytes 23048 | tf_op jit(solution)/shard_map/ppermute | solution.py:86
  30.4 11.5 %all-to-all-start.1 = ((bf16[16,24,128]{2,1,0:T(8,128)(2,1)}), bf16[16,24,128]{2,1,0:T(8,128)(2,1)S(1)}, u32[]{:S(2)}, u32[]{:S(2)}) async-start(bf16[16,24,128]{2,1,0:T(8,128)(2,1)} %broadcast_in_dim.19), calls=%async_computation.1 | async-start | bytes 196608 | tf_op jit(solution)/shard_map/all_to_all | solution.py:28
  43.9 1.0 %copy-start.4 = (bf16[1280,2]{0,1:T(2,128)(2,1)S(1)}, bf16[1280,2]{0,1:T(2,128)(2,1)}, u32[]{:S(2)}) copy-start(bf16[1280,2]{0,1:T(2,128)(2,1)} %param.8) | copy-start | bytes 15364
  44.8 2.2 %collective-permute-start.1 = (f32[1,20,128]{2,1,0:T(8,128)S(1)}, f32[1,20,128]{2,1,0:T(8,128)S(1)}, u32[]{:S(2)}, u32[]{:S(2)}) collective-permute-start(f32[1,20,128]{2,1,0:T(8,128)S(1)} %reshape.158), channel_id=1, source_target_pairs={{0,1},{1,0},{2,3},{3,2},{4,5},{5,4},{6,7},{7,6},{8,9},{9,8},{10,11... | collective-permute-start | bytes 30728 | tf_op jit(solution)/shard_map/ppermute | solution.py:119
  47.6 8.1 %all-to-all-start.2 = ((f32[4,20,128]{2,1,0:T(8,128)}), f32[4,20,128]{2,1,0:T(8,128)S(1)}, u32[]{:S(2)}, u32[]{:S(2)}) async-start(f32[4,20,128]{2,1,0:T(8,128)} %broadcast_in_dim.43), calls=%async_computation.2 | async-start | bytes 98304 | tf_op jit(solution)/shard_map/all_to_all | solution.py:131
  56.3 8.9 %all-to-all-start.3 = ((f32[4,20,128]{2,1,0:T(8,128)}), f32[4,20,128]{2,1,0:T(8,128)S(1)}, u32[]{:S(2)}, u32[]{:S(2)}) async-start(f32[4,20,128]{2,1,0:T(8,128)} %broadcast_in_dim.44), calls=%async_computation.3 | async-start | bytes 98304 | tf_op jit(solution)/shard_map/all_to_all | solution.py:131

commit v4 on v2

v4 whole, which is shorter than its diff:
```python
import jax
import jax.numpy as jnp
from jax import lax
from jax.sharding import PartitionSpec as P

epsilon = 1e-06


def gelu_slope(pre_act):
    cdf = 0.5 * (1.0 + lax.erf(pre_act * 0.7071067811865476))
    return cdf + pre_act * jnp.exp(-0.5 * pre_act * pre_act) * 0.3989422804014327


LANES = 128
AXES = ("seq", "dp")


def send(value, pairs):
    return lax.ppermute(value, AXES, pairs)


def total_of(terms):
    terms = list(terms)
    while len(terms) > 1:
        pairs = [terms[i] + terms[i + 1] for i in range(0, len(terms) - 1, 2)]
        terms = pairs + terms[len(terms) - len(terms) % 2 :]
    return terms[0]


def in_parts(value):
    parts = []
    for _ in range(3):
        high = lax.reduce_precision(value, 8, 7)
        parts.append(high.astype(jnp.bfloat16))
        value = value - high
    return parts


def root_member(clip, slot, group):
    return (group // 2 * ((slot + 1) % 2) + 3 * (clip % 2)) % group


def flat(seq, clip, clips):
    return seq * clips + clip


def gather_pairs(size, clips, group, across, step):
    pairs = []
    for clip in range(clips):
        for slot in range(size // group):
            root = root_member(clip, slot, group)
            source = (slot ^ across) * group + (root ^ step)
            pairs.append((flat(source, clip, clips), flat(slot * group + root, clip, clips)))
    return pairs


def turned(pairs):
    return [(there, here) for here, there in pairs]


def per_device(tokens, cotangent, router, logit_scale, expert_in, expert_out):
    f32, bf16 = jnp.float32, jnp.bfloat16
    tok_in = tokens[0]
    tok_cot = cotangent[0]
    experts = router.shape[1]
    width = router.shape[0]
    size = lax.axis_size("seq")
    group = size // experts
    phi_f32 = router.astype(f32)
    phi_scale = lax.rsqrt(jnp.sum(phi_f32 * phi_f32, axis=0, keepdims=True) + epsilon)
    phi_unit = phi_f32 * phi_scale
    phi_norm = phi_unit.astype(bf16)
    tok_f32 = tok_in.astype(f32)
    tok_scale = lax.rsqrt(jnp.sum(tok_f32 * tok_f32, axis=1, keepdims=True) + epsilon)
    tok_unit = tok_f32 * tok_scale
    tok_norm = tok_unit.astype(bf16)
    logits = logit_scale[0] * jnp.dot(tok_norm, phi_norm, preferred_element_type=f32)
    exp_scores = jnp.exp(logits)
    combine_f = exp_scores / jnp.sum(exp_scores, axis=1, keepdims=True)
    combine = combine_f.astype(bf16)
    exp_high = lax.reduce_precision(exp_scores, 8, 7)
    exp_low = (exp_scores - exp_high).astype(bf16)
    exp_high = exp_high.astype(bf16)
    both = jnp.einsum(
        "ns,nd->sd",
        jnp.concatenate([exp_high, exp_low], axis=1),
        tok_in,
        preferred_element_type=f32,
    )
    in_part = both[:experts] + both[experts:]
    cot_part = jnp.einsum("ns,nd->sd", combine, tok_cot, preferred_element_type=f32)
    local_total = jnp.sum(exp_scores, axis=0)
    clips = lax.axis_size("dp")
    clip = lax.axis_index("dp")
    place = lax.axis_index("seq")
    owned = place // group
    roots = jnp.array(
        [[slot * group + root_member(c, slot, group) for slot in range(experts)] for c in range(clips)]
    )
    is_root = jnp.any(roots[clip] == place)
    messages = jnp.concatenate(
        [in_part, cot_part, jnp.pad(local_total[:, None], ((0, 0), (0, LANES - 1)))], axis=1
    )

    def part_for(slot):
        return lax.dynamic_slice_in_dim(messages, slot, 1, 0)

    def steps(across):
        return [step for step in range(group - 1, -1, -1) if across or step]

    arrived = [part_for(owned)]
    for across in range(experts):
        message = part_for(owned ^ across)
        for step in steps(across):
            arrived.append(send(message, gather_pairs(size, clips, group, across, step)))
    arrived = total_of(arrived)
    root_total = arrived[:, 2 * width : 2 * width + 1]
    root_in = arrived[:, :width] / root_total
    root_rows = jnp.concatenate([root_in, arrived[:, width : 2 * width]], axis=1).astype(bf16)
    own_rows = jnp.where(is_root, root_rows, jnp.zeros_like(root_rows))
    for step in steps(0):
        own_rows = own_rows + send(root_rows, turned(gather_pairs(size, clips, group, 0, step)))
    row_x = own_rows[:, :width]
    row_cot = own_rows[:, width:]
    pre_act = jnp.dot(row_x, expert_in, preferred_element_type=f32)
    hidden = jax.nn.gelu(pre_act, approximate=False).astype(bf16)
    part_out = jnp.dot(hidden, expert_out, preferred_element_type=f32)
    hid_grad = jnp.einsum("od,hd->oh", row_cot, expert_out, preferred_element_type=f32)
    pre_grad = (hid_grad * gelu_slope(pre_act)).astype(bf16)
    part_dx = jnp.einsum("oh,dh->od", pre_grad, expert_in, preferred_element_type=f32)
    message = jnp.concatenate([part_out, part_dx], axis=1)
    arrived = [message]
    for step in steps(0):
        arrived.append(send(message, gather_pairs(size, clips, group, 0, step)))
    arrived = total_of(arrived)
    root_rows = arrived.astype(bf16)
    root_stat = jnp.sum(
        root_in * root_rows[:, width:].astype(f32), axis=1, keepdims=True
    )
    extra = jnp.concatenate(in_parts(root_stat) + in_parts(root_total), axis=1)
    extra = jnp.pad(extra, ((0, 0), (0, LANES - extra.shape[1])))
    root_rows = jnp.concatenate([root_rows, extra], axis=1)
    by_slot = []
    for across in range(experts):
        got = [send(root_rows, turned(gather_pairs(size, clips, group, across, step))) for step in steps(across)]
        if not across:
            got.append(jnp.where(is_root, root_rows, jnp.zeros_like(root_rows)))
        by_slot.append(total_of(got))
    by_slot = jnp.concatenate(by_slot, axis=0)
    by_slot = jnp.concatenate(
        [lax.dynamic_slice_in_dim(by_slot, owned ^ slot, 1, 0) for slot in range(experts)], axis=0
    )
    slot_y = by_slot[:, :width]
    slot_dx = by_slot[:, width : 2 * width]
    extra = by_slot[:, 2 * width :].astype(f32)
    column_stat = (extra[:, 0:1] + extra[:, 1:2] + extra[:, 2:3]).T
    totals = (extra[:, 3:4] + extra[:, 4:5] + extra[:, 5:6]).T
    rows = jnp.concatenate([row_x, row_cot, hidden, pre_grad], axis=1)
    rows, slot_y, slot_dx = lax.optimization_barrier((rows, slot_y, slot_dx))
    all_rows = [rows] + [
        lax.ppermute(rows, "dp", [(i, (i + step) % clips) for i in range(clips)])
        for step in range(1, clips)
    ]
    all_rows = jnp.concatenate(all_rows, axis=0)
    units = expert_in.shape[1]
    all_x, all_cot = all_rows[:, :width], all_rows[:, width : 2 * width]
    all_hidden = all_rows[:, 2 * width : 2 * width + units]
    all_grad = all_rows[:, 2 * width + units :]
    share = width // clips
    mine_x = lax.dynamic_slice_in_dim(all_x, clip * share, share, 1)
    mine_cot = lax.dynamic_slice_in_dim(all_cot, clip * share, share, 1)
    grad_expert_in = jnp.einsum("od,oh->dh", mine_x, all_grad, preferred_element_type=f32)
    grad_expert_out = jnp.einsum("oh,od->hd", all_hidden, mine_cot, preferred_element_type=f32)
    mixed = jnp.dot(combine, slot_y, preferred_element_type=f32).astype(bf16)
    comb_dot = jnp.einsum("nd,sd->ns", tok_cot, slot_y, preferred_element_type=f32)
    grad_comb = combine_f * (comb_dot - jnp.sum(combine_f * comb_dot, axis=1, keepdims=True))
    dispatch_f = exp_scores / totals
    dispatch = dispatch_f.astype(bf16)
    disp_dot = jnp.einsum("nd,sd->ns", tok_in, slot_dx, preferred_element_type=f32)
    grad_disp = dispatch_f * (disp_dot - column_stat)
    score_grad = (logit_scale[0] * (grad_comb + grad_disp)).astype(bf16)
    norm_grad = jnp.einsum("ns,ds->nd", score_grad, phi_norm, preferred_element_type=f32)
    phi_part = jnp.einsum("nd,ns->sd", tok_norm, score_grad, preferred_element_type=f32)
    last = clips - 1
    phi_flat = phi_part.reshape(1, -1)
    hops = [[(flat(p, c, clips), flat(p, last, clips)) for p in range(size)] for c in range(last)]
    phi_flat = total_of([phi_flat] + [send(phi_flat, hop) for hop in hops])
    top = (experts - 1) // 2 * group + root_member(last, (experts - 1) // 2, group)
    lines = [[(flat(top ^ step, last, clips), flat(top, last, clips))] for step in range(1, size)]
    phi_flat = total_of([phi_flat] + [send(phi_flat, line) for line in lines])
    phi_back = total_of(
        [jnp.where(place == top, phi_flat, jnp.zeros_like(phi_flat))]
        + [send(phi_flat, turned(line)) for line in lines]
    )
    phi_back = total_of(
        [jnp.where(clip == last, phi_back, jnp.zeros_like(phi_back))]
        + [send(phi_back, turned(hop)) for hop in hops]
    )
    phi_grad = phi_back.reshape(experts, width).T
    through = jnp.dot(dispatch, slot_dx, preferred_element_type=f32)
    back_norm = tok_scale * (
        norm_grad - tok_unit * jnp.sum(tok_unit * norm_grad, axis=1, keepdims=True)
    )
    grad_tokens = (through + back_norm).astype(bf16)
    grad_router = phi_scale * (
        phi_grad - phi_unit * jnp.sum(phi_unit * phi_grad, axis=0, keepdims=True)
    )
    return (mixed[None], grad_tokens[None], grad_expert_in, grad_expert_out, grad_router)


def solution(mesh):
    return jax.shard_map(
        per_device,
        mesh=mesh,
        in_specs=(
            P("dp", "seq", None),
            P("dp", "seq", None),
            P(),
            P(),
            P(None, "seq"),
            P("seq", None),
        ),
        out_specs=(P("dp", "seq", None), P("dp", "seq", None), P("dp", "seq"), P("seq", "dp"), P()),
        check_vma=False,
    )
```

time: 70.9 us -> 278 us (3.92)
  starting transfers between devices: 17.1 us -> 224 us
  between operations: 1.6 us -> 13.5 us
  waiting for transfers between devices: 23.4 us -> 12.6 us
  matrix products: 19.7 us -> 15.9 us
    ppermute x0 -> x76, starting transfers between devices: none -> 219 us  [send(): return lax.ppermute(value, AXES, pairs)]
    all_to_all x4 -> x0, waiting for transfers between devices: 23.4 us -> none  [to_each(): return lax.all_to_all(value, axis, split_axis=0, concat_axis=0)]
    all_to_all x4 -> x0, starting transfers between devices: 17 us -> none  [to_each(): return lax.all_to_all(value, axis, split_axis=0, concat_axis=0)]
    ppermute x0 -> x76, waiting for transfers between devices: none -> 12.6 us  [send(): return lax.ppermute(value, AXES, pairs)]
    ppermute x1, starting transfers between devices: 0.07 us -> 5.77 us  [per_device(): lax.ppermute(rows, 'dp', [(i, (i + step) % clips) for i in range(clips)])]
  transfers between devices with their start and end apart: 5 -> 77, of which waited for: 4 -> 3; matrix products, arithmetic and copies ran while one was open for 16% -> 3% of each run, Pallas kernels for 0% -> 0%
where the time goes in v4:
time: 278 us; the launch traced here: 276 us
  starting transfers between devices  224 us (81%)
  matrix products  15.9 us (6%)
  between operations  13.5 us (5%)
  waiting for transfers between devices  12.6 us (5%)
  other arithmetic  7.7 us (3%)
    ppermute x76, starting transfers between devices, send(): return lax.ppermute(value, AXES, pairs)  219 us
    ppermute x76, waiting for transfers between devices, send(): return lax.ppermute(value, AXES, pairs)  12.6 us
    ppermute x1, starting transfers between devices, per_device(): lax.ppermute(rows, 'dp', [(i, (i + step) % clips) for i in range(clips)])  5.77 us
  transfers between devices with their start and end apart: 77, of which 3 were waited for; matrix products, arithmetic and copies ran while one was open for 3% of the time, Pallas kernels for 0%

profile of v4, /device:TPU:0, one launch (start us, length us, event | category | flops | bytes accessed | tf_op | source)
XLA Modules:
  0.0 276.2 jit_solution(9123687217460406319)
XLA Ops:
  0.7 1.8 fusion.9
  2.5 0.8 fusion.53
  4.0 2.0 reduce-precision_convert_fusion
  6.4 1.6 fusion.12
  10.0 9.3 %collective-permute-start.11 = (f32[1,2688]{1,0:T(1,128)S(1)}, f32[1,2688]{1,0:T(1,128)S(1)}, u32[]{:S(2)}, u32[]{:S(2)}) collective-permute-start(f32[1,2688]{1,0:T(1,128)S(1)} %get-tuple-element.22), channel_id=1, source_target_pairs={{30,8},{6,16},{25,15},{1,23}} | collective-permute-start | bytes 32264 | tf_op jit(solution)/shard_map/ppermute | solution.py:19
  19.3 7.0 %collective-permute-start.12 = (f32[1,2688]{1,0:T(1,128)S(1)}, f32[1,2688]{1,0:T(1,128)S(1)}, u32[]{:S(2)}, u32[]{:S(2)}) collective-permute-start(f32[1,2688]{1,0:T(1,128)S(1)} %get-tuple-element.22), channel_id=1, source_target_pairs={{28,8},{4,16},{27,15},{3,23}} | collective-permute-start | bytes 32264 | tf_op jit(solution)/shard_map/ppermute | solution.py:19
  26.4 6.3 %collective-permute-start.13 = (f32[1,2688]{1,0:T(1,128)S(1)}, f32[1,2688]{1,0:T(1,128)S(1)}, u32[]{:S(2)}, u32[]{:S(2)}) collective-permute-start(f32[1,2688]{1,0:T(1,128)S(1)} %get-tuple-element.22), channel_id=1, source_target_pairs={{26,8},{2,16},{29,15},{5,23}} | collective-permute-start | bytes 32264 | tf_op jit(solution)/shard_map/ppermute | solution.py:19
  32.7 7.0 %collective-permute-start.14 = (f32[1,2688]{1,0:T(1,128)S(1)}, f32[1,2688]{1,0:T(1,128)S(1)}, u32[]{:S(2)}, u32[]{:S(2)}) collective-permute-start(f32[1,2688]{1,0:T(1,128)S(1)} %get-tuple-element.22), channel_id=1, source_target_pairs={{24,8},{0,16},{31,15},{7,23}} | collective-permute-start | bytes 32264 | tf_op jit(solution)/shard_map/ppermute | solution.py:19
  40.4 3.8 %collective-permute-start.3 = (f32[1,2688]{1,0:T(1,128)S(1)}, f32[1,2688]{1,0:T(1,128)S(1)}, u32[]{:S(2)}, u32[]{:S(2)}) collective-permute-start(f32[1,2688]{1,0:T(1,128)S(1)} %get-tuple-element.21), channel_id=1, source_target_pairs={{0,8},{24,16},{7,15},{31,23}} | collective-permute-start | bytes 32264 | tf_op jit(solution)/shard_map/ppermute | solution.py:19
  45.6 0.7 collective-permute-start.6
  46.2 5.4 %collective-permute-start.7 = (f32[1,2688]{1,0:T(1,128)S(1)}, f32[1,2688]{1,0:T(1,128)S(1)}, u32[]{:S(2)}, u32[]{:S(2)}) collective-permute-start(f32[1,2688]{1,0:T(1,128)S(1)} %get-tuple-element.22), channel_id=1, source_target_pairs={{22,8},{14,16},{17,15},{9,23}} | collective-permute-start | bytes 32264 | tf_op jit(solution)/shard_map/ppermute | solution.py:19
  51.7 6.3 %collective-permute-start.8 = (f32[1,2688]{1,0:T(1,128)S(1)}, f32[1,2688]{1,0:T(1,128)S(1)}, u32[]{:S(2)}, u32[]{:S(2)}) collective-permute-start(f32[1,2688]{1,0:T(1,128)S(1)} %get-tuple-element.22), channel_id=1, source_target_pairs={{20,8},{12,16},{19,15},{11,23}} | collective-permute-start | bytes 32264 | tf_op jit(solution)/shard_map/ppermute | solution.py:19
  58.1 6.3 %collective-permute-start.9 = (f32[1,2688]{1,0:T(1,128)S(1)}, f32[1,2688]{1,0:T(1,128)S(1)}, u32[]{:S(2)}, u32[]{:S(2)}) collective-permute-start(f32[1,2688]{1,0:T(1,128)S(1)} %get-tuple-element.22), channel_id=1, source_target_pairs={{18,8},{10,16},{21,15},{13,23}} | collective-permute-start | bytes 32264 | tf_op jit(solution)/shard_map/ppermute | solution.py:19
  67.8 1.3 collective-permute-start.18
  71.8 7.3 %collective-permute-done.18 = bf16[1,2560]{1,0:T(2,128)(2,1)S(1)} collective-permute-done((bf16[1,2560]{1,0:T(2,128)(2,1)S(1)}, bf16[1,2560]{1,0:T(2,128)(2,1)S(1)}, u32[]{:S(2)}, u32[]{:S(2)}) %collective-permute-start.18) | collective-permute-done | bytes 5152 | tf_op jit(solution)/shard_map/ppermute | solution.py:19
  79.1 0.7 add_add_fusion.4
  83.7 7.4 %collective-permute-start.25 = (f32[1,2560]{1,0:T(1,128)S(1)}, f32[1,2560]{1,0:T(1,128)S(1)}, u32[]{:S(2)}, u32[]{:S(2)}) collective-permute-start(f32[1,2560]{1,0:T(1,128)S(1)} %pad_maximum_fusion.2), channel_id=1, source_target_pairs={{0,8},{24,16},{7,15},{31,23}} | collective-permute-start | bytes 30728 | tf_op jit(solution)/shard_map/ppermute | solution.py:19
  104.7 1.4 concatenate.57
  108.1 1.3 collective-permute-start.32
  111.5 7.4 %collective-permute-start.36 = (bf16[1,2688]{1,0:T(2,128)(2,1)S(1)}, bf16[1,2688]{1,0:T(2,128)(2,1)S(1)}, u32[]{:S(2)}, u32[]{:S(2)}) collective-permute-start(bf16[1,2688]{1,0:T(2,128)(2,1)S(1)} %fusion.46), channel_id=1, source_target_pairs={{8,22},{16,14},{15,17},{23,9}} | collective-permute-start | bytes 16136 | tf_op jit(solution)/shard_map/ppermute | solution.py:19
  118.9 6.3 %collective-permute-start.37 = (bf16[1,2688]{1,0:T(2,128)(2,1)S(1)}, bf16[1,2688]{1,0:T(2,128)(2,1)S(1)}, u32[]{:S(2)}, u32[]{:S(2)}) collective-permute-start(bf16[1,2688]{1,0:T(2,128)(2,1)S(1)} %fusion.46), channel_id=1, source_target_pairs={{8,20},{16,12},{15,19},{23,11}} | collective-permute-start | bytes 16136 | tf_op jit(solution)/shard_map/ppermute | solution.py:19
  125.2 6.3 %collective-permute-start.38 = (bf16[1,2688]{1,0:T(2,128)(2,1)S(1)}, bf16[1,2688]{1,0:T(2,128)(2,1)S(1)}, u32[]{:S(2)}, u32[]{:S(2)}) collective-permute-start(bf16[1,2688]{1,0:T(2,128)(2,1)S(1)} %fusion.46), channel_id=1, source_target_pairs={{8,18},{16,10},{15,21},{23,13}} | collective-permute-start | bytes 16136 | tf_op jit(solution)/shard_map/ppermute | solution.py:19
  132.3 7.3 %collective-permute-start.40 = (bf16[1,2688]{1,0:T(2,128)(2,1)S(1)}, bf16[1,2688]{1,0:T(2,128)(2,1)S(1)}, u32[]{:S(2)}, u32[]{:S(2)}) collective-permute-start(bf16[1,2688]{1,0:T(2,128)(2,1)S(1)} %fusion.46), channel_id=1, source_target_pairs={{8,30},{16,6},{15,25},{23,1}} | collective-permute-start | bytes 16136 | tf_op jit(solution)/shard_map/ppermute | solution.py:19
  139.6 6.3 %collective-permute-start.41 = (bf16[1,2688]{1,0:T(2,128)(2,1)S(1)}, bf16[1,2688]{1,0:T(2,128)(2,1)S(1)}, u32[]{:S(2)}, u32[]{:S(2)}) collective-permute-start(bf16[1,2688]{1,0:T(2,128)(2,1)S(1)} %fusion.46), channel_id=1, source_target_pairs={{8,28},{16,4},{15,27},{23,3}} | collective-permute-start | bytes 16136 | tf_op jit(solution)/shard_map/ppermute | solution.py:19
  146.0 6.3 %collective-permute-start.42 = (bf16[1,2688]{1,0:T(2,128)(2,1)S(1)}, bf16[1,2688]{1,0:T(2,128)(2,1)S(1)}, u32[]{:S(2)}, u32[]{:S(2)}) collective-permute-start(bf16[1,2688]{1,0:T(2,128)(2,1)S(1)} %fusion.46), channel_id=1, source_target_pairs={{8,26},{16,2},{15,29},{23,5}} | collective-permute-start | bytes 16136 | tf_op jit(solution)/shard_map/ppermute | solution.py:19
  152.4 6.3 %collective-permute-start.43 = (bf16[1,2688]{1,0:T(2,128)(2,1)S(1)}, bf16[1,2688]{1,0:T(2,128)(2,1)S(1)}, u32[]{:S(2)}, u32[]{:S(2)}) collective-permute-start(bf16[1,2688]{1,0:T(2,128)(2,1)S(1)} %fusion.46), channel_id=1, source_target_pairs={{8,24},{16,0},{15,31},{23,7}} | collective-permute-start | bytes 16136 | tf_op jit(solution)/shard_map/ppermute | solution.py:19
  158.7 0.7 fusion.45
  159.5 4.3 %collective-permute-done.43 = bf16[1,2688]{1,0:T(2,128)(2,1)S(1)} collective-permute-done((bf16[1,2688]{1,0:T(2,128)(2,1)S(1)}, bf16[1,2688]{1,0:T(2,128)(2,1)S(1)}, u32[]{:S(2)}, u32[]{:S(2)}) %collective-permute-start.43) | collective-permute-done | bytes 5408 | tf_op jit(solution)/shard_map/ppermute | solution.py:19
  164.2 1.8 multiply_reduce_fusion
  166.9 3.6 %collective-permute-start.45 = (f32[1,2560]{1,0:T(1,128)S(1)}, f32[1,2560]{1,0:T(1,128)S(1)}, u32[]{:S(2)}, u32[]{:S(2)}) collective-permute-start(f32[1,2560]{1,0:T(1,128)S(1)} %bitcast.81), channel_id=1, source_target_pairs={{0,1},{2,3},{4,5},{6,7},{8,9},{10,11},{12,13},{14,15},{16,17},{18,... | collective-permute-start | bytes 30728 | tf_op jit(solution)/shard_map/ppermute | solution.py:19
  170.5 0.8 collective-permute-done.45
  174.6 0.7 fusion.6
  176.7 9.6 %collective-permute-start.53 = (f32[1,2560]{1,0:T(1,128)S(1)}, f32[1,2560]{1,0:T(1,128)S(1)}, u32[]{:S(2)}, u32[]{:S(2)}) collective-permute-start(f32[1,2560]{1,0:T(1,128)S(1)} %add.353), channel_id=1, source_target_pairs={{31,15}} | collective-permute-start | bytes 30728 | tf_op jit(solution)/shard_map/ppermute | solution.py:19
  186.3 6.8 %collective-permute-start.54 = (f32[1,2560]{1,0:T(1,128)S(1)}, f32[1,2560]{1,0:T(1,128)S(1)}, u32[]{:S(2)}, u32[]{:S(2)}) collective-permute-start(f32[1,2560]{1,0:T(1,128)S(1)} %add.353), channel_id=1, source_target_pairs={{29,15}} | collective-permute-start | bytes 30728 | tf_op jit(solution)/shard_map/ppermute | solution.py:19
  193.1 6.3 %collective-permute-start.55 = (f32[1,2560]{1,0:T(1,128)S(1)}, f32[1,2560]{1,0:T(1,128)S(1)}, u32[]{:S(2)}, u32[]{:S(2)}) collective-permute-start(f32[1,2560]{1,0:T(1,128)S(1)} %add.353), channel_id=1, source_target_pairs={{27,15}} | collective-permute-start | bytes 30728 | tf_op jit(solution)/shard_map/ppermute | solution.py:19
  199.5 2.1 fusion.4
  201.5 6.4 %collective-permute-start.56 = (f32[1,2560]{1,0:T(1,128)S(1)}, f32[1,2560]{1,0:T(1,128)S(1)}, u32[]{:S(2)}, u32[]{:S(2)}) collective-permute-start(f32[1,2560]{1,0:T(1,128)S(1)} %add.353), channel_id=1, source_target_pairs={{25,15}} | collective-permute-start | bytes 30728 | tf_op jit(solution)/shard_map/ppermute | solution.py:19
  207.9 6.3 %collective-permute-start.57 = (f32[1,2560]{1,0:T(1,128)S(1)}, f32[1,2560]{1,0:T(1,128)S(1)}, u32[]{:S(2)}, u32[]{:S(2)}) collective-permute-start(f32[1,2560]{1,0:T(1,128)S(1)} %add.353), channel_id=1, source_target_pairs={{23,15}} | collective-permute-start | bytes 30728 | tf_op jit(solution)/shard_map/ppermute | solution.py:19
  214.3 6.3 %collective-permute-start.58 = (f32[1,2560]{1,0:T(1,128)S(1)}, f32[1,2560]{1,0:T(1,128)S(1)}, u32[]{:S(2)}, u32[]{:S(2)}) collective-permute-start(f32[1,2560]{1,0:T(1,128)S(1)} %add.353), channel_id=1, source_target_pairs={{21,15}} | collective-permute-start | bytes 30728 | tf_op jit(solution)/shard_map/ppermute | solution.py:19
  220.6 6.3 %collective-permute-start.59 = (f32[1,2560]{1,0:T(1,128)S(1)}, f32[1,2560]{1,0:T(1,128)S(1)}, u32[]{:S(2)}, u32[]{:S(2)}) collective-permute-start(f32[1,2560]{1,0:T(1,128)S(1)} %add.353), channel_id=1, source_target_pairs={{19,15}} | collective-permute-start | bytes 30728 | tf_op jit(solution)/shard_map/ppermute | solution.py:19
  227.0 6.3 %collective-permute-start.60 = (f32[1,2560]{1,0:T(1,128)S(1)}, f32[1,2560]{1,0:T(1,128)S(1)}, u32[]{:S(2)}, u32[]{:S(2)}) collective-permute-start(f32[1,2560]{1,0:T(1,128)S(1)} %add.353), channel_id=1, source_target_pairs={{17,15}} | collective-permute-start | bytes 30728 | tf_op jit(solution)/shard_map/ppermute | solution.py:19
  233.4 5.8 %collective-permute-start.44 = (bf16[1,3840]{1,0:T(2,128)(2,1)S(1)}, bf16[1,3840]{1,0:T(2,128)(2,1)S(1)}, u32[]{:S(2)}, u32[]{:S(2)}) collective-permute-start(bf16[1,3840]{1,0:T(2,128)(2,1)S(1)} %pad_maximum_fusion), channel_id=1, source_target_pairs={{0,1},{1,0},{2,3},{3,2},{4,5},{5,4},{6,7},{7,6},{8,9},{9,8},{10,11... | collective-permute-start | bytes 23048 | tf_op jit(solution)/shard_map/ppermute | solution.py:161
  242.6 1.6 fusion.5
  245.6 9.5 %collective-permute-start.68 = (f32[1,2560]{1,0:T(1,128)S(1)}, f32[1,2560]{1,0:T(1,128)S(1)}, u32[]{:S(2)}, u32[]{:S(2)}) collective-permute-start(f32[1,2560]{1,0:T(1,128)S(1)} %add_add_fusion.3), channel_id=1, source_target_pairs={{15,31}} | collective-permute-start | bytes 30728 | tf_op jit(solution)/shard_map/ppermute | solution.py:19
  259.9 1.6 fusion.87
  261.7 11.9 %collective-permute-start.76 = (f32[1,2560]{1,0:T(1,128)S(1)}, f32[1,2560]{1,0:T(1,128)S(1)}, u32[]{:S(2)}, u32[]{:S(2)}) collective-permute-start(f32[1,2560]{1,0:T(1,128)S(1)} %add_add_fusion.2), channel_id=1, source_target_pairs={{1,0},{3,2},{5,4},{7,6},{9,8},{11,10},{13,12},{15,14},{17,16},{19,... | collective-permute-start | bytes 30728 | tf_op jit(solution)/shard_map/ppermute | solution.py:19
  273.6 1.6 fusion.90
  275.5 0.7 fusion.52
  (173 shorter events, 37.3 us)
Async XLA Ops:
  8.0 18.4 %collective-permute-start = (f32[1,2688]{1,0:T(1,128)S(1)}, f32[1,2688]{1,0:T(1,128)S(1)}, u32[]{:S(2)}, u32[]{:S(2)}) collective-permute-start(f32[1,2688]{1,0:T(1,128)S(1)} %get-tuple-element.21), channel_id=1, source_target_pairs={{6,8},{30,16},{1,15},{25,23}} | collective-permute-start | bytes 32264 | tf_op jit(solution)/shard_map/ppermute | solution.py:19
  8.7 24.0 %collective-permute-start.1 = (f32[1,2688]{1,0:T(1,128)S(1)}, f32[1,2688]{1,0:T(1,128)S(1)}, u32[]{:S(2)}, u32[]{:S(2)}) collective-permute-start(f32[1,2688]{1,0:T(1,128)S(1)} %get-tuple-element.21), channel_id=1, source_target_pairs={{4,8},{28,16},{3,15},{27,23}} | collective-permute-start | bytes 32264 | tf_op jit(solution)/shard_map/ppermute | solution.py:19
  9.3 30.4 %collective-permute-start.10 = (f32[1,2688]{1,0:T(1,128)S(1)}, f32[1,2688]{1,0:T(1,128)S(1)}, u32[]{:S(2)}, u32[]{:S(2)}) collective-permute-start(f32[1,2688]{1,0:T(1,128)S(1)} %get-tuple-element.22), channel_id=1, source_target_pairs={{16,8},{8,16},{23,15},{15,23}} | collective-permute-start | bytes 32264 | tf_op jit(solution)/shard_map/ppermute | solution.py:19
  10.0 30.4 %collective-permute-start.11 = (f32[1,2688]{1,0:T(1,128)S(1)}, f32[1,2688]{1,0:T(1,128)S(1)}, u32[]{:S(2)}, u32[]{:S(2)}) collective-permute-start(f32[1,2688]{1,0:T(1,128)S(1)} %get-tuple-element.22), channel_id=1, source_target_pairs={{30,8},{6,16},{25,15},{1,23}} | collective-permute-start | bytes 32264 | tf_op jit(solution)/shard_map/ppermute | solution.py:19
  19.3 24.8 %collective-permute-start.12 = (f32[1,2688]{1,0:T(1,128)S(1)}, f32[1,2688]{1,0:T(1,128)S(1)}, u32[]{:S(2)}, u32[]{:S(2)}) collective-permute-start(f32[1,2688]{1,0:T(1,128)S(1)} %get-tuple-element.22), channel_id=1, source_target_pairs={{28,8},{4,16},{27,15},{3,23}} | collective-permute-start | bytes 32264 | tf_op jit(solution)/shard_map/ppermute | solution.py:19
  26.4 18.5 %collective-permute-start.13 = (f32[1,2688]{1,0:T(1,128)S(1)}, f32[1,2688]{1,0:T(1,128)S(1)}, u32[]{:S(2)}, u32[]{:S(2)}) collective-permute-start(f32[1,2688]{1,0:T(1,128)S(1)} %get-tuple-element.22), channel_id=1, source_target_pairs={{26,8},{2,16},{29,15},{5,23}} | collective-permute-start | bytes 32264 | tf_op jit(solution)/shard_map/ppermute | solution.py:19
  32.7 12.8 %collective-permute-start.14 = (f32[1,2688]{1,0:T(1,128)S(1)}, f32[1,2688]{1,0:T(1,128)S(1)}, u32[]{:S(2)}, u32[]{:S(2)}) collective-permute-start(f32[1,2688]{1,0:T(1,128)S(1)} %get-tuple-element.22), channel_id=1, source_target_pairs={{24,8},{0,16},{31,15},{7,23}} | collective-permute-start | bytes 32264 | tf_op jit(solution)/shard_map/ppermute | solution.py:19
  40.4 11.3 %collective-permute-start.3 = (f32[1,2688]{1,0:T(1,128)S(1)}, f32[1,2688]{1,0:T(1,128)S(1)}, u32[]{:S(2)}, u32[]{:S(2)}) collective-permute-start(f32[1,2688]{1,0:T(1,128)S(1)} %get-tuple-element.21), channel_id=1, source_target_pairs={{0,8},{24,16},{7,15},{31,23}} | collective-permute-start | bytes 32264 | tf_op jit(solution)/shard_map/ppermute | solution.py:19
  44.2 13.9 %collective-permute-start.4 = (f32[1,2688]{1,0:T(1,128)S(1)}, f32[1,2688]{1,0:T(1,128)S(1)}, u32[]{:S(2)}, u32[]{:S(2)}) collective-permute-start(f32[1,2688]{1,0:T(1,128)S(1)} %get-tuple-element.21), channel_id=1, source_target_pairs={{14,8},{22,16},{9,15},{17,23}} | collective-permute-start | bytes 32264 | tf_op jit(solution)/shard_map/ppermute | solution.py:19
  44.9 19.5 %collective-permute-start.5 = (f32[1,2688]{1,0:T(1,128)S(1)}, f32[1,2688]{1,0:T(1,128)S(1)}, u32[]{:S(2)}, u32[]{:S(2)}) collective-permute-start(f32[1,2688]{1,0:T(1,128)S(1)} %get-tuple-element.21), channel_id=1, source_target_pairs={{12,8},{20,16},{11,15},{19,23}} | collective-permute-start | bytes 32264 | tf_op jit(solution)/shard_map/ppermute | solution.py:19
  45.6 18.9 %collective-permute-start.6 = (f32[1,2688]{1,0:T(1,128)S(1)}, f32[1,2688]{1,0:T(1,128)S(1)}, u32[]{:S(2)}, u32[]{:S(2)}) collective-permute-start(f32[1,2688]{1,0:T(1,128)S(1)} %get-tuple-element.21), channel_id=1, source_target_pairs={{10,8},{18,16},{13,15},{21,23}} | collective-permute-start | bytes 32264 | tf_op jit(solution)/shard_map/ppermute | solution.py:19
  46.2 18.2 %collective-permute-start.7 = (f32[1,2688]{1,0:T(1,128)S(1)}, f32[1,2688]{1,0:T(1,128)S(1)}, u32[]{:S(2)}, u32[]{:S(2)}) collective-permute-start(f32[1,2688]{1,0:T(1,128)S(1)} %get-tuple-element.22), channel_id=1, source_target_pairs={{22,8},{14,16},{17,15},{9,23}} | collective-permute-start | bytes 32264 | tf_op jit(solution)/shard_map/ppermute | solution.py:19
  51.7 12.8 %collective-permute-start.8 = (f32[1,2688]{1,0:T(1,128)S(1)}, f32[1,2688]{1,0:T(1,128)S(1)}, u32[]{:S(2)}, u32[]{:S(2)}) collective-permute-start(f32[1,2688]{1,0:T(1,128)S(1)} %get-tuple-element.22), channel_id=1, source_target_pairs={{20,8},{12,16},{19,15},{11,23}} | collective-permute-start | bytes 32264 | tf_op jit(solution)/shard_map/ppermute | solution.py:19
  67.8 11.3 %collective-permute-start.18 = (bf16[1,2560]{1,0:T(2,128)(2,1)S(1)}, bf16[1,2560]{1,0:T(2,128)(2,1)S(1)}, u32[]{:S(2)}, u32[]{:S(2)}) collective-permute-start(bf16[1,2560]{1,0:T(2,128)(2,1)S(1)} %pad_maximum_fusion.1), channel_id=1, source_target_pairs={{8,0},{16,24},{15,7},{23,31}} | collective-permute-start | bytes 15368 | tf_op jit(solution)/shard_map/ppermute | solution.py:19
  81.6 10.1 %collective-permute-start.22 = (f32[1,2560]{1,0:T(1,128)S(1)}, f32[1,2560]{1,0:T(1,128)S(1)}, u32[]{:S(2)}, u32[]{:S(2)}) collective-permute-start(f32[1,2560]{1,0:T(1,128)S(1)} %pad_maximum_fusion.2), channel_id=1, source_target_pairs={{6,8},{30,16},{1,15},{25,23}} | collective-permute-start | bytes 30728 | tf_op jit(solution)/shard_map/ppermute | solution.py:19
  82.3 10.1 %collective-permute-start.23 = (f32[1,2560]{1,0:T(1,128)S(1)}, f32[1,2560]{1,0:T(1,128)S(1)}, u32[]{:S(2)}, u32[]{:S(2)}) collective-permute-start(f32[1,2560]{1,0:T(1,128)S(1)} %pad_maximum_fusion.2), channel_id=1, source_target_pairs={{4,8},{28,16},{3,15},{27,23}} | collective-permute-start | bytes 30728 | tf_op jit(solution)/shard_map/ppermute | solution.py:19
  83.0 15.6 %collective-permute-start.24 = (f32[1,2560]{1,0:T(1,128)S(1)}, f32[1,2560]{1,0:T(1,128)S(1)}, u32[]{:S(2)}, u32[]{:S(2)}) collective-permute-start(f32[1,2560]{1,0:T(1,128)S(1)} %pad_maximum_fusion.2), channel_id=1, source_target_pairs={{2,8},{26,16},{5,15},{29,23}} | collective-permute-start | bytes 30728 | tf_op jit(solution)/shard_map/ppermute | solution.py:19
  83.7 14.9 %collective-permute-start.25 = (f32[1,2560]{1,0:T(1,128)S(1)}, f32[1,2560]{1,0:T(1,128)S(1)}, u32[]{:S(2)}, u32[]{:S(2)}) collective-permute-start(f32[1,2560]{1,0:T(1,128)S(1)} %pad_maximum_fusion.2), channel_id=1, source_target_pairs={{0,8},{24,16},{7,15},{31,23}} | collective-permute-start | bytes 30728 | tf_op jit(solution)/shard_map/ppermute | solution.py:19
  108.1 10.8 %collective-permute-start.32 = (bf16[1,2688]{1,0:T(2,128)(2,1)S(1)}, bf16[1,2688]{1,0:T(2,128)(2,1)S(1)}, u32[]{:S(2)}, u32[]{:S(2)}) collective-permute-start(bf16[1,2688]{1,0:T(2,128)(2,1)S(1)} %fusion.46), channel_id=1, source_target_pairs={{8,0},{16,24},{15,7},{23,31}} | collective-permute-start | bytes 16136 | tf_op jit(solution)/shard_map/ppermute | solution.py:19
  109.4 15.8 %collective-permute-start.33 = (bf16[1,2688]{1,0:T(2,128)(2,1)S(1)}, bf16[1,2688]{1,0:T(2,128)(2,1)S(1)}, u32[]{:S(2)}, u32[]{:S(2)}) collective-permute-start(bf16[1,2688]{1,0:T(2,128)(2,1)S(1)} %fusion.46), channel_id=1, source_target_pairs={{8,14},{16,22},{15,9},{23,17}} | collective-permute-start | bytes 16136 | tf_op jit(solution)/shard_map/ppermute | solution.py:19
  110.1 21.5 %collective-permute-start.34 = (bf16[1,2688]{1,0:T(2,128)(2,1)S(1)}, bf16[1,2688]{1,0:T(2,128)(2,1)S(1)}, u32[]{:S(2)}, u32[]{:S(2)}) collective-permute-start(bf16[1,2688]{1,0:T(2,128)(2,1)S(1)} %fusion.46), channel_id=1, source_target_pairs={{8,12},{16,20},{15,11},{23,19}} | collective-permute-start | bytes 16136 | tf_op jit(solution)/shard_map/ppermute | solution.py:19
  110.8 21.5 %collective-permute-start.35 = (bf16[1,2688]{1,0:T(2,128)(2,1)S(1)}, bf16[1,2688]{1,0:T(2,128)(2,1)S(1)}, u32[]{:S(2)}, u32[]{:S(2)}) collective-permute-start(bf16[1,2688]{1,0:T(2,128)(2,1)S(1)} %fusion.46), channel_id=1, source_target_pairs={{8,10},{16,18},{15,13},{23,21}} | collective-permute-start | bytes 16136 | tf_op jit(solution)/shard_map/ppermute | solution.py:19
  111.5 28.2 %collective-permute-start.36 = (bf16[1,2688]{1,0:T(2,128)(2,1)S(1)}, bf16[1,2688]{1,0:T(2,128)(2,1)S(1)}, u32[]{:S(2)}, u32[]{:S(2)}) collective-permute-start(bf16[1,2688]{1,0:T(2,128)(2,1)S(1)} %fusion.46), channel_id=1, source_target_pairs={{8,22},{16,14},{15,17},{23,9}} | collective-permute-start | bytes 16136 | tf_op jit(solution)/shard_map/ppermute | solution.py:19
  118.9 27.1 %collective-permute-start.37 = (bf16[1,2688]{1,0:T(2,128)(2,1)S(1)}, bf16[1,2688]{1,0:T(2,128)(2,1)S(1)}, u32[]{:S(2)}, u32[]{:S(2)}) collective-permute-start(bf16[1,2688]{1,0:T(2,128)(2,1)S(1)} %fusion.46), channel_id=1, source_target_pairs={{8,20},{16,12},{15,19},{23,11}} | collective-permute-start | bytes 16136 | tf_op jit(solution)/shard_map/ppermute | solution.py:19
  125.2 27.1 %collective-permute-start.38 = (bf16[1,2688]{1,0:T(2,128)(2,1)S(1)}, bf16[1,2688]{1,0:T(2,128)(2,1)S(1)}, u32[]{:S(2)}, u32[]{:S(2)}) collective-permute-start(bf16[1,2688]{1,0:T(2,128)(2,1)S(1)} %fusion.46), channel_id=1, source_target_pairs={{8,18},{16,10},{15,21},{23,13}} | collective-permute-start | bytes 16136 | tf_op jit(solution)/shard_map/ppermute | solution.py:19
  131.6 27.8 %collective-permute-start.39 = (bf16[1,2688]{1,0:T(2,128)(2,1)S(1)}, bf16[1,2688]{1,0:T(2,128)(2,1)S(1)}, u32[]{:S(2)}, u32[]{:S(2)}) collective-permute-start(bf16[1,2688]{1,0:T(2,128)(2,1)S(1)} %fusion.46), channel_id=1, source_target_pairs={{8,16},{16,8},{15,23},{23,15}} | collective-permute-start | bytes 16136 | tf_op jit(solution)/shard_map/ppermute | solution.py:19
  132.3 27.2 %collective-permute-start.40 = (bf16[1,2688]{1,0:T(2,128)(2,1)S(1)}, bf16[1,2688]{1,0:T(2,128)(2,1)S(1)}, u32[]{:S(2)}, u32[]{:S(2)}) collective-permute-start(bf16[1,2688]{1,0:T(2,128)(2,1)S(1)} %fusion.46), channel_id=1, source_target_pairs={{8,30},{16,6},{15,25},{23,1}} | collective-permute-start | bytes 16136 | tf_op jit(solution)/shard_map/ppermute | solution.py:19
  139.6 19.8 %collective-permute-start.41 = (bf16[1,2688]{1,0:T(2,128)(2,1)S(1)}, bf16[1,2688]{1,0:T(2,128)(2,1)S(1)}, u32[]{:S(2)}, u32[]{:S(2)}) collective-permute-start(bf16[1,2688]{1,0:T(2,128)(2,1)S(1)} %fusion.46), channel_id=1, source_target_pairs={{8,28},{16,4},{15,27},{23,3}} | collective-permute-start | bytes 16136 | tf_op jit(solution)/shard_map/ppermute | solution.py:19
  146.0 13.5 %collective-permute-start.42 = (bf16[1,2688]{1,0:T(2,128)(2,1)S(1)}, bf16[1,2688]{1,0:T(2,128)(2,1)S(1)}, u32[]{:S(2)}, u32[]{:S(2)}) collective-permute-start(bf16[1,2688]{1,0:T(2,128)(2,1)S(1)} %fusion.46), channel_id=1, source_target_pairs={{8,26},{16,2},{15,29},{23,5}} | collective-permute-start | bytes 16136 | tf_op jit(solution)/shard_map/ppermute | solution.py:19
  152.4 11.4 %collective-permute-start.43 = (bf16[1,2688]{1,0:T(2,128)(2,1)S(1)}, bf16[1,2688]{1,0:T(2,128)(2,1)S(1)}, u32[]{:S(2)}, u32[]{:S(2)}) collective-permute-start(bf16[1,2688]{1,0:T(2,128)(2,1)S(1)} %fusion.46), channel_id=1, source_target_pairs={{8,24},{16,0},{15,31},{23,7}} | collective-permute-start | bytes 16136 | tf_op jit(solution)/shard_map/ppermute | solution.py:19
  173.3 13.0 %collective-permute-start.49 = (f32[1,2560]{1,0:T(1,128)S(1)}, f32[1,2560]{1,0:T(1,128)S(1)}, u32[]{:S(2)}, u32[]{:S(2)}) collective-permute-start(f32[1,2560]{1,0:T(1,128)S(1)} %add.353), channel_id=1, source_target_pairs={{7,15}} | collective-permute-start | bytes 30728 | tf_op jit(solution)/shard_map/ppermute | solution.py:19
  174.0 19.1 %collective-permute-start.50 = (f32[1,2560]{1,0:T(1,128)S(1)}, f32[1,2560]{1,0:T(1,128)S(1)}, u32[]{:S(2)}, u32[]{:S(2)}) collective-permute-start(f32[1,2560]{1,0:T(1,128)S(1)} %add.353), channel_id=1, source_target_pairs={{5,15}} | collective-permute-start | bytes 30728 | tf_op jit(solution)/shard_map/ppermute | solution.py:19
  175.4 26.1 %collective-permute-start.51 = (f32[1,2560]{1,0:T(1,128)S(1)}, f32[1,2560]{1,0:T(1,128)S(1)}, u32[]{:S(2)}, u32[]{:S(2)}) collective-permute-start(f32[1,2560]{1,0:T(1,128)S(1)} %add.353), channel_id=1, source_target_pairs={{3,15}} | collective-permute-start | bytes 30728 | tf_op jit(solution)/shard_map/ppermute | solution.py:19
  176.1 31.8 %collective-permute-start.52 = (f32[1,2560]{1,0:T(1,128)S(1)}, f32[1,2560]{1,0:T(1,128)S(1)}, u32[]{:S(2)}, u32[]{:S(2)}) collective-permute-start(f32[1,2560]{1,0:T(1,128)S(1)} %add.353), channel_id=1, source_target_pairs={{1,15}} | collective-permute-start | bytes 30728 | tf_op jit(solution)/shard_map/ppermute | solution.py:19
  176.7 37.5 %collective-permute-start.53 = (f32[1,2560]{1,0:T(1,128)S(1)}, f32[1,2560]{1,0:T(1,128)S(1)}, u32[]{:S(2)}, u32[]{:S(2)}) collective-permute-start(f32[1,2560]{1,0:T(1,128)S(1)} %add.353), channel_id=1, source_target_pairs={{31,15}} | collective-permute-start | bytes 30728 | tf_op jit(solution)/shard_map/ppermute | solution.py:19
  186.3 34.3 %collective-permute-start.54 = (f32[1,2560]{1,0:T(1,128)S(1)}, f32[1,2560]{1,0:T(1,128)S(1)}, u32[]{:S(2)}, u32[]{:S(2)}) collective-permute-start(f32[1,2560]{1,0:T(1,128)S(1)} %add.353), channel_id=1, source_target_pairs={{29,15}} | collective-permute-start | bytes 30728 | tf_op jit(solution)/shard_map/ppermute | solution.py:19
  193.1 33.9 %collective-permute-start.55 = (f32[1,2560]{1,0:T(1,128)S(1)}, f32[1,2560]{1,0:T(1,128)S(1)}, u32[]{:S(2)}, u32[]{:S(2)}) collective-permute-start(f32[1,2560]{1,0:T(1,128)S(1)} %add.353), channel_id=1, source_target_pairs={{27,15}} | collective-permute-start | bytes 30728 | tf_op jit(solution)/shard_map/ppermute | solution.py:19
  201.5 31.8 %collective-permute-start.56 = (f32[1,2560]{1,0:T(1,128)S(1)}, f32[1,2560]{1,0:T(1,128)S(1)}, u32[]{:S(2)}, u32[]{:S(2)}) collective-permute-start(f32[1,2560]{1,0:T(1,128)S(1)} %add.353), channel_id=1, source_target_pairs={{25,15}} | collective-permute-start | bytes 30728 | tf_op jit(solution)/shard_map/ppermute | solution.py:19
  207.9 31.3 %collective-permute-start.57 = (f32[1,2560]{1,0:T(1,128)S(1)}, f32[1,2560]{1,0:T(1,128)S(1)}, u32[]{:S(2)}, u32[]{:S(2)}) collective-permute-start(f32[1,2560]{1,0:T(1,128)S(1)} %add.353), channel_id=1, source_target_pairs={{23,15}} | collective-permute-start | bytes 30728 | tf_op jit(solution)/shard_map/ppermute | solution.py:19
  214.3 24.9 %collective-permute-start.58 = (f32[1,2560]{1,0:T(1,128)S(1)}, f32[1,2560]{1,0:T(1,128)S(1)}, u32[]{:S(2)}, u32[]{:S(2)}) collective-permute-start(f32[1,2560]{1,0:T(1,128)S(1)} %add.353), channel_id=1, source_target_pairs={{21,15}} | collective-permute-start | bytes 30728 | tf_op jit(solution)/shard_map/ppermute | solution.py:19
  220.6 18.5 %collective-permute-start.59 = (f32[1,2560]{1,0:T(1,128)S(1)}, f32[1,2560]{1,0:T(1,128)S(1)}, u32[]{:S(2)}, u32[]{:S(2)}) collective-permute-start(f32[1,2560]{1,0:T(1,128)S(1)} %add.353), channel_id=1, source_target_pairs={{19,15}} | collective-permute-start | bytes 30728 | tf_op jit(solution)/shard_map/ppermute | solution.py:19
  227.0 12.2 %collective-permute-start.60 = (f32[1,2560]{1,0:T(1,128)S(1)}, f32[1,2560]{1,0:T(1,128)S(1)}, u32[]{:S(2)}, u32[]{:S(2)}) collective-permute-start(f32[1,2560]{1,0:T(1,128)S(1)} %add.353), channel_id=1, source_target_pairs={{17,15}} | collective-permute-start | bytes 30728 | tf_op jit(solution)/shard_map/ppermute | solution.py:19
  241.3 13.8 %collective-permute-start.64 = (f32[1,2560]{1,0:T(1,128)S(1)}, f32[1,2560]{1,0:T(1,128)S(1)}, u32[]{:S(2)}, u32[]{:S(2)}) collective-permute-start(f32[1,2560]{1,0:T(1,128)S(1)} %add_add_fusion.3), channel_id=1, source_target_pairs={{15,7}} | collective-permute-start | bytes 30728 | tf_op jit(solution)/shard_map/ppermute | solution.py:19
  242.0 13.8 %collective-permute-start.65 = (f32[1,2560]{1,0:T(1,128)S(1)}, f32[1,2560]{1,0:T(1,128)S(1)}, u32[]{:S(2)}, u32[]{:S(2)}) collective-permute-start(f32[1,2560]{1,0:T(1,128)S(1)} %add_add_fusion.3), channel_id=1, source_target_pairs={{15,5}} | collective-permute-start | bytes 30728 | tf_op jit(solution)/shard_map/ppermute | solution.py:19
  244.2 12.3 %collective-permute-start.66 = (f32[1,2560]{1,0:T(1,128)S(1)}, f32[1,2560]{1,0:T(1,128)S(1)}, u32[]{:S(2)}, u32[]{:S(2)}) collective-permute-start(f32[1,2560]{1,0:T(1,128)S(1)} %add_add_fusion.3), channel_id=1, source_target_pairs={{15,3}} | collective-permute-start | bytes 30728 | tf_op jit(solution)/shard_map/ppermute | solution.py:19
  244.9 12.3 %collective-permute-start.67 = (f32[1,2560]{1,0:T(1,128)S(1)}, f32[1,2560]{1,0:T(1,128)S(1)}, u32[]{:S(2)}, u32[]{:S(2)}) collective-permute-start(f32[1,2560]{1,0:T(1,128)S(1)} %add_add_fusion.3), channel_id=1, source_target_pairs={{15,1}} | collective-permute-start | bytes 30728 | tf_op jit(solution)/shard_map/ppermute | solution.py:19
  245.6 12.3 %collective-permute-start.68 = (f32[1,2560]{1,0:T(1,128)S(1)}, f32[1,2560]{1,0:T(1,128)S(1)}, u32[]{:S(2)}, u32[]{:S(2)}) collective-permute-start(f32[1,2560]{1,0:T(1,128)S(1)} %add_add_fusion.3), channel_id=1, source_target_pairs={{15,31}} | collective-permute-start | bytes 30728 | tf_op jit(solution)/shard_map/ppermute | solution.py:19
  261.7 13.6 %collective-permute-start.76 = (f32[1,2560]{1,0:T(1,128)S(1)}, f32[1,2560]{1,0:T(1,128)S(1)}, u32[]{:S(2)}, u32[]{:S(2)}) collective-permute-start(f32[1,2560]{1,0:T(1,128)S(1)} %add_add_fusion.2), channel_id=1, source_target_pairs={{1,0},{3,2},{5,4},{7,6},{9,8},{11,10},{13,12},{15,14},{17,16},{19,... | collective-permute-start | bytes 30728 | tf_op jit(solution)/shard_map/ppermute | solution.py:19
  (34 other events, 318.8 us)

commit v5 on v2

v5 whole, which is shorter than its diff:
```python
import jax
import jax.numpy as jnp
from jax import lax
from jax.sharding import PartitionSpec as P

epsilon = 1e-06
AXES = ("seq", "dp")


def gelu_slope(pre_act):
    cdf = 0.5 * (1.0 + lax.erf(pre_act * 0.7071067811865476))
    return cdf + pre_act * jnp.exp(-0.5 * pre_act * pre_act) * 0.3989422804014327


def exchange(value, mask):
    clips = lax.axis_size("dp")
    pairs = []
    for place in range(lax.axis_size("seq")):
        for clip in range(clips):
            there = place ^ mask if clip == clips - 1 else place
            pairs.append((place * clips + clip, there * clips + clip))
    return lax.ppermute(value, AXES, pairs)


def hop(value, step):
    return lax.ppermute(value, "dp", [(i, i ^ step) for i in range(lax.axis_size("dp"))])


def of_clips(value):
    clips = lax.axis_size("dp")
    clip = lax.axis_index("dp")
    got = [value] + [hop(value, step) for step in range(1, clips)]
    ordered = []
    for index in range(clips):
        picked = got[0]
        for step in range(1, clips):
            picked = jnp.where(clip ^ step == index, got[step], picked)
        ordered.append(picked)
    return ordered


def rounds(size):
    masks = [1 << bit for bit in range(size.bit_length() - 1)]
    return [masks[i : i + 2] for i in range(0, len(masks), 2)]


def round_masks(pair):
    return pair if len(pair) == 1 else [pair[0], pair[1], pair[0] | pair[1]]


def sum_to_owner(value, group):
    place = lax.axis_index("seq")
    for pair in reversed(rounds(lax.axis_size("seq"))):
        owner_masks = [mask for mask in pair if mask >= group]
        blocks = value.reshape((1 << len(owner_masks), -1) + value.shape[1:])

        def block_for(mask):
            index = 0
            for bit, owner_mask in enumerate(owner_masks):
                index = index + jnp.where((place ^ mask) & owner_mask != 0, 1 << bit, 0)
            return lax.dynamic_index_in_dim(blocks, index, 0, keepdims=False)

        got = [block_for(0)] + [exchange(block_for(mask), mask) for mask in round_masks(pair)]
        value = got[0] + got[1] if len(got) == 2 else (got[0] + got[1]) + (got[2] + got[3])
    return value


def sum_to_all(value, group):
    place = lax.axis_index("seq")
    for pair in rounds(lax.axis_size("seq")):
        terms = {0: value}
        for mask in round_masks(pair):
            terms[mask] = exchange(value, mask)
        for mask in pair:
            upper = (place & mask) != 0
            merged = {}
            for key in terms:
                if key & mask:
                    continue
                near, far = terms[key], terms[key | mask]
                if mask < group:
                    merged[key] = near + far
                else:
                    merged[key] = jnp.where(
                        upper, jnp.concatenate([far, near]), jnp.concatenate([near, far])
                    )
            terms = merged
        value = terms[0]
    return value


def per_device(tokens, cotangent, router, logit_scale, expert_in, expert_out):
    f32, bf16 = jnp.float32, jnp.bfloat16
    tok_in = tokens[0]
    tok_cot = cotangent[0]
    experts = router.shape[1]
    width = router.shape[0]
    size = lax.axis_size("seq")
    group = size // experts
    clips = lax.axis_size("dp")
    clip = lax.axis_index("dp")
    owned = lax.axis_index("seq") // group
    phi_f32 = router.astype(f32)
    phi_scale = lax.rsqrt(jnp.sum(phi_f32 * phi_f32, axis=0, keepdims=True) + epsilon)
    phi_unit = phi_f32 * phi_scale
    phi_norm = phi_unit.astype(bf16)
    tok_f32 = tok_in.astype(f32)
    tok_scale = lax.rsqrt(jnp.sum(tok_f32 * tok_f32, axis=1, keepdims=True) + epsilon)
    tok_unit = tok_f32 * tok_scale
    tok_norm = tok_unit.astype(bf16)
    logits = logit_scale[0] * jnp.dot(tok_norm, phi_norm, preferred_element_type=f32)
    exp_scores = jnp.exp(logits)
    combine_f = exp_scores / jnp.sum(exp_scores, axis=1, keepdims=True)
    combine = combine_f.astype(bf16)
    exp_high = lax.reduce_precision(exp_scores, 8, 7)
    exp_low = (exp_scores - exp_high).astype(bf16)
    exp_high = exp_high.astype(bf16)
    both = jnp.einsum(
        "ns,nd->sd",
        jnp.concatenate([exp_high, exp_low], axis=1),
        tok_in,
        preferred_element_type=f32,
    )
    in_part = both[:experts] + both[experts:]
    cot_part = jnp.einsum("ns,nd->sd", combine, tok_cot, preferred_element_type=f32)
    local_total = jnp.sum(exp_scores, axis=0)
    all_totals = jnp.broadcast_to(local_total[None, :], (experts, experts))
    message = jnp.stack(
        of_clips(jnp.concatenate([in_part, cot_part, all_totals], axis=1)), axis=1
    )
    message = sum_to_owner(message, group)[0]
    totals = message[:, 2 * width :]
    own_total = lax.dynamic_slice_in_dim(totals, owned, 1, 1)
    own_in = message[:, :width] / own_total
    row_x = own_in.astype(bf16)
    row_cot = message[:, width : 2 * width].astype(bf16)
    pre_act = jnp.dot(row_x, expert_in, preferred_element_type=f32)
    hidden = jax.nn.gelu(pre_act, approximate=False).astype(bf16)
    part_out = jnp.dot(hidden, expert_out, preferred_element_type=f32)
    hid_grad = jnp.einsum("od,hd->oh", row_cot, expert_out, preferred_element_type=f32)
    pre_grad = (hid_grad * gelu_slope(pre_act)).astype(bf16)
    part_dx = jnp.einsum("oh,dh->od", pre_grad, expert_in, preferred_element_type=f32)
    dot_part = jnp.sum(own_in * part_dx, axis=1, keepdims=True)
    message = jnp.concatenate([part_out, part_dx, dot_part], axis=1)[None]
    message = sum_to_all(message, group)
    whole_totals = jnp.broadcast_to(totals.T[:, :, None], (experts, clips, 1))
    message = jnp.concatenate([message, whole_totals], axis=2)
    handed = message[:, clips - 1]
    for step in range(1, clips):
        got = hop(message[:, (clips - 1) ^ step], step)
        handed = jnp.where(clip ^ step == clips - 1, got, handed)
    slot_y = handed[:, :width].astype(bf16)
    slot_dx = handed[:, width : 2 * width].astype(bf16)
    column_stat = handed[:, 2 * width : 2 * width + 1].T
    totals = handed[:, 2 * width + 1 :].T
    rows = jnp.concatenate([row_x, row_cot, hidden, pre_grad], axis=1)
    rows, slot_y, slot_dx = lax.optimization_barrier((rows, slot_y, slot_dx))
    all_rows = of_clips(rows)[clips - 1]
    units = expert_in.shape[1]
    all_x, all_cot = all_rows[:, :width], all_rows[:, width : 2 * width]
    all_hidden = all_rows[:, 2 * width : 2 * width + units]
    all_grad = all_rows[:, 2 * width + units :]
    share = width // clips
    mine_x = lax.dynamic_slice_in_dim(all_x, clip * share, share, 1)
    mine_cot = lax.dynamic_slice_in_dim(all_cot, clip * share, share, 1)
    grad_expert_in = jnp.einsum("od,oh->dh", mine_x, all_grad, preferred_element_type=f32)
    grad_expert_out = jnp.einsum("oh,od->hd", all_hidden, mine_cot, preferred_element_type=f32)
    mixed = jnp.dot(combine, slot_y, preferred_element_type=f32).astype(bf16)
    comb_dot = jnp.einsum("nd,sd->ns", tok_cot, slot_y, preferred_element_type=f32)
    grad_comb = combine_f * (comb_dot - jnp.sum(combine_f * comb_dot, axis=1, keepdims=True))
    dispatch_f = exp_scores / totals
    dispatch = dispatch_f.astype(bf16)
    disp_dot = jnp.einsum("nd,sd->ns", tok_in, slot_dx, preferred_element_type=f32)
    grad_disp = dispatch_f * (disp_dot - column_stat)
    score_grad = (logit_scale[0] * (grad_comb + grad_disp)).astype(bf16)
    norm_grad = jnp.einsum("ns,ds->nd", score_grad, phi_norm, preferred_element_type=f32)
    phi_part = jnp.einsum("nd,ns->sd", tok_norm, score_grad, preferred_element_type=f32)
    phi_flat = sum(of_clips(phi_part.reshape(1, 1, -1)))
    phi_flat = sum_to_all(phi_flat, size)
    phi_grad = of_clips(phi_flat)[clips - 1].reshape(experts, width).T
    through = jnp.dot(dispatch, slot_dx, preferred_element_type=f32)
    back_norm = tok_scale * (
        norm_grad - tok_unit * jnp.sum(tok_unit * norm_grad, axis=1, keepdims=True)
    )
    grad_tokens = (through + back_norm).astype(bf16)
    grad_router = phi_scale * (
        phi_grad - phi_unit * jnp.sum(phi_unit * phi_grad, axis=0, keepdims=True)
    )
    return (mixed[None], grad_tokens[None], grad_expert_in, grad_expert_out, grad_router)


def solution(mesh):
    return jax.shard_map(
        per_device,
        mesh=mesh,
        in_specs=(
            P("dp", "seq", None),
            P("dp", "seq", None),
            P(),
            P(),
            P(None, "seq"),
            P("seq", None),
        ),
        out_specs=(P("dp", "seq", None), P("dp", "seq", None), P("dp", "seq"), P("seq", "dp"), P()),
        check_vma=False,
    )
```

time: 70.9 us -> 97.3 us (1.37)
  starting transfers between devices: 17.1 us -> 71.1 us
  waiting for transfers between devices: 23.4 us -> 1.73 us
  matrix products: 19.7 us -> 16 us
  local copies, waits for them, and re-layouts: 3.5 us -> 1.37 us
    ppermute x1 -> x23, starting transfers between devices: 0.07 us -> 71.1 us  [the longest x5 59.2 us: hop(): lax.ppermute(value, 'dp', [(i, i ^ step) for i in range(lax.axis_size('dp...]
    all_to_all x4 -> x0, waiting for transfers between devices: 23.4 us -> none  [to_each(): return lax.all_to_all(value, axis, split_axis=0, concat_axis=0)]
    all_to_all x4 -> x0, starting transfers between devices: 17 us -> none  [to_each(): return lax.all_to_all(value, axis, split_axis=0, concat_axis=0)]
    broadcast_in_dim x3 -> x4, local copies, waits for them, and re-layouts: 1.99 us -> 0.21 us  [the longest x2 0.1 us: per_device(): whole_totals = jnp.broadcast_to(totals.T[:, :, None], (experts, clips, 1))]
    ppermute x1 -> x23, waiting for transfers between devices: 0.01 us -> 1.73 us  [the longest x5 1.68 us: hop(): lax.ppermute(value, 'dp', [(i, i ^ step) for i in range(lax.axis_size('dp...]
    dot_general x1, matrix products: 3.73 us -> 2.06 us  [per_device(): through = jnp.dot(dispatch, slot_dx, preferred_element_type=f32)]
    dot_general x1, matrix products: 0.32 us -> 1.76 us  [per_device(): part_out = jnp.dot(hidden, expert_out, preferred_element_type=f32)]
    dot_general x1, matrix products: 1.96 us -> 0.53 us  [per_device(): jnp.einsum('od,hd->oh', row_cot, expert_out, preferred_element_type=f32)]
  transfers between devices with their start and end apart: 5 -> 23, of which waited for: 4 -> 2; matrix products, arithmetic and copies ran while one was open for 16% -> 8% of each run, Pallas kernels for 0% -> 0%
where the time goes in v5:
time: 97.3 us; the launch traced here: 96.6 us
  starting transfers between devices  71.1 us (73%)
  matrix products  16 us (16%)
  other arithmetic  4.52 us (5%)
  between operations  1.84 us (2%)
  waiting for transfers between devices  1.73 us (2%)
  local copies, waits for them, and re-layouts  1.37 us (1%)
    ppermute x5, starting transfers between devices, hop(): lax.ppermute(value, 'dp', [(i, i ^ step) for i in range(lax.axis_size('dp...  59.2 us
    ppermute x18, starting transfers between devices, exchange(): return lax.ppermute(value, AXES, pairs)  11.9 us
    dot_general x1, matrix products, per_device(): through = jnp.dot(dispatch, slot_dx, preferred_element_type=f32)  2.06 us
    dot_general x1, matrix products, per_device(): jnp.dot(tok_norm, phi_norm, preferred_element_type=f32)  1.97 us
  transfers between devices with their start and end apart: 23, of which 2 were waited for; matrix products, arithmetic and copies ran while one was open for 8% of the time, Pallas kernels for 0%

profile of v5, /device:TPU:0, one launch (start us, length us, event | category | flops | bytes accessed | tf_op | source)
XLA Modules:
  0.0 96.6 jit_solution(10968849740726703502)
XLA Ops:
  0.7 1.8 %fusion.9 = f32[512]{0:T(512)S(1)} fusion(bf16[1,512,1280]{2,1,0:T(8,128)(2,1)} %param.6), kind=kLoop, calls=%fused_computation.13 | loop fusion | flops 1965568 | bytes 1312768 | tf_op jit(solution)/shard_map/reduce_sum | solution.py:108
  2.5 0.9 fusion.41
  4.1 2.0 %fusion.78 = (f32[2]{0:T(128)S(1)}, f32[512]{0:T(512)S(1)}, bf16[512,2]{0,1:T(2,128)(2,1)S(1)}, bf16[512,2]{0,1:T(2,128)(2,1)S(1)}, f32[512,2]{0,1:T(2,128)S(1)}) fusion(bf16[1280,2]{0,1:T(2,128)(2,1)} %param.8, f32[2]{0:T(128)S(1)} %add_rsqrt_fusion.1, bf16[1,512,1280]{2,1,0:T(8,128)(2,1)} %param.6, f32[512]{0:T(512)S(1)} %add_rsqrt_fusion, f32[]{:T(128)} %bitcast.74), kind=kOutput, calls=%fused_computation.131 | convolution fusion | flops 4601854 | bytes 1328148 | tf_op jit(solution)/shard_map/dot_general | solution.py:111
  6.0 0.3 fusion.16
  6.4 0.3 fusion.12
  6.7 0.5 collective-permute-start
  7.2 0.8 collective-permute-done
  8.1 0.7 collective-permute-start.1
  8.8 0.7 collective-permute-start.2
  9.5 0.7 collective-permute-start.3
  10.3 0.7 collective-permute-start.4
  10.9 0.7 collective-permute-start.5
  11.6 0.7 collective-permute-start.6
  12.4 0.2 fusion.72
  12.7 0.4 fusion.50
  13.0 0.7 copy-done.2
  13.7 0.5 fusion.22
  14.3 0.5 fusion.86
  14.8 0.1 multiply_reduce_fusion
  15.0 1.8 %fusion.85 = f32[2,1280]{1,0:T(2,128)S(1)} fusion(bf16[2,640]{1,0:T(2,128)(2,1)S(1)} %get-tuple-element.33, bf16[640,1280]{1,0:T(8,128)(2,1)} %param.11), kind=kOutput, calls=%fused_computation.137 | convolution fusion | flops 3276800 | bytes 1651200 | tf_op jit(solution)/shard_map/dot_general | solution.py:139
  16.9 0.7 collective-permute-start.7
  17.5 0.7 collective-permute-start.8
  18.2 0.7 collective-permute-start.9
  18.9 0.7 collective-permute-start.12
  19.6 0.7 collective-permute-start.10
  20.3 0.7 collective-permute-start.11
  21.3 38.2 %collective-permute-start.13 = (f32[2,2562]{1,0:T(2,128)S(1)}, f32[2,2562]{1,0:T(2,128)S(1)}, u32[]{:S(2)}, u32[]{:S(2)}) collective-permute-start(f32[2,2562]{1,0:T(2,128)S(1)} %fusion.27), channel_id=1, source_target_pairs={{0,1},{1,0},{2,3},{3,2},{4,5},{5,4},{6,7},{7,6},{8,9},{9,8},{10,11... | collective-permute-start | bytes 61496 | tf_op jit(solution)/shard_map/ppermute | solution.py:26
  59.5 0.8 collective-permute-done.13
  60.5 1.8 %multiply_reduce_fusion.1 = (f32[512]{0:T(512)S(1)}, f32[512,2]{0,1:T(2,128)S(1)}) fusion(f32[512,2]{0,1:T(2,128)S(1)} %get-tuple-element.32, f32[512]{0:T(512)S(1)} %get-tuple-element.14, bf16[2,1280]{1,0:T(2,128)(2,1)S(1)} %get-tuple-element.8, bf16[1,512,1280]{2,1,0:T(8,128)(2,1)} %param.7), kind=kOutput, calls=%fused_computation.106 | convolution fusion | flops 2624000 | bytes 1328128 | tf_op jit(solution)/shard_map/nd,sd->ns/dot_general | solution.py:169
  62.3 0.4 fusion.14
  62.7 0.2 slice_reduce_fusion.1
  62.9 0.4 fusion.23
  63.4 0.4 collective-permute-start.15
  63.8 0.8 fusion.6
  64.6 2.1 %fusion.4 = bf16[1,512,1280]{2,1,0:T(8,128)(2,1)} fusion(bf16[2,1280]{1,0:T(2,128)(2,1)S(1)} %get-tuple-element.9, f32[512,1280]{1,0:T(8,128)S(1)} %get-tuple-element.38, bf16[1,512,1280]{2,1,0:T(8,128)(2,1)S(1)} %copy-done.1, f32[512]{0:T(512)S(1)} %get-tuple-element.37, f32[512]{0:T(512)S(1)} %add_rsqrt_fusion, f32[512,2]{0,1:T(2,128)S(1)} %get-tuple-element.32, ...), kind=kOutput, calls=%fused_computation.8 | convolution fusion | flops 7211008 | bytes 5256200 | tf_op jit(solution)/shard_map/dot_general | solution.py:181
  66.6 1.6 %fusion.5 = bf16[1,512,1280]{2,1,0:T(8,128)(2,1)} fusion(bf16[2,1280]{1,0:T(2,128)(2,1)S(1)} %get-tuple-element.8, f32[512,2]{0,1:T(2,128)S(1)} %get-tuple-element.32, f32[512]{0:T(512)S(1)} %get-tuple-element.14), kind=kOutput, calls=%fused_computation.9 | convolution fusion | flops 3278848 | bytes 1321984 | tf_op jit(solution)/shard_map/dot_general | solution.py:168
  68.2 0.2 collective-permute-start.14
  68.4 0.7 collective-permute-start.16
  69.1 0.7 collective-permute-start.17
  69.8 0.7 collective-permute-start.18
  70.6 0.7 collective-permute-start.19
  71.2 0.7 collective-permute-start.20
  71.9 0.7 collective-permute-start.21
  72.6 1.6 %fusion.60 = f32[640,640]{1,0:T(8,128)} fusion(bf16[2,1280]{1,0:T(2,128)(2,1)S(1)} %get-tuple-element.27, s32[]{:T(128)S(6)} %select_n.102, bf16[2,3840]{1,0:T(2,128)(2,1)S(1)} %broadcast_select_fusion), kind=kOutput, calls=%fused_computation.110 | convolution fusion | flops 1638400 | bytes 1643524 | tf_op jit(solution)/shard_map/od,oh->dh/dot_general | solution.py:166
  74.2 19.9 %collective-permute-start.22 = (f32[1,1,2560]{2,1,0:T(1,128)S(1)}, f32[1,1,2560]{2,1,0:T(1,128)S(1)}, u32[]{:S(2)}, u32[]{:S(2)}) collective-permute-start(f32[1,1,2560]{2,1,0:T(1,128)S(1)} %add_add_fusion.3), channel_id=1, source_target_pairs={{0,1},{1,0},{2,3},{3,2},{4,5},{5,4},{6,7},{7,6},{8,9},{9,8},{10,11... | collective-permute-start | bytes 30728 | tf_op jit(solution)/shard_map/ppermute | solution.py:26
  94.1 1.6 %fusion.61 = f32[640,640]{1,0:T(8,128)} fusion(bf16[2,1280]{1,0:T(2,128)(2,1)S(1)} %get-tuple-element.26, s32[]{:T(128)S(6)} %select_n.102, bf16[2,3840]{1,0:T(2,128)(2,1)S(1)} %broadcast_select_fusion), kind=kOutput, calls=%fused_computation.111 | convolution fusion | flops 1638400 | bytes 1643524 | tf_op jit(solution)/shard_map/oh,od->hd/dot_general | solution.py:167
  95.7 0.2 fusion.38
  95.9 0.7 fusion.40
  (63 shorter events, 1.2 us)
Async XLA Ops:
  0.6 12.0 %copy-start = (bf16[1280,640]{1,0:T(8,128)(2,1)S(1)}, bf16[1280,640]{1,0:T(8,128)(2,1)}, u32[]{:S(2)}) copy-start(bf16[1280,640]{1,0:T(8,128)(2,1)} %param.10) | copy-start | bytes 4915204
  0.6 5.4 %copy-start.1 = (bf16[1,512,1280]{2,1,0:T(8,128)(2,1)S(1)}, bf16[1,512,1280]{2,1,0:T(8,128)(2,1)}, u32[]{:S(2)}) copy-start(bf16[1,512,1280]{2,1,0:T(8,128)(2,1)} %param.6) | copy-start | bytes 3932164
  2.5 3.9 %copy-start.3 = (bf16[1,512,1280]{2,1,0:T(8,128)(2,1)S(1)}, bf16[1,512,1280]{2,1,0:T(8,128)(2,1)}, u32[]{:S(2)}) copy-start(bf16[1,512,1280]{2,1,0:T(8,128)(2,1)} %param.7) | copy-start | bytes 3932164
  6.7 1.4 %collective-permute-start = (f32[2,2562]{1,0:T(2,128)S(1)}, f32[2,2562]{1,0:T(2,128)S(1)}, u32[]{:S(2)}, u32[]{:S(2)}) collective-permute-start(f32[2,2562]{1,0:T(2,128)S(1)} %maximum_maximum_fusion), channel_id=1, source_target_pairs={{0,1},{1,0},{2,3},{3,2},{4,5},{5,4},{6,7},{7,6},{8,9},{9,8},{10,11... | collective-permute-start | bytes 61496 | tf_op jit(solution)/shard_map/ppermute | solution.py:26
  8.1 2.0 %collective-permute-start.1 = (f32[1,2,2562]{2,0,1:T(1,128)S(1)}, f32[1,2,2562]{2,0,1:T(1,128)S(1)}, u32[]{:S(2)}, u32[]{:S(2)}) collective-permute-start(f32[1,2,2562]{2,0,1:T(1,128)S(1)} %get-tuple-element.19), channel_id=1, source_target_pairs={{0,0},{1,9},{2,2},{3,11},{4,4},{5,13},{6,6},{7,15},{8,8},{9,1},{10... | collective-permute-start | bytes 61496 | tf_op jit(solution)/shard_map/ppermute | solution.py:22
  8.8 1.4 %collective-permute-start.2 = (f32[1,2,2562]{2,0,1:T(1,128)S(1)}, f32[1,2,2562]{2,0,1:T(1,128)S(1)}, u32[]{:S(2)}, u32[]{:S(2)}) collective-permute-start(f32[1,2,2562]{2,0,1:T(1,128)S(1)} %get-tuple-element.20), channel_id=1, source_target_pairs={{0,0},{1,17},{2,2},{3,19},{4,4},{5,21},{6,6},{7,23},{8,8},{9,25},{... | collective-permute-start | bytes 61496 | tf_op jit(solution)/shard_map/ppermute | solution.py:22
  9.5 0.7 collective-permute-start.3
  10.3 2.0 %collective-permute-start.4 = (f32[1,2,2562]{2,0,1:T(1,128)S(1)}, f32[1,2,2562]{2,0,1:T(1,128)S(1)}, u32[]{:S(2)}, u32[]{:S(2)}) collective-permute-start(f32[1,2,2562]{2,0,1:T(1,128)S(1)} %add_add_fusion.2), channel_id=1, source_target_pairs={{0,0},{1,3},{2,2},{3,1},{4,4},{5,7},{6,6},{7,5},{8,8},{9,11},{10,1... | collective-permute-start | bytes 61496 | tf_op jit(solution)/shard_map/ppermute | solution.py:22
  10.9 1.4 %collective-permute-start.5 = (f32[1,2,2562]{2,0,1:T(1,128)S(1)}, f32[1,2,2562]{2,0,1:T(1,128)S(1)}, u32[]{:S(2)}, u32[]{:S(2)}) collective-permute-start(f32[1,2,2562]{2,0,1:T(1,128)S(1)} %add_add_fusion.2), channel_id=1, source_target_pairs={{0,0},{1,5},{2,2},{3,7},{4,4},{5,1},{6,6},{7,3},{8,8},{9,13},{10,1... | collective-permute-start | bytes 61496 | tf_op jit(solution)/shard_map/ppermute | solution.py:22
  11.6 0.7 collective-permute-start.6
  12.3 1.4 %copy-start.2 = (bf16[640,1280]{1,0:T(8,128)(2,1)S(1)}, bf16[640,1280]{1,0:T(8,128)(2,1)}, u32[]{:S(2)}) copy-start(bf16[640,1280]{1,0:T(8,128)(2,1)} %param.11) | copy-start | bytes 4915204
  16.9 2.0 %collective-permute-start.7 = (f32[1,2,2561]{2,0,1:T(1,128)S(1)}, f32[1,2,2561]{2,0,1:T(1,128)S(1)}, u32[]{:S(2)}, u32[]{:S(2)}) collective-permute-start(f32[1,2,2561]{2,0,1:T(1,128)S(1)} %broadcast_in_dim.14), channel_id=1, source_target_pairs={{0,0},{1,3},{2,2},{3,1},{4,4},{5,7},{6,6},{7,5},{8,8},{9,11},{10,1... | collective-permute-start | bytes 61472 | tf_op jit(solution)/shard_map/ppermute | solution.py:22
  17.5 1.4 %collective-permute-start.8 = (f32[1,2,2561]{2,0,1:T(1,128)S(1)}, f32[1,2,2561]{2,0,1:T(1,128)S(1)}, u32[]{:S(2)}, u32[]{:S(2)}) collective-permute-start(f32[1,2,2561]{2,0,1:T(1,128)S(1)} %broadcast_in_dim.14), channel_id=1, source_target_pairs={{0,0},{1,5},{2,2},{3,7},{4,4},{5,1},{6,6},{7,3},{8,8},{9,13},{10,1... | collective-permute-start | bytes 61472 | tf_op jit(solution)/shard_map/ppermute | solution.py:22
  18.2 0.7 collective-permute-start.9
  18.9 2.1 %collective-permute-start.12 = (f32[1,2,2561]{2,0,1:T(1,128)S(1)}, f32[1,2,2561]{2,0,1:T(1,128)S(1)}, u32[]{:S(2)}, u32[]{:S(2)}) collective-permute-start(f32[1,2,2561]{2,0,1:T(1,128)S(1)} %add_add_fusion), channel_id=1, source_target_pairs={{0,0},{1,9},{2,2},{3,11},{4,4},{5,13},{6,6},{7,15},{8,8},{9,1},{10... | collective-permute-start | bytes 61472 | tf_op jit(solution)/shard_map/ppermute | solution.py:22
  19.6 1.5 %collective-permute-start.10 = (f32[1,2,2561]{2,0,1:T(1,128)S(1)}, f32[1,2,2561]{2,0,1:T(1,128)S(1)}, u32[]{:S(2)}, u32[]{:S(2)}) collective-permute-start(f32[1,2,2561]{2,0,1:T(1,128)S(1)} %add_add_fusion), channel_id=1, source_target_pairs={{0,0},{1,17},{2,2},{3,19},{4,4},{5,21},{6,6},{7,23},{8,8},{9,25},{... | collective-permute-start | bytes 61472 | tf_op jit(solution)/shard_map/ppermute | solution.py:22
  20.3 0.8 collective-permute-start.11
  21.3 39.0 %collective-permute-start.13 = (f32[2,2562]{1,0:T(2,128)S(1)}, f32[2,2562]{1,0:T(2,128)S(1)}, u32[]{:S(2)}, u32[]{:S(2)}) collective-permute-start(f32[2,2562]{1,0:T(2,128)S(1)} %fusion.27), channel_id=1, source_target_pairs={{0,1},{1,0},{2,3},{3,2},{4,5},{5,4},{6,7},{7,6},{8,9},{9,8},{10,11... | collective-permute-start | bytes 61496 | tf_op jit(solution)/shard_map/ppermute | solution.py:26
  62.2 1.5 %copy-start.4 = (bf16[1280,2]{0,1:T(2,128)(2,1)S(1)}, bf16[1280,2]{0,1:T(2,128)(2,1)}, u32[]{:S(2)}) copy-start(bf16[1280,2]{0,1:T(2,128)(2,1)} %param.8) | copy-start | bytes 15364
  63.4 5.1 %collective-permute-start.15 = (f32[1,1,2560]{2,1,0:T(1,128)S(1)}, f32[1,1,2560]{2,1,0:T(1,128)S(1)}, u32[]{:S(2)}, u32[]{:S(2)}) collective-permute-start(f32[1,1,2560]{2,1,0:T(1,128)S(1)} %reshape.47), channel_id=1, source_target_pairs={{0,1},{1,0},{2,3},{3,2},{4,5},{5,4},{6,7},{7,6},{8,9},{9,8},{10,11... | collective-permute-start | bytes 30728 | tf_op jit(solution)/shard_map/ppermute | solution.py:26
  68.2 2.2 %collective-permute-start.14 = (bf16[2,3840]{1,0:T(2,128)(2,1)S(1)}, bf16[2,3840]{1,0:T(2,128)(2,1)S(1)}, u32[]{:S(2)}, u32[]{:S(2)}) collective-permute-start(bf16[2,3840]{1,0:T(2,128)(2,1)S(1)} %pad_maximum_fusion.2), channel_id=1, source_target_pairs={{0,1},{1,0},{2,3},{3,2},{4,5},{5,4},{6,7},{7,6},{8,9},{9,8},{10,11... | collective-permute-start | bytes 46088 | tf_op jit(solution)/shard_map/ppermute | solution.py:26
  68.4 2.1 %collective-permute-start.16 = (f32[1,1,2560]{2,1,0:T(1,128)S(1)}, f32[1,1,2560]{2,1,0:T(1,128)S(1)}, u32[]{:S(2)}, u32[]{:S(2)}) collective-permute-start(f32[1,1,2560]{2,1,0:T(1,128)S(1)} %fusion.42), channel_id=1, source_target_pairs={{0,0},{1,3},{2,2},{3,1},{4,4},{5,7},{6,6},{7,5},{8,8},{9,11},{10,1... | collective-permute-start | bytes 30728 | tf_op jit(solution)/shard_map/ppermute | solution.py:22
  69.1 1.4 %collective-permute-start.17 = (f32[1,1,2560]{2,1,0:T(1,128)S(1)}, f32[1,1,2560]{2,1,0:T(1,128)S(1)}, u32[]{:S(2)}, u32[]{:S(2)}) collective-permute-start(f32[1,1,2560]{2,1,0:T(1,128)S(1)} %fusion.42), channel_id=1, source_target_pairs={{0,0},{1,5},{2,2},{3,7},{4,4},{5,1},{6,6},{7,3},{8,8},{9,13},{10,1... | collective-permute-start | bytes 30728 | tf_op jit(solution)/shard_map/ppermute | solution.py:22
  69.8 0.8 collective-permute-start.18
  70.6 3.6 %collective-permute-start.19 = (f32[1,1,2560]{2,1,0:T(1,128)S(1)}, f32[1,1,2560]{2,1,0:T(1,128)S(1)}, u32[]{:S(2)}, u32[]{:S(2)}) collective-permute-start(f32[1,1,2560]{2,1,0:T(1,128)S(1)} %add_add_fusion.4), channel_id=1, source_target_pairs={{0,0},{1,9},{2,2},{3,11},{4,4},{5,13},{6,6},{7,15},{8,8},{9,1},{10... | collective-permute-start | bytes 30728 | tf_op jit(solution)/shard_map/ppermute | solution.py:22
  71.2 2.9 %collective-permute-start.20 = (f32[1,1,2560]{2,1,0:T(1,128)S(1)}, f32[1,1,2560]{2,1,0:T(1,128)S(1)}, u32[]{:S(2)}, u32[]{:S(2)}) collective-permute-start(f32[1,1,2560]{2,1,0:T(1,128)S(1)} %add_add_fusion.4), channel_id=1, source_target_pairs={{0,0},{1,17},{2,2},{3,19},{4,4},{5,21},{6,6},{7,23},{8,8},{9,25},{... | collective-permute-start | bytes 30728 | tf_op jit(solution)/shard_map/ppermute | solution.py:22
  71.9 2.3 %collective-permute-start.21 = (f32[1,1,2560]{2,1,0:T(1,128)S(1)}, f32[1,1,2560]{2,1,0:T(1,128)S(1)}, u32[]{:S(2)}, u32[]{:S(2)}) collective-permute-start(f32[1,1,2560]{2,1,0:T(1,128)S(1)} %add_add_fusion.4), channel_id=1, source_target_pairs={{0,0},{1,25},{2,2},{3,27},{4,4},{5,29},{6,6},{7,31},{8,8},{9,17},{... | collective-permute-start | bytes 30728 | tf_op jit(solution)/shard_map/ppermute | solution.py:22
  74.2 21.5 %collective-permute-start.22 = (f32[1,1,2560]{2,1,0:T(1,128)S(1)}, f32[1,1,2560]{2,1,0:T(1,128)S(1)}, u32[]{:S(2)}, u32[]{:S(2)}) collective-permute-start(f32[1,1,2560]{2,1,0:T(1,128)S(1)} %add_add_fusion.3), channel_id=1, source_target_pairs={{0,1},{1,0},{2,3},{3,2},{4,5},{5,4},{6,7},{7,6},{8,9},{9,8},{10,11... | collective-permute-start | bytes 30728 | tf_op jit(solution)/shard_map/ppermute | solution.py:26

commit v6 on v5

--- a/solution.py
+++ b/solution.py
@@ -17,8 +17,8 @@
     pairs = []
     for place in range(lax.axis_size("seq")):
         for clip in range(clips):
-            there = place ^ mask if clip == clips - 1 else place
-            pairs.append((place * clips + clip, there * clips + clip))
+            there = (place ^ mask) * clips + (clip ^ 1 if clips % 2 == 0 else clip)
+            pairs.append((place * clips + clip, there))
     return lax.ppermute(value, AXES, pairs)
 
 
@@ -145,26 +145,16 @@
     message = sum_to_all(message, group)
     whole_totals = jnp.broadcast_to(totals.T[:, :, None], (experts, clips, 1))
     message = jnp.concatenate([message, whole_totals], axis=2)
-    handed = message[:, clips - 1]
-    for step in range(1, clips):
-        got = hop(message[:, (clips - 1) ^ step], step)
-        handed = jnp.where(clip ^ step == clips - 1, got, handed)
+    handed = lax.dynamic_index_in_dim(message, clip, 1, keepdims=False)
     slot_y = handed[:, :width].astype(bf16)
     slot_dx = handed[:, width : 2 * width].astype(bf16)
     column_stat = handed[:, 2 * width : 2 * width + 1].T
     totals = handed[:, 2 * width + 1 :].T
-    rows = jnp.concatenate([row_x, row_cot, hidden, pre_grad], axis=1)
-    rows, slot_y, slot_dx = lax.optimization_barrier((rows, slot_y, slot_dx))
-    all_rows = of_clips(rows)[clips - 1]
-    units = expert_in.shape[1]
-    all_x, all_cot = all_rows[:, :width], all_rows[:, width : 2 * width]
-    all_hidden = all_rows[:, 2 * width : 2 * width + units]
-    all_grad = all_rows[:, 2 * width + units :]
     share = width // clips
-    mine_x = lax.dynamic_slice_in_dim(all_x, clip * share, share, 1)
-    mine_cot = lax.dynamic_slice_in_dim(all_cot, clip * share, share, 1)
-    grad_expert_in = jnp.einsum("od,oh->dh", mine_x, all_grad, preferred_element_type=f32)
-    grad_expert_out = jnp.einsum("oh,od->hd", all_hidden, mine_cot, preferred_element_type=f32)
+    mine_x = lax.dynamic_slice_in_dim(row_x, clip * share, share, 1)
+    mine_cot = lax.dynamic_slice_in_dim(row_cot, clip * share, share, 1)
+    grad_expert_in = jnp.einsum("od,oh->dh", mine_x, pre_grad, preferred_element_type=f32)
+    grad_expert_out = jnp.einsum("oh,od->hd", hidden, mine_cot, preferred_element_type=f32)
     mixed = jnp.dot(combine, slot_y, preferred_element_type=f32).astype(bf16)
     comb_dot = jnp.einsum("nd,sd->ns", tok_cot, slot_y, preferred_element_type=f32)
     grad_comb = combine_f * (comb_dot - jnp.sum(combine_f * comb_dot, axis=1, keepdims=True))
@@ -177,7 +167,7 @@
     phi_part = jnp.einsum("nd,ns->sd", tok_norm, score_grad, preferred_element_type=f32)
     phi_flat = sum(of_clips(phi_part.reshape(1, 1, -1)))
     phi_flat = sum_to_all(phi_flat, size)
-    phi_grad = of_clips(phi_flat)[clips - 1].reshape(experts, width).T
+    phi_grad = phi_flat.reshape(experts, width).T
     through = jnp.dot(dispatch, slot_dx, preferred_element_type=f32)
     back_norm = tok_scale * (
         norm_grad - tok_unit * jnp.sum(tok_unit * norm_grad, axis=1, keepdims=True)

time: 97.3 us -> 59.3 us (0.61)
  starting transfers between devices: 71.1 us -> 22.5 us
  waiting for transfers between devices: 1.73 us -> 13.5 us
    ppermute x5 -> x2, starting transfers between devices: 59.2 us -> 0.86 us  [hop(): lax.ppermute(value, 'dp', [(i, i ^ step) for i in range(lax.axis_size('dp...]
    ppermute x18, waiting for transfers between devices: 0.05 us -> 12.5 us  [exchange(): return lax.ppermute(value, AXES, pairs)]
    ppermute x18, starting transfers between devices: 11.9 us -> 21.6 us  [exchange(): return lax.ppermute(value, AXES, pairs)]
    dot_general x1, matrix products: 0.36 us -> 1.76 us  [per_device(): pre_act = jnp.dot(row_x, expert_in, preferred_element_type=f32)]
    dot_general x1, matrix products: 1.76 us -> 0.38 us  [per_device(): part_out = jnp.dot(hidden, expert_out, preferred_element_type=f32)]
  transfers between devices with their start and end apart: 23 -> 20, of which waited for: 2 -> 11; matrix products, arithmetic and copies ran while one was open for 8% -> 13% of each run, Pallas kernels for 0% -> 0%
where the time goes in v6:
time: 59.3 us; the launch traced here: 59.1 us
  starting transfers between devices  22.5 us (38%)
  matrix products  16 us (27%)
  waiting for transfers between devices  13.5 us (23%)
  other arithmetic  4.29 us (7%)
  between operations  1.51 us (3%)
  local copies, waits for them, and re-layouts  1.2 us (2%)
    ppermute x18, starting transfers between devices, exchange(): return lax.ppermute(value, AXES, pairs)  21.6 us
    ppermute x18, waiting for transfers between devices, exchange(): return lax.ppermute(value, AXES, pairs)  12.5 us
    dot_general x1, matrix products, per_device(): through = jnp.dot(dispatch, slot_dx, preferred_element_type=f32)  2.05 us
    dot_general x1, matrix products, per_device(): jnp.dot(tok_norm, phi_norm, preferred_element_type=f32)  1.97 us
    reduce_sum x1, other arithmetic, per_device(): jnp.sum(tok_f32 * tok_f32, axis=1, keepdims=True) + epsilon  1.8 us
    dot_general x1, matrix products, per_device(): jnp.einsum('nd,sd->ns', tok_cot, slot_y, preferred_element_type=f32)  1.78 us
    dot_general x1, matrix products, per_device(): pre_act = jnp.dot(row_x, expert_in, preferred_element_type=f32)  1.76 us
    dot_general x1, matrix products, per_device(): jnp.einsum('oh,od->hd', hidden, mine_cot, preferred_element_type=f32)  1.63 us
  transfers between devices with their start and end apart: 20, of which 11 were waited for; matrix products, arithmetic and copies ran while one was open for 13% of the time, Pallas kernels for 0%

profile of v6, /device:TPU:0, one launch (start us, length us, event | category | flops | bytes accessed | tf_op | source)
XLA Modules:
  0.0 59.1 jit_solution(14293620060741151993)
XLA Ops:
  0.7 1.8 %fusion.9 = f32[512]{0:T(512)S(1)} fusion(bf16[1,512,1280]{2,1,0:T(8,128)(2,1)} %param.6), kind=kLoop, calls=%fused_computation.13 | loop fusion | flops 1965568 | bytes 1312768 | tf_op jit(solution)/shard_map/reduce_sum | solution.py:108
  2.5 0.9 %fusion.56 = f32[2]{0:T(128)S(1)} fusion(bf16[1280,2]{0,1:T(2,128)(2,1)} %param.8), kind=kLoop, calls=%fused_computation.70 | loop fusion | flops 7678 | bytes 5128 | tf_op jit(solution)/shard_map/reduce_sum | solution.py:104
  4.1 2.0 %fusion.89 = (f32[2]{0:T(128)S(1)}, f32[512]{0:T(512)S(1)}, bf16[512,2]{0,1:T(2,128)(2,1)S(1)}, bf16[512,2]{0,1:T(2,128)(2,1)S(1)}, f32[512,2]{0,1:T(2,128)S(1)}) fusion(bf16[1280,2]{0,1:T(2,128)(2,1)} %param.8, f32[2]{0:T(128)S(1)} %add_rsqrt_fusion.1, bf16[1,512,1280]{2,1,0:T(8,128)(2,1)} %param.6, f32[512]{0:T(512)S(1)} %add_rsqrt_fusion, f32[]{:T(128)} %bitcast.85), kind=kOutput, calls=%fused_computation.126 | convolution fusion | flops 4601854 | bytes 1328148 | tf_op jit(solution)/shard_map/dot_general | solution.py:111
  6.0 0.3 fusion.16
  6.4 0.3 fusion.12
  6.7 0.5 collective-permute-start
  7.2 0.8 %collective-permute-done = f32[2,2562]{1,0:T(2,128)S(1)} collective-permute-done((f32[2,2562]{1,0:T(2,128)S(1)}, f32[2,2562]{1,0:T(2,128)S(1)}, u32[]{:S(2)}, u32[]{:S(2)}) %collective-permute-start) | collective-permute-done | bytes 20528 | tf_op jit(solution)/shard_map/ppermute | solution.py:26
  8.1 2.8 %collective-permute-start.1 = (f32[1,2,2562]{2,0,1:T(1,128)S(1)}, f32[1,2,2562]{2,0,1:T(1,128)S(1)}, u32[]{:S(2)}, u32[]{:S(2)}) collective-permute-start(f32[1,2,2562]{2,0,1:T(1,128)S(1)} %get-tuple-element.11), channel_id=1, source_target_pairs={{0,9},{1,8},{2,11},{3,10},{4,13},{5,12},{6,15},{7,14},{8,1},{9,0},... | collective-permute-start | bytes 61496 | tf_op jit(solution)/shard_map/ppermute | solution.py:22
  10.9 2.5 %collective-permute-start.2 = (f32[1,2,2562]{2,0,1:T(1,128)S(1)}, f32[1,2,2562]{2,0,1:T(1,128)S(1)}, u32[]{:S(2)}, u32[]{:S(2)}) collective-permute-start(f32[1,2,2562]{2,0,1:T(1,128)S(1)} %get-tuple-element.12), channel_id=1, source_target_pairs={{0,17},{1,16},{2,19},{3,18},{4,21},{5,20},{6,23},{7,22},{8,25},{9,... | collective-permute-start | bytes 61496 | tf_op jit(solution)/shard_map/ppermute | solution.py:22
  13.4 1.8 %collective-permute-done.2 = f32[1,2,2562]{2,0,1:T(1,128)S(1)} collective-permute-done((f32[1,2,2562]{2,0,1:T(1,128)S(1)}, f32[1,2,2562]{2,0,1:T(1,128)S(1)}, u32[]{:S(2)}, u32[]{:S(2)}) %collective-permute-start.2) | collective-permute-done | bytes 20528 | tf_op jit(solution)/shard_map/ppermute | solution.py:22
  15.2 3.2 %collective-permute-done.3 = f32[1,2,2562]{2,0,1:T(1,128)S(1)} collective-permute-done((f32[1,2,2562]{2,0,1:T(1,128)S(1)}, f32[1,2,2562]{2,0,1:T(1,128)S(1)}, u32[]{:S(2)}, u32[]{:S(2)}) %collective-permute-start.3) | collective-permute-done | bytes 20528 | tf_op jit(solution)/shard_map/ppermute | solution.py:22
  18.5 1.3 %collective-permute-start.4 = (f32[1,2,2562]{2,0,1:T(1,128)S(1)}, f32[1,2,2562]{2,0,1:T(1,128)S(1)}, u32[]{:S(2)}, u32[]{:S(2)}) collective-permute-start(f32[1,2,2562]{2,0,1:T(1,128)S(1)} %add_add_fusion.2), channel_id=1, source_target_pairs={{0,3},{1,2},{2,1},{3,0},{4,7},{5,6},{6,5},{7,4},{8,11},{9,10},{10,... | collective-permute-start | bytes 61496 | tf_op jit(solution)/shard_map/ppermute | solution.py:22
  19.8 1.5 %collective-permute-start.5 = (f32[1,2,2562]{2,0,1:T(1,128)S(1)}, f32[1,2,2562]{2,0,1:T(1,128)S(1)}, u32[]{:S(2)}, u32[]{:S(2)}) collective-permute-start(f32[1,2,2562]{2,0,1:T(1,128)S(1)} %add_add_fusion.2), channel_id=1, source_target_pairs={{0,5},{1,4},{2,7},{3,6},{4,1},{5,0},{6,3},{7,2},{8,13},{9,12},{10,... | collective-permute-start | bytes 61496 | tf_op jit(solution)/shard_map/ppermute | solution.py:22
  21.3 0.2 collective-permute-start.6
  21.6 0.2 collective-permute-done.4
  21.8 1.3 %collective-permute-done.5 = f32[1,2,2562]{2,0,1:T(1,128)S(1)} collective-permute-done((f32[1,2,2562]{2,0,1:T(1,128)S(1)}, f32[1,2,2562]{2,0,1:T(1,128)S(1)}, u32[]{:S(2)}, u32[]{:S(2)}) %collective-permute-start.5) | collective-permute-done | bytes 20528 | tf_op jit(solution)/shard_map/ppermute | solution.py:22
  23.1 2.4 %collective-permute-done.6 = f32[1,2,2562]{2,0,1:T(1,128)S(1)} collective-permute-done((f32[1,2,2562]{2,0,1:T(1,128)S(1)}, f32[1,2,2562]{2,0,1:T(1,128)S(1)}, u32[]{:S(2)}, u32[]{:S(2)}) %collective-permute-start.6) | collective-permute-done | bytes 20528 | tf_op jit(solution)/shard_map/ppermute | solution.py:22
  25.8 1.8 %fusion.92 = f32[2,640]{1,0:T(2,128)S(1)} fusion(bf16[2,1280]{1,0:T(2,128)(2,1)S(1)} %get-tuple-element.9, bf16[1280,640]{1,0:T(8,128)(2,1)} %param.10), kind=kOutput, calls=%fused_computation.129 | convolution fusion | flops 3276800 | bytes 1648640 | tf_op jit(solution)/shard_map/dot_general | solution.py:137
  27.5 0.5 fusion.37
  28.1 0.4 fusion.87
  28.5 0.5 copy-done.2
  29.0 0.5 fusion.93
  29.8 0.4 collective-permute-start.7
  30.1 0.5 collective-permute-start.8
  30.6 2.2 %collective-permute-start.9 = (f32[1,2,2561]{2,1,0:T(2,128)S(1)}, f32[1,2,2561]{2,1,0:T(2,128)S(1)}, u32[]{:S(2)}, u32[]{:S(2)}) collective-permute-start(f32[1,2,2561]{2,1,0:T(2,128)S(1)} %maximum_bitcast_fusion), channel_id=1, source_target_pairs={{0,7},{1,6},{2,5},{3,4},{4,3},{5,2},{6,1},{7,0},{8,15},{9,14},{10,... | collective-permute-start | bytes 61472 | tf_op jit(solution)/shard_map/ppermute | solution.py:22
  32.8 1.6 %fusion.76 = f32[640,640]{1,0:T(8,128)} fusion(bf16[2,1280]{1,0:T(2,128)(2,1)S(1)} %slice.63, s32[]{:T(128)S(6)} %select_n.88, f32[2,640]{1,0:T(2,128)S(1)} %fusion.92), kind=kOutput, calls=%fused_computation.110 | convolution fusion | flops 1721600 | bytes 1646084 | tf_op jit(solution)/shard_map/oh,od->hd/dot_general | solution.py:157
  34.4 0.3 collective-permute-done.9
  34.8 0.7 %collective-permute-start.11 = (f32[1,2,2561]{2,1,0:T(2,128)S(1)}, f32[1,2,2561]{2,1,0:T(2,128)S(1)}, u32[]{:S(2)}, u32[]{:S(2)}) collective-permute-start(f32[1,2,2561]{2,1,0:T(2,128)S(1)} %add_add_fusion), channel_id=1, source_target_pairs={{0,25},{1,24},{2,27},{3,26},{4,29},{5,28},{6,31},{7,30},{8,17},{9,... | collective-permute-start | bytes 61472 | tf_op jit(solution)/shard_map/ppermute | solution.py:22
  35.5 2.2 %collective-permute-start.12 = (f32[1,2,2561]{2,1,0:T(2,128)S(1)}, f32[1,2,2561]{2,1,0:T(2,128)S(1)}, u32[]{:S(2)}, u32[]{:S(2)}) collective-permute-start(f32[1,2,2561]{2,1,0:T(2,128)S(1)} %add_add_fusion), channel_id=1, source_target_pairs={{0,9},{1,8},{2,11},{3,10},{4,13},{5,12},{6,15},{7,14},{8,1},{9,0},... | collective-permute-start | bytes 61472 | tf_op jit(solution)/shard_map/ppermute | solution.py:22
  37.8 1.6 %fusion.75 = f32[640,640]{1,0:T(8,128)} fusion(bf16[2,640]{1,0:T(2,128)(2,1)S(1)} %fusion.37, bf16[2,1280]{1,0:T(2,128)(2,1)S(1)} %get-tuple-element.9, s32[]{:T(128)S(6)} %select_n.88), kind=kOutput, calls=%fused_computation.109 | convolution fusion | flops 1638400 | bytes 1643524 | tf_op jit(solution)/shard_map/od,oh->dh/dot_general | solution.py:156
  39.5 0.4 collective-permute-done.11
  40.1 1.8 %multiply_reduce_fusion.1 = (f32[512]{0:T(512)S(1)}, f32[512,2]{0,1:T(2,128)S(1)}) fusion(f32[512,2]{0,1:T(2,128)S(1)} %get-tuple-element.20, f32[512]{0:T(512)S(1)} %get-tuple-element.8, bf16[1,512,1280]{2,1,0:T(8,128)(2,1)} %param.7, bf16[2,2562]{1,0:T(2,128)(2,1)S(1)} %bitcast.91), kind=kOutput, calls=%fused_computation.101 | convolution fusion | flops 2624000 | bytes 1328128 | tf_op jit(solution)/shard_map/nd,sd->ns/dot_general | solution.py:159
  42.1 0.4 fusion.38
  42.5 0.4 fusion.41
  43.0 0.3 collective-permute-start.13
  43.3 0.7 %fusion.6 = (f32[512]{0:T(512)S(1)}, f32[512,1280]{1,0:T(8,128)S(1)}) fusion(bf16[1,512,1280]{2,1,0:T(8,128)(2,1)S(1)} %copy-done.1, f32[512]{0:T(512)S(1)} %add_rsqrt_fusion, bf16[512,2]{0,1:T(2,128)(2,1)S(1)} %fusion.38, bf16[1280,2]{0,1:T(2,128)(2,1)S(1)} %copy-done.4, f32[2]{0:T(128)S(1)} %add_rsqrt_fusion.1), kind=kOutput, calls=%fused_computation.10 | convolution fusion | flops 5250048 | bytes 3943432 | tf_op jit(solution)/shard_map/ns,ds->nd/dot_general | solution.py:166
  44.3 1.4 %collective-permute-start.14 = (f32[1,1,2560]{2,1,0:T(1,128)S(1)}, f32[1,1,2560]{2,1,0:T(1,128)S(1)}, u32[]{:S(2)}, u32[]{:S(2)}) collective-permute-start(f32[1,1,2560]{2,1,0:T(1,128)S(1)} %fusion.57), channel_id=1, source_target_pairs={{0,3},{1,2},{2,1},{3,0},{4,7},{5,6},{6,5},{7,4},{8,11},{9,10},{10,... | collective-permute-start | bytes 30728 | tf_op jit(solution)/shard_map/ppermute | solution.py:22
  45.7 1.4 %collective-permute-start.15 = (f32[1,1,2560]{2,1,0:T(1,128)S(1)}, f32[1,1,2560]{2,1,0:T(1,128)S(1)}, u32[]{:S(2)}, u32[]{:S(2)}) collective-permute-start(f32[1,1,2560]{2,1,0:T(1,128)S(1)} %fusion.57), channel_id=1, source_target_pairs={{0,5},{1,4},{2,7},{3,6},{4,1},{5,0},{6,3},{7,2},{8,13},{9,12},{10,... | collective-permute-start | bytes 30728 | tf_op jit(solution)/shard_map/ppermute | solution.py:22
  47.0 0.4 collective-permute-start.16
  47.4 2.1 %fusion.4 = bf16[1,512,1280]{2,1,0:T(8,128)(2,1)} fusion(f32[512,1280]{1,0:T(8,128)S(1)} %get-tuple-element.24, bf16[1,512,1280]{2,1,0:T(8,128)(2,1)S(1)} %copy-done.1, f32[512]{0:T(512)S(1)} %get-tuple-element.23, f32[512]{0:T(512)S(1)} %add_rsqrt_fusion, bf16[2,2562]{1,0:T(2,128)(2,1)S(1)} %bitcast.93, f32[512,2]{0,1:T(2,128)S(1)} %get-tuple-element.20, ...), kind=kOutput, calls=%fused_computation.8 | convolution fusion | flops 7211008 | bytes 5256704 | tf_op jit(solution)/shard_map/dot_general | solution.py:171
  49.5 1.6 %collective-permute-done.16 = f32[1,1,2560]{2,1,0:T(1,128)S(1)} collective-permute-done((f32[1,1,2560]{2,1,0:T(1,128)S(1)}, f32[1,1,2560]{2,1,0:T(1,128)S(1)}, u32[]{:S(2)}, u32[]{:S(2)}) %collective-permute-start.16) | collective-permute-done | bytes 10272 | tf_op jit(solution)/shard_map/ppermute | solution.py:22
  51.1 1.2 %collective-permute-start.17 = (f32[1,1,2560]{2,1,0:T(1,128)S(1)}, f32[1,1,2560]{2,1,0:T(1,128)S(1)}, u32[]{:S(2)}, u32[]{:S(2)}) collective-permute-start(f32[1,1,2560]{2,1,0:T(1,128)S(1)} %add_add_fusion.3), channel_id=1, source_target_pairs={{0,9},{1,8},{2,11},{3,10},{4,13},{5,12},{6,15},{7,14},{8,1},{9,0},... | collective-permute-start | bytes 30728 | tf_op jit(solution)/shard_map/ppermute | solution.py:22
  52.3 1.0 %collective-permute-start.18 = (f32[1,1,2560]{2,1,0:T(1,128)S(1)}, f32[1,1,2560]{2,1,0:T(1,128)S(1)}, u32[]{:S(2)}, u32[]{:S(2)}) collective-permute-start(f32[1,1,2560]{2,1,0:T(1,128)S(1)} %add_add_fusion.3), channel_id=1, source_target_pairs={{0,17},{1,16},{2,19},{3,18},{4,21},{5,20},{6,23},{7,22},{8,25},{9,... | collective-permute-start | bytes 30728 | tf_op jit(solution)/shard_map/ppermute | solution.py:22
  53.2 1.9 %collective-permute-start.19 = (f32[1,1,2560]{2,1,0:T(1,128)S(1)}, f32[1,1,2560]{2,1,0:T(1,128)S(1)}, u32[]{:S(2)}, u32[]{:S(2)}) collective-permute-start(f32[1,1,2560]{2,1,0:T(1,128)S(1)} %add_add_fusion.3), channel_id=1, source_target_pairs={{0,25},{1,24},{2,27},{3,26},{4,29},{5,28},{6,31},{7,30},{8,17},{9,... | collective-permute-start | bytes 30728 | tf_op jit(solution)/shard_map/ppermute | solution.py:22
  55.1 1.6 %fusion.5 = bf16[1,512,1280]{2,1,0:T(8,128)(2,1)} fusion(bf16[2,2562]{1,0:T(2,128)(2,1)S(1)} %bitcast.94, f32[512,2]{0,1:T(2,128)S(1)} %get-tuple-element.20, f32[512]{0:T(512)S(1)} %get-tuple-element.8), kind=kOutput, calls=%fused_computation.9 | convolution fusion | flops 3278848 | bytes 1321984 | tf_op jit(solution)/shard_map/dot_general | solution.py:158
  56.8 1.4 %collective-permute-done.19 = f32[1,1,2560]{2,1,0:T(1,128)S(1)} collective-permute-done((f32[1,1,2560]{2,1,0:T(1,128)S(1)}, f32[1,1,2560]{2,1,0:T(1,128)S(1)}, u32[]{:S(2)}, u32[]{:S(2)}) %collective-permute-start.19) | collective-permute-done | bytes 10272 | tf_op jit(solution)/shard_map/ppermute | solution.py:22
  58.2 0.2 fusion.53
  58.4 0.7 %fusion.55 = f32[1280,2]{0,1:T(2,128)} fusion(bf16[1280,2]{0,1:T(2,128)(2,1)S(1)} %copy-done.4, f32[2,1280]{1,0:T(2,128)S(1)} %reshape.48, f32[2]{0:T(128)S(1)} %fusion.53, f32[2]{0:T(128)S(1)} %add_rsqrt_fusion.1), kind=kLoop, calls=%fused_computation.69 | loop fusion | flops 12800 | bytes 25616 | tf_op jit(solution)/shard_map/mul | solution.py:176
  (52 shorter events, 1.7 us)
Async XLA Ops:
  0.6 26.9 %copy-start = (bf16[640,1280]{1,0:T(8,128)(2,1)S(1)}, bf16[640,1280]{1,0:T(8,128)(2,1)}, u32[]{:S(2)}) copy-start(bf16[640,1280]{1,0:T(8,128)(2,1)} %param.11) | copy-start | bytes 4915204
  0.6 5.4 %copy-start.1 = (bf16[1,512,1280]{2,1,0:T(8,128)(2,1)S(1)}, bf16[1,512,1280]{2,1,0:T(8,128)(2,1)}, u32[]{:S(2)}) copy-start(bf16[1,512,1280]{2,1,0:T(8,128)(2,1)} %param.6) | copy-start | bytes 3932164
  2.5 3.9 %copy-start.3 = (bf16[1,512,1280]{2,1,0:T(8,128)(2,1)S(1)}, bf16[1,512,1280]{2,1,0:T(8,128)(2,1)}, u32[]{:S(2)}) copy-start(bf16[1,512,1280]{2,1,0:T(8,128)(2,1)} %param.7) | copy-start | bytes 3932164
  6.7 1.4 %collective-permute-start = (f32[2,2562]{1,0:T(2,128)S(1)}, f32[2,2562]{1,0:T(2,128)S(1)}, u32[]{:S(2)}, u32[]{:S(2)}) collective-permute-start(f32[2,2562]{1,0:T(2,128)S(1)} %maximum_maximum_fusion), channel_id=1, source_target_pairs={{0,1},{1,0},{2,3},{3,2},{4,5},{5,4},{6,7},{7,6},{8,9},{9,8},{10,11... | collective-permute-start | bytes 61496 | tf_op jit(solution)/shard_map/ppermute | solution.py:26
  8.1 5.3 %collective-permute-start.1 = (f32[1,2,2562]{2,0,1:T(1,128)S(1)}, f32[1,2,2562]{2,0,1:T(1,128)S(1)}, u32[]{:S(2)}, u32[]{:S(2)}) collective-permute-start(f32[1,2,2562]{2,0,1:T(1,128)S(1)} %get-tuple-element.11), channel_id=1, source_target_pairs={{0,9},{1,8},{2,11},{3,10},{4,13},{5,12},{6,15},{7,14},{8,1},{9,0},... | collective-permute-start | bytes 61496 | tf_op jit(solution)/shard_map/ppermute | solution.py:22
  10.9 4.3 %collective-permute-start.2 = (f32[1,2,2562]{2,0,1:T(1,128)S(1)}, f32[1,2,2562]{2,0,1:T(1,128)S(1)}, u32[]{:S(2)}, u32[]{:S(2)}) collective-permute-start(f32[1,2,2562]{2,0,1:T(1,128)S(1)} %get-tuple-element.12), channel_id=1, source_target_pairs={{0,17},{1,16},{2,19},{3,18},{4,21},{5,20},{6,23},{7,22},{8,25},{9,... | collective-permute-start | bytes 61496 | tf_op jit(solution)/shard_map/ppermute | solution.py:22
  13.4 5.0 %collective-permute-start.3 = (f32[1,2,2562]{2,0,1:T(1,128)S(1)}, f32[1,2,2562]{2,0,1:T(1,128)S(1)}, u32[]{:S(2)}, u32[]{:S(2)}) collective-permute-start(f32[1,2,2562]{2,0,1:T(1,128)S(1)} %get-tuple-element.13), channel_id=1, source_target_pairs={{0,25},{1,24},{2,27},{3,26},{4,29},{5,28},{6,31},{7,30},{8,17},{9,... | collective-permute-start | bytes 61496 | tf_op jit(solution)/shard_map/ppermute | solution.py:22
  18.5 3.3 %collective-permute-start.4 = (f32[1,2,2562]{2,0,1:T(1,128)S(1)}, f32[1,2,2562]{2,0,1:T(1,128)S(1)}, u32[]{:S(2)}, u32[]{:S(2)}) collective-permute-start(f32[1,2,2562]{2,0,1:T(1,128)S(1)} %add_add_fusion.2), channel_id=1, source_target_pairs={{0,3},{1,2},{2,1},{3,0},{4,7},{5,6},{6,5},{7,4},{8,11},{9,10},{10,... | collective-permute-start | bytes 61496 | tf_op jit(solution)/shard_map/ppermute | solution.py:22
  19.8 3.2 %collective-permute-start.5 = (f32[1,2,2562]{2,0,1:T(1,128)S(1)}, f32[1,2,2562]{2,0,1:T(1,128)S(1)}, u32[]{:S(2)}, u32[]{:S(2)}) collective-permute-start(f32[1,2,2562]{2,0,1:T(1,128)S(1)} %add_add_fusion.2), channel_id=1, source_target_pairs={{0,5},{1,4},{2,7},{3,6},{4,1},{5,0},{6,3},{7,2},{8,13},{9,12},{10,... | collective-permute-start | bytes 61496 | tf_op jit(solution)/shard_map/ppermute | solution.py:22
  21.3 4.1 %collective-permute-start.6 = (f32[1,2,2562]{2,0,1:T(1,128)S(1)}, f32[1,2,2562]{2,0,1:T(1,128)S(1)}, u32[]{:S(2)}, u32[]{:S(2)}) collective-permute-start(f32[1,2,2562]{2,0,1:T(1,128)S(1)} %add_add_fusion.2), channel_id=1, source_target_pairs={{0,7},{1,6},{2,5},{3,4},{4,3},{5,2},{6,1},{7,0},{8,15},{9,14},{10,... | collective-permute-start | bytes 61496 | tf_op jit(solution)/shard_map/ppermute | solution.py:22
  27.5 1.4 %copy-start.2 = (bf16[1280,640]{1,0:T(8,128)(2,1)S(1)}, bf16[1280,640]{1,0:T(8,128)(2,1)}, u32[]{:S(2)}) copy-start(bf16[1280,640]{1,0:T(8,128)(2,1)} %param.10) | copy-start | bytes 4915204
  29.8 4.7 %collective-permute-start.7 = (f32[1,2,2561]{2,1,0:T(2,128)S(1)}, f32[1,2,2561]{2,1,0:T(2,128)S(1)}, u32[]{:S(2)}, u32[]{:S(2)}) collective-permute-start(f32[1,2,2561]{2,1,0:T(2,128)S(1)} %maximum_bitcast_fusion), channel_id=1, source_target_pairs={{0,3},{1,2},{2,1},{3,0},{4,7},{5,6},{6,5},{7,4},{8,11},{9,10},{10,... | collective-permute-start | bytes 61472 | tf_op jit(solution)/shard_map/ppermute | solution.py:22
  30.1 4.3 %collective-permute-start.8 = (f32[1,2,2561]{2,1,0:T(2,128)S(1)}, f32[1,2,2561]{2,1,0:T(2,128)S(1)}, u32[]{:S(2)}, u32[]{:S(2)}) collective-permute-start(f32[1,2,2561]{2,1,0:T(2,128)S(1)} %maximum_bitcast_fusion), channel_id=1, source_target_pairs={{0,5},{1,4},{2,7},{3,6},{4,1},{5,0},{6,3},{7,2},{8,13},{9,12},{10,... | collective-permute-start | bytes 61472 | tf_op jit(solution)/shard_map/ppermute | solution.py:22
  30.6 4.1 %collective-permute-start.9 = (f32[1,2,2561]{2,1,0:T(2,128)S(1)}, f32[1,2,2561]{2,1,0:T(2,128)S(1)}, u32[]{:S(2)}, u32[]{:S(2)}) collective-permute-start(f32[1,2,2561]{2,1,0:T(2,128)S(1)} %maximum_bitcast_fusion), channel_id=1, source_target_pairs={{0,7},{1,6},{2,5},{3,4},{4,3},{5,2},{6,1},{7,0},{8,15},{9,14},{10,... | collective-permute-start | bytes 61472 | tf_op jit(solution)/shard_map/ppermute | solution.py:22
  34.7 4.8 %collective-permute-start.10 = (f32[1,2,2561]{2,1,0:T(2,128)S(1)}, f32[1,2,2561]{2,1,0:T(2,128)S(1)}, u32[]{:S(2)}, u32[]{:S(2)}) collective-permute-start(f32[1,2,2561]{2,1,0:T(2,128)S(1)} %add_add_fusion), channel_id=1, source_target_pairs={{0,17},{1,16},{2,19},{3,18},{4,21},{5,20},{6,23},{7,22},{8,25},{9,... | collective-permute-start | bytes 61472 | tf_op jit(solution)/shard_map/ppermute | solution.py:22
  34.8 5.1 %collective-permute-start.11 = (f32[1,2,2561]{2,1,0:T(2,128)S(1)}, f32[1,2,2561]{2,1,0:T(2,128)S(1)}, u32[]{:S(2)}, u32[]{:S(2)}) collective-permute-start(f32[1,2,2561]{2,1,0:T(2,128)S(1)} %add_add_fusion), channel_id=1, source_target_pairs={{0,25},{1,24},{2,27},{3,26},{4,29},{5,28},{6,31},{7,30},{8,17},{9,... | collective-permute-start | bytes 61472 | tf_op jit(solution)/shard_map/ppermute | solution.py:22
  35.5 3.9 %collective-permute-start.12 = (f32[1,2,2561]{2,1,0:T(2,128)S(1)}, f32[1,2,2561]{2,1,0:T(2,128)S(1)}, u32[]{:S(2)}, u32[]{:S(2)}) collective-permute-start(f32[1,2,2561]{2,1,0:T(2,128)S(1)} %add_add_fusion), channel_id=1, source_target_pairs={{0,9},{1,8},{2,11},{3,10},{4,13},{5,12},{6,15},{7,14},{8,1},{9,0},... | collective-permute-start | bytes 61472 | tf_op jit(solution)/shard_map/ppermute | solution.py:22
  41.9 1.5 %copy-start.4 = (bf16[1280,2]{0,1:T(2,128)(2,1)S(1)}, bf16[1280,2]{0,1:T(2,128)(2,1)}, u32[]{:S(2)}) copy-start(bf16[1280,2]{0,1:T(2,128)(2,1)} %param.8) | copy-start | bytes 15364
  43.0 1.2 %collective-permute-start.13 = (f32[1,1,2560]{2,1,0:T(1,128)S(1)}, f32[1,1,2560]{2,1,0:T(1,128)S(1)}, u32[]{:S(2)}, u32[]{:S(2)}) collective-permute-start(f32[1,1,2560]{2,1,0:T(1,128)S(1)} %reshape.47), channel_id=1, source_target_pairs={{0,1},{1,0},{2,3},{3,2},{4,5},{5,4},{6,7},{7,6},{8,9},{9,8},{10,11... | collective-permute-start | bytes 30728 | tf_op jit(solution)/shard_map/ppermute | solution.py:26
  44.3 5.2 %collective-permute-start.14 = (f32[1,1,2560]{2,1,0:T(1,128)S(1)}, f32[1,1,2560]{2,1,0:T(1,128)S(1)}, u32[]{:S(2)}, u32[]{:S(2)}) collective-permute-start(f32[1,1,2560]{2,1,0:T(1,128)S(1)} %fusion.57), channel_id=1, source_target_pairs={{0,3},{1,2},{2,1},{3,0},{4,7},{5,6},{6,5},{7,4},{8,11},{9,10},{10,... | collective-permute-start | bytes 30728 | tf_op jit(solution)/shard_map/ppermute | solution.py:22
  45.7 3.8 %collective-permute-start.15 = (f32[1,1,2560]{2,1,0:T(1,128)S(1)}, f32[1,1,2560]{2,1,0:T(1,128)S(1)}, u32[]{:S(2)}, u32[]{:S(2)}) collective-permute-start(f32[1,1,2560]{2,1,0:T(1,128)S(1)} %fusion.57), channel_id=1, source_target_pairs={{0,5},{1,4},{2,7},{3,6},{4,1},{5,0},{6,3},{7,2},{8,13},{9,12},{10,... | collective-permute-start | bytes 30728 | tf_op jit(solution)/shard_map/ppermute | solution.py:22
  47.0 4.0 %collective-permute-start.16 = (f32[1,1,2560]{2,1,0:T(1,128)S(1)}, f32[1,1,2560]{2,1,0:T(1,128)S(1)}, u32[]{:S(2)}, u32[]{:S(2)}) collective-permute-start(f32[1,1,2560]{2,1,0:T(1,128)S(1)} %fusion.57), channel_id=1, source_target_pairs={{0,7},{1,6},{2,5},{3,4},{4,3},{5,2},{6,1},{7,0},{8,15},{9,14},{10,... | collective-permute-start | bytes 30728 | tf_op jit(solution)/shard_map/ppermute | solution.py:22
  51.1 5.7 %collective-permute-start.17 = (f32[1,1,2560]{2,1,0:T(1,128)S(1)}, f32[1,1,2560]{2,1,0:T(1,128)S(1)}, u32[]{:S(2)}, u32[]{:S(2)}) collective-permute-start(f32[1,1,2560]{2,1,0:T(1,128)S(1)} %add_add_fusion.3), channel_id=1, source_target_pairs={{0,9},{1,8},{2,11},{3,10},{4,13},{5,12},{6,15},{7,14},{8,1},{9,0},... | collective-permute-start | bytes 30728 | tf_op jit(solution)/shard_map/ppermute | solution.py:22
  52.3 4.5 %collective-permute-start.18 = (f32[1,1,2560]{2,1,0:T(1,128)S(1)}, f32[1,1,2560]{2,1,0:T(1,128)S(1)}, u32[]{:S(2)}, u32[]{:S(2)}) collective-permute-start(f32[1,1,2560]{2,1,0:T(1,128)S(1)} %add_add_fusion.3), channel_id=1, source_target_pairs={{0,17},{1,16},{2,19},{3,18},{4,21},{5,20},{6,23},{7,22},{8,25},{9,... | collective-permute-start | bytes 30728 | tf_op jit(solution)/shard_map/ppermute | solution.py:22
  53.2 4.9 %collective-permute-start.19 = (f32[1,1,2560]{2,1,0:T(1,128)S(1)}, f32[1,1,2560]{2,1,0:T(1,128)S(1)}, u32[]{:S(2)}, u32[]{:S(2)}) collective-permute-start(f32[1,1,2560]{2,1,0:T(1,128)S(1)} %add_add_fusion.3), channel_id=1, source_target_pairs={{0,25},{1,24},{2,27},{3,26},{4,29},{5,28},{6,31},{7,30},{8,17},{9,... | collective-permute-start | bytes 30728 | tf_op jit(solution)/shard_map/ppermute | solution.py:22

commit v7 on v6

v7 whole, which is shorter than its diff:
```python
import jax
import jax.numpy as jnp
from jax import lax
from jax.experimental import pallas as pl
from jax.experimental.pallas import tpu as pltpu
from jax.sharding import PartitionSpec as P

epsilon = 1e-06
AXES = ("seq", "dp")
LANES = 128
BLOCK = 128
VMEM_BYTES = 24 * 2**20
ROWS = (((1,), (1,)), ((), ()))
COLUMNS = (((0,), (0,)), ((), ()))
f32, bf16 = jnp.float32, jnp.bfloat16


def exchange(value, mask):
    clips = lax.axis_size("dp")
    pairs = []
    for place in range(lax.axis_size("seq")):
        for clip in range(clips):
            there = (place ^ mask) * clips + (clip ^ 1 if clips % 2 == 0 else clip)
            pairs.append((place * clips + clip, there))
    return lax.ppermute(value, AXES, pairs)


def hop(value, step):
    return lax.ppermute(value, "dp", [(i, i ^ step) for i in range(lax.axis_size("dp"))])


def of_clips(value):
    clips = lax.axis_size("dp")
    clip = lax.axis_index("dp")
    got = [value] + [hop(value, step) for step in range(1, clips)]
    ordered = []
    for index in range(clips):
        picked = got[0]
        for step in range(1, clips):
            picked = jnp.where(clip ^ step == index, got[step], picked)
        ordered.append(picked)
    return ordered


def rounds(size):
    masks = [1 << bit for bit in range(size.bit_length() - 1)]
    return [masks[i : i + 2] for i in range(0, len(masks), 2)]


def round_masks(pair):
    return pair if len(pair) == 1 else [pair[0], pair[1], pair[0] | pair[1]]


def sum_to_owner(value, group):
    place = lax.axis_index("seq")
    for pair in reversed(rounds(lax.axis_size("seq"))):
        owner_masks = [mask for mask in pair if mask >= group]
        blocks = value.reshape((1 << len(owner_masks), -1) + value.shape[1:])

        def block_for(mask):
            index = 0
            for bit, owner_mask in enumerate(owner_masks):
                index = index + jnp.where((place ^ mask) & owner_mask != 0, 1 << bit, 0)
            return lax.dynamic_index_in_dim(blocks, index, 0, keepdims=False)

        got = [block_for(0)] + [exchange(block_for(mask), mask) for mask in round_masks(pair)]
        value = got[0] + got[1] if len(got) == 2 else (got[0] + got[1]) + (got[2] + got[3])
    return value


def sum_to_all(value, group):
    place = lax.axis_index("seq")
    for pair in rounds(lax.axis_size("seq")):
        terms = {0: value}
        for mask in round_masks(pair):
            terms[mask] = exchange(value, mask)
        for mask in pair:
            upper = (place & mask) != 0
            merged = {}
            for key in terms:
                if key & mask:
                    continue
                near, far = terms[key], terms[key | mask]
                if mask < group:
                    merged[key] = near + far
                else:
                    merged[key] = jnp.where(
                        upper, jnp.concatenate([far, near]), jnp.concatenate([near, far])
                    )
            terms = merged
        value = terms[0]
    return value


def token_sums(scale_ref, phi_ref, tok_ref, cot_ref, message_ref, exp_ref, tok_scale_ref, norm_ref):
    experts, width = phi_ref.shape[1], phi_ref.shape[0]

    @pl.when(pl.program_id(0) == 0)
    def _():
        phi = phi_ref[...].astype(f32)
        phi_scale = lax.rsqrt(jnp.sum(phi * phi, axis=0, keepdims=True) + epsilon)
        norm_ref[...] = (phi * phi_scale).astype(bf16)
        message_ref[...] = jnp.zeros_like(message_ref)

    tok_in = tok_ref[...]
    tok_f32 = tok_in.astype(f32)
    tok_scale = lax.rsqrt(jnp.sum(tok_f32 * tok_f32, axis=1, keepdims=True) + epsilon)
    tok_norm = (tok_f32 * tok_scale).astype(bf16)
    logits = scale_ref[0] * jnp.dot(tok_norm, norm_ref[...], preferred_element_type=f32)
    exp_scores = jnp.exp(logits)
    combine = (exp_scores / jnp.sum(exp_scores, axis=1, keepdims=True)).astype(bf16)
    exp_high = exp_scores.astype(bf16)
    exp_low = (exp_scores - exp_high.astype(f32)).astype(bf16)
    in_part = lax.dot_general(exp_high, tok_in, COLUMNS, preferred_element_type=f32)
    in_part = in_part + lax.dot_general(exp_low, tok_in, COLUMNS, preferred_element_type=f32)
    cot_part = lax.dot_general(combine, cot_ref[...], COLUMNS, preferred_element_type=f32)
    message_ref[:, :width] += in_part
    message_ref[:, width : 2 * width] += cot_part
    total = jnp.sum(exp_scores, axis=0, keepdims=True)
    message_ref[:, 2 * width : 2 * width + experts] += jnp.broadcast_to(total, (experts, experts))
    exp_ref[...] = exp_scores
    tok_scale_ref[...] = tok_scale


def expert_rows(owned_ref, sums_ref, in_ref, out_ref, message_ref, row_x_ref, row_cot_ref, hidden_ref, pre_grad_ref):
    width, units = in_ref.shape
    spare = sums_ref[:, 2 * width :]
    lane = lax.broadcasted_iota(jnp.int32, spare.shape, 1)
    own_total = jnp.sum(jnp.where(lane == owned_ref[0], spare, 0.0), axis=1, keepdims=True)
    own_in = sums_ref[:, :width] / own_total
    row_x = own_in.astype(bf16)
    row_cot = sums_ref[:, width : 2 * width].astype(bf16)
    pre_act = jnp.dot(row_x, in_ref[...], preferred_element_type=f32)
    hid_grad = lax.dot_general(row_cot, out_ref[...], ROWS, preferred_element_type=f32)
    cdf = 0.5 * (1.0 + lax.erf(pre_act * 0.7071067811865476))
    hidden = (pre_act * cdf).astype(bf16)
    slope = cdf + pre_act * jnp.exp(-0.5 * pre_act * pre_act) * 0.3989422804014327
    pre_grad = (hid_grad * slope).astype(bf16)
    part_out = jnp.dot(hidden, out_ref[...], preferred_element_type=f32)
    part_dx = lax.dot_general(pre_grad, in_ref[...], ROWS, preferred_element_type=f32)
    message_ref[:, :width] = part_out
    message_ref[:, width : 2 * width] = part_dx
    dot_part = jnp.sum(own_in * part_dx, axis=1, keepdims=True)
    message_ref[:, 2 * width :] = jnp.broadcast_to(dot_part, spare.shape)
    row_x_ref[...] = row_x
    row_cot_ref[...] = row_cot
    hidden_ref[...] = hidden
    pre_grad_ref[...] = pre_grad


def as_row(column):
    slots = column.shape[0]
    shape = (slots, slots)
    same = lax.broadcasted_iota(jnp.int32, shape, 0) == lax.broadcasted_iota(jnp.int32, shape, 1)
    return jnp.sum(jnp.where(same, column, 0.0), axis=0, keepdims=True)


def score_grads(scale_ref, slots_ref, totals_ref, tok_ref, cot_ref, exp_ref, tok_scale_ref, grad_ref, phi_ref):
    width = tok_ref.shape[1]

    @pl.when(pl.program_id(0) == 0)
    def _():
        phi_ref[...] = jnp.zeros_like(phi_ref)

    slot_y = slots_ref[:, :width].astype(bf16)
    slot_dx = slots_ref[:, width : 2 * width].astype(bf16)
    column_stat = as_row(slots_ref[:, 2 * width : 2 * width + 1])
    totals = totals_ref[:, : slot_y.shape[0]]
    tok_in = tok_ref[...]
    exp_scores = exp_ref[...]
    combine_f = exp_scores / jnp.sum(exp_scores, axis=1, keepdims=True)
    comb_dot = lax.dot_general(cot_ref[...], slot_y, ROWS, preferred_element_type=f32)
    grad_comb = combine_f * (comb_dot - jnp.sum(combine_f * comb_dot, axis=1, keepdims=True))
    disp_dot = lax.dot_general(tok_in, slot_dx, ROWS, preferred_element_type=f32)
    grad_disp = exp_scores / totals * (disp_dot - column_stat)
    score_grad = (scale_ref[0] * (grad_comb + grad_disp)).astype(bf16)
    tok_norm = (tok_in.astype(f32) * tok_scale_ref[...]).astype(bf16)
    phi_ref[...] += lax.dot_general(score_grad, tok_norm, COLUMNS, preferred_element_type=f32)
    grad_ref[...] = score_grad.astype(f32)


def whole(shape):
    return pl.BlockSpec(shape, lambda *_: (0,) * len(shape))


def block_of(rows, columns):
    return pl.BlockSpec((rows, columns), lambda i: (i, 0))


def per_device(tokens, cotangent, router, logit_scale, expert_in, expert_out):
    tok_in = tokens[0]
    tok_cot = cotangent[0]
    count = tok_in.shape[0]
    width, experts = router.shape
    units = expert_in.shape[1]
    size = lax.axis_size("seq")
    group = size // experts
    clips = lax.axis_size("dp")
    clip = lax.axis_index("dp")
    owned = lax.axis_index("seq") // group
    length = 2 * width + -(-experts // LANES) * LANES
    rows = min(BLOCK, count)
    scalar = pl.BlockSpec(memory_space=pltpu.SMEM)
    params = pltpu.CompilerParams(vmem_limit_bytes=VMEM_BYTES)
    message, exp_scores, tok_scale = pl.pallas_call(
        token_sums,
        grid=(count // rows,),
        in_specs=[scalar, whole((width, experts)), block_of(rows, width), block_of(rows, width)],
        out_specs=[whole((experts, length)), block_of(rows, experts), block_of(rows, 1)],
        out_shape=[
            jax.ShapeDtypeStruct((experts, length), f32),
            jax.ShapeDtypeStruct((count, experts), f32),
            jax.ShapeDtypeStruct((count, 1), f32),
        ],
        scratch_shapes=[pltpu.VMEM((width, experts), bf16)],
        compiler_params=params,
        name="token_sums",
    )(logit_scale, router, tok_in, tok_cot)
    message = sum_to_owner(jnp.stack(of_clips(message), axis=1), group)[0]
    totals = message[:, 2 * width :]
    message, row_x, row_cot, hidden, pre_grad = pl.pallas_call(
        expert_rows,
        in_specs=[scalar] + [pl.BlockSpec(memory_space=pltpu.VMEM)] * 3,
        out_shape=[
            jax.ShapeDtypeStruct((clips, length), f32),
            jax.ShapeDtypeStruct((clips, width), bf16),
            jax.ShapeDtypeStruct((clips, width), bf16),
            jax.ShapeDtypeStruct((clips, units), bf16),
            jax.ShapeDtypeStruct((clips, units), bf16),
        ],
        compiler_params=params,
        name="expert_rows",
    )(owned[None], message, expert_in, expert_out)
    message = sum_to_all(message[None], group)
    slots = lax.dynamic_index_in_dim(message, clip, 1, keepdims=False)
    totals = lax.dynamic_index_in_dim(totals, clip, 0, keepdims=True)
    share = width // clips
    mine_x = lax.dynamic_slice_in_dim(row_x, clip * share, share, 1)
    mine_cot = lax.dynamic_slice_in_dim(row_cot, clip * share, share, 1)
    grad_expert_in = jnp.einsum("od,oh->dh", mine_x, pre_grad, preferred_element_type=f32)
    grad_expert_out = jnp.einsum("oh,od->hd", hidden, mine_cot, preferred_element_type=f32)
    score_grad, phi_part = pl.pallas_call(
        score_grads,
        grid=(count // rows,),
        in_specs=[
            scalar,
            whole((experts, length)),
            whole((1, length - 2 * width)),
            block_of(rows, width),
            block_of(rows, width),
            block_of(rows, experts),
            block_of(rows, 1),
        ],
        out_specs=[block_of(rows, experts), whole((experts, width))],
        out_shape=[
            jax.ShapeDtypeStruct((count, experts), f32),
            jax.ShapeDtypeStruct((experts, width), f32),
        ],
        compiler_params=params,
        name="score_grads",
    )(logit_scale, slots, totals, tok_in, tok_cot, exp_scores, tok_scale)
    phi_flat = sum(of_clips(phi_part.reshape(1, 1, -1)))
    phi_grad = sum_to_all(phi_flat, size).reshape(experts, width).T
    phi_f32 = router.astype(f32)
    phi_scale = lax.rsqrt(jnp.sum(phi_f32 * phi_f32, axis=0, keepdims=True) + epsilon)
    phi_unit = phi_f32 * phi_scale
    phi_norm = phi_unit.astype(bf16)
    slot_y = slots[:, :width].astype(bf16)
    slot_dx = slots[:, width : 2 * width].astype(bf16)
    combine = (exp_scores / jnp.sum(exp_scores, axis=1, keepdims=True)).astype(bf16)
    dispatch = (exp_scores / totals[:, :experts]).astype(bf16)
    mixed = jnp.dot(combine, slot_y, preferred_element_type=f32).astype(bf16)
    norm_grad = jnp.einsum(
        "ns,ds->nd", score_grad.astype(bf16), phi_norm, preferred_element_type=f32
    )
    through = jnp.dot(dispatch, slot_dx, preferred_element_type=f32)
    tok_unit = tok_in.astype(f32) * tok_scale
    back_norm = tok_scale * (
        norm_grad - tok_unit * jnp.sum(tok_unit * norm_grad, axis=1, keepdims=True)
    )
    grad_tokens = (through + back_norm).astype(bf16)
    grad_router = phi_scale * (
        phi_grad - phi_unit * jnp.sum(phi_unit * phi_grad, axis=0, keepdims=True)
    )
    return (mixed[None], grad_tokens[None], grad_expert_in, grad_expert_out, grad_router)


def solution(mesh):
    return jax.shard_map(
        per_device,
        mesh=mesh,
        in_specs=(
            P("dp", "seq", None),
            P("dp", "seq", None),
            P(),
            P(),
            P(None, "seq"),
            P("seq", None),
        ),
        out_specs=(P("dp", "seq", None), P("dp", "seq", None), P("dp", "seq"), P("seq", "dp"), P()),
        check_vma=False,
    )
```

time: 59.3 us -> 58 us (0.978)
  matrix products: 16 us -> 7.25 us
  Pallas kernels: 0 us -> 6.97 us
  local copies, waits for them, and re-layouts: 1.2 us -> 5.11 us
  other arithmetic: 4.29 us -> 1.6 us
  waiting for transfers between devices: 13.5 us -> 12.2 us
  starting transfers between devices: 22.5 us -> 23.1 us
    dot_general x11 -> x1, matrix products: 9.12 us -> 0.63 us  [per_device(): jnp.einsum('ns,ds->nd', score_grad.astype(bf16), phi_norm, preferred_elem...]
    pallas_call x0 -> x3, Pallas kernels: none -> 6.97 us  [the longest x1 2.82 us: per_device(): pl.pallas_call(token_sums, grid=(count // rows,), in_specs=[scalar, whole...]
    unnamed x13 -> x17, local copies, waits for them, and re-layouts: 0.58 us -> 5.02 us
    reduce_sum x2 -> x1, other arithmetic: 1.95 us -> 0.14 us  [per_device(): jnp.sum(exp_scores, axis=1, keepdims=True)]
    ppermute x18, waiting for transfers between devices: 12.5 us -> 11 us  [exchange(): return lax.ppermute(value, AXES, pairs)]
    reduce_sum x1, other arithmetic: 0.91 us -> 0.12 us  [per_device(): jnp.sum(phi_f32 * phi_f32, axis=0, keepdims=True) + epsilon]
    ppermute x18, starting transfers between devices: 21.6 us -> 22.3 us  [exchange(): return lax.ppermute(value, AXES, pairs)]
where the time goes in v7:
time: 58 us; the launch traced here: 57.8 us
  starting transfers between devices  23.1 us (40%)
  waiting for transfers between devices  12.2 us (21%)
  matrix products  7.25 us (12%)
  Pallas kernels  6.97 us (12%)
  local copies, waits for them, and re-layouts  5.11 us (9%)
  other arithmetic  1.6 us (3%)
  between operations  1.53 us (3%)
    ppermute x18, starting transfers between devices, exchange(): return lax.ppermute(value, AXES, pairs)  22.3 us
    ppermute x18, waiting for transfers between devices, exchange(): return lax.ppermute(value, AXES, pairs)  11 us
    unnamed x17, local copies, waits for them, and re-layouts  5.02 us
    pallas_call x1, Pallas kernels, per_device(): pl.pallas_call(token_sums, grid=(count // rows,), in_specs=[scalar, whole...  2.82 us
    pallas_call x1, Pallas kernels, per_device(): pl.pallas_call(score_grads, grid=(count // rows,), in_specs=[scalar, whol...  2.62 us
    dot_general x1, matrix products, per_device(): through = jnp.dot(dispatch, slot_dx, preferred_element_type=f32)  1.83 us
    dot_general x1, matrix products, per_device(): mixed = jnp.dot(combine, slot_y, preferred_element_type=f32).astype(bf16)  1.61 us
    dot_general x1, matrix products, per_device(): jnp.einsum('oh,od->hd', hidden, mine_cot, preferred_element_type=f32)  1.59 us
  transfers between devices with their start and end apart: 20, of which 11 were waited for; matrix products, arithmetic and copies ran while one was open for 13% of the time, Pallas kernels for 0%

profile of v7, /device:TPU:0, one launch (start us, length us, event | category | flops | bytes accessed | tf_op | source)
XLA Modules:
  0.0 57.8 jit_solution(13352870431956343242)
XLA Ops:
  1.3 0.9 %copy.13.phi_ref = bf16[1280,2]{1,0:T(8,128)(2,1)S(1)} copy(bf16[1280,2]{0,1:T(2,128)(2,1)} %param.8) | data formatting | bytes 10240 | tf_op args[2]
  2.2 1.3 %copy-done = bf16[1,512,1280]{2,1,0:T(8,128)(2,1)S(1)} copy-done((bf16[1,512,1280]{2,1,0:T(8,128)(2,1)S(1)}, bf16[1,512,1280]{2,1,0:T(8,128)(2,1)}, u32[]{:S(2)}) %copy-start) | copy-done | bytes 1310744
  3.6 1.3 %copy-done.2 = bf16[1,512,1280]{2,1,0:T(8,128)(2,1)S(1)} copy-done((bf16[1,512,1280]{2,1,0:T(8,128)(2,1)S(1)}, bf16[1,512,1280]{2,1,0:T(8,128)(2,1)}, u32[]{:S(2)}) %copy-start.2) | copy-done | bytes 1310744
  4.9 2.8 %token_sums.1 = (f32[2,2688]{1,0:T(2,128)S(1)}, f32[512,2]{1,0:T(8,128)S(1)}, f32[512,1]{1,0:T(8,128)S(1)}) custom-call(f32[1]{0:T(128)S(6)} %copy.21.scale_ref, bf16[1280,2]{1,0:T(8,128)(2,1)S(1)} %copy.13.phi_ref, bf16[512,1280]{1,0:T(8,128)(2,1)S(1)} %bitcast.28, bf16[512,1280]{1,0:T(8,128)(2,1)S(1)} %bitcast.30), custom_call_target="tpu_custom_call" | custom-call | tf_op jit(solution)/shard_map/token_sums/pallas_call | solution.py:205
  7.7 0.5 collective-permute-start
  8.2 0.8 %collective-permute-done = f32[2,2688]{1,0:T(2,128)S(1)} collective-permute-done((f32[2,2688]{1,0:T(2,128)S(1)}, f32[2,2688]{1,0:T(2,128)S(1)}, u32[]{:S(2)}, u32[]{:S(2)}) %collective-permute-start) | collective-permute-done | bytes 21536 | tf_op jit(solution)/shard_map/ppermute | solution.py:29
  9.1 0.1 fusion.9
  9.2 2.8 %collective-permute-start.1 = (f32[1,2,2688]{2,1,0:T(2,128)S(1)}, f32[1,2,2688]{2,1,0:T(2,128)S(1)}, u32[]{:S(2)}, u32[]{:S(2)}) collective-permute-start(f32[1,2,2688]{2,1,0:T(2,128)S(1)} %get-tuple-element.26), channel_id=1, source_target_pairs={{0,9},{1,8},{2,11},{3,10},{4,13},{5,12},{6,15},{7,14},{8,1},{9,0},... | collective-permute-start | bytes 64520 | tf_op jit(solution)/shard_map/ppermute | solution.py:25
  12.0 2.5 %collective-permute-start.2 = (f32[1,2,2688]{2,1,0:T(2,128)S(1)}, f32[1,2,2688]{2,1,0:T(2,128)S(1)}, u32[]{:S(2)}, u32[]{:S(2)}) collective-permute-start(f32[1,2,2688]{2,1,0:T(2,128)S(1)} %get-tuple-element.27), channel_id=1, source_target_pairs={{0,17},{1,16},{2,19},{3,18},{4,21},{5,20},{6,23},{7,22},{8,25},{9,... | collective-permute-start | bytes 64520 | tf_op jit(solution)/shard_map/ppermute | solution.py:25
  14.5 0.1 fusion.21
  14.6 1.7 %collective-permute-done.2 = f32[1,2,2688]{2,1,0:T(2,128)S(1)} collective-permute-done((f32[1,2,2688]{2,1,0:T(2,128)S(1)}, f32[1,2,2688]{2,1,0:T(2,128)S(1)}, u32[]{:S(2)}, u32[]{:S(2)}) %collective-permute-start.2) | collective-permute-done | bytes 21536 | tf_op jit(solution)/shard_map/ppermute | solution.py:25
  16.3 3.2 %collective-permute-done.3 = f32[1,2,2688]{2,1,0:T(2,128)S(1)} collective-permute-done((f32[1,2,2688]{2,1,0:T(2,128)S(1)}, f32[1,2,2688]{2,1,0:T(2,128)S(1)}, u32[]{:S(2)}, u32[]{:S(2)}) %collective-permute-start.3) | collective-permute-done | bytes 21536 | tf_op jit(solution)/shard_map/ppermute | solution.py:25
  19.6 1.4 %collective-permute-start.5 = (f32[1,2,2688]{2,1,0:T(2,128)S(1)}, f32[1,2,2688]{2,1,0:T(2,128)S(1)}, u32[]{:S(2)}, u32[]{:S(2)}) collective-permute-start(f32[1,2,2688]{2,1,0:T(2,128)S(1)} %fusion.12), channel_id=1, source_target_pairs={{0,5},{1,4},{2,7},{3,6},{4,1},{5,0},{6,3},{7,2},{8,13},{9,12},{10,... | collective-permute-start | bytes 64520 | tf_op jit(solution)/shard_map/ppermute | solution.py:25
  20.9 1.4 %collective-permute-start.6 = (f32[1,2,2688]{2,1,0:T(2,128)S(1)}, f32[1,2,2688]{2,1,0:T(2,128)S(1)}, u32[]{:S(2)}, u32[]{:S(2)}) collective-permute-start(f32[1,2,2688]{2,1,0:T(2,128)S(1)} %fusion.12), channel_id=1, source_target_pairs={{0,7},{1,6},{2,5},{3,4},{4,3},{5,2},{6,1},{7,0},{8,15},{9,14},{10,... | collective-permute-start | bytes 64520 | tf_op jit(solution)/shard_map/ppermute | solution.py:25
  22.3 0.3 collective-permute-start.4
  22.6 0.1 reduce_sum.36
  22.8 0.1 reduce
  22.9 2.1 %collective-permute-done.6 = f32[1,2,2688]{2,1,0:T(2,128)S(1)} collective-permute-done((f32[1,2,2688]{2,1,0:T(2,128)S(1)}, f32[1,2,2688]{2,1,0:T(2,128)S(1)}, u32[]{:S(2)}, u32[]{:S(2)}) %collective-permute-start.6) | collective-permute-done | bytes 21536 | tf_op jit(solution)/shard_map/ppermute | solution.py:25
  25.0 0.5 collective-permute-done.4
  25.6 1.4 %copy-done.5 = bf16[640,1280]{1,0:T(8,128)(2,1)S(1)} copy-done((bf16[640,1280]{1,0:T(8,128)(2,1)S(1)}, bf16[640,1280]{1,0:T(8,128)(2,1)}, u32[]{:S(2)}) %copy-start.5) | copy-done | bytes 1638424
  27.0 1.5 %expert_rows.1 = (f32[2,2688]{1,0:T(2,128)S(1)}, bf16[2,1280]{1,0:T(2,128)(2,1)S(1)}, bf16[2,1280]{1,0:T(2,128)(2,1)S(1)}, bf16[2,640]{1,0:T(2,128)(2,1)S(1)}, bf16[2,640]{1,0:T(2,128)(2,1)S(1)}) custom-call(s32[1]{0:T(128)} %bitcast.2.owned_ref, f32[2,2688]{1,0:T(2,128)S(1)} %add_bitcast_fusion.sums_ref, bf16[1280,640]{1,0:T(8,128)(2,1)S(1)} %copy-done.4, ...), custom_call_target="tpu_custom_call" | custom-call | tf_op jit(solution)/shard_map/expert_rows/pallas_call | solution.py:221
  28.5 1.3 %collective-permute-start.8 = (f32[1,2,2688]{2,1,0:T(2,128)S(1)}, f32[1,2,2688]{2,1,0:T(2,128)S(1)}, u32[]{:S(2)}, u32[]{:S(2)}) collective-permute-start(f32[1,2,2688]{2,1,0:T(2,128)S(1)} %bitcast.33), channel_id=1, source_target_pairs={{0,5},{1,4},{2,7},{3,6},{4,1},{5,0},{6,3},{7,2},{8,13},{9,12},{10,... | collective-permute-start | bytes 64520 | tf_op jit(solution)/shard_map/ppermute | solution.py:25
  29.8 0.9 %collective-permute-start.9 = (f32[1,2,2688]{2,1,0:T(2,128)S(1)}, f32[1,2,2688]{2,1,0:T(2,128)S(1)}, u32[]{:S(2)}, u32[]{:S(2)}) collective-permute-start(f32[1,2,2688]{2,1,0:T(2,128)S(1)} %bitcast.34), channel_id=1, source_target_pairs={{0,7},{1,6},{2,5},{3,4},{4,3},{5,2},{6,1},{7,0},{8,15},{9,14},{10,... | collective-permute-start | bytes 64520 | tf_op jit(solution)/shard_map/ppermute | solution.py:25
  30.7 0.8 %collective-permute-start.7 = (f32[1,2,2688]{2,1,0:T(2,128)S(1)}, f32[1,2,2688]{2,1,0:T(2,128)S(1)}, u32[]{:S(2)}, u32[]{:S(2)}) collective-permute-start(f32[1,2,2688]{2,1,0:T(2,128)S(1)} %bitcast.35), channel_id=1, source_target_pairs={{0,3},{1,2},{2,1},{3,0},{4,7},{5,6},{6,5},{7,4},{8,11},{9,10},{10,... | collective-permute-start | bytes 64520 | tf_op jit(solution)/shard_map/ppermute | solution.py:25
  31.5 1.6 %fusion.26 = f32[640,640]{1,0:T(8,128)} fusion(bf16[2,640]{1,0:T(2,128)(2,1)S(1)} %get-tuple-element.21, bf16[2,1280]{1,0:T(2,128)(2,1)S(1)} %get-tuple-element.20, s32[]{:T(128)S(6)} %select_n.86), kind=kOutput, calls=%fused_computation.58 | convolution fusion | flops 1638400 | bytes 1643524 | tf_op jit(solution)/shard_map/od,oh->dh/dot_general | solution.py:240
  33.1 1.6 %fusion.27 = f32[640,640]{1,0:T(8,128)} fusion(bf16[2,640]{1,0:T(2,128)(2,1)S(1)} %get-tuple-element.22, bf16[2,1280]{1,0:T(2,128)(2,1)S(1)} %get-tuple-element.23, s32[]{:T(128)S(6)} %select_n.86), kind=kOutput, calls=%fused_computation.59 | convolution fusion | flops 1638400 | bytes 1643524 | tf_op jit(solution)/shard_map/oh,od->hd/dot_general | solution.py:241
  34.8 0.1 collective-permute-start.12
  34.9 0.7 %collective-permute-start.10 = (f32[1,2,2688]{2,1,0:T(2,128)S(1)}, f32[1,2,2688]{2,1,0:T(2,128)S(1)}, u32[]{:S(2)}, u32[]{:S(2)}) collective-permute-start(f32[1,2,2688]{2,1,0:T(2,128)S(1)} %add_add_fusion), channel_id=1, source_target_pairs={{0,17},{1,16},{2,19},{3,18},{4,21},{5,20},{6,23},{7,22},{8,25},{9,... | collective-permute-start | bytes 64520 | tf_op jit(solution)/shard_map/ppermute | solution.py:25
  35.6 3.3 %collective-permute-start.11 = (f32[1,2,2688]{2,1,0:T(2,128)S(1)}, f32[1,2,2688]{2,1,0:T(2,128)S(1)}, u32[]{:S(2)}, u32[]{:S(2)}) collective-permute-start(f32[1,2,2688]{2,1,0:T(2,128)S(1)} %add_add_fusion), channel_id=1, source_target_pairs={{0,25},{1,24},{2,27},{3,26},{4,29},{5,28},{6,31},{7,30},{8,17},{9,... | collective-permute-start | bytes 64520 | tf_op jit(solution)/shard_map/ppermute | solution.py:25
  38.9 0.1 collective-permute-done.10
  39.0 1.7 %collective-permute-done.11 = f32[1,2,2688]{2,1,0:T(2,128)S(1)} collective-permute-done((f32[1,2,2688]{2,1,0:T(2,128)S(1)}, f32[1,2,2688]{2,1,0:T(2,128)S(1)}, u32[]{:S(2)}, u32[]{:S(2)}) %collective-permute-start.11) | collective-permute-done | bytes 21536 | tf_op jit(solution)/shard_map/ppermute | solution.py:25
  40.8 2.6 %score_grads.1 = (f32[512,2]{1,0:T(8,128)S(1)}, f32[2,1280]{1,0:T(2,128)S(1)}) custom-call(f32[1]{0:T(128)S(6)} %copy.21.scale_ref, f32[2,2688]{1,0:T(2,128)S(1)} %bitcast.32, f32[1,128]{1,0:T(1,128)S(1)} %constant_dynamic-slice_fusion.2.totals_ref, bf16[512,1280]{1,0:T(8,128)(2,1)S(1)} %bitcast.29, bf16[512,1280]{1,0:T(8,128)(2,1)S(1)} %bitcast.31, ...), custom_call_target="tpu_custom_call" | custom-call | tf_op jit(solution)/shard_map/score_grads/pallas_call | solution.py:242
  43.5 0.2 collective-permute-start.13
  43.7 0.6 %multiply_reduce_fusion = (f32[512]{0:T(512)S(1)}, f32[512,1280]{1,0:T(8,128)S(1)}) fusion(f32[512]{0:T(512)S(1)} %reduce, bf16[1,512,1280]{2,1,0:T(8,128)(2,1)S(1)} %copy-done.1, bf16[1280,2]{0,1:T(2,128)(2,1)S(1)} %copy-done.6, f32[2]{0:T(128)S(1)} %add_rsqrt_fusion, f32[512,2]{1,0:T(8,128)S(1)} %get-tuple-element.19), kind=kOutput, calls=%fused_computation.5 | convolution fusion | flops 5251072 | bytes 3945480 | tf_op jit(solution)/shard_map/ns,ds->nd/dot_general | solution.py:273
  44.4 0.4 collective-permute-done.13
  44.8 1.4 %collective-permute-start.15 = (f32[1,1,2560]{2,1,0:T(1,128)S(1)}, f32[1,1,2560]{2,1,0:T(1,128)S(1)}, u32[]{:S(2)}, u32[]{:S(2)}) collective-permute-start(f32[1,1,2560]{2,1,0:T(1,128)S(1)} %fusion.22), channel_id=1, source_target_pairs={{0,5},{1,4},{2,7},{3,6},{4,1},{5,0},{6,3},{7,2},{8,13},{9,12},{10,... | collective-permute-start | bytes 30728 | tf_op jit(solution)/shard_map/ppermute | solution.py:25
  46.1 1.1 %collective-permute-start.16 = (f32[1,1,2560]{2,1,0:T(1,128)S(1)}, f32[1,1,2560]{2,1,0:T(1,128)S(1)}, u32[]{:S(2)}, u32[]{:S(2)}) collective-permute-start(f32[1,1,2560]{2,1,0:T(1,128)S(1)} %fusion.22), channel_id=1, source_target_pairs={{0,7},{1,6},{2,5},{3,4},{4,3},{5,2},{6,1},{7,0},{8,15},{9,14},{10,... | collective-permute-start | bytes 30728 | tf_op jit(solution)/shard_map/ppermute | solution.py:25
  47.2 0.6 %collective-permute-start.14 = (f32[1,1,2560]{2,1,0:T(1,128)S(1)}, f32[1,1,2560]{2,1,0:T(1,128)S(1)}, u32[]{:S(2)}, u32[]{:S(2)}) collective-permute-start(f32[1,1,2560]{2,1,0:T(1,128)S(1)} %fusion.22), channel_id=1, source_target_pairs={{0,3},{1,2},{2,1},{3,0},{4,7},{5,6},{6,5},{7,4},{8,11},{9,10},{10,... | collective-permute-start | bytes 30728 | tf_op jit(solution)/shard_map/ppermute | solution.py:25
  47.8 1.8 %fusion.1 = bf16[1,512,1280]{2,1,0:T(8,128)(2,1)} fusion(f32[512,1280]{1,0:T(8,128)S(1)} %get-tuple-element.31, f32[512]{0:T(512)S(1)} %get-tuple-element.30, f32[512]{0:T(512)S(1)} %reduce, f32[512,2]{1,0:T(8,128)S(1)} %get-tuple-element.15.exp_ref, f32[2]{0:T(128)S(1)} %slice_bitcast_fusion, bf16[2,2688]{1,0:T(2,128)(2,1)S(1)} %bitcast.36, ...), kind=kOutput, calls=%fused_computation.3 | convolution fusion | flops 7211008 | bytes 5514752 | tf_op jit(solution)/shard_map/dot_general | solution.py:276
  49.6 0.5 collective-permute-done.16
  50.1 0.2 collective-permute-done.14
  50.3 0.3 collective-permute-start.18
  50.6 3.1 %collective-permute-start.19 = (f32[1,1,2560]{2,1,0:T(1,128)S(1)}, f32[1,1,2560]{2,1,0:T(1,128)S(1)}, u32[]{:S(2)}, u32[]{:S(2)}) collective-permute-start(f32[1,1,2560]{2,1,0:T(1,128)S(1)} %add_add_fusion.1), channel_id=1, source_target_pairs={{0,25},{1,24},{2,27},{3,26},{4,29},{5,28},{6,31},{7,30},{8,17},{9,... | collective-permute-start | bytes 30728 | tf_op jit(solution)/shard_map/ppermute | solution.py:25
  53.7 0.4 collective-permute-start.17
  54.2 1.6 %fusion.2 = bf16[1,512,1280]{2,1,0:T(8,128)(2,1)} fusion(f32[512,2]{1,0:T(8,128)S(1)} %get-tuple-element.15.exp_ref, f32[512]{0:T(512)S(1)} %reduce_sum.36, bf16[2,2688]{1,0:T(2,128)(2,1)S(1)} %bitcast.37), kind=kOutput, calls=%fused_computation.4 | convolution fusion | flops 3278848 | bytes 1580032 | tf_op jit(solution)/shard_map/dot_general | solution.py:272
  55.8 1.0 %collective-permute-done.17 = f32[1,1,2560]{2,1,0:T(1,128)S(1)} collective-permute-done((f32[1,1,2560]{2,1,0:T(1,128)S(1)}, f32[1,1,2560]{2,1,0:T(1,128)S(1)}, u32[]{:S(2)}, u32[]{:S(2)}) %collective-permute-start.17) | collective-permute-done | bytes 10272 | tf_op jit(solution)/shard_map/ppermute | solution.py:25
  56.9 0.2 fusion.18
  57.1 0.7 %fusion.20 = f32[1280,2]{0,1:T(2,128)} fusion(bf16[1280,2]{0,1:T(2,128)(2,1)S(1)} %copy-done.6, f32[2,1280]{1,0:T(2,128)S(1)} %reshape.38, f32[2]{0:T(128)S(1)} %fusion.18, f32[2]{0:T(128)S(1)} %add_rsqrt_fusion), kind=kLoop, calls=%fused_computation.48 | loop fusion | flops 12800 | bytes 25616 | tf_op jit(solution)/shard_map/mul | solution.py:282
  (41 shorter events, 0.4 us)
Async XLA Ops:
  0.6 13.9 %copy-start.6 = (bf16[1280,2]{0,1:T(2,128)(2,1)S(1)}, bf16[1280,2]{0,1:T(2,128)(2,1)}, u32[]{:S(2)}) copy-start(bf16[1280,2]{0,1:T(2,128)(2,1)} %param.8) | copy-start | bytes 15364
  2.2 1.3 %copy-start = (bf16[1,512,1280]{2,1,0:T(8,128)(2,1)S(1)}, bf16[1,512,1280]{2,1,0:T(8,128)(2,1)}, u32[]{:S(2)}) copy-start(bf16[1,512,1280]{2,1,0:T(8,128)(2,1)} %param.6) | copy-start | bytes 3932164
  3.6 1.3 %copy-start.2 = (bf16[1,512,1280]{2,1,0:T(8,128)(2,1)S(1)}, bf16[1,512,1280]{2,1,0:T(8,128)(2,1)}, u32[]{:S(2)}) copy-start(bf16[1,512,1280]{2,1,0:T(8,128)(2,1)} %param.7) | copy-start | bytes 3932164
  4.9 20.7 %copy-start.4 = (bf16[1280,640]{1,0:T(8,128)(2,1)S(1)}, bf16[1280,640]{1,0:T(8,128)(2,1)}, u32[]{:S(2)}) copy-start(bf16[1280,640]{1,0:T(8,128)(2,1)} %in_ref.1) | copy-start | bytes 4915204
  7.7 1.3 %collective-permute-start = (f32[2,2688]{1,0:T(2,128)S(1)}, f32[2,2688]{1,0:T(2,128)S(1)}, u32[]{:S(2)}, u32[]{:S(2)}) collective-permute-start(f32[2,2688]{1,0:T(2,128)S(1)} %get-tuple-element.16), channel_id=1, source_target_pairs={{0,1},{1,0},{2,3},{3,2},{4,5},{5,4},{6,7},{7,6},{8,9},{9,8},{10,11... | collective-permute-start | bytes 64520 | tf_op jit(solution)/shard_map/ppermute | solution.py:29
  9.2 5.4 %collective-permute-start.1 = (f32[1,2,2688]{2,1,0:T(2,128)S(1)}, f32[1,2,2688]{2,1,0:T(2,128)S(1)}, u32[]{:S(2)}, u32[]{:S(2)}) collective-permute-start(f32[1,2,2688]{2,1,0:T(2,128)S(1)} %get-tuple-element.26), channel_id=1, source_target_pairs={{0,9},{1,8},{2,11},{3,10},{4,13},{5,12},{6,15},{7,14},{8,1},{9,0},... | collective-permute-start | bytes 64520 | tf_op jit(solution)/shard_map/ppermute | solution.py:25
  12.0 4.3 %collective-permute-start.2 = (f32[1,2,2688]{2,1,0:T(2,128)S(1)}, f32[1,2,2688]{2,1,0:T(2,128)S(1)}, u32[]{:S(2)}, u32[]{:S(2)}) collective-permute-start(f32[1,2,2688]{2,1,0:T(2,128)S(1)} %get-tuple-element.27), channel_id=1, source_target_pairs={{0,17},{1,16},{2,19},{3,18},{4,21},{5,20},{6,23},{7,22},{8,25},{9,... | collective-permute-start | bytes 64520 | tf_op jit(solution)/shard_map/ppermute | solution.py:25
  14.5 5.0 %collective-permute-start.3 = (f32[1,2,2688]{2,1,0:T(2,128)S(1)}, f32[1,2,2688]{2,1,0:T(2,128)S(1)}, u32[]{:S(2)}, u32[]{:S(2)}) collective-permute-start(f32[1,2,2688]{2,1,0:T(2,128)S(1)} %get-tuple-element.25), channel_id=1, source_target_pairs={{0,25},{1,24},{2,27},{3,26},{4,29},{5,28},{6,31},{7,30},{8,17},{9,... | collective-permute-start | bytes 64520 | tf_op jit(solution)/shard_map/ppermute | solution.py:25
  19.6 3.4 %collective-permute-start.5 = (f32[1,2,2688]{2,1,0:T(2,128)S(1)}, f32[1,2,2688]{2,1,0:T(2,128)S(1)}, u32[]{:S(2)}, u32[]{:S(2)}) collective-permute-start(f32[1,2,2688]{2,1,0:T(2,128)S(1)} %fusion.12), channel_id=1, source_target_pairs={{0,5},{1,4},{2,7},{3,6},{4,1},{5,0},{6,3},{7,2},{8,13},{9,12},{10,... | collective-permute-start | bytes 64520 | tf_op jit(solution)/shard_map/ppermute | solution.py:25
  20.9 4.1 %collective-permute-start.6 = (f32[1,2,2688]{2,1,0:T(2,128)S(1)}, f32[1,2,2688]{2,1,0:T(2,128)S(1)}, u32[]{:S(2)}, u32[]{:S(2)}) collective-permute-start(f32[1,2,2688]{2,1,0:T(2,128)S(1)} %fusion.12), channel_id=1, source_target_pairs={{0,7},{1,6},{2,5},{3,4},{4,3},{5,2},{6,1},{7,0},{8,15},{9,14},{10,... | collective-permute-start | bytes 64520 | tf_op jit(solution)/shard_map/ppermute | solution.py:25
  22.3 3.2 %collective-permute-start.4 = (f32[1,2,2688]{2,1,0:T(2,128)S(1)}, f32[1,2,2688]{2,1,0:T(2,128)S(1)}, u32[]{:S(2)}, u32[]{:S(2)}) collective-permute-start(f32[1,2,2688]{2,1,0:T(2,128)S(1)} %fusion.12), channel_id=1, source_target_pairs={{0,3},{1,2},{2,1},{3,0},{4,7},{5,6},{6,5},{7,4},{8,11},{9,10},{10,... | collective-permute-start | bytes 64520 | tf_op jit(solution)/shard_map/ppermute | solution.py:25
  25.6 1.4 %copy-start.5 = (bf16[640,1280]{1,0:T(8,128)(2,1)S(1)}, bf16[640,1280]{1,0:T(8,128)(2,1)}, u32[]{:S(2)}) copy-start(bf16[640,1280]{1,0:T(8,128)(2,1)} %out_ref.1) | copy-start | bytes 4915204
  28.5 12.3 %copy-start.1 = (bf16[1,512,1280]{2,1,0:T(8,128)(2,1)S(1)}, bf16[1,512,1280]{2,1,0:T(8,128)(2,1)}, u32[]{:S(2)}) copy-start(bf16[1,512,1280]{2,1,0:T(8,128)(2,1)} %param.6) | copy-start | bytes 3932164
  28.5 12.3 %copy-start.3 = (bf16[1,512,1280]{2,1,0:T(8,128)(2,1)S(1)}, bf16[1,512,1280]{2,1,0:T(8,128)(2,1)}, u32[]{:S(2)}) copy-start(bf16[1,512,1280]{2,1,0:T(8,128)(2,1)} %param.7) | copy-start | bytes 3932164
  28.5 6.2 %collective-permute-start.8 = (f32[1,2,2688]{2,1,0:T(2,128)S(1)}, f32[1,2,2688]{2,1,0:T(2,128)S(1)}, u32[]{:S(2)}, u32[]{:S(2)}) collective-permute-start(f32[1,2,2688]{2,1,0:T(2,128)S(1)} %bitcast.33), channel_id=1, source_target_pairs={{0,5},{1,4},{2,7},{3,6},{4,1},{5,0},{6,3},{7,2},{8,13},{9,12},{10,... | collective-permute-start | bytes 64520 | tf_op jit(solution)/shard_map/ppermute | solution.py:25
  29.8 4.9 %collective-permute-start.9 = (f32[1,2,2688]{2,1,0:T(2,128)S(1)}, f32[1,2,2688]{2,1,0:T(2,128)S(1)}, u32[]{:S(2)}, u32[]{:S(2)}) collective-permute-start(f32[1,2,2688]{2,1,0:T(2,128)S(1)} %bitcast.34), channel_id=1, source_target_pairs={{0,7},{1,6},{2,5},{3,4},{4,3},{5,2},{6,1},{7,0},{8,15},{9,14},{10,... | collective-permute-start | bytes 64520 | tf_op jit(solution)/shard_map/ppermute | solution.py:25
  30.7 4.0 %collective-permute-start.7 = (f32[1,2,2688]{2,1,0:T(2,128)S(1)}, f32[1,2,2688]{2,1,0:T(2,128)S(1)}, u32[]{:S(2)}, u32[]{:S(2)}) collective-permute-start(f32[1,2,2688]{2,1,0:T(2,128)S(1)} %bitcast.35), channel_id=1, source_target_pairs={{0,3},{1,2},{2,1},{3,0},{4,7},{5,6},{6,5},{7,4},{8,11},{9,10},{10,... | collective-permute-start | bytes 64520 | tf_op jit(solution)/shard_map/ppermute | solution.py:25
  34.8 4.1 %collective-permute-start.12 = (f32[1,2,2688]{2,1,0:T(2,128)S(1)}, f32[1,2,2688]{2,1,0:T(2,128)S(1)}, u32[]{:S(2)}, u32[]{:S(2)}) collective-permute-start(f32[1,2,2688]{2,1,0:T(2,128)S(1)} %add_add_fusion), channel_id=1, source_target_pairs={{0,9},{1,8},{2,11},{3,10},{4,13},{5,12},{6,15},{7,14},{8,1},{9,0},... | collective-permute-start | bytes 64520 | tf_op jit(solution)/shard_map/ppermute | solution.py:25
  34.9 4.2 %collective-permute-start.10 = (f32[1,2,2688]{2,1,0:T(2,128)S(1)}, f32[1,2,2688]{2,1,0:T(2,128)S(1)}, u32[]{:S(2)}, u32[]{:S(2)}) collective-permute-start(f32[1,2,2688]{2,1,0:T(2,128)S(1)} %add_add_fusion), channel_id=1, source_target_pairs={{0,17},{1,16},{2,19},{3,18},{4,21},{5,20},{6,23},{7,22},{8,25},{9,... | collective-permute-start | bytes 64520 | tf_op jit(solution)/shard_map/ppermute | solution.py:25
  35.6 5.1 %collective-permute-start.11 = (f32[1,2,2688]{2,1,0:T(2,128)S(1)}, f32[1,2,2688]{2,1,0:T(2,128)S(1)}, u32[]{:S(2)}, u32[]{:S(2)}) collective-permute-start(f32[1,2,2688]{2,1,0:T(2,128)S(1)} %add_add_fusion), channel_id=1, source_target_pairs={{0,25},{1,24},{2,27},{3,26},{4,29},{5,28},{6,31},{7,30},{8,17},{9,... | collective-permute-start | bytes 64520 | tf_op jit(solution)/shard_map/ppermute | solution.py:25
  43.5 1.2 %collective-permute-start.13 = (f32[1,1,2560]{2,1,0:T(1,128)S(1)}, f32[1,1,2560]{2,1,0:T(1,128)S(1)}, u32[]{:S(2)}, u32[]{:S(2)}) collective-permute-start(f32[1,1,2560]{2,1,0:T(1,128)S(1)} %reshape.37), channel_id=1, source_target_pairs={{0,1},{1,0},{2,3},{3,2},{4,5},{5,4},{6,7},{7,6},{8,9},{9,8},{10,11... | collective-permute-start | bytes 30728 | tf_op jit(solution)/shard_map/ppermute | solution.py:29
  44.8 4.9 %collective-permute-start.15 = (f32[1,1,2560]{2,1,0:T(1,128)S(1)}, f32[1,1,2560]{2,1,0:T(1,128)S(1)}, u32[]{:S(2)}, u32[]{:S(2)}) collective-permute-start(f32[1,1,2560]{2,1,0:T(1,128)S(1)} %fusion.22), channel_id=1, source_target_pairs={{0,5},{1,4},{2,7},{3,6},{4,1},{5,0},{6,3},{7,2},{8,13},{9,12},{10,... | collective-permute-start | bytes 30728 | tf_op jit(solution)/shard_map/ppermute | solution.py:25
  46.1 4.0 %collective-permute-start.16 = (f32[1,1,2560]{2,1,0:T(1,128)S(1)}, f32[1,1,2560]{2,1,0:T(1,128)S(1)}, u32[]{:S(2)}, u32[]{:S(2)}) collective-permute-start(f32[1,1,2560]{2,1,0:T(1,128)S(1)} %fusion.22), channel_id=1, source_target_pairs={{0,7},{1,6},{2,5},{3,4},{4,3},{5,2},{6,1},{7,0},{8,15},{9,14},{10,... | collective-permute-start | bytes 30728 | tf_op jit(solution)/shard_map/ppermute | solution.py:25
  47.2 3.1 %collective-permute-start.14 = (f32[1,1,2560]{2,1,0:T(1,128)S(1)}, f32[1,1,2560]{2,1,0:T(1,128)S(1)}, u32[]{:S(2)}, u32[]{:S(2)}) collective-permute-start(f32[1,1,2560]{2,1,0:T(1,128)S(1)} %fusion.22), channel_id=1, source_target_pairs={{0,3},{1,2},{2,1},{3,0},{4,7},{5,6},{6,5},{7,4},{8,11},{9,10},{10,... | collective-permute-start | bytes 30728 | tf_op jit(solution)/shard_map/ppermute | solution.py:25
  50.3 5.5 %collective-permute-start.18 = (f32[1,1,2560]{2,1,0:T(1,128)S(1)}, f32[1,1,2560]{2,1,0:T(1,128)S(1)}, u32[]{:S(2)}, u32[]{:S(2)}) collective-permute-start(f32[1,1,2560]{2,1,0:T(1,128)S(1)} %add_add_fusion.1), channel_id=1, source_target_pairs={{0,17},{1,16},{2,19},{3,18},{4,21},{5,20},{6,23},{7,22},{8,25},{9,... | collective-permute-start | bytes 30728 | tf_op jit(solution)/shard_map/ppermute | solution.py:25
  50.6 5.2 %collective-permute-start.19 = (f32[1,1,2560]{2,1,0:T(1,128)S(1)}, f32[1,1,2560]{2,1,0:T(1,128)S(1)}, u32[]{:S(2)}, u32[]{:S(2)}) collective-permute-start(f32[1,1,2560]{2,1,0:T(1,128)S(1)} %add_add_fusion.1), channel_id=1, source_target_pairs={{0,25},{1,24},{2,27},{3,26},{4,29},{5,28},{6,31},{7,30},{8,17},{9,... | collective-permute-start | bytes 30728 | tf_op jit(solution)/shard_map/ppermute | solution.py:25
  53.7 3.1 %collective-permute-start.17 = (f32[1,1,2560]{2,1,0:T(1,128)S(1)}, f32[1,1,2560]{2,1,0:T(1,128)S(1)}, u32[]{:S(2)}, u32[]{:S(2)}) collective-permute-start(f32[1,1,2560]{2,1,0:T(1,128)S(1)} %add_add_fusion.1), channel_id=1, source_target_pairs={{0,9},{1,8},{2,11},{3,10},{4,13},{5,12},{6,15},{7,14},{8,1},{9,0},... | collective-permute-start | bytes 30728 | tf_op jit(solution)/shard_map/ppermute | solution.py:25

commit v8 on v7

v8 whole, which is shorter than its diff:
```python
import jax
import jax.numpy as jnp
from jax import lax
from jax.experimental import pallas as pl
from jax.experimental.pallas import tpu as pltpu
from jax.sharding import PartitionSpec as P

epsilon = 1e-06
AXES = ("seq", "dp")
LANES = 128
PIECES = 4
VMEM_BYTES = 20 * 2**20
ROWS = (((1,), (1,)), ((), ()))
COLUMNS = (((0,), (0,)), ((), ()))
f32, bf16 = jnp.float32, jnp.bfloat16


def exchange(value, mask):
    clips = lax.axis_size("dp")
    pairs = []
    for place in range(lax.axis_size("seq")):
        for clip in range(clips):
            there = (place ^ mask) * clips + (clip ^ 1 if clips % 2 == 0 else clip)
            pairs.append((place * clips + clip, there))
    return lax.ppermute(value, AXES, pairs)


def hop(value, step):
    return lax.ppermute(value, "dp", [(i, i ^ step) for i in range(lax.axis_size("dp"))])


def of_clips(value):
    clips = lax.axis_size("dp")
    clip = lax.axis_index("dp")
    got = [value] + [hop(value, step) for step in range(1, clips)]
    ordered = []
    for index in range(clips):
        picked = got[0]
        for step in range(1, clips):
            picked = jnp.where(clip ^ step == index, got[step], picked)
        ordered.append(picked)
    return ordered


def rounds(size):
    masks = [1 << bit for bit in range(size.bit_length() - 1)]
    return [masks[i : i + 2] for i in range(0, len(masks), 2)]


def round_masks(pair):
    return pair if len(pair) == 1 else [pair[0], pair[1], pair[0] | pair[1]]


def sum_to_owner(value, group):
    place = lax.axis_index("seq")
    for pair in reversed(rounds(lax.axis_size("seq"))):
        owner_masks = [mask for mask in pair if mask >= group]
        blocks = value.reshape((1 << len(owner_masks), -1) + value.shape[1:])

        def block_for(mask):
            index = 0
            for bit, owner_mask in enumerate(owner_masks):
                index = index + jnp.where((place ^ mask) & owner_mask != 0, 1 << bit, 0)
            return lax.dynamic_index_in_dim(blocks, index, 0, keepdims=False)

        got = [block_for(0)] + [exchange(block_for(mask), mask) for mask in round_masks(pair)]
        value = got[0] + got[1] if len(got) == 2 else (got[0] + got[1]) + (got[2] + got[3])
    return value


def sum_to_all(value, group, later=()):
    place = lax.axis_index("seq")
    for pair in rounds(lax.axis_size("seq")):
        terms = {0: value}
        for mask in round_masks(pair):
            terms[mask] = exchange(value, mask)
        for mask in pair:
            upper = (place & mask) != 0
            merged = {}
            for key in terms:
                if key & mask:
                    continue
                near, far = terms[key], terms[key | mask]
                if mask < group:
                    merged[key] = near + far
                else:
                    merged[key] = jnp.where(
                        upper, jnp.concatenate([far, near]), jnp.concatenate([near, far])
                    )
            terms = merged
        value = terms[0]
        if later and pair[0] == 1:
            value, *later = lax.optimization_barrier((value, *later))
    return (value, *later) if later else value


def token_sums(scale_ref, phi_ref, tok_ref, cot_ref, message_ref, exp_ref, combine_ref, tok_scale_ref, norm_ref, tok_buf, cot_buf, sems):
    experts, width = phi_ref.shape
    blocks = sems.shape[1]
    rows = tok_buf.shape[0] // blocks
    pieces = [pl.ds(index * rows, rows) for index in range(blocks)]
    tok_copies = [
        pltpu.make_async_copy(tok_ref.at[piece], tok_buf.at[piece], sems.at[0, index])
        for index, piece in enumerate(pieces)
    ]
    cot_copies = [
        pltpu.make_async_copy(cot_ref.at[piece], cot_buf.at[piece], sems.at[1, index])
        for index, piece in enumerate(pieces)
    ]
    for copy in tok_copies + cot_copies:
        copy.start()
    phi = phi_ref[...].astype(f32)
    phi_scale = lax.rsqrt(jnp.sum(phi * phi, axis=1, keepdims=True) + epsilon)
    phi_norm = (phi * phi_scale).astype(bf16)
    for copy, piece in zip(tok_copies, pieces):
        copy.wait()
        tok_f32 = tok_buf[piece, :].astype(f32)
        tok_scale = lax.rsqrt(jnp.sum(tok_f32 * tok_f32, axis=1, keepdims=True) + epsilon)
        norm_ref[piece, :] = (tok_f32 * tok_scale).astype(bf16)
        tok_scale_ref[piece, :] = tok_scale
    logits = scale_ref[0] * lax.dot_general(phi_norm, norm_ref[...], ROWS, preferred_element_type=f32)
    exp_scores = jnp.exp(logits)
    combine = (exp_scores / jnp.sum(exp_scores, axis=0, keepdims=True)).astype(bf16)
    exp_high = exp_scores.astype(bf16).astype(f32)
    halves = jnp.concatenate([exp_high, exp_scores - exp_high], axis=0).astype(bf16)
    in_parts = jnp.dot(halves, tok_buf[...], preferred_element_type=f32)
    message_ref[:, :width] = in_parts[:experts] + in_parts[experts:]
    spare = message_ref.shape[1] - 2 * width
    total = as_row(jnp.sum(exp_scores, axis=1, keepdims=True), spare)
    message_ref[:, 2 * width :] = jnp.broadcast_to(total, (experts, spare))
    exp_ref[...] = exp_scores
    combine_ref[...] = combine
    for copy in cot_copies:
        copy.wait()
    message_ref[:, width : 2 * width] = jnp.dot(combine, cot_buf[...], preferred_element_type=f32)


def expert_rows(owned_ref, sums_ref, in_ref, out_ref, message_ref, row_x_ref, row_cot_ref, hidden_ref, pre_grad_ref):
    width, units = in_ref.shape
    spare = sums_ref[:, 2 * width :]
    lane = lax.broadcasted_iota(jnp.int32, spare.shape, 1)
    own_total = jnp.sum(jnp.where(lane == owned_ref[0], spare, 0.0), axis=1, keepdims=True)
    own_in = sums_ref[:, :width] / own_total
    row_x = own_in.astype(bf16)
    row_cot = sums_ref[:, width : 2 * width].astype(bf16)
    pre_act = jnp.dot(row_x, in_ref[...], preferred_element_type=f32)
    hid_grad = lax.dot_general(row_cot, out_ref[...], ROWS, preferred_element_type=f32)
    cdf = 0.5 * (1.0 + lax.erf(pre_act * 0.7071067811865476))
    hidden = (pre_act * cdf).astype(bf16)
    slope = cdf + pre_act * jnp.exp(-0.5 * pre_act * pre_act) * 0.3989422804014327
    pre_grad = (hid_grad * slope).astype(bf16)
    part_out = jnp.dot(hidden, out_ref[...], preferred_element_type=f32)
    part_dx = lax.dot_general(pre_grad, in_ref[...], ROWS, preferred_element_type=f32)
    message_ref[:, :width] = part_out
    message_ref[:, width : 2 * width] = part_dx
    dot_part = jnp.sum(own_in * part_dx, axis=1, keepdims=True)
    message_ref[:, 2 * width :] = jnp.broadcast_to(dot_part, spare.shape)
    row_x_ref[...] = row_x
    row_cot_ref[...] = row_cot
    hidden_ref[...] = hidden
    pre_grad_ref[...] = pre_grad


def as_row(column, lanes):
    shape = (column.shape[0], lanes)
    same = lax.broadcasted_iota(jnp.int32, shape, 0) == lax.broadcasted_iota(jnp.int32, shape, 1)
    return jnp.sum(jnp.where(same, column, 0.0), axis=0, keepdims=True)


def as_column(row, slots):
    shape = (slots, row.shape[1])
    same = lax.broadcasted_iota(jnp.int32, shape, 0) == lax.broadcasted_iota(jnp.int32, shape, 1)
    return jnp.sum(jnp.where(same, row, 0.0), axis=1, keepdims=True)


def score_grads(scale_ref, slots_ref, totals_ref, tok_ref, cot_ref, norm_ref, exp_ref, grad_ref, dispatch_ref, phi_ref):
    width = tok_ref.shape[1]
    slot_y = slots_ref[:, :width].astype(bf16)
    slot_dx = slots_ref[:, width : 2 * width].astype(bf16)
    column_stat = slots_ref[:, 2 * width : 2 * width + 1]
    totals = as_column(totals_ref[...], slot_y.shape[0])
    exp_scores = exp_ref[...]
    combine_f = exp_scores / jnp.sum(exp_scores, axis=0, keepdims=True)
    comb_dot = lax.dot_general(slot_y, cot_ref[...], ROWS, preferred_element_type=f32)
    grad_comb = combine_f * (comb_dot - jnp.sum(combine_f * comb_dot, axis=0, keepdims=True))
    disp_dot = lax.dot_general(slot_dx, tok_ref[...], ROWS, preferred_element_type=f32)
    dispatch_f = exp_scores / totals
    grad_disp = dispatch_f * (disp_dot - column_stat)
    score_grad = (scale_ref[0] * (grad_comb + grad_disp)).astype(bf16)
    phi_ref[...] = jnp.dot(score_grad, norm_ref[...], preferred_element_type=f32)
    grad_ref[...] = score_grad
    dispatch_ref[...] = dispatch_f.astype(bf16)


def per_device(tokens, cotangent, router, logit_scale, expert_in, expert_out):
    tok_in = tokens[0]
    tok_cot = cotangent[0]
    count = tok_in.shape[0]
    width, experts = router.shape
    units = expert_in.shape[1]
    size = lax.axis_size("seq")
    group = size // experts
    clips = lax.axis_size("dp")
    clip = lax.axis_index("dp")
    owned = lax.axis_index("seq") // group
    length = 2 * width + -(-experts // LANES) * LANES
    scalar = pl.BlockSpec(memory_space=pltpu.SMEM)
    in_vmem = pl.BlockSpec(memory_space=pltpu.VMEM)
    in_hbm = pl.BlockSpec(memory_space=pltpu.HBM)
    params = pltpu.CompilerParams(vmem_limit_bytes=VMEM_BYTES)
    phi = router.T
    message, exp_scores, combine, tok_scale, tok_norm = pl.pallas_call(
        token_sums,
        in_specs=[scalar, in_vmem, in_hbm, in_hbm],
        out_shape=[
            jax.ShapeDtypeStruct((experts, length), f32),
            jax.ShapeDtypeStruct((experts, count), f32),
            jax.ShapeDtypeStruct((experts, count), bf16),
            jax.ShapeDtypeStruct((count, 1), f32),
            jax.ShapeDtypeStruct((count, width), bf16),
        ],
        scratch_shapes=[
            pltpu.VMEM((count, width), bf16),
            pltpu.VMEM((count, width), bf16),
            pltpu.SemaphoreType.DMA((2, PIECES)),
        ],
        compiler_params=params,
        name="token_sums",
    )(logit_scale, phi, *[pltpu.with_memory_space_constraint(x, pltpu.HBM) for x in (tok_in, tok_cot)])
    message = sum_to_owner(jnp.stack(of_clips(message), axis=1), group)[0]
    totals = message[:, 2 * width :]
    message, row_x, row_cot, hidden, pre_grad = pl.pallas_call(
        expert_rows,
        in_specs=[scalar] + [in_vmem] * 3,
        out_shape=[
            jax.ShapeDtypeStruct((clips, length), f32),
            jax.ShapeDtypeStruct((clips, width), bf16),
            jax.ShapeDtypeStruct((clips, width), bf16),
            jax.ShapeDtypeStruct((clips, units), bf16),
            jax.ShapeDtypeStruct((clips, units), bf16),
        ],
        compiler_params=params,
        name="expert_rows",
    )(owned[None], message, expert_in, expert_out)
    message, hidden, row_cot = sum_to_all(message[None], group, (hidden, row_cot))
    slots = lax.dynamic_index_in_dim(message, clip, 1, keepdims=False)
    totals = lax.dynamic_index_in_dim(totals, clip, 0, keepdims=True)
    share = width // clips
    mine_x = lax.dynamic_slice_in_dim(row_x, clip * share, share, 1)
    mine_cot = lax.dynamic_slice_in_dim(row_cot, clip * share, share, 1)
    grad_expert_in = jnp.einsum("od,oh->dh", mine_x, pre_grad, preferred_element_type=f32)
    grad_expert_out = jnp.einsum("oh,od->hd", hidden, mine_cot, preferred_element_type=f32)
    score_grad, dispatch, phi_part = pl.pallas_call(
        score_grads,
        in_specs=[scalar] + [in_vmem] * 6,
        out_shape=[
            jax.ShapeDtypeStruct((experts, count), bf16),
            jax.ShapeDtypeStruct((experts, count), bf16),
            jax.ShapeDtypeStruct((experts, width), f32),
        ],
        compiler_params=params,
        name="score_grads",
    )(logit_scale, slots, totals, tok_in, tok_cot, tok_norm, exp_scores)
    phi_flat = sum(of_clips(phi_part.reshape(1, 1, -1)))
    phi_grad = sum_to_all(phi_flat, size).reshape(experts, width)
    phi_f32 = phi.astype(f32)
    phi_scale = lax.rsqrt(jnp.sum(phi_f32 * phi_f32, axis=1, keepdims=True) + epsilon)
    phi_unit = phi_f32 * phi_scale
    phi_norm = phi_unit.astype(bf16)
    slot_y = slots[:, :width].astype(bf16)
    slot_dx = slots[:, width : 2 * width].astype(bf16)
    mixed = jnp.einsum("sn,sd->nd", combine, slot_y, preferred_element_type=f32).astype(bf16)
    norm_grad = jnp.einsum("sn,sd->nd", score_grad, phi_norm, preferred_element_type=f32)
    through = jnp.einsum("sn,sd->nd", dispatch, slot_dx, preferred_element_type=f32)
    tok_unit = tok_in.astype(f32) * tok_scale
    back_norm = tok_scale * (
        norm_grad - tok_unit * jnp.sum(tok_unit * norm_grad, axis=1, keepdims=True)
    )
    grad_tokens = (through + back_norm).astype(bf16)
    grad_router = phi_scale * (
        phi_grad - phi_unit * jnp.sum(phi_unit * phi_grad, axis=1, keepdims=True)
    )
    return (mixed[None], grad_tokens[None], grad_expert_in, grad_expert_out, grad_router.T)


def solution(mesh):
    return jax.shard_map(
        per_device,
        mesh=mesh,
        in_specs=(
            P("dp", "seq", None),
            P("dp", "seq", None),
            P(),
            P(),
            P(None, "seq"),
            P("seq", None),
        ),
        out_specs=(P("dp", "seq", None), P("dp", "seq", None), P("dp", "seq"), P("seq", "dp"), P()),
        check_vma=False,
    )
```

time: 58 us -> 59.7 us (1.029)
  other arithmetic: 1.6 us -> 5.68 us
  local copies, waits for them, and re-layouts: 5.11 us -> 2.63 us
  waiting for transfers between devices: 12.2 us -> 13.7 us
  Pallas kernels: 6.97 us -> 5.86 us
  starting transfers between devices: 23.1 us -> 22.3 us
    unnamed x17 -> x22, local copies, waits for them, and re-layouts: 5.02 us -> 2.54 us
    add x1, other arithmetic: 0.04 us -> 1.44 us  [sum_to_owner(): got[0] + got[1] + (got[2] + got[3])]
    ppermute x18, waiting for transfers between devices: 11 us -> 12.4 us  [exchange(): return lax.ppermute(value, AXES, pairs)]
    pallas_call x3, Pallas kernels: 6.97 us -> 5.86 us  [the longest x1 3.27 us: per_device(): pl.pallas_call(token_sums, in_specs=[scalar, in_vmem, in_hbm, in_hbm], ou...]
    ppermute x18, starting transfers between devices: 22.3 us -> 21.5 us  [exchange(): return lax.ppermute(value, AXES, pairs)]
    squeeze x1, other arithmetic: 0.02 us -> 0.8 us  [per_device(): message = sum_to_owner(jnp.stack(of_clips(message), axis=1), group)[0]]
    select_n x1, other arithmetic: 0.02 us -> 0.76 us  [of_clips(): picked = jnp.where(clip ^ step == index, got[step], picked)]
    mul x1 -> x0, other arithmetic: 0.68 us -> none  [per_device(): phi_scale * (phi_grad - phi_unit * jnp.sum(phi_unit * phi_grad, axis=0, k...]
  transfers between devices with their start and end apart: 20 -> 20, of which waited for: 11 -> 12; matrix products, arithmetic and copies ran while one was open for 13% -> 14% of each run, Pallas kernels for 0% -> 0%
where the time goes in v8:
time: 59.7 us; the launch traced here: 59.3 us
  starting transfers between devices  22.3 us (37%)
  waiting for transfers between devices  13.7 us (23%)
  matrix products  7.54 us (13%)
  Pallas kernels  5.86 us (10%)
  other arithmetic  5.68 us (10%)
  local copies, waits for them, and re-layouts  2.63 us (4%)
  between operations  1.67 us (3%)
    ppermute x18, starting transfers between devices, exchange(): return lax.ppermute(value, AXES, pairs)  21.5 us
    ppermute x18, waiting for transfers between devices, exchange(): return lax.ppermute(value, AXES, pairs)  12.4 us
    pallas_call x1, Pallas kernels, per_device(): pl.pallas_call(token_sums, in_specs=[scalar, in_vmem, in_hbm, in_hbm], ou...  3.27 us
    unnamed x22, local copies, waits for them, and re-layouts  2.54 us
    dot_general x1, matrix products, per_device(): jnp.einsum('sn,sd->nd', dispatch, slot_dx, preferred_element_type=f32)  2 us
    dot_general x1, matrix products, per_device(): jnp.einsum('sn,sd->nd', combine, slot_y, preferred_element_type=f32)  1.61 us
    dot_general x1, matrix products, per_device(): jnp.einsum('oh,od->hd', hidden, mine_cot, preferred_element_type=f32)  1.59 us
    dot_general x1, matrix products, per_device(): jnp.einsum('od,oh->dh', mine_x, pre_grad, preferred_element_type=f32)  1.59 us
  transfers between devices with their start and end apart: 20, of which 12 were waited for; matrix products, arithmetic and copies ran while one was open for 14% of the time, Pallas kernels for 0%

profile of v8, /device:TPU:0, one launch (start us, length us, event | category | flops | bytes accessed | tf_op | source)
XLA Modules:
  0.0 59.3 jit_solution(10997878648926452286)
XLA Ops:
  1.5 0.9 %copy-done.6 = bf16[1280,2]{0,1:T(2,128)(2,1)S(1)} copy-done((bf16[1280,2]{0,1:T(2,128)(2,1)S(1)}, bf16[1280,2]{0,1:T(2,128)(2,1)}, u32[]{:S(2)}) %copy-start.6) | copy-done | bytes 5144
  2.3 3.3 %token_sums.1 = (f32[2,2688]{1,0:T(2,128)}, f32[2,512]{1,0:T(2,128)S(1)}, bf16[2,512]{1,0:T(2,128)(2,1)S(1)}, f32[512,1]{1,0:T(8,128)S(1)}, bf16[512,1280]{1,0:T(8,128)(2,1)S(1)}) custom-call(f32[1]{0:T(128)S(6)} %copy.19.scale_ref, bf16[2,1280]{1,0:T(2,128)(2,1)S(1)} %bitcast.42, bf16[512,1280]{1,0:T(8,128)(2,1)} %bitcast.38, bf16[512,1280]{1,0:T(8,128)(2,1)} %bitcast.40), custom_call_target="tpu_custom_call" | custom-call | tf_op jit(solution)/shard_map/token_sums/pallas_call | solution.py:212
  5.6 1.0 %copy-done.4 = bf16[512,1280]{1,0:T(8,128)(2,1)} copy-done((bf16[512,1280]{1,0:T(8,128)(2,1)}, bf16[512,1280]{1,0:T(8,128)(2,1)S(1)}, u32[]{:S(2)}) %copy-start.4) | copy-done | bytes 1310744
  6.7 0.5 collective-permute-start
  7.1 1.2 %collective-permute-done = f32[2,2688]{1,0:T(2,128)} collective-permute-done((f32[2,2688]{1,0:T(2,128)}, f32[2,2688]{1,0:T(2,128)}, u32[]{:S(2)}, u32[]{:S(2)}) %collective-permute-start) | collective-permute-done | bytes 21536 | tf_op jit(solution)/shard_map/ppermute | solution.py:29
  8.3 0.8 %broadcast_select_fusion.1 = (f32[2,2688]{1,0:T(2,128)S(1)}, f32[2,1,2688]{2,0,1:T(2,128)S(1)}) fusion(f32[2,2688]{1,0:T(2,128)} %collective-permute-done, f32[2,2688]{1,0:T(2,128)} %get-tuple-element.22, pred[]{:T(512)S(6)} %eq.9, pred[]{:T(512)S(6)} %eq.8), kind=kLoop, calls=%fused_computation.32 | loop fusion | flops 10752 | bytes 86018 | tf_op jit(solution)/shard_map/jit(_where)/select_n | solution.py:40
  9.1 0.6 copy-done.8
  9.7 0.7 %fusion.5 = (f32[1,2,2688]{2,1,0:T(2,128)}, f32[1,2,2688]{2,1,0:T(2,128)}, f32[1,2,2688]{2,1,0:T(2,128)}) fusion(s32[]{:T(128)S(6)} %select_n.83, f32[2,1,2688]{2,1,0:T(1,128)S(1)} %copy.12, f32[2,1,2688]{2,1,0:T(1,128)S(1)} %stack.10, s32[]{:T(128)S(6)} %select_n.81, s32[]{:T(128)S(6)} %select_n.82), kind=kLoop, calls=%fused_computation.22 | loop fusion | flops 16128 | bytes 107532 | tf_op jit(solution)/shard_map/stack | solution.py:230
  10.4 2.7 %collective-permute-start.1 = (f32[1,2,2688]{2,1,0:T(2,128)}, f32[1,2,2688]{2,1,0:T(2,128)}, u32[]{:S(2)}, u32[]{:S(2)}) collective-permute-start(f32[1,2,2688]{2,1,0:T(2,128)} %get-tuple-element.38), channel_id=1, source_target_pairs={{0,9},{1,8},{2,11},{3,10},{4,13},{5,12},{6,15},{7,14},{8,1},{9,0},... | collective-permute-start | bytes 64520 | tf_op jit(solution)/shard_map/ppermute | solution.py:25
  13.1 2.5 %collective-permute-start.2 = (f32[1,2,2688]{2,1,0:T(2,128)}, f32[1,2,2688]{2,1,0:T(2,128)}, u32[]{:S(2)}, u32[]{:S(2)}) collective-permute-start(f32[1,2,2688]{2,1,0:T(2,128)} %get-tuple-element.39), channel_id=1, source_target_pairs={{0,17},{1,16},{2,19},{3,18},{4,21},{5,20},{6,23},{7,22},{8,25},{9,... | collective-permute-start | bytes 64520 | tf_op jit(solution)/shard_map/ppermute | solution.py:25
  15.6 0.8 %fusion.18 = f32[2]{0:T(128)S(1)} fusion(bf16[1280,2]{0,1:T(2,128)(2,1)} %param.8), kind=kLoop, calls=%fused_computation.44 | loop fusion | flops 7678 | bytes 5128 | tf_op jit(solution)/shard_map/reduce_sum | solution.py:267
  16.4 1.3 %collective-permute-done.2 = f32[1,2,2688]{2,1,0:T(2,128)} collective-permute-done((f32[1,2,2688]{2,1,0:T(2,128)}, f32[1,2,2688]{2,1,0:T(2,128)}, u32[]{:S(2)}, u32[]{:S(2)}) %collective-permute-start.2) | collective-permute-done | bytes 21536 | tf_op jit(solution)/shard_map/ppermute | solution.py:25
  17.7 3.2 %collective-permute-done.3 = f32[1,2,2688]{2,1,0:T(2,128)} collective-permute-done((f32[1,2,2688]{2,1,0:T(2,128)}, f32[1,2,2688]{2,1,0:T(2,128)}, u32[]{:S(2)}, u32[]{:S(2)}) %collective-permute-start.3) | collective-permute-done | bytes 21536 | tf_op jit(solution)/shard_map/ppermute | solution.py:25
  20.9 1.4 %fusion.8 = f32[1,2,2688]{2,1,0:T(2,128)} fusion(f32[1,2,2688]{2,1,0:T(2,128)} %collective-permute-done.1, s32[]{:T(128)S(6)} %select_n.80, f32[2,1,2688]{2,1,0:T(1,128)} %copy-done.8, f32[2,1,2688]{2,1,0:T(1,128)} %copy-done.9, f32[1,2,2688]{2,1,0:T(2,128)} %collective-permute-done.2, f32[1,2,2688]{2,1,0:T(2,128)} %collective-permute-done.3), kind=kLoop, calls=%fused_computation.25 | loop fusion | flops 21504 | bytes 129028 | tf_op jit(solution)/shard_map/add | solution.py:67
  22.4 1.3 %collective-permute-start.4 = (f32[1,2,2688]{2,1,0:T(2,128)}, f32[1,2,2688]{2,1,0:T(2,128)}, u32[]{:S(2)}, u32[]{:S(2)}) collective-permute-start(f32[1,2,2688]{2,1,0:T(2,128)} %fusion.8), channel_id=1, source_target_pairs={{0,3},{1,2},{2,1},{3,0},{4,7},{5,6},{6,5},{7,4},{8,11},{9,10},{10,... | collective-permute-start | bytes 64520 | tf_op jit(solution)/shard_map/ppermute | solution.py:25
  23.6 1.5 %collective-permute-start.5 = (f32[1,2,2688]{2,1,0:T(2,128)}, f32[1,2,2688]{2,1,0:T(2,128)}, u32[]{:S(2)}, u32[]{:S(2)}) collective-permute-start(f32[1,2,2688]{2,1,0:T(2,128)} %fusion.8), channel_id=1, source_target_pairs={{0,5},{1,4},{2,7},{3,6},{4,1},{5,0},{6,3},{7,2},{8,13},{9,12},{10,... | collective-permute-start | bytes 64520 | tf_op jit(solution)/shard_map/ppermute | solution.py:25
  25.1 0.2 collective-permute-start.6
  25.4 0.1 reduce
  25.5 0.4 collective-permute-done.4
  25.9 1.3 %collective-permute-done.5 = f32[1,2,2688]{2,1,0:T(2,128)} collective-permute-done((f32[1,2,2688]{2,1,0:T(2,128)}, f32[1,2,2688]{2,1,0:T(2,128)}, u32[]{:S(2)}, u32[]{:S(2)}) %collective-permute-start.5) | collective-permute-done | bytes 21536 | tf_op jit(solution)/shard_map/ppermute | solution.py:25
  27.2 2.4 %collective-permute-done.6 = f32[1,2,2688]{2,1,0:T(2,128)} collective-permute-done((f32[1,2,2688]{2,1,0:T(2,128)}, f32[1,2,2688]{2,1,0:T(2,128)}, u32[]{:S(2)}, u32[]{:S(2)}) %collective-permute-start.6) | collective-permute-done | bytes 21536 | tf_op jit(solution)/shard_map/ppermute | solution.py:25
  29.6 0.8 %add_bitcast_fusion.sums_ref = f32[2,2688]{1,0:T(2,128)S(1)} fusion(f32[1,2,2688]{2,1,0:T(2,128)} %collective-permute-done.5, f32[1,2,2688]{2,1,0:T(2,128)} %collective-permute-done.6, f32[1,2,2688]{2,1,0:T(2,128)} %fusion.8, f32[1,2,2688]{2,1,0:T(2,128)} %collective-permute-done.4), kind=kLoop, calls=%fused_computation.30 | loop fusion | flops 16128 | bytes 107520 | tf_op jit(solution)/shard_map/squeeze | solution.py:230
  30.4 1.5 %expert_rows.1 = (f32[2,2688]{1,0:T(2,128)S(1)}, bf16[2,1280]{1,0:T(2,128)(2,1)S(1)}, bf16[2,1280]{1,0:T(2,128)(2,1)S(1)}, bf16[2,640]{1,0:T(2,128)(2,1)S(1)}, bf16[2,640]{1,0:T(2,128)(2,1)S(1)}) custom-call(s32[1]{0:T(128)} %bitcast.3.owned_ref, f32[2,2688]{1,0:T(2,128)S(1)} %add_bitcast_fusion.sums_ref, bf16[1280,640]{1,0:T(8,128)(2,1)S(1)} %copy-done.2, ...), custom_call_target="tpu_custom_call" | custom-call | tf_op jit(solution)/shard_map/expert_rows/pallas_call | solution.py:232
  31.9 0.3 collective-permute-start.7
  32.3 0.5 collective-permute-start.8
  32.7 2.2 %collective-permute-start.9 = (f32[1,2,2688]{2,1,0:T(2,128)S(1)}, f32[1,2,2688]{2,1,0:T(2,128)S(1)}, u32[]{:S(2)}, u32[]{:S(2)}) collective-permute-start(f32[1,2,2688]{2,1,0:T(2,128)S(1)} %bitcast.46), channel_id=1, source_target_pairs={{0,7},{1,6},{2,5},{3,4},{4,3},{5,2},{6,1},{7,0},{8,15},{9,14},{10,... | collective-permute-start | bytes 64520 | tf_op jit(solution)/shard_map/ppermute | solution.py:25
  34.9 1.6 %fusion.24 = f32[640,640]{1,0:T(8,128)} fusion(bf16[2,640]{1,0:T(2,128)(2,1)S(1)} %get-tuple-element.33, bf16[2,1280]{1,0:T(2,128)(2,1)S(1)} %get-tuple-element.32, s32[]{:T(128)S(6)} %select_n.86), kind=kOutput, calls=%fused_computation.54 | convolution fusion | flops 1638400 | bytes 1643524 | tf_op jit(solution)/shard_map/od,oh->dh/dot_general | solution.py:251
  36.5 0.3 collective-permute-done.9
  36.9 0.7 %collective-permute-start.11 = (f32[1,2,2688]{2,1,0:T(2,128)S(1)}, f32[1,2,2688]{2,1,0:T(2,128)S(1)}, u32[]{:S(2)}, u32[]{:S(2)}) collective-permute-start(f32[1,2,2688]{2,1,0:T(2,128)S(1)} %add_add_fusion), channel_id=1, source_target_pairs={{0,25},{1,24},{2,27},{3,26},{4,29},{5,28},{6,31},{7,30},{8,17},{9,... | collective-permute-start | bytes 64520 | tf_op jit(solution)/shard_map/ppermute | solution.py:25
  37.7 2.2 %collective-permute-start.12 = (f32[1,2,2688]{2,1,0:T(2,128)S(1)}, f32[1,2,2688]{2,1,0:T(2,128)S(1)}, u32[]{:S(2)}, u32[]{:S(2)}) collective-permute-start(f32[1,2,2688]{2,1,0:T(2,128)S(1)} %add_add_fusion), channel_id=1, source_target_pairs={{0,9},{1,8},{2,11},{3,10},{4,13},{5,12},{6,15},{7,14},{8,1},{9,0},... | collective-permute-start | bytes 64520 | tf_op jit(solution)/shard_map/ppermute | solution.py:25
  39.9 1.6 %fusion.25 = f32[640,640]{1,0:T(8,128)} fusion(bf16[2,640]{1,0:T(2,128)(2,1)S(1)} %get-tuple-element.34, bf16[2,1280]{1,0:T(2,128)(2,1)S(1)} %get-tuple-element.35, s32[]{:T(128)S(6)} %select_n.86), kind=kOutput, calls=%fused_computation.55 | convolution fusion | flops 1638400 | bytes 1643524 | tf_op jit(solution)/shard_map/oh,od->hd/dot_general | solution.py:252
  41.6 0.4 collective-permute-done.11
  42.2 1.1 %score_grads.1 = (bf16[2,512]{1,0:T(2,128)(2,1)S(1)}, bf16[2,512]{1,0:T(2,128)(2,1)S(1)}, f32[2,1280]{1,0:T(2,128)S(1)}) custom-call(f32[1]{0:T(128)S(6)} %copy.19.scale_ref, f32[2,2688]{1,0:T(2,128)S(1)} %bitcast.43, f32[1,128]{1,0:T(1,128)S(1)} %constant_dynamic-slice_fusion.2.totals_ref, bf16[512,1280]{1,0:T(8,128)(2,1)S(1)} %bitcast.39, ...), custom_call_target="tpu_custom_call" | custom-call | tf_op jit(solution)/shard_map/score_grads/pallas_call | solution.py:253
  43.3 0.3 collective-permute-start.13
  43.6 0.7 %multiply_reduce_fusion = (f32[512]{0:T(512)S(1)}, f32[512,1280]{1,0:T(8,128)S(1)}) fusion(f32[512]{0:T(512)S(1)} %reduce, bf16[1,512,1280]{2,1,0:T(8,128)(2,1)S(1)} %copy-done, bf16[2,512]{1,0:T(2,128)(2,1)S(1)} %get-tuple-element.31, f32[2]{0:T(128)S(1)} %add_rsqrt_fusion, bf16[1280,2]{0,1:T(2,128)(2,1)S(1)} %copy-done.7), kind=kOutput, calls=%fused_computation.5 | convolution fusion | flops 5250048 | bytes 3943432 | tf_op jit(solution)/shard_map/sn,sd->nd/dot_general | solution.py:273
  44.4 0.1 collective-permute-done.13
  44.5 1.4 %collective-permute-start.14 = (f32[1,1,2560]{2,1,0:T(1,128)S(1)}, f32[1,1,2560]{2,1,0:T(1,128)S(1)}, u32[]{:S(2)}, u32[]{:S(2)}) collective-permute-start(f32[1,1,2560]{2,1,0:T(1,128)S(1)} %fusion.19), channel_id=1, source_target_pairs={{0,3},{1,2},{2,1},{3,0},{4,7},{5,6},{6,5},{7,4},{8,11},{9,10},{10,... | collective-permute-start | bytes 30728 | tf_op jit(solution)/shard_map/ppermute | solution.py:25
  46.0 1.4 %collective-permute-start.15 = (f32[1,1,2560]{2,1,0:T(1,128)S(1)}, f32[1,1,2560]{2,1,0:T(1,128)S(1)}, u32[]{:S(2)}, u32[]{:S(2)}) collective-permute-start(f32[1,1,2560]{2,1,0:T(1,128)S(1)} %fusion.19), channel_id=1, source_target_pairs={{0,5},{1,4},{2,7},{3,6},{4,1},{5,0},{6,3},{7,2},{8,13},{9,12},{10,... | collective-permute-start | bytes 30728 | tf_op jit(solution)/shard_map/ppermute | solution.py:25
  47.3 0.4 collective-permute-start.16
  47.7 2.0 %fusion.1 = bf16[1,512,1280]{2,1,0:T(8,128)(2,1)} fusion(bf16[2,512]{1,0:T(2,128)(2,1)S(1)} %get-tuple-element.29, f32[512,1280]{1,0:T(8,128)S(1)} %get-tuple-element.43, f32[512]{0:T(512)S(1)} %get-tuple-element.42, f32[512]{0:T(512)S(1)} %reduce, bf16[2,2688]{1,0:T(2,128)(2,1)S(1)} %bitcast.47, bf16[1,512,1280]{2,1,0:T(8,128)(2,1)S(1)} %copy-done), kind=kOutput, calls=%fused_computation.3 | convolution fusion | flops 7208960 | bytes 5254144 | tf_op jit(solution)/shard_map/sn,sd->nd/dot_general | solution.py:274
  49.7 1.6 %collective-permute-done.16 = f32[1,1,2560]{2,1,0:T(1,128)S(1)} collective-permute-done((f32[1,1,2560]{2,1,0:T(1,128)S(1)}, f32[1,1,2560]{2,1,0:T(1,128)S(1)}, u32[]{:S(2)}, u32[]{:S(2)}) %collective-permute-start.16) | collective-permute-done | bytes 10272 | tf_op jit(solution)/shard_map/ppermute | solution.py:25
  51.3 1.2 %collective-permute-start.17 = (f32[1,1,2560]{2,1,0:T(1,128)S(1)}, f32[1,1,2560]{2,1,0:T(1,128)S(1)}, u32[]{:S(2)}, u32[]{:S(2)}) collective-permute-start(f32[1,1,2560]{2,1,0:T(1,128)S(1)} %add_add_fusion.1), channel_id=1, source_target_pairs={{0,9},{1,8},{2,11},{3,10},{4,13},{5,12},{6,15},{7,14},{8,1},{9,0},... | collective-permute-start | bytes 30728 | tf_op jit(solution)/shard_map/ppermute | solution.py:25
  52.5 1.0 %collective-permute-start.18 = (f32[1,1,2560]{2,1,0:T(1,128)S(1)}, f32[1,1,2560]{2,1,0:T(1,128)S(1)}, u32[]{:S(2)}, u32[]{:S(2)}) collective-permute-start(f32[1,1,2560]{2,1,0:T(1,128)S(1)} %add_add_fusion.1), channel_id=1, source_target_pairs={{0,17},{1,16},{2,19},{3,18},{4,21},{5,20},{6,23},{7,22},{8,25},{9,... | collective-permute-start | bytes 30728 | tf_op jit(solution)/shard_map/ppermute | solution.py:25
  53.5 1.9 %collective-permute-start.19 = (f32[1,1,2560]{2,1,0:T(1,128)S(1)}, f32[1,1,2560]{2,1,0:T(1,128)S(1)}, u32[]{:S(2)}, u32[]{:S(2)}) collective-permute-start(f32[1,1,2560]{2,1,0:T(1,128)S(1)} %add_add_fusion.1), channel_id=1, source_target_pairs={{0,25},{1,24},{2,27},{3,26},{4,29},{5,28},{6,31},{7,30},{8,17},{9,... | collective-permute-start | bytes 30728 | tf_op jit(solution)/shard_map/ppermute | solution.py:25
  55.4 1.6 %fusion.2 = bf16[1,512,1280]{2,1,0:T(8,128)(2,1)} fusion(bf16[2,512]{1,0:T(2,128)(2,1)S(1)} %get-tuple-element.21, bf16[2,2688]{1,0:T(2,128)(2,1)S(1)} %bitcast.48), kind=kOutput, calls=%fused_computation.4 | convolution fusion | flops 3276800 | bytes 1317888 | tf_op jit(solution)/shard_map/sn,sd->nd/dot_general | solution.py:272
  57.0 1.4 %collective-permute-done.19 = f32[1,1,2560]{2,1,0:T(1,128)S(1)} collective-permute-done((f32[1,1,2560]{2,1,0:T(1,128)S(1)}, f32[1,1,2560]{2,1,0:T(1,128)S(1)}, u32[]{:S(2)}, u32[]{:S(2)}) %collective-permute-start.19) | collective-permute-done | bytes 10272 | tf_op jit(solution)/shard_map/ppermute | solution.py:25
  58.5 0.2 fusion.14
  58.7 0.7 %fusion.17 = f32[1280,2]{0,1:T(2,128)} fusion(f32[2,1280]{1,0:T(2,128)S(1)} %reshape.37, f32[2]{0:T(128)S(1)} %fusion.14, f32[2]{0:T(128)S(1)} %add_rsqrt_fusion, bf16[1280,2]{0,1:T(2,128)(2,1)S(1)} %copy-done.7), kind=kLoop, calls=%fused_computation.43 | loop fusion | flops 12800 | bytes 25616 | tf_op jit(solution)/shard_map/transpose | solution.py:283
  (44 shorter events, 0.5 us)
Async XLA Ops:
  0.6 29.7 %copy-start.2 = (bf16[1280,640]{1,0:T(8,128)(2,1)S(1)}, bf16[1280,640]{1,0:T(8,128)(2,1)}, u32[]{:S(2)}) copy-start(bf16[1280,640]{1,0:T(8,128)(2,1)} %in_ref.1) | copy-start | bytes 4915204
  0.6 29.7 %copy-start.3 = (bf16[640,1280]{1,0:T(8,128)(2,1)S(1)}, bf16[640,1280]{1,0:T(8,128)(2,1)}, u32[]{:S(2)}) copy-start(bf16[640,1280]{1,0:T(8,128)(2,1)} %out_ref.1) | copy-start | bytes 4915204
  1.4 0.9 %copy-start.6 = (bf16[1280,2]{0,1:T(2,128)(2,1)S(1)}, bf16[1280,2]{0,1:T(2,128)(2,1)}, u32[]{:S(2)}) copy-start(bf16[1280,2]{0,1:T(2,128)(2,1)} %param.8) | copy-start | bytes 15364
  5.6 1.1 %copy-start.4 = (bf16[512,1280]{1,0:T(8,128)(2,1)}, bf16[512,1280]{1,0:T(8,128)(2,1)S(1)}, u32[]{:S(2)}) copy-start(bf16[512,1280]{1,0:T(8,128)(2,1)S(1)} %get-tuple-element.27.norm_ref) | copy-start | bytes 3932164
  6.7 1.6 %collective-permute-start = (f32[2,2688]{1,0:T(2,128)}, f32[2,2688]{1,0:T(2,128)}, u32[]{:S(2)}, u32[]{:S(2)}) collective-permute-start(f32[2,2688]{1,0:T(2,128)} %get-tuple-element.22), channel_id=1, source_target_pairs={{0,1},{1,0},{2,3},{3,2},{4,5},{5,4},{6,7},{7,6},{8,9},{9,8},{10,11... | collective-permute-start | bytes 64520 | tf_op jit(solution)/shard_map/ppermute | solution.py:29
  9.1 0.6 %copy-start.8 = (f32[2,1,2688]{2,1,0:T(1,128)}, f32[2,1,2688]{2,1,0:T(1,128)S(1)}, u32[]{:S(2)}) copy-start(f32[2,1,2688]{2,1,0:T(1,128)S(1)} %copy.12) | copy-start | bytes 64516
  9.7 0.7 %copy-start.9 = (f32[2,1,2688]{2,1,0:T(1,128)}, f32[2,1,2688]{2,1,0:T(1,128)S(1)}, u32[]{:S(2)}) copy-start(f32[2,1,2688]{2,1,0:T(1,128)S(1)} %stack.10) | copy-start | bytes 64516
  10.4 6.0 %collective-permute-start.1 = (f32[1,2,2688]{2,1,0:T(2,128)}, f32[1,2,2688]{2,1,0:T(2,128)}, u32[]{:S(2)}, u32[]{:S(2)}) collective-permute-start(f32[1,2,2688]{2,1,0:T(2,128)} %get-tuple-element.38), channel_id=1, source_target_pairs={{0,9},{1,8},{2,11},{3,10},{4,13},{5,12},{6,15},{7,14},{8,1},{9,0},... | collective-permute-start | bytes 64520 | tf_op jit(solution)/shard_map/ppermute | solution.py:25
  13.1 4.7 %collective-permute-start.2 = (f32[1,2,2688]{2,1,0:T(2,128)}, f32[1,2,2688]{2,1,0:T(2,128)}, u32[]{:S(2)}, u32[]{:S(2)}) collective-permute-start(f32[1,2,2688]{2,1,0:T(2,128)} %get-tuple-element.39), channel_id=1, source_target_pairs={{0,17},{1,16},{2,19},{3,18},{4,21},{5,20},{6,23},{7,22},{8,25},{9,... | collective-permute-start | bytes 64520 | tf_op jit(solution)/shard_map/ppermute | solution.py:25
  15.6 5.3 %collective-permute-start.3 = (f32[1,2,2688]{2,1,0:T(2,128)}, f32[1,2,2688]{2,1,0:T(2,128)}, u32[]{:S(2)}, u32[]{:S(2)}) collective-permute-start(f32[1,2,2688]{2,1,0:T(2,128)} %get-tuple-element.37), channel_id=1, source_target_pairs={{0,25},{1,24},{2,27},{3,26},{4,29},{5,28},{6,31},{7,30},{8,17},{9,... | collective-permute-start | bytes 64520 | tf_op jit(solution)/shard_map/ppermute | solution.py:25
  22.4 3.5 %collective-permute-start.4 = (f32[1,2,2688]{2,1,0:T(2,128)}, f32[1,2,2688]{2,1,0:T(2,128)}, u32[]{:S(2)}, u32[]{:S(2)}) collective-permute-start(f32[1,2,2688]{2,1,0:T(2,128)} %fusion.8), channel_id=1, source_target_pairs={{0,3},{1,2},{2,1},{3,0},{4,7},{5,6},{6,5},{7,4},{8,11},{9,10},{10,... | collective-permute-start | bytes 64520 | tf_op jit(solution)/shard_map/ppermute | solution.py:25
  23.6 3.5 %collective-permute-start.5 = (f32[1,2,2688]{2,1,0:T(2,128)}, f32[1,2,2688]{2,1,0:T(2,128)}, u32[]{:S(2)}, u32[]{:S(2)}) collective-permute-start(f32[1,2,2688]{2,1,0:T(2,128)} %fusion.8), channel_id=1, source_target_pairs={{0,5},{1,4},{2,7},{3,6},{4,1},{5,0},{6,3},{7,2},{8,13},{9,12},{10,... | collective-permute-start | bytes 64520 | tf_op jit(solution)/shard_map/ppermute | solution.py:25
  25.1 4.4 %collective-permute-start.6 = (f32[1,2,2688]{2,1,0:T(2,128)}, f32[1,2,2688]{2,1,0:T(2,128)}, u32[]{:S(2)}, u32[]{:S(2)}) collective-permute-start(f32[1,2,2688]{2,1,0:T(2,128)} %fusion.8), channel_id=1, source_target_pairs={{0,7},{1,6},{2,5},{3,4},{4,3},{5,2},{6,1},{7,0},{8,15},{9,14},{10,... | collective-permute-start | bytes 64520 | tf_op jit(solution)/shard_map/ppermute | solution.py:25
  30.4 11.8 %copy-start.5 = (bf16[512,1280]{1,0:T(8,128)(2,1)S(1)}, bf16[512,1280]{1,0:T(8,128)(2,1)}, u32[]{:S(2)}) copy-start(bf16[512,1280]{1,0:T(8,128)(2,1)} %copy-done.4) | copy-start | bytes 3932164
  31.9 10.2 %copy-start = (bf16[1,512,1280]{2,1,0:T(8,128)(2,1)S(1)}, bf16[1,512,1280]{2,1,0:T(8,128)(2,1)}, u32[]{:S(2)}) copy-start(bf16[1,512,1280]{2,1,0:T(8,128)(2,1)} %param.6) | copy-start | bytes 3932164
  31.9 10.2 %copy-start.1 = (bf16[1,512,1280]{2,1,0:T(8,128)(2,1)S(1)}, bf16[1,512,1280]{2,1,0:T(8,128)(2,1)}, u32[]{:S(2)}) copy-start(bf16[1,512,1280]{2,1,0:T(8,128)(2,1)} %param.7) | copy-start | bytes 3932164
  31.9 4.6 %collective-permute-start.7 = (f32[1,2,2688]{2,1,0:T(2,128)S(1)}, f32[1,2,2688]{2,1,0:T(2,128)S(1)}, u32[]{:S(2)}, u32[]{:S(2)}) collective-permute-start(f32[1,2,2688]{2,1,0:T(2,128)S(1)} %bitcast.44), channel_id=1, source_target_pairs={{0,3},{1,2},{2,1},{3,0},{4,7},{5,6},{6,5},{7,4},{8,11},{9,10},{10,... | collective-permute-start | bytes 64520 | tf_op jit(solution)/shard_map/ppermute | solution.py:25
  32.3 4.3 %collective-permute-start.8 = (f32[1,2,2688]{2,1,0:T(2,128)S(1)}, f32[1,2,2688]{2,1,0:T(2,128)S(1)}, u32[]{:S(2)}, u32[]{:S(2)}) collective-permute-start(f32[1,2,2688]{2,1,0:T(2,128)S(1)} %bitcast.45), channel_id=1, source_target_pairs={{0,5},{1,4},{2,7},{3,6},{4,1},{5,0},{6,3},{7,2},{8,13},{9,12},{10,... | collective-permute-start | bytes 64520 | tf_op jit(solution)/shard_map/ppermute | solution.py:25
  32.7 4.1 %collective-permute-start.9 = (f32[1,2,2688]{2,1,0:T(2,128)S(1)}, f32[1,2,2688]{2,1,0:T(2,128)S(1)}, u32[]{:S(2)}, u32[]{:S(2)}) collective-permute-start(f32[1,2,2688]{2,1,0:T(2,128)S(1)} %bitcast.46), channel_id=1, source_target_pairs={{0,7},{1,6},{2,5},{3,4},{4,3},{5,2},{6,1},{7,0},{8,15},{9,14},{10,... | collective-permute-start | bytes 64520 | tf_op jit(solution)/shard_map/ppermute | solution.py:25
  36.9 6.8 %copy-start.7 = (bf16[1280,2]{0,1:T(2,128)(2,1)S(1)}, bf16[1280,2]{0,1:T(2,128)(2,1)}, u32[]{:S(2)}) copy-start(bf16[1280,2]{0,1:T(2,128)(2,1)} %param.8) | copy-start | bytes 15364
  36.9 4.8 %collective-permute-start.10 = (f32[1,2,2688]{2,1,0:T(2,128)S(1)}, f32[1,2,2688]{2,1,0:T(2,128)S(1)}, u32[]{:S(2)}, u32[]{:S(2)}) collective-permute-start(f32[1,2,2688]{2,1,0:T(2,128)S(1)} %add_add_fusion), channel_id=1, source_target_pairs={{0,17},{1,16},{2,19},{3,18},{4,21},{5,20},{6,23},{7,22},{8,25},{9,... | collective-permute-start | bytes 64520 | tf_op jit(solution)/shard_map/ppermute | solution.py:25
  36.9 5.1 %collective-permute-start.11 = (f32[1,2,2688]{2,1,0:T(2,128)S(1)}, f32[1,2,2688]{2,1,0:T(2,128)S(1)}, u32[]{:S(2)}, u32[]{:S(2)}) collective-permute-start(f32[1,2,2688]{2,1,0:T(2,128)S(1)} %add_add_fusion), channel_id=1, source_target_pairs={{0,25},{1,24},{2,27},{3,26},{4,29},{5,28},{6,31},{7,30},{8,17},{9,... | collective-permute-start | bytes 64520 | tf_op jit(solution)/shard_map/ppermute | solution.py:25
  37.7 3.9 %collective-permute-start.12 = (f32[1,2,2688]{2,1,0:T(2,128)S(1)}, f32[1,2,2688]{2,1,0:T(2,128)S(1)}, u32[]{:S(2)}, u32[]{:S(2)}) collective-permute-start(f32[1,2,2688]{2,1,0:T(2,128)S(1)} %add_add_fusion), channel_id=1, source_target_pairs={{0,9},{1,8},{2,11},{3,10},{4,13},{5,12},{6,15},{7,14},{8,1},{9,0},... | collective-permute-start | bytes 64520 | tf_op jit(solution)/shard_map/ppermute | solution.py:25
  43.3 1.2 %collective-permute-start.13 = (f32[1,1,2560]{2,1,0:T(1,128)S(1)}, f32[1,1,2560]{2,1,0:T(1,128)S(1)}, u32[]{:S(2)}, u32[]{:S(2)}) collective-permute-start(f32[1,1,2560]{2,1,0:T(1,128)S(1)} %reshape.36), channel_id=1, source_target_pairs={{0,1},{1,0},{2,3},{3,2},{4,5},{5,4},{6,7},{7,6},{8,9},{9,8},{10,11... | collective-permute-start | bytes 30728 | tf_op jit(solution)/shard_map/ppermute | solution.py:29
  44.5 5.2 %collective-permute-start.14 = (f32[1,1,2560]{2,1,0:T(1,128)S(1)}, f32[1,1,2560]{2,1,0:T(1,128)S(1)}, u32[]{:S(2)}, u32[]{:S(2)}) collective-permute-start(f32[1,1,2560]{2,1,0:T(1,128)S(1)} %fusion.19), channel_id=1, source_target_pairs={{0,3},{1,2},{2,1},{3,0},{4,7},{5,6},{6,5},{7,4},{8,11},{9,10},{10,... | collective-permute-start | bytes 30728 | tf_op jit(solution)/shard_map/ppermute | solution.py:25
  46.0 3.7 %collective-permute-start.15 = (f32[1,1,2560]{2,1,0:T(1,128)S(1)}, f32[1,1,2560]{2,1,0:T(1,128)S(1)}, u32[]{:S(2)}, u32[]{:S(2)}) collective-permute-start(f32[1,1,2560]{2,1,0:T(1,128)S(1)} %fusion.19), channel_id=1, source_target_pairs={{0,5},{1,4},{2,7},{3,6},{4,1},{5,0},{6,3},{7,2},{8,13},{9,12},{10,... | collective-permute-start | bytes 30728 | tf_op jit(solution)/shard_map/ppermute | solution.py:25
  47.3 4.0 %collective-permute-start.16 = (f32[1,1,2560]{2,1,0:T(1,128)S(1)}, f32[1,1,2560]{2,1,0:T(1,128)S(1)}, u32[]{:S(2)}, u32[]{:S(2)}) collective-permute-start(f32[1,1,2560]{2,1,0:T(1,128)S(1)} %fusion.19), channel_id=1, source_target_pairs={{0,7},{1,6},{2,5},{3,4},{4,3},{5,2},{6,1},{7,0},{8,15},{9,14},{10,... | collective-permute-start | bytes 30728 | tf_op jit(solution)/shard_map/ppermute | solution.py:25
  51.3 5.7 %collective-permute-start.17 = (f32[1,1,2560]{2,1,0:T(1,128)S(1)}, f32[1,1,2560]{2,1,0:T(1,128)S(1)}, u32[]{:S(2)}, u32[]{:S(2)}) collective-permute-start(f32[1,1,2560]{2,1,0:T(1,128)S(1)} %add_add_fusion.1), channel_id=1, source_target_pairs={{0,9},{1,8},{2,11},{3,10},{4,13},{5,12},{6,15},{7,14},{8,1},{9,0},... | collective-permute-start | bytes 30728 | tf_op jit(solution)/shard_map/ppermute | solution.py:25
  52.5 4.5 %collective-permute-start.18 = (f32[1,1,2560]{2,1,0:T(1,128)S(1)}, f32[1,1,2560]{2,1,0:T(1,128)S(1)}, u32[]{:S(2)}, u32[]{:S(2)}) collective-permute-start(f32[1,1,2560]{2,1,0:T(1,128)S(1)} %add_add_fusion.1), channel_id=1, source_target_pairs={{0,17},{1,16},{2,19},{3,18},{4,21},{5,20},{6,23},{7,22},{8,25},{9,... | collective-permute-start | bytes 30728 | tf_op jit(solution)/shard_map/ppermute | solution.py:25
  53.5 4.9 %collective-permute-start.19 = (f32[1,1,2560]{2,1,0:T(1,128)S(1)}, f32[1,1,2560]{2,1,0:T(1,128)S(1)}, u32[]{:S(2)}, u32[]{:S(2)}) collective-permute-start(f32[1,1,2560]{2,1,0:T(1,128)S(1)} %add_add_fusion.1), channel_id=1, source_target_pairs={{0,25},{1,24},{2,27},{3,26},{4,29},{5,28},{6,31},{7,30},{8,17},{9,... | collective-permute-start | bytes 30728 | tf_op jit(solution)/shard_map/ppermute | solution.py:25

commit v9 on v8

--- a/solution.py
+++ b/solution.py
@@ -9,7 +9,7 @@
 AXES = ("seq", "dp")
 LANES = 128
 PIECES = 4
-VMEM_BYTES = 20 * 2**20
+VMEM_BYTES = 10 * 2**20
 ROWS = (((1,), (1,)), ((), ()))
 COLUMNS = (((0,), (0,)), ((), ()))
 f32, bf16 = jnp.float32, jnp.bfloat16
@@ -135,6 +135,21 @@
     message_ref[:, width : 2 * width] = jnp.dot(combine, cot_buf[...], preferred_element_type=f32)
 
 
+def fetch(in_ref, out_ref, in_buf, out_buf, sems):
+    copies = []
+    for which, (source, target) in enumerate([(in_ref, in_buf), (out_ref, out_buf)]):
+        rows = source.shape[0] // sems.shape[1]
+        for index in range(sems.shape[1]):
+            piece = pl.ds(index * rows, rows)
+            copies.append(
+                pltpu.make_async_copy(source.at[piece], target.at[piece], sems.at[which, index])
+            )
+    for copy in copies:
+        copy.start()
+    for copy in copies:
+        copy.wait()
+
+
 def expert_rows(owned_ref, sums_ref, in_ref, out_ref, message_ref, row_x_ref, row_cot_ref, hidden_ref, pre_grad_ref):
     width, units = in_ref.shape
     spare = sums_ref[:, 2 * width :]
@@ -190,6 +205,10 @@
     phi_ref[...] = jnp.dot(score_grad, norm_ref[...], preferred_element_type=f32)
     grad_ref[...] = score_grad
     dispatch_ref[...] = dispatch_f.astype(bf16)
+
+
+def in_place(operand):
+    return pltpu.with_memory_space_constraint(operand, pltpu.HBM)
 
 
 def per_device(tokens, cotangent, router, logit_scale, expert_in, expert_out):
@@ -226,8 +245,25 @@
         ],
         compiler_params=params,
         name="token_sums",
-    )(logit_scale, phi, *[pltpu.with_memory_space_constraint(x, pltpu.HBM) for x in (tok_in, tok_cot)])
-    message = sum_to_owner(jnp.stack(of_clips(message), axis=1), group)[0]
+    )(logit_scale, phi, in_place(tok_in), in_place(tok_cot))
+    message = jnp.stack(of_clips(message), axis=1)
+    message, expert_in, expert_out = lax.optimization_barrier((message, expert_in, expert_out))
+    expert_in, expert_out = pl.pallas_call(
+        fetch,
+        in_specs=[in_hbm] * 2,
+        out_specs=[in_vmem] * 2,
+        out_shape=[
+            jax.ShapeDtypeStruct(expert_in.shape, bf16),
+            jax.ShapeDtypeStruct(expert_out.shape, bf16),
+        ],
+        scratch_shapes=[pltpu.SemaphoreType.DMA((2, PIECES))],
+        compiler_params=params,
+        cost_estimate=pl.CostEstimate(
+            flops=0, bytes_accessed=4 * expert_in.size + 4 * expert_out.size, transcendentals=0
+        ),
+        name="fetch_weights",
+    )(in_place(expert_in), in_place(expert_out))
+    message = sum_to_owner(message, group)[0]
     totals = message[:, 2 * width :]
     message, row_x, row_cot, hidden, pre_grad = pl.pallas_call(
         expert_rows,

time: 59.7 us -> 49.6 us (0.83)
  waiting for transfers between devices: 13.7 us -> 7.62 us
  other arithmetic: 5.68 us -> 1.41 us
  local copies, waits for them, and re-layouts: 2.63 us -> 0.82 us
  Pallas kernels: 5.86 us -> 7.18 us
  starting transfers between devices: 22.3 us -> 23.4 us
    ppermute x18, waiting for transfers between devices: 12.4 us -> 6.7 us  [exchange(): return lax.ppermute(value, AXES, pairs)]
    pallas_call x0 -> x1, Pallas kernels: none -> 1.94 us  [per_device(): pl.pallas_call(fetch, in_specs=[in_hbm] * 2, out_specs=[in_vmem] * 2, out...]
    unnamed x22 -> x10, local copies, waits for them, and re-layouts: 2.54 us -> 0.72 us
    add x1, other arithmetic: 1.44 us -> 0.02 us  [sum_to_owner(): got[0] + got[1] + (got[2] + got[3])]
    squeeze x1, other arithmetic: 0.8 us -> 0.02 us  [per_device(): message = sum_to_owner(message, group)[0]]
    select_n x1 -> x0, other arithmetic: 0.76 us -> none  [of_clips(): picked = jnp.where(clip ^ step == index, got[step], picked)]
    ppermute x18, starting transfers between devices: 21.5 us -> 22.2 us  [exchange(): return lax.ppermute(value, AXES, pairs)]
    reduce_sum x1, other arithmetic: 0.81 us -> 0.12 us  [per_device(): jnp.sum(phi_f32 * phi_f32, axis=1, keepdims=True) + epsilon]
  transfers between devices with their start and end apart: 20 -> 20, of which waited for: 12 -> 8; matrix products, arithmetic and copies ran while one was open for 14% -> 16% of each run, Pallas kernels for 0% -> 4%
where the time goes in v9:
time: 49.6 us; the launch traced here: 49.4 us
  starting transfers between devices  23.4 us (47%)
  waiting for transfers between devices  7.62 us (15%)
  matrix products  7.5 us (15%)
  Pallas kernels  7.18 us (14%)
  between operations  1.51 us (3%)
  other arithmetic  1.41 us (3%)
  local copies, waits for them, and re-layouts  0.82 us (2%)
    ppermute x18, starting transfers between devices, exchange(): return lax.ppermute(value, AXES, pairs)  22.2 us
    ppermute x18, waiting for transfers between devices, exchange(): return lax.ppermute(value, AXES, pairs)  6.7 us
    pallas_call x1, Pallas kernels, per_device(): pl.pallas_call(token_sums, in_specs=[scalar, in_vmem, in_hbm, in_hbm], ou...  2.64 us
    dot_general x1, matrix products, per_device(): jnp.einsum('sn,sd->nd', dispatch, slot_dx, preferred_element_type=f32)  1.98 us
    pallas_call x1, Pallas kernels, per_device(): pl.pallas_call(fetch, in_specs=[in_hbm] * 2, out_specs=[in_vmem] * 2, out...  1.94 us
    dot_general x1, matrix products, per_device(): jnp.einsum('sn,sd->nd', combine, slot_y, preferred_element_type=f32)  1.61 us
    dot_general x1, matrix products, per_device(): jnp.einsum('oh,od->hd', hidden, mine_cot, preferred_element_type=f32)  1.59 us
    dot_general x1, matrix products, per_device(): jnp.einsum('od,oh->dh', mine_x, pre_grad, preferred_element_type=f32)  1.59 us
  transfers between devices with their start and end apart: 20, of which 8 were waited for; matrix products, arithmetic and copies ran while one was open for 16% of the time, Pallas kernels for 4%

profile of v9, /device:TPU:0, one launch (start us, length us, event | category | flops | bytes accessed | tf_op | source)
XLA Modules:
  0.0 49.4 jit_solution(15968812423373315457)
XLA Ops:
  1.3 0.7 %copy-done.2 = bf16[1280,2]{0,1:T(2,128)(2,1)S(1)} copy-done((bf16[1280,2]{0,1:T(2,128)(2,1)S(1)}, bf16[1280,2]{0,1:T(2,128)(2,1)}, u32[]{:S(2)}) %copy-start.2) | copy-done | bytes 5144
  2.0 2.6 %token_sums.1 = (f32[2,2688]{1,0:T(2,128)S(1)}, f32[2,512]{1,0:T(2,128)S(1)}, bf16[2,512]{1,0:T(2,128)(2,1)S(1)}, f32[512,1]{1,0:T(8,128)S(1)}, bf16[512,1280]{1,0:T(8,128)(2,1)S(1)}) custom-call(f32[1]{0:T(128)S(6)} %copy.19.scale_ref, bf16[2,1280]{1,0:T(2,128)(2,1)S(1)} %bitcast.42, bf16[512,1280]{1,0:T(8,128)(2,1)} %bitcast.38, bf16[512,1280]{1,0:T(8,128)(2,1)} %bitcast.40), custom_call_target="tpu_custom_call" | custom-call | tf_op jit(solution)/shard_map/token_sums/pallas_call | solution.py:231
  4.6 0.5 %collective-permute-start = (f32[2,2688]{1,0:T(2,128)S(1)}, f32[2,2688]{1,0:T(2,128)S(1)}, u32[]{:S(2)}, u32[]{:S(2)}) collective-permute-start(f32[2,2688]{1,0:T(2,128)S(1)} %get-tuple-element.27), channel_id=1, source_target_pairs={{0,1},{1,0},{2,3},{3,2},{4,5},{5,4},{6,7},{7,6},{8,9},{9,8},{10,11... | collective-permute-start | bytes 64520 | tf_op jit(solution)/shard_map/ppermute | solution.py:29
  5.2 0.8 %collective-permute-done = f32[2,2688]{1,0:T(2,128)S(1)} collective-permute-done((f32[2,2688]{1,0:T(2,128)S(1)}, f32[2,2688]{1,0:T(2,128)S(1)}, u32[]{:S(2)}, u32[]{:S(2)}) %collective-permute-start) | collective-permute-done | bytes 21536 | tf_op jit(solution)/shard_map/ppermute | solution.py:29
  6.2 3.8 %collective-permute-start.2 = (f32[1,2,2688]{2,1,0:T(2,128)S(1)}, f32[1,2,2688]{2,1,0:T(2,128)S(1)}, u32[]{:S(2)}, u32[]{:S(2)}) collective-permute-start(f32[1,2,2688]{2,1,0:T(2,128)S(1)} %get-tuple-element.49), channel_id=1, source_target_pairs={{0,17},{1,16},{2,19},{3,18},{4,21},{5,20},{6,23},{7,22},{8,25},{9,... | collective-permute-start | bytes 64520 | tf_op jit(solution)/shard_map/ppermute | solution.py:25
  9.9 1.3 %collective-permute-start.3 = (f32[1,2,2688]{2,1,0:T(2,128)S(1)}, f32[1,2,2688]{2,1,0:T(2,128)S(1)}, u32[]{:S(2)}, u32[]{:S(2)}) collective-permute-start(f32[1,2,2688]{2,1,0:T(2,128)S(1)} %get-tuple-element.48), channel_id=1, source_target_pairs={{0,25},{1,24},{2,27},{3,26},{4,29},{5,28},{6,31},{7,30},{8,17},{9,... | collective-permute-start | bytes 64520 | tf_op jit(solution)/shard_map/ppermute | solution.py:25
  11.2 0.2 collective-permute-start.1
  11.5 0.1 fusion.12
  11.6 3.4 %collective-permute-done.3 = f32[1,2,2688]{2,1,0:T(2,128)S(1)} collective-permute-done((f32[1,2,2688]{2,1,0:T(2,128)S(1)}, f32[1,2,2688]{2,1,0:T(2,128)S(1)}, u32[]{:S(2)}, u32[]{:S(2)}) %collective-permute-start.3) | collective-permute-done | bytes 21536 | tf_op jit(solution)/shard_map/ppermute | solution.py:25
  15.0 0.0 collective-permute-done.1
  15.0 1.6 %collective-permute-start.5 = (f32[1,2,2688]{2,1,0:T(2,128)S(1)}, f32[1,2,2688]{2,1,0:T(2,128)S(1)}, u32[]{:S(2)}, u32[]{:S(2)}) collective-permute-start(f32[1,2,2688]{2,1,0:T(2,128)S(1)} %add_add_fusion.1), channel_id=1, source_target_pairs={{0,5},{1,4},{2,7},{3,6},{4,1},{5,0},{6,3},{7,2},{8,13},{9,12},{10,... | collective-permute-start | bytes 64520 | tf_op jit(solution)/shard_map/ppermute | solution.py:25
  16.7 1.1 %collective-permute-start.6 = (f32[1,2,2688]{2,1,0:T(2,128)S(1)}, f32[1,2,2688]{2,1,0:T(2,128)S(1)}, u32[]{:S(2)}, u32[]{:S(2)}) collective-permute-start(f32[1,2,2688]{2,1,0:T(2,128)S(1)} %add_add_fusion.1), channel_id=1, source_target_pairs={{0,7},{1,6},{2,5},{3,4},{4,3},{5,2},{6,1},{7,0},{8,15},{9,14},{10,... | collective-permute-start | bytes 64520 | tf_op jit(solution)/shard_map/ppermute | solution.py:25
  17.8 0.6 %collective-permute-start.4 = (f32[1,2,2688]{2,1,0:T(2,128)S(1)}, f32[1,2,2688]{2,1,0:T(2,128)S(1)}, u32[]{:S(2)}, u32[]{:S(2)}) collective-permute-start(f32[1,2,2688]{2,1,0:T(2,128)S(1)} %add_add_fusion.1), channel_id=1, source_target_pairs={{0,3},{1,2},{2,1},{3,0},{4,7},{5,6},{6,5},{7,4},{8,11},{9,10},{10,... | collective-permute-start | bytes 64520 | tf_op jit(solution)/shard_map/ppermute | solution.py:25
  18.4 0.1 reduce
  18.5 1.9 %fetch_weights.1 = (bf16[1280,640]{1,0:T(8,128)(2,1)S(1)}, bf16[640,1280]{1,0:T(8,128)(2,1)S(1)}) custom-call(bf16[1280,640]{1,0:T(8,128)(2,1)} %in_ref, bf16[640,1280]{1,0:T(8,128)(2,1)} %out_ref), custom_call_target="tpu_custom_call" | custom-call | bytes 6553600 | tf_op jit(solution)/shard_map/fetch_weights/pallas_call | solution.py:251
  20.5 0.0 collective-permute-done.5
  20.5 0.3 collective-permute-done.6
  20.8 0.2 collective-permute-done.4
  21.0 1.5 %expert_rows.1 = (f32[2,2688]{1,0:T(2,128)S(1)}, bf16[2,1280]{1,0:T(2,128)(2,1)S(1)}, bf16[2,1280]{1,0:T(2,128)(2,1)S(1)}, bf16[2,640]{1,0:T(2,128)(2,1)S(1)}, bf16[2,640]{1,0:T(2,128)(2,1)S(1)}) custom-call(s32[1]{0:T(128)} %bitcast.3.owned_ref, f32[2,2688]{1,0:T(2,128)S(1)} %add_bitcast_fusion.sums_ref, bf16[1280,640]{1,0:T(8,128)(2,1)S(1)} %get-tuple-element.31.in_ref, ...), custom_call_target="tpu_custom_call" | custom-call | tf_op jit(solution)/shard_map/expert_rows/pallas_call | solution.py:268
  22.6 1.6 %collective-permute-start.8 = (f32[1,2,2688]{2,1,0:T(2,128)S(1)}, f32[1,2,2688]{2,1,0:T(2,128)S(1)}, u32[]{:S(2)}, u32[]{:S(2)}) collective-permute-start(f32[1,2,2688]{2,1,0:T(2,128)S(1)} %bitcast.44), channel_id=1, source_target_pairs={{0,5},{1,4},{2,7},{3,6},{4,1},{5,0},{6,3},{7,2},{8,13},{9,12},{10,... | collective-permute-start | bytes 64520 | tf_op jit(solution)/shard_map/ppermute | solution.py:25
  24.2 0.9 %collective-permute-start.9 = (f32[1,2,2688]{2,1,0:T(2,128)S(1)}, f32[1,2,2688]{2,1,0:T(2,128)S(1)}, u32[]{:S(2)}, u32[]{:S(2)}) collective-permute-start(f32[1,2,2688]{2,1,0:T(2,128)S(1)} %bitcast.45), channel_id=1, source_target_pairs={{0,7},{1,6},{2,5},{3,4},{4,3},{5,2},{6,1},{7,0},{8,15},{9,14},{10,... | collective-permute-start | bytes 64520 | tf_op jit(solution)/shard_map/ppermute | solution.py:25
  25.0 0.8 %collective-permute-start.7 = (f32[1,2,2688]{2,1,0:T(2,128)S(1)}, f32[1,2,2688]{2,1,0:T(2,128)S(1)}, u32[]{:S(2)}, u32[]{:S(2)}) collective-permute-start(f32[1,2,2688]{2,1,0:T(2,128)S(1)} %bitcast.46), channel_id=1, source_target_pairs={{0,3},{1,2},{2,1},{3,0},{4,7},{5,6},{6,5},{7,4},{8,11},{9,10},{10,... | collective-permute-start | bytes 64520 | tf_op jit(solution)/shard_map/ppermute | solution.py:25
  25.9 1.6 %fusion.18 = f32[640,640]{1,0:T(8,128)} fusion(bf16[2,640]{1,0:T(2,128)(2,1)S(1)} %get-tuple-element.43, bf16[2,1280]{1,0:T(2,128)(2,1)S(1)} %get-tuple-element.42, s32[]{:T(128)S(6)} %select_n.86), kind=kOutput, calls=%fused_computation.45 | convolution fusion | flops 1638400 | bytes 1643524 | tf_op jit(solution)/shard_map/od,oh->dh/dot_general | solution.py:287
  27.4 0.0 collective-permute-done.8
  27.5 0.8 %collective-permute-done.9 = f32[1,2,2688]{2,1,0:T(2,128)S(1)} collective-permute-done((f32[1,2,2688]{2,1,0:T(2,128)S(1)}, f32[1,2,2688]{2,1,0:T(2,128)S(1)}, u32[]{:S(2)}, u32[]{:S(2)}) %collective-permute-start.9) | collective-permute-done | bytes 21536 | tf_op jit(solution)/shard_map/ppermute | solution.py:25
  28.3 0.0 collective-permute-done.7
  28.3 0.1 collective-permute-start.12
  28.4 2.0 %collective-permute-start.10 = (f32[1,2,2688]{2,1,0:T(2,128)S(1)}, f32[1,2,2688]{2,1,0:T(2,128)S(1)}, u32[]{:S(2)}, u32[]{:S(2)}) collective-permute-start(f32[1,2,2688]{2,1,0:T(2,128)S(1)} %add_add_fusion), channel_id=1, source_target_pairs={{0,17},{1,16},{2,19},{3,18},{4,21},{5,20},{6,23},{7,22},{8,25},{9,... | collective-permute-start | bytes 64520 | tf_op jit(solution)/shard_map/ppermute | solution.py:25
  30.4 2.0 %collective-permute-start.11 = (f32[1,2,2688]{2,1,0:T(2,128)S(1)}, f32[1,2,2688]{2,1,0:T(2,128)S(1)}, u32[]{:S(2)}, u32[]{:S(2)}) collective-permute-start(f32[1,2,2688]{2,1,0:T(2,128)S(1)} %add_add_fusion), channel_id=1, source_target_pairs={{0,25},{1,24},{2,27},{3,26},{4,29},{5,28},{6,31},{7,30},{8,17},{9,... | collective-permute-start | bytes 64520 | tf_op jit(solution)/shard_map/ppermute | solution.py:25
  32.4 1.6 %fusion.19 = f32[640,640]{1,0:T(8,128)} fusion(bf16[2,640]{1,0:T(2,128)(2,1)S(1)} %get-tuple-element.44, bf16[2,1280]{1,0:T(2,128)(2,1)S(1)} %get-tuple-element.45, s32[]{:T(128)S(6)} %select_n.86), kind=kOutput, calls=%fused_computation.46 | convolution fusion | flops 1638400 | bytes 1643524 | tf_op jit(solution)/shard_map/oh,od->hd/dot_general | solution.py:288
  33.9 0.0 collective-permute-done.12
  34.0 1.4 %collective-permute-done.11 = f32[1,2,2688]{2,1,0:T(2,128)S(1)} collective-permute-done((f32[1,2,2688]{2,1,0:T(2,128)S(1)}, f32[1,2,2688]{2,1,0:T(2,128)S(1)}, u32[]{:S(2)}, u32[]{:S(2)}) %collective-permute-start.11) | collective-permute-done | bytes 21536 | tf_op jit(solution)/shard_map/ppermute | solution.py:25
  35.5 1.1 %score_grads.1 = (bf16[2,512]{1,0:T(2,128)(2,1)S(1)}, bf16[2,512]{1,0:T(2,128)(2,1)S(1)}, f32[2,1280]{1,0:T(2,128)S(1)}) custom-call(f32[1]{0:T(128)S(6)} %copy.19.scale_ref, f32[2,2688]{1,0:T(2,128)S(1)} %bitcast.43, f32[1,128]{1,0:T(1,128)S(1)} %constant_dynamic-slice_fusion.2.totals_ref, bf16[512,1280]{1,0:T(8,128)(2,1)S(1)} %bitcast.39, ...), custom_call_target="tpu_custom_call" | custom-call | tf_op jit(solution)/shard_map/score_grads/pallas_call | solution.py:289
  36.6 0.7 %collective-permute-start.13 = (f32[1,1,2560]{2,1,0:T(1,128)S(1)}, f32[1,1,2560]{2,1,0:T(1,128)S(1)}, u32[]{:S(2)}, u32[]{:S(2)}) collective-permute-start(f32[1,1,2560]{2,1,0:T(1,128)S(1)} %reshape.36), channel_id=1, source_target_pairs={{0,1},{1,0},{2,3},{3,2},{4,5},{5,4},{6,7},{7,6},{8,9},{9,8},{10,11... | collective-permute-start | bytes 30728 | tf_op jit(solution)/shard_map/ppermute | solution.py:29
  37.3 0.7 %multiply_reduce_fusion = (f32[512]{0:T(512)S(1)}, f32[512,1280]{1,0:T(8,128)S(1)}) fusion(f32[512]{0:T(512)S(1)} %reduce, bf16[1,512,1280]{2,1,0:T(8,128)(2,1)S(1)} %copy-done, bf16[2,512]{1,0:T(2,128)(2,1)S(1)} %get-tuple-element.41, f32[2]{0:T(128)S(1)} %add_rsqrt_fusion, bf16[1280,2]{0,1:T(2,128)(2,1)S(1)} %copy-done.3), kind=kOutput, calls=%fused_computation.5 | convolution fusion | flops 5250048 | bytes 3943432 | tf_op jit(solution)/shard_map/sn,sd->nd/dot_general | solution.py:309
  38.0 0.1 collective-permute-done.13
  38.1 1.0 %collective-permute-start.15 = (f32[1,1,2560]{2,1,0:T(1,128)S(1)}, f32[1,1,2560]{2,1,0:T(1,128)S(1)}, u32[]{:S(2)}, u32[]{:S(2)}) collective-permute-start(f32[1,1,2560]{2,1,0:T(1,128)S(1)} %fusion.13), channel_id=1, source_target_pairs={{0,5},{1,4},{2,7},{3,6},{4,1},{5,0},{6,3},{7,2},{8,13},{9,12},{10,... | collective-permute-start | bytes 30728 | tf_op jit(solution)/shard_map/ppermute | solution.py:25
  39.2 1.1 %collective-permute-start.16 = (f32[1,1,2560]{2,1,0:T(1,128)S(1)}, f32[1,1,2560]{2,1,0:T(1,128)S(1)}, u32[]{:S(2)}, u32[]{:S(2)}) collective-permute-start(f32[1,1,2560]{2,1,0:T(1,128)S(1)} %fusion.13), channel_id=1, source_target_pairs={{0,7},{1,6},{2,5},{3,4},{4,3},{5,2},{6,1},{7,0},{8,15},{9,14},{10,... | collective-permute-start | bytes 30728 | tf_op jit(solution)/shard_map/ppermute | solution.py:25
  40.3 1.1 %collective-permute-start.14 = (f32[1,1,2560]{2,1,0:T(1,128)S(1)}, f32[1,1,2560]{2,1,0:T(1,128)S(1)}, u32[]{:S(2)}, u32[]{:S(2)}) collective-permute-start(f32[1,1,2560]{2,1,0:T(1,128)S(1)} %fusion.13), channel_id=1, source_target_pairs={{0,3},{1,2},{2,1},{3,0},{4,7},{5,6},{6,5},{7,4},{8,11},{9,10},{10,... | collective-permute-start | bytes 30728 | tf_op jit(solution)/shard_map/ppermute | solution.py:25
  41.3 2.0 %fusion.1 = bf16[1,512,1280]{2,1,0:T(8,128)(2,1)} fusion(bf16[2,512]{1,0:T(2,128)(2,1)S(1)} %get-tuple-element.39, f32[512,1280]{1,0:T(8,128)S(1)} %get-tuple-element.53, f32[512]{0:T(512)S(1)} %get-tuple-element.52, f32[512]{0:T(512)S(1)} %reduce, bf16[2,2688]{1,0:T(2,128)(2,1)S(1)} %bitcast.47, bf16[1,512,1280]{2,1,0:T(8,128)(2,1)S(1)} %copy-done), kind=kOutput, calls=%fused_computation.3 | convolution fusion | flops 7208960 | bytes 5254144 | tf_op jit(solution)/shard_map/sn,sd->nd/dot_general | solution.py:310
  43.3 0.0 collective-permute-done.14
  43.4 0.1 collective-permute-start.18
  43.5 1.8 %collective-permute-start.19 = (f32[1,1,2560]{2,1,0:T(1,128)S(1)}, f32[1,1,2560]{2,1,0:T(1,128)S(1)}, u32[]{:S(2)}, u32[]{:S(2)}) collective-permute-start(f32[1,1,2560]{2,1,0:T(1,128)S(1)} %add_add_fusion.2), channel_id=1, source_target_pairs={{0,25},{1,24},{2,27},{3,26},{4,29},{5,28},{6,31},{7,30},{8,17},{9,... | collective-permute-start | bytes 30728 | tf_op jit(solution)/shard_map/ppermute | solution.py:25
  45.3 1.2 %collective-permute-start.17 = (f32[1,1,2560]{2,1,0:T(1,128)S(1)}, f32[1,1,2560]{2,1,0:T(1,128)S(1)}, u32[]{:S(2)}, u32[]{:S(2)}) collective-permute-start(f32[1,1,2560]{2,1,0:T(1,128)S(1)} %add_add_fusion.2), channel_id=1, source_target_pairs={{0,9},{1,8},{2,11},{3,10},{4,13},{5,12},{6,15},{7,14},{8,1},{9,0},... | collective-permute-start | bytes 30728 | tf_op jit(solution)/shard_map/ppermute | solution.py:25
  46.4 1.6 %fusion.2 = bf16[1,512,1280]{2,1,0:T(8,128)(2,1)} fusion(bf16[2,512]{1,0:T(2,128)(2,1)S(1)} %get-tuple-element.26, bf16[2,2688]{1,0:T(2,128)(2,1)S(1)} %bitcast.48), kind=kOutput, calls=%fused_computation.4 | convolution fusion | flops 3276800 | bytes 1317888 | tf_op jit(solution)/shard_map/sn,sd->nd/dot_general | solution.py:308
  48.0 0.4 collective-permute-done.19
  48.5 0.2 fusion.8
  48.7 0.7 %fusion.11 = f32[1280,2]{0,1:T(2,128)} fusion(f32[2,1280]{1,0:T(2,128)S(1)} %reshape.37, f32[2]{0:T(128)S(1)} %fusion.8, f32[2]{0:T(128)S(1)} %add_rsqrt_fusion, bf16[1280,2]{0,1:T(2,128)(2,1)S(1)} %copy-done.3), kind=kLoop, calls=%fused_computation.31 | loop fusion | flops 12800 | bytes 25616 | tf_op jit(solution)/shard_map/transpose | solution.py:319
  (34 shorter events, 0.4 us)
Async XLA Ops:
  0.6 10.8 %copy-start.3 = (bf16[1280,2]{0,1:T(2,128)(2,1)S(1)}, bf16[1280,2]{0,1:T(2,128)(2,1)}, u32[]{:S(2)}) copy-start(bf16[1280,2]{0,1:T(2,128)(2,1)} %param.8) | copy-start | bytes 15364
  1.3 0.7 %copy-start.2 = (bf16[1280,2]{0,1:T(2,128)(2,1)S(1)}, bf16[1280,2]{0,1:T(2,128)(2,1)}, u32[]{:S(2)}) copy-start(bf16[1280,2]{0,1:T(2,128)(2,1)} %param.8) | copy-start | bytes 15364
  4.6 1.4 %collective-permute-start = (f32[2,2688]{1,0:T(2,128)S(1)}, f32[2,2688]{1,0:T(2,128)S(1)}, u32[]{:S(2)}, u32[]{:S(2)}) collective-permute-start(f32[2,2688]{1,0:T(2,128)S(1)} %get-tuple-element.27), channel_id=1, source_target_pairs={{0,1},{1,0},{2,3},{3,2},{4,5},{5,4},{6,7},{7,6},{8,9},{9,8},{10,11... | collective-permute-start | bytes 64520 | tf_op jit(solution)/shard_map/ppermute | solution.py:29
  6.2 5.4 %collective-permute-start.2 = (f32[1,2,2688]{2,1,0:T(2,128)S(1)}, f32[1,2,2688]{2,1,0:T(2,128)S(1)}, u32[]{:S(2)}, u32[]{:S(2)}) collective-permute-start(f32[1,2,2688]{2,1,0:T(2,128)S(1)} %get-tuple-element.49), channel_id=1, source_target_pairs={{0,17},{1,16},{2,19},{3,18},{4,21},{5,20},{6,23},{7,22},{8,25},{9,... | collective-permute-start | bytes 64520 | tf_op jit(solution)/shard_map/ppermute | solution.py:25
  9.9 5.1 %collective-permute-start.3 = (f32[1,2,2688]{2,1,0:T(2,128)S(1)}, f32[1,2,2688]{2,1,0:T(2,128)S(1)}, u32[]{:S(2)}, u32[]{:S(2)}) collective-permute-start(f32[1,2,2688]{2,1,0:T(2,128)S(1)} %get-tuple-element.48), channel_id=1, source_target_pairs={{0,25},{1,24},{2,27},{3,26},{4,29},{5,28},{6,31},{7,30},{8,17},{9,... | collective-permute-start | bytes 64520 | tf_op jit(solution)/shard_map/ppermute | solution.py:25
  11.2 3.8 %collective-permute-start.1 = (f32[1,2,2688]{2,1,0:T(2,128)S(1)}, f32[1,2,2688]{2,1,0:T(2,128)S(1)}, u32[]{:S(2)}, u32[]{:S(2)}) collective-permute-start(f32[1,2,2688]{2,1,0:T(2,128)S(1)} %get-tuple-element.47), channel_id=1, source_target_pairs={{0,9},{1,8},{2,11},{3,10},{4,13},{5,12},{6,15},{7,14},{8,1},{9,0},... | collective-permute-start | bytes 64520 | tf_op jit(solution)/shard_map/ppermute | solution.py:25
  15.0 5.4 %collective-permute-start.5 = (f32[1,2,2688]{2,1,0:T(2,128)S(1)}, f32[1,2,2688]{2,1,0:T(2,128)S(1)}, u32[]{:S(2)}, u32[]{:S(2)}) collective-permute-start(f32[1,2,2688]{2,1,0:T(2,128)S(1)} %add_add_fusion.1), channel_id=1, source_target_pairs={{0,5},{1,4},{2,7},{3,6},{4,1},{5,0},{6,3},{7,2},{8,13},{9,12},{10,... | collective-permute-start | bytes 64520 | tf_op jit(solution)/shard_map/ppermute | solution.py:25
  16.7 4.1 %collective-permute-start.6 = (f32[1,2,2688]{2,1,0:T(2,128)S(1)}, f32[1,2,2688]{2,1,0:T(2,128)S(1)}, u32[]{:S(2)}, u32[]{:S(2)}) collective-permute-start(f32[1,2,2688]{2,1,0:T(2,128)S(1)} %add_add_fusion.1), channel_id=1, source_target_pairs={{0,7},{1,6},{2,5},{3,4},{4,3},{5,2},{6,1},{7,0},{8,15},{9,14},{10,... | collective-permute-start | bytes 64520 | tf_op jit(solution)/shard_map/ppermute | solution.py:25
  17.8 3.2 %collective-permute-start.4 = (f32[1,2,2688]{2,1,0:T(2,128)S(1)}, f32[1,2,2688]{2,1,0:T(2,128)S(1)}, u32[]{:S(2)}, u32[]{:S(2)}) collective-permute-start(f32[1,2,2688]{2,1,0:T(2,128)S(1)} %add_add_fusion.1), channel_id=1, source_target_pairs={{0,3},{1,2},{2,1},{3,0},{4,7},{5,6},{6,5},{7,4},{8,11},{9,10},{10,... | collective-permute-start | bytes 64520 | tf_op jit(solution)/shard_map/ppermute | solution.py:25
  22.6 12.9 %copy-start = (bf16[1,512,1280]{2,1,0:T(8,128)(2,1)S(1)}, bf16[1,512,1280]{2,1,0:T(8,128)(2,1)}, u32[]{:S(2)}) copy-start(bf16[1,512,1280]{2,1,0:T(8,128)(2,1)} %param.6) | copy-start | bytes 3932164
  22.6 12.9 %copy-start.1 = (bf16[1,512,1280]{2,1,0:T(8,128)(2,1)S(1)}, bf16[1,512,1280]{2,1,0:T(8,128)(2,1)}, u32[]{:S(2)}) copy-start(bf16[1,512,1280]{2,1,0:T(8,128)(2,1)} %param.7) | copy-start | bytes 3932164
  22.6 4.9 %collective-permute-start.8 = (f32[1,2,2688]{2,1,0:T(2,128)S(1)}, f32[1,2,2688]{2,1,0:T(2,128)S(1)}, u32[]{:S(2)}, u32[]{:S(2)}) collective-permute-start(f32[1,2,2688]{2,1,0:T(2,128)S(1)} %bitcast.44), channel_id=1, source_target_pairs={{0,5},{1,4},{2,7},{3,6},{4,1},{5,0},{6,3},{7,2},{8,13},{9,12},{10,... | collective-permute-start | bytes 64520 | tf_op jit(solution)/shard_map/ppermute | solution.py:25
  24.2 4.1 %collective-permute-start.9 = (f32[1,2,2688]{2,1,0:T(2,128)S(1)}, f32[1,2,2688]{2,1,0:T(2,128)S(1)}, u32[]{:S(2)}, u32[]{:S(2)}) collective-permute-start(f32[1,2,2688]{2,1,0:T(2,128)S(1)} %bitcast.45), channel_id=1, source_target_pairs={{0,7},{1,6},{2,5},{3,4},{4,3},{5,2},{6,1},{7,0},{8,15},{9,14},{10,... | collective-permute-start | bytes 64520 | tf_op jit(solution)/shard_map/ppermute | solution.py:25
  25.0 3.2 %collective-permute-start.7 = (f32[1,2,2688]{2,1,0:T(2,128)S(1)}, f32[1,2,2688]{2,1,0:T(2,128)S(1)}, u32[]{:S(2)}, u32[]{:S(2)}) collective-permute-start(f32[1,2,2688]{2,1,0:T(2,128)S(1)} %bitcast.46), channel_id=1, source_target_pairs={{0,3},{1,2},{2,1},{3,0},{4,7},{5,6},{6,5},{7,4},{8,11},{9,10},{10,... | collective-permute-start | bytes 64520 | tf_op jit(solution)/shard_map/ppermute | solution.py:25
  28.3 5.6 %collective-permute-start.12 = (f32[1,2,2688]{2,1,0:T(2,128)S(1)}, f32[1,2,2688]{2,1,0:T(2,128)S(1)}, u32[]{:S(2)}, u32[]{:S(2)}) collective-permute-start(f32[1,2,2688]{2,1,0:T(2,128)S(1)} %add_add_fusion), channel_id=1, source_target_pairs={{0,9},{1,8},{2,11},{3,10},{4,13},{5,12},{6,15},{7,14},{8,1},{9,0},... | collective-permute-start | bytes 64520 | tf_op jit(solution)/shard_map/ppermute | solution.py:25
  28.4 5.6 %collective-permute-start.10 = (f32[1,2,2688]{2,1,0:T(2,128)S(1)}, f32[1,2,2688]{2,1,0:T(2,128)S(1)}, u32[]{:S(2)}, u32[]{:S(2)}) collective-permute-start(f32[1,2,2688]{2,1,0:T(2,128)S(1)} %add_add_fusion), channel_id=1, source_target_pairs={{0,17},{1,16},{2,19},{3,18},{4,21},{5,20},{6,23},{7,22},{8,25},{9,... | collective-permute-start | bytes 64520 | tf_op jit(solution)/shard_map/ppermute | solution.py:25
  30.4 5.0 %collective-permute-start.11 = (f32[1,2,2688]{2,1,0:T(2,128)S(1)}, f32[1,2,2688]{2,1,0:T(2,128)S(1)}, u32[]{:S(2)}, u32[]{:S(2)}) collective-permute-start(f32[1,2,2688]{2,1,0:T(2,128)S(1)} %add_add_fusion), channel_id=1, source_target_pairs={{0,25},{1,24},{2,27},{3,26},{4,29},{5,28},{6,31},{7,30},{8,17},{9,... | collective-permute-start | bytes 64520 | tf_op jit(solution)/shard_map/ppermute | solution.py:25
  36.6 1.5 %collective-permute-start.13 = (f32[1,1,2560]{2,1,0:T(1,128)S(1)}, f32[1,1,2560]{2,1,0:T(1,128)S(1)}, u32[]{:S(2)}, u32[]{:S(2)}) collective-permute-start(f32[1,1,2560]{2,1,0:T(1,128)S(1)} %reshape.36), channel_id=1, source_target_pairs={{0,1},{1,0},{2,3},{3,2},{4,5},{5,4},{6,7},{7,6},{8,9},{9,8},{10,11... | collective-permute-start | bytes 30728 | tf_op jit(solution)/shard_map/ppermute | solution.py:29
  38.1 5.2 %collective-permute-start.15 = (f32[1,1,2560]{2,1,0:T(1,128)S(1)}, f32[1,1,2560]{2,1,0:T(1,128)S(1)}, u32[]{:S(2)}, u32[]{:S(2)}) collective-permute-start(f32[1,1,2560]{2,1,0:T(1,128)S(1)} %fusion.13), channel_id=1, source_target_pairs={{0,5},{1,4},{2,7},{3,6},{4,1},{5,0},{6,3},{7,2},{8,13},{9,12},{10,... | collective-permute-start | bytes 30728 | tf_op jit(solution)/shard_map/ppermute | solution.py:25
  39.2 4.2 %collective-permute-start.16 = (f32[1,1,2560]{2,1,0:T(1,128)S(1)}, f32[1,1,2560]{2,1,0:T(1,128)S(1)}, u32[]{:S(2)}, u32[]{:S(2)}) collective-permute-start(f32[1,1,2560]{2,1,0:T(1,128)S(1)} %fusion.13), channel_id=1, source_target_pairs={{0,7},{1,6},{2,5},{3,4},{4,3},{5,2},{6,1},{7,0},{8,15},{9,14},{10,... | collective-permute-start | bytes 30728 | tf_op jit(solution)/shard_map/ppermute | solution.py:25
  40.3 3.1 %collective-permute-start.14 = (f32[1,1,2560]{2,1,0:T(1,128)S(1)}, f32[1,1,2560]{2,1,0:T(1,128)S(1)}, u32[]{:S(2)}, u32[]{:S(2)}) collective-permute-start(f32[1,1,2560]{2,1,0:T(1,128)S(1)} %fusion.13), channel_id=1, source_target_pairs={{0,3},{1,2},{2,1},{3,0},{4,7},{5,6},{6,5},{7,4},{8,11},{9,10},{10,... | collective-permute-start | bytes 30728 | tf_op jit(solution)/shard_map/ppermute | solution.py:25
  43.4 4.7 %collective-permute-start.18 = (f32[1,1,2560]{2,1,0:T(1,128)S(1)}, f32[1,1,2560]{2,1,0:T(1,128)S(1)}, u32[]{:S(2)}, u32[]{:S(2)}) collective-permute-start(f32[1,1,2560]{2,1,0:T(1,128)S(1)} %add_add_fusion.2), channel_id=1, source_target_pairs={{0,17},{1,16},{2,19},{3,18},{4,21},{5,20},{6,23},{7,22},{8,25},{9,... | collective-permute-start | bytes 30728 | tf_op jit(solution)/shard_map/ppermute | solution.py:25
  43.5 5.0 %collective-permute-start.19 = (f32[1,1,2560]{2,1,0:T(1,128)S(1)}, f32[1,1,2560]{2,1,0:T(1,128)S(1)}, u32[]{:S(2)}, u32[]{:S(2)}) collective-permute-start(f32[1,1,2560]{2,1,0:T(1,128)S(1)} %add_add_fusion.2), channel_id=1, source_target_pairs={{0,25},{1,24},{2,27},{3,26},{4,29},{5,28},{6,31},{7,30},{8,17},{9,... | collective-permute-start | bytes 30728 | tf_op jit(solution)/shard_map/ppermute | solution.py:25
  45.3 3.2 %collective-permute-start.17 = (f32[1,1,2560]{2,1,0:T(1,128)S(1)}, f32[1,1,2560]{2,1,0:T(1,128)S(1)}, u32[]{:S(2)}, u32[]{:S(2)}) collective-permute-start(f32[1,1,2560]{2,1,0:T(1,128)S(1)} %add_add_fusion.2), channel_id=1, source_target_pairs={{0,9},{1,8},{2,11},{3,10},{4,13},{5,12},{6,15},{7,14},{8,1},{9,0},... | collective-permute-start | bytes 30728 | tf_op jit(solution)/shard_map/ppermute | solution.py:25

commit v10 on v9

--- a/solution.py
+++ b/solution.py
@@ -47,8 +47,15 @@
     return [masks[i : i + 2] for i in range(0, len(masks), 2)]
 
 
-def round_masks(pair):
-    return pair if len(pair) == 1 else [pair[0], pair[1], pair[0] | pair[1]]
+def swaps(pair):
+    return pair if len(pair) == 1 else [pair[0], pair[0] | pair[1], pair[1]]
+
+
+def added(terms, masks):
+    if len(masks) == 1:
+        return terms[masks[0]] + terms[0]
+    low, high = masks
+    return (terms[0] + terms[low]) + (terms[low | high] + terms[high])
 
 
 def sum_to_owner(value, group):
@@ -63,42 +70,54 @@
                 index = index + jnp.where((place ^ mask) & owner_mask != 0, 1 << bit, 0)
             return lax.dynamic_index_in_dim(blocks, index, 0, keepdims=False)
 
-        got = [block_for(0)] + [exchange(block_for(mask), mask) for mask in round_masks(pair)]
-        value = got[0] + got[1] if len(got) == 2 else (got[0] + got[1]) + (got[2] + got[3])
+        terms = {0: block_for(0)}
+        for mask in swaps(pair):
+            terms[mask] = exchange(block_for(mask), mask)
+        value = added(terms, pair)
     return value
+
+
+def round_terms(value, pair):
+    terms = {0: value}
+    for mask in swaps(pair):
+        terms[mask] = exchange(value, mask)
+    return terms
 
 
 def sum_to_all(value, group, later=()):
     place = lax.axis_index("seq")
     for pair in rounds(lax.axis_size("seq")):
-        terms = {0: value}
-        for mask in round_masks(pair):
-            terms[mask] = exchange(value, mask)
-        for mask in pair:
-            upper = (place & mask) != 0
+        terms = round_terms(value, pair)
+        inner = [mask for mask in pair if mask < group]
+        outer = [mask for mask in pair if mask >= group]
+        if inner:
             merged = {}
+            for far in [0] + outer if len(outer) == 1 else [0]:
+                merged[far] = added({mask ^ far: terms[mask] for mask in terms}, inner)
+            terms = merged
+        value = terms[0]
+        for mask in outer:
+            kept = {}
             for key in terms:
                 if key & mask:
                     continue
-                near, far = terms[key], terms[key | mask]
-                if mask < group:
-                    merged[key] = near + far
-                else:
-                    merged[key] = jnp.where(
-                        upper, jnp.concatenate([far, near]), jnp.concatenate([near, far])
-                    )
-            terms = merged
-        value = terms[0]
+                side = lax.broadcasted_iota(jnp.int32, (2,) + (1,) * value.ndim, 0)
+                same = side == jnp.where((place & mask) != 0, 1, 0)
+                both = jnp.where(same, terms[key][None], terms[key | mask][None])
+                kept[key] = both.reshape((-1,) + both.shape[2:])
+            terms = kept
+            value = terms[0]
         if later and pair[0] == 1:
             value, *later = lax.optimization_barrier((value, *later))
     return (value, *later) if later else value
 
 
-def token_sums(scale_ref, phi_ref, tok_ref, cot_ref, message_ref, exp_ref, combine_ref, tok_scale_ref, norm_ref, tok_buf, cot_buf, sems):
+def token_sums(scale_ref, phi_ref, tok_ref, cot_ref, message_ref, exp_ref, combine_ref, tok_scale_ref, norm_ref, phi_buf, tok_buf, cot_buf, phi_sem, sems):
     experts, width = phi_ref.shape
     blocks = sems.shape[1]
     rows = tok_buf.shape[0] // blocks
     pieces = [pl.ds(index * rows, rows) for index in range(blocks)]
+    phi_copy = pltpu.make_async_copy(phi_ref, phi_buf, phi_sem)
     tok_copies = [
         pltpu.make_async_copy(tok_ref.at[piece], tok_buf.at[piece], sems.at[0, index])
         for index, piece in enumerate(pieces)
@@ -107,32 +126,36 @@
         pltpu.make_async_copy(cot_ref.at[piece], cot_buf.at[piece], sems.at[1, index])
         for index, piece in enumerate(pieces)
     ]
-    for copy in tok_copies + cot_copies:
+    for copy in [phi_copy] + tok_copies + cot_copies:
         copy.start()
-    phi = phi_ref[...].astype(f32)
+    phi_copy.wait()
+    phi = phi_buf[...].astype(f32)
     phi_scale = lax.rsqrt(jnp.sum(phi * phi, axis=1, keepdims=True) + epsilon)
     phi_norm = (phi * phi_scale).astype(bf16)
+    in_parts = 0.0
+    totals = 0.0
     for copy, piece in zip(tok_copies, pieces):
         copy.wait()
-        tok_f32 = tok_buf[piece, :].astype(f32)
+        tok_in = tok_buf[piece, :]
+        tok_f32 = tok_in.astype(f32)
         tok_scale = lax.rsqrt(jnp.sum(tok_f32 * tok_f32, axis=1, keepdims=True) + epsilon)
-        norm_ref[piece, :] = (tok_f32 * tok_scale).astype(bf16)
+        tok_norm = (tok_f32 * tok_scale).astype(bf16)
+        norm_ref[piece, :] = tok_norm
         tok_scale_ref[piece, :] = tok_scale
-    logits = scale_ref[0] * lax.dot_general(phi_norm, norm_ref[...], ROWS, preferred_element_type=f32)
-    exp_scores = jnp.exp(logits)
-    combine = (exp_scores / jnp.sum(exp_scores, axis=0, keepdims=True)).astype(bf16)
-    exp_high = exp_scores.astype(bf16).astype(f32)
-    halves = jnp.concatenate([exp_high, exp_scores - exp_high], axis=0).astype(bf16)
-    in_parts = jnp.dot(halves, tok_buf[...], preferred_element_type=f32)
+        logits = scale_ref[0] * lax.dot_general(phi_norm, tok_norm, ROWS, preferred_element_type=f32)
+        exp_scores = jnp.exp(logits)
+        exp_high = exp_scores.astype(bf16).astype(f32)
+        halves = jnp.concatenate([exp_high, exp_scores - exp_high], axis=0).astype(bf16)
+        in_parts += jnp.dot(halves, tok_in, preferred_element_type=f32)
+        totals += jnp.sum(exp_scores, axis=1, keepdims=True)
+        exp_ref[:, piece] = exp_scores
+        combine_ref[:, piece] = (exp_scores / jnp.sum(exp_scores, axis=0, keepdims=True)).astype(bf16)
     message_ref[:, :width] = in_parts[:experts] + in_parts[experts:]
     spare = message_ref.shape[1] - 2 * width
-    total = as_row(jnp.sum(exp_scores, axis=1, keepdims=True), spare)
-    message_ref[:, 2 * width :] = jnp.broadcast_to(total, (experts, spare))
-    exp_ref[...] = exp_scores
-    combine_ref[...] = combine
+    message_ref[:, 2 * width :] = jnp.broadcast_to(as_row(totals, spare), (experts, spare))
     for copy in cot_copies:
         copy.wait()
-    message_ref[:, width : 2 * width] = jnp.dot(combine, cot_buf[...], preferred_element_type=f32)
+    message_ref[:, width : 2 * width] = jnp.dot(combine_ref[...], cot_buf[...], preferred_element_type=f32)
 
 
 def fetch(in_ref, out_ref, in_buf, out_buf, sems):
@@ -207,6 +230,19 @@
     dispatch_ref[...] = dispatch_f.astype(bf16)
 
 
+def finish(phi_ref, *refs):
+    *term_refs, grad_ref = refs
+    own, *others = [ref[0] for ref in term_refs]
+    phi_grad = own + others[-1]
+    if len(others) > 1:
+        phi_grad = phi_grad + (others[0] + others[1])
+    phi = phi_ref[...].astype(f32)
+    phi_scale = lax.rsqrt(jnp.sum(phi * phi, axis=1, keepdims=True) + epsilon)
+    phi_unit = phi * phi_scale
+    along = jnp.sum(phi_unit * phi_grad, axis=1, keepdims=True)
+    grad_ref[...] = phi_scale * (phi_grad - phi_unit * along)
+
+
 def in_place(operand):
     return pltpu.with_memory_space_constraint(operand, pltpu.HBM)
 
@@ -230,7 +266,7 @@
     phi = router.T
     message, exp_scores, combine, tok_scale, tok_norm = pl.pallas_call(
         token_sums,
-        in_specs=[scalar, in_vmem, in_hbm, in_hbm],
+        in_specs=[scalar, in_hbm, in_hbm, in_hbm],
         out_shape=[
             jax.ShapeDtypeStruct((experts, length), f32),
             jax.ShapeDtypeStruct((experts, count), f32),
@@ -239,13 +275,15 @@
             jax.ShapeDtypeStruct((count, width), bf16),
         ],
         scratch_shapes=[
+            pltpu.VMEM((experts, width), bf16),
             pltpu.VMEM((count, width), bf16),
             pltpu.VMEM((count, width), bf16),
-            pltpu.SemaphoreType.DMA((2, PIECES)),
+            pltpu.SemaphoreType.DMA,
+            pltpu.SemaphoreType.DMA((2, 2)),
         ],
         compiler_params=params,
         name="token_sums",
-    )(logit_scale, phi, in_place(tok_in), in_place(tok_cot))
+    )(logit_scale, in_place(phi), in_place(tok_in), in_place(tok_cot))
     message = jnp.stack(of_clips(message), axis=1)
     message, expert_in, expert_out = lax.optimization_barrier((message, expert_in, expert_out))
     expert_in, expert_out = pl.pallas_call(
@@ -297,8 +335,18 @@
         compiler_params=params,
         name="score_grads",
     )(logit_scale, slots, totals, tok_in, tok_cot, tok_norm, exp_scores)
-    phi_flat = sum(of_clips(phi_part.reshape(1, 1, -1)))
-    phi_grad = sum_to_all(phi_flat, size).reshape(experts, width)
+    phi_sum = sum(of_clips(phi_part[None]))
+    *earlier, final = rounds(size)
+    for pair in earlier:
+        phi_sum = added(round_terms(phi_sum, pair), pair)
+    terms = round_terms(phi_sum, final)
+    grad_router = pl.pallas_call(
+        finish,
+        in_specs=[in_vmem] * (1 + len(terms)),
+        out_shape=jax.ShapeDtypeStruct((experts, width), f32),
+        compiler_params=params,
+        name="finish",
+    )(phi, terms.pop(0), *[terms[mask] for mask in sorted(terms, reverse=True)])
     phi_f32 = phi.astype(f32)
     phi_scale = lax.rsqrt(jnp.sum(phi_f32 * phi_f32, axis=1, keepdims=True) + epsilon)
     phi_unit = phi_f32 * phi_scale
@@ -313,9 +361,6 @@
         norm_grad - tok_unit * jnp.sum(tok_unit * norm_grad, axis=1, keepdims=True)
     )
     grad_tokens = (through + back_norm).astype(bf16)
-    grad_router = phi_scale * (
-        phi_grad - phi_unit * jnp.sum(phi_unit * phi_grad, axis=1, keepdims=True)
-    )
     return (mixed[None], grad_tokens[None], grad_expert_in, grad_expert_out, grad_router.T)
 
 

time: 49.6 us -> 49.6 us (level)
  Pallas kernels: 7.18 us -> 9.02 us
  other arithmetic: 1.41 us -> 0.53 us
  local copies, waits for them, and re-layouts: 0.82 us -> 0.11 us
    pallas_call x1 -> x2, Pallas kernels: 2.64 us -> 4.48 us  [the longest x1 3.68 us: per_device(): pl.pallas_call(token_sums, in_specs=[scalar, in_hbm, in_hbm, in_hbm], out...]
    unnamed x10 -> x6, local copies, waits for them, and re-layouts: 0.72 us -> 0.01 us
    transpose x1 -> x0, other arithmetic: 0.68 us -> none  [per_device(): return (mixed[None], grad_tokens[None], grad_expert_in, grad_expert_out,...]
    ppermute x18, starting transfers between devices: 22.2 us -> 22.7 us  [exchange(): return lax.ppermute(value, AXES, pairs)]
  transfers between devices with their start and end apart: 20 -> 20, of which waited for: 8 -> 13; matrix products, arithmetic and copies ran while one was open for 16% -> 16% of each run, Pallas kernels for 4% -> 4%
where the time goes in v10:
time: 49.6 us; the launch traced here: 49.4 us
  starting transfers between devices  23.4 us (47%)
  Pallas kernels  9.02 us (18%)
  matrix products  7.52 us (15%)
  waiting for transfers between devices  7.35 us (15%)
  between operations  1.47 us (3%)
  other arithmetic  0.53 us (1%)
    ppermute x18, starting transfers between devices, exchange(): return lax.ppermute(value, AXES, pairs)  22.7 us
    ppermute x18, waiting for transfers between devices, exchange(): return lax.ppermute(value, AXES, pairs)  6.37 us
    pallas_call x1, Pallas kernels, per_device(): pl.pallas_call(token_sums, in_specs=[scalar, in_hbm, in_hbm, in_hbm], out...  3.68 us
    dot_general x1, matrix products, per_device(): jnp.einsum('sn,sd->nd', dispatch, slot_dx, preferred_element_type=f32)  1.99 us
    pallas_call x1, Pallas kernels, per_device(): pl.pallas_call(fetch, in_specs=[in_hbm] * 2, out_specs=[in_vmem] * 2, out...  1.94 us
    dot_general x1, matrix products, per_device(): jnp.einsum('sn,sd->nd', combine, slot_y, preferred_element_type=f32)  1.61 us
    dot_general x1, matrix products, per_device(): jnp.einsum('od,oh->dh', mine_x, pre_grad, preferred_element_type=f32)  1.59 us
    dot_general x1, matrix products, per_device(): jnp.einsum('oh,od->hd', hidden, mine_cot, preferred_element_type=f32)  1.59 us
  transfers between devices with their start and end apart: 20, of which 13 were waited for; matrix products, arithmetic and copies ran while one was open for 16% of the time, Pallas kernels for 4%

profile of v10, /device:TPU:0, one launch (start us, length us, event | category | flops | bytes accessed | tf_op | source)
XLA Modules:
  0.0 49.4 jit_solution(9940054310503270311)
XLA Ops:
  1.3 3.7 %token_sums.1 = (f32[2,2688]{1,0:T(2,128)S(1)}, f32[2,512]{1,0:T(2,128)S(1)}, bf16[2,512]{1,0:T(2,128)(2,1)S(1)}, f32[512,1]{1,0:T(8,128)S(1)}, bf16[512,1280]{1,0:T(8,128)(2,1)S(1)}) custom-call(f32[1]{0:T(128)S(6)} %copy.13.scale_ref, bf16[2,1280]{1,0:T(2,128)(2,1)} %bitcast.42, bf16[512,1280]{1,0:T(8,128)(2,1)} %bitcast.38, bf16[512,1280]{1,0:T(8,128)(2,1)} %bitcast.40), custom_call_target="tpu_custom_call" | custom-call | tf_op jit(solution)/shard_map/token_sums/pallas_call | solution.py:267
  5.0 0.5 %collective-permute-start = (f32[2,2688]{1,0:T(2,128)S(1)}, f32[2,2688]{1,0:T(2,128)S(1)}, u32[]{:S(2)}, u32[]{:S(2)}) collective-permute-start(f32[2,2688]{1,0:T(2,128)S(1)} %get-tuple-element.27), channel_id=1, source_target_pairs={{0,1},{1,0},{2,3},{3,2},{4,5},{5,4},{6,7},{7,6},{8,9},{9,8},{10,11... | collective-permute-start | bytes 64520 | tf_op jit(solution)/shard_map/ppermute | solution.py:29
  5.5 0.1 fusion.3
  5.7 0.7 %collective-permute-done = f32[2,2688]{1,0:T(2,128)S(1)} collective-permute-done((f32[2,2688]{1,0:T(2,128)S(1)}, f32[2,2688]{1,0:T(2,128)S(1)}, u32[]{:S(2)}, u32[]{:S(2)}) %collective-permute-start) | collective-permute-done | bytes 21536 | tf_op jit(solution)/shard_map/ppermute | solution.py:29
  6.5 4.8 %collective-permute-start.2 = (f32[1,2,2688]{2,1,0:T(2,128)S(1)}, f32[1,2,2688]{2,1,0:T(2,128)S(1)}, u32[]{:S(2)}, u32[]{:S(2)}) collective-permute-start(f32[1,2,2688]{2,1,0:T(2,128)S(1)} %get-tuple-element.51), channel_id=1, source_target_pairs={{0,25},{1,24},{2,27},{3,26},{4,29},{5,28},{6,31},{7,30},{8,17},{9,... | collective-permute-start | bytes 64520 | tf_op jit(solution)/shard_map/ppermute | solution.py:25
  11.3 0.6 %collective-permute-start.1 = (f32[1,2,2688]{2,1,0:T(2,128)S(1)}, f32[1,2,2688]{2,1,0:T(2,128)S(1)}, u32[]{:S(2)}, u32[]{:S(2)}) collective-permute-start(f32[1,2,2688]{2,1,0:T(2,128)S(1)} %get-tuple-element.49), channel_id=1, source_target_pairs={{0,9},{1,8},{2,11},{3,10},{4,13},{5,12},{6,15},{7,14},{8,1},{9,0},... | collective-permute-start | bytes 64520 | tf_op jit(solution)/shard_map/ppermute | solution.py:25
  11.9 0.9 %collective-permute-done.2 = f32[1,2,2688]{2,1,0:T(2,128)S(1)} collective-permute-done((f32[1,2,2688]{2,1,0:T(2,128)S(1)}, f32[1,2,2688]{2,1,0:T(2,128)S(1)}, u32[]{:S(2)}, u32[]{:S(2)}) %collective-permute-start.2) | collective-permute-done | bytes 21536 | tf_op jit(solution)/shard_map/ppermute | solution.py:25
  12.8 2.6 %collective-permute-done.3 = f32[1,2,2688]{2,1,0:T(2,128)S(1)} collective-permute-done((f32[1,2,2688]{2,1,0:T(2,128)S(1)}, f32[1,2,2688]{2,1,0:T(2,128)S(1)}, u32[]{:S(2)}, u32[]{:S(2)}) %collective-permute-start.3) | collective-permute-done | bytes 21536 | tf_op jit(solution)/shard_map/ppermute | solution.py:25
  15.4 2.5 %collective-permute-start.5 = (f32[1,2,2688]{2,1,0:T(2,128)S(1)}, f32[1,2,2688]{2,1,0:T(2,128)S(1)}, u32[]{:S(2)}, u32[]{:S(2)}) collective-permute-start(f32[1,2,2688]{2,1,0:T(2,128)S(1)} %add_add_fusion.1), channel_id=1, source_target_pairs={{0,7},{1,6},{2,5},{3,4},{4,3},{5,2},{6,1},{7,0},{8,15},{9,14},{10,... | collective-permute-start | bytes 64520 | tf_op jit(solution)/shard_map/ppermute | solution.py:25
  17.9 0.3 collective-permute-start.6
  18.2 0.5 collective-permute-start.4
  18.7 0.1 reduce
  18.8 1.9 %fetch_weights.1 = (bf16[1280,640]{1,0:T(8,128)(2,1)S(1)}, bf16[640,1280]{1,0:T(8,128)(2,1)S(1)}) custom-call(bf16[1280,640]{1,0:T(8,128)(2,1)} %in_ref, bf16[640,1280]{1,0:T(8,128)(2,1)} %out_ref), custom_call_target="tpu_custom_call" | custom-call | bytes 6553600 | tf_op jit(solution)/shard_map/fetch_weights/pallas_call | solution.py:289
  20.8 0.0 collective-permute-done.5
  20.8 0.3 collective-permute-done.6
  21.1 0.3 collective-permute-done.4
  21.4 1.5 %expert_rows.1 = (f32[2,2688]{1,0:T(2,128)S(1)}, bf16[2,1280]{1,0:T(2,128)(2,1)S(1)}, bf16[2,1280]{1,0:T(2,128)(2,1)S(1)}, bf16[2,640]{1,0:T(2,128)(2,1)S(1)}, bf16[2,640]{1,0:T(2,128)(2,1)S(1)}) custom-call(s32[1]{0:T(128)} %bitcast.3.owned_ref, f32[2,2688]{1,0:T(2,128)S(1)} %add_bitcast_fusion.2.sums_ref, bf16[1280,640]{1,0:T(8,128)(2,1)S(1)} %get-tuple-element.31.in_ref, ...), custom_call_target="tpu_custom_call" | custom-call | tf_op jit(solution)/shard_map/expert_rows/pallas_call | solution.py:306
  22.9 1.6 %collective-permute-start.8 = (f32[1,2,2688]{2,1,0:T(2,128)S(1)}, f32[1,2,2688]{2,1,0:T(2,128)S(1)}, u32[]{:S(2)}, u32[]{:S(2)}) collective-permute-start(f32[1,2,2688]{2,1,0:T(2,128)S(1)} %bitcast.44), channel_id=1, source_target_pairs={{0,7},{1,6},{2,5},{3,4},{4,3},{5,2},{6,1},{7,0},{8,15},{9,14},{10,... | collective-permute-start | bytes 64520 | tf_op jit(solution)/shard_map/ppermute | solution.py:25
  24.6 0.5 collective-permute-start.9
  25.0 1.1 %collective-permute-start.7 = (f32[1,2,2688]{2,1,0:T(2,128)S(1)}, f32[1,2,2688]{2,1,0:T(2,128)S(1)}, u32[]{:S(2)}, u32[]{:S(2)}) collective-permute-start(f32[1,2,2688]{2,1,0:T(2,128)S(1)} %bitcast.46), channel_id=1, source_target_pairs={{0,3},{1,2},{2,1},{3,0},{4,7},{5,6},{6,5},{7,4},{8,11},{9,10},{10,... | collective-permute-start | bytes 64520 | tf_op jit(solution)/shard_map/ppermute | solution.py:25
  26.1 1.6 %fusion.11 = f32[640,640]{1,0:T(8,128)} fusion(bf16[2,640]{1,0:T(2,128)(2,1)S(1)} %get-tuple-element.43, bf16[2,1280]{1,0:T(2,128)(2,1)S(1)} %get-tuple-element.42, s32[]{:T(128)S(6)} %select_n.90), kind=kOutput, calls=%fused_computation.27 | convolution fusion | flops 1638400 | bytes 1643524 | tf_op jit(solution)/shard_map/od,oh->dh/dot_general | solution.py:325
  27.7 0.1 collective-permute-done.9
  27.8 0.4 collective-permute-done.7
  28.3 1.5 %collective-permute-start.11 = (f32[1,2,2688]{2,1,0:T(2,128)S(1)}, f32[1,2,2688]{2,1,0:T(2,128)S(1)}, u32[]{:S(2)}, u32[]{:S(2)}) collective-permute-start(f32[1,2,2688]{2,1,0:T(2,128)S(1)} %add_add_fusion), channel_id=1, source_target_pairs={{0,25},{1,24},{2,27},{3,26},{4,29},{5,28},{6,31},{7,30},{8,17},{9,... | collective-permute-start | bytes 64520 | tf_op jit(solution)/shard_map/ppermute | solution.py:25
  29.8 0.4 collective-permute-start.12
  30.2 2.1 %collective-permute-start.10 = (f32[1,2,2688]{2,1,0:T(2,128)S(1)}, f32[1,2,2688]{2,1,0:T(2,128)S(1)}, u32[]{:S(2)}, u32[]{:S(2)}) collective-permute-start(f32[1,2,2688]{2,1,0:T(2,128)S(1)} %add_add_fusion), channel_id=1, source_target_pairs={{0,9},{1,8},{2,11},{3,10},{4,13},{5,12},{6,15},{7,14},{8,1},{9,0},... | collective-permute-start | bytes 64520 | tf_op jit(solution)/shard_map/ppermute | solution.py:25
  32.2 1.6 %fusion.9 = f32[640,640]{1,0:T(8,128)} fusion(bf16[2,640]{1,0:T(2,128)(2,1)S(1)} %get-tuple-element.44, bf16[2,1280]{1,0:T(2,128)(2,1)S(1)} %get-tuple-element.45, s32[]{:T(128)S(6)} %select_n.90), kind=kOutput, calls=%fused_computation.25 | convolution fusion | flops 1638400 | bytes 1643524 | tf_op jit(solution)/shard_map/oh,od->hd/dot_general | solution.py:326
  33.8 0.0 collective-permute-done.11
  33.8 0.2 collective-permute-done.12
  34.1 0.3 collective-permute-done.10
  34.4 0.1 fusion.16
  34.6 1.1 %score_grads.1 = (bf16[2,512]{1,0:T(2,128)(2,1)S(1)}, bf16[2,512]{1,0:T(2,128)(2,1)S(1)}, f32[2,1280]{1,0:T(2,128)S(1)}) custom-call(f32[1]{0:T(128)S(6)} %copy.13.scale_ref, f32[2,2688]{1,0:T(2,128)S(1)} %get-tuple-element.48.slots_ref, f32[1,128]{1,0:T(1,128)S(1)} %constant_dynamic-slice_fusion.1.totals_ref, bf16[512,1280]{1,0:T(8,128)(2,1)S(1)} %bitcast.39, ...), custom_call_target="tpu_custom_call" | custom-call | tf_op jit(solution)/shard_map/score_grads/pallas_call | solution.py:327
  35.6 0.2 collective-permute-start.13
  35.8 0.7 %multiply_reduce_fusion = (f32[512]{0:T(512)S(1)}, f32[512,1280]{1,0:T(8,128)S(1)}) fusion(f32[512]{0:T(512)S(1)} %reduce, bf16[1,512,1280]{2,1,0:T(8,128)(2,1)S(1)} %copy-done, bf16[2,512]{1,0:T(2,128)(2,1)S(1)} %get-tuple-element.41, f32[2]{0:T(128)S(1)} %add_rsqrt_fusion, bf16[1280,2]{0,1:T(2,128)(2,1)S(1)} %copy-done.2), kind=kOutput, calls=%fused_computation.5 | convolution fusion | flops 5250048 | bytes 3943432 | tf_op jit(solution)/shard_map/sn,sd->nd/dot_general | solution.py:357
  36.5 0.3 collective-permute-done.13
  36.8 2.1 %collective-permute-start.15 = (f32[1,2,1280]{2,1,0:T(2,128)S(1)}, f32[1,2,1280]{2,1,0:T(2,128)S(1)}, u32[]{:S(2)}, u32[]{:S(2)}) collective-permute-start(f32[1,2,1280]{2,1,0:T(2,128)S(1)} %select_add_fusion), channel_id=1, source_target_pairs={{0,7},{1,6},{2,5},{3,4},{4,3},{5,2},{6,1},{7,0},{8,15},{9,14},{10,... | collective-permute-start | bytes 30728 | tf_op jit(solution)/shard_map/ppermute | solution.py:25
  39.0 0.5 collective-permute-start.16
  39.4 0.4 collective-permute-start.14
  39.9 2.0 %fusion.1 = bf16[1,512,1280]{2,1,0:T(8,128)(2,1)} fusion(bf16[2,512]{1,0:T(2,128)(2,1)S(1)} %get-tuple-element.39, f32[512,1280]{1,0:T(8,128)S(1)} %get-tuple-element.55, f32[512]{0:T(512)S(1)} %get-tuple-element.54, f32[512]{0:T(512)S(1)} %reduce, bf16[2,2688]{1,0:T(2,128)(2,1)S(1)} %get-tuple-element.47, bf16[1,512,1280]{2,1,0:T(8,128)(2,1)S(1)} %copy-done), kind=kOutput, calls=%fused_computation.3 | convolution fusion | flops 7208960 | bytes 5254144 | tf_op jit(solution)/shard_map/sn,sd->nd/dot_general | solution.py:358
  41.8 0.0 collective-permute-done.15
  41.9 0.2 collective-permute-done.16
  42.1 0.5 collective-permute-done.14
  42.5 1.9 %collective-permute-start.17 = (f32[1,2,1280]{2,1,0:T(2,128)S(1)}, f32[1,2,1280]{2,1,0:T(2,128)S(1)}, u32[]{:S(2)}, u32[]{:S(2)}) collective-permute-start(f32[1,2,1280]{2,1,0:T(2,128)S(1)} %add_add_fusion.2.refs_0_), channel_id=1, source_target_pairs={{0,25},{1,24},{2,27},{3,26},{4,29},{5,28},{6,31},{7,30},{8,17},{9,... | collective-permute-start | bytes 30728 | tf_op jit(solution)/shard_map/ppermute | solution.py:25
  44.5 0.4 collective-permute-start.18
  44.8 1.6 %collective-permute-start.19 = (f32[1,2,1280]{2,1,0:T(2,128)S(1)}, f32[1,2,1280]{2,1,0:T(2,128)S(1)}, u32[]{:S(2)}, u32[]{:S(2)}) collective-permute-start(f32[1,2,1280]{2,1,0:T(2,128)S(1)} %add_add_fusion.2.refs_0_), channel_id=1, source_target_pairs={{0,9},{1,8},{2,11},{3,10},{4,13},{5,12},{6,15},{7,14},{8,1},{9,0},... | collective-permute-start | bytes 30728 | tf_op jit(solution)/shard_map/ppermute | solution.py:25
  46.5 1.6 %fusion.2 = bf16[1,512,1280]{2,1,0:T(8,128)(2,1)} fusion(bf16[2,512]{1,0:T(2,128)(2,1)S(1)} %get-tuple-element.26, bf16[2,2688]{1,0:T(2,128)(2,1)S(1)} %get-tuple-element.47), kind=kOutput, calls=%fused_computation.4 | convolution fusion | flops 3276800 | bytes 1317888 | tf_op jit(solution)/shard_map/sn,sd->nd/dot_general | solution.py:356
  48.1 0.5 collective-permute-done.18.refs_2_
  48.6 0.8 %finish.1 = f32[2,1280]{1,0:T(2,128)} custom-call(bf16[2,1280]{1,0:T(2,128)(2,1)S(1)} %bitcast.43, f32[1,2,1280]{2,1,0:T(2,128)S(1)} %add_add_fusion.2.refs_0_, f32[1,2,1280]{2,1,0:T(2,128)S(1)} %collective-permute-done.17.refs_1_, f32[1,2,1280]{2,1,0:T(2,128)S(1)} %collective-permute-done.18.refs_2_, f32[1,2,1280]{2,1,0:T(2,128)S(1)} %collective-permute-done.19.refs_3_), custom_call_target="tpu_custom_call" | custom-call | tf_op jit(solution)/shard_map/finish/pallas_call | solution.py:343
  (29 shorter events, 0.3 us)
Async XLA Ops:
  0.6 4.9 %copy-start.2 = (bf16[1280,2]{0,1:T(2,128)(2,1)S(1)}, bf16[1280,2]{0,1:T(2,128)(2,1)}, u32[]{:S(2)}) copy-start(bf16[1280,2]{0,1:T(2,128)(2,1)} %param.8) | copy-start | bytes 15364
  5.0 1.4 %collective-permute-start = (f32[2,2688]{1,0:T(2,128)S(1)}, f32[2,2688]{1,0:T(2,128)S(1)}, u32[]{:S(2)}, u32[]{:S(2)}) collective-permute-start(f32[2,2688]{1,0:T(2,128)S(1)} %get-tuple-element.27), channel_id=1, source_target_pairs={{0,1},{1,0},{2,3},{3,2},{4,5},{5,4},{6,7},{7,6},{8,9},{9,8},{10,11... | collective-permute-start | bytes 64520 | tf_op jit(solution)/shard_map/ppermute | solution.py:29
  6.5 6.3 %collective-permute-start.2 = (f32[1,2,2688]{2,1,0:T(2,128)S(1)}, f32[1,2,2688]{2,1,0:T(2,128)S(1)}, u32[]{:S(2)}, u32[]{:S(2)}) collective-permute-start(f32[1,2,2688]{2,1,0:T(2,128)S(1)} %get-tuple-element.51), channel_id=1, source_target_pairs={{0,25},{1,24},{2,27},{3,26},{4,29},{5,28},{6,31},{7,30},{8,17},{9,... | collective-permute-start | bytes 64520 | tf_op jit(solution)/shard_map/ppermute | solution.py:25
  11.3 4.1 %collective-permute-start.3 = (f32[1,2,2688]{2,1,0:T(2,128)S(1)}, f32[1,2,2688]{2,1,0:T(2,128)S(1)}, u32[]{:S(2)}, u32[]{:S(2)}) collective-permute-start(f32[1,2,2688]{2,1,0:T(2,128)S(1)} %get-tuple-element.50), channel_id=1, source_target_pairs={{0,17},{1,16},{2,19},{3,18},{4,21},{5,20},{6,23},{7,22},{8,25},{9,... | collective-permute-start | bytes 64520 | tf_op jit(solution)/shard_map/ppermute | solution.py:25
  11.3 4.1 %collective-permute-start.1 = (f32[1,2,2688]{2,1,0:T(2,128)S(1)}, f32[1,2,2688]{2,1,0:T(2,128)S(1)}, u32[]{:S(2)}, u32[]{:S(2)}) collective-permute-start(f32[1,2,2688]{2,1,0:T(2,128)S(1)} %get-tuple-element.49), channel_id=1, source_target_pairs={{0,9},{1,8},{2,11},{3,10},{4,13},{5,12},{6,15},{7,14},{8,1},{9,0},... | collective-permute-start | bytes 64520 | tf_op jit(solution)/shard_map/ppermute | solution.py:25
  15.4 5.3 %collective-permute-start.5 = (f32[1,2,2688]{2,1,0:T(2,128)S(1)}, f32[1,2,2688]{2,1,0:T(2,128)S(1)}, u32[]{:S(2)}, u32[]{:S(2)}) collective-permute-start(f32[1,2,2688]{2,1,0:T(2,128)S(1)} %add_add_fusion.1), channel_id=1, source_target_pairs={{0,7},{1,6},{2,5},{3,4},{4,3},{5,2},{6,1},{7,0},{8,15},{9,14},{10,... | collective-permute-start | bytes 64520 | tf_op jit(solution)/shard_map/ppermute | solution.py:25
  17.9 3.2 %collective-permute-start.6 = (f32[1,2,2688]{2,1,0:T(2,128)S(1)}, f32[1,2,2688]{2,1,0:T(2,128)S(1)}, u32[]{:S(2)}, u32[]{:S(2)}) collective-permute-start(f32[1,2,2688]{2,1,0:T(2,128)S(1)} %add_add_fusion.1), channel_id=1, source_target_pairs={{0,5},{1,4},{2,7},{3,6},{4,1},{5,0},{6,3},{7,2},{8,13},{9,12},{10,... | collective-permute-start | bytes 64520 | tf_op jit(solution)/shard_map/ppermute | solution.py:25
  18.2 3.2 %collective-permute-start.4 = (f32[1,2,2688]{2,1,0:T(2,128)S(1)}, f32[1,2,2688]{2,1,0:T(2,128)S(1)}, u32[]{:S(2)}, u32[]{:S(2)}) collective-permute-start(f32[1,2,2688]{2,1,0:T(2,128)S(1)} %add_add_fusion.1), channel_id=1, source_target_pairs={{0,3},{1,2},{2,1},{3,0},{4,7},{5,6},{6,5},{7,4},{8,11},{9,10},{10,... | collective-permute-start | bytes 64520 | tf_op jit(solution)/shard_map/ppermute | solution.py:25
  22.9 11.6 %copy-start = (bf16[1,512,1280]{2,1,0:T(8,128)(2,1)S(1)}, bf16[1,512,1280]{2,1,0:T(8,128)(2,1)}, u32[]{:S(2)}) copy-start(bf16[1,512,1280]{2,1,0:T(8,128)(2,1)} %param.6) | copy-start | bytes 3932164
  22.9 11.6 %copy-start.1 = (bf16[1,512,1280]{2,1,0:T(8,128)(2,1)S(1)}, bf16[1,512,1280]{2,1,0:T(8,128)(2,1)}, u32[]{:S(2)}) copy-start(bf16[1,512,1280]{2,1,0:T(8,128)(2,1)} %param.7) | copy-start | bytes 3932164
  22.9 4.8 %collective-permute-start.8 = (f32[1,2,2688]{2,1,0:T(2,128)S(1)}, f32[1,2,2688]{2,1,0:T(2,128)S(1)}, u32[]{:S(2)}, u32[]{:S(2)}) collective-permute-start(f32[1,2,2688]{2,1,0:T(2,128)S(1)} %bitcast.44), channel_id=1, source_target_pairs={{0,7},{1,6},{2,5},{3,4},{4,3},{5,2},{6,1},{7,0},{8,15},{9,14},{10,... | collective-permute-start | bytes 64520 | tf_op jit(solution)/shard_map/ppermute | solution.py:25
  24.6 3.3 %collective-permute-start.9 = (f32[1,2,2688]{2,1,0:T(2,128)S(1)}, f32[1,2,2688]{2,1,0:T(2,128)S(1)}, u32[]{:S(2)}, u32[]{:S(2)}) collective-permute-start(f32[1,2,2688]{2,1,0:T(2,128)S(1)} %bitcast.45), channel_id=1, source_target_pairs={{0,5},{1,4},{2,7},{3,6},{4,1},{5,0},{6,3},{7,2},{8,13},{9,12},{10,... | collective-permute-start | bytes 64520 | tf_op jit(solution)/shard_map/ppermute | solution.py:25
  25.0 3.2 %collective-permute-start.7 = (f32[1,2,2688]{2,1,0:T(2,128)S(1)}, f32[1,2,2688]{2,1,0:T(2,128)S(1)}, u32[]{:S(2)}, u32[]{:S(2)}) collective-permute-start(f32[1,2,2688]{2,1,0:T(2,128)S(1)} %bitcast.46), channel_id=1, source_target_pairs={{0,3},{1,2},{2,1},{3,0},{4,7},{5,6},{6,5},{7,4},{8,11},{9,10},{10,... | collective-permute-start | bytes 64520 | tf_op jit(solution)/shard_map/ppermute | solution.py:25
  28.3 5.5 %collective-permute-start.11 = (f32[1,2,2688]{2,1,0:T(2,128)S(1)}, f32[1,2,2688]{2,1,0:T(2,128)S(1)}, u32[]{:S(2)}, u32[]{:S(2)}) collective-permute-start(f32[1,2,2688]{2,1,0:T(2,128)S(1)} %add_add_fusion), channel_id=1, source_target_pairs={{0,25},{1,24},{2,27},{3,26},{4,29},{5,28},{6,31},{7,30},{8,17},{9,... | collective-permute-start | bytes 64520 | tf_op jit(solution)/shard_map/ppermute | solution.py:25
  29.8 4.2 %collective-permute-start.12 = (f32[1,2,2688]{2,1,0:T(2,128)S(1)}, f32[1,2,2688]{2,1,0:T(2,128)S(1)}, u32[]{:S(2)}, u32[]{:S(2)}) collective-permute-start(f32[1,2,2688]{2,1,0:T(2,128)S(1)} %add_add_fusion), channel_id=1, source_target_pairs={{0,17},{1,16},{2,19},{3,18},{4,21},{5,20},{6,23},{7,22},{8,25},{9,... | collective-permute-start | bytes 64520 | tf_op jit(solution)/shard_map/ppermute | solution.py:25
  30.2 4.2 %collective-permute-start.10 = (f32[1,2,2688]{2,1,0:T(2,128)S(1)}, f32[1,2,2688]{2,1,0:T(2,128)S(1)}, u32[]{:S(2)}, u32[]{:S(2)}) collective-permute-start(f32[1,2,2688]{2,1,0:T(2,128)S(1)} %add_add_fusion), channel_id=1, source_target_pairs={{0,9},{1,8},{2,11},{3,10},{4,13},{5,12},{6,15},{7,14},{8,1},{9,0},... | collective-permute-start | bytes 64520 | tf_op jit(solution)/shard_map/ppermute | solution.py:25
  35.6 1.2 %collective-permute-start.13 = (f32[1,2,1280]{2,1,0:T(2,128)S(1)}, f32[1,2,1280]{2,1,0:T(2,128)S(1)}, u32[]{:S(2)}, u32[]{:S(2)}) collective-permute-start(f32[1,2,1280]{2,1,0:T(2,128)S(1)} %bitcast.47), channel_id=1, source_target_pairs={{0,1},{1,0},{2,3},{3,2},{4,5},{5,4},{6,7},{7,6},{8,9},{9,8},{10,11... | collective-permute-start | bytes 30728 | tf_op jit(solution)/shard_map/ppermute | solution.py:29
  36.8 5.0 %collective-permute-start.15 = (f32[1,2,1280]{2,1,0:T(2,128)S(1)}, f32[1,2,1280]{2,1,0:T(2,128)S(1)}, u32[]{:S(2)}, u32[]{:S(2)}) collective-permute-start(f32[1,2,1280]{2,1,0:T(2,128)S(1)} %select_add_fusion), channel_id=1, source_target_pairs={{0,7},{1,6},{2,5},{3,4},{4,3},{5,2},{6,1},{7,0},{8,15},{9,14},{10,... | collective-permute-start | bytes 30728 | tf_op jit(solution)/shard_map/ppermute | solution.py:25
  39.0 3.1 %collective-permute-start.16 = (f32[1,2,1280]{2,1,0:T(2,128)S(1)}, f32[1,2,1280]{2,1,0:T(2,128)S(1)}, u32[]{:S(2)}, u32[]{:S(2)}) collective-permute-start(f32[1,2,1280]{2,1,0:T(2,128)S(1)} %select_add_fusion), channel_id=1, source_target_pairs={{0,5},{1,4},{2,7},{3,6},{4,1},{5,0},{6,3},{7,2},{8,13},{9,12},{10,... | collective-permute-start | bytes 30728 | tf_op jit(solution)/shard_map/ppermute | solution.py:25
  39.4 3.1 %collective-permute-start.14 = (f32[1,2,1280]{2,1,0:T(2,128)S(1)}, f32[1,2,1280]{2,1,0:T(2,128)S(1)}, u32[]{:S(2)}, u32[]{:S(2)}) collective-permute-start(f32[1,2,1280]{2,1,0:T(2,128)S(1)} %select_add_fusion), channel_id=1, source_target_pairs={{0,3},{1,2},{2,1},{3,0},{4,7},{5,6},{6,5},{7,4},{8,11},{9,10},{10,... | collective-permute-start | bytes 30728 | tf_op jit(solution)/shard_map/ppermute | solution.py:25
  42.5 5.6 %collective-permute-start.17 = (f32[1,2,1280]{2,1,0:T(2,128)S(1)}, f32[1,2,1280]{2,1,0:T(2,128)S(1)}, u32[]{:S(2)}, u32[]{:S(2)}) collective-permute-start(f32[1,2,1280]{2,1,0:T(2,128)S(1)} %add_add_fusion.2.refs_0_), channel_id=1, source_target_pairs={{0,25},{1,24},{2,27},{3,26},{4,29},{5,28},{6,31},{7,30},{8,17},{9,... | collective-permute-start | bytes 30728 | tf_op jit(solution)/shard_map/ppermute | solution.py:25
  44.5 4.1 %collective-permute-start.18 = (f32[1,2,1280]{2,1,0:T(2,128)S(1)}, f32[1,2,1280]{2,1,0:T(2,128)S(1)}, u32[]{:S(2)}, u32[]{:S(2)}) collective-permute-start(f32[1,2,1280]{2,1,0:T(2,128)S(1)} %add_add_fusion.2.refs_0_), channel_id=1, source_target_pairs={{0,17},{1,16},{2,19},{3,18},{4,21},{5,20},{6,23},{7,22},{8,25},{9,... | collective-permute-start | bytes 30728 | tf_op jit(solution)/shard_map/ppermute | solution.py:25
  44.8 3.7 %collective-permute-start.19 = (f32[1,2,1280]{2,1,0:T(2,128)S(1)}, f32[1,2,1280]{2,1,0:T(2,128)S(1)}, u32[]{:S(2)}, u32[]{:S(2)}) collective-permute-start(f32[1,2,1280]{2,1,0:T(2,128)S(1)} %add_add_fusion.2.refs_0_), channel_id=1, source_target_pairs={{0,9},{1,8},{2,11},{3,10},{4,13},{5,12},{6,15},{7,14},{8,1},{9,0},... | collective-permute-start | bytes 30728 | tf_op jit(solution)/shard_map/ppermute | solution.py:25

commit v11 on v10

--- a/solution.py
+++ b/solution.py
@@ -126,36 +126,34 @@
         pltpu.make_async_copy(cot_ref.at[piece], cot_buf.at[piece], sems.at[1, index])
         for index, piece in enumerate(pieces)
     ]
-    for copy in [phi_copy] + tok_copies + cot_copies:
+    for copy in [phi_copy] + tok_copies:
         copy.start()
     phi_copy.wait()
     phi = phi_buf[...].astype(f32)
     phi_scale = lax.rsqrt(jnp.sum(phi * phi, axis=1, keepdims=True) + epsilon)
     phi_norm = (phi * phi_scale).astype(bf16)
-    in_parts = 0.0
-    totals = 0.0
-    for copy, piece in zip(tok_copies, pieces):
-        copy.wait()
-        tok_in = tok_buf[piece, :]
-        tok_f32 = tok_in.astype(f32)
+    for tok_copy, cot_copy, piece in zip(tok_copies, cot_copies, pieces):
+        tok_copy.wait()
+        cot_copy.start()
+        tok_f32 = tok_buf[piece, :].astype(f32)
         tok_scale = lax.rsqrt(jnp.sum(tok_f32 * tok_f32, axis=1, keepdims=True) + epsilon)
-        tok_norm = (tok_f32 * tok_scale).astype(bf16)
-        norm_ref[piece, :] = tok_norm
+        norm_ref[piece, :] = (tok_f32 * tok_scale).astype(bf16)
         tok_scale_ref[piece, :] = tok_scale
-        logits = scale_ref[0] * lax.dot_general(phi_norm, tok_norm, ROWS, preferred_element_type=f32)
-        exp_scores = jnp.exp(logits)
-        exp_high = exp_scores.astype(bf16).astype(f32)
-        halves = jnp.concatenate([exp_high, exp_scores - exp_high], axis=0).astype(bf16)
-        in_parts += jnp.dot(halves, tok_in, preferred_element_type=f32)
-        totals += jnp.sum(exp_scores, axis=1, keepdims=True)
-        exp_ref[:, piece] = exp_scores
-        combine_ref[:, piece] = (exp_scores / jnp.sum(exp_scores, axis=0, keepdims=True)).astype(bf16)
+    logits = scale_ref[0] * lax.dot_general(phi_norm, norm_ref[...], ROWS, preferred_element_type=f32)
+    exp_scores = jnp.exp(logits)
+    combine = (exp_scores / jnp.sum(exp_scores, axis=0, keepdims=True)).astype(bf16)
+    exp_high = exp_scores.astype(bf16).astype(f32)
+    halves = jnp.concatenate([exp_high, exp_scores - exp_high], axis=0).astype(bf16)
+    in_parts = jnp.dot(halves, tok_buf[...], preferred_element_type=f32)
     message_ref[:, :width] = in_parts[:experts] + in_parts[experts:]
     spare = message_ref.shape[1] - 2 * width
-    message_ref[:, 2 * width :] = jnp.broadcast_to(as_row(totals, spare), (experts, spare))
+    total = as_row(jnp.sum(exp_scores, axis=1, keepdims=True), spare)
+    message_ref[:, 2 * width :] = jnp.broadcast_to(total, (experts, spare))
+    exp_ref[...] = exp_scores
+    combine_ref[...] = combine
     for copy in cot_copies:
         copy.wait()
-    message_ref[:, width : 2 * width] = jnp.dot(combine_ref[...], cot_buf[...], preferred_element_type=f32)
+    message_ref[:, width : 2 * width] = jnp.dot(combine, cot_buf[...], preferred_element_type=f32)
 
 
 def fetch(in_ref, out_ref, in_buf, out_buf, sems):
@@ -279,7 +277,7 @@
             pltpu.VMEM((count, width), bf16),
             pltpu.VMEM((count, width), bf16),
             pltpu.SemaphoreType.DMA,
-            pltpu.SemaphoreType.DMA((2, 2)),
+            pltpu.SemaphoreType.DMA((2, PIECES)),
         ],
         compiler_params=params,
         name="token_sums",

time: 49.6 us -> 49.1 us (0.990)
  Pallas kernels: 9.02 us -> 8.51 us
    pallas_call x1, Pallas kernels: 3.68 us -> 3.17 us  [per_device(): pl.pallas_call(token_sums, in_specs=[scalar, in_hbm, in_hbm, in_hbm], out...]
where the time goes in v11:
time: 49.1 us; the launch traced here: 48.9 us
  starting transfers between devices  23.4 us (48%)
  Pallas kernels  8.51 us (17%)
  matrix products  7.52 us (15%)
  waiting for transfers between devices  7.36 us (15%)
  between operations  1.47 us (3%)
  other arithmetic  0.53 us (1%)
    ppermute x18, starting transfers between devices, exchange(): return lax.ppermute(value, AXES, pairs)  22.7 us
    ppermute x18, waiting for transfers between devices, exchange(): return lax.ppermute(value, AXES, pairs)  6.38 us
    pallas_call x1, Pallas kernels, per_device(): pl.pallas_call(token_sums, in_specs=[scalar, in_hbm, in_hbm, in_hbm], out...  3.17 us
    dot_general x1, matrix products, per_device(): jnp.einsum('sn,sd->nd', dispatch, slot_dx, preferred_element_type=f32)  1.98 us
    pallas_call x1, Pallas kernels, per_device(): pl.pallas_call(fetch, in_specs=[in_hbm] * 2, out_specs=[in_vmem] * 2, out...  1.94 us
    dot_general x1, matrix products, per_device(): jnp.einsum('sn,sd->nd', combine, slot_y, preferred_element_type=f32)  1.61 us
    dot_general x1, matrix products, per_device(): jnp.einsum('od,oh->dh', mine_x, pre_grad, preferred_element_type=f32)  1.59 us
    dot_general x1, matrix products, per_device(): jnp.einsum('oh,od->hd', hidden, mine_cot, preferred_element_type=f32)  1.59 us
  transfers between devices with their start and end apart: 20, of which 13 were waited for; matrix products, arithmetic and copies ran while one was open for 16% of the time, Pallas kernels for 4%

profile of v11, /device:TPU:0, one launch (start us, length us, event | category | flops | bytes accessed | tf_op | source)
XLA Modules:
  0.0 48.9 jit_solution(10036816185570418680)
XLA Ops:
  1.3 3.2 %token_sums.1 = (f32[2,2688]{1,0:T(2,128)S(1)}, f32[2,512]{1,0:T(2,128)S(1)}, bf16[2,512]{1,0:T(2,128)(2,1)S(1)}, f32[512,1]{1,0:T(8,128)S(1)}, bf16[512,1280]{1,0:T(8,128)(2,1)S(1)}) custom-call(f32[1]{0:T(128)S(6)} %copy.13.scale_ref, bf16[2,1280]{1,0:T(2,128)(2,1)} %bitcast.42, bf16[512,1280]{1,0:T(8,128)(2,1)} %bitcast.38, bf16[512,1280]{1,0:T(8,128)(2,1)} %bitcast.40), custom_call_target="tpu_custom_call" | custom-call | tf_op jit(solution)/shard_map/token_sums/pallas_call | solution.py:265
  4.5 0.5 %collective-permute-start = (f32[2,2688]{1,0:T(2,128)S(1)}, f32[2,2688]{1,0:T(2,128)S(1)}, u32[]{:S(2)}, u32[]{:S(2)}) collective-permute-start(f32[2,2688]{1,0:T(2,128)S(1)} %get-tuple-element.27), channel_id=1, source_target_pairs={{0,1},{1,0},{2,3},{3,2},{4,5},{5,4},{6,7},{7,6},{8,9},{9,8},{10,11... | collective-permute-start | bytes 64520 | tf_op jit(solution)/shard_map/ppermute | solution.py:29
  5.0 0.1 fusion.3
  5.1 0.7 %collective-permute-done = f32[2,2688]{1,0:T(2,128)S(1)} collective-permute-done((f32[2,2688]{1,0:T(2,128)S(1)}, f32[2,2688]{1,0:T(2,128)S(1)}, u32[]{:S(2)}, u32[]{:S(2)}) %collective-permute-start) | collective-permute-done | bytes 21536 | tf_op jit(solution)/shard_map/ppermute | solution.py:29
  6.0 4.8 %collective-permute-start.2 = (f32[1,2,2688]{2,1,0:T(2,128)S(1)}, f32[1,2,2688]{2,1,0:T(2,128)S(1)}, u32[]{:S(2)}, u32[]{:S(2)}) collective-permute-start(f32[1,2,2688]{2,1,0:T(2,128)S(1)} %get-tuple-element.51), channel_id=1, source_target_pairs={{0,25},{1,24},{2,27},{3,26},{4,29},{5,28},{6,31},{7,30},{8,17},{9,... | collective-permute-start | bytes 64520 | tf_op jit(solution)/shard_map/ppermute | solution.py:25
  10.8 0.6 %collective-permute-start.1 = (f32[1,2,2688]{2,1,0:T(2,128)S(1)}, f32[1,2,2688]{2,1,0:T(2,128)S(1)}, u32[]{:S(2)}, u32[]{:S(2)}) collective-permute-start(f32[1,2,2688]{2,1,0:T(2,128)S(1)} %get-tuple-element.49), channel_id=1, source_target_pairs={{0,9},{1,8},{2,11},{3,10},{4,13},{5,12},{6,15},{7,14},{8,1},{9,0},... | collective-permute-start | bytes 64520 | tf_op jit(solution)/shard_map/ppermute | solution.py:25
  11.4 0.9 %collective-permute-done.2 = f32[1,2,2688]{2,1,0:T(2,128)S(1)} collective-permute-done((f32[1,2,2688]{2,1,0:T(2,128)S(1)}, f32[1,2,2688]{2,1,0:T(2,128)S(1)}, u32[]{:S(2)}, u32[]{:S(2)}) %collective-permute-start.2) | collective-permute-done | bytes 21536 | tf_op jit(solution)/shard_map/ppermute | solution.py:25
  12.3 2.6 %collective-permute-done.3 = f32[1,2,2688]{2,1,0:T(2,128)S(1)} collective-permute-done((f32[1,2,2688]{2,1,0:T(2,128)S(1)}, f32[1,2,2688]{2,1,0:T(2,128)S(1)}, u32[]{:S(2)}, u32[]{:S(2)}) %collective-permute-start.3) | collective-permute-done | bytes 21536 | tf_op jit(solution)/shard_map/ppermute | solution.py:25
  14.9 2.5 %collective-permute-start.5 = (f32[1,2,2688]{2,1,0:T(2,128)S(1)}, f32[1,2,2688]{2,1,0:T(2,128)S(1)}, u32[]{:S(2)}, u32[]{:S(2)}) collective-permute-start(f32[1,2,2688]{2,1,0:T(2,128)S(1)} %add_add_fusion.1), channel_id=1, source_target_pairs={{0,7},{1,6},{2,5},{3,4},{4,3},{5,2},{6,1},{7,0},{8,15},{9,14},{10,... | collective-permute-start | bytes 64520 | tf_op jit(solution)/shard_map/ppermute | solution.py:25
  17.4 0.3 collective-permute-start.6
  17.7 0.5 collective-permute-start.4
  18.2 0.1 reduce
  18.3 1.9 %fetch_weights.1 = (bf16[1280,640]{1,0:T(8,128)(2,1)S(1)}, bf16[640,1280]{1,0:T(8,128)(2,1)S(1)}) custom-call(bf16[1280,640]{1,0:T(8,128)(2,1)} %in_ref, bf16[640,1280]{1,0:T(8,128)(2,1)} %out_ref), custom_call_target="tpu_custom_call" | custom-call | bytes 6553600 | tf_op jit(solution)/shard_map/fetch_weights/pallas_call | solution.py:287
  20.2 0.0 collective-permute-done.5
  20.3 0.3 collective-permute-done.6
  20.6 0.3 collective-permute-done.4
  20.9 1.5 %expert_rows.1 = (f32[2,2688]{1,0:T(2,128)S(1)}, bf16[2,1280]{1,0:T(2,128)(2,1)S(1)}, bf16[2,1280]{1,0:T(2,128)(2,1)S(1)}, bf16[2,640]{1,0:T(2,128)(2,1)S(1)}, bf16[2,640]{1,0:T(2,128)(2,1)S(1)}) custom-call(s32[1]{0:T(128)} %bitcast.3.owned_ref, f32[2,2688]{1,0:T(2,128)S(1)} %add_bitcast_fusion.2.sums_ref, bf16[1280,640]{1,0:T(8,128)(2,1)S(1)} %get-tuple-element.31.in_ref, ...), custom_call_target="tpu_custom_call" | custom-call | tf_op jit(solution)/shard_map/expert_rows/pallas_call | solution.py:304
  22.4 1.6 %collective-permute-start.8 = (f32[1,2,2688]{2,1,0:T(2,128)S(1)}, f32[1,2,2688]{2,1,0:T(2,128)S(1)}, u32[]{:S(2)}, u32[]{:S(2)}) collective-permute-start(f32[1,2,2688]{2,1,0:T(2,128)S(1)} %bitcast.44), channel_id=1, source_target_pairs={{0,7},{1,6},{2,5},{3,4},{4,3},{5,2},{6,1},{7,0},{8,15},{9,14},{10,... | collective-permute-start | bytes 64520 | tf_op jit(solution)/shard_map/ppermute | solution.py:25
  24.1 0.5 collective-permute-start.9
  24.5 1.1 %collective-permute-start.7 = (f32[1,2,2688]{2,1,0:T(2,128)S(1)}, f32[1,2,2688]{2,1,0:T(2,128)S(1)}, u32[]{:S(2)}, u32[]{:S(2)}) collective-permute-start(f32[1,2,2688]{2,1,0:T(2,128)S(1)} %bitcast.46), channel_id=1, source_target_pairs={{0,3},{1,2},{2,1},{3,0},{4,7},{5,6},{6,5},{7,4},{8,11},{9,10},{10,... | collective-permute-start | bytes 64520 | tf_op jit(solution)/shard_map/ppermute | solution.py:25
  25.6 1.6 %fusion.11 = f32[640,640]{1,0:T(8,128)} fusion(bf16[2,640]{1,0:T(2,128)(2,1)S(1)} %get-tuple-element.43, bf16[2,1280]{1,0:T(2,128)(2,1)S(1)} %get-tuple-element.42, s32[]{:T(128)S(6)} %select_n.90), kind=kOutput, calls=%fused_computation.27 | convolution fusion | flops 1638400 | bytes 1643524 | tf_op jit(solution)/shard_map/od,oh->dh/dot_general | solution.py:323
  27.2 0.1 collective-permute-done.9
  27.3 0.4 collective-permute-done.7
  27.8 1.5 %collective-permute-start.11 = (f32[1,2,2688]{2,1,0:T(2,128)S(1)}, f32[1,2,2688]{2,1,0:T(2,128)S(1)}, u32[]{:S(2)}, u32[]{:S(2)}) collective-permute-start(f32[1,2,2688]{2,1,0:T(2,128)S(1)} %add_add_fusion), channel_id=1, source_target_pairs={{0,25},{1,24},{2,27},{3,26},{4,29},{5,28},{6,31},{7,30},{8,17},{9,... | collective-permute-start | bytes 64520 | tf_op jit(solution)/shard_map/ppermute | solution.py:25
  29.3 0.4 collective-permute-start.12
  29.7 2.1 %collective-permute-start.10 = (f32[1,2,2688]{2,1,0:T(2,128)S(1)}, f32[1,2,2688]{2,1,0:T(2,128)S(1)}, u32[]{:S(2)}, u32[]{:S(2)}) collective-permute-start(f32[1,2,2688]{2,1,0:T(2,128)S(1)} %add_add_fusion), channel_id=1, source_target_pairs={{0,9},{1,8},{2,11},{3,10},{4,13},{5,12},{6,15},{7,14},{8,1},{9,0},... | collective-permute-start | bytes 64520 | tf_op jit(solution)/shard_map/ppermute | solution.py:25
  31.7 1.6 %fusion.9 = f32[640,640]{1,0:T(8,128)} fusion(bf16[2,640]{1,0:T(2,128)(2,1)S(1)} %get-tuple-element.44, bf16[2,1280]{1,0:T(2,128)(2,1)S(1)} %get-tuple-element.45, s32[]{:T(128)S(6)} %select_n.90), kind=kOutput, calls=%fused_computation.25 | convolution fusion | flops 1638400 | bytes 1643524 | tf_op jit(solution)/shard_map/oh,od->hd/dot_general | solution.py:324
  33.3 0.2 collective-permute-done.12
  33.6 0.3 collective-permute-done.10
  33.9 0.1 fusion.16
  34.0 1.1 %score_grads.1 = (bf16[2,512]{1,0:T(2,128)(2,1)S(1)}, bf16[2,512]{1,0:T(2,128)(2,1)S(1)}, f32[2,1280]{1,0:T(2,128)S(1)}) custom-call(f32[1]{0:T(128)S(6)} %copy.13.scale_ref, f32[2,2688]{1,0:T(2,128)S(1)} %get-tuple-element.48.slots_ref, f32[1,128]{1,0:T(1,128)S(1)} %constant_dynamic-slice_fusion.1.totals_ref, bf16[512,1280]{1,0:T(8,128)(2,1)S(1)} %bitcast.39, ...), custom_call_target="tpu_custom_call" | custom-call | tf_op jit(solution)/shard_map/score_grads/pallas_call | solution.py:325
  35.1 0.2 collective-permute-start.13
  35.3 0.7 %multiply_reduce_fusion = (f32[512]{0:T(512)S(1)}, f32[512,1280]{1,0:T(8,128)S(1)}) fusion(f32[512]{0:T(512)S(1)} %reduce, bf16[1,512,1280]{2,1,0:T(8,128)(2,1)S(1)} %copy-done, bf16[2,512]{1,0:T(2,128)(2,1)S(1)} %get-tuple-element.41, f32[2]{0:T(128)S(1)} %add_rsqrt_fusion, bf16[1280,2]{0,1:T(2,128)(2,1)S(1)} %copy-done.2), kind=kOutput, calls=%fused_computation.5 | convolution fusion | flops 5250048 | bytes 3943432 | tf_op jit(solution)/shard_map/sn,sd->nd/dot_general | solution.py:355
  36.0 0.3 collective-permute-done.13
  36.3 2.1 %collective-permute-start.15 = (f32[1,2,1280]{2,1,0:T(2,128)S(1)}, f32[1,2,1280]{2,1,0:T(2,128)S(1)}, u32[]{:S(2)}, u32[]{:S(2)}) collective-permute-start(f32[1,2,1280]{2,1,0:T(2,128)S(1)} %select_add_fusion), channel_id=1, source_target_pairs={{0,7},{1,6},{2,5},{3,4},{4,3},{5,2},{6,1},{7,0},{8,15},{9,14},{10,... | collective-permute-start | bytes 30728 | tf_op jit(solution)/shard_map/ppermute | solution.py:25
  38.4 0.5 collective-permute-start.16
  38.9 0.4 collective-permute-start.14
  39.4 2.0 %fusion.1 = bf16[1,512,1280]{2,1,0:T(8,128)(2,1)} fusion(bf16[2,512]{1,0:T(2,128)(2,1)S(1)} %get-tuple-element.39, f32[512,1280]{1,0:T(8,128)S(1)} %get-tuple-element.55, f32[512]{0:T(512)S(1)} %get-tuple-element.54, f32[512]{0:T(512)S(1)} %reduce, bf16[2,2688]{1,0:T(2,128)(2,1)S(1)} %get-tuple-element.47, bf16[1,512,1280]{2,1,0:T(8,128)(2,1)S(1)} %copy-done), kind=kOutput, calls=%fused_computation.3 | convolution fusion | flops 7208960 | bytes 5254144 | tf_op jit(solution)/shard_map/sn,sd->nd/dot_general | solution.py:356
  41.3 0.0 collective-permute-done.15
  41.3 0.2 collective-permute-done.16
  41.5 0.5 collective-permute-done.14
  42.0 1.9 %collective-permute-start.17 = (f32[1,2,1280]{2,1,0:T(2,128)S(1)}, f32[1,2,1280]{2,1,0:T(2,128)S(1)}, u32[]{:S(2)}, u32[]{:S(2)}) collective-permute-start(f32[1,2,1280]{2,1,0:T(2,128)S(1)} %add_add_fusion.2.refs_0_), channel_id=1, source_target_pairs={{0,25},{1,24},{2,27},{3,26},{4,29},{5,28},{6,31},{7,30},{8,17},{9,... | collective-permute-start | bytes 30728 | tf_op jit(solution)/shard_map/ppermute | solution.py:25
  44.0 0.4 collective-permute-start.18
  44.3 1.6 %collective-permute-start.19 = (f32[1,2,1280]{2,1,0:T(2,128)S(1)}, f32[1,2,1280]{2,1,0:T(2,128)S(1)}, u32[]{:S(2)}, u32[]{:S(2)}) collective-permute-start(f32[1,2,1280]{2,1,0:T(2,128)S(1)} %add_add_fusion.2.refs_0_), channel_id=1, source_target_pairs={{0,9},{1,8},{2,11},{3,10},{4,13},{5,12},{6,15},{7,14},{8,1},{9,0},... | collective-permute-start | bytes 30728 | tf_op jit(solution)/shard_map/ppermute | solution.py:25
  46.0 1.6 %fusion.2 = bf16[1,512,1280]{2,1,0:T(8,128)(2,1)} fusion(bf16[2,512]{1,0:T(2,128)(2,1)S(1)} %get-tuple-element.26, bf16[2,2688]{1,0:T(2,128)(2,1)S(1)} %get-tuple-element.47), kind=kOutput, calls=%fused_computation.4 | convolution fusion | flops 3276800 | bytes 1317888 | tf_op jit(solution)/shard_map/sn,sd->nd/dot_general | solution.py:354
  47.6 0.0 collective-permute-done.17.refs_1_
  47.6 0.5 collective-permute-done.18.refs_2_
  48.1 0.8 %finish.1 = f32[2,1280]{1,0:T(2,128)} custom-call(bf16[2,1280]{1,0:T(2,128)(2,1)S(1)} %bitcast.43, f32[1,2,1280]{2,1,0:T(2,128)S(1)} %add_add_fusion.2.refs_0_, f32[1,2,1280]{2,1,0:T(2,128)S(1)} %collective-permute-done.17.refs_1_, f32[1,2,1280]{2,1,0:T(2,128)S(1)} %collective-permute-done.18.refs_2_, f32[1,2,1280]{2,1,0:T(2,128)S(1)} %collective-permute-done.19.refs_3_), custom_call_target="tpu_custom_call" | custom-call | tf_op jit(solution)/shard_map/finish/pallas_call | solution.py:341
  (29 shorter events, 0.3 us)
Async XLA Ops:
  0.6 4.4 %copy-start.2 = (bf16[1280,2]{0,1:T(2,128)(2,1)S(1)}, bf16[1280,2]{0,1:T(2,128)(2,1)}, u32[]{:S(2)}) copy-start(bf16[1280,2]{0,1:T(2,128)(2,1)} %param.8) | copy-start | bytes 15364
  4.5 1.4 %collective-permute-start = (f32[2,2688]{1,0:T(2,128)S(1)}, f32[2,2688]{1,0:T(2,128)S(1)}, u32[]{:S(2)}, u32[]{:S(2)}) collective-permute-start(f32[2,2688]{1,0:T(2,128)S(1)} %get-tuple-element.27), channel_id=1, source_target_pairs={{0,1},{1,0},{2,3},{3,2},{4,5},{5,4},{6,7},{7,6},{8,9},{9,8},{10,11... | collective-permute-start | bytes 64520 | tf_op jit(solution)/shard_map/ppermute | solution.py:29
  6.0 6.3 %collective-permute-start.2 = (f32[1,2,2688]{2,1,0:T(2,128)S(1)}, f32[1,2,2688]{2,1,0:T(2,128)S(1)}, u32[]{:S(2)}, u32[]{:S(2)}) collective-permute-start(f32[1,2,2688]{2,1,0:T(2,128)S(1)} %get-tuple-element.51), channel_id=1, source_target_pairs={{0,25},{1,24},{2,27},{3,26},{4,29},{5,28},{6,31},{7,30},{8,17},{9,... | collective-permute-start | bytes 64520 | tf_op jit(solution)/shard_map/ppermute | solution.py:25
  10.8 4.1 %collective-permute-start.3 = (f32[1,2,2688]{2,1,0:T(2,128)S(1)}, f32[1,2,2688]{2,1,0:T(2,128)S(1)}, u32[]{:S(2)}, u32[]{:S(2)}) collective-permute-start(f32[1,2,2688]{2,1,0:T(2,128)S(1)} %get-tuple-element.50), channel_id=1, source_target_pairs={{0,17},{1,16},{2,19},{3,18},{4,21},{5,20},{6,23},{7,22},{8,25},{9,... | collective-permute-start | bytes 64520 | tf_op jit(solution)/shard_map/ppermute | solution.py:25
  10.8 4.1 %collective-permute-start.1 = (f32[1,2,2688]{2,1,0:T(2,128)S(1)}, f32[1,2,2688]{2,1,0:T(2,128)S(1)}, u32[]{:S(2)}, u32[]{:S(2)}) collective-permute-start(f32[1,2,2688]{2,1,0:T(2,128)S(1)} %get-tuple-element.49), channel_id=1, source_target_pairs={{0,9},{1,8},{2,11},{3,10},{4,13},{5,12},{6,15},{7,14},{8,1},{9,0},... | collective-permute-start | bytes 64520 | tf_op jit(solution)/shard_map/ppermute | solution.py:25
  14.9 5.3 %collective-permute-start.5 = (f32[1,2,2688]{2,1,0:T(2,128)S(1)}, f32[1,2,2688]{2,1,0:T(2,128)S(1)}, u32[]{:S(2)}, u32[]{:S(2)}) collective-permute-start(f32[1,2,2688]{2,1,0:T(2,128)S(1)} %add_add_fusion.1), channel_id=1, source_target_pairs={{0,7},{1,6},{2,5},{3,4},{4,3},{5,2},{6,1},{7,0},{8,15},{9,14},{10,... | collective-permute-start | bytes 64520 | tf_op jit(solution)/shard_map/ppermute | solution.py:25
  17.4 3.2 %collective-permute-start.6 = (f32[1,2,2688]{2,1,0:T(2,128)S(1)}, f32[1,2,2688]{2,1,0:T(2,128)S(1)}, u32[]{:S(2)}, u32[]{:S(2)}) collective-permute-start(f32[1,2,2688]{2,1,0:T(2,128)S(1)} %add_add_fusion.1), channel_id=1, source_target_pairs={{0,5},{1,4},{2,7},{3,6},{4,1},{5,0},{6,3},{7,2},{8,13},{9,12},{10,... | collective-permute-start | bytes 64520 | tf_op jit(solution)/shard_map/ppermute | solution.py:25
  17.7 3.2 %collective-permute-start.4 = (f32[1,2,2688]{2,1,0:T(2,128)S(1)}, f32[1,2,2688]{2,1,0:T(2,128)S(1)}, u32[]{:S(2)}, u32[]{:S(2)}) collective-permute-start(f32[1,2,2688]{2,1,0:T(2,128)S(1)} %add_add_fusion.1), channel_id=1, source_target_pairs={{0,3},{1,2},{2,1},{3,0},{4,7},{5,6},{6,5},{7,4},{8,11},{9,10},{10,... | collective-permute-start | bytes 64520 | tf_op jit(solution)/shard_map/ppermute | solution.py:25
  22.4 11.6 %copy-start = (bf16[1,512,1280]{2,1,0:T(8,128)(2,1)S(1)}, bf16[1,512,1280]{2,1,0:T(8,128)(2,1)}, u32[]{:S(2)}) copy-start(bf16[1,512,1280]{2,1,0:T(8,128)(2,1)} %param.6) | copy-start | bytes 3932164
  22.4 11.6 %copy-start.1 = (bf16[1,512,1280]{2,1,0:T(8,128)(2,1)S(1)}, bf16[1,512,1280]{2,1,0:T(8,128)(2,1)}, u32[]{:S(2)}) copy-start(bf16[1,512,1280]{2,1,0:T(8,128)(2,1)} %param.7) | copy-start | bytes 3932164
  22.4 4.8 %collective-permute-start.8 = (f32[1,2,2688]{2,1,0:T(2,128)S(1)}, f32[1,2,2688]{2,1,0:T(2,128)S(1)}, u32[]{:S(2)}, u32[]{:S(2)}) collective-permute-start(f32[1,2,2688]{2,1,0:T(2,128)S(1)} %bitcast.44), channel_id=1, source_target_pairs={{0,7},{1,6},{2,5},{3,4},{4,3},{5,2},{6,1},{7,0},{8,15},{9,14},{10,... | collective-permute-start | bytes 64520 | tf_op jit(solution)/shard_map/ppermute | solution.py:25
  24.1 3.3 %collective-permute-start.9 = (f32[1,2,2688]{2,1,0:T(2,128)S(1)}, f32[1,2,2688]{2,1,0:T(2,128)S(1)}, u32[]{:S(2)}, u32[]{:S(2)}) collective-permute-start(f32[1,2,2688]{2,1,0:T(2,128)S(1)} %bitcast.45), channel_id=1, source_target_pairs={{0,5},{1,4},{2,7},{3,6},{4,1},{5,0},{6,3},{7,2},{8,13},{9,12},{10,... | collective-permute-start | bytes 64520 | tf_op jit(solution)/shard_map/ppermute | solution.py:25
  24.5 3.2 %collective-permute-start.7 = (f32[1,2,2688]{2,1,0:T(2,128)S(1)}, f32[1,2,2688]{2,1,0:T(2,128)S(1)}, u32[]{:S(2)}, u32[]{:S(2)}) collective-permute-start(f32[1,2,2688]{2,1,0:T(2,128)S(1)} %bitcast.46), channel_id=1, source_target_pairs={{0,3},{1,2},{2,1},{3,0},{4,7},{5,6},{6,5},{7,4},{8,11},{9,10},{10,... | collective-permute-start | bytes 64520 | tf_op jit(solution)/shard_map/ppermute | solution.py:25
  27.8 5.5 %collective-permute-start.11 = (f32[1,2,2688]{2,1,0:T(2,128)S(1)}, f32[1,2,2688]{2,1,0:T(2,128)S(1)}, u32[]{:S(2)}, u32[]{:S(2)}) collective-permute-start(f32[1,2,2688]{2,1,0:T(2,128)S(1)} %add_add_fusion), channel_id=1, source_target_pairs={{0,25},{1,24},{2,27},{3,26},{4,29},{5,28},{6,31},{7,30},{8,17},{9,... | collective-permute-start | bytes 64520 | tf_op jit(solution)/shard_map/ppermute | solution.py:25
  29.3 4.2 %collective-permute-start.12 = (f32[1,2,2688]{2,1,0:T(2,128)S(1)}, f32[1,2,2688]{2,1,0:T(2,128)S(1)}, u32[]{:S(2)}, u32[]{:S(2)}) collective-permute-start(f32[1,2,2688]{2,1,0:T(2,128)S(1)} %add_add_fusion), channel_id=1, source_target_pairs={{0,17},{1,16},{2,19},{3,18},{4,21},{5,20},{6,23},{7,22},{8,25},{9,... | collective-permute-start | bytes 64520 | tf_op jit(solution)/shard_map/ppermute | solution.py:25
  29.7 4.2 %collective-permute-start.10 = (f32[1,2,2688]{2,1,0:T(2,128)S(1)}, f32[1,2,2688]{2,1,0:T(2,128)S(1)}, u32[]{:S(2)}, u32[]{:S(2)}) collective-permute-start(f32[1,2,2688]{2,1,0:T(2,128)S(1)} %add_add_fusion), channel_id=1, source_target_pairs={{0,9},{1,8},{2,11},{3,10},{4,13},{5,12},{6,15},{7,14},{8,1},{9,0},... | collective-permute-start | bytes 64520 | tf_op jit(solution)/shard_map/ppermute | solution.py:25
  35.1 1.2 %collective-permute-start.13 = (f32[1,2,1280]{2,1,0:T(2,128)S(1)}, f32[1,2,1280]{2,1,0:T(2,128)S(1)}, u32[]{:S(2)}, u32[]{:S(2)}) collective-permute-start(f32[1,2,1280]{2,1,0:T(2,128)S(1)} %bitcast.47), channel_id=1, source_target_pairs={{0,1},{1,0},{2,3},{3,2},{4,5},{5,4},{6,7},{7,6},{8,9},{9,8},{10,11... | collective-permute-start | bytes 30728 | tf_op jit(solution)/shard_map/ppermute | solution.py:29
  36.3 5.0 %collective-permute-start.15 = (f32[1,2,1280]{2,1,0:T(2,128)S(1)}, f32[1,2,1280]{2,1,0:T(2,128)S(1)}, u32[]{:S(2)}, u32[]{:S(2)}) collective-permute-start(f32[1,2,1280]{2,1,0:T(2,128)S(1)} %select_add_fusion), channel_id=1, source_target_pairs={{0,7},{1,6},{2,5},{3,4},{4,3},{5,2},{6,1},{7,0},{8,15},{9,14},{10,... | collective-permute-start | bytes 30728 | tf_op jit(solution)/shard_map/ppermute | solution.py:25
  38.4 3.1 %collective-permute-start.16 = (f32[1,2,1280]{2,1,0:T(2,128)S(1)}, f32[1,2,1280]{2,1,0:T(2,128)S(1)}, u32[]{:S(2)}, u32[]{:S(2)}) collective-permute-start(f32[1,2,1280]{2,1,0:T(2,128)S(1)} %select_add_fusion), channel_id=1, source_target_pairs={{0,5},{1,4},{2,7},{3,6},{4,1},{5,0},{6,3},{7,2},{8,13},{9,12},{10,... | collective-permute-start | bytes 30728 | tf_op jit(solution)/shard_map/ppermute | solution.py:25
  38.9 3.1 %collective-permute-start.14 = (f32[1,2,1280]{2,1,0:T(2,128)S(1)}, f32[1,2,1280]{2,1,0:T(2,128)S(1)}, u32[]{:S(2)}, u32[]{:S(2)}) collective-permute-start(f32[1,2,1280]{2,1,0:T(2,128)S(1)} %select_add_fusion), channel_id=1, source_target_pairs={{0,3},{1,2},{2,1},{3,0},{4,7},{5,6},{6,5},{7,4},{8,11},{9,10},{10,... | collective-permute-start | bytes 30728 | tf_op jit(solution)/shard_map/ppermute | solution.py:25
  42.0 5.6 %collective-permute-start.17 = (f32[1,2,1280]{2,1,0:T(2,128)S(1)}, f32[1,2,1280]{2,1,0:T(2,128)S(1)}, u32[]{:S(2)}, u32[]{:S(2)}) collective-permute-start(f32[1,2,1280]{2,1,0:T(2,128)S(1)} %add_add_fusion.2.refs_0_), channel_id=1, source_target_pairs={{0,25},{1,24},{2,27},{3,26},{4,29},{5,28},{6,31},{7,30},{8,17},{9,... | collective-permute-start | bytes 30728 | tf_op jit(solution)/shard_map/ppermute | solution.py:25
  44.0 4.1 %collective-permute-start.18 = (f32[1,2,1280]{2,1,0:T(2,128)S(1)}, f32[1,2,1280]{2,1,0:T(2,128)S(1)}, u32[]{:S(2)}, u32[]{:S(2)}) collective-permute-start(f32[1,2,1280]{2,1,0:T(2,128)S(1)} %add_add_fusion.2.refs_0_), channel_id=1, source_target_pairs={{0,17},{1,16},{2,19},{3,18},{4,21},{5,20},{6,23},{7,22},{8,25},{9,... | collective-permute-start | bytes 30728 | tf_op jit(solution)/shard_map/ppermute | solution.py:25
  44.3 3.7 %collective-permute-start.19 = (f32[1,2,1280]{2,1,0:T(2,128)S(1)}, f32[1,2,1280]{2,1,0:T(2,128)S(1)}, u32[]{:S(2)}, u32[]{:S(2)}) collective-permute-start(f32[1,2,1280]{2,1,0:T(2,128)S(1)} %add_add_fusion.2.refs_0_), channel_id=1, source_target_pairs={{0,9},{1,8},{2,11},{3,10},{4,13},{5,12},{6,15},{7,14},{8,1},{9,0},... | collective-permute-start | bytes 30728 | tf_op jit(solution)/shard_map/ppermute | solution.py:25

commit v12 on v11

--- a/solution.py
+++ b/solution.py
@@ -126,19 +126,18 @@
         pltpu.make_async_copy(cot_ref.at[piece], cot_buf.at[piece], sems.at[1, index])
         for index, piece in enumerate(pieces)
     ]
-    for copy in [phi_copy] + tok_copies:
+    for copy in tok_copies + [phi_copy] + cot_copies:
         copy.start()
+    for copy, piece in zip(tok_copies, pieces):
+        copy.wait()
+        tok_f32 = tok_buf[piece, :].astype(f32)
+        tok_scale = lax.rsqrt(jnp.sum(tok_f32 * tok_f32, axis=1, keepdims=True) + epsilon)
+        norm_ref[piece, :] = (tok_f32 * tok_scale).astype(bf16)
+        tok_scale_ref[piece, :] = tok_scale
     phi_copy.wait()
     phi = phi_buf[...].astype(f32)
     phi_scale = lax.rsqrt(jnp.sum(phi * phi, axis=1, keepdims=True) + epsilon)
     phi_norm = (phi * phi_scale).astype(bf16)
-    for tok_copy, cot_copy, piece in zip(tok_copies, cot_copies, pieces):
-        tok_copy.wait()
-        cot_copy.start()
-        tok_f32 = tok_buf[piece, :].astype(f32)
-        tok_scale = lax.rsqrt(jnp.sum(tok_f32 * tok_f32, axis=1, keepdims=True) + epsilon)
-        norm_ref[piece, :] = (tok_f32 * tok_scale).astype(bf16)
-        tok_scale_ref[piece, :] = tok_scale
     logits = scale_ref[0] * lax.dot_general(phi_norm, norm_ref[...], ROWS, preferred_element_type=f32)
     exp_scores = jnp.exp(logits)
     combine = (exp_scores / jnp.sum(exp_scores, axis=0, keepdims=True)).astype(bf16)

time: 49.1 us -> 48.7 us (level)
  no operation moved by 1% of the time
where the time goes in v12:
time: 48.7 us; the launch traced here: 48.5 us
  starting transfers between devices  23.4 us (48%)
  Pallas kernels  8.13 us (17%)
  matrix products  7.52 us (15%)
  waiting for transfers between devices  7.35 us (15%)
  between operations  1.47 us (3%)
  other arithmetic  0.53 us (1%)
    ppermute x18, starting transfers between devices, exchange(): return lax.ppermute(value, AXES, pairs)  22.7 us
    ppermute x18, waiting for transfers between devices, exchange(): return lax.ppermute(value, AXES, pairs)  6.37 us
    pallas_call x1, Pallas kernels, per_device(): pl.pallas_call(token_sums, in_specs=[scalar, in_hbm, in_hbm, in_hbm], out...  2.79 us
    dot_general x1, matrix products, per_device(): jnp.einsum('sn,sd->nd', dispatch, slot_dx, preferred_element_type=f32)  1.99 us
    pallas_call x1, Pallas kernels, per_device(): pl.pallas_call(fetch, in_specs=[in_hbm] * 2, out_specs=[in_vmem] * 2, out...  1.94 us
    dot_general x1, matrix products, per_device(): jnp.einsum('sn,sd->nd', combine, slot_y, preferred_element_type=f32)  1.61 us
    dot_general x1, matrix products, per_device(): jnp.einsum('od,oh->dh', mine_x, pre_grad, preferred_element_type=f32)  1.59 us
    dot_general x1, matrix products, per_device(): jnp.einsum('oh,od->hd', hidden, mine_cot, preferred_element_type=f32)  1.59 us
  transfers between devices with their start and end apart: 20, of which 13 were waited for; matrix products, arithmetic and copies ran while one was open for 16% of the time, Pallas kernels for 4%

profile of v12, /device:TPU:0, one launch (start us, length us, event | category | flops | bytes accessed | tf_op | source)
XLA Modules:
  0.0 48.5 jit_solution(14595628169988141365)
XLA Ops:
  1.3 2.8 %token_sums.1 = (f32[2,2688]{1,0:T(2,128)S(1)}, f32[2,512]{1,0:T(2,128)S(1)}, bf16[2,512]{1,0:T(2,128)(2,1)S(1)}, f32[512,1]{1,0:T(8,128)S(1)}, bf16[512,1280]{1,0:T(8,128)(2,1)S(1)}) custom-call(f32[1]{0:T(128)S(6)} %copy.13.scale_ref, bf16[2,1280]{1,0:T(2,128)(2,1)} %bitcast.42, bf16[512,1280]{1,0:T(8,128)(2,1)} %bitcast.38, bf16[512,1280]{1,0:T(8,128)(2,1)} %bitcast.40), custom_call_target="tpu_custom_call" | custom-call | tf_op jit(solution)/shard_map/token_sums/pallas_call | solution.py:264
  4.1 0.5 %collective-permute-start = (f32[2,2688]{1,0:T(2,128)S(1)}, f32[2,2688]{1,0:T(2,128)S(1)}, u32[]{:S(2)}, u32[]{:S(2)}) collective-permute-start(f32[2,2688]{1,0:T(2,128)S(1)} %get-tuple-element.27), channel_id=1, source_target_pairs={{0,1},{1,0},{2,3},{3,2},{4,5},{5,4},{6,7},{7,6},{8,9},{9,8},{10,11... | collective-permute-start | bytes 64520 | tf_op jit(solution)/shard_map/ppermute | solution.py:29
  4.6 0.1 fusion.3
  4.8 0.7 %collective-permute-done = f32[2,2688]{1,0:T(2,128)S(1)} collective-permute-done((f32[2,2688]{1,0:T(2,128)S(1)}, f32[2,2688]{1,0:T(2,128)S(1)}, u32[]{:S(2)}, u32[]{:S(2)}) %collective-permute-start) | collective-permute-done | bytes 21536 | tf_op jit(solution)/shard_map/ppermute | solution.py:29
  5.6 4.8 %collective-permute-start.2 = (f32[1,2,2688]{2,1,0:T(2,128)S(1)}, f32[1,2,2688]{2,1,0:T(2,128)S(1)}, u32[]{:S(2)}, u32[]{:S(2)}) collective-permute-start(f32[1,2,2688]{2,1,0:T(2,128)S(1)} %get-tuple-element.51), channel_id=1, source_target_pairs={{0,25},{1,24},{2,27},{3,26},{4,29},{5,28},{6,31},{7,30},{8,17},{9,... | collective-permute-start | bytes 64520 | tf_op jit(solution)/shard_map/ppermute | solution.py:25
  10.4 0.0 collective-permute-start.3
  10.4 0.6 %collective-permute-start.1 = (f32[1,2,2688]{2,1,0:T(2,128)S(1)}, f32[1,2,2688]{2,1,0:T(2,128)S(1)}, u32[]{:S(2)}, u32[]{:S(2)}) collective-permute-start(f32[1,2,2688]{2,1,0:T(2,128)S(1)} %get-tuple-element.49), channel_id=1, source_target_pairs={{0,9},{1,8},{2,11},{3,10},{4,13},{5,12},{6,15},{7,14},{8,1},{9,0},... | collective-permute-start | bytes 64520 | tf_op jit(solution)/shard_map/ppermute | solution.py:25
  11.0 0.9 %collective-permute-done.2 = f32[1,2,2688]{2,1,0:T(2,128)S(1)} collective-permute-done((f32[1,2,2688]{2,1,0:T(2,128)S(1)}, f32[1,2,2688]{2,1,0:T(2,128)S(1)}, u32[]{:S(2)}, u32[]{:S(2)}) %collective-permute-start.2) | collective-permute-done | bytes 21536 | tf_op jit(solution)/shard_map/ppermute | solution.py:25
  11.9 2.6 %collective-permute-done.3 = f32[1,2,2688]{2,1,0:T(2,128)S(1)} collective-permute-done((f32[1,2,2688]{2,1,0:T(2,128)S(1)}, f32[1,2,2688]{2,1,0:T(2,128)S(1)}, u32[]{:S(2)}, u32[]{:S(2)}) %collective-permute-start.3) | collective-permute-done | bytes 21536 | tf_op jit(solution)/shard_map/ppermute | solution.py:25
  14.5 0.0 collective-permute-done.1
  14.5 2.5 %collective-permute-start.5 = (f32[1,2,2688]{2,1,0:T(2,128)S(1)}, f32[1,2,2688]{2,1,0:T(2,128)S(1)}, u32[]{:S(2)}, u32[]{:S(2)}) collective-permute-start(f32[1,2,2688]{2,1,0:T(2,128)S(1)} %add_add_fusion.1), channel_id=1, source_target_pairs={{0,7},{1,6},{2,5},{3,4},{4,3},{5,2},{6,1},{7,0},{8,15},{9,14},{10,... | collective-permute-start | bytes 64520 | tf_op jit(solution)/shard_map/ppermute | solution.py:25
  17.0 0.3 collective-permute-start.6
  17.3 0.5 %collective-permute-start.4 = (f32[1,2,2688]{2,1,0:T(2,128)S(1)}, f32[1,2,2688]{2,1,0:T(2,128)S(1)}, u32[]{:S(2)}, u32[]{:S(2)}) collective-permute-start(f32[1,2,2688]{2,1,0:T(2,128)S(1)} %add_add_fusion.1), channel_id=1, source_target_pairs={{0,3},{1,2},{2,1},{3,0},{4,7},{5,6},{6,5},{7,4},{8,11},{9,10},{10,... | collective-permute-start | bytes 64520 | tf_op jit(solution)/shard_map/ppermute | solution.py:25
  17.8 0.1 reduce
  17.9 1.9 %fetch_weights.1 = (bf16[1280,640]{1,0:T(8,128)(2,1)S(1)}, bf16[640,1280]{1,0:T(8,128)(2,1)S(1)}) custom-call(bf16[1280,640]{1,0:T(8,128)(2,1)} %in_ref, bf16[640,1280]{1,0:T(8,128)(2,1)} %out_ref), custom_call_target="tpu_custom_call" | custom-call | bytes 6553600 | tf_op jit(solution)/shard_map/fetch_weights/pallas_call | solution.py:286
  19.9 0.0 collective-permute-done.5
  19.9 0.3 collective-permute-done.6
  20.2 0.3 collective-permute-done.4
  20.5 1.5 %expert_rows.1 = (f32[2,2688]{1,0:T(2,128)S(1)}, bf16[2,1280]{1,0:T(2,128)(2,1)S(1)}, bf16[2,1280]{1,0:T(2,128)(2,1)S(1)}, bf16[2,640]{1,0:T(2,128)(2,1)S(1)}, bf16[2,640]{1,0:T(2,128)(2,1)S(1)}) custom-call(s32[1]{0:T(128)} %bitcast.3.owned_ref, f32[2,2688]{1,0:T(2,128)S(1)} %add_bitcast_fusion.2.sums_ref, bf16[1280,640]{1,0:T(8,128)(2,1)S(1)} %get-tuple-element.31.in_ref, ...), custom_call_target="tpu_custom_call" | custom-call | tf_op jit(solution)/shard_map/expert_rows/pallas_call | solution.py:303
  22.1 1.6 %collective-permute-start.8 = (f32[1,2,2688]{2,1,0:T(2,128)S(1)}, f32[1,2,2688]{2,1,0:T(2,128)S(1)}, u32[]{:S(2)}, u32[]{:S(2)}) collective-permute-start(f32[1,2,2688]{2,1,0:T(2,128)S(1)} %bitcast.44), channel_id=1, source_target_pairs={{0,7},{1,6},{2,5},{3,4},{4,3},{5,2},{6,1},{7,0},{8,15},{9,14},{10,... | collective-permute-start | bytes 64520 | tf_op jit(solution)/shard_map/ppermute | solution.py:25
  23.7 0.5 collective-permute-start.9
  24.2 1.1 %collective-permute-start.7 = (f32[1,2,2688]{2,1,0:T(2,128)S(1)}, f32[1,2,2688]{2,1,0:T(2,128)S(1)}, u32[]{:S(2)}, u32[]{:S(2)}) collective-permute-start(f32[1,2,2688]{2,1,0:T(2,128)S(1)} %bitcast.46), channel_id=1, source_target_pairs={{0,3},{1,2},{2,1},{3,0},{4,7},{5,6},{6,5},{7,4},{8,11},{9,10},{10,... | collective-permute-start | bytes 64520 | tf_op jit(solution)/shard_map/ppermute | solution.py:25
  25.2 1.6 %fusion.11 = f32[640,640]{1,0:T(8,128)} fusion(bf16[2,640]{1,0:T(2,128)(2,1)S(1)} %get-tuple-element.43, bf16[2,1280]{1,0:T(2,128)(2,1)S(1)} %get-tuple-element.42, s32[]{:T(128)S(6)} %select_n.90), kind=kOutput, calls=%fused_computation.27 | convolution fusion | flops 1638400 | bytes 1643524 | tf_op jit(solution)/shard_map/od,oh->dh/dot_general | solution.py:322
  26.9 0.1 collective-permute-done.9
  27.0 0.4 collective-permute-done.7
  27.4 1.5 %collective-permute-start.11 = (f32[1,2,2688]{2,1,0:T(2,128)S(1)}, f32[1,2,2688]{2,1,0:T(2,128)S(1)}, u32[]{:S(2)}, u32[]{:S(2)}) collective-permute-start(f32[1,2,2688]{2,1,0:T(2,128)S(1)} %add_add_fusion), channel_id=1, source_target_pairs={{0,25},{1,24},{2,27},{3,26},{4,29},{5,28},{6,31},{7,30},{8,17},{9,... | collective-permute-start | bytes 64520 | tf_op jit(solution)/shard_map/ppermute | solution.py:25
  28.9 0.4 collective-permute-start.12
  29.3 2.1 %collective-permute-start.10 = (f32[1,2,2688]{2,1,0:T(2,128)S(1)}, f32[1,2,2688]{2,1,0:T(2,128)S(1)}, u32[]{:S(2)}, u32[]{:S(2)}) collective-permute-start(f32[1,2,2688]{2,1,0:T(2,128)S(1)} %add_add_fusion), channel_id=1, source_target_pairs={{0,9},{1,8},{2,11},{3,10},{4,13},{5,12},{6,15},{7,14},{8,1},{9,0},... | collective-permute-start | bytes 64520 | tf_op jit(solution)/shard_map/ppermute | solution.py:25
  31.3 1.6 %fusion.9 = f32[640,640]{1,0:T(8,128)} fusion(bf16[2,640]{1,0:T(2,128)(2,1)S(1)} %get-tuple-element.44, bf16[2,1280]{1,0:T(2,128)(2,1)S(1)} %get-tuple-element.45, s32[]{:T(128)S(6)} %select_n.90), kind=kOutput, calls=%fused_computation.25 | convolution fusion | flops 1638400 | bytes 1643524 | tf_op jit(solution)/shard_map/oh,od->hd/dot_general | solution.py:323
  32.9 0.2 collective-permute-done.12
  33.2 0.3 collective-permute-done.10
  33.6 0.1 fusion.16
  33.7 1.1 %score_grads.1 = (bf16[2,512]{1,0:T(2,128)(2,1)S(1)}, bf16[2,512]{1,0:T(2,128)(2,1)S(1)}, f32[2,1280]{1,0:T(2,128)S(1)}) custom-call(f32[1]{0:T(128)S(6)} %copy.13.scale_ref, f32[2,2688]{1,0:T(2,128)S(1)} %get-tuple-element.48.slots_ref, f32[1,128]{1,0:T(1,128)S(1)} %constant_dynamic-slice_fusion.1.totals_ref, bf16[512,1280]{1,0:T(8,128)(2,1)S(1)} %bitcast.39, ...), custom_call_target="tpu_custom_call" | custom-call | tf_op jit(solution)/shard_map/score_grads/pallas_call | solution.py:324
  34.7 0.2 collective-permute-start.13
  34.9 0.7 %multiply_reduce_fusion = (f32[512]{0:T(512)S(1)}, f32[512,1280]{1,0:T(8,128)S(1)}) fusion(f32[512]{0:T(512)S(1)} %reduce, bf16[1,512,1280]{2,1,0:T(8,128)(2,1)S(1)} %copy-done, bf16[2,512]{1,0:T(2,128)(2,1)S(1)} %get-tuple-element.41, f32[2]{0:T(128)S(1)} %add_rsqrt_fusion, bf16[1280,2]{0,1:T(2,128)(2,1)S(1)} %copy-done.2), kind=kOutput, calls=%fused_computation.5 | convolution fusion | flops 5250048 | bytes 3943432 | tf_op jit(solution)/shard_map/sn,sd->nd/dot_general | solution.py:354
  35.6 0.3 collective-permute-done.13
  35.9 2.1 %collective-permute-start.15 = (f32[1,2,1280]{2,1,0:T(2,128)S(1)}, f32[1,2,1280]{2,1,0:T(2,128)S(1)}, u32[]{:S(2)}, u32[]{:S(2)}) collective-permute-start(f32[1,2,1280]{2,1,0:T(2,128)S(1)} %select_add_fusion), channel_id=1, source_target_pairs={{0,7},{1,6},{2,5},{3,4},{4,3},{5,2},{6,1},{7,0},{8,15},{9,14},{10,... | collective-permute-start | bytes 30728 | tf_op jit(solution)/shard_map/ppermute | solution.py:25
  38.1 0.5 collective-permute-start.16
  38.5 0.4 collective-permute-start.14
  39.0 2.0 %fusion.1 = bf16[1,512,1280]{2,1,0:T(8,128)(2,1)} fusion(bf16[2,512]{1,0:T(2,128)(2,1)S(1)} %get-tuple-element.39, f32[512,1280]{1,0:T(8,128)S(1)} %get-tuple-element.55, f32[512]{0:T(512)S(1)} %get-tuple-element.54, f32[512]{0:T(512)S(1)} %reduce, bf16[2,2688]{1,0:T(2,128)(2,1)S(1)} %get-tuple-element.47, bf16[1,512,1280]{2,1,0:T(8,128)(2,1)S(1)} %copy-done), kind=kOutput, calls=%fused_computation.3 | convolution fusion | flops 7208960 | bytes 5254144 | tf_op jit(solution)/shard_map/sn,sd->nd/dot_general | solution.py:355
  41.0 0.2 collective-permute-done.16
  41.2 0.5 collective-permute-done.14
  41.6 1.9 %collective-permute-start.17 = (f32[1,2,1280]{2,1,0:T(2,128)S(1)}, f32[1,2,1280]{2,1,0:T(2,128)S(1)}, u32[]{:S(2)}, u32[]{:S(2)}) collective-permute-start(f32[1,2,1280]{2,1,0:T(2,128)S(1)} %add_add_fusion.2.refs_0_), channel_id=1, source_target_pairs={{0,25},{1,24},{2,27},{3,26},{4,29},{5,28},{6,31},{7,30},{8,17},{9,... | collective-permute-start | bytes 30728 | tf_op jit(solution)/shard_map/ppermute | solution.py:25
  43.6 0.4 collective-permute-start.18
  44.0 1.6 %collective-permute-start.19 = (f32[1,2,1280]{2,1,0:T(2,128)S(1)}, f32[1,2,1280]{2,1,0:T(2,128)S(1)}, u32[]{:S(2)}, u32[]{:S(2)}) collective-permute-start(f32[1,2,1280]{2,1,0:T(2,128)S(1)} %add_add_fusion.2.refs_0_), channel_id=1, source_target_pairs={{0,9},{1,8},{2,11},{3,10},{4,13},{5,12},{6,15},{7,14},{8,1},{9,0},... | collective-permute-start | bytes 30728 | tf_op jit(solution)/shard_map/ppermute | solution.py:25
  45.6 1.6 %fusion.2 = bf16[1,512,1280]{2,1,0:T(8,128)(2,1)} fusion(bf16[2,512]{1,0:T(2,128)(2,1)S(1)} %get-tuple-element.26, bf16[2,2688]{1,0:T(2,128)(2,1)S(1)} %get-tuple-element.47), kind=kOutput, calls=%fused_computation.4 | convolution fusion | flops 3276800 | bytes 1317888 | tf_op jit(solution)/shard_map/sn,sd->nd/dot_general | solution.py:353
  47.2 0.5 collective-permute-done.18.refs_2_
  47.7 0.8 %finish.1 = f32[2,1280]{1,0:T(2,128)} custom-call(bf16[2,1280]{1,0:T(2,128)(2,1)S(1)} %bitcast.43, f32[1,2,1280]{2,1,0:T(2,128)S(1)} %add_add_fusion.2.refs_0_, f32[1,2,1280]{2,1,0:T(2,128)S(1)} %collective-permute-done.17.refs_1_, f32[1,2,1280]{2,1,0:T(2,128)S(1)} %collective-permute-done.18.refs_2_, f32[1,2,1280]{2,1,0:T(2,128)S(1)} %collective-permute-done.19.refs_3_), custom_call_target="tpu_custom_call" | custom-call | tf_op jit(solution)/shard_map/finish/pallas_call | solution.py:340
  (29 shorter events, 0.3 us)
Async XLA Ops:
  0.6 4.0 %copy-start.2 = (bf16[1280,2]{0,1:T(2,128)(2,1)S(1)}, bf16[1280,2]{0,1:T(2,128)(2,1)}, u32[]{:S(2)}) copy-start(bf16[1280,2]{0,1:T(2,128)(2,1)} %param.8) | copy-start | bytes 15364
  4.1 1.4 %collective-permute-start = (f32[2,2688]{1,0:T(2,128)S(1)}, f32[2,2688]{1,0:T(2,128)S(1)}, u32[]{:S(2)}, u32[]{:S(2)}) collective-permute-start(f32[2,2688]{1,0:T(2,128)S(1)} %get-tuple-element.27), channel_id=1, source_target_pairs={{0,1},{1,0},{2,3},{3,2},{4,5},{5,4},{6,7},{7,6},{8,9},{9,8},{10,11... | collective-permute-start | bytes 64520 | tf_op jit(solution)/shard_map/ppermute | solution.py:29
  5.6 6.3 %collective-permute-start.2 = (f32[1,2,2688]{2,1,0:T(2,128)S(1)}, f32[1,2,2688]{2,1,0:T(2,128)S(1)}, u32[]{:S(2)}, u32[]{:S(2)}) collective-permute-start(f32[1,2,2688]{2,1,0:T(2,128)S(1)} %get-tuple-element.51), channel_id=1, source_target_pairs={{0,25},{1,24},{2,27},{3,26},{4,29},{5,28},{6,31},{7,30},{8,17},{9,... | collective-permute-start | bytes 64520 | tf_op jit(solution)/shard_map/ppermute | solution.py:25
  10.4 4.1 %collective-permute-start.3 = (f32[1,2,2688]{2,1,0:T(2,128)S(1)}, f32[1,2,2688]{2,1,0:T(2,128)S(1)}, u32[]{:S(2)}, u32[]{:S(2)}) collective-permute-start(f32[1,2,2688]{2,1,0:T(2,128)S(1)} %get-tuple-element.50), channel_id=1, source_target_pairs={{0,17},{1,16},{2,19},{3,18},{4,21},{5,20},{6,23},{7,22},{8,25},{9,... | collective-permute-start | bytes 64520 | tf_op jit(solution)/shard_map/ppermute | solution.py:25
  10.4 4.1 %collective-permute-start.1 = (f32[1,2,2688]{2,1,0:T(2,128)S(1)}, f32[1,2,2688]{2,1,0:T(2,128)S(1)}, u32[]{:S(2)}, u32[]{:S(2)}) collective-permute-start(f32[1,2,2688]{2,1,0:T(2,128)S(1)} %get-tuple-element.49), channel_id=1, source_target_pairs={{0,9},{1,8},{2,11},{3,10},{4,13},{5,12},{6,15},{7,14},{8,1},{9,0},... | collective-permute-start | bytes 64520 | tf_op jit(solution)/shard_map/ppermute | solution.py:25
  14.5 5.3 %collective-permute-start.5 = (f32[1,2,2688]{2,1,0:T(2,128)S(1)}, f32[1,2,2688]{2,1,0:T(2,128)S(1)}, u32[]{:S(2)}, u32[]{:S(2)}) collective-permute-start(f32[1,2,2688]{2,1,0:T(2,128)S(1)} %add_add_fusion.1), channel_id=1, source_target_pairs={{0,7},{1,6},{2,5},{3,4},{4,3},{5,2},{6,1},{7,0},{8,15},{9,14},{10,... | collective-permute-start | bytes 64520 | tf_op jit(solution)/shard_map/ppermute | solution.py:25
  17.0 3.2 %collective-permute-start.6 = (f32[1,2,2688]{2,1,0:T(2,128)S(1)}, f32[1,2,2688]{2,1,0:T(2,128)S(1)}, u32[]{:S(2)}, u32[]{:S(2)}) collective-permute-start(f32[1,2,2688]{2,1,0:T(2,128)S(1)} %add_add_fusion.1), channel_id=1, source_target_pairs={{0,5},{1,4},{2,7},{3,6},{4,1},{5,0},{6,3},{7,2},{8,13},{9,12},{10,... | collective-permute-start | bytes 64520 | tf_op jit(solution)/shard_map/ppermute | solution.py:25
  17.3 3.2 %collective-permute-start.4 = (f32[1,2,2688]{2,1,0:T(2,128)S(1)}, f32[1,2,2688]{2,1,0:T(2,128)S(1)}, u32[]{:S(2)}, u32[]{:S(2)}) collective-permute-start(f32[1,2,2688]{2,1,0:T(2,128)S(1)} %add_add_fusion.1), channel_id=1, source_target_pairs={{0,3},{1,2},{2,1},{3,0},{4,7},{5,6},{6,5},{7,4},{8,11},{9,10},{10,... | collective-permute-start | bytes 64520 | tf_op jit(solution)/shard_map/ppermute | solution.py:25
  22.1 11.6 %copy-start = (bf16[1,512,1280]{2,1,0:T(8,128)(2,1)S(1)}, bf16[1,512,1280]{2,1,0:T(8,128)(2,1)}, u32[]{:S(2)}) copy-start(bf16[1,512,1280]{2,1,0:T(8,128)(2,1)} %param.6) | copy-start | bytes 3932164
  22.1 11.6 %copy-start.1 = (bf16[1,512,1280]{2,1,0:T(8,128)(2,1)S(1)}, bf16[1,512,1280]{2,1,0:T(8,128)(2,1)}, u32[]{:S(2)}) copy-start(bf16[1,512,1280]{2,1,0:T(8,128)(2,1)} %param.7) | copy-start | bytes 3932164
  22.1 4.8 %collective-permute-start.8 = (f32[1,2,2688]{2,1,0:T(2,128)S(1)}, f32[1,2,2688]{2,1,0:T(2,128)S(1)}, u32[]{:S(2)}, u32[]{:S(2)}) collective-permute-start(f32[1,2,2688]{2,1,0:T(2,128)S(1)} %bitcast.44), channel_id=1, source_target_pairs={{0,7},{1,6},{2,5},{3,4},{4,3},{5,2},{6,1},{7,0},{8,15},{9,14},{10,... | collective-permute-start | bytes 64520 | tf_op jit(solution)/shard_map/ppermute | solution.py:25
  23.7 3.3 %collective-permute-start.9 = (f32[1,2,2688]{2,1,0:T(2,128)S(1)}, f32[1,2,2688]{2,1,0:T(2,128)S(1)}, u32[]{:S(2)}, u32[]{:S(2)}) collective-permute-start(f32[1,2,2688]{2,1,0:T(2,128)S(1)} %bitcast.45), channel_id=1, source_target_pairs={{0,5},{1,4},{2,7},{3,6},{4,1},{5,0},{6,3},{7,2},{8,13},{9,12},{10,... | collective-permute-start | bytes 64520 | tf_op jit(solution)/shard_map/ppermute | solution.py:25
  24.2 3.2 %collective-permute-start.7 = (f32[1,2,2688]{2,1,0:T(2,128)S(1)}, f32[1,2,2688]{2,1,0:T(2,128)S(1)}, u32[]{:S(2)}, u32[]{:S(2)}) collective-permute-start(f32[1,2,2688]{2,1,0:T(2,128)S(1)} %bitcast.46), channel_id=1, source_target_pairs={{0,3},{1,2},{2,1},{3,0},{4,7},{5,6},{6,5},{7,4},{8,11},{9,10},{10,... | collective-permute-start | bytes 64520 | tf_op jit(solution)/shard_map/ppermute | solution.py:25
  27.4 5.5 %collective-permute-start.11 = (f32[1,2,2688]{2,1,0:T(2,128)S(1)}, f32[1,2,2688]{2,1,0:T(2,128)S(1)}, u32[]{:S(2)}, u32[]{:S(2)}) collective-permute-start(f32[1,2,2688]{2,1,0:T(2,128)S(1)} %add_add_fusion), channel_id=1, source_target_pairs={{0,25},{1,24},{2,27},{3,26},{4,29},{5,28},{6,31},{7,30},{8,17},{9,... | collective-permute-start | bytes 64520 | tf_op jit(solution)/shard_map/ppermute | solution.py:25
  28.9 4.2 %collective-permute-start.12 = (f32[1,2,2688]{2,1,0:T(2,128)S(1)}, f32[1,2,2688]{2,1,0:T(2,128)S(1)}, u32[]{:S(2)}, u32[]{:S(2)}) collective-permute-start(f32[1,2,2688]{2,1,0:T(2,128)S(1)} %add_add_fusion), channel_id=1, source_target_pairs={{0,17},{1,16},{2,19},{3,18},{4,21},{5,20},{6,23},{7,22},{8,25},{9,... | collective-permute-start | bytes 64520 | tf_op jit(solution)/shard_map/ppermute | solution.py:25
  29.3 4.2 %collective-permute-start.10 = (f32[1,2,2688]{2,1,0:T(2,128)S(1)}, f32[1,2,2688]{2,1,0:T(2,128)S(1)}, u32[]{:S(2)}, u32[]{:S(2)}) collective-permute-start(f32[1,2,2688]{2,1,0:T(2,128)S(1)} %add_add_fusion), channel_id=1, source_target_pairs={{0,9},{1,8},{2,11},{3,10},{4,13},{5,12},{6,15},{7,14},{8,1},{9,0},... | collective-permute-start | bytes 64520 | tf_op jit(solution)/shard_map/ppermute | solution.py:25
  34.7 1.2 %collective-permute-start.13 = (f32[1,2,1280]{2,1,0:T(2,128)S(1)}, f32[1,2,1280]{2,1,0:T(2,128)S(1)}, u32[]{:S(2)}, u32[]{:S(2)}) collective-permute-start(f32[1,2,1280]{2,1,0:T(2,128)S(1)} %bitcast.47), channel_id=1, source_target_pairs={{0,1},{1,0},{2,3},{3,2},{4,5},{5,4},{6,7},{7,6},{8,9},{9,8},{10,11... | collective-permute-start | bytes 30728 | tf_op jit(solution)/shard_map/ppermute | solution.py:29
  35.9 5.0 %collective-permute-start.15 = (f32[1,2,1280]{2,1,0:T(2,128)S(1)}, f32[1,2,1280]{2,1,0:T(2,128)S(1)}, u32[]{:S(2)}, u32[]{:S(2)}) collective-permute-start(f32[1,2,1280]{2,1,0:T(2,128)S(1)} %select_add_fusion), channel_id=1, source_target_pairs={{0,7},{1,6},{2,5},{3,4},{4,3},{5,2},{6,1},{7,0},{8,15},{9,14},{10,... | collective-permute-start | bytes 30728 | tf_op jit(solution)/shard_map/ppermute | solution.py:25
  38.1 3.1 %collective-permute-start.16 = (f32[1,2,1280]{2,1,0:T(2,128)S(1)}, f32[1,2,1280]{2,1,0:T(2,128)S(1)}, u32[]{:S(2)}, u32[]{:S(2)}) collective-permute-start(f32[1,2,1280]{2,1,0:T(2,128)S(1)} %select_add_fusion), channel_id=1, source_target_pairs={{0,5},{1,4},{2,7},{3,6},{4,1},{5,0},{6,3},{7,2},{8,13},{9,12},{10,... | collective-permute-start | bytes 30728 | tf_op jit(solution)/shard_map/ppermute | solution.py:25
  38.5 3.1 %collective-permute-start.14 = (f32[1,2,1280]{2,1,0:T(2,128)S(1)}, f32[1,2,1280]{2,1,0:T(2,128)S(1)}, u32[]{:S(2)}, u32[]{:S(2)}) collective-permute-start(f32[1,2,1280]{2,1,0:T(2,128)S(1)} %select_add_fusion), channel_id=1, source_target_pairs={{0,3},{1,2},{2,1},{3,0},{4,7},{5,6},{6,5},{7,4},{8,11},{9,10},{10,... | collective-permute-start | bytes 30728 | tf_op jit(solution)/shard_map/ppermute | solution.py:25
  41.6 5.6 %collective-permute-start.17 = (f32[1,2,1280]{2,1,0:T(2,128)S(1)}, f32[1,2,1280]{2,1,0:T(2,128)S(1)}, u32[]{:S(2)}, u32[]{:S(2)}) collective-permute-start(f32[1,2,1280]{2,1,0:T(2,128)S(1)} %add_add_fusion.2.refs_0_), channel_id=1, source_target_pairs={{0,25},{1,24},{2,27},{3,26},{4,29},{5,28},{6,31},{7,30},{8,17},{9,... | collective-permute-start | bytes 30728 | tf_op jit(solution)/shard_map/ppermute | solution.py:25
  43.6 4.1 %collective-permute-start.18 = (f32[1,2,1280]{2,1,0:T(2,128)S(1)}, f32[1,2,1280]{2,1,0:T(2,128)S(1)}, u32[]{:S(2)}, u32[]{:S(2)}) collective-permute-start(f32[1,2,1280]{2,1,0:T(2,128)S(1)} %add_add_fusion.2.refs_0_), channel_id=1, source_target_pairs={{0,17},{1,16},{2,19},{3,18},{4,21},{5,20},{6,23},{7,22},{8,25},{9,... | collective-permute-start | bytes 30728 | tf_op jit(solution)/shard_map/ppermute | solution.py:25
  44.0 3.7 %collective-permute-start.19 = (f32[1,2,1280]{2,1,0:T(2,128)S(1)}, f32[1,2,1280]{2,1,0:T(2,128)S(1)}, u32[]{:S(2)}, u32[]{:S(2)}) collective-permute-start(f32[1,2,1280]{2,1,0:T(2,128)S(1)} %add_add_fusion.2.refs_0_), channel_id=1, source_target_pairs={{0,9},{1,8},{2,11},{3,10},{4,13},{5,12},{6,15},{7,14},{8,1},{9,0},... | collective-permute-start | bytes 30728 | tf_op jit(solution)/shard_map/ppermute | solution.py:25

commit v13 on v12

--- a/solution.py
+++ b/solution.py
@@ -47,6 +47,12 @@
     return [masks[i : i + 2] for i in range(0, len(masks), 2)]
 
 
+def narrow(value):
+    lane = lax.broadcasted_iota(jnp.int32, value.shape, value.ndim - 1)
+    lost = value - lax.reduce_precision(value, 8, 7)
+    return jnp.where(lane < value.shape[-1] - LANES, value, lost).astype(bf16)
+
+
 def swaps(pair):
     return pair if len(pair) == 1 else [pair[0], pair[0] | pair[1], pair[1]]
 
@@ -73,7 +79,7 @@
         terms = {0: block_for(0)}
         for mask in swaps(pair):
             terms[mask] = exchange(block_for(mask), mask)
-        value = added(terms, pair)
+        value = added({mask: term.astype(f32) for mask, term in terms.items()}, pair)
     return value
 
 
@@ -87,7 +93,8 @@
 def sum_to_all(value, group, later=()):
     place = lax.axis_index("seq")
     for pair in rounds(lax.axis_size("seq")):
-        terms = round_terms(value, pair)
+        terms = round_terms(value if pair[0] == 1 else narrow(value), pair)
+        terms = {mask: term.astype(f32) for mask, term in terms.items()}
         inner = [mask for mask in pair if mask < group]
         outer = [mask for mask in pair if mask >= group]
         if inner:
@@ -144,15 +151,17 @@
     exp_high = exp_scores.astype(bf16).astype(f32)
     halves = jnp.concatenate([exp_high, exp_scores - exp_high], axis=0).astype(bf16)
     in_parts = jnp.dot(halves, tok_buf[...], preferred_element_type=f32)
-    message_ref[:, :width] = in_parts[:experts] + in_parts[experts:]
-    spare = message_ref.shape[1] - 2 * width
-    total = as_row(jnp.sum(exp_scores, axis=1, keepdims=True), spare)
-    message_ref[:, 2 * width :] = jnp.broadcast_to(total, (experts, spare))
+    message_ref[:, :width] = (in_parts[:experts] + in_parts[experts:]).astype(bf16)
+    total = as_row(jnp.sum(exp_scores, axis=1, keepdims=True), LANES)
+    high = total.astype(bf16).astype(f32)
+    total = jnp.concatenate([high, total - high], axis=1).astype(bf16)
+    message_ref[:, 2 * width :] = jnp.broadcast_to(total, (experts, 2 * LANES))
     exp_ref[...] = exp_scores
     combine_ref[...] = combine
     for copy in cot_copies:
         copy.wait()
-    message_ref[:, width : 2 * width] = jnp.dot(combine, cot_buf[...], preferred_element_type=f32)
+    cot_part = jnp.dot(combine, cot_buf[...], preferred_element_type=f32)
+    message_ref[:, width : 2 * width] = cot_part.astype(bf16)
 
 
 def fetch(in_ref, out_ref, in_buf, out_buf, sems):
@@ -170,11 +179,11 @@
         copy.wait()
 
 
-def expert_rows(owned_ref, sums_ref, in_ref, out_ref, message_ref, row_x_ref, row_cot_ref, hidden_ref, pre_grad_ref):
+def expert_rows(owned_ref, sums_ref, in_ref, out_ref, message_ref, totals_ref, row_x_ref, row_cot_ref, hidden_ref, pre_grad_ref):
     width, units = in_ref.shape
-    spare = sums_ref[:, 2 * width :]
-    lane = lax.broadcasted_iota(jnp.int32, spare.shape, 1)
-    own_total = jnp.sum(jnp.where(lane == owned_ref[0], spare, 0.0), axis=1, keepdims=True)
+    totals = sums_ref[:, 2 * width : 2 * width + LANES] + sums_ref[:, 2 * width + LANES :]
+    lane = lax.broadcasted_iota(jnp.int32, totals.shape, 1)
+    own_total = jnp.sum(jnp.where(lane == owned_ref[0], totals, 0.0), axis=1, keepdims=True)
     own_in = sums_ref[:, :width] / own_total
     row_x = own_in.astype(bf16)
     row_cot = sums_ref[:, width : 2 * width].astype(bf16)
@@ -189,7 +198,8 @@
     message_ref[:, :width] = part_out
     message_ref[:, width : 2 * width] = part_dx
     dot_part = jnp.sum(own_in * part_dx, axis=1, keepdims=True)
-    message_ref[:, 2 * width :] = jnp.broadcast_to(dot_part, spare.shape)
+    message_ref[:, 2 * width :] = jnp.broadcast_to(dot_part, (totals.shape[0], 2 * LANES))
+    totals_ref[...] = totals
     row_x_ref[...] = row_x
     row_cot_ref[...] = row_cot
     hidden_ref[...] = hidden
@@ -212,7 +222,8 @@
     width = tok_ref.shape[1]
     slot_y = slots_ref[:, :width].astype(bf16)
     slot_dx = slots_ref[:, width : 2 * width].astype(bf16)
-    column_stat = slots_ref[:, 2 * width : 2 * width + 1]
+    low = 2 * width + LANES
+    column_stat = slots_ref[:, 2 * width : 2 * width + 1] + slots_ref[:, low : low + 1]
     totals = as_column(totals_ref[...], slot_y.shape[0])
     exp_scores = exp_ref[...]
     combine_f = exp_scores / jnp.sum(exp_scores, axis=0, keepdims=True)
@@ -227,6 +238,27 @@
     dispatch_ref[...] = dispatch_f.astype(bf16)
 
 
+def mix(slots_ref, combine_ref, mixed_ref):
+    slot_y = slots_ref[:, : mixed_ref.shape[1]].astype(bf16)
+    mixed_ref[...] = lax.dot_general(
+        combine_ref[...], slot_y, COLUMNS, preferred_element_type=f32
+    ).astype(bf16)
+
+
+def token_grads(phi_ref, slots_ref, grad_ref, dispatch_ref, scale_ref, tok_ref, out_ref):
+    width = tok_ref.shape[1]
+    phi = phi_ref[...].astype(f32)
+    phi_scale = lax.rsqrt(jnp.sum(phi * phi, axis=1, keepdims=True) + epsilon)
+    phi_norm = (phi * phi_scale).astype(bf16)
+    slot_dx = slots_ref[:, width : 2 * width].astype(bf16)
+    norm_grad = lax.dot_general(grad_ref[...], phi_norm, COLUMNS, preferred_element_type=f32)
+    through = lax.dot_general(dispatch_ref[...], slot_dx, COLUMNS, preferred_element_type=f32)
+    tok_scale = scale_ref[...]
+    tok_unit = tok_ref[...].astype(f32) * tok_scale
+    along = jnp.sum(tok_unit * norm_grad, axis=1, keepdims=True)
+    out_ref[...] = (through + tok_scale * (norm_grad - tok_unit * along)).astype(bf16)
+
+
 def finish(phi_ref, *refs):
     *term_refs, grad_ref = refs
     own, *others = [ref[0] for ref in term_refs]
@@ -255,7 +287,7 @@
     clips = lax.axis_size("dp")
     clip = lax.axis_index("dp")
     owned = lax.axis_index("seq") // group
-    length = 2 * width + -(-experts // LANES) * LANES
+    length = 2 * width + 2 * LANES
     scalar = pl.BlockSpec(memory_space=pltpu.SMEM)
     in_vmem = pl.BlockSpec(memory_space=pltpu.VMEM)
     in_hbm = pl.BlockSpec(memory_space=pltpu.HBM)
@@ -265,7 +297,7 @@
         token_sums,
         in_specs=[scalar, in_hbm, in_hbm, in_hbm],
         out_shape=[
-            jax.ShapeDtypeStruct((experts, length), f32),
+            jax.ShapeDtypeStruct((experts, length), bf16),
             jax.ShapeDtypeStruct((experts, count), f32),
             jax.ShapeDtypeStruct((experts, count), bf16),
             jax.ShapeDtypeStruct((count, 1), f32),
@@ -299,12 +331,12 @@
         name="fetch_weights",
     )(in_place(expert_in), in_place(expert_out))
     message = sum_to_owner(message, group)[0]
-    totals = message[:, 2 * width :]
-    message, row_x, row_cot, hidden, pre_grad = pl.pallas_call(
+    message, totals, row_x, row_cot, hidden, pre_grad = pl.pallas_call(
         expert_rows,
         in_specs=[scalar] + [in_vmem] * 3,
         out_shape=[
             jax.ShapeDtypeStruct((clips, length), f32),
+            jax.ShapeDtypeStruct((clips, LANES), f32),
             jax.ShapeDtypeStruct((clips, width), bf16),
             jax.ShapeDtypeStruct((clips, width), bf16),
             jax.ShapeDtypeStruct((clips, units), bf16),
@@ -313,14 +345,17 @@
         compiler_params=params,
         name="expert_rows",
     )(owned[None], message, expert_in, expert_out)
-    message, hidden, row_cot = sum_to_all(message[None], group, (hidden, row_cot))
+    share = width // clips
+    mine_x = lax.dynamic_slice_in_dim(row_x, clip * share, share, 1)
+    grad_expert_in = jnp.einsum("od,oh->dh", mine_x, pre_grad, preferred_element_type=f32)
+    message, grad_expert_in, hidden, row_cot = sum_to_all(
+        message[None], group, (grad_expert_in, hidden, row_cot)
+    )
+    mine_cot = lax.dynamic_slice_in_dim(row_cot, clip * share, share, 1)
+    grad_expert_out = jnp.einsum("oh,od->hd", hidden, mine_cot, preferred_element_type=f32)
+    message, grad_expert_out = lax.optimization_barrier((message, grad_expert_out))
     slots = lax.dynamic_index_in_dim(message, clip, 1, keepdims=False)
     totals = lax.dynamic_index_in_dim(totals, clip, 0, keepdims=True)
-    share = width // clips
-    mine_x = lax.dynamic_slice_in_dim(row_x, clip * share, share, 1)
-    mine_cot = lax.dynamic_slice_in_dim(row_cot, clip * share, share, 1)
-    grad_expert_in = jnp.einsum("od,oh->dh", mine_x, pre_grad, preferred_element_type=f32)
-    grad_expert_out = jnp.einsum("oh,od->hd", hidden, mine_cot, preferred_element_type=f32)
     score_grad, dispatch, phi_part = pl.pallas_call(
         score_grads,
         in_specs=[scalar] + [in_vmem] * 6,
@@ -332,10 +367,43 @@
         compiler_params=params,
         name="score_grads",
     )(logit_scale, slots, totals, tok_in, tok_cot, tok_norm, exp_scores)
+    rows = count // PIECES
+    whole = [pl.BlockSpec(shape, lambda i: (0, 0)) for shape in [(experts, width), (experts, length)]]
+    of_slots = pl.BlockSpec((experts, rows), lambda i: (0, i))
+    of_tokens = [pl.BlockSpec((rows, last), lambda i: (i, 0)) for last in (1, width)]
+    token_shape = jax.ShapeDtypeStruct((count, width), bf16)
     phi_sum = sum(of_clips(phi_part[None]))
+    mixed = pl.pallas_call(
+        mix,
+        grid=(PIECES,),
+        in_specs=[whole[1], of_slots],
+        out_specs=of_tokens[1],
+        out_shape=token_shape,
+        compiler_params=params,
+        cost_estimate=pl.CostEstimate(
+            flops=2 * experts * tok_in.size, bytes_accessed=2 * tok_in.size, transcendentals=0
+        ),
+        name="mix",
+    )(slots, combine)
+    phi_sum, mixed, score_grad, dispatch = lax.optimization_barrier(
+        (phi_sum, mixed, score_grad, dispatch)
+    )
+    grad_tokens = pl.pallas_call(
+        token_grads,
+        grid=(PIECES,),
+        in_specs=[*whole, of_slots, of_slots, *of_tokens],
+        out_specs=of_tokens[1],
+        out_shape=token_shape,
+        compiler_params=params,
+        cost_estimate=pl.CostEstimate(
+            flops=4 * experts * tok_in.size, bytes_accessed=4 * tok_in.size, transcendentals=0
+        ),
+        name="token_grads",
+    )(phi, slots, score_grad, dispatch, tok_scale, tok_in)
     *earlier, final = rounds(size)
     for pair in earlier:
         phi_sum = added(round_terms(phi_sum, pair), pair)
+    phi_sum, grad_tokens = lax.optimization_barrier((phi_sum, grad_tokens))
     terms = round_terms(phi_sum, final)
     grad_router = pl.pallas_call(
         finish,
@@ -344,20 +412,6 @@
         compiler_params=params,
         name="finish",
     )(phi, terms.pop(0), *[terms[mask] for mask in sorted(terms, reverse=True)])
-    phi_f32 = phi.astype(f32)
-    phi_scale = lax.rsqrt(jnp.sum(phi_f32 * phi_f32, axis=1, keepdims=True) + epsilon)
-    phi_unit = phi_f32 * phi_scale
-    phi_norm = phi_unit.astype(bf16)
-    slot_y = slots[:, :width].astype(bf16)
-    slot_dx = slots[:, width : 2 * width].astype(bf16)
-    mixed = jnp.einsum("sn,sd->nd", combine, slot_y, preferred_element_type=f32).astype(bf16)
-    norm_grad = jnp.einsum("sn,sd->nd", score_grad, phi_norm, preferred_element_type=f32)
-    through = jnp.einsum("sn,sd->nd", dispatch, slot_dx, preferred_element_type=f32)
-    tok_unit = tok_in.astype(f32) * tok_scale
-    back_norm = tok_scale * (
-        norm_grad - tok_unit * jnp.sum(tok_unit * norm_grad, axis=1, keepdims=True)
-    )
-    grad_tokens = (through + back_norm).astype(bf16)
     return (mixed[None], grad_tokens[None], grad_expert_in, grad_expert_out, grad_router.T)
 
 

time: 48.7 us -> 53 us (1.088)
  Pallas kernels: 8.13 us -> 13.4 us
  matrix products: 7.52 us -> 3.18 us
  waiting for transfers between devices: 7.35 us -> 11.1 us
    pallas_call x0 -> x2, Pallas kernels: none -> 5.24 us  [the longest x1 2.95 us: per_device(): pl.pallas_call(token_grads, grid=(PIECES,), in_specs=[*whole, of_slots, o...]
    dot_general x3 -> x0, matrix products: 4.34 us -> none  [the longest x1 1.99 us: per_device(): jnp.einsum('sn,sd->nd', dispatch, slot_dx, preferred_element_type=f32)]
    ppermute x18, waiting for transfers between devices: 6.37 us -> 10.2 us  [exchange(): return lax.ppermute(value, AXES, pairs)]
  transfers between devices with their start and end apart: 20 -> 20, of which waited for: 13 -> 9; matrix products, arithmetic and copies ran while one was open for 16% -> 6% of each run, Pallas kernels for 4% -> 14%
where the time goes in v13:
time: 53 us; the launch traced here: 52.9 us
  starting transfers between devices  23.4 us (44%)
  Pallas kernels  13.4 us (25%)
  waiting for transfers between devices  11.1 us (21%)
  matrix products  3.18 us (6%)
  between operations  1.47 us (3%)
    ppermute x18, starting transfers between devices, exchange(): return lax.ppermute(value, AXES, pairs)  22.8 us
    ppermute x18, waiting for transfers between devices, exchange(): return lax.ppermute(value, AXES, pairs)  10.2 us
    pallas_call x1, Pallas kernels, per_device(): pl.pallas_call(token_grads, grid=(PIECES,), in_specs=[*whole, of_slots, o...  2.95 us
    pallas_call x1, Pallas kernels, per_device(): pl.pallas_call(token_sums, in_specs=[scalar, in_hbm, in_hbm, in_hbm], out...  2.8 us
    pallas_call x1, Pallas kernels, per_device(): pl.pallas_call(mix, grid=(PIECES,), in_specs=[whole[1], of_slots], out_sp...  2.29 us
    pallas_call x1, Pallas kernels, per_device(): pl.pallas_call(fetch, in_specs=[in_hbm] * 2, out_specs=[in_vmem] * 2, out...  1.93 us
    dot_general x1, matrix products, per_device(): jnp.einsum('od,oh->dh', mine_x, pre_grad, preferred_element_type=f32)  1.59 us
    dot_general x1, matrix products, per_device(): jnp.einsum('oh,od->hd', hidden, mine_cot, preferred_element_type=f32)  1.59 us
  transfers between devices with their start and end apart: 20, of which 9 were waited for; matrix products, arithmetic and copies ran while one was open for 6% of the time, Pallas kernels for 14%

profile of v13, /device:TPU:0, one launch (start us, length us, event | category | flops | bytes accessed | tf_op | source)
XLA Modules:
  0.0 52.9 jit_solution(14814570700661707931)
XLA Ops:
  1.3 2.8 %token_sums.1 = (bf16[2,2816]{1,0:T(2,128)(2,1)S(1)}, f32[2,512]{1,0:T(2,128)S(1)}, bf16[2,512]{1,0:T(2,128)(2,1)S(1)}, f32[512,1]{1,0:T(8,128)S(1)}, bf16[512,1280]{1,0:T(8,128)(2,1)S(1)}) custom-call(f32[1]{0:T(128)S(6)} %copy.15.scale_ref, bf16[2,1280]{1,0:T(2,128)(2,1)} %bitcast.30, bf16[512,1280]{1,0:T(8,128)(2,1)} %bitcast.25, bf16[512,1280]{1,0:T(8,128)(2,1)} %bitcast.28), custom_call_target="tpu_custom_call" | custom-call | tf_op jit(solution)/shard_map/token_sums/pallas_call | solution.py:296
  4.1 0.5 collective-permute-start
  4.6 0.8 %collective-permute-done = bf16[2,2816]{1,0:T(2,128)(2,1)S(1)} collective-permute-done((bf16[2,2816]{1,0:T(2,128)(2,1)S(1)}, bf16[2,2816]{1,0:T(2,128)(2,1)S(1)}, u32[]{:S(2)}, u32[]{:S(2)}) %collective-permute-start) | collective-permute-done | bytes 11296 | tf_op jit(solution)/shard_map/ppermute | solution.py:29
  5.5 0.1 pad_maximum_fusion
  5.6 2.8 %collective-permute-start.1 = (bf16[1,2,2816]{2,1,0:T(2,128)(2,1)S(1)}, bf16[1,2,2816]{2,1,0:T(2,128)(2,1)S(1)}, u32[]{:S(2)}, u32[]{:S(2)}) collective-permute-start(bf16[1,2,2816]{2,1,0:T(2,128)(2,1)S(1)} %get-tuple-element.67), channel_id=1, source_target_pairs={{0,9},{1,8},{2,11},{3,10},{4,13},{5,12},{6,15},{7,14},{8,1},{9,0},... | collective-permute-start | bytes 33800 | tf_op jit(solution)/shard_map/ppermute | solution.py:25
  8.4 2.5 %collective-permute-start.3 = (bf16[1,2,2816]{2,1,0:T(2,128)(2,1)S(1)}, bf16[1,2,2816]{2,1,0:T(2,128)(2,1)S(1)}, u32[]{:S(2)}, u32[]{:S(2)}) collective-permute-start(bf16[1,2,2816]{2,1,0:T(2,128)(2,1)S(1)} %get-tuple-element.68), channel_id=1, source_target_pairs={{0,17},{1,16},{2,19},{3,18},{4,21},{5,20},{6,23},{7,22},{8,25},{9,... | collective-permute-start | bytes 33800 | tf_op jit(solution)/shard_map/ppermute | solution.py:25
  10.9 0.0 collective-permute-start.2
  10.9 0.0 collective-permute-done.1
  10.9 1.5 %collective-permute-done.3 = bf16[1,2,2816]{2,1,0:T(2,128)(2,1)S(1)} collective-permute-done((bf16[1,2,2816]{2,1,0:T(2,128)(2,1)S(1)}, bf16[1,2,2816]{2,1,0:T(2,128)(2,1)S(1)}, u32[]{:S(2)}, u32[]{:S(2)}) %collective-permute-start.3) | collective-permute-done | bytes 11296 | tf_op jit(solution)/shard_map/ppermute | solution.py:25
  12.4 3.4 %collective-permute-done.2 = bf16[1,2,2816]{2,1,0:T(2,128)(2,1)S(1)} collective-permute-done((bf16[1,2,2816]{2,1,0:T(2,128)(2,1)S(1)}, bf16[1,2,2816]{2,1,0:T(2,128)(2,1)S(1)}, u32[]{:S(2)}, u32[]{:S(2)}) %collective-permute-start.2) | collective-permute-done | bytes 11296 | tf_op jit(solution)/shard_map/ppermute | solution.py:25
  15.9 1.4 %collective-permute-start.6 = (f32[1,2,2816]{2,1,0:T(2,128)S(1)}, f32[1,2,2816]{2,1,0:T(2,128)S(1)}, u32[]{:S(2)}, u32[]{:S(2)}) collective-permute-start(f32[1,2,2816]{2,1,0:T(2,128)S(1)} %add_add_fusion.1), channel_id=1, source_target_pairs={{0,5},{1,4},{2,7},{3,6},{4,1},{5,0},{6,3},{7,2},{8,13},{9,12},{10,... | collective-permute-start | bytes 67592 | tf_op jit(solution)/shard_map/ppermute | solution.py:25
  17.2 1.4 %collective-permute-start.5 = (f32[1,2,2816]{2,1,0:T(2,128)S(1)}, f32[1,2,2816]{2,1,0:T(2,128)S(1)}, u32[]{:S(2)}, u32[]{:S(2)}) collective-permute-start(f32[1,2,2816]{2,1,0:T(2,128)S(1)} %add_add_fusion.1), channel_id=1, source_target_pairs={{0,7},{1,6},{2,5},{3,4},{4,3},{5,2},{6,1},{7,0},{8,15},{9,14},{10,... | collective-permute-start | bytes 67592 | tf_op jit(solution)/shard_map/ppermute | solution.py:25
  18.6 0.3 collective-permute-start.4
  18.9 1.9 %fetch_weights.1 = (bf16[1280,640]{1,0:T(8,128)(2,1)S(1)}, bf16[640,1280]{1,0:T(8,128)(2,1)S(1)}) custom-call(bf16[1280,640]{1,0:T(8,128)(2,1)} %in_ref, bf16[640,1280]{1,0:T(8,128)(2,1)} %out_ref), custom_call_target="tpu_custom_call" | custom-call | bytes 6553600 | tf_op jit(solution)/shard_map/fetch_weights/pallas_call | solution.py:318
  20.8 0.0 collective-permute-done.6
  20.9 0.5 collective-permute-done.5
  21.3 0.5 collective-permute-done.4
  21.8 1.5 %expert_rows.1 = (f32[2,2816]{1,0:T(2,128)S(1)}, f32[2,128]{1,0:T(2,128)S(1)}, bf16[2,1280]{1,0:T(2,128)(2,1)S(1)}, bf16[2,1280]{1,0:T(2,128)(2,1)S(1)}, bf16[2,...) custom-call(s32[1]{0:T(128)} %bitcast.owned_ref, f32[2,2816]{1,0:T(2,128)S(1)} %add_bitcast_fusion.2.sums_ref, ...), custom_call_target="tpu_custom_call" | custom-call | tf_op jit(solution)/shard_map/expert_rows/pallas_call | solution.py:334
  23.4 1.5 %collective-permute-start.8 = (f32[1,2,2816]{2,1,0:T(2,128)S(1)}, f32[1,2,2816]{2,1,0:T(2,128)S(1)}, u32[]{:S(2)}, u32[]{:S(2)}) collective-permute-start(f32[1,2,2816]{2,1,0:T(2,128)S(1)} %bitcast.33), channel_id=1, source_target_pairs={{0,7},{1,6},{2,5},{3,4},{4,3},{5,2},{6,1},{7,0},{8,15},{9,14},{10,... | collective-permute-start | bytes 67592 | tf_op jit(solution)/shard_map/ppermute | solution.py:25
  24.8 0.7 %collective-permute-start.9 = (f32[1,2,2816]{2,1,0:T(2,128)S(1)}, f32[1,2,2816]{2,1,0:T(2,128)S(1)}, u32[]{:S(2)}, u32[]{:S(2)}) collective-permute-start(f32[1,2,2816]{2,1,0:T(2,128)S(1)} %bitcast.34), channel_id=1, source_target_pairs={{0,5},{1,4},{2,7},{3,6},{4,1},{5,0},{6,3},{7,2},{8,13},{9,12},{10,... | collective-permute-start | bytes 67592 | tf_op jit(solution)/shard_map/ppermute | solution.py:25
  25.6 0.8 %collective-permute-start.7 = (f32[1,2,2816]{2,1,0:T(2,128)S(1)}, f32[1,2,2816]{2,1,0:T(2,128)S(1)}, u32[]{:S(2)}, u32[]{:S(2)}) collective-permute-start(f32[1,2,2816]{2,1,0:T(2,128)S(1)} %bitcast.35), channel_id=1, source_target_pairs={{0,3},{1,2},{2,1},{3,0},{4,7},{5,6},{6,5},{7,4},{8,11},{9,10},{10,... | collective-permute-start | bytes 67592 | tf_op jit(solution)/shard_map/ppermute | solution.py:25
  26.4 1.6 %fusion.5 = f32[640,640]{1,0:T(8,128)} fusion(bf16[2,640]{1,0:T(2,128)(2,1)S(1)} %get-tuple-element.44, bf16[2,1280]{1,0:T(2,128)(2,1)S(1)} %get-tuple-element.43, s32[]{:T(128)S(6)} %select_n.88), kind=kOutput, calls=%fused_computation.19 | convolution fusion | flops 1638400 | bytes 1643524 | tf_op jit(solution)/shard_map/od,oh->dh/dot_general | solution.py:350
  28.0 0.0 collective-permute-done.8
  28.0 0.1 collective-permute-done.9
  28.1 0.7 %collective-permute-done.7 = f32[1,2,2816]{2,1,0:T(2,128)S(1)} collective-permute-done((f32[1,2,2816]{2,1,0:T(2,128)S(1)}, f32[1,2,2816]{2,1,0:T(2,128)S(1)}, u32[]{:S(2)}, u32[]{:S(2)}) %collective-permute-start.7) | collective-permute-done | bytes 22560 | tf_op jit(solution)/shard_map/ppermute | solution.py:25
  28.9 0.5 collective-permute-start.11
  29.3 0.0 collective-permute-start.12
  29.3 3.9 %collective-permute-start.10 = (bf16[1,2,2816]{2,1,0:T(2,128)(2,1)S(1)}, bf16[1,2,2816]{2,1,0:T(2,128)(2,1)S(1)}, u32[]{:S(2)}, u32[]{:S(2)}) collective-permute-start(bf16[1,2,2816]{2,1,0:T(2,128)(2,1)S(1)} %fusion), channel_id=1, source_target_pairs={{0,9},{1,8},{2,11},{3,10},{4,13},{5,12},{6,15},{7,14},{8,1},{9,0},... | collective-permute-start | bytes 33800 | tf_op jit(solution)/shard_map/ppermute | solution.py:25
  33.2 1.6 %fusion.3 = f32[640,640]{1,0:T(8,128)} fusion(bf16[2,640]{1,0:T(2,128)(2,1)S(1)} %get-tuple-element.48, bf16[2,1280]{1,0:T(2,128)(2,1)S(1)} %get-tuple-element.49, s32[]{:T(128)S(6)} %select_n.88), kind=kOutput, calls=%fused_computation.17 | convolution fusion | flops 1638400 | bytes 1643524 | tf_op jit(solution)/shard_map/oh,od->hd/dot_general | solution.py:355
  34.8 0.0 collective-permute-done.10
  34.8 0.0 collective-permute-done.11
  34.8 0.0 collective-permute-done.12
  34.9 0.1 broadcast_select_fusion
  35.0 0.0 copy-start.2
  35.0 1.1 %score_grads.1 = (bf16[2,512]{1,0:T(2,128)(2,1)S(1)}, bf16[2,512]{1,0:T(2,128)(2,1)S(1)}, f32[2,1280]{1,0:T(2,128)S(1)}) custom-call(f32[1]{0:T(128)S(6)} %copy.15.scale_ref, f32[2,2816]{1,0:T(2,128)S(1)} %dynamic-slice_bitcast_fusion.slots_ref, f32[1,128]{1,0:T(1,128)S(1)} %constant_dynamic-slice_fusion.totals_ref, bf16[512,1280]{1,0:T(8,128)(2,1)S(1)} %bitcast.26, ...), custom_call_target="tpu_custom_call" | custom-call | tf_op jit(solution)/shard_map/score_grads/pallas_call | solution.py:359
  36.1 0.0 collective-permute-start.13
  36.1 2.3 %mix.1 = bf16[512,1280]{1,0:T(8,128)(2,1)} custom-call(f32[2,2816]{1,0:T(2,128)S(1)} %dynamic-slice_bitcast_fusion.slots_ref, bf16[2,512]{1,0:T(2,128)(2,1)S(1)} %get-tuple-element.55.combine_ref), custom_call_target="tpu_custom_call" | custom-call | flops 2621440 | bytes 1310720 | tf_op jit(solution)/shard_map/mix/pallas_call | solution.py:376
  38.4 0.0 collective-permute-done.13
  38.4 1.0 %collective-permute-start.16 = (f32[1,2,1280]{2,1,0:T(2,128)S(1)}, f32[1,2,1280]{2,1,0:T(2,128)S(1)}, u32[]{:S(2)}, u32[]{:S(2)}) collective-permute-start(f32[1,2,1280]{2,1,0:T(2,128)S(1)} %select_add_fusion), channel_id=1, source_target_pairs={{0,5},{1,4},{2,7},{3,6},{4,1},{5,0},{6,3},{7,2},{8,13},{9,12},{10,... | collective-permute-start | bytes 30728 | tf_op jit(solution)/shard_map/ppermute | solution.py:25
  39.4 1.2 %collective-permute-start.15 = (f32[1,2,1280]{2,1,0:T(2,128)S(1)}, f32[1,2,1280]{2,1,0:T(2,128)S(1)}, u32[]{:S(2)}, u32[]{:S(2)}) collective-permute-start(f32[1,2,1280]{2,1,0:T(2,128)S(1)} %select_add_fusion), channel_id=1, source_target_pairs={{0,7},{1,6},{2,5},{3,4},{4,3},{5,2},{6,1},{7,0},{8,15},{9,14},{10,... | collective-permute-start | bytes 30728 | tf_op jit(solution)/shard_map/ppermute | solution.py:25
  40.6 1.2 %collective-permute-start.14 = (f32[1,2,1280]{2,1,0:T(2,128)S(1)}, f32[1,2,1280]{2,1,0:T(2,128)S(1)}, u32[]{:S(2)}, u32[]{:S(2)}) collective-permute-start(f32[1,2,1280]{2,1,0:T(2,128)S(1)} %select_add_fusion), channel_id=1, source_target_pairs={{0,3},{1,2},{2,1},{3,0},{4,7},{5,6},{6,5},{7,4},{8,11},{9,10},{10,... | collective-permute-start | bytes 30728 | tf_op jit(solution)/shard_map/ppermute | solution.py:25
  41.8 3.0 %token_grads.1 = bf16[512,1280]{1,0:T(8,128)(2,1)} custom-call(bf16[2,1280]{1,0:T(2,128)(2,1)S(1)} %bitcast.31, f32[2,2816]{1,0:T(2,128)S(1)} %dynamic-slice_bitcast_fusion.slots_ref, bf16[2,512]{1,0:T(2,128)(2,1)S(1)} %get-tuple-element.60.grad_ref, bf16[2,512]{1,0:T(2,128)(2,1)S(1)} %get-tuple-element.61.dispatch_ref, ...), custom_call_target="tpu_custom_call" | custom-call | flops 5242880 | bytes 2621440 | tf_op jit(solution)/shard_map/token_grads/pallas_call | solution.py:391
  44.8 1.6 %collective-permute-start.19 = (f32[1,2,1280]{2,1,0:T(2,128)S(1)}, f32[1,2,1280]{2,1,0:T(2,128)S(1)}, u32[]{:S(2)}, u32[]{:S(2)}) collective-permute-start(f32[1,2,1280]{2,1,0:T(2,128)S(1)} %add_add_fusion.2.refs_0_), channel_id=1, source_target_pairs={{0,9},{1,8},{2,11},{3,10},{4,13},{5,12},{6,15},{7,14},{8,1},{9,0},... | collective-permute-start | bytes 30728 | tf_op jit(solution)/shard_map/ppermute | solution.py:25
  46.3 0.8 %collective-permute-start.18 = (f32[1,2,1280]{2,1,0:T(2,128)S(1)}, f32[1,2,1280]{2,1,0:T(2,128)S(1)}, u32[]{:S(2)}, u32[]{:S(2)}) collective-permute-start(f32[1,2,1280]{2,1,0:T(2,128)S(1)} %add_add_fusion.2.refs_0_), channel_id=1, source_target_pairs={{0,17},{1,16},{2,19},{3,18},{4,21},{5,20},{6,23},{7,22},{8,25},{9,... | collective-permute-start | bytes 30728 | tf_op jit(solution)/shard_map/ppermute | solution.py:25
  47.2 1.4 %collective-permute-start.17 = (f32[1,2,1280]{2,1,0:T(2,128)S(1)}, f32[1,2,1280]{2,1,0:T(2,128)S(1)}, u32[]{:S(2)}, u32[]{:S(2)}) collective-permute-start(f32[1,2,1280]{2,1,0:T(2,128)S(1)} %add_add_fusion.2.refs_0_), channel_id=1, source_target_pairs={{0,25},{1,24},{2,27},{3,26},{4,29},{5,28},{6,31},{7,30},{8,17},{9,... | collective-permute-start | bytes 30728 | tf_op jit(solution)/shard_map/ppermute | solution.py:25
  48.6 1.8 %collective-permute-done.18.refs_2_ = f32[1,2,1280]{2,1,0:T(2,128)S(1)} collective-permute-done((f32[1,2,1280]{2,1,0:T(2,128)S(1)}, f32[1,2,1280]{2,1,0:T(2,128)S(1)}, u32[]{:S(2)}, u32[]{:S(2)}) %collective-permute-start.18) | collective-permute-done | bytes 10272 | tf_op jit(solution)/shard_map/ppermute | solution.py:25
  50.3 1.7 %collective-permute-done.17.refs_1_ = f32[1,2,1280]{2,1,0:T(2,128)S(1)} collective-permute-done((f32[1,2,1280]{2,1,0:T(2,128)S(1)}, f32[1,2,1280]{2,1,0:T(2,128)S(1)}, u32[]{:S(2)}, u32[]{:S(2)}) %collective-permute-start.17) | collective-permute-done | bytes 10272 | tf_op jit(solution)/shard_map/ppermute | solution.py:25
  52.1 0.8 %finish.1 = f32[2,1280]{1,0:T(2,128)} custom-call(bf16[2,1280]{1,0:T(2,128)(2,1)S(1)} %bitcast.32, f32[1,2,1280]{2,1,0:T(2,128)S(1)} %add_add_fusion.2.refs_0_, f32[1,2,1280]{2,1,0:T(2,128)S(1)} %collective-permute-done.17.refs_1_, f32[1,2,1280]{2,1,0:T(2,128)S(1)} %collective-permute-done.18.refs_2_, f32[1,2,1280]{2,1,0:T(2,128)S(1)} %collective-permute-done.19.refs_3_), custom_call_target="tpu_custom_call" | custom-call | tf_op jit(solution)/shard_map/finish/pallas_call | solution.py:408
  (25 shorter events, 0.3 us)
Async XLA Ops:
  4.1 1.4 %collective-permute-start = (bf16[2,2816]{1,0:T(2,128)(2,1)S(1)}, bf16[2,2816]{1,0:T(2,128)(2,1)S(1)}, u32[]{:S(2)}, u32[]{:S(2)}) collective-permute-start(bf16[2,2816]{1,0:T(2,128)(2,1)S(1)} %get-tuple-element.36), channel_id=1, source_target_pairs={{0,1},{1,0},{2,3},{3,2},{4,5},{5,4},{6,7},{7,6},{8,9},{9,8},{10,11... | collective-permute-start | bytes 33800 | tf_op jit(solution)/shard_map/ppermute | solution.py:29
  5.6 5.3 %collective-permute-start.1 = (bf16[1,2,2816]{2,1,0:T(2,128)(2,1)S(1)}, bf16[1,2,2816]{2,1,0:T(2,128)(2,1)S(1)}, u32[]{:S(2)}, u32[]{:S(2)}) collective-permute-start(bf16[1,2,2816]{2,1,0:T(2,128)(2,1)S(1)} %get-tuple-element.67), channel_id=1, source_target_pairs={{0,9},{1,8},{2,11},{3,10},{4,13},{5,12},{6,15},{7,14},{8,1},{9,0},... | collective-permute-start | bytes 33800 | tf_op jit(solution)/shard_map/ppermute | solution.py:25
  8.4 4.0 %collective-permute-start.3 = (bf16[1,2,2816]{2,1,0:T(2,128)(2,1)S(1)}, bf16[1,2,2816]{2,1,0:T(2,128)(2,1)S(1)}, u32[]{:S(2)}, u32[]{:S(2)}) collective-permute-start(bf16[1,2,2816]{2,1,0:T(2,128)(2,1)S(1)} %get-tuple-element.68), channel_id=1, source_target_pairs={{0,17},{1,16},{2,19},{3,18},{4,21},{5,20},{6,23},{7,22},{8,25},{9,... | collective-permute-start | bytes 33800 | tf_op jit(solution)/shard_map/ppermute | solution.py:25
  10.9 4.9 %collective-permute-start.2 = (bf16[1,2,2816]{2,1,0:T(2,128)(2,1)S(1)}, bf16[1,2,2816]{2,1,0:T(2,128)(2,1)S(1)}, u32[]{:S(2)}, u32[]{:S(2)}) collective-permute-start(bf16[1,2,2816]{2,1,0:T(2,128)(2,1)S(1)} %get-tuple-element.69), channel_id=1, source_target_pairs={{0,25},{1,24},{2,27},{3,26},{4,29},{5,28},{6,31},{7,30},{8,17},{9,... | collective-permute-start | bytes 33800 | tf_op jit(solution)/shard_map/ppermute | solution.py:25
  15.9 5.0 %collective-permute-start.6 = (f32[1,2,2816]{2,1,0:T(2,128)S(1)}, f32[1,2,2816]{2,1,0:T(2,128)S(1)}, u32[]{:S(2)}, u32[]{:S(2)}) collective-permute-start(f32[1,2,2816]{2,1,0:T(2,128)S(1)} %add_add_fusion.1), channel_id=1, source_target_pairs={{0,5},{1,4},{2,7},{3,6},{4,1},{5,0},{6,3},{7,2},{8,13},{9,12},{10,... | collective-permute-start | bytes 67592 | tf_op jit(solution)/shard_map/ppermute | solution.py:25
  17.2 4.1 %collective-permute-start.5 = (f32[1,2,2816]{2,1,0:T(2,128)S(1)}, f32[1,2,2816]{2,1,0:T(2,128)S(1)}, u32[]{:S(2)}, u32[]{:S(2)}) collective-permute-start(f32[1,2,2816]{2,1,0:T(2,128)S(1)} %add_add_fusion.1), channel_id=1, source_target_pairs={{0,7},{1,6},{2,5},{3,4},{4,3},{5,2},{6,1},{7,0},{8,15},{9,14},{10,... | collective-permute-start | bytes 67592 | tf_op jit(solution)/shard_map/ppermute | solution.py:25
  18.6 3.2 %collective-permute-start.4 = (f32[1,2,2816]{2,1,0:T(2,128)S(1)}, f32[1,2,2816]{2,1,0:T(2,128)S(1)}, u32[]{:S(2)}, u32[]{:S(2)}) collective-permute-start(f32[1,2,2816]{2,1,0:T(2,128)S(1)} %add_add_fusion.1), channel_id=1, source_target_pairs={{0,3},{1,2},{2,1},{3,0},{4,7},{5,6},{6,5},{7,4},{8,11},{9,10},{10,... | collective-permute-start | bytes 67592 | tf_op jit(solution)/shard_map/ppermute | solution.py:25
  23.4 4.6 %collective-permute-start.8 = (f32[1,2,2816]{2,1,0:T(2,128)S(1)}, f32[1,2,2816]{2,1,0:T(2,128)S(1)}, u32[]{:S(2)}, u32[]{:S(2)}) collective-permute-start(f32[1,2,2816]{2,1,0:T(2,128)S(1)} %bitcast.33), channel_id=1, source_target_pairs={{0,7},{1,6},{2,5},{3,4},{4,3},{5,2},{6,1},{7,0},{8,15},{9,14},{10,... | collective-permute-start | bytes 67592 | tf_op jit(solution)/shard_map/ppermute | solution.py:25
  24.8 3.3 %collective-permute-start.9 = (f32[1,2,2816]{2,1,0:T(2,128)S(1)}, f32[1,2,2816]{2,1,0:T(2,128)S(1)}, u32[]{:S(2)}, u32[]{:S(2)}) collective-permute-start(f32[1,2,2816]{2,1,0:T(2,128)S(1)} %bitcast.34), channel_id=1, source_target_pairs={{0,5},{1,4},{2,7},{3,6},{4,1},{5,0},{6,3},{7,2},{8,13},{9,12},{10,... | collective-permute-start | bytes 67592 | tf_op jit(solution)/shard_map/ppermute | solution.py:25
  25.6 3.2 %collective-permute-start.7 = (f32[1,2,2816]{2,1,0:T(2,128)S(1)}, f32[1,2,2816]{2,1,0:T(2,128)S(1)}, u32[]{:S(2)}, u32[]{:S(2)}) collective-permute-start(f32[1,2,2816]{2,1,0:T(2,128)S(1)} %bitcast.35), channel_id=1, source_target_pairs={{0,3},{1,2},{2,1},{3,0},{4,7},{5,6},{6,5},{7,4},{8,11},{9,10},{10,... | collective-permute-start | bytes 67592 | tf_op jit(solution)/shard_map/ppermute | solution.py:25
  26.4 8.6 %copy-start = (bf16[1,512,1280]{2,1,0:T(8,128)(2,1)S(1)}, bf16[1,512,1280]{2,1,0:T(8,128)(2,1)}, u32[]{:S(2)}) copy-start(bf16[1,512,1280]{2,1,0:T(8,128)(2,1)} %param.6) | copy-start | bytes 3932164
  26.4 8.6 %copy-start.1 = (bf16[1,512,1280]{2,1,0:T(8,128)(2,1)S(1)}, bf16[1,512,1280]{2,1,0:T(8,128)(2,1)}, u32[]{:S(2)}) copy-start(bf16[1,512,1280]{2,1,0:T(8,128)(2,1)} %param.7) | copy-start | bytes 3932164
  28.9 6.0 %collective-permute-start.11 = (bf16[1,2,2816]{2,1,0:T(2,128)(2,1)S(1)}, bf16[1,2,2816]{2,1,0:T(2,128)(2,1)S(1)}, u32[]{:S(2)}, u32[]{:S(2)}) collective-permute-start(bf16[1,2,2816]{2,1,0:T(2,128)(2,1)S(1)} %fusion), channel_id=1, source_target_pairs={{0,25},{1,24},{2,27},{3,26},{4,29},{5,28},{6,31},{7,30},{8,17},{9,... | collective-permute-start | bytes 33800 | tf_op jit(solution)/shard_map/ppermute | solution.py:25
  29.3 5.5 %collective-permute-start.12 = (bf16[1,2,2816]{2,1,0:T(2,128)(2,1)S(1)}, bf16[1,2,2816]{2,1,0:T(2,128)(2,1)S(1)}, u32[]{:S(2)}, u32[]{:S(2)}) collective-permute-start(bf16[1,2,2816]{2,1,0:T(2,128)(2,1)S(1)} %fusion), channel_id=1, source_target_pairs={{0,17},{1,16},{2,19},{3,18},{4,21},{5,20},{6,23},{7,22},{8,25},{9,... | collective-permute-start | bytes 33800 | tf_op jit(solution)/shard_map/ppermute | solution.py:25
  29.3 5.4 %collective-permute-start.10 = (bf16[1,2,2816]{2,1,0:T(2,128)(2,1)S(1)}, bf16[1,2,2816]{2,1,0:T(2,128)(2,1)S(1)}, u32[]{:S(2)}, u32[]{:S(2)}) collective-permute-start(bf16[1,2,2816]{2,1,0:T(2,128)(2,1)S(1)} %fusion), channel_id=1, source_target_pairs={{0,9},{1,8},{2,11},{3,10},{4,13},{5,12},{6,15},{7,14},{8,1},{9,0},... | collective-permute-start | bytes 33800 | tf_op jit(solution)/shard_map/ppermute | solution.py:25
  35.0 6.8 %copy-start.2 = (bf16[1280,2]{0,1:T(2,128)(2,1)S(1)}, bf16[1280,2]{0,1:T(2,128)(2,1)}, u32[]{:S(2)}) copy-start(bf16[1280,2]{0,1:T(2,128)(2,1)} %param.8) | copy-start | bytes 15364
  36.1 2.3 %collective-permute-start.13 = (f32[1,2,1280]{2,1,0:T(2,128)S(1)}, f32[1,2,1280]{2,1,0:T(2,128)S(1)}, u32[]{:S(2)}, u32[]{:S(2)}) collective-permute-start(f32[1,2,1280]{2,1,0:T(2,128)S(1)} %bitcast.36), channel_id=1, source_target_pairs={{0,1},{1,0},{2,3},{3,2},{4,5},{5,4},{6,7},{7,6},{8,9},{9,8},{10,11... | collective-permute-start | bytes 30728 | tf_op jit(solution)/shard_map/ppermute | solution.py:29
  38.4 6.3 %collective-permute-start.16 = (f32[1,2,1280]{2,1,0:T(2,128)S(1)}, f32[1,2,1280]{2,1,0:T(2,128)S(1)}, u32[]{:S(2)}, u32[]{:S(2)}) collective-permute-start(f32[1,2,1280]{2,1,0:T(2,128)S(1)} %select_add_fusion), channel_id=1, source_target_pairs={{0,5},{1,4},{2,7},{3,6},{4,1},{5,0},{6,3},{7,2},{8,13},{9,12},{10,... | collective-permute-start | bytes 30728 | tf_op jit(solution)/shard_map/ppermute | solution.py:25
  39.4 5.3 %collective-permute-start.15 = (f32[1,2,1280]{2,1,0:T(2,128)S(1)}, f32[1,2,1280]{2,1,0:T(2,128)S(1)}, u32[]{:S(2)}, u32[]{:S(2)}) collective-permute-start(f32[1,2,1280]{2,1,0:T(2,128)S(1)} %select_add_fusion), channel_id=1, source_target_pairs={{0,7},{1,6},{2,5},{3,4},{4,3},{5,2},{6,1},{7,0},{8,15},{9,14},{10,... | collective-permute-start | bytes 30728 | tf_op jit(solution)/shard_map/ppermute | solution.py:25
  40.6 4.1 %collective-permute-start.14 = (f32[1,2,1280]{2,1,0:T(2,128)S(1)}, f32[1,2,1280]{2,1,0:T(2,128)S(1)}, u32[]{:S(2)}, u32[]{:S(2)}) collective-permute-start(f32[1,2,1280]{2,1,0:T(2,128)S(1)} %select_add_fusion), channel_id=1, source_target_pairs={{0,3},{1,2},{2,1},{3,0},{4,7},{5,6},{6,5},{7,4},{8,11},{9,10},{10,... | collective-permute-start | bytes 30728 | tf_op jit(solution)/shard_map/ppermute | solution.py:25
  44.8 3.8 %collective-permute-start.19 = (f32[1,2,1280]{2,1,0:T(2,128)S(1)}, f32[1,2,1280]{2,1,0:T(2,128)S(1)}, u32[]{:S(2)}, u32[]{:S(2)}) collective-permute-start(f32[1,2,1280]{2,1,0:T(2,128)S(1)} %add_add_fusion.2.refs_0_), channel_id=1, source_target_pairs={{0,9},{1,8},{2,11},{3,10},{4,13},{5,12},{6,15},{7,14},{8,1},{9,0},... | collective-permute-start | bytes 30728 | tf_op jit(solution)/shard_map/ppermute | solution.py:25
  46.3 4.0 %collective-permute-start.18 = (f32[1,2,1280]{2,1,0:T(2,128)S(1)}, f32[1,2,1280]{2,1,0:T(2,128)S(1)}, u32[]{:S(2)}, u32[]{:S(2)}) collective-permute-start(f32[1,2,1280]{2,1,0:T(2,128)S(1)} %add_add_fusion.2.refs_0_), channel_id=1, source_target_pairs={{0,17},{1,16},{2,19},{3,18},{4,21},{5,20},{6,23},{7,22},{8,25},{9,... | collective-permute-start | bytes 30728 | tf_op jit(solution)/shard_map/ppermute | solution.py:25
  47.2 4.9 %collective-permute-start.17 = (f32[1,2,1280]{2,1,0:T(2,128)S(1)}, f32[1,2,1280]{2,1,0:T(2,128)S(1)}, u32[]{:S(2)}, u32[]{:S(2)}) collective-permute-start(f32[1,2,1280]{2,1,0:T(2,128)S(1)} %add_add_fusion.2.refs_0_), channel_id=1, source_target_pairs={{0,25},{1,24},{2,27},{3,26},{4,29},{5,28},{6,31},{7,30},{8,17},{9,... | collective-permute-start | bytes 30728 | tf_op jit(solution)/shard_map/ppermute | solution.py:25

commit v14 on v12

--- a/solution.py
+++ b/solution.py
@@ -31,20 +31,22 @@
 
 def of_clips(value):
     clips = lax.axis_size("dp")
-    clip = lax.axis_index("dp")
-    got = [value] + [hop(value, step) for step in range(1, clips)]
-    ordered = []
-    for index in range(clips):
-        picked = got[0]
-        for step in range(1, clips):
-            picked = jnp.where(clip ^ step == index, got[step], picked)
-        ordered.append(picked)
-    return ordered
+    apart = lax.broadcasted_iota(jnp.int32, (1, clips, 1), 1) ^ lax.axis_index("dp")
+    merged = value[:, None]
+    for step in range(1, clips):
+        merged = jnp.where(apart == step, hop(value, step)[:, None], merged)
+    return merged
 
 
 def rounds(size):
     masks = [1 << bit for bit in range(size.bit_length() - 1)]
     return [masks[i : i + 2] for i in range(0, len(masks), 2)]
+
+
+def narrow(value):
+    lane = lax.broadcasted_iota(jnp.int32, value.shape, value.ndim - 1)
+    lost = value - lax.reduce_precision(value, 8, 7)
+    return jnp.where(lane < value.shape[-1] - LANES, value, lost).astype(bf16)
 
 
 def swaps(pair):
@@ -73,7 +75,7 @@
         terms = {0: block_for(0)}
         for mask in swaps(pair):
             terms[mask] = exchange(block_for(mask), mask)
-        value = added(terms, pair)
+        value = added({mask: term.astype(f32) for mask, term in terms.items()}, pair)
     return value
 
 
@@ -87,7 +89,8 @@
 def sum_to_all(value, group, later=()):
     place = lax.axis_index("seq")
     for pair in rounds(lax.axis_size("seq")):
-        terms = round_terms(value, pair)
+        terms = round_terms(value if pair[0] == 1 else narrow(value), pair)
+        terms = {mask: term.astype(f32) for mask, term in terms.items()}
         inner = [mask for mask in pair if mask < group]
         outer = [mask for mask in pair if mask >= group]
         if inner:
@@ -144,15 +147,17 @@
     exp_high = exp_scores.astype(bf16).astype(f32)
     halves = jnp.concatenate([exp_high, exp_scores - exp_high], axis=0).astype(bf16)
     in_parts = jnp.dot(halves, tok_buf[...], preferred_element_type=f32)
-    message_ref[:, :width] = in_parts[:experts] + in_parts[experts:]
-    spare = message_ref.shape[1] - 2 * width
-    total = as_row(jnp.sum(exp_scores, axis=1, keepdims=True), spare)
-    message_ref[:, 2 * width :] = jnp.broadcast_to(total, (experts, spare))
+    message_ref[:, :width] = (in_parts[:experts] + in_parts[experts:]).astype(bf16)
+    total = as_row(jnp.sum(exp_scores, axis=1, keepdims=True), LANES)
+    high = total.astype(bf16).astype(f32)
+    total = jnp.concatenate([high, total - high], axis=1).astype(bf16)
+    message_ref[:, 2 * width :] = jnp.broadcast_to(total, (experts, 2 * LANES))
     exp_ref[...] = exp_scores
     combine_ref[...] = combine
     for copy in cot_copies:
         copy.wait()
-    message_ref[:, width : 2 * width] = jnp.dot(combine, cot_buf[...], preferred_element_type=f32)
+    cot_part = jnp.dot(combine, cot_buf[...], preferred_element_type=f32)
+    message_ref[:, width : 2 * width] = cot_part.astype(bf16)
 
 
 def fetch(in_ref, out_ref, in_buf, out_buf, sems):
@@ -170,11 +175,11 @@
         copy.wait()
 
 
-def expert_rows(owned_ref, sums_ref, in_ref, out_ref, message_ref, row_x_ref, row_cot_ref, hidden_ref, pre_grad_ref):
+def expert_rows(owned_ref, sums_ref, in_ref, out_ref, message_ref, totals_ref, row_x_ref, row_cot_ref, hidden_ref, pre_grad_ref):
     width, units = in_ref.shape
-    spare = sums_ref[:, 2 * width :]
-    lane = lax.broadcasted_iota(jnp.int32, spare.shape, 1)
-    own_total = jnp.sum(jnp.where(lane == owned_ref[0], spare, 0.0), axis=1, keepdims=True)
+    totals = sums_ref[:, 2 * width : 2 * width + LANES] + sums_ref[:, 2 * width + LANES :]
+    lane = lax.broadcasted_iota(jnp.int32, totals.shape, 1)
+    own_total = jnp.sum(jnp.where(lane == owned_ref[0], totals, 0.0), axis=1, keepdims=True)
     own_in = sums_ref[:, :width] / own_total
     row_x = own_in.astype(bf16)
     row_cot = sums_ref[:, width : 2 * width].astype(bf16)
@@ -189,7 +194,8 @@
     message_ref[:, :width] = part_out
     message_ref[:, width : 2 * width] = part_dx
     dot_part = jnp.sum(own_in * part_dx, axis=1, keepdims=True)
-    message_ref[:, 2 * width :] = jnp.broadcast_to(dot_part, spare.shape)
+    message_ref[:, 2 * width :] = jnp.broadcast_to(dot_part, (totals.shape[0], 2 * LANES))
+    totals_ref[...] = totals
     row_x_ref[...] = row_x
     row_cot_ref[...] = row_cot
     hidden_ref[...] = hidden
@@ -212,7 +218,8 @@
     width = tok_ref.shape[1]
     slot_y = slots_ref[:, :width].astype(bf16)
     slot_dx = slots_ref[:, width : 2 * width].astype(bf16)
-    column_stat = slots_ref[:, 2 * width : 2 * width + 1]
+    low = 2 * width + LANES
+    column_stat = slots_ref[:, 2 * width : 2 * width + 1] + slots_ref[:, low : low + 1]
     totals = as_column(totals_ref[...], slot_y.shape[0])
     exp_scores = exp_ref[...]
     combine_f = exp_scores / jnp.sum(exp_scores, axis=0, keepdims=True)
@@ -255,7 +262,7 @@
     clips = lax.axis_size("dp")
     clip = lax.axis_index("dp")
     owned = lax.axis_index("seq") // group
-    length = 2 * width + -(-experts // LANES) * LANES
+    length = 2 * width + 2 * LANES
     scalar = pl.BlockSpec(memory_space=pltpu.SMEM)
     in_vmem = pl.BlockSpec(memory_space=pltpu.VMEM)
     in_hbm = pl.BlockSpec(memory_space=pltpu.HBM)
@@ -265,7 +272,7 @@
         token_sums,
         in_specs=[scalar, in_hbm, in_hbm, in_hbm],
         out_shape=[
-            jax.ShapeDtypeStruct((experts, length), f32),
+            jax.ShapeDtypeStruct((experts, length), bf16),
             jax.ShapeDtypeStruct((experts, count), f32),
             jax.ShapeDtypeStruct((experts, count), bf16),
             jax.ShapeDtypeStruct((count, 1), f32),
@@ -276,12 +283,12 @@
             pltpu.VMEM((count, width), bf16),
             pltpu.VMEM((count, width), bf16),
             pltpu.SemaphoreType.DMA,
-            pltpu.SemaphoreType.DMA((2, PIECES)),
+            pltpu.SemaphoreType.DMA((2, 2 * PIECES)),
         ],
         compiler_params=params,
         name="token_sums",
     )(logit_scale, in_place(phi), in_place(tok_in), in_place(tok_cot))
-    message = jnp.stack(of_clips(message), axis=1)
+    message = of_clips(message)
     message, expert_in, expert_out = lax.optimization_barrier((message, expert_in, expert_out))
     expert_in, expert_out = pl.pallas_call(
         fetch,
@@ -299,12 +306,12 @@
         name="fetch_weights",
     )(in_place(expert_in), in_place(expert_out))
     message = sum_to_owner(message, group)[0]
-    totals = message[:, 2 * width :]
-    message, row_x, row_cot, hidden, pre_grad = pl.pallas_call(
+    message, totals, row_x, row_cot, hidden, pre_grad = pl.pallas_call(
         expert_rows,
         in_specs=[scalar] + [in_vmem] * 3,
         out_shape=[
             jax.ShapeDtypeStruct((clips, length), f32),
+            jax.ShapeDtypeStruct((clips, LANES), f32),
             jax.ShapeDtypeStruct((clips, width), bf16),
             jax.ShapeDtypeStruct((clips, width), bf16),
             jax.ShapeDtypeStruct((clips, units), bf16),
@@ -332,7 +339,10 @@
         compiler_params=params,
         name="score_grads",
     )(logit_scale, slots, totals, tok_in, tok_cot, tok_norm, exp_scores)
-    phi_sum = sum(of_clips(phi_part[None]))
+    phi_sum = phi_part
+    for step in range(1, clips):
+        phi_sum = phi_sum + hop(phi_part, step)
+    phi_sum = phi_sum[None]
     *earlier, final = rounds(size)
     for pair in earlier:
         phi_sum = added(round_terms(phi_sum, pair), pair)
@@ -343,7 +353,7 @@
         out_shape=jax.ShapeDtypeStruct((experts, width), f32),
         compiler_params=params,
         name="finish",
-    )(phi, terms.pop(0), *[terms[mask] for mask in sorted(terms, reverse=True)])
+    )(phi, terms[0], *[terms[mask] for mask in [*final[1:], sum(final), final[0]][-len(terms) + 1 :]])
     phi_f32 = phi.astype(f32)
     phi_scale = lax.rsqrt(jnp.sum(phi_f32 * phi_f32, axis=1, keepdims=True) + epsilon)
     phi_unit = phi_f32 * phi_scale

time: 48.7 us -> 48.3 us (level)
  starting transfers between devices: 23.4 us -> 21.7 us
  waiting for transfers between devices: 7.35 us -> 8.15 us
    ppermute x18, starting transfers between devices: 22.7 us -> 21 us  [exchange(): return lax.ppermute(value, AXES, pairs)]
    ppermute x18, waiting for transfers between devices: 6.37 us -> 7.22 us  [exchange(): return lax.ppermute(value, AXES, pairs)]
  transfers between devices with their start and end apart: 20 -> 20, of which waited for: 13 -> 11; matrix products, arithmetic and copies ran while one was open for 16% -> 16% of each run, Pallas kernels for 4% -> 4%
where the time goes in v14:
time: 48.3 us; the launch traced here: 48.1 us
  starting transfers between devices  21.7 us (45%)
  Pallas kernels  8.53 us (18%)
  waiting for transfers between devices  8.15 us (17%)
  matrix products  7.52 us (16%)
  between operations  1.47 us (3%)
  other arithmetic  0.62 us (1%)
    ppermute x18, starting transfers between devices, exchange(): return lax.ppermute(value, AXES, pairs)  21 us
    ppermute x18, waiting for transfers between devices, exchange(): return lax.ppermute(value, AXES, pairs)  7.22 us
    pallas_call x1, Pallas kernels, per_device(): pl.pallas_call(token_sums, in_specs=[scalar, in_hbm, in_hbm, in_hbm], out...  3.19 us
    dot_general x1, matrix products, per_device(): jnp.einsum('sn,sd->nd', dispatch, slot_dx, preferred_element_type=f32)  1.99 us
    pallas_call x1, Pallas kernels, per_device(): pl.pallas_call(fetch, in_specs=[in_hbm] * 2, out_specs=[in_vmem] * 2, out...  1.94 us
    dot_general x1, matrix products, per_device(): jnp.einsum('sn,sd->nd', combine, slot_y, preferred_element_type=f32)  1.61 us
    dot_general x1, matrix products, per_device(): jnp.einsum('od,oh->dh', mine_x, pre_grad, preferred_element_type=f32)  1.59 us
    dot_general x1, matrix products, per_device(): jnp.einsum('oh,od->hd', hidden, mine_cot, preferred_element_type=f32)  1.59 us
  transfers between devices with their start and end apart: 20, of which 11 were waited for; matrix products, arithmetic and copies ran while one was open for 16% of the time, Pallas kernels for 4%

profile of v14, /device:TPU:0, one launch (start us, length us, event | category | flops | bytes accessed | tf_op | source)
XLA Modules:
  0.0 48.1 jit_solution(11686108749056659668)
XLA Ops:
  1.3 3.2 %token_sums.1 = (bf16[2,2816]{1,0:T(2,128)(2,1)S(1)}, f32[2,512]{1,0:T(2,128)S(1)}, bf16[2,512]{1,0:T(2,128)(2,1)S(1)}, f32[512,1]{1,0:T(8,128)S(1)}, bf16[512,1280]{1,0:T(8,128)(2,1)S(1)}) custom-call(f32[1]{0:T(128)S(6)} %copy.11.scale_ref, bf16[2,1280]{1,0:T(2,128)(2,1)} %bitcast.40, bf16[512,1280]{1,0:T(8,128)(2,1)} %bitcast.36, bf16[512,1280]{1,0:T(8,128)(2,1)} %bitcast.38), custom_call_target="tpu_custom_call" | custom-call | tf_op jit(solution)/shard_map/token_sums/pallas_call | solution.py:271
  4.5 0.5 %collective-permute-start = (bf16[2,2816]{1,0:T(2,128)(2,1)S(1)}, bf16[2,2816]{1,0:T(2,128)(2,1)S(1)}, u32[]{:S(2)}, u32[]{:S(2)}) collective-permute-start(bf16[2,2816]{1,0:T(2,128)(2,1)S(1)} %get-tuple-element.28), channel_id=1, source_target_pairs={{0,1},{1,0},{2,3},{3,2},{4,5},{5,4},{6,7},{7,6},{8,9},{9,8},{10,11... | collective-permute-start | bytes 33800 | tf_op jit(solution)/shard_map/ppermute | solution.py:29
  5.0 0.1 fusion.4
  5.2 0.7 %collective-permute-done = bf16[2,2816]{1,0:T(2,128)(2,1)S(1)} collective-permute-done((bf16[2,2816]{1,0:T(2,128)(2,1)S(1)}, bf16[2,2816]{1,0:T(2,128)(2,1)S(1)}, u32[]{:S(2)}, u32[]{:S(2)}) %collective-permute-start) | collective-permute-done | bytes 11296 | tf_op jit(solution)/shard_map/ppermute | solution.py:29
  5.9 0.1 broadcast_select_fusion
  6.0 3.8 %collective-permute-start.3 = (bf16[1,2,2816]{2,1,0:T(2,128)(2,1)S(1)}, bf16[1,2,2816]{2,1,0:T(2,128)(2,1)S(1)}, u32[]{:S(2)}, u32[]{:S(2)}) collective-permute-start(bf16[1,2,2816]{2,1,0:T(2,128)(2,1)S(1)} %get-tuple-element.52), channel_id=1, source_target_pairs={{0,17},{1,16},{2,19},{3,18},{4,21},{5,20},{6,23},{7,22},{8,25},{9,... | collective-permute-start | bytes 33800 | tf_op jit(solution)/shard_map/ppermute | solution.py:25
  9.8 1.3 %collective-permute-start.2 = (bf16[1,2,2816]{2,1,0:T(2,128)(2,1)S(1)}, bf16[1,2,2816]{2,1,0:T(2,128)(2,1)S(1)}, u32[]{:S(2)}, u32[]{:S(2)}) collective-permute-start(bf16[1,2,2816]{2,1,0:T(2,128)(2,1)S(1)} %get-tuple-element.53), channel_id=1, source_target_pairs={{0,25},{1,24},{2,27},{3,26},{4,29},{5,28},{6,31},{7,30},{8,17},{9,... | collective-permute-start | bytes 33800 | tf_op jit(solution)/shard_map/ppermute | solution.py:25
  11.1 0.2 collective-permute-start.1
  11.3 0.0 collective-permute-done.3
  11.3 3.4 %collective-permute-done.2 = bf16[1,2,2816]{2,1,0:T(2,128)(2,1)S(1)} collective-permute-done((bf16[1,2,2816]{2,1,0:T(2,128)(2,1)S(1)}, bf16[1,2,2816]{2,1,0:T(2,128)(2,1)S(1)}, u32[]{:S(2)}, u32[]{:S(2)}) %collective-permute-start.2) | collective-permute-done | bytes 11296 | tf_op jit(solution)/shard_map/ppermute | solution.py:25
  14.7 0.0 collective-permute-done.1
  14.7 2.5 %collective-permute-start.5 = (f32[1,2,2816]{2,1,0:T(2,128)S(1)}, f32[1,2,2816]{2,1,0:T(2,128)S(1)}, u32[]{:S(2)}, u32[]{:S(2)}) collective-permute-start(f32[1,2,2816]{2,1,0:T(2,128)S(1)} %add_add_fusion.1), channel_id=1, source_target_pairs={{0,7},{1,6},{2,5},{3,4},{4,3},{5,2},{6,1},{7,0},{8,15},{9,14},{10,... | collective-permute-start | bytes 67592 | tf_op jit(solution)/shard_map/ppermute | solution.py:25
  17.2 0.3 collective-permute-start.6
  17.4 0.5 %collective-permute-start.4 = (f32[1,2,2816]{2,1,0:T(2,128)S(1)}, f32[1,2,2816]{2,1,0:T(2,128)S(1)}, u32[]{:S(2)}, u32[]{:S(2)}) collective-permute-start(f32[1,2,2816]{2,1,0:T(2,128)S(1)} %add_add_fusion.1), channel_id=1, source_target_pairs={{0,3},{1,2},{2,1},{3,0},{4,7},{5,6},{6,5},{7,4},{8,11},{9,10},{10,... | collective-permute-start | bytes 67592 | tf_op jit(solution)/shard_map/ppermute | solution.py:25
  17.9 0.1 reduce
  18.1 1.9 %fetch_weights.1 = (bf16[1280,640]{1,0:T(8,128)(2,1)S(1)}, bf16[640,1280]{1,0:T(8,128)(2,1)S(1)}) custom-call(bf16[1280,640]{1,0:T(8,128)(2,1)} %in_ref, bf16[640,1280]{1,0:T(8,128)(2,1)} %out_ref), custom_call_target="tpu_custom_call" | custom-call | bytes 6553600 | tf_op jit(solution)/shard_map/fetch_weights/pallas_call | solution.py:293
  20.0 0.4 collective-permute-done.6
  20.4 0.3 collective-permute-done.4
  20.7 1.5 %expert_rows.1 = (f32[2,2816]{1,0:T(2,128)S(1)}, f32[2,128]{1,0:T(2,128)S(1)}, bf16[2,1280]{1,0:T(2,128)(2,1)S(1)}, bf16[2,1280]{1,0:T(2,128)(2,1)S(1)}, bf16[2,...) custom-call(s32[1]{0:T(128)} %bitcast.3.owned_ref, f32[2,2816]{1,0:T(2,128)S(1)} %add_bitcast_fusion.2.sums_ref, ...), custom_call_target="tpu_custom_call" | custom-call | tf_op jit(solution)/shard_map/expert_rows/pallas_call | solution.py:309
  22.2 1.6 %collective-permute-start.8 = (f32[1,2,2816]{2,1,0:T(2,128)S(1)}, f32[1,2,2816]{2,1,0:T(2,128)S(1)}, u32[]{:S(2)}, u32[]{:S(2)}) collective-permute-start(f32[1,2,2816]{2,1,0:T(2,128)S(1)} %bitcast.42), channel_id=1, source_target_pairs={{0,7},{1,6},{2,5},{3,4},{4,3},{5,2},{6,1},{7,0},{8,15},{9,14},{10,... | collective-permute-start | bytes 67592 | tf_op jit(solution)/shard_map/ppermute | solution.py:25
  23.9 0.5 collective-permute-start.9
  24.3 1.1 %collective-permute-start.7 = (f32[1,2,2816]{2,1,0:T(2,128)S(1)}, f32[1,2,2816]{2,1,0:T(2,128)S(1)}, u32[]{:S(2)}, u32[]{:S(2)}) collective-permute-start(f32[1,2,2816]{2,1,0:T(2,128)S(1)} %bitcast.44), channel_id=1, source_target_pairs={{0,3},{1,2},{2,1},{3,0},{4,7},{5,6},{6,5},{7,4},{8,11},{9,10},{10,... | collective-permute-start | bytes 67592 | tf_op jit(solution)/shard_map/ppermute | solution.py:25
  25.4 1.6 %fusion.12 = f32[640,640]{1,0:T(8,128)} fusion(bf16[2,640]{1,0:T(2,128)(2,1)S(1)} %get-tuple-element.45, bf16[2,1280]{1,0:T(2,128)(2,1)S(1)} %get-tuple-element.44, s32[]{:T(128)S(6)} %select_n.68), kind=kOutput, calls=%fused_computation.28 | convolution fusion | flops 1638400 | bytes 1643524 | tf_op jit(solution)/shard_map/od,oh->dh/dot_general | solution.py:329
  27.0 0.1 collective-permute-done.9
  27.2 0.4 collective-permute-done.7
  27.6 1.0 %collective-permute-start.12 = (bf16[1,2,2816]{2,1,0:T(2,128)(2,1)S(1)}, bf16[1,2,2816]{2,1,0:T(2,128)(2,1)S(1)}, u32[]{:S(2)}, u32[]{:S(2)}) collective-permute-start(bf16[1,2,2816]{2,1,0:T(2,128)(2,1)S(1)} %fusion.3), channel_id=1, source_target_pairs={{0,17},{1,16},{2,19},{3,18},{4,21},{5,20},{6,23},{7,22},{8,25},{9,... | collective-permute-start | bytes 33800 | tf_op jit(solution)/shard_map/ppermute | solution.py:25
  28.6 0.9 %collective-permute-start.11 = (bf16[1,2,2816]{2,1,0:T(2,128)(2,1)S(1)}, bf16[1,2,2816]{2,1,0:T(2,128)(2,1)S(1)}, u32[]{:S(2)}, u32[]{:S(2)}) collective-permute-start(bf16[1,2,2816]{2,1,0:T(2,128)(2,1)S(1)} %fusion.3), channel_id=1, source_target_pairs={{0,25},{1,24},{2,27},{3,26},{4,29},{5,28},{6,31},{7,30},{8,17},{9,... | collective-permute-start | bytes 33800 | tf_op jit(solution)/shard_map/ppermute | solution.py:25
  29.5 1.1 %collective-permute-start.10 = (bf16[1,2,2816]{2,1,0:T(2,128)(2,1)S(1)}, bf16[1,2,2816]{2,1,0:T(2,128)(2,1)S(1)}, u32[]{:S(2)}, u32[]{:S(2)}) collective-permute-start(bf16[1,2,2816]{2,1,0:T(2,128)(2,1)S(1)} %fusion.3), channel_id=1, source_target_pairs={{0,9},{1,8},{2,11},{3,10},{4,13},{5,12},{6,15},{7,14},{8,1},{9,0},... | collective-permute-start | bytes 33800 | tf_op jit(solution)/shard_map/ppermute | solution.py:25
  30.7 1.6 %fusion.10 = f32[640,640]{1,0:T(8,128)} fusion(bf16[2,640]{1,0:T(2,128)(2,1)S(1)} %get-tuple-element.46, bf16[2,1280]{1,0:T(2,128)(2,1)S(1)} %get-tuple-element.47, s32[]{:T(128)S(6)} %select_n.68), kind=kOutput, calls=%fused_computation.26 | convolution fusion | flops 1638400 | bytes 1643524 | tf_op jit(solution)/shard_map/oh,od->hd/dot_general | solution.py:330
  32.2 0.0 collective-permute-done.12
  32.3 1.3 %collective-permute-done.11 = bf16[1,2,2816]{2,1,0:T(2,128)(2,1)S(1)} collective-permute-done((bf16[1,2,2816]{2,1,0:T(2,128)(2,1)S(1)}, bf16[1,2,2816]{2,1,0:T(2,128)(2,1)S(1)}, u32[]{:S(2)}, u32[]{:S(2)}) %collective-permute-start.11) | collective-permute-done | bytes 11296 | tf_op jit(solution)/shard_map/ppermute | solution.py:25
  33.7 0.1 fusion.17
  33.8 1.1 %score_grads.1 = (bf16[2,512]{1,0:T(2,128)(2,1)S(1)}, bf16[2,512]{1,0:T(2,128)(2,1)S(1)}, f32[2,1280]{1,0:T(2,128)S(1)}) custom-call(f32[1]{0:T(128)S(6)} %copy.11.scale_ref, f32[2,2816]{1,0:T(2,128)S(1)} %get-tuple-element.50.slots_ref, f32[1,128]{1,0:T(1,128)S(1)} %constant_dynamic-slice_fusion.1.totals_ref, bf16[512,1280]{1,0:T(8,128)(2,1)S(1)} %bitcast.37, ...), custom_call_target="tpu_custom_call" | custom-call | tf_op jit(solution)/shard_map/score_grads/pallas_call | solution.py:331
  34.8 0.2 collective-permute-start.13
  35.0 0.7 %multiply_reduce_fusion = (f32[512]{0:T(512)S(1)}, f32[512,1280]{1,0:T(8,128)S(1)}) fusion(f32[512]{0:T(512)S(1)} %reduce, bf16[1,512,1280]{2,1,0:T(8,128)(2,1)S(1)} %copy-done, bf16[2,512]{1,0:T(2,128)(2,1)S(1)} %get-tuple-element.43, f32[2]{0:T(128)S(1)} %add_rsqrt_fusion, bf16[1280,2]{0,1:T(2,128)(2,1)S(1)} %copy-done.2), kind=kOutput, calls=%fused_computation.5 | convolution fusion | flops 5250048 | bytes 3943432 | tf_op jit(solution)/shard_map/sn,sd->nd/dot_general | solution.py:364
  35.7 0.3 collective-permute-done.13
  36.0 2.1 %collective-permute-start.15 = (f32[1,2,1280]{2,1,0:T(2,128)S(1)}, f32[1,2,1280]{2,1,0:T(2,128)S(1)}, u32[]{:S(2)}, u32[]{:S(2)}) collective-permute-start(f32[1,2,1280]{2,1,0:T(2,128)S(1)} %add_bitcast_fusion.3), channel_id=1, source_target_pairs={{0,7},{1,6},{2,5},{3,4},{4,3},{5,2},{6,1},{7,0},{8,15},{9,14},{10,... | collective-permute-start | bytes 30728 | tf_op jit(solution)/shard_map/ppermute | solution.py:25
  38.1 0.3 collective-permute-start.16
  38.4 0.7 %collective-permute-start.14 = (f32[1,2,1280]{2,1,0:T(2,128)S(1)}, f32[1,2,1280]{2,1,0:T(2,128)S(1)}, u32[]{:S(2)}, u32[]{:S(2)}) collective-permute-start(f32[1,2,1280]{2,1,0:T(2,128)S(1)} %add_bitcast_fusion.3), channel_id=1, source_target_pairs={{0,3},{1,2},{2,1},{3,0},{4,7},{5,6},{6,5},{7,4},{8,11},{9,10},{10,... | collective-permute-start | bytes 30728 | tf_op jit(solution)/shard_map/ppermute | solution.py:25
  39.1 2.0 %fusion.1 = bf16[1,512,1280]{2,1,0:T(8,128)(2,1)} fusion(bf16[2,512]{1,0:T(2,128)(2,1)S(1)} %get-tuple-element.41, f32[512,1280]{1,0:T(8,128)S(1)} %get-tuple-element.55, f32[512]{0:T(512)S(1)} %get-tuple-element.54, f32[512]{0:T(512)S(1)} %reduce, bf16[2,2816]{1,0:T(2,128)(2,1)S(1)} %get-tuple-element.49, bf16[1,512,1280]{2,1,0:T(8,128)(2,1)S(1)} %copy-done), kind=kOutput, calls=%fused_computation.3 | convolution fusion | flops 7208960 | bytes 5254144 | tf_op jit(solution)/shard_map/sn,sd->nd/dot_general | solution.py:365
  41.0 0.2 collective-permute-done.16
  41.2 0.3 collective-permute-done.14
  41.5 0.8 %collective-permute-start.17 = (f32[1,2,1280]{2,1,0:T(2,128)S(1)}, f32[1,2,1280]{2,1,0:T(2,128)S(1)}, u32[]{:S(2)}, u32[]{:S(2)}) collective-permute-start(f32[1,2,1280]{2,1,0:T(2,128)S(1)} %add_add_fusion.2.refs_0_), channel_id=1, source_target_pairs={{0,17},{1,16},{2,19},{3,18},{4,21},{5,20},{6,23},{7,22},{8,25},{9,... | collective-permute-start | bytes 30728 | tf_op jit(solution)/shard_map/ppermute | solution.py:25
  42.3 1.7 %collective-permute-start.18 = (f32[1,2,1280]{2,1,0:T(2,128)S(1)}, f32[1,2,1280]{2,1,0:T(2,128)S(1)}, u32[]{:S(2)}, u32[]{:S(2)}) collective-permute-start(f32[1,2,1280]{2,1,0:T(2,128)S(1)} %add_add_fusion.2.refs_0_), channel_id=1, source_target_pairs={{0,25},{1,24},{2,27},{3,26},{4,29},{5,28},{6,31},{7,30},{8,17},{9,... | collective-permute-start | bytes 30728 | tf_op jit(solution)/shard_map/ppermute | solution.py:25
  44.1 0.7 %collective-permute-start.19 = (f32[1,2,1280]{2,1,0:T(2,128)S(1)}, f32[1,2,1280]{2,1,0:T(2,128)S(1)}, u32[]{:S(2)}, u32[]{:S(2)}) collective-permute-start(f32[1,2,1280]{2,1,0:T(2,128)S(1)} %add_add_fusion.2.refs_0_), channel_id=1, source_target_pairs={{0,9},{1,8},{2,11},{3,10},{4,13},{5,12},{6,15},{7,14},{8,1},{9,0},... | collective-permute-start | bytes 30728 | tf_op jit(solution)/shard_map/ppermute | solution.py:25
  44.7 1.6 %fusion.2 = bf16[1,512,1280]{2,1,0:T(8,128)(2,1)} fusion(bf16[2,512]{1,0:T(2,128)(2,1)S(1)} %get-tuple-element.27, bf16[2,2816]{1,0:T(2,128)(2,1)S(1)} %get-tuple-element.49), kind=kOutput, calls=%fused_computation.4 | convolution fusion | flops 3276800 | bytes 1317888 | tf_op jit(solution)/shard_map/sn,sd->nd/dot_general | solution.py:363
  46.4 0.9 %collective-permute-done.18.refs_2_ = f32[1,2,1280]{2,1,0:T(2,128)S(1)} collective-permute-done((f32[1,2,1280]{2,1,0:T(2,128)S(1)}, f32[1,2,1280]{2,1,0:T(2,128)S(1)}, u32[]{:S(2)}, u32[]{:S(2)}) %collective-permute-start.18) | collective-permute-done | bytes 10272 | tf_op jit(solution)/shard_map/ppermute | solution.py:25
  47.3 0.8 %finish.1 = f32[2,1280]{1,0:T(2,128)} custom-call(bf16[2,1280]{1,0:T(2,128)(2,1)S(1)} %bitcast.41, f32[1,2,1280]{2,1,0:T(2,128)S(1)} %add_add_fusion.2.refs_0_, f32[1,2,1280]{2,1,0:T(2,128)S(1)} %collective-permute-done.17.refs_1_, f32[1,2,1280]{2,1,0:T(2,128)S(1)} %collective-permute-done.18.refs_2_, f32[1,2,1280]{2,1,0:T(2,128)S(1)} %collective-permute-done.19.refs_3_), custom_call_target="tpu_custom_call" | custom-call | tf_op jit(solution)/shard_map/finish/pallas_call | solution.py:350
  (28 shorter events, 0.3 us)
Async XLA Ops:
  0.6 4.4 %copy-start.2 = (bf16[1280,2]{0,1:T(2,128)(2,1)S(1)}, bf16[1280,2]{0,1:T(2,128)(2,1)}, u32[]{:S(2)}) copy-start(bf16[1280,2]{0,1:T(2,128)(2,1)} %param.8) | copy-start | bytes 15364
  4.5 1.4 %collective-permute-start = (bf16[2,2816]{1,0:T(2,128)(2,1)S(1)}, bf16[2,2816]{1,0:T(2,128)(2,1)S(1)}, u32[]{:S(2)}, u32[]{:S(2)}) collective-permute-start(bf16[2,2816]{1,0:T(2,128)(2,1)S(1)} %get-tuple-element.28), channel_id=1, source_target_pairs={{0,1},{1,0},{2,3},{3,2},{4,5},{5,4},{6,7},{7,6},{8,9},{9,8},{10,11... | collective-permute-start | bytes 33800 | tf_op jit(solution)/shard_map/ppermute | solution.py:29
  6.0 5.3 %collective-permute-start.3 = (bf16[1,2,2816]{2,1,0:T(2,128)(2,1)S(1)}, bf16[1,2,2816]{2,1,0:T(2,128)(2,1)S(1)}, u32[]{:S(2)}, u32[]{:S(2)}) collective-permute-start(bf16[1,2,2816]{2,1,0:T(2,128)(2,1)S(1)} %get-tuple-element.52), channel_id=1, source_target_pairs={{0,17},{1,16},{2,19},{3,18},{4,21},{5,20},{6,23},{7,22},{8,25},{9,... | collective-permute-start | bytes 33800 | tf_op jit(solution)/shard_map/ppermute | solution.py:25
  9.8 4.9 %collective-permute-start.2 = (bf16[1,2,2816]{2,1,0:T(2,128)(2,1)S(1)}, bf16[1,2,2816]{2,1,0:T(2,128)(2,1)S(1)}, u32[]{:S(2)}, u32[]{:S(2)}) collective-permute-start(bf16[1,2,2816]{2,1,0:T(2,128)(2,1)S(1)} %get-tuple-element.53), channel_id=1, source_target_pairs={{0,25},{1,24},{2,27},{3,26},{4,29},{5,28},{6,31},{7,30},{8,17},{9,... | collective-permute-start | bytes 33800 | tf_op jit(solution)/shard_map/ppermute | solution.py:25
  11.1 3.6 %collective-permute-start.1 = (bf16[1,2,2816]{2,1,0:T(2,128)(2,1)S(1)}, bf16[1,2,2816]{2,1,0:T(2,128)(2,1)S(1)}, u32[]{:S(2)}, u32[]{:S(2)}) collective-permute-start(bf16[1,2,2816]{2,1,0:T(2,128)(2,1)S(1)} %get-tuple-element.51), channel_id=1, source_target_pairs={{0,9},{1,8},{2,11},{3,10},{4,13},{5,12},{6,15},{7,14},{8,1},{9,0},... | collective-permute-start | bytes 33800 | tf_op jit(solution)/shard_map/ppermute | solution.py:25
  14.7 5.3 %collective-permute-start.5 = (f32[1,2,2816]{2,1,0:T(2,128)S(1)}, f32[1,2,2816]{2,1,0:T(2,128)S(1)}, u32[]{:S(2)}, u32[]{:S(2)}) collective-permute-start(f32[1,2,2816]{2,1,0:T(2,128)S(1)} %add_add_fusion.1), channel_id=1, source_target_pairs={{0,7},{1,6},{2,5},{3,4},{4,3},{5,2},{6,1},{7,0},{8,15},{9,14},{10,... | collective-permute-start | bytes 67592 | tf_op jit(solution)/shard_map/ppermute | solution.py:25
  17.2 3.2 %collective-permute-start.6 = (f32[1,2,2816]{2,1,0:T(2,128)S(1)}, f32[1,2,2816]{2,1,0:T(2,128)S(1)}, u32[]{:S(2)}, u32[]{:S(2)}) collective-permute-start(f32[1,2,2816]{2,1,0:T(2,128)S(1)} %add_add_fusion.1), channel_id=1, source_target_pairs={{0,5},{1,4},{2,7},{3,6},{4,1},{5,0},{6,3},{7,2},{8,13},{9,12},{10,... | collective-permute-start | bytes 67592 | tf_op jit(solution)/shard_map/ppermute | solution.py:25
  17.4 3.2 %collective-permute-start.4 = (f32[1,2,2816]{2,1,0:T(2,128)S(1)}, f32[1,2,2816]{2,1,0:T(2,128)S(1)}, u32[]{:S(2)}, u32[]{:S(2)}) collective-permute-start(f32[1,2,2816]{2,1,0:T(2,128)S(1)} %add_add_fusion.1), channel_id=1, source_target_pairs={{0,3},{1,2},{2,1},{3,0},{4,7},{5,6},{6,5},{7,4},{8,11},{9,10},{10,... | collective-permute-start | bytes 67592 | tf_op jit(solution)/shard_map/ppermute | solution.py:25
  22.2 11.5 %copy-start = (bf16[1,512,1280]{2,1,0:T(8,128)(2,1)S(1)}, bf16[1,512,1280]{2,1,0:T(8,128)(2,1)}, u32[]{:S(2)}) copy-start(bf16[1,512,1280]{2,1,0:T(8,128)(2,1)} %param.6) | copy-start | bytes 3932164
  22.2 11.5 %copy-start.1 = (bf16[1,512,1280]{2,1,0:T(8,128)(2,1)S(1)}, bf16[1,512,1280]{2,1,0:T(8,128)(2,1)}, u32[]{:S(2)}) copy-start(bf16[1,512,1280]{2,1,0:T(8,128)(2,1)} %param.7) | copy-start | bytes 3932164
  22.2 4.8 %collective-permute-start.8 = (f32[1,2,2816]{2,1,0:T(2,128)S(1)}, f32[1,2,2816]{2,1,0:T(2,128)S(1)}, u32[]{:S(2)}, u32[]{:S(2)}) collective-permute-start(f32[1,2,2816]{2,1,0:T(2,128)S(1)} %bitcast.42), channel_id=1, source_target_pairs={{0,7},{1,6},{2,5},{3,4},{4,3},{5,2},{6,1},{7,0},{8,15},{9,14},{10,... | collective-permute-start | bytes 67592 | tf_op jit(solution)/shard_map/ppermute | solution.py:25
  23.9 3.3 %collective-permute-start.9 = (f32[1,2,2816]{2,1,0:T(2,128)S(1)}, f32[1,2,2816]{2,1,0:T(2,128)S(1)}, u32[]{:S(2)}, u32[]{:S(2)}) collective-permute-start(f32[1,2,2816]{2,1,0:T(2,128)S(1)} %bitcast.43), channel_id=1, source_target_pairs={{0,5},{1,4},{2,7},{3,6},{4,1},{5,0},{6,3},{7,2},{8,13},{9,12},{10,... | collective-permute-start | bytes 67592 | tf_op jit(solution)/shard_map/ppermute | solution.py:25
  24.3 3.2 %collective-permute-start.7 = (f32[1,2,2816]{2,1,0:T(2,128)S(1)}, f32[1,2,2816]{2,1,0:T(2,128)S(1)}, u32[]{:S(2)}, u32[]{:S(2)}) collective-permute-start(f32[1,2,2816]{2,1,0:T(2,128)S(1)} %bitcast.44), channel_id=1, source_target_pairs={{0,3},{1,2},{2,1},{3,0},{4,7},{5,6},{6,5},{7,4},{8,11},{9,10},{10,... | collective-permute-start | bytes 67592 | tf_op jit(solution)/shard_map/ppermute | solution.py:25
  27.6 4.6 %collective-permute-start.12 = (bf16[1,2,2816]{2,1,0:T(2,128)(2,1)S(1)}, bf16[1,2,2816]{2,1,0:T(2,128)(2,1)S(1)}, u32[]{:S(2)}, u32[]{:S(2)}) collective-permute-start(bf16[1,2,2816]{2,1,0:T(2,128)(2,1)S(1)} %fusion.3), channel_id=1, source_target_pairs={{0,17},{1,16},{2,19},{3,18},{4,21},{5,20},{6,23},{7,22},{8,25},{9,... | collective-permute-start | bytes 33800 | tf_op jit(solution)/shard_map/ppermute | solution.py:25
  28.6 4.9 %collective-permute-start.11 = (bf16[1,2,2816]{2,1,0:T(2,128)(2,1)S(1)}, bf16[1,2,2816]{2,1,0:T(2,128)(2,1)S(1)}, u32[]{:S(2)}, u32[]{:S(2)}) collective-permute-start(bf16[1,2,2816]{2,1,0:T(2,128)(2,1)S(1)} %fusion.3), channel_id=1, source_target_pairs={{0,25},{1,24},{2,27},{3,26},{4,29},{5,28},{6,31},{7,30},{8,17},{9,... | collective-permute-start | bytes 33800 | tf_op jit(solution)/shard_map/ppermute | solution.py:25
  29.5 4.1 %collective-permute-start.10 = (bf16[1,2,2816]{2,1,0:T(2,128)(2,1)S(1)}, bf16[1,2,2816]{2,1,0:T(2,128)(2,1)S(1)}, u32[]{:S(2)}, u32[]{:S(2)}) collective-permute-start(bf16[1,2,2816]{2,1,0:T(2,128)(2,1)S(1)} %fusion.3), channel_id=1, source_target_pairs={{0,9},{1,8},{2,11},{3,10},{4,13},{5,12},{6,15},{7,14},{8,1},{9,0},... | collective-permute-start | bytes 33800 | tf_op jit(solution)/shard_map/ppermute | solution.py:25
  34.8 1.2 %collective-permute-start.13 = (f32[2,1280]{1,0:T(2,128)S(1)}, f32[2,1280]{1,0:T(2,128)S(1)}, u32[]{:S(2)}, u32[]{:S(2)}) collective-permute-start(f32[2,1280]{1,0:T(2,128)S(1)} %get-tuple-element.48), channel_id=1, source_target_pairs={{0,1},{1,0},{2,3},{3,2},{4,5},{5,4},{6,7},{7,6},{8,9},{9,8},{10,11... | collective-permute-start | bytes 30728 | tf_op jit(solution)/shard_map/ppermute | solution.py:29
  36.0 5.0 %collective-permute-start.15 = (f32[1,2,1280]{2,1,0:T(2,128)S(1)}, f32[1,2,1280]{2,1,0:T(2,128)S(1)}, u32[]{:S(2)}, u32[]{:S(2)}) collective-permute-start(f32[1,2,1280]{2,1,0:T(2,128)S(1)} %add_bitcast_fusion.3), channel_id=1, source_target_pairs={{0,7},{1,6},{2,5},{3,4},{4,3},{5,2},{6,1},{7,0},{8,15},{9,14},{10,... | collective-permute-start | bytes 30728 | tf_op jit(solution)/shard_map/ppermute | solution.py:25
  38.1 3.1 %collective-permute-start.16 = (f32[1,2,1280]{2,1,0:T(2,128)S(1)}, f32[1,2,1280]{2,1,0:T(2,128)S(1)}, u32[]{:S(2)}, u32[]{:S(2)}) collective-permute-start(f32[1,2,1280]{2,1,0:T(2,128)S(1)} %add_bitcast_fusion.3), channel_id=1, source_target_pairs={{0,5},{1,4},{2,7},{3,6},{4,1},{5,0},{6,3},{7,2},{8,13},{9,12},{10,... | collective-permute-start | bytes 30728 | tf_op jit(solution)/shard_map/ppermute | solution.py:25
  38.4 3.1 %collective-permute-start.14 = (f32[1,2,1280]{2,1,0:T(2,128)S(1)}, f32[1,2,1280]{2,1,0:T(2,128)S(1)}, u32[]{:S(2)}, u32[]{:S(2)}) collective-permute-start(f32[1,2,1280]{2,1,0:T(2,128)S(1)} %add_bitcast_fusion.3), channel_id=1, source_target_pairs={{0,3},{1,2},{2,1},{3,0},{4,7},{5,6},{6,5},{7,4},{8,11},{9,10},{10,... | collective-permute-start | bytes 30728 | tf_op jit(solution)/shard_map/ppermute | solution.py:25
  41.5 4.8 %collective-permute-start.17 = (f32[1,2,1280]{2,1,0:T(2,128)S(1)}, f32[1,2,1280]{2,1,0:T(2,128)S(1)}, u32[]{:S(2)}, u32[]{:S(2)}) collective-permute-start(f32[1,2,1280]{2,1,0:T(2,128)S(1)} %add_add_fusion.2.refs_0_), channel_id=1, source_target_pairs={{0,17},{1,16},{2,19},{3,18},{4,21},{5,20},{6,23},{7,22},{8,25},{9,... | collective-permute-start | bytes 30728 | tf_op jit(solution)/shard_map/ppermute | solution.py:25
  42.3 4.9 %collective-permute-start.18 = (f32[1,2,1280]{2,1,0:T(2,128)S(1)}, f32[1,2,1280]{2,1,0:T(2,128)S(1)}, u32[]{:S(2)}, u32[]{:S(2)}) collective-permute-start(f32[1,2,1280]{2,1,0:T(2,128)S(1)} %add_add_fusion.2.refs_0_), channel_id=1, source_target_pairs={{0,25},{1,24},{2,27},{3,26},{4,29},{5,28},{6,31},{7,30},{8,17},{9,... | collective-permute-start | bytes 30728 | tf_op jit(solution)/shard_map/ppermute | solution.py:25
  44.1 3.2 %collective-permute-start.19 = (f32[1,2,1280]{2,1,0:T(2,128)S(1)}, f32[1,2,1280]{2,1,0:T(2,128)S(1)}, u32[]{:S(2)}, u32[]{:S(2)}) collective-permute-start(f32[1,2,1280]{2,1,0:T(2,128)S(1)} %add_add_fusion.2.refs_0_), channel_id=1, source_target_pairs={{0,9},{1,8},{2,11},{3,10},{4,13},{5,12},{6,15},{7,14},{8,1},{9,0},... | collective-permute-start | bytes 30728 | tf_op jit(solution)/shard_map/ppermute | solution.py:25

commit v15 on v14

--- a/solution.py
+++ b/solution.py
@@ -131,8 +131,10 @@
     ]
     for copy in tok_copies + [phi_copy] + cot_copies:
         copy.start()
-    for copy, piece in zip(tok_copies, pieces):
-        copy.wait()
+    for index in range(0, blocks, 2):
+        for copy in tok_copies[index : index + 2]:
+            copy.wait()
+        piece = pl.ds(index * rows, 2 * rows)
         tok_f32 = tok_buf[piece, :].astype(f32)
         tok_scale = lax.rsqrt(jnp.sum(tok_f32 * tok_f32, axis=1, keepdims=True) + epsilon)
         norm_ref[piece, :] = (tok_f32 * tok_scale).astype(bf16)
@@ -283,7 +285,7 @@
             pltpu.VMEM((count, width), bf16),
             pltpu.VMEM((count, width), bf16),
             pltpu.SemaphoreType.DMA,
-            pltpu.SemaphoreType.DMA((2, 2 * PIECES)),
+            pltpu.SemaphoreType.DMA((2, PIECES)),
         ],
         compiler_params=params,
         name="token_sums",

time: 48.3 us -> 47.8 us (0.990)
  no operation moved by 1% of the time
where the time goes in v15:
time: 47.8 us; the launch traced here: 47.6 us
  starting transfers between devices  21.7 us (45%)
  waiting for transfers between devices  8.15 us (17%)
  Pallas kernels  8.05 us (17%)
  matrix products  7.52 us (16%)
  between operations  1.47 us (3%)
  other arithmetic  0.62 us (1%)
    ppermute x18, starting transfers between devices, exchange(): return lax.ppermute(value, AXES, pairs)  21 us
    ppermute x18, waiting for transfers between devices, exchange(): return lax.ppermute(value, AXES, pairs)  7.22 us
    pallas_call x1, Pallas kernels, per_device(): pl.pallas_call(token_sums, in_specs=[scalar, in_hbm, in_hbm, in_hbm], out...  2.71 us
    dot_general x1, matrix products, per_device(): jnp.einsum('sn,sd->nd', dispatch, slot_dx, preferred_element_type=f32)  1.98 us
    pallas_call x1, Pallas kernels, per_device(): pl.pallas_call(fetch, in_specs=[in_hbm] * 2, out_specs=[in_vmem] * 2, out...  1.94 us
    dot_general x1, matrix products, per_device(): jnp.einsum('sn,sd->nd', combine, slot_y, preferred_element_type=f32)  1.61 us
    dot_general x1, matrix products, per_device(): jnp.einsum('oh,od->hd', hidden, mine_cot, preferred_element_type=f32)  1.59 us
    dot_general x1, matrix products, per_device(): jnp.einsum('od,oh->dh', mine_x, pre_grad, preferred_element_type=f32)  1.59 us
  transfers between devices with their start and end apart: 20, of which 11 were waited for; matrix products, arithmetic and copies ran while one was open for 16% of the time, Pallas kernels for 4%

profile of v15, /device:TPU:0, one launch (start us, length us, event | category | flops | bytes accessed | tf_op | source)
XLA Modules:
  0.0 47.6 jit_solution(3981732312879347711)
XLA Ops:
  1.3 2.7 %token_sums.1 = (bf16[2,2816]{1,0:T(2,128)(2,1)S(1)}, f32[2,512]{1,0:T(2,128)S(1)}, bf16[2,512]{1,0:T(2,128)(2,1)S(1)}, f32[512,1]{1,0:T(8,128)S(1)}, bf16[512,1280]{1,0:T(8,128)(2,1)S(1)}) custom-call(f32[1]{0:T(128)S(6)} %copy.11.scale_ref, bf16[2,1280]{1,0:T(2,128)(2,1)} %bitcast.40, bf16[512,1280]{1,0:T(8,128)(2,1)} %bitcast.36, bf16[512,1280]{1,0:T(8,128)(2,1)} %bitcast.38), custom_call_target="tpu_custom_call" | custom-call | tf_op jit(solution)/shard_map/token_sums/pallas_call | solution.py:273
  4.0 0.5 %collective-permute-start = (bf16[2,2816]{1,0:T(2,128)(2,1)S(1)}, bf16[2,2816]{1,0:T(2,128)(2,1)S(1)}, u32[]{:S(2)}, u32[]{:S(2)}) collective-permute-start(bf16[2,2816]{1,0:T(2,128)(2,1)S(1)} %get-tuple-element.28), channel_id=1, source_target_pairs={{0,1},{1,0},{2,3},{3,2},{4,5},{5,4},{6,7},{7,6},{8,9},{9,8},{10,11... | collective-permute-start | bytes 33800 | tf_op jit(solution)/shard_map/ppermute | solution.py:29
  4.5 0.1 fusion.4
  4.7 0.7 %collective-permute-done = bf16[2,2816]{1,0:T(2,128)(2,1)S(1)} collective-permute-done((bf16[2,2816]{1,0:T(2,128)(2,1)S(1)}, bf16[2,2816]{1,0:T(2,128)(2,1)S(1)}, u32[]{:S(2)}, u32[]{:S(2)}) %collective-permute-start) | collective-permute-done | bytes 11296 | tf_op jit(solution)/shard_map/ppermute | solution.py:29
  5.4 0.1 broadcast_select_fusion
  5.5 3.8 %collective-permute-start.3 = (bf16[1,2,2816]{2,1,0:T(2,128)(2,1)S(1)}, bf16[1,2,2816]{2,1,0:T(2,128)(2,1)S(1)}, u32[]{:S(2)}, u32[]{:S(2)}) collective-permute-start(bf16[1,2,2816]{2,1,0:T(2,128)(2,1)S(1)} %get-tuple-element.52), channel_id=1, source_target_pairs={{0,17},{1,16},{2,19},{3,18},{4,21},{5,20},{6,23},{7,22},{8,25},{9,... | collective-permute-start | bytes 33800 | tf_op jit(solution)/shard_map/ppermute | solution.py:25
  9.3 1.3 %collective-permute-start.2 = (bf16[1,2,2816]{2,1,0:T(2,128)(2,1)S(1)}, bf16[1,2,2816]{2,1,0:T(2,128)(2,1)S(1)}, u32[]{:S(2)}, u32[]{:S(2)}) collective-permute-start(bf16[1,2,2816]{2,1,0:T(2,128)(2,1)S(1)} %get-tuple-element.53), channel_id=1, source_target_pairs={{0,25},{1,24},{2,27},{3,26},{4,29},{5,28},{6,31},{7,30},{8,17},{9,... | collective-permute-start | bytes 33800 | tf_op jit(solution)/shard_map/ppermute | solution.py:25
  10.6 0.2 collective-permute-start.1
  10.8 0.0 collective-permute-done.3
  10.8 3.4 %collective-permute-done.2 = bf16[1,2,2816]{2,1,0:T(2,128)(2,1)S(1)} collective-permute-done((bf16[1,2,2816]{2,1,0:T(2,128)(2,1)S(1)}, bf16[1,2,2816]{2,1,0:T(2,128)(2,1)S(1)}, u32[]{:S(2)}, u32[]{:S(2)}) %collective-permute-start.2) | collective-permute-done | bytes 11296 | tf_op jit(solution)/shard_map/ppermute | solution.py:25
  14.2 0.0 collective-permute-done.1
  14.2 2.5 %collective-permute-start.5 = (f32[1,2,2816]{2,1,0:T(2,128)S(1)}, f32[1,2,2816]{2,1,0:T(2,128)S(1)}, u32[]{:S(2)}, u32[]{:S(2)}) collective-permute-start(f32[1,2,2816]{2,1,0:T(2,128)S(1)} %add_add_fusion.1), channel_id=1, source_target_pairs={{0,7},{1,6},{2,5},{3,4},{4,3},{5,2},{6,1},{7,0},{8,15},{9,14},{10,... | collective-permute-start | bytes 67592 | tf_op jit(solution)/shard_map/ppermute | solution.py:25
  16.7 0.3 collective-permute-start.6
  17.0 0.5 %collective-permute-start.4 = (f32[1,2,2816]{2,1,0:T(2,128)S(1)}, f32[1,2,2816]{2,1,0:T(2,128)S(1)}, u32[]{:S(2)}, u32[]{:S(2)}) collective-permute-start(f32[1,2,2816]{2,1,0:T(2,128)S(1)} %add_add_fusion.1), channel_id=1, source_target_pairs={{0,3},{1,2},{2,1},{3,0},{4,7},{5,6},{6,5},{7,4},{8,11},{9,10},{10,... | collective-permute-start | bytes 67592 | tf_op jit(solution)/shard_map/ppermute | solution.py:25
  17.5 0.1 reduce
  17.6 1.9 %fetch_weights.1 = (bf16[1280,640]{1,0:T(8,128)(2,1)S(1)}, bf16[640,1280]{1,0:T(8,128)(2,1)S(1)}) custom-call(bf16[1280,640]{1,0:T(8,128)(2,1)} %in_ref, bf16[640,1280]{1,0:T(8,128)(2,1)} %out_ref), custom_call_target="tpu_custom_call" | custom-call | bytes 6553600 | tf_op jit(solution)/shard_map/fetch_weights/pallas_call | solution.py:295
  19.6 0.0 collective-permute-done.5
  19.6 0.4 collective-permute-done.6
  19.9 0.3 collective-permute-done.4
  20.2 1.5 %expert_rows.1 = (f32[2,2816]{1,0:T(2,128)S(1)}, f32[2,128]{1,0:T(2,128)S(1)}, bf16[2,1280]{1,0:T(2,128)(2,1)S(1)}, bf16[2,1280]{1,0:T(2,128)(2,1)S(1)}, bf16[2,...) custom-call(s32[1]{0:T(128)} %bitcast.3.owned_ref, f32[2,2816]{1,0:T(2,128)S(1)} %add_bitcast_fusion.2.sums_ref, ...), custom_call_target="tpu_custom_call" | custom-call | tf_op jit(solution)/shard_map/expert_rows/pallas_call | solution.py:311
  21.8 1.6 %collective-permute-start.8 = (f32[1,2,2816]{2,1,0:T(2,128)S(1)}, f32[1,2,2816]{2,1,0:T(2,128)S(1)}, u32[]{:S(2)}, u32[]{:S(2)}) collective-permute-start(f32[1,2,2816]{2,1,0:T(2,128)S(1)} %bitcast.42), channel_id=1, source_target_pairs={{0,7},{1,6},{2,5},{3,4},{4,3},{5,2},{6,1},{7,0},{8,15},{9,14},{10,... | collective-permute-start | bytes 67592 | tf_op jit(solution)/shard_map/ppermute | solution.py:25
  23.4 0.5 collective-permute-start.9
  23.8 1.1 %collective-permute-start.7 = (f32[1,2,2816]{2,1,0:T(2,128)S(1)}, f32[1,2,2816]{2,1,0:T(2,128)S(1)}, u32[]{:S(2)}, u32[]{:S(2)}) collective-permute-start(f32[1,2,2816]{2,1,0:T(2,128)S(1)} %bitcast.44), channel_id=1, source_target_pairs={{0,3},{1,2},{2,1},{3,0},{4,7},{5,6},{6,5},{7,4},{8,11},{9,10},{10,... | collective-permute-start | bytes 67592 | tf_op jit(solution)/shard_map/ppermute | solution.py:25
  24.9 1.6 %fusion.12 = f32[640,640]{1,0:T(8,128)} fusion(bf16[2,640]{1,0:T(2,128)(2,1)S(1)} %get-tuple-element.45, bf16[2,1280]{1,0:T(2,128)(2,1)S(1)} %get-tuple-element.44, s32[]{:T(128)S(6)} %select_n.68), kind=kOutput, calls=%fused_computation.28 | convolution fusion | flops 1638400 | bytes 1643524 | tf_op jit(solution)/shard_map/od,oh->dh/dot_general | solution.py:331
  26.5 0.1 collective-permute-done.9
  26.7 0.4 collective-permute-done.7
  27.1 1.0 %collective-permute-start.12 = (bf16[1,2,2816]{2,1,0:T(2,128)(2,1)S(1)}, bf16[1,2,2816]{2,1,0:T(2,128)(2,1)S(1)}, u32[]{:S(2)}, u32[]{:S(2)}) collective-permute-start(bf16[1,2,2816]{2,1,0:T(2,128)(2,1)S(1)} %fusion.3), channel_id=1, source_target_pairs={{0,17},{1,16},{2,19},{3,18},{4,21},{5,20},{6,23},{7,22},{8,25},{9,... | collective-permute-start | bytes 33800 | tf_op jit(solution)/shard_map/ppermute | solution.py:25
  28.2 0.9 %collective-permute-start.11 = (bf16[1,2,2816]{2,1,0:T(2,128)(2,1)S(1)}, bf16[1,2,2816]{2,1,0:T(2,128)(2,1)S(1)}, u32[]{:S(2)}, u32[]{:S(2)}) collective-permute-start(bf16[1,2,2816]{2,1,0:T(2,128)(2,1)S(1)} %fusion.3), channel_id=1, source_target_pairs={{0,25},{1,24},{2,27},{3,26},{4,29},{5,28},{6,31},{7,30},{8,17},{9,... | collective-permute-start | bytes 33800 | tf_op jit(solution)/shard_map/ppermute | solution.py:25
  29.0 1.1 %collective-permute-start.10 = (bf16[1,2,2816]{2,1,0:T(2,128)(2,1)S(1)}, bf16[1,2,2816]{2,1,0:T(2,128)(2,1)S(1)}, u32[]{:S(2)}, u32[]{:S(2)}) collective-permute-start(bf16[1,2,2816]{2,1,0:T(2,128)(2,1)S(1)} %fusion.3), channel_id=1, source_target_pairs={{0,9},{1,8},{2,11},{3,10},{4,13},{5,12},{6,15},{7,14},{8,1},{9,0},... | collective-permute-start | bytes 33800 | tf_op jit(solution)/shard_map/ppermute | solution.py:25
  30.2 1.6 %fusion.10 = f32[640,640]{1,0:T(8,128)} fusion(bf16[2,640]{1,0:T(2,128)(2,1)S(1)} %get-tuple-element.46, bf16[2,1280]{1,0:T(2,128)(2,1)S(1)} %get-tuple-element.47, s32[]{:T(128)S(6)} %select_n.68), kind=kOutput, calls=%fused_computation.26 | convolution fusion | flops 1638400 | bytes 1643524 | tf_op jit(solution)/shard_map/oh,od->hd/dot_general | solution.py:332
  31.8 1.3 %collective-permute-done.11 = bf16[1,2,2816]{2,1,0:T(2,128)(2,1)S(1)} collective-permute-done((bf16[1,2,2816]{2,1,0:T(2,128)(2,1)S(1)}, bf16[1,2,2816]{2,1,0:T(2,128)(2,1)S(1)}, u32[]{:S(2)}, u32[]{:S(2)}) %collective-permute-start.11) | collective-permute-done | bytes 11296 | tf_op jit(solution)/shard_map/ppermute | solution.py:25
  33.2 0.1 fusion.17
  33.3 1.1 %score_grads.1 = (bf16[2,512]{1,0:T(2,128)(2,1)S(1)}, bf16[2,512]{1,0:T(2,128)(2,1)S(1)}, f32[2,1280]{1,0:T(2,128)S(1)}) custom-call(f32[1]{0:T(128)S(6)} %copy.11.scale_ref, f32[2,2816]{1,0:T(2,128)S(1)} %get-tuple-element.50.slots_ref, f32[1,128]{1,0:T(1,128)S(1)} %constant_dynamic-slice_fusion.1.totals_ref, bf16[512,1280]{1,0:T(8,128)(2,1)S(1)} %bitcast.37, ...), custom_call_target="tpu_custom_call" | custom-call | tf_op jit(solution)/shard_map/score_grads/pallas_call | solution.py:333
  34.3 0.2 collective-permute-start.13
  34.5 0.7 %multiply_reduce_fusion = (f32[512]{0:T(512)S(1)}, f32[512,1280]{1,0:T(8,128)S(1)}) fusion(f32[512]{0:T(512)S(1)} %reduce, bf16[1,512,1280]{2,1,0:T(8,128)(2,1)S(1)} %copy-done, bf16[2,512]{1,0:T(2,128)(2,1)S(1)} %get-tuple-element.43, f32[2]{0:T(128)S(1)} %add_rsqrt_fusion, bf16[1280,2]{0,1:T(2,128)(2,1)S(1)} %copy-done.2), kind=kOutput, calls=%fused_computation.5 | convolution fusion | flops 5250048 | bytes 3943432 | tf_op jit(solution)/shard_map/sn,sd->nd/dot_general | solution.py:366
  35.3 0.3 collective-permute-done.13
  35.5 2.1 %collective-permute-start.15 = (f32[1,2,1280]{2,1,0:T(2,128)S(1)}, f32[1,2,1280]{2,1,0:T(2,128)S(1)}, u32[]{:S(2)}, u32[]{:S(2)}) collective-permute-start(f32[1,2,1280]{2,1,0:T(2,128)S(1)} %add_bitcast_fusion.3), channel_id=1, source_target_pairs={{0,7},{1,6},{2,5},{3,4},{4,3},{5,2},{6,1},{7,0},{8,15},{9,14},{10,... | collective-permute-start | bytes 30728 | tf_op jit(solution)/shard_map/ppermute | solution.py:25
  37.7 0.3 collective-permute-start.16
  37.9 0.7 %collective-permute-start.14 = (f32[1,2,1280]{2,1,0:T(2,128)S(1)}, f32[1,2,1280]{2,1,0:T(2,128)S(1)}, u32[]{:S(2)}, u32[]{:S(2)}) collective-permute-start(f32[1,2,1280]{2,1,0:T(2,128)S(1)} %add_bitcast_fusion.3), channel_id=1, source_target_pairs={{0,3},{1,2},{2,1},{3,0},{4,7},{5,6},{6,5},{7,4},{8,11},{9,10},{10,... | collective-permute-start | bytes 30728 | tf_op jit(solution)/shard_map/ppermute | solution.py:25
  38.6 2.0 %fusion.1 = bf16[1,512,1280]{2,1,0:T(8,128)(2,1)} fusion(bf16[2,512]{1,0:T(2,128)(2,1)S(1)} %get-tuple-element.41, f32[512,1280]{1,0:T(8,128)S(1)} %get-tuple-element.55, f32[512]{0:T(512)S(1)} %get-tuple-element.54, f32[512]{0:T(512)S(1)} %reduce, bf16[2,2816]{1,0:T(2,128)(2,1)S(1)} %get-tuple-element.49, bf16[1,512,1280]{2,1,0:T(8,128)(2,1)S(1)} %copy-done), kind=kOutput, calls=%fused_computation.3 | convolution fusion | flops 7208960 | bytes 5254144 | tf_op jit(solution)/shard_map/sn,sd->nd/dot_general | solution.py:367
  40.6 0.2 collective-permute-done.16
  40.7 0.3 collective-permute-done.14
  41.0 0.8 %collective-permute-start.17 = (f32[1,2,1280]{2,1,0:T(2,128)S(1)}, f32[1,2,1280]{2,1,0:T(2,128)S(1)}, u32[]{:S(2)}, u32[]{:S(2)}) collective-permute-start(f32[1,2,1280]{2,1,0:T(2,128)S(1)} %add_add_fusion.2.refs_0_), channel_id=1, source_target_pairs={{0,17},{1,16},{2,19},{3,18},{4,21},{5,20},{6,23},{7,22},{8,25},{9,... | collective-permute-start | bytes 30728 | tf_op jit(solution)/shard_map/ppermute | solution.py:25
  41.9 1.7 %collective-permute-start.18 = (f32[1,2,1280]{2,1,0:T(2,128)S(1)}, f32[1,2,1280]{2,1,0:T(2,128)S(1)}, u32[]{:S(2)}, u32[]{:S(2)}) collective-permute-start(f32[1,2,1280]{2,1,0:T(2,128)S(1)} %add_add_fusion.2.refs_0_), channel_id=1, source_target_pairs={{0,25},{1,24},{2,27},{3,26},{4,29},{5,28},{6,31},{7,30},{8,17},{9,... | collective-permute-start | bytes 30728 | tf_op jit(solution)/shard_map/ppermute | solution.py:25
  43.6 0.7 %collective-permute-start.19 = (f32[1,2,1280]{2,1,0:T(2,128)S(1)}, f32[1,2,1280]{2,1,0:T(2,128)S(1)}, u32[]{:S(2)}, u32[]{:S(2)}) collective-permute-start(f32[1,2,1280]{2,1,0:T(2,128)S(1)} %add_add_fusion.2.refs_0_), channel_id=1, source_target_pairs={{0,9},{1,8},{2,11},{3,10},{4,13},{5,12},{6,15},{7,14},{8,1},{9,0},... | collective-permute-start | bytes 30728 | tf_op jit(solution)/shard_map/ppermute | solution.py:25
  44.3 1.6 %fusion.2 = bf16[1,512,1280]{2,1,0:T(8,128)(2,1)} fusion(bf16[2,512]{1,0:T(2,128)(2,1)S(1)} %get-tuple-element.27, bf16[2,2816]{1,0:T(2,128)(2,1)S(1)} %get-tuple-element.49), kind=kOutput, calls=%fused_computation.4 | convolution fusion | flops 3276800 | bytes 1317888 | tf_op jit(solution)/shard_map/sn,sd->nd/dot_general | solution.py:365
  45.9 0.9 %collective-permute-done.18.refs_2_ = f32[1,2,1280]{2,1,0:T(2,128)S(1)} collective-permute-done((f32[1,2,1280]{2,1,0:T(2,128)S(1)}, f32[1,2,1280]{2,1,0:T(2,128)S(1)}, u32[]{:S(2)}, u32[]{:S(2)}) %collective-permute-start.18) | collective-permute-done | bytes 10272 | tf_op jit(solution)/shard_map/ppermute | solution.py:25
  46.8 0.8 %finish.1 = f32[2,1280]{1,0:T(2,128)} custom-call(bf16[2,1280]{1,0:T(2,128)(2,1)S(1)} %bitcast.41, f32[1,2,1280]{2,1,0:T(2,128)S(1)} %add_add_fusion.2.refs_0_, f32[1,2,1280]{2,1,0:T(2,128)S(1)} %collective-permute-done.17.refs_1_, f32[1,2,1280]{2,1,0:T(2,128)S(1)} %collective-permute-done.18.refs_2_, f32[1,2,1280]{2,1,0:T(2,128)S(1)} %collective-permute-done.19.refs_3_), custom_call_target="tpu_custom_call" | custom-call | tf_op jit(solution)/shard_map/finish/pallas_call | solution.py:352
  (28 shorter events, 0.3 us)
Async XLA Ops:
  0.6 3.9 %copy-start.2 = (bf16[1280,2]{0,1:T(2,128)(2,1)S(1)}, bf16[1280,2]{0,1:T(2,128)(2,1)}, u32[]{:S(2)}) copy-start(bf16[1280,2]{0,1:T(2,128)(2,1)} %param.8) | copy-start | bytes 15364
  4.0 1.4 %collective-permute-start = (bf16[2,2816]{1,0:T(2,128)(2,1)S(1)}, bf16[2,2816]{1,0:T(2,128)(2,1)S(1)}, u32[]{:S(2)}, u32[]{:S(2)}) collective-permute-start(bf16[2,2816]{1,0:T(2,128)(2,1)S(1)} %get-tuple-element.28), channel_id=1, source_target_pairs={{0,1},{1,0},{2,3},{3,2},{4,5},{5,4},{6,7},{7,6},{8,9},{9,8},{10,11... | collective-permute-start | bytes 33800 | tf_op jit(solution)/shard_map/ppermute | solution.py:29
  5.5 5.3 %collective-permute-start.3 = (bf16[1,2,2816]{2,1,0:T(2,128)(2,1)S(1)}, bf16[1,2,2816]{2,1,0:T(2,128)(2,1)S(1)}, u32[]{:S(2)}, u32[]{:S(2)}) collective-permute-start(bf16[1,2,2816]{2,1,0:T(2,128)(2,1)S(1)} %get-tuple-element.52), channel_id=1, source_target_pairs={{0,17},{1,16},{2,19},{3,18},{4,21},{5,20},{6,23},{7,22},{8,25},{9,... | collective-permute-start | bytes 33800 | tf_op jit(solution)/shard_map/ppermute | solution.py:25
  9.3 4.9 %collective-permute-start.2 = (bf16[1,2,2816]{2,1,0:T(2,128)(2,1)S(1)}, bf16[1,2,2816]{2,1,0:T(2,128)(2,1)S(1)}, u32[]{:S(2)}, u32[]{:S(2)}) collective-permute-start(bf16[1,2,2816]{2,1,0:T(2,128)(2,1)S(1)} %get-tuple-element.53), channel_id=1, source_target_pairs={{0,25},{1,24},{2,27},{3,26},{4,29},{5,28},{6,31},{7,30},{8,17},{9,... | collective-permute-start | bytes 33800 | tf_op jit(solution)/shard_map/ppermute | solution.py:25
  10.6 3.6 %collective-permute-start.1 = (bf16[1,2,2816]{2,1,0:T(2,128)(2,1)S(1)}, bf16[1,2,2816]{2,1,0:T(2,128)(2,1)S(1)}, u32[]{:S(2)}, u32[]{:S(2)}) collective-permute-start(bf16[1,2,2816]{2,1,0:T(2,128)(2,1)S(1)} %get-tuple-element.51), channel_id=1, source_target_pairs={{0,9},{1,8},{2,11},{3,10},{4,13},{5,12},{6,15},{7,14},{8,1},{9,0},... | collective-permute-start | bytes 33800 | tf_op jit(solution)/shard_map/ppermute | solution.py:25
  14.2 5.3 %collective-permute-start.5 = (f32[1,2,2816]{2,1,0:T(2,128)S(1)}, f32[1,2,2816]{2,1,0:T(2,128)S(1)}, u32[]{:S(2)}, u32[]{:S(2)}) collective-permute-start(f32[1,2,2816]{2,1,0:T(2,128)S(1)} %add_add_fusion.1), channel_id=1, source_target_pairs={{0,7},{1,6},{2,5},{3,4},{4,3},{5,2},{6,1},{7,0},{8,15},{9,14},{10,... | collective-permute-start | bytes 67592 | tf_op jit(solution)/shard_map/ppermute | solution.py:25
  16.7 3.2 %collective-permute-start.6 = (f32[1,2,2816]{2,1,0:T(2,128)S(1)}, f32[1,2,2816]{2,1,0:T(2,128)S(1)}, u32[]{:S(2)}, u32[]{:S(2)}) collective-permute-start(f32[1,2,2816]{2,1,0:T(2,128)S(1)} %add_add_fusion.1), channel_id=1, source_target_pairs={{0,5},{1,4},{2,7},{3,6},{4,1},{5,0},{6,3},{7,2},{8,13},{9,12},{10,... | collective-permute-start | bytes 67592 | tf_op jit(solution)/shard_map/ppermute | solution.py:25
  17.0 3.2 %collective-permute-start.4 = (f32[1,2,2816]{2,1,0:T(2,128)S(1)}, f32[1,2,2816]{2,1,0:T(2,128)S(1)}, u32[]{:S(2)}, u32[]{:S(2)}) collective-permute-start(f32[1,2,2816]{2,1,0:T(2,128)S(1)} %add_add_fusion.1), channel_id=1, source_target_pairs={{0,3},{1,2},{2,1},{3,0},{4,7},{5,6},{6,5},{7,4},{8,11},{9,10},{10,... | collective-permute-start | bytes 67592 | tf_op jit(solution)/shard_map/ppermute | solution.py:25
  21.8 11.5 %copy-start = (bf16[1,512,1280]{2,1,0:T(8,128)(2,1)S(1)}, bf16[1,512,1280]{2,1,0:T(8,128)(2,1)}, u32[]{:S(2)}) copy-start(bf16[1,512,1280]{2,1,0:T(8,128)(2,1)} %param.6) | copy-start | bytes 3932164
  21.8 11.5 %copy-start.1 = (bf16[1,512,1280]{2,1,0:T(8,128)(2,1)S(1)}, bf16[1,512,1280]{2,1,0:T(8,128)(2,1)}, u32[]{:S(2)}) copy-start(bf16[1,512,1280]{2,1,0:T(8,128)(2,1)} %param.7) | copy-start | bytes 3932164
  21.8 4.8 %collective-permute-start.8 = (f32[1,2,2816]{2,1,0:T(2,128)S(1)}, f32[1,2,2816]{2,1,0:T(2,128)S(1)}, u32[]{:S(2)}, u32[]{:S(2)}) collective-permute-start(f32[1,2,2816]{2,1,0:T(2,128)S(1)} %bitcast.42), channel_id=1, source_target_pairs={{0,7},{1,6},{2,5},{3,4},{4,3},{5,2},{6,1},{7,0},{8,15},{9,14},{10,... | collective-permute-start | bytes 67592 | tf_op jit(solution)/shard_map/ppermute | solution.py:25
  23.4 3.3 %collective-permute-start.9 = (f32[1,2,2816]{2,1,0:T(2,128)S(1)}, f32[1,2,2816]{2,1,0:T(2,128)S(1)}, u32[]{:S(2)}, u32[]{:S(2)}) collective-permute-start(f32[1,2,2816]{2,1,0:T(2,128)S(1)} %bitcast.43), channel_id=1, source_target_pairs={{0,5},{1,4},{2,7},{3,6},{4,1},{5,0},{6,3},{7,2},{8,13},{9,12},{10,... | collective-permute-start | bytes 67592 | tf_op jit(solution)/shard_map/ppermute | solution.py:25
  23.8 3.2 %collective-permute-start.7 = (f32[1,2,2816]{2,1,0:T(2,128)S(1)}, f32[1,2,2816]{2,1,0:T(2,128)S(1)}, u32[]{:S(2)}, u32[]{:S(2)}) collective-permute-start(f32[1,2,2816]{2,1,0:T(2,128)S(1)} %bitcast.44), channel_id=1, source_target_pairs={{0,3},{1,2},{2,1},{3,0},{4,7},{5,6},{6,5},{7,4},{8,11},{9,10},{10,... | collective-permute-start | bytes 67592 | tf_op jit(solution)/shard_map/ppermute | solution.py:25
  27.1 4.6 %collective-permute-start.12 = (bf16[1,2,2816]{2,1,0:T(2,128)(2,1)S(1)}, bf16[1,2,2816]{2,1,0:T(2,128)(2,1)S(1)}, u32[]{:S(2)}, u32[]{:S(2)}) collective-permute-start(bf16[1,2,2816]{2,1,0:T(2,128)(2,1)S(1)} %fusion.3), channel_id=1, source_target_pairs={{0,17},{1,16},{2,19},{3,18},{4,21},{5,20},{6,23},{7,22},{8,25},{9,... | collective-permute-start | bytes 33800 | tf_op jit(solution)/shard_map/ppermute | solution.py:25
  28.2 4.9 %collective-permute-start.11 = (bf16[1,2,2816]{2,1,0:T(2,128)(2,1)S(1)}, bf16[1,2,2816]{2,1,0:T(2,128)(2,1)S(1)}, u32[]{:S(2)}, u32[]{:S(2)}) collective-permute-start(bf16[1,2,2816]{2,1,0:T(2,128)(2,1)S(1)} %fusion.3), channel_id=1, source_target_pairs={{0,25},{1,24},{2,27},{3,26},{4,29},{5,28},{6,31},{7,30},{8,17},{9,... | collective-permute-start | bytes 33800 | tf_op jit(solution)/shard_map/ppermute | solution.py:25
  29.0 4.1 %collective-permute-start.10 = (bf16[1,2,2816]{2,1,0:T(2,128)(2,1)S(1)}, bf16[1,2,2816]{2,1,0:T(2,128)(2,1)S(1)}, u32[]{:S(2)}, u32[]{:S(2)}) collective-permute-start(bf16[1,2,2816]{2,1,0:T(2,128)(2,1)S(1)} %fusion.3), channel_id=1, source_target_pairs={{0,9},{1,8},{2,11},{3,10},{4,13},{5,12},{6,15},{7,14},{8,1},{9,0},... | collective-permute-start | bytes 33800 | tf_op jit(solution)/shard_map/ppermute | solution.py:25
  34.3 1.2 %collective-permute-start.13 = (f32[2,1280]{1,0:T(2,128)S(1)}, f32[2,1280]{1,0:T(2,128)S(1)}, u32[]{:S(2)}, u32[]{:S(2)}) collective-permute-start(f32[2,1280]{1,0:T(2,128)S(1)} %get-tuple-element.48), channel_id=1, source_target_pairs={{0,1},{1,0},{2,3},{3,2},{4,5},{5,4},{6,7},{7,6},{8,9},{9,8},{10,11... | collective-permute-start | bytes 30728 | tf_op jit(solution)/shard_map/ppermute | solution.py:29
  35.5 5.0 %collective-permute-start.15 = (f32[1,2,1280]{2,1,0:T(2,128)S(1)}, f32[1,2,1280]{2,1,0:T(2,128)S(1)}, u32[]{:S(2)}, u32[]{:S(2)}) collective-permute-start(f32[1,2,1280]{2,1,0:T(2,128)S(1)} %add_bitcast_fusion.3), channel_id=1, source_target_pairs={{0,7},{1,6},{2,5},{3,4},{4,3},{5,2},{6,1},{7,0},{8,15},{9,14},{10,... | collective-permute-start | bytes 30728 | tf_op jit(solution)/shard_map/ppermute | solution.py:25
  37.7 3.1 %collective-permute-start.16 = (f32[1,2,1280]{2,1,0:T(2,128)S(1)}, f32[1,2,1280]{2,1,0:T(2,128)S(1)}, u32[]{:S(2)}, u32[]{:S(2)}) collective-permute-start(f32[1,2,1280]{2,1,0:T(2,128)S(1)} %add_bitcast_fusion.3), channel_id=1, source_target_pairs={{0,5},{1,4},{2,7},{3,6},{4,1},{5,0},{6,3},{7,2},{8,13},{9,12},{10,... | collective-permute-start | bytes 30728 | tf_op jit(solution)/shard_map/ppermute | solution.py:25
  37.9 3.1 %collective-permute-start.14 = (f32[1,2,1280]{2,1,0:T(2,128)S(1)}, f32[1,2,1280]{2,1,0:T(2,128)S(1)}, u32[]{:S(2)}, u32[]{:S(2)}) collective-permute-start(f32[1,2,1280]{2,1,0:T(2,128)S(1)} %add_bitcast_fusion.3), channel_id=1, source_target_pairs={{0,3},{1,2},{2,1},{3,0},{4,7},{5,6},{6,5},{7,4},{8,11},{9,10},{10,... | collective-permute-start | bytes 30728 | tf_op jit(solution)/shard_map/ppermute | solution.py:25
  41.0 4.8 %collective-permute-start.17 = (f32[1,2,1280]{2,1,0:T(2,128)S(1)}, f32[1,2,1280]{2,1,0:T(2,128)S(1)}, u32[]{:S(2)}, u32[]{:S(2)}) collective-permute-start(f32[1,2,1280]{2,1,0:T(2,128)S(1)} %add_add_fusion.2.refs_0_), channel_id=1, source_target_pairs={{0,17},{1,16},{2,19},{3,18},{4,21},{5,20},{6,23},{7,22},{8,25},{9,... | collective-permute-start | bytes 30728 | tf_op jit(solution)/shard_map/ppermute | solution.py:25
  41.9 4.9 %collective-permute-start.18 = (f32[1,2,1280]{2,1,0:T(2,128)S(1)}, f32[1,2,1280]{2,1,0:T(2,128)S(1)}, u32[]{:S(2)}, u32[]{:S(2)}) collective-permute-start(f32[1,2,1280]{2,1,0:T(2,128)S(1)} %add_add_fusion.2.refs_0_), channel_id=1, source_target_pairs={{0,25},{1,24},{2,27},{3,26},{4,29},{5,28},{6,31},{7,30},{8,17},{9,... | collective-permute-start | bytes 30728 | tf_op jit(solution)/shard_map/ppermute | solution.py:25
  43.6 3.2 %collective-permute-start.19 = (f32[1,2,1280]{2,1,0:T(2,128)S(1)}, f32[1,2,1280]{2,1,0:T(2,128)S(1)}, u32[]{:S(2)}, u32[]{:S(2)}) collective-permute-start(f32[1,2,1280]{2,1,0:T(2,128)S(1)} %add_add_fusion.2.refs_0_), channel_id=1, source_target_pairs={{0,9},{1,8},{2,11},{3,10},{4,13},{5,12},{6,15},{7,14},{8,1},{9,0},... | collective-permute-start | bytes 30728 | tf_op jit(solution)/shard_map/ppermute | solution.py:25

commit v16 on v14

--- a/solution.py
+++ b/solution.py
@@ -131,12 +131,12 @@
     ]
     for copy in tok_copies + [phi_copy] + cot_copies:
         copy.start()
-    for copy, piece in zip(tok_copies, pieces):
+    for copy in tok_copies:
         copy.wait()
-        tok_f32 = tok_buf[piece, :].astype(f32)
-        tok_scale = lax.rsqrt(jnp.sum(tok_f32 * tok_f32, axis=1, keepdims=True) + epsilon)
-        norm_ref[piece, :] = (tok_f32 * tok_scale).astype(bf16)
-        tok_scale_ref[piece, :] = tok_scale
+    tok_f32 = tok_buf[...].astype(f32)
+    tok_scale = lax.rsqrt(jnp.sum(tok_f32 * tok_f32, axis=1, keepdims=True) + epsilon)
+    norm_ref[...] = (tok_f32 * tok_scale).astype(bf16)
+    tok_scale_ref[...] = tok_scale
     phi_copy.wait()
     phi = phi_buf[...].astype(f32)
     phi_scale = lax.rsqrt(jnp.sum(phi * phi, axis=1, keepdims=True) + epsilon)
@@ -214,13 +214,22 @@
     return jnp.sum(jnp.where(same, row, 0.0), axis=1, keepdims=True)
 
 
-def score_grads(scale_ref, slots_ref, totals_ref, tok_ref, cot_ref, norm_ref, exp_ref, grad_ref, dispatch_ref, phi_ref):
+def score_grads(clip_ref, scale_ref, message_ref, totals_ref, tok_ref, cot_ref, norm_ref, exp_ref, grad_ref, dispatch_ref, phi_ref, slot_y_ref, slot_dx_ref):
     width = tok_ref.shape[1]
-    slot_y = slots_ref[:, :width].astype(bf16)
-    slot_dx = slots_ref[:, width : 2 * width].astype(bf16)
+    experts = message_ref.shape[0]
+
+    def of_clip(values):
+        mine = lax.broadcasted_iota(jnp.int32, values.shape, 0) == clip_ref[0]
+        return jnp.sum(jnp.where(mine, values, 0.0), axis=0, keepdims=True)
+
+    slots = jnp.concatenate([of_clip(message_ref[slot]) for slot in range(experts)], axis=0)
+    slot_y = slots[:, :width].astype(bf16)
+    slot_dx = slots[:, width : 2 * width].astype(bf16)
+    slot_y_ref[...] = slot_y
+    slot_dx_ref[...] = slot_dx
     low = 2 * width + LANES
-    column_stat = slots_ref[:, 2 * width : 2 * width + 1] + slots_ref[:, low : low + 1]
-    totals = as_column(totals_ref[...], slot_y.shape[0])
+    column_stat = slots[:, 2 * width : 2 * width + 1] + slots[:, low : low + 1]
+    totals = as_column(of_clip(totals_ref[...]), experts)
     exp_scores = exp_ref[...]
     combine_f = exp_scores / jnp.sum(exp_scores, axis=0, keepdims=True)
     comb_dot = lax.dot_general(slot_y, cot_ref[...], ROWS, preferred_element_type=f32)
@@ -283,7 +292,7 @@
             pltpu.VMEM((count, width), bf16),
             pltpu.VMEM((count, width), bf16),
             pltpu.SemaphoreType.DMA,
-            pltpu.SemaphoreType.DMA((2, 2 * PIECES)),
+            pltpu.SemaphoreType.DMA((2, PIECES)),
         ],
         compiler_params=params,
         name="token_sums",
@@ -321,24 +330,24 @@
         name="expert_rows",
     )(owned[None], message, expert_in, expert_out)
     message, hidden, row_cot = sum_to_all(message[None], group, (hidden, row_cot))
-    slots = lax.dynamic_index_in_dim(message, clip, 1, keepdims=False)
-    totals = lax.dynamic_index_in_dim(totals, clip, 0, keepdims=True)
     share = width // clips
     mine_x = lax.dynamic_slice_in_dim(row_x, clip * share, share, 1)
     mine_cot = lax.dynamic_slice_in_dim(row_cot, clip * share, share, 1)
     grad_expert_in = jnp.einsum("od,oh->dh", mine_x, pre_grad, preferred_element_type=f32)
     grad_expert_out = jnp.einsum("oh,od->hd", hidden, mine_cot, preferred_element_type=f32)
-    score_grad, dispatch, phi_part = pl.pallas_call(
+    score_grad, dispatch, phi_part, slot_y, slot_dx = pl.pallas_call(
         score_grads,
-        in_specs=[scalar] + [in_vmem] * 6,
+        in_specs=[scalar, scalar] + [in_vmem] * 6,
         out_shape=[
             jax.ShapeDtypeStruct((experts, count), bf16),
             jax.ShapeDtypeStruct((experts, count), bf16),
             jax.ShapeDtypeStruct((experts, width), f32),
+            jax.ShapeDtypeStruct((experts, width), bf16),
+            jax.ShapeDtypeStruct((experts, width), bf16),
         ],
         compiler_params=params,
         name="score_grads",
-    )(logit_scale, slots, totals, tok_in, tok_cot, tok_norm, exp_scores)
+    )(clip[None], logit_scale, message, totals, tok_in, tok_cot, tok_norm, exp_scores)
     phi_sum = phi_part
     for step in range(1, clips):
         phi_sum = phi_sum + hop(phi_part, step)
@@ -358,8 +367,6 @@
     phi_scale = lax.rsqrt(jnp.sum(phi_f32 * phi_f32, axis=1, keepdims=True) + epsilon)
     phi_unit = phi_f32 * phi_scale
     phi_norm = phi_unit.astype(bf16)
-    slot_y = slots[:, :width].astype(bf16)
-    slot_dx = slots[:, width : 2 * width].astype(bf16)
     mixed = jnp.einsum("sn,sd->nd", combine, slot_y, preferred_element_type=f32).astype(bf16)
     norm_grad = jnp.einsum("sn,sd->nd", score_grad, phi_norm, preferred_element_type=f32)
     through = jnp.einsum("sn,sd->nd", dispatch, slot_dx, preferred_element_type=f32)

time: 48.3 us -> 48 us (level)
  transfers between devices with their start and end apart: 20 -> 20, of which waited for: 11 -> 12; matrix products, arithmetic and copies ran while one was open for 16% -> 16% of each run, Pallas kernels for 4% -> 4%
where the time goes in v16:
time: 48 us; the launch traced here: 47.8 us
  starting transfers between devices  21.7 us (45%)
  waiting for transfers between devices  8.23 us (17%)
  Pallas kernels  8.21 us (17%)
  matrix products  7.52 us (16%)
  between operations  1.45 us (3%)
  other arithmetic  0.62 us (1%)
    ppermute x18, starting transfers between devices, exchange(): return lax.ppermute(value, AXES, pairs)  21 us
    ppermute x18, waiting for transfers between devices, exchange(): return lax.ppermute(value, AXES, pairs)  7.3 us
    pallas_call x1, Pallas kernels, per_device(): pl.pallas_call(token_sums, in_specs=[scalar, in_hbm, in_hbm, in_hbm], out...  2.88 us
    dot_general x1, matrix products, per_device(): jnp.einsum('sn,sd->nd', dispatch, slot_dx, preferred_element_type=f32)  1.98 us
    pallas_call x1, Pallas kernels, per_device(): pl.pallas_call(fetch, in_specs=[in_hbm] * 2, out_specs=[in_vmem] * 2, out...  1.94 us
    dot_general x1, matrix products, per_device(): jnp.einsum('sn,sd->nd', combine, slot_y, preferred_element_type=f32)  1.61 us
    dot_general x1, matrix products, per_device(): jnp.einsum('od,oh->dh', mine_x, pre_grad, preferred_element_type=f32)  1.59 us
    dot_general x1, matrix products, per_device(): jnp.einsum('oh,od->hd', hidden, mine_cot, preferred_element_type=f32)  1.59 us
  transfers between devices with their start and end apart: 20, of which 12 were waited for; matrix products, arithmetic and copies ran while one was open for 16% of the time, Pallas kernels for 4%

profile of v16, /device:TPU:0, one launch (start us, length us, event | category | flops | bytes accessed | tf_op | source)
XLA Modules:
  0.0 47.8 jit_solution(12010379051473980394)
XLA Ops:
  1.3 2.9 %token_sums.1 = (bf16[2,2816]{1,0:T(2,128)(2,1)S(1)}, f32[2,512]{1,0:T(2,128)S(1)}, bf16[2,512]{1,0:T(2,128)(2,1)S(1)}, f32[512,1]{1,0:T(8,128)S(1)}, bf16[512,1280]{1,0:T(8,128)(2,1)S(1)}) custom-call(f32[1]{0:T(128)S(6)} %copy.11.scale_ref, bf16[2,1280]{1,0:T(2,128)(2,1)} %bitcast.40, bf16[512,1280]{1,0:T(8,128)(2,1)} %bitcast.36, bf16[512,1280]{1,0:T(8,128)(2,1)} %bitcast.38), custom_call_target="tpu_custom_call" | custom-call | tf_op jit(solution)/shard_map/token_sums/pallas_call | solution.py:280
  4.2 0.5 %collective-permute-start = (bf16[2,2816]{1,0:T(2,128)(2,1)S(1)}, bf16[2,2816]{1,0:T(2,128)(2,1)S(1)}, u32[]{:S(2)}, u32[]{:S(2)}) collective-permute-start(bf16[2,2816]{1,0:T(2,128)(2,1)S(1)} %get-tuple-element.30), channel_id=1, source_target_pairs={{0,1},{1,0},{2,3},{3,2},{4,5},{5,4},{6,7},{7,6},{8,9},{9,8},{10,11... | collective-permute-start | bytes 33800 | tf_op jit(solution)/shard_map/ppermute | solution.py:29
  4.7 0.1 fusion.4
  4.9 0.7 %collective-permute-done = bf16[2,2816]{1,0:T(2,128)(2,1)S(1)} collective-permute-done((bf16[2,2816]{1,0:T(2,128)(2,1)S(1)}, bf16[2,2816]{1,0:T(2,128)(2,1)S(1)}, u32[]{:S(2)}, u32[]{:S(2)}) %collective-permute-start) | collective-permute-done | bytes 11296 | tf_op jit(solution)/shard_map/ppermute | solution.py:29
  5.5 0.1 broadcast_select_fusion.1
  5.7 3.8 %collective-permute-start.3 = (bf16[1,2,2816]{2,1,0:T(2,128)(2,1)S(1)}, bf16[1,2,2816]{2,1,0:T(2,128)(2,1)S(1)}, u32[]{:S(2)}, u32[]{:S(2)}) collective-permute-start(bf16[1,2,2816]{2,1,0:T(2,128)(2,1)S(1)} %get-tuple-element.54), channel_id=1, source_target_pairs={{0,17},{1,16},{2,19},{3,18},{4,21},{5,20},{6,23},{7,22},{8,25},{9,... | collective-permute-start | bytes 33800 | tf_op jit(solution)/shard_map/ppermute | solution.py:25
  9.4 1.3 %collective-permute-start.2 = (bf16[1,2,2816]{2,1,0:T(2,128)(2,1)S(1)}, bf16[1,2,2816]{2,1,0:T(2,128)(2,1)S(1)}, u32[]{:S(2)}, u32[]{:S(2)}) collective-permute-start(bf16[1,2,2816]{2,1,0:T(2,128)(2,1)S(1)} %get-tuple-element.55), channel_id=1, source_target_pairs={{0,25},{1,24},{2,27},{3,26},{4,29},{5,28},{6,31},{7,30},{8,17},{9,... | collective-permute-start | bytes 33800 | tf_op jit(solution)/shard_map/ppermute | solution.py:25
  10.7 0.2 collective-permute-start.1
  11.0 3.4 %collective-permute-done.2 = bf16[1,2,2816]{2,1,0:T(2,128)(2,1)S(1)} collective-permute-done((bf16[1,2,2816]{2,1,0:T(2,128)(2,1)S(1)}, bf16[1,2,2816]{2,1,0:T(2,128)(2,1)S(1)}, u32[]{:S(2)}, u32[]{:S(2)}) %collective-permute-start.2) | collective-permute-done | bytes 11296 | tf_op jit(solution)/shard_map/ppermute | solution.py:25
  14.4 2.5 %collective-permute-start.5 = (f32[1,2,2816]{2,1,0:T(2,128)S(1)}, f32[1,2,2816]{2,1,0:T(2,128)S(1)}, u32[]{:S(2)}, u32[]{:S(2)}) collective-permute-start(f32[1,2,2816]{2,1,0:T(2,128)S(1)} %add_add_fusion.1), channel_id=1, source_target_pairs={{0,7},{1,6},{2,5},{3,4},{4,3},{5,2},{6,1},{7,0},{8,15},{9,14},{10,... | collective-permute-start | bytes 67592 | tf_op jit(solution)/shard_map/ppermute | solution.py:25
  16.9 0.3 collective-permute-start.6
  17.1 0.5 %collective-permute-start.4 = (f32[1,2,2816]{2,1,0:T(2,128)S(1)}, f32[1,2,2816]{2,1,0:T(2,128)S(1)}, u32[]{:S(2)}, u32[]{:S(2)}) collective-permute-start(f32[1,2,2816]{2,1,0:T(2,128)S(1)} %add_add_fusion.1), channel_id=1, source_target_pairs={{0,3},{1,2},{2,1},{3,0},{4,7},{5,6},{6,5},{7,4},{8,11},{9,10},{10,... | collective-permute-start | bytes 67592 | tf_op jit(solution)/shard_map/ppermute | solution.py:25
  17.6 0.1 reduce
  17.8 1.9 %fetch_weights.1 = (bf16[1280,640]{1,0:T(8,128)(2,1)S(1)}, bf16[640,1280]{1,0:T(8,128)(2,1)S(1)}) custom-call(bf16[1280,640]{1,0:T(8,128)(2,1)} %in_ref, bf16[640,1280]{1,0:T(8,128)(2,1)} %out_ref), custom_call_target="tpu_custom_call" | custom-call | bytes 6553600 | tf_op jit(solution)/shard_map/fetch_weights/pallas_call | solution.py:302
  19.7 0.4 collective-permute-done.6
  20.1 0.3 collective-permute-done.4
  20.4 1.5 %expert_rows.1 = (f32[2,2816]{1,0:T(2,128)S(1)}, f32[2,128]{1,0:T(2,128)S(1)}, bf16[2,1280]{1,0:T(2,128)(2,1)S(1)}, bf16[2,1280]{1,0:T(2,128)(2,1)S(1)}, bf16[2,...) custom-call(s32[1]{0:T(128)} %bitcast.4.owned_ref, f32[2,2816]{1,0:T(2,128)S(1)} %add_bitcast_fusion.2.sums_ref, ...), custom_call_target="tpu_custom_call" | custom-call | tf_op jit(solution)/shard_map/expert_rows/pallas_call | solution.py:318
  21.9 1.6 %collective-permute-start.8 = (f32[1,2,2816]{2,1,0:T(2,128)S(1)}, f32[1,2,2816]{2,1,0:T(2,128)S(1)}, u32[]{:S(2)}, u32[]{:S(2)}) collective-permute-start(f32[1,2,2816]{2,1,0:T(2,128)S(1)} %bitcast.42), channel_id=1, source_target_pairs={{0,7},{1,6},{2,5},{3,4},{4,3},{5,2},{6,1},{7,0},{8,15},{9,14},{10,... | collective-permute-start | bytes 67592 | tf_op jit(solution)/shard_map/ppermute | solution.py:25
  23.6 0.5 collective-permute-start.9
  24.0 1.1 %collective-permute-start.7 = (f32[1,2,2816]{2,1,0:T(2,128)S(1)}, f32[1,2,2816]{2,1,0:T(2,128)S(1)}, u32[]{:S(2)}, u32[]{:S(2)}) collective-permute-start(f32[1,2,2816]{2,1,0:T(2,128)S(1)} %bitcast.44), channel_id=1, source_target_pairs={{0,3},{1,2},{2,1},{3,0},{4,7},{5,6},{6,5},{7,4},{8,11},{9,10},{10,... | collective-permute-start | bytes 67592 | tf_op jit(solution)/shard_map/ppermute | solution.py:25
  25.1 1.6 %fusion.10 = f32[640,640]{1,0:T(8,128)} fusion(bf16[2,640]{1,0:T(2,128)(2,1)S(1)} %get-tuple-element.49, bf16[2,1280]{1,0:T(2,128)(2,1)S(1)} %get-tuple-element.48, s32[]{:T(128)S(6)} %select_n.56), kind=kOutput, calls=%fused_computation.26 | convolution fusion | flops 1638400 | bytes 1643524 | tf_op jit(solution)/shard_map/od,oh->dh/dot_general | solution.py:336
  26.7 0.1 collective-permute-done.9
  26.8 0.4 collective-permute-done.7
  27.3 1.0 %collective-permute-start.12 = (bf16[1,2,2816]{2,1,0:T(2,128)(2,1)S(1)}, bf16[1,2,2816]{2,1,0:T(2,128)(2,1)S(1)}, u32[]{:S(2)}, u32[]{:S(2)}) collective-permute-start(bf16[1,2,2816]{2,1,0:T(2,128)(2,1)S(1)} %fusion.3), channel_id=1, source_target_pairs={{0,17},{1,16},{2,19},{3,18},{4,21},{5,20},{6,23},{7,22},{8,25},{9,... | collective-permute-start | bytes 33800 | tf_op jit(solution)/shard_map/ppermute | solution.py:25
  28.3 0.9 %collective-permute-start.11 = (bf16[1,2,2816]{2,1,0:T(2,128)(2,1)S(1)}, bf16[1,2,2816]{2,1,0:T(2,128)(2,1)S(1)}, u32[]{:S(2)}, u32[]{:S(2)}) collective-permute-start(bf16[1,2,2816]{2,1,0:T(2,128)(2,1)S(1)} %fusion.3), channel_id=1, source_target_pairs={{0,25},{1,24},{2,27},{3,26},{4,29},{5,28},{6,31},{7,30},{8,17},{9,... | collective-permute-start | bytes 33800 | tf_op jit(solution)/shard_map/ppermute | solution.py:25
  29.2 1.1 %collective-permute-start.10 = (bf16[1,2,2816]{2,1,0:T(2,128)(2,1)S(1)}, bf16[1,2,2816]{2,1,0:T(2,128)(2,1)S(1)}, u32[]{:S(2)}, u32[]{:S(2)}) collective-permute-start(bf16[1,2,2816]{2,1,0:T(2,128)(2,1)S(1)} %fusion.3), channel_id=1, source_target_pairs={{0,9},{1,8},{2,11},{3,10},{4,13},{5,12},{6,15},{7,14},{8,1},{9,0},... | collective-permute-start | bytes 33800 | tf_op jit(solution)/shard_map/ppermute | solution.py:25
  30.3 1.6 %fusion.8 = f32[640,640]{1,0:T(8,128)} fusion(bf16[2,640]{1,0:T(2,128)(2,1)S(1)} %get-tuple-element.50, bf16[2,1280]{1,0:T(2,128)(2,1)S(1)} %get-tuple-element.51, s32[]{:T(128)S(6)} %select_n.56), kind=kOutput, calls=%fused_computation.24 | convolution fusion | flops 1638400 | bytes 1643524 | tf_op jit(solution)/shard_map/oh,od->hd/dot_general | solution.py:337
  31.9 0.4 collective-permute-done.10
  32.4 0.0 collective-permute-done.12
  32.4 0.9 %collective-permute-done.11 = bf16[1,2,2816]{2,1,0:T(2,128)(2,1)S(1)} collective-permute-done((bf16[1,2,2816]{2,1,0:T(2,128)(2,1)S(1)}, bf16[1,2,2816]{2,1,0:T(2,128)(2,1)S(1)}, u32[]{:S(2)}, u32[]{:S(2)}) %collective-permute-start.11) | collective-permute-done | bytes 11296 | tf_op jit(solution)/shard_map/ppermute | solution.py:25
  33.3 0.1 broadcast_select_fusion.message_ref
  33.4 1.1 %score_grads.1 = (bf16[2,512]{1,0:T(2,128)(2,1)S(1)}, bf16[2,512]{1,0:T(2,128)(2,1)S(1)}, f32[2,1280]{1,0:T(2,128)S(1)}, bf16[2,1280]{1,0:T(2,128)(2,1)S(1)}, bf16[2,1280]{1,0:T(2,128)(2,1)S(1)}) custom-call(s32[1]{0:T(128)} %bitcast.3.clip_ref, f32[1]{0:T(128)S(6)} %copy.11.scale_ref, f32[2,2,2816]{2,1,0:T(2,128)S(1)} %broadcast_select_fusion.message_ref, ...), custom_call_target="tpu_custom_call" | custom-call | tf_op jit(solution)/shard_map/score_grads/pallas_call | solution.py:338
  34.4 0.2 collective-permute-start.13
  34.6 0.7 %multiply_reduce_fusion = (f32[512]{0:T(512)S(1)}, f32[512,1280]{1,0:T(8,128)S(1)}) fusion(f32[512]{0:T(512)S(1)} %reduce, bf16[1,512,1280]{2,1,0:T(8,128)(2,1)S(1)} %copy-done, bf16[2,512]{1,0:T(2,128)(2,1)S(1)} %get-tuple-element.47, f32[2]{0:T(128)S(1)} %add_rsqrt_fusion, bf16[1280,2]{0,1:T(2,128)(2,1)S(1)} %copy-done.2), kind=kOutput, calls=%fused_computation.5 | convolution fusion | flops 5250048 | bytes 3943432 | tf_op jit(solution)/shard_map/sn,sd->nd/dot_general | solution.py:371
  35.3 0.3 collective-permute-done.13
  35.6 2.1 %collective-permute-start.15 = (f32[1,2,1280]{2,1,0:T(2,128)S(1)}, f32[1,2,1280]{2,1,0:T(2,128)S(1)}, u32[]{:S(2)}, u32[]{:S(2)}) collective-permute-start(f32[1,2,1280]{2,1,0:T(2,128)S(1)} %add_bitcast_fusion.3), channel_id=1, source_target_pairs={{0,7},{1,6},{2,5},{3,4},{4,3},{5,2},{6,1},{7,0},{8,15},{9,14},{10,... | collective-permute-start | bytes 30728 | tf_op jit(solution)/shard_map/ppermute | solution.py:25
  37.7 0.3 collective-permute-start.16
  38.0 0.7 %collective-permute-start.14 = (f32[1,2,1280]{2,1,0:T(2,128)S(1)}, f32[1,2,1280]{2,1,0:T(2,128)S(1)}, u32[]{:S(2)}, u32[]{:S(2)}) collective-permute-start(f32[1,2,1280]{2,1,0:T(2,128)S(1)} %add_bitcast_fusion.3), channel_id=1, source_target_pairs={{0,3},{1,2},{2,1},{3,0},{4,7},{5,6},{6,5},{7,4},{8,11},{9,10},{10,... | collective-permute-start | bytes 30728 | tf_op jit(solution)/shard_map/ppermute | solution.py:25
  38.6 2.0 %fusion.1 = bf16[1,512,1280]{2,1,0:T(8,128)(2,1)} fusion(bf16[2,512]{1,0:T(2,128)(2,1)S(1)} %get-tuple-element.44, bf16[2,1280]{1,0:T(2,128)(2,1)S(1)} %get-tuple-element.45, f32[512,1280]{1,0:T(8,128)S(1)} %get-tuple-element.57, f32[512]{0:T(512)S(1)} %get-tuple-element.56, f32[512]{0:T(512)S(1)} %reduce, bf16[1,512,1280]{2,1,0:T(8,128)(2,1)S(1)} %copy-done), kind=kOutput, calls=%fused_computation.3 | convolution fusion | flops 7208960 | bytes 5254144 | tf_op jit(solution)/shard_map/sn,sd->nd/dot_general | solution.py:372
  40.6 0.0 collective-permute-done.15
  40.6 0.2 collective-permute-done.16
  40.8 0.3 collective-permute-done.14
  41.1 0.9 %collective-permute-start.17 = (f32[1,2,1280]{2,1,0:T(2,128)S(1)}, f32[1,2,1280]{2,1,0:T(2,128)S(1)}, u32[]{:S(2)}, u32[]{:S(2)}) collective-permute-start(f32[1,2,1280]{2,1,0:T(2,128)S(1)} %add_add_fusion.2.refs_0_), channel_id=1, source_target_pairs={{0,17},{1,16},{2,19},{3,18},{4,21},{5,20},{6,23},{7,22},{8,25},{9,... | collective-permute-start | bytes 30728 | tf_op jit(solution)/shard_map/ppermute | solution.py:25
  42.0 1.8 %collective-permute-start.18 = (f32[1,2,1280]{2,1,0:T(2,128)S(1)}, f32[1,2,1280]{2,1,0:T(2,128)S(1)}, u32[]{:S(2)}, u32[]{:S(2)}) collective-permute-start(f32[1,2,1280]{2,1,0:T(2,128)S(1)} %add_add_fusion.2.refs_0_), channel_id=1, source_target_pairs={{0,25},{1,24},{2,27},{3,26},{4,29},{5,28},{6,31},{7,30},{8,17},{9,... | collective-permute-start | bytes 30728 | tf_op jit(solution)/shard_map/ppermute | solution.py:25
  43.8 0.6 %collective-permute-start.19 = (f32[1,2,1280]{2,1,0:T(2,128)S(1)}, f32[1,2,1280]{2,1,0:T(2,128)S(1)}, u32[]{:S(2)}, u32[]{:S(2)}) collective-permute-start(f32[1,2,1280]{2,1,0:T(2,128)S(1)} %add_add_fusion.2.refs_0_), channel_id=1, source_target_pairs={{0,9},{1,8},{2,11},{3,10},{4,13},{5,12},{6,15},{7,14},{8,1},{9,0},... | collective-permute-start | bytes 30728 | tf_op jit(solution)/shard_map/ppermute | solution.py:25
  44.3 1.6 %fusion.2 = bf16[1,512,1280]{2,1,0:T(8,128)(2,1)} fusion(bf16[2,512]{1,0:T(2,128)(2,1)S(1)} %get-tuple-element.29, bf16[2,1280]{1,0:T(2,128)(2,1)S(1)} %get-tuple-element.43), kind=kOutput, calls=%fused_computation.4 | convolution fusion | flops 3276800 | bytes 1317888 | tf_op jit(solution)/shard_map/sn,sd->nd/dot_general | solution.py:370
  45.9 1.0 %collective-permute-done.18.refs_2_ = f32[1,2,1280]{2,1,0:T(2,128)S(1)} collective-permute-done((f32[1,2,1280]{2,1,0:T(2,128)S(1)}, f32[1,2,1280]{2,1,0:T(2,128)S(1)}, u32[]{:S(2)}, u32[]{:S(2)}) %collective-permute-start.18) | collective-permute-done | bytes 10272 | tf_op jit(solution)/shard_map/ppermute | solution.py:25
  47.0 0.8 %finish.1 = f32[2,1280]{1,0:T(2,128)} custom-call(bf16[2,1280]{1,0:T(2,128)(2,1)S(1)} %bitcast.41, f32[1,2,1280]{2,1,0:T(2,128)S(1)} %add_add_fusion.2.refs_0_, f32[1,2,1280]{2,1,0:T(2,128)S(1)} %collective-permute-done.17.refs_1_, f32[1,2,1280]{2,1,0:T(2,128)S(1)} %collective-permute-done.18.refs_2_, f32[1,2,1280]{2,1,0:T(2,128)S(1)} %collective-permute-done.19.refs_3_), custom_call_target="tpu_custom_call" | custom-call | tf_op jit(solution)/shard_map/finish/pallas_call | solution.py:359
  (25 shorter events, 0.2 us)
Async XLA Ops:
  0.6 4.1 %copy-start.2 = (bf16[1280,2]{0,1:T(2,128)(2,1)S(1)}, bf16[1280,2]{0,1:T(2,128)(2,1)}, u32[]{:S(2)}) copy-start(bf16[1280,2]{0,1:T(2,128)(2,1)} %param.8) | copy-start | bytes 15364
  4.2 1.4 %collective-permute-start = (bf16[2,2816]{1,0:T(2,128)(2,1)S(1)}, bf16[2,2816]{1,0:T(2,128)(2,1)S(1)}, u32[]{:S(2)}, u32[]{:S(2)}) collective-permute-start(bf16[2,2816]{1,0:T(2,128)(2,1)S(1)} %get-tuple-element.30), channel_id=1, source_target_pairs={{0,1},{1,0},{2,3},{3,2},{4,5},{5,4},{6,7},{7,6},{8,9},{9,8},{10,11... | collective-permute-start | bytes 33800 | tf_op jit(solution)/shard_map/ppermute | solution.py:29
  5.7 5.3 %collective-permute-start.3 = (bf16[1,2,2816]{2,1,0:T(2,128)(2,1)S(1)}, bf16[1,2,2816]{2,1,0:T(2,128)(2,1)S(1)}, u32[]{:S(2)}, u32[]{:S(2)}) collective-permute-start(bf16[1,2,2816]{2,1,0:T(2,128)(2,1)S(1)} %get-tuple-element.54), channel_id=1, source_target_pairs={{0,17},{1,16},{2,19},{3,18},{4,21},{5,20},{6,23},{7,22},{8,25},{9,... | collective-permute-start | bytes 33800 | tf_op jit(solution)/shard_map/ppermute | solution.py:25
  9.4 4.9 %collective-permute-start.2 = (bf16[1,2,2816]{2,1,0:T(2,128)(2,1)S(1)}, bf16[1,2,2816]{2,1,0:T(2,128)(2,1)S(1)}, u32[]{:S(2)}, u32[]{:S(2)}) collective-permute-start(bf16[1,2,2816]{2,1,0:T(2,128)(2,1)S(1)} %get-tuple-element.55), channel_id=1, source_target_pairs={{0,25},{1,24},{2,27},{3,26},{4,29},{5,28},{6,31},{7,30},{8,17},{9,... | collective-permute-start | bytes 33800 | tf_op jit(solution)/shard_map/ppermute | solution.py:25
  10.7 3.6 %collective-permute-start.1 = (bf16[1,2,2816]{2,1,0:T(2,128)(2,1)S(1)}, bf16[1,2,2816]{2,1,0:T(2,128)(2,1)S(1)}, u32[]{:S(2)}, u32[]{:S(2)}) collective-permute-start(bf16[1,2,2816]{2,1,0:T(2,128)(2,1)S(1)} %get-tuple-element.53), channel_id=1, source_target_pairs={{0,9},{1,8},{2,11},{3,10},{4,13},{5,12},{6,15},{7,14},{8,1},{9,0},... | collective-permute-start | bytes 33800 | tf_op jit(solution)/shard_map/ppermute | solution.py:25
  14.4 5.3 %collective-permute-start.5 = (f32[1,2,2816]{2,1,0:T(2,128)S(1)}, f32[1,2,2816]{2,1,0:T(2,128)S(1)}, u32[]{:S(2)}, u32[]{:S(2)}) collective-permute-start(f32[1,2,2816]{2,1,0:T(2,128)S(1)} %add_add_fusion.1), channel_id=1, source_target_pairs={{0,7},{1,6},{2,5},{3,4},{4,3},{5,2},{6,1},{7,0},{8,15},{9,14},{10,... | collective-permute-start | bytes 67592 | tf_op jit(solution)/shard_map/ppermute | solution.py:25
  16.9 3.2 %collective-permute-start.6 = (f32[1,2,2816]{2,1,0:T(2,128)S(1)}, f32[1,2,2816]{2,1,0:T(2,128)S(1)}, u32[]{:S(2)}, u32[]{:S(2)}) collective-permute-start(f32[1,2,2816]{2,1,0:T(2,128)S(1)} %add_add_fusion.1), channel_id=1, source_target_pairs={{0,5},{1,4},{2,7},{3,6},{4,1},{5,0},{6,3},{7,2},{8,13},{9,12},{10,... | collective-permute-start | bytes 67592 | tf_op jit(solution)/shard_map/ppermute | solution.py:25
  17.1 3.2 %collective-permute-start.4 = (f32[1,2,2816]{2,1,0:T(2,128)S(1)}, f32[1,2,2816]{2,1,0:T(2,128)S(1)}, u32[]{:S(2)}, u32[]{:S(2)}) collective-permute-start(f32[1,2,2816]{2,1,0:T(2,128)S(1)} %add_add_fusion.1), channel_id=1, source_target_pairs={{0,3},{1,2},{2,1},{3,0},{4,7},{5,6},{6,5},{7,4},{8,11},{9,10},{10,... | collective-permute-start | bytes 67592 | tf_op jit(solution)/shard_map/ppermute | solution.py:25
  21.9 11.4 %copy-start = (bf16[1,512,1280]{2,1,0:T(8,128)(2,1)S(1)}, bf16[1,512,1280]{2,1,0:T(8,128)(2,1)}, u32[]{:S(2)}) copy-start(bf16[1,512,1280]{2,1,0:T(8,128)(2,1)} %param.6) | copy-start | bytes 3932164
  21.9 11.4 %copy-start.1 = (bf16[1,512,1280]{2,1,0:T(8,128)(2,1)S(1)}, bf16[1,512,1280]{2,1,0:T(8,128)(2,1)}, u32[]{:S(2)}) copy-start(bf16[1,512,1280]{2,1,0:T(8,128)(2,1)} %param.7) | copy-start | bytes 3932164
  21.9 4.8 %collective-permute-start.8 = (f32[1,2,2816]{2,1,0:T(2,128)S(1)}, f32[1,2,2816]{2,1,0:T(2,128)S(1)}, u32[]{:S(2)}, u32[]{:S(2)}) collective-permute-start(f32[1,2,2816]{2,1,0:T(2,128)S(1)} %bitcast.42), channel_id=1, source_target_pairs={{0,7},{1,6},{2,5},{3,4},{4,3},{5,2},{6,1},{7,0},{8,15},{9,14},{10,... | collective-permute-start | bytes 67592 | tf_op jit(solution)/shard_map/ppermute | solution.py:25
  23.6 3.3 %collective-permute-start.9 = (f32[1,2,2816]{2,1,0:T(2,128)S(1)}, f32[1,2,2816]{2,1,0:T(2,128)S(1)}, u32[]{:S(2)}, u32[]{:S(2)}) collective-permute-start(f32[1,2,2816]{2,1,0:T(2,128)S(1)} %bitcast.43), channel_id=1, source_target_pairs={{0,5},{1,4},{2,7},{3,6},{4,1},{5,0},{6,3},{7,2},{8,13},{9,12},{10,... | collective-permute-start | bytes 67592 | tf_op jit(solution)/shard_map/ppermute | solution.py:25
  24.0 3.2 %collective-permute-start.7 = (f32[1,2,2816]{2,1,0:T(2,128)S(1)}, f32[1,2,2816]{2,1,0:T(2,128)S(1)}, u32[]{:S(2)}, u32[]{:S(2)}) collective-permute-start(f32[1,2,2816]{2,1,0:T(2,128)S(1)} %bitcast.44), channel_id=1, source_target_pairs={{0,3},{1,2},{2,1},{3,0},{4,7},{5,6},{6,5},{7,4},{8,11},{9,10},{10,... | collective-permute-start | bytes 67592 | tf_op jit(solution)/shard_map/ppermute | solution.py:25
  27.3 5.1 %collective-permute-start.12 = (bf16[1,2,2816]{2,1,0:T(2,128)(2,1)S(1)}, bf16[1,2,2816]{2,1,0:T(2,128)(2,1)S(1)}, u32[]{:S(2)}, u32[]{:S(2)}) collective-permute-start(bf16[1,2,2816]{2,1,0:T(2,128)(2,1)S(1)} %fusion.3), channel_id=1, source_target_pairs={{0,17},{1,16},{2,19},{3,18},{4,21},{5,20},{6,23},{7,22},{8,25},{9,... | collective-permute-start | bytes 33800 | tf_op jit(solution)/shard_map/ppermute | solution.py:25
  28.3 4.9 %collective-permute-start.11 = (bf16[1,2,2816]{2,1,0:T(2,128)(2,1)S(1)}, bf16[1,2,2816]{2,1,0:T(2,128)(2,1)S(1)}, u32[]{:S(2)}, u32[]{:S(2)}) collective-permute-start(bf16[1,2,2816]{2,1,0:T(2,128)(2,1)S(1)} %fusion.3), channel_id=1, source_target_pairs={{0,25},{1,24},{2,27},{3,26},{4,29},{5,28},{6,31},{7,30},{8,17},{9,... | collective-permute-start | bytes 33800 | tf_op jit(solution)/shard_map/ppermute | solution.py:25
  29.2 3.1 %collective-permute-start.10 = (bf16[1,2,2816]{2,1,0:T(2,128)(2,1)S(1)}, bf16[1,2,2816]{2,1,0:T(2,128)(2,1)S(1)}, u32[]{:S(2)}, u32[]{:S(2)}) collective-permute-start(bf16[1,2,2816]{2,1,0:T(2,128)(2,1)S(1)} %fusion.3), channel_id=1, source_target_pairs={{0,9},{1,8},{2,11},{3,10},{4,13},{5,12},{6,15},{7,14},{8,1},{9,0},... | collective-permute-start | bytes 33800 | tf_op jit(solution)/shard_map/ppermute | solution.py:25
  34.4 1.2 %collective-permute-start.13 = (f32[2,1280]{1,0:T(2,128)S(1)}, f32[2,1280]{1,0:T(2,128)S(1)}, u32[]{:S(2)}, u32[]{:S(2)}) collective-permute-start(f32[2,1280]{1,0:T(2,128)S(1)} %get-tuple-element.52), channel_id=1, source_target_pairs={{0,1},{1,0},{2,3},{3,2},{4,5},{5,4},{6,7},{7,6},{8,9},{9,8},{10,11... | collective-permute-start | bytes 30728 | tf_op jit(solution)/shard_map/ppermute | solution.py:29
  35.6 5.0 %collective-permute-start.15 = (f32[1,2,1280]{2,1,0:T(2,128)S(1)}, f32[1,2,1280]{2,1,0:T(2,128)S(1)}, u32[]{:S(2)}, u32[]{:S(2)}) collective-permute-start(f32[1,2,1280]{2,1,0:T(2,128)S(1)} %add_bitcast_fusion.3), channel_id=1, source_target_pairs={{0,7},{1,6},{2,5},{3,4},{4,3},{5,2},{6,1},{7,0},{8,15},{9,14},{10,... | collective-permute-start | bytes 30728 | tf_op jit(solution)/shard_map/ppermute | solution.py:25
  37.7 3.1 %collective-permute-start.16 = (f32[1,2,1280]{2,1,0:T(2,128)S(1)}, f32[1,2,1280]{2,1,0:T(2,128)S(1)}, u32[]{:S(2)}, u32[]{:S(2)}) collective-permute-start(f32[1,2,1280]{2,1,0:T(2,128)S(1)} %add_bitcast_fusion.3), channel_id=1, source_target_pairs={{0,5},{1,4},{2,7},{3,6},{4,1},{5,0},{6,3},{7,2},{8,13},{9,12},{10,... | collective-permute-start | bytes 30728 | tf_op jit(solution)/shard_map/ppermute | solution.py:25
  38.0 3.1 %collective-permute-start.14 = (f32[1,2,1280]{2,1,0:T(2,128)S(1)}, f32[1,2,1280]{2,1,0:T(2,128)S(1)}, u32[]{:S(2)}, u32[]{:S(2)}) collective-permute-start(f32[1,2,1280]{2,1,0:T(2,128)S(1)} %add_bitcast_fusion.3), channel_id=1, source_target_pairs={{0,3},{1,2},{2,1},{3,0},{4,7},{5,6},{6,5},{7,4},{8,11},{9,10},{10,... | collective-permute-start | bytes 30728 | tf_op jit(solution)/shard_map/ppermute | solution.py:25
  41.1 4.8 %collective-permute-start.17 = (f32[1,2,1280]{2,1,0:T(2,128)S(1)}, f32[1,2,1280]{2,1,0:T(2,128)S(1)}, u32[]{:S(2)}, u32[]{:S(2)}) collective-permute-start(f32[1,2,1280]{2,1,0:T(2,128)S(1)} %add_add_fusion.2.refs_0_), channel_id=1, source_target_pairs={{0,17},{1,16},{2,19},{3,18},{4,21},{5,20},{6,23},{7,22},{8,25},{9,... | collective-permute-start | bytes 30728 | tf_op jit(solution)/shard_map/ppermute | solution.py:25
  42.0 5.0 %collective-permute-start.18 = (f32[1,2,1280]{2,1,0:T(2,128)S(1)}, f32[1,2,1280]{2,1,0:T(2,128)S(1)}, u32[]{:S(2)}, u32[]{:S(2)}) collective-permute-start(f32[1,2,1280]{2,1,0:T(2,128)S(1)} %add_add_fusion.2.refs_0_), channel_id=1, source_target_pairs={{0,25},{1,24},{2,27},{3,26},{4,29},{5,28},{6,31},{7,30},{8,17},{9,... | collective-permute-start | bytes 30728 | tf_op jit(solution)/shard_map/ppermute | solution.py:25
  43.8 3.2 %collective-permute-start.19 = (f32[1,2,1280]{2,1,0:T(2,128)S(1)}, f32[1,2,1280]{2,1,0:T(2,128)S(1)}, u32[]{:S(2)}, u32[]{:S(2)}) collective-permute-start(f32[1,2,1280]{2,1,0:T(2,128)S(1)} %add_add_fusion.2.refs_0_), channel_id=1, source_target_pairs={{0,9},{1,8},{2,11},{3,10},{4,13},{5,12},{6,15},{7,14},{8,1},{9,0},... | collective-permute-start | bytes 30728 | tf_op jit(solution)/shard_map/ppermute | solution.py:25

commit v17 on v15

--- a/solution.py
+++ b/solution.py
@@ -60,7 +60,7 @@
     return (terms[0] + terms[low]) + (terms[low | high] + terms[high])
 
 
-def sum_to_owner(value, group):
+def sum_to_owner(value, group, beside):
     place = lax.axis_index("seq")
     for pair in reversed(rounds(lax.axis_size("seq"))):
         owner_masks = [mask for mask in pair if mask >= group]
@@ -76,7 +76,8 @@
         for mask in swaps(pair):
             terms[mask] = exchange(block_for(mask), mask)
         value = added({mask: term.astype(f32) for mask, term in terms.items()}, pair)
-    return value
+        value, *beside = lax.optimization_barrier((value, *beside))
+    return (value, *beside)
 
 
 def round_terms(value, pair):
@@ -307,7 +308,8 @@
         ),
         name="fetch_weights",
     )(in_place(expert_in), in_place(expert_out))
-    message = sum_to_owner(message, group)[0]
+    message, expert_in, expert_out = sum_to_owner(message, group, (expert_in, expert_out))
+    message = message[0]
     message, totals, row_x, row_cot, hidden, pre_grad = pl.pallas_call(
         expert_rows,
         in_specs=[scalar] + [in_vmem] * 3,

time: 47.8 us -> 52.4 us (1.096)
  other arithmetic: 0.62 us -> 5.08 us
  local copies, waits for them, and re-layouts: 0.09 us -> 1.79 us
  waiting for transfers between devices: 8.15 us -> 6.65 us
    add x3 -> x4, other arithmetic: 0.06 us -> 2.21 us  [added(): return terms[0] + terms[low] + (terms[low | high] + terms[high])]
    unnamed x6 -> x22, local copies, waits for them, and re-layouts: 0.01 us -> 1.09 us
    ppermute x18, waiting for transfers between devices: 7.22 us -> 6.34 us  [exchange(): return lax.ppermute(value, AXES, pairs)]
    ppermute x2, waiting for transfers between devices: 0.93 us -> 0.31 us  [hop(): lax.ppermute(value, 'dp', [(i, i ^ step) for i in range(lax.axis_size('dp...]
    squeeze x1, local copies, waits for them, and re-layouts: 0.04 us -> 0.66 us  [block_for(): return lax.dynamic_index_in_dim(blocks, index, 0, keepdims=False)]
    pallas_call x1, other arithmetic: 0.14 us -> 0.74 us  [per_device(): pl.pallas_call(token_sums, in_specs=[scalar, in_hbm, in_hbm, in_hbm], out...]
    rsqrt x1, other arithmetic: 0.01 us -> 0.59 us  [per_device(): lax.rsqrt(jnp.sum(phi_f32 * phi_f32, axis=1, keepdims=True) + epsilon)]
    lt x1, other arithmetic: 0.01 us -> 0.58 us  [narrow(): return jnp.where(lane < value.shape[-1] - LANES, value, lost).astype(bf16)]
  transfers between devices with their start and end apart: 20 -> 20, of which waited for: 11 -> 10; matrix products, arithmetic and copies ran while one was open for 16% -> 19% of each run, Pallas kernels for 4% -> 4%
where the time goes in v17:
time: 52.4 us; the launch traced here: 52.1 us
  starting transfers between devices  21.6 us (41%)
  Pallas kernels  8.05 us (15%)
  matrix products  7.49 us (14%)
  waiting for transfers between devices  6.65 us (13%)
  other arithmetic  5.08 us (10%)
  local copies, waits for them, and re-layouts  1.79 us (3%)
  between operations  1.5 us (3%)
    ppermute x18, starting transfers between devices, exchange(): return lax.ppermute(value, AXES, pairs)  20.9 us
    ppermute x18, waiting for transfers between devices, exchange(): return lax.ppermute(value, AXES, pairs)  6.34 us
    pallas_call x1, Pallas kernels, per_device(): pl.pallas_call(token_sums, in_specs=[scalar, in_hbm, in_hbm, in_hbm], out...  2.71 us
    add x4, other arithmetic, added(): return terms[0] + terms[low] + (terms[low | high] + terms[high])  2.21 us
    dot_general x1, matrix products, per_device(): jnp.einsum('sn,sd->nd', dispatch, slot_dx, preferred_element_type=f32)  1.96 us
    pallas_call x1, Pallas kernels, per_device(): pl.pallas_call(fetch, in_specs=[in_hbm] * 2, out_specs=[in_vmem] * 2, out...  1.94 us
    dot_general x1, matrix products, per_device(): jnp.einsum('sn,sd->nd', combine, slot_y, preferred_element_type=f32)  1.61 us
    dot_general x1, matrix products, per_device(): jnp.einsum('od,oh->dh', mine_x, pre_grad, preferred_element_type=f32)  1.59 us
  transfers between devices with their start and end apart: 20, of which 10 were waited for; matrix products, arithmetic and copies ran while one was open for 19% of the time, Pallas kernels for 4%

profile of v17, /device:TPU:0, one launch (start us, length us, event | category | flops | bytes accessed | tf_op | source)
XLA Modules:
  0.0 52.1 jit_solution(3722459615905525273)
XLA Ops:
  1.3 2.7 %token_sums.1 = (bf16[2,2816]{1,0:T(2,128)(2,1)S(1)}, f32[2,512]{1,0:T(2,128)S(1)}, bf16[2,512]{1,0:T(2,128)(2,1)S(1)}, f32[512,1]{1,0:T(8,128)S(1)}, bf16[512,1280]{1,0:T(8,128)(2,1)S(1)}) custom-call(f32[1]{0:T(128)S(6)} %copy.11.scale_ref, bf16[2,1280]{1,0:T(2,128)(2,1)} %bitcast.40, bf16[512,1280]{1,0:T(8,128)(2,1)} %bitcast.35, bf16[512,1280]{1,0:T(8,128)(2,1)} %bitcast.37), custom_call_target="tpu_custom_call" | custom-call | tf_op jit(solution)/shard_map/token_sums/pallas_call | solution.py:274
  4.0 1.0 %copy-done.2 = bf16[512,1280]{1,0:T(8,128)(2,1)} copy-done((bf16[512,1280]{1,0:T(8,128)(2,1)}, bf16[512,1280]{1,0:T(8,128)(2,1)S(1)}, u32[]{:S(2)}) %copy-start.2) | copy-done | bytes 1310744
  5.1 0.5 collective-permute-start
  5.5 0.1 fusion.4
  5.7 0.6 %add_rsqrt_fusion = f32[2]{0:T(128)} fusion(f32[2]{0:T(128)S(1)} %fusion.4), kind=kLoop, calls=%fused_computation.38 | loop fusion | flops 2 | bytes 16 | tf_op jit(solution)/shard_map/rsqrt | solution.py:362
  6.5 0.7 %constant_dynamic-slice_fusion.5 = (bf16[1,2,2816]{2,1,0:T(2,128)(2,1)}, bf16[1,2,2816]{2,1,0:T(2,128)(2,1)}, bf16[1,2,2816]{2,1,0:T(2,128)(2,1)}) fusion(bf16[2,2,2816]{2,1,0:T(2,128)(2,1)S(1)} %broadcast_select_fusion, s32[]{:T(128)S(6)} %select_n.62, s32[]{:T(128)S(6)} %select_n.64, s32[]{:T(128)S(6)} %select_n.63), kind=kLoop, calls=%fused_computation.37 | loop fusion | bytes 67596 | tf_op jit(solution)/shard_map/jit(dynamic_index_in_dim)/squeeze | solution.py:73
  7.1 3.7 %collective-permute-start.3 = (bf16[1,2,2816]{2,1,0:T(2,128)(2,1)}, bf16[1,2,2816]{2,1,0:T(2,128)(2,1)}, u32[]{:S(2)}, u32[]{:S(2)}) collective-permute-start(bf16[1,2,2816]{2,1,0:T(2,128)(2,1)} %get-tuple-element.64), channel_id=1, source_target_pairs={{0,17},{1,16},{2,19},{3,18},{4,21},{5,20},{6,23},{7,22},{8,25},{9,... | collective-permute-start | bytes 33800 | tf_op jit(solution)/shard_map/ppermute | solution.py:25
  10.8 1.3 %collective-permute-start.2 = (bf16[1,2,2816]{2,1,0:T(2,128)(2,1)}, bf16[1,2,2816]{2,1,0:T(2,128)(2,1)}, u32[]{:S(2)}, u32[]{:S(2)}) collective-permute-start(bf16[1,2,2816]{2,1,0:T(2,128)(2,1)} %get-tuple-element.65), channel_id=1, source_target_pairs={{0,25},{1,24},{2,27},{3,26},{4,29},{5,28},{6,31},{7,30},{8,17},{9,... | collective-permute-start | bytes 33800 | tf_op jit(solution)/shard_map/ppermute | solution.py:25
  12.1 0.2 collective-permute-start.1
  12.4 0.6 %iota_compare_fusion = pred[2816]{0:T(1024)(128)(4,1)} fusion(), kind=kLoop, calls=%fused_computation.18 | loop fusion | flops 2816 | bytes 2816 | tf_op jit(solution)/shard_map/lt | solution.py:49
  12.9 1.9 %fetch_weights.1 = (bf16[1280,640]{1,0:T(8,128)(2,1)S(1)}, bf16[640,1280]{1,0:T(8,128)(2,1)S(1)}) custom-call(bf16[1280,640]{1,0:T(8,128)(2,1)} %in_ref, bf16[640,1280]{1,0:T(8,128)(2,1)} %out_ref), custom_call_target="tpu_custom_call" | custom-call | bytes 6553600 | tf_op jit(solution)/shard_map/fetch_weights/pallas_call | solution.py:296
  14.9 1.1 %collective-permute-done.2 = bf16[1,2,2816]{2,1,0:T(2,128)(2,1)} collective-permute-done((bf16[1,2,2816]{2,1,0:T(2,128)(2,1)}, bf16[1,2,2816]{2,1,0:T(2,128)(2,1)}, u32[]{:S(2)}, u32[]{:S(2)}) %collective-permute-start.2) | collective-permute-done | bytes 11296 | tf_op jit(solution)/shard_map/ppermute | solution.py:25
  16.1 1.4 %add_add_fusion.2 = f32[1,2,2816]{2,1,0:T(2,128)} fusion(bf16[1,2,2816]{2,1,0:T(2,128)(2,1)} %collective-permute-done.3, bf16[1,2,2816]{2,1,0:T(2,128)(2,1)} %collective-permute-done.2, bf16[1,2,2816]{2,1,0:T(2,128)(2,1)} %collective-permute-done.1, bf16[2,2,2816]{2,1,0:T(2,128)(2,1)S(1)} %copy-done.6, s32[]{:T(128)S(6)} %select_n.59), kind=kLoop, calls=%fused_computation.15 | loop fusion | flops 39424 | bytes 67588 | tf_op jit(solution)/shard_map/add | solution.py:60
  17.4 2.4 %collective-permute-start.5 = (f32[1,2,2816]{2,1,0:T(2,128)}, f32[1,2,2816]{2,1,0:T(2,128)}, u32[]{:S(2)}, u32[]{:S(2)}) collective-permute-start(f32[1,2,2816]{2,1,0:T(2,128)} %add_add_fusion.2), channel_id=1, source_target_pairs={{0,7},{1,6},{2,5},{3,4},{4,3},{5,2},{6,1},{7,0},{8,15},{9,14},{10,... | collective-permute-start | bytes 67592 | tf_op jit(solution)/shard_map/ppermute | solution.py:25
  19.8 0.3 collective-permute-start.6
  20.1 0.5 collective-permute-start.4
  20.6 0.6 %iota_compare_fusion.1 = pred[2]{0:T(512)(128)(4,1)} fusion(s32[]{:T(128)S(6)} %select_n.59), kind=kLoop, calls=%fused_computation.40 | loop fusion | flops 2 | bytes 6 | tf_op jit(solution)/shard_map/eq | solution.py:109
  21.2 0.7 %reduce = f32[512]{0:T(512)} reduce(f32[512,1]{1,0:T(8,128)S(1)} %get-tuple-element.54, f32[]{:T(128)} %constant.79), dimensions={1}, to_apply=%get-tuple-element.54.reduce_sub_computation | reduce | bytes 4100 | tf_op jit(solution)/shard_map/token_sums/pallas_call | solution.py:274
  21.9 1.5 %collective-permute-done.6 = f32[1,2,2816]{2,1,0:T(2,128)} collective-permute-done((f32[1,2,2816]{2,1,0:T(2,128)}, f32[1,2,2816]{2,1,0:T(2,128)}, u32[]{:S(2)}, u32[]{:S(2)}) %collective-permute-start.6) | collective-permute-done | bytes 22560 | tf_op jit(solution)/shard_map/ppermute | solution.py:25
  23.4 0.3 collective-permute-done.4
  23.7 0.8 %add_add_fusion.1 = f32[1,2,2816]{2,1,0:T(2,128)S(1)} fusion(f32[1,2,2816]{2,1,0:T(2,128)} %collective-permute-done.5, f32[1,2,2816]{2,1,0:T(2,128)} %collective-permute-done.6, f32[1,2,2816]{2,1,0:T(2,128)} %add_add_fusion.2, f32[1,2,2816]{2,1,0:T(2,128)} %collective-permute-done.4), kind=kLoop, calls=%fused_computation.14 | loop fusion | flops 16896 | bytes 112640 | tf_op jit(solution)/shard_map/add | solution.py:60
  24.5 1.5 %expert_rows.1 = (f32[2,2816]{1,0:T(2,128)S(1)}, f32[2,128]{1,0:T(2,128)S(1)}, bf16[2,1280]{1,0:T(2,128)(2,1)S(1)}, bf16[2,1280]{1,0:T(2,128)(2,1)S(1)}, bf16[2,...) custom-call(s32[1]{0:T(128)} %bitcast.3.owned_ref, f32[2,2816]{1,0:T(2,128)S(1)} %bitcast.39, ...), custom_call_target="tpu_custom_call" | custom-call | tf_op jit(solution)/shard_map/expert_rows/pallas_call | solution.py:313
  26.0 1.5 %collective-permute-start.8 = (f32[1,2,2816]{2,1,0:T(2,128)S(1)}, f32[1,2,2816]{2,1,0:T(2,128)S(1)}, u32[]{:S(2)}, u32[]{:S(2)}) collective-permute-start(f32[1,2,2816]{2,1,0:T(2,128)S(1)} %bitcast.42), channel_id=1, source_target_pairs={{0,7},{1,6},{2,5},{3,4},{4,3},{5,2},{6,1},{7,0},{8,15},{9,14},{10,... | collective-permute-start | bytes 67592 | tf_op jit(solution)/shard_map/ppermute | solution.py:25
  27.5 0.3 collective-permute-start.9
  27.8 1.4 %collective-permute-start.7 = (f32[1,2,2816]{2,1,0:T(2,128)S(1)}, f32[1,2,2816]{2,1,0:T(2,128)S(1)}, u32[]{:S(2)}, u32[]{:S(2)}) collective-permute-start(f32[1,2,2816]{2,1,0:T(2,128)S(1)} %bitcast.44), channel_id=1, source_target_pairs={{0,3},{1,2},{2,1},{3,0},{4,7},{5,6},{6,5},{7,4},{8,11},{9,10},{10,... | collective-permute-start | bytes 67592 | tf_op jit(solution)/shard_map/ppermute | solution.py:25
  29.2 1.6 %fusion.12 = f32[640,640]{1,0:T(8,128)} fusion(bf16[2,640]{1,0:T(2,128)(2,1)S(1)} %get-tuple-element.57, bf16[2,1280]{1,0:T(2,128)(2,1)S(1)} %get-tuple-element.56, s32[]{:T(128)S(6)} %select_n.68), kind=kOutput, calls=%fused_computation.28 | convolution fusion | flops 1638400 | bytes 1643524 | tf_op jit(solution)/shard_map/od,oh->dh/dot_general | solution.py:333
  30.8 0.3 collective-permute-done.9
  31.2 1.4 %collective-permute-start.12 = (bf16[1,2,2816]{2,1,0:T(2,128)(2,1)S(1)}, bf16[1,2,2816]{2,1,0:T(2,128)(2,1)S(1)}, u32[]{:S(2)}, u32[]{:S(2)}) collective-permute-start(bf16[1,2,2816]{2,1,0:T(2,128)(2,1)S(1)} %fusion.3), channel_id=1, source_target_pairs={{0,17},{1,16},{2,19},{3,18},{4,21},{5,20},{6,23},{7,22},{8,25},{9,... | collective-permute-start | bytes 33800 | tf_op jit(solution)/shard_map/ppermute | solution.py:25
  32.6 1.2 %collective-permute-start.11 = (bf16[1,2,2816]{2,1,0:T(2,128)(2,1)S(1)}, bf16[1,2,2816]{2,1,0:T(2,128)(2,1)S(1)}, u32[]{:S(2)}, u32[]{:S(2)}) collective-permute-start(bf16[1,2,2816]{2,1,0:T(2,128)(2,1)S(1)} %fusion.3), channel_id=1, source_target_pairs={{0,25},{1,24},{2,27},{3,26},{4,29},{5,28},{6,31},{7,30},{8,17},{9,... | collective-permute-start | bytes 33800 | tf_op jit(solution)/shard_map/ppermute | solution.py:25
  33.7 0.6 %collective-permute-start.10 = (bf16[1,2,2816]{2,1,0:T(2,128)(2,1)S(1)}, bf16[1,2,2816]{2,1,0:T(2,128)(2,1)S(1)}, u32[]{:S(2)}, u32[]{:S(2)}) collective-permute-start(bf16[1,2,2816]{2,1,0:T(2,128)(2,1)S(1)} %fusion.3), channel_id=1, source_target_pairs={{0,9},{1,8},{2,11},{3,10},{4,13},{5,12},{6,15},{7,14},{8,1},{9,0},... | collective-permute-start | bytes 33800 | tf_op jit(solution)/shard_map/ppermute | solution.py:25
  34.3 1.6 %fusion.10 = f32[640,640]{1,0:T(8,128)} fusion(bf16[2,640]{1,0:T(2,128)(2,1)S(1)} %get-tuple-element.58, bf16[2,1280]{1,0:T(2,128)(2,1)S(1)} %get-tuple-element.59, s32[]{:T(128)S(6)} %select_n.68), kind=kOutput, calls=%fused_computation.26 | convolution fusion | flops 1638400 | bytes 1643524 | tf_op jit(solution)/shard_map/oh,od->hd/dot_general | solution.py:334
  35.9 1.6 %collective-permute-done.11 = bf16[1,2,2816]{2,1,0:T(2,128)(2,1)S(1)} collective-permute-done((bf16[1,2,2816]{2,1,0:T(2,128)(2,1)S(1)}, bf16[1,2,2816]{2,1,0:T(2,128)(2,1)S(1)}, u32[]{:S(2)}, u32[]{:S(2)}) %collective-permute-start.11) | collective-permute-done | bytes 11296 | tf_op jit(solution)/shard_map/ppermute | solution.py:25
  37.7 1.1 %score_grads.1 = (bf16[2,512]{1,0:T(2,128)(2,1)S(1)}, bf16[2,512]{1,0:T(2,128)(2,1)S(1)}, f32[2,1280]{1,0:T(2,128)S(1)}) custom-call(f32[1]{0:T(128)S(6)} %copy.11.scale_ref, f32[2,2816]{1,0:T(2,128)S(1)} %get-tuple-element.62.slots_ref, f32[1,128]{1,0:T(1,128)S(1)} %constant_dynamic-slice_fusion.1.totals_ref, bf16[512,1280]{1,0:T(8,128)(2,1)S(1)} %bitcast.36, ...), custom_call_target="tpu_custom_call" | custom-call | tf_op jit(solution)/shard_map/score_grads/pallas_call | solution.py:335
  38.8 0.2 collective-permute-start.13
  39.0 0.7 %multiply_reduce_fusion = (f32[512]{0:T(512)S(1)}, f32[512,1280]{1,0:T(8,128)S(1)}) fusion(f32[512]{0:T(512)S(1)} %copy-done.8, bf16[1,512,1280]{2,1,0:T(8,128)(2,1)S(1)} %copy-done, bf16[2,512]{1,0:T(2,128)(2,1)S(1)} %get-tuple-element.55, f32[2]{0:T(128)S(1)} %copy-done.9, bf16[1280,2]{0,1:T(2,128)(2,1)S(1)} %copy-done.4), kind=kOutput, calls=%fused_computation.5 | convolution fusion | flops 5250048 | bytes 3943432 | tf_op jit(solution)/shard_map/sn,sd->nd/dot_general | solution.py:368
  39.8 0.2 collective-permute-done.13
  40.0 2.3 %collective-permute-start.15 = (f32[1,2,1280]{2,1,0:T(2,128)S(1)}, f32[1,2,1280]{2,1,0:T(2,128)S(1)}, u32[]{:S(2)}, u32[]{:S(2)}) collective-permute-start(f32[1,2,1280]{2,1,0:T(2,128)S(1)} %add_bitcast_fusion.2), channel_id=1, source_target_pairs={{0,7},{1,6},{2,5},{3,4},{4,3},{5,2},{6,1},{7,0},{8,15},{9,14},{10,... | collective-permute-start | bytes 30728 | tf_op jit(solution)/shard_map/ppermute | solution.py:25
  42.2 0.5 collective-permute-start.16
  42.7 0.4 collective-permute-start.14
  43.1 2.0 %fusion.1 = bf16[1,512,1280]{2,1,0:T(8,128)(2,1)} fusion(bf16[2,512]{1,0:T(2,128)(2,1)S(1)} %get-tuple-element.53, f32[512,1280]{1,0:T(8,128)S(1)} %get-tuple-element.67, f32[512]{0:T(512)S(1)} %get-tuple-element.66, f32[512]{0:T(512)S(1)} %copy-done.8, bf16[2,2816]{1,0:T(2,128)(2,1)S(1)} %get-tuple-element.61, bf16[1,512,1280]{2,1,0:T(8,128)(2,1)S(1)} %copy-done), kind=kOutput, calls=%fused_computation.3 | convolution fusion | flops 7208960 | bytes 5254144 | tf_op jit(solution)/shard_map/sn,sd->nd/dot_general | solution.py:369
  45.0 0.3 collective-permute-done.16
  45.3 0.5 collective-permute-done.14
  45.8 0.6 %collective-permute-start.17 = (f32[1,2,1280]{2,1,0:T(2,128)S(1)}, f32[1,2,1280]{2,1,0:T(2,128)S(1)}, u32[]{:S(2)}, u32[]{:S(2)}) collective-permute-start(f32[1,2,1280]{2,1,0:T(2,128)S(1)} %add_add_fusion.3.refs_0_), channel_id=1, source_target_pairs={{0,17},{1,16},{2,19},{3,18},{4,21},{5,20},{6,23},{7,22},{8,25},{9,... | collective-permute-start | bytes 30728 | tf_op jit(solution)/shard_map/ppermute | solution.py:25
  46.4 1.5 %collective-permute-start.18 = (f32[1,2,1280]{2,1,0:T(2,128)S(1)}, f32[1,2,1280]{2,1,0:T(2,128)S(1)}, u32[]{:S(2)}, u32[]{:S(2)}) collective-permute-start(f32[1,2,1280]{2,1,0:T(2,128)S(1)} %add_add_fusion.3.refs_0_), channel_id=1, source_target_pairs={{0,25},{1,24},{2,27},{3,26},{4,29},{5,28},{6,31},{7,30},{8,17},{9,... | collective-permute-start | bytes 30728 | tf_op jit(solution)/shard_map/ppermute | solution.py:25
  47.9 0.9 %collective-permute-start.19 = (f32[1,2,1280]{2,1,0:T(2,128)S(1)}, f32[1,2,1280]{2,1,0:T(2,128)S(1)}, u32[]{:S(2)}, u32[]{:S(2)}) collective-permute-start(f32[1,2,1280]{2,1,0:T(2,128)S(1)} %add_add_fusion.3.refs_0_), channel_id=1, source_target_pairs={{0,9},{1,8},{2,11},{3,10},{4,13},{5,12},{6,15},{7,14},{8,1},{9,0},... | collective-permute-start | bytes 30728 | tf_op jit(solution)/shard_map/ppermute | solution.py:25
  48.9 1.6 %fusion.2 = bf16[1,512,1280]{2,1,0:T(8,128)(2,1)} fusion(bf16[2,512]{1,0:T(2,128)(2,1)S(1)} %get-tuple-element.33, bf16[2,2816]{1,0:T(2,128)(2,1)S(1)} %get-tuple-element.61), kind=kOutput, calls=%fused_computation.4 | convolution fusion | flops 3276800 | bytes 1317888 | tf_op jit(solution)/shard_map/sn,sd->nd/dot_general | solution.py:367
  50.5 0.9 %collective-permute-done.18.refs_2_ = f32[1,2,1280]{2,1,0:T(2,128)S(1)} collective-permute-done((f32[1,2,1280]{2,1,0:T(2,128)S(1)}, f32[1,2,1280]{2,1,0:T(2,128)S(1)}, u32[]{:S(2)}, u32[]{:S(2)}) %collective-permute-start.18) | collective-permute-done | bytes 10272 | tf_op jit(solution)/shard_map/ppermute | solution.py:25
  51.3 0.8 %finish.1 = f32[2,1280]{1,0:T(2,128)} custom-call(bf16[2,1280]{1,0:T(2,128)(2,1)S(1)} %bitcast.41, f32[1,2,1280]{2,1,0:T(2,128)S(1)} %add_add_fusion.3.refs_0_, f32[1,2,1280]{2,1,0:T(2,128)S(1)} %collective-permute-done.17.refs_1_, f32[1,2,1280]{2,1,0:T(2,128)S(1)} %collective-permute-done.18.refs_2_, f32[1,2,1280]{2,1,0:T(2,128)S(1)} %collective-permute-done.19.refs_3_), custom_call_target="tpu_custom_call" | custom-call | tf_op jit(solution)/shard_map/finish/pallas_call | solution.py:354
  (44 shorter events, 0.5 us)
Async XLA Ops:
  0.6 4.9 %copy-start.4 = (bf16[1280,2]{0,1:T(2,128)(2,1)S(1)}, bf16[1280,2]{0,1:T(2,128)(2,1)}, u32[]{:S(2)}) copy-start(bf16[1280,2]{0,1:T(2,128)(2,1)} %param.8) | copy-start | bytes 15364
  4.0 1.1 %copy-start.2 = (bf16[512,1280]{1,0:T(8,128)(2,1)}, bf16[512,1280]{1,0:T(8,128)(2,1)S(1)}, u32[]{:S(2)}) copy-start(bf16[512,1280]{1,0:T(8,128)(2,1)S(1)} %get-tuple-element.51.norm_ref) | copy-start | bytes 3932164
  5.1 1.3 %collective-permute-start = (bf16[2,2816]{1,0:T(2,128)(2,1)S(1)}, bf16[2,2816]{1,0:T(2,128)(2,1)S(1)}, u32[]{:S(2)}, u32[]{:S(2)}) collective-permute-start(bf16[2,2816]{1,0:T(2,128)(2,1)S(1)} %get-tuple-element.34), channel_id=1, source_target_pairs={{0,1},{1,0},{2,3},{3,2},{4,5},{5,4},{6,7},{7,6},{8,9},{9,8},{10,11... | collective-permute-start | bytes 33800 | tf_op jit(solution)/shard_map/ppermute | solution.py:29
  6.5 6.5 %copy-start.5 = (bf16[2,2,2816]{2,1,0:T(2,128)(2,1)}, bf16[2,2,2816]{2,1,0:T(2,128)(2,1)S(1)}, u32[]{:S(2)}) copy-start(bf16[2,2,2816]{2,1,0:T(2,128)(2,1)S(1)} %broadcast_select_fusion) | copy-start | bytes 67588
  7.1 7.8 %collective-permute-start.3 = (bf16[1,2,2816]{2,1,0:T(2,128)(2,1)}, bf16[1,2,2816]{2,1,0:T(2,128)(2,1)}, u32[]{:S(2)}, u32[]{:S(2)}) collective-permute-start(bf16[1,2,2816]{2,1,0:T(2,128)(2,1)} %get-tuple-element.64), channel_id=1, source_target_pairs={{0,17},{1,16},{2,19},{3,18},{4,21},{5,20},{6,23},{7,22},{8,25},{9,... | collective-permute-start | bytes 33800 | tf_op jit(solution)/shard_map/ppermute | solution.py:25
  10.8 5.2 %collective-permute-start.2 = (bf16[1,2,2816]{2,1,0:T(2,128)(2,1)}, bf16[1,2,2816]{2,1,0:T(2,128)(2,1)}, u32[]{:S(2)}, u32[]{:S(2)}) collective-permute-start(bf16[1,2,2816]{2,1,0:T(2,128)(2,1)} %get-tuple-element.65), channel_id=1, source_target_pairs={{0,25},{1,24},{2,27},{3,26},{4,29},{5,28},{6,31},{7,30},{8,17},{9,... | collective-permute-start | bytes 33800 | tf_op jit(solution)/shard_map/ppermute | solution.py:25
  12.1 3.9 %collective-permute-start.1 = (bf16[1,2,2816]{2,1,0:T(2,128)(2,1)}, bf16[1,2,2816]{2,1,0:T(2,128)(2,1)}, u32[]{:S(2)}, u32[]{:S(2)}) collective-permute-start(bf16[1,2,2816]{2,1,0:T(2,128)(2,1)} %get-tuple-element.63), channel_id=1, source_target_pairs={{0,9},{1,8},{2,11},{3,10},{4,13},{5,12},{6,15},{7,14},{8,1},{9,0},... | collective-permute-start | bytes 33800 | tf_op jit(solution)/shard_map/ppermute | solution.py:25
  12.9 3.1 %copy-start.6 = (bf16[2,2,2816]{2,1,0:T(2,128)(2,1)S(1)}, bf16[2,2,2816]{2,1,0:T(2,128)(2,1)}, u32[]{:S(2)}) copy-start(bf16[2,2,2816]{2,1,0:T(2,128)(2,1)} %copy-done.5) | copy-start | bytes 67588
  17.4 4.5 %collective-permute-start.5 = (f32[1,2,2816]{2,1,0:T(2,128)}, f32[1,2,2816]{2,1,0:T(2,128)}, u32[]{:S(2)}, u32[]{:S(2)}) collective-permute-start(f32[1,2,2816]{2,1,0:T(2,128)} %add_add_fusion.2), channel_id=1, source_target_pairs={{0,7},{1,6},{2,5},{3,4},{4,3},{5,2},{6,1},{7,0},{8,15},{9,14},{10,... | collective-permute-start | bytes 67592 | tf_op jit(solution)/shard_map/ppermute | solution.py:25
  19.8 3.5 %collective-permute-start.6 = (f32[1,2,2816]{2,1,0:T(2,128)}, f32[1,2,2816]{2,1,0:T(2,128)}, u32[]{:S(2)}, u32[]{:S(2)}) collective-permute-start(f32[1,2,2816]{2,1,0:T(2,128)} %add_add_fusion.2), channel_id=1, source_target_pairs={{0,5},{1,4},{2,7},{3,6},{4,1},{5,0},{6,3},{7,2},{8,13},{9,12},{10,... | collective-permute-start | bytes 67592 | tf_op jit(solution)/shard_map/ppermute | solution.py:25
  20.1 3.5 %collective-permute-start.4 = (f32[1,2,2816]{2,1,0:T(2,128)}, f32[1,2,2816]{2,1,0:T(2,128)}, u32[]{:S(2)}, u32[]{:S(2)}) collective-permute-start(f32[1,2,2816]{2,1,0:T(2,128)} %add_add_fusion.2), channel_id=1, source_target_pairs={{0,3},{1,2},{2,1},{3,0},{4,7},{5,6},{6,5},{7,4},{8,11},{9,10},{10,... | collective-permute-start | bytes 67592 | tf_op jit(solution)/shard_map/ppermute | solution.py:25
  21.9 9.2 %copy-start.7 = (pred[2816]{0:T(1024)(128)(4,1)S(1)}, pred[2816]{0:T(1024)(128)(4,1)}, u32[]{:S(2)}) copy-start(pred[2816]{0:T(1024)(128)(4,1)} %iota_compare_fusion) | copy-start | bytes 8452
  24.5 13.2 %copy-start.3 = (bf16[512,1280]{1,0:T(8,128)(2,1)S(1)}, bf16[512,1280]{1,0:T(8,128)(2,1)}, u32[]{:S(2)}) copy-start(bf16[512,1280]{1,0:T(8,128)(2,1)} %copy-done.2) | copy-start | bytes 3932164
  26.0 11.6 %copy-start.10 = (pred[2]{0:T(512)(128)(4,1)S(1)}, pred[2]{0:T(512)(128)(4,1)}, u32[]{:S(2)}) copy-start(pred[2]{0:T(512)(128)(4,1)} %iota_compare_fusion.1) | copy-start | bytes 10
  26.0 11.7 %copy-start = (bf16[1,512,1280]{2,1,0:T(8,128)(2,1)S(1)}, bf16[1,512,1280]{2,1,0:T(8,128)(2,1)}, u32[]{:S(2)}) copy-start(bf16[1,512,1280]{2,1,0:T(8,128)(2,1)} %param.6) | copy-start | bytes 3932164
  26.0 11.7 %copy-start.1 = (bf16[1,512,1280]{2,1,0:T(8,128)(2,1)S(1)}, bf16[1,512,1280]{2,1,0:T(8,128)(2,1)}, u32[]{:S(2)}) copy-start(bf16[1,512,1280]{2,1,0:T(8,128)(2,1)} %param.7) | copy-start | bytes 3932164
  26.0 4.8 %collective-permute-start.8 = (f32[1,2,2816]{2,1,0:T(2,128)S(1)}, f32[1,2,2816]{2,1,0:T(2,128)S(1)}, u32[]{:S(2)}, u32[]{:S(2)}) collective-permute-start(f32[1,2,2816]{2,1,0:T(2,128)S(1)} %bitcast.42), channel_id=1, source_target_pairs={{0,7},{1,6},{2,5},{3,4},{4,3},{5,2},{6,1},{7,0},{8,15},{9,14},{10,... | collective-permute-start | bytes 67592 | tf_op jit(solution)/shard_map/ppermute | solution.py:25
  27.5 3.6 %collective-permute-start.9 = (f32[1,2,2816]{2,1,0:T(2,128)S(1)}, f32[1,2,2816]{2,1,0:T(2,128)S(1)}, u32[]{:S(2)}, u32[]{:S(2)}) collective-permute-start(f32[1,2,2816]{2,1,0:T(2,128)S(1)} %bitcast.43), channel_id=1, source_target_pairs={{0,5},{1,4},{2,7},{3,6},{4,1},{5,0},{6,3},{7,2},{8,13},{9,12},{10,... | collective-permute-start | bytes 67592 | tf_op jit(solution)/shard_map/ppermute | solution.py:25
  27.8 3.2 %collective-permute-start.7 = (f32[1,2,2816]{2,1,0:T(2,128)S(1)}, f32[1,2,2816]{2,1,0:T(2,128)S(1)}, u32[]{:S(2)}, u32[]{:S(2)}) collective-permute-start(f32[1,2,2816]{2,1,0:T(2,128)S(1)} %bitcast.44), channel_id=1, source_target_pairs={{0,3},{1,2},{2,1},{3,0},{4,7},{5,6},{6,5},{7,4},{8,11},{9,10},{10,... | collective-permute-start | bytes 67592 | tf_op jit(solution)/shard_map/ppermute | solution.py:25
  31.1 7.9 %copy-start.8 = (f32[512]{0:T(512)S(1)}, f32[512]{0:T(512)}, u32[]{:S(2)}) copy-start(f32[512]{0:T(512)} %reduce) | copy-start | bytes 6148
  31.2 7.9 %copy-start.9 = (f32[2]{0:T(128)S(1)}, f32[2]{0:T(128)}, u32[]{:S(2)}) copy-start(f32[2]{0:T(128)} %add_rsqrt_fusion) | copy-start | bytes 28
  31.2 4.7 %collective-permute-start.12 = (bf16[1,2,2816]{2,1,0:T(2,128)(2,1)S(1)}, bf16[1,2,2816]{2,1,0:T(2,128)(2,1)S(1)}, u32[]{:S(2)}, u32[]{:S(2)}) collective-permute-start(bf16[1,2,2816]{2,1,0:T(2,128)(2,1)S(1)} %fusion.3), channel_id=1, source_target_pairs={{0,17},{1,16},{2,19},{3,18},{4,21},{5,20},{6,23},{7,22},{8,25},{9,... | collective-permute-start | bytes 33800 | tf_op jit(solution)/shard_map/ppermute | solution.py:25
  32.6 4.9 %collective-permute-start.11 = (bf16[1,2,2816]{2,1,0:T(2,128)(2,1)S(1)}, bf16[1,2,2816]{2,1,0:T(2,128)(2,1)S(1)}, u32[]{:S(2)}, u32[]{:S(2)}) collective-permute-start(bf16[1,2,2816]{2,1,0:T(2,128)(2,1)S(1)} %fusion.3), channel_id=1, source_target_pairs={{0,25},{1,24},{2,27},{3,26},{4,29},{5,28},{6,31},{7,30},{8,17},{9,... | collective-permute-start | bytes 33800 | tf_op jit(solution)/shard_map/ppermute | solution.py:25
  33.7 3.8 %collective-permute-start.10 = (bf16[1,2,2816]{2,1,0:T(2,128)(2,1)S(1)}, bf16[1,2,2816]{2,1,0:T(2,128)(2,1)S(1)}, u32[]{:S(2)}, u32[]{:S(2)}) collective-permute-start(bf16[1,2,2816]{2,1,0:T(2,128)(2,1)S(1)} %fusion.3), channel_id=1, source_target_pairs={{0,9},{1,8},{2,11},{3,10},{4,13},{5,12},{6,15},{7,14},{8,1},{9,0},... | collective-permute-start | bytes 33800 | tf_op jit(solution)/shard_map/ppermute | solution.py:25
  38.8 1.2 %collective-permute-start.13 = (f32[2,1280]{1,0:T(2,128)S(1)}, f32[2,1280]{1,0:T(2,128)S(1)}, u32[]{:S(2)}, u32[]{:S(2)}) collective-permute-start(f32[2,1280]{1,0:T(2,128)S(1)} %get-tuple-element.60), channel_id=1, source_target_pairs={{0,1},{1,0},{2,3},{3,2},{4,5},{5,4},{6,7},{7,6},{8,9},{9,8},{10,11... | collective-permute-start | bytes 30728 | tf_op jit(solution)/shard_map/ppermute | solution.py:29
  40.0 5.1 %collective-permute-start.15 = (f32[1,2,1280]{2,1,0:T(2,128)S(1)}, f32[1,2,1280]{2,1,0:T(2,128)S(1)}, u32[]{:S(2)}, u32[]{:S(2)}) collective-permute-start(f32[1,2,1280]{2,1,0:T(2,128)S(1)} %add_bitcast_fusion.2), channel_id=1, source_target_pairs={{0,7},{1,6},{2,5},{3,4},{4,3},{5,2},{6,1},{7,0},{8,15},{9,14},{10,... | collective-permute-start | bytes 30728 | tf_op jit(solution)/shard_map/ppermute | solution.py:25
  42.2 3.1 %collective-permute-start.16 = (f32[1,2,1280]{2,1,0:T(2,128)S(1)}, f32[1,2,1280]{2,1,0:T(2,128)S(1)}, u32[]{:S(2)}, u32[]{:S(2)}) collective-permute-start(f32[1,2,1280]{2,1,0:T(2,128)S(1)} %add_bitcast_fusion.2), channel_id=1, source_target_pairs={{0,5},{1,4},{2,7},{3,6},{4,1},{5,0},{6,3},{7,2},{8,13},{9,12},{10,... | collective-permute-start | bytes 30728 | tf_op jit(solution)/shard_map/ppermute | solution.py:25
  42.7 3.1 %collective-permute-start.14 = (f32[1,2,1280]{2,1,0:T(2,128)S(1)}, f32[1,2,1280]{2,1,0:T(2,128)S(1)}, u32[]{:S(2)}, u32[]{:S(2)}) collective-permute-start(f32[1,2,1280]{2,1,0:T(2,128)S(1)} %add_bitcast_fusion.2), channel_id=1, source_target_pairs={{0,3},{1,2},{2,1},{3,0},{4,7},{5,6},{6,5},{7,4},{8,11},{9,10},{10,... | collective-permute-start | bytes 30728 | tf_op jit(solution)/shard_map/ppermute | solution.py:25
  45.8 4.7 %collective-permute-start.17 = (f32[1,2,1280]{2,1,0:T(2,128)S(1)}, f32[1,2,1280]{2,1,0:T(2,128)S(1)}, u32[]{:S(2)}, u32[]{:S(2)}) collective-permute-start(f32[1,2,1280]{2,1,0:T(2,128)S(1)} %add_add_fusion.3.refs_0_), channel_id=1, source_target_pairs={{0,17},{1,16},{2,19},{3,18},{4,21},{5,20},{6,23},{7,22},{8,25},{9,... | collective-permute-start | bytes 30728 | tf_op jit(solution)/shard_map/ppermute | solution.py:25
  46.4 4.9 %collective-permute-start.18 = (f32[1,2,1280]{2,1,0:T(2,128)S(1)}, f32[1,2,1280]{2,1,0:T(2,128)S(1)}, u32[]{:S(2)}, u32[]{:S(2)}) collective-permute-start(f32[1,2,1280]{2,1,0:T(2,128)S(1)} %add_add_fusion.3.refs_0_), channel_id=1, source_target_pairs={{0,25},{1,24},{2,27},{3,26},{4,29},{5,28},{6,31},{7,30},{8,17},{9,... | collective-permute-start | bytes 30728 | tf_op jit(solution)/shard_map/ppermute | solution.py:25
  47.9 3.4 %collective-permute-start.19 = (f32[1,2,1280]{2,1,0:T(2,128)S(1)}, f32[1,2,1280]{2,1,0:T(2,128)S(1)}, u32[]{:S(2)}, u32[]{:S(2)}) collective-permute-start(f32[1,2,1280]{2,1,0:T(2,128)S(1)} %add_add_fusion.3.refs_0_), channel_id=1, source_target_pairs={{0,9},{1,8},{2,11},{3,10},{4,13},{5,12},{6,15},{7,14},{8,1},{9,0},... | collective-permute-start | bytes 30728 | tf_op jit(solution)/shard_map/ppermute | solution.py:25

commit v18 on v12

--- a/solution.py
+++ b/solution.py
@@ -31,15 +31,11 @@
 
 def of_clips(value):
     clips = lax.axis_size("dp")
-    clip = lax.axis_index("dp")
-    got = [value] + [hop(value, step) for step in range(1, clips)]
-    ordered = []
-    for index in range(clips):
-        picked = got[0]
-        for step in range(1, clips):
-            picked = jnp.where(clip ^ step == index, got[step], picked)
-        ordered.append(picked)
-    return ordered
+    apart = lax.broadcasted_iota(jnp.int32, (1, clips, 1), 1) ^ lax.axis_index("dp")
+    merged = value[:, None]
+    for step in range(1, clips):
+        merged = jnp.where(apart == step, hop(value, step)[:, None], merged)
+    return merged
 
 
 def rounds(size):
@@ -53,9 +49,9 @@
 
 def added(terms, masks):
     if len(masks) == 1:
-        return terms[masks[0]] + terms[0]
+        return terms[0] + terms[masks[0]]
     low, high = masks
-    return (terms[0] + terms[low]) + (terms[low | high] + terms[high])
+    return (terms[0] + terms[low]) + (terms[high] + terms[low | high])
 
 
 def sum_to_owner(value, group):
@@ -128,8 +124,10 @@
     ]
     for copy in tok_copies + [phi_copy] + cot_copies:
         copy.start()
-    for copy, piece in zip(tok_copies, pieces):
-        copy.wait()
+    for index in range(0, blocks, 2):
+        for copy in tok_copies[index : index + 2]:
+            copy.wait()
+        piece = pl.ds(index * rows, 2 * rows)
         tok_f32 = tok_buf[piece, :].astype(f32)
         tok_scale = lax.rsqrt(jnp.sum(tok_f32 * tok_f32, axis=1, keepdims=True) + epsilon)
         norm_ref[piece, :] = (tok_f32 * tok_scale).astype(bf16)
@@ -281,7 +279,7 @@
         compiler_params=params,
         name="token_sums",
     )(logit_scale, in_place(phi), in_place(tok_in), in_place(tok_cot))
-    message = jnp.stack(of_clips(message), axis=1)
+    message = of_clips(message)
     message, expert_in, expert_out = lax.optimization_barrier((message, expert_in, expert_out))
     expert_in, expert_out = pl.pallas_call(
         fetch,
@@ -332,7 +330,10 @@
         compiler_params=params,
         name="score_grads",
     )(logit_scale, slots, totals, tok_in, tok_cot, tok_norm, exp_scores)
-    phi_sum = sum(of_clips(phi_part[None]))
+    phi_sum = phi_part
+    for step in range(1, clips):
+        phi_sum = phi_sum + hop(phi_part, step)
+    phi_sum = phi_sum[None]
     *earlier, final = rounds(size)
     for pair in earlier:
         phi_sum = added(round_terms(phi_sum, pair), pair)
@@ -343,7 +344,7 @@
         out_shape=jax.ShapeDtypeStruct((experts, width), f32),
         compiler_params=params,
         name="finish",
-    )(phi, terms.pop(0), *[terms[mask] for mask in sorted(terms, reverse=True)])
+    )(phi, terms[0], *[terms[mask] for mask in [*final[1:], sum(final), final[0]][-len(terms) + 1 :]])
     phi_f32 = phi.astype(f32)
     phi_scale = lax.rsqrt(jnp.sum(phi_f32 * phi_f32, axis=1, keepdims=True) + epsilon)
     phi_unit = phi_f32 * phi_scale

time: 48.7 us -> 48.3 us (level)
  starting transfers between devices: 23.4 us -> 21.9 us
  waiting for transfers between devices: 7.35 us -> 8.47 us
    ppermute x18, starting transfers between devices: 22.7 us -> 21.3 us  [exchange(): return lax.ppermute(value, AXES, pairs)]
    ppermute x18, waiting for transfers between devices: 6.37 us -> 7.47 us  [exchange(): return lax.ppermute(value, AXES, pairs)]
  transfers between devices with their start and end apart: 20 -> 20, of which waited for: 13 -> 8; matrix products, arithmetic and copies ran while one was open for 16% -> 16% of each run, Pallas kernels for 4% -> 4%
where the time goes in v18:
time: 48.3 us; the launch traced here: 48.1 us
  starting transfers between devices  21.9 us (45%)
  waiting for transfers between devices  8.47 us (18%)
  Pallas kernels  8.05 us (17%)
  matrix products  7.52 us (16%)
  between operations  1.46 us (3%)
  other arithmetic  0.56 us (1%)
    ppermute x18, starting transfers between devices, exchange(): return lax.ppermute(value, AXES, pairs)  21.3 us
    ppermute x18, waiting for transfers between devices, exchange(): return lax.ppermute(value, AXES, pairs)  7.47 us
    pallas_call x1, Pallas kernels, per_device(): pl.pallas_call(token_sums, in_specs=[scalar, in_hbm, in_hbm, in_hbm], out...  2.71 us
    dot_general x1, matrix products, per_device(): jnp.einsum('sn,sd->nd', dispatch, slot_dx, preferred_element_type=f32)  1.98 us
    pallas_call x1, Pallas kernels, per_device(): pl.pallas_call(fetch, in_specs=[in_hbm] * 2, out_specs=[in_vmem] * 2, out...  1.94 us
    dot_general x1, matrix products, per_device(): jnp.einsum('sn,sd->nd', combine, slot_y, preferred_element_type=f32)  1.61 us
    dot_general x1, matrix products, per_device(): jnp.einsum('od,oh->dh', mine_x, pre_grad, preferred_element_type=f32)  1.59 us
    dot_general x1, matrix products, per_device(): jnp.einsum('oh,od->hd', hidden, mine_cot, preferred_element_type=f32)  1.59 us
  transfers between devices with their start and end apart: 20, of which 8 were waited for; matrix products, arithmetic and copies ran while one was open for 16% of the time, Pallas kernels for 4%

profile of v18, /device:TPU:0, one launch (start us, length us, event | category | flops | bytes accessed | tf_op | source)
XLA Modules:
  0.0 48.1 jit_solution(3750826625885848710)
XLA Ops:
  1.3 2.7 %token_sums.1 = (f32[2,2688]{1,0:T(2,128)S(1)}, f32[2,512]{1,0:T(2,128)S(1)}, bf16[2,512]{1,0:T(2,128)(2,1)S(1)}, f32[512,1]{1,0:T(8,128)S(1)}, bf16[512,1280]{1,0:T(8,128)(2,1)S(1)}) custom-call(f32[1]{0:T(128)S(6)} %copy.11.scale_ref, bf16[2,1280]{1,0:T(2,128)(2,1)} %bitcast.40, bf16[512,1280]{1,0:T(8,128)(2,1)} %bitcast.36, bf16[512,1280]{1,0:T(8,128)(2,1)} %bitcast.38), custom_call_target="tpu_custom_call" | custom-call | tf_op jit(solution)/shard_map/token_sums/pallas_call | solution.py:262
  4.0 0.5 %collective-permute-start = (f32[2,2688]{1,0:T(2,128)S(1)}, f32[2,2688]{1,0:T(2,128)S(1)}, u32[]{:S(2)}, u32[]{:S(2)}) collective-permute-start(f32[2,2688]{1,0:T(2,128)S(1)} %get-tuple-element.27), channel_id=1, source_target_pairs={{0,1},{1,0},{2,3},{3,2},{4,5},{5,4},{6,7},{7,6},{8,9},{9,8},{10,11... | collective-permute-start | bytes 64520 | tf_op jit(solution)/shard_map/ppermute | solution.py:29
  4.5 0.1 fusion.3
  4.7 0.7 %collective-permute-done = f32[2,2688]{1,0:T(2,128)S(1)} collective-permute-done((f32[2,2688]{1,0:T(2,128)S(1)}, f32[2,2688]{1,0:T(2,128)S(1)}, u32[]{:S(2)}, u32[]{:S(2)}) %collective-permute-start) | collective-permute-done | bytes 21536 | tf_op jit(solution)/shard_map/ppermute | solution.py:29
  5.4 0.1 broadcast_select_fusion
  5.5 3.8 %collective-permute-start.2 = (f32[1,2,2688]{2,1,0:T(2,128)S(1)}, f32[1,2,2688]{2,1,0:T(2,128)S(1)}, u32[]{:S(2)}, u32[]{:S(2)}) collective-permute-start(f32[1,2,2688]{2,1,0:T(2,128)S(1)} %get-tuple-element.51), channel_id=1, source_target_pairs={{0,17},{1,16},{2,19},{3,18},{4,21},{5,20},{6,23},{7,22},{8,25},{9,... | collective-permute-start | bytes 64520 | tf_op jit(solution)/shard_map/ppermute | solution.py:25
  9.3 1.3 %collective-permute-start.3 = (f32[1,2,2688]{2,1,0:T(2,128)S(1)}, f32[1,2,2688]{2,1,0:T(2,128)S(1)}, u32[]{:S(2)}, u32[]{:S(2)}) collective-permute-start(f32[1,2,2688]{2,1,0:T(2,128)S(1)} %get-tuple-element.50), channel_id=1, source_target_pairs={{0,25},{1,24},{2,27},{3,26},{4,29},{5,28},{6,31},{7,30},{8,17},{9,... | collective-permute-start | bytes 64520 | tf_op jit(solution)/shard_map/ppermute | solution.py:25
  10.6 0.2 collective-permute-start.1
  10.8 0.0 collective-permute-done.2
  10.8 3.6 %collective-permute-done.3 = f32[1,2,2688]{2,1,0:T(2,128)S(1)} collective-permute-done((f32[1,2,2688]{2,1,0:T(2,128)S(1)}, f32[1,2,2688]{2,1,0:T(2,128)S(1)}, u32[]{:S(2)}, u32[]{:S(2)}) %collective-permute-start.3) | collective-permute-done | bytes 21536 | tf_op jit(solution)/shard_map/ppermute | solution.py:25
  14.4 0.0 collective-permute-done.1
  14.4 1.6 %collective-permute-start.5 = (f32[1,2,2688]{2,1,0:T(2,128)S(1)}, f32[1,2,2688]{2,1,0:T(2,128)S(1)}, u32[]{:S(2)}, u32[]{:S(2)}) collective-permute-start(f32[1,2,2688]{2,1,0:T(2,128)S(1)} %add_add_fusion.1), channel_id=1, source_target_pairs={{0,5},{1,4},{2,7},{3,6},{4,1},{5,0},{6,3},{7,2},{8,13},{9,12},{10,... | collective-permute-start | bytes 64520 | tf_op jit(solution)/shard_map/ppermute | solution.py:25
  16.0 1.1 %collective-permute-start.6 = (f32[1,2,2688]{2,1,0:T(2,128)S(1)}, f32[1,2,2688]{2,1,0:T(2,128)S(1)}, u32[]{:S(2)}, u32[]{:S(2)}) collective-permute-start(f32[1,2,2688]{2,1,0:T(2,128)S(1)} %add_add_fusion.1), channel_id=1, source_target_pairs={{0,7},{1,6},{2,5},{3,4},{4,3},{5,2},{6,1},{7,0},{8,15},{9,14},{10,... | collective-permute-start | bytes 64520 | tf_op jit(solution)/shard_map/ppermute | solution.py:25
  17.1 0.6 %collective-permute-start.4 = (f32[1,2,2688]{2,1,0:T(2,128)S(1)}, f32[1,2,2688]{2,1,0:T(2,128)S(1)}, u32[]{:S(2)}, u32[]{:S(2)}) collective-permute-start(f32[1,2,2688]{2,1,0:T(2,128)S(1)} %add_add_fusion.1), channel_id=1, source_target_pairs={{0,3},{1,2},{2,1},{3,0},{4,7},{5,6},{6,5},{7,4},{8,11},{9,10},{10,... | collective-permute-start | bytes 64520 | tf_op jit(solution)/shard_map/ppermute | solution.py:25
  17.7 0.1 reduce
  17.9 1.9 %fetch_weights.1 = (bf16[1280,640]{1,0:T(8,128)(2,1)S(1)}, bf16[640,1280]{1,0:T(8,128)(2,1)S(1)}) custom-call(bf16[1280,640]{1,0:T(8,128)(2,1)} %in_ref, bf16[640,1280]{1,0:T(8,128)(2,1)} %out_ref), custom_call_target="tpu_custom_call" | custom-call | bytes 6553600 | tf_op jit(solution)/shard_map/fetch_weights/pallas_call | solution.py:284
  19.8 0.3 collective-permute-done.6
  20.1 0.2 collective-permute-done.4
  20.4 1.5 %expert_rows.1 = (f32[2,2688]{1,0:T(2,128)S(1)}, bf16[2,1280]{1,0:T(2,128)(2,1)S(1)}, bf16[2,1280]{1,0:T(2,128)(2,1)S(1)}, bf16[2,640]{1,0:T(2,128)(2,1)S(1)}, bf16[2,640]{1,0:T(2,128)(2,1)S(1)}) custom-call(s32[1]{0:T(128)} %bitcast.3.owned_ref, f32[2,2688]{1,0:T(2,128)S(1)} %add_bitcast_fusion.2.sums_ref, bf16[1280,640]{1,0:T(8,128)(2,1)S(1)} %get-tuple-element.31.in_ref, ...), custom_call_target="tpu_custom_call" | custom-call | tf_op jit(solution)/shard_map/expert_rows/pallas_call | solution.py:301
  21.9 1.6 %collective-permute-start.8 = (f32[1,2,2688]{2,1,0:T(2,128)S(1)}, f32[1,2,2688]{2,1,0:T(2,128)S(1)}, u32[]{:S(2)}, u32[]{:S(2)}) collective-permute-start(f32[1,2,2688]{2,1,0:T(2,128)S(1)} %bitcast.42), channel_id=1, source_target_pairs={{0,5},{1,4},{2,7},{3,6},{4,1},{5,0},{6,3},{7,2},{8,13},{9,12},{10,... | collective-permute-start | bytes 64520 | tf_op jit(solution)/shard_map/ppermute | solution.py:25
  23.5 0.9 %collective-permute-start.9 = (f32[1,2,2688]{2,1,0:T(2,128)S(1)}, f32[1,2,2688]{2,1,0:T(2,128)S(1)}, u32[]{:S(2)}, u32[]{:S(2)}) collective-permute-start(f32[1,2,2688]{2,1,0:T(2,128)S(1)} %bitcast.43), channel_id=1, source_target_pairs={{0,7},{1,6},{2,5},{3,4},{4,3},{5,2},{6,1},{7,0},{8,15},{9,14},{10,... | collective-permute-start | bytes 64520 | tf_op jit(solution)/shard_map/ppermute | solution.py:25
  24.4 0.8 %collective-permute-start.7 = (f32[1,2,2688]{2,1,0:T(2,128)S(1)}, f32[1,2,2688]{2,1,0:T(2,128)S(1)}, u32[]{:S(2)}, u32[]{:S(2)}) collective-permute-start(f32[1,2,2688]{2,1,0:T(2,128)S(1)} %bitcast.44), channel_id=1, source_target_pairs={{0,3},{1,2},{2,1},{3,0},{4,7},{5,6},{6,5},{7,4},{8,11},{9,10},{10,... | collective-permute-start | bytes 64520 | tf_op jit(solution)/shard_map/ppermute | solution.py:25
  25.2 1.6 %fusion.11 = f32[640,640]{1,0:T(8,128)} fusion(bf16[2,640]{1,0:T(2,128)(2,1)S(1)} %get-tuple-element.43, bf16[2,1280]{1,0:T(2,128)(2,1)S(1)} %get-tuple-element.42, s32[]{:T(128)S(6)} %select_n.63), kind=kOutput, calls=%fused_computation.25 | convolution fusion | flops 1638400 | bytes 1643524 | tf_op jit(solution)/shard_map/od,oh->dh/dot_general | solution.py:320
  26.8 0.8 %collective-permute-done.9 = f32[1,2,2688]{2,1,0:T(2,128)S(1)} collective-permute-done((f32[1,2,2688]{2,1,0:T(2,128)S(1)}, f32[1,2,2688]{2,1,0:T(2,128)S(1)}, u32[]{:S(2)}, u32[]{:S(2)}) %collective-permute-start.9) | collective-permute-done | bytes 21536 | tf_op jit(solution)/shard_map/ppermute | solution.py:25
  27.6 1.2 %collective-permute-start.11 = (f32[1,2,2688]{2,1,0:T(2,128)S(1)}, f32[1,2,2688]{2,1,0:T(2,128)S(1)}, u32[]{:S(2)}, u32[]{:S(2)}) collective-permute-start(f32[1,2,2688]{2,1,0:T(2,128)S(1)} %add_add_fusion), channel_id=1, source_target_pairs={{0,17},{1,16},{2,19},{3,18},{4,21},{5,20},{6,23},{7,22},{8,25},{9,... | collective-permute-start | bytes 64520 | tf_op jit(solution)/shard_map/ppermute | solution.py:25
  28.9 0.9 %collective-permute-start.12 = (f32[1,2,2688]{2,1,0:T(2,128)S(1)}, f32[1,2,2688]{2,1,0:T(2,128)S(1)}, u32[]{:S(2)}, u32[]{:S(2)}) collective-permute-start(f32[1,2,2688]{2,1,0:T(2,128)S(1)} %add_add_fusion), channel_id=1, source_target_pairs={{0,25},{1,24},{2,27},{3,26},{4,29},{5,28},{6,31},{7,30},{8,17},{9,... | collective-permute-start | bytes 64520 | tf_op jit(solution)/shard_map/ppermute | solution.py:25
  29.7 1.1 %collective-permute-start.10 = (f32[1,2,2688]{2,1,0:T(2,128)S(1)}, f32[1,2,2688]{2,1,0:T(2,128)S(1)}, u32[]{:S(2)}, u32[]{:S(2)}) collective-permute-start(f32[1,2,2688]{2,1,0:T(2,128)S(1)} %add_add_fusion), channel_id=1, source_target_pairs={{0,9},{1,8},{2,11},{3,10},{4,13},{5,12},{6,15},{7,14},{8,1},{9,0},... | collective-permute-start | bytes 64520 | tf_op jit(solution)/shard_map/ppermute | solution.py:25
  30.8 1.6 %fusion.9 = f32[640,640]{1,0:T(8,128)} fusion(bf16[2,640]{1,0:T(2,128)(2,1)S(1)} %get-tuple-element.44, bf16[2,1280]{1,0:T(2,128)(2,1)S(1)} %get-tuple-element.45, s32[]{:T(128)S(6)} %select_n.63), kind=kOutput, calls=%fused_computation.23 | convolution fusion | flops 1638400 | bytes 1643524 | tf_op jit(solution)/shard_map/oh,od->hd/dot_general | solution.py:321
  32.4 0.0 collective-permute-done.11
  32.4 1.6 %collective-permute-done.12 = f32[1,2,2688]{2,1,0:T(2,128)S(1)} collective-permute-done((f32[1,2,2688]{2,1,0:T(2,128)S(1)}, f32[1,2,2688]{2,1,0:T(2,128)S(1)}, u32[]{:S(2)}, u32[]{:S(2)}) %collective-permute-start.12) | collective-permute-done | bytes 21536 | tf_op jit(solution)/shard_map/ppermute | solution.py:25
  34.0 0.0 collective-permute-done.10
  34.1 0.1 fusion.16
  34.2 1.1 %score_grads.1 = (bf16[2,512]{1,0:T(2,128)(2,1)S(1)}, bf16[2,512]{1,0:T(2,128)(2,1)S(1)}, f32[2,1280]{1,0:T(2,128)S(1)}) custom-call(f32[1]{0:T(128)S(6)} %copy.11.scale_ref, f32[2,2688]{1,0:T(2,128)S(1)} %get-tuple-element.48.slots_ref, f32[1,128]{1,0:T(1,128)S(1)} %constant_dynamic-slice_fusion.1.totals_ref, bf16[512,1280]{1,0:T(8,128)(2,1)S(1)} %bitcast.37, ...), custom_call_target="tpu_custom_call" | custom-call | tf_op jit(solution)/shard_map/score_grads/pallas_call | solution.py:322
  35.3 0.1 collective-permute-start.13
  35.4 0.7 %multiply_reduce_fusion = (f32[512]{0:T(512)S(1)}, f32[512,1280]{1,0:T(8,128)S(1)}) fusion(f32[512]{0:T(512)S(1)} %reduce, bf16[1,512,1280]{2,1,0:T(8,128)(2,1)S(1)} %copy-done, bf16[2,512]{1,0:T(2,128)(2,1)S(1)} %get-tuple-element.41, f32[2]{0:T(128)S(1)} %add_rsqrt_fusion, bf16[1280,2]{0,1:T(2,128)(2,1)S(1)} %copy-done.2), kind=kOutput, calls=%fused_computation.5 | convolution fusion | flops 5250048 | bytes 3943432 | tf_op jit(solution)/shard_map/sn,sd->nd/dot_general | solution.py:355
  36.1 0.3 collective-permute-done.13
  36.5 1.0 %collective-permute-start.15 = (f32[1,2,1280]{2,1,0:T(2,128)S(1)}, f32[1,2,1280]{2,1,0:T(2,128)S(1)}, u32[]{:S(2)}, u32[]{:S(2)}) collective-permute-start(f32[1,2,1280]{2,1,0:T(2,128)S(1)} %add_bitcast_fusion.3), channel_id=1, source_target_pairs={{0,5},{1,4},{2,7},{3,6},{4,1},{5,0},{6,3},{7,2},{8,13},{9,12},{10,... | collective-permute-start | bytes 30728 | tf_op jit(solution)/shard_map/ppermute | solution.py:25
  37.4 1.0 %collective-permute-start.16 = (f32[1,2,1280]{2,1,0:T(2,128)S(1)}, f32[1,2,1280]{2,1,0:T(2,128)S(1)}, u32[]{:S(2)}, u32[]{:S(2)}) collective-permute-start(f32[1,2,1280]{2,1,0:T(2,128)S(1)} %add_bitcast_fusion.3), channel_id=1, source_target_pairs={{0,7},{1,6},{2,5},{3,4},{4,3},{5,2},{6,1},{7,0},{8,15},{9,14},{10,... | collective-permute-start | bytes 30728 | tf_op jit(solution)/shard_map/ppermute | solution.py:25
  38.4 1.1 %collective-permute-start.14 = (f32[1,2,1280]{2,1,0:T(2,128)S(1)}, f32[1,2,1280]{2,1,0:T(2,128)S(1)}, u32[]{:S(2)}, u32[]{:S(2)}) collective-permute-start(f32[1,2,1280]{2,1,0:T(2,128)S(1)} %add_bitcast_fusion.3), channel_id=1, source_target_pairs={{0,3},{1,2},{2,1},{3,0},{4,7},{5,6},{6,5},{7,4},{8,11},{9,10},{10,... | collective-permute-start | bytes 30728 | tf_op jit(solution)/shard_map/ppermute | solution.py:25
  39.5 2.0 %fusion.1 = bf16[1,512,1280]{2,1,0:T(8,128)(2,1)} fusion(bf16[2,512]{1,0:T(2,128)(2,1)S(1)} %get-tuple-element.39, f32[512,1280]{1,0:T(8,128)S(1)} %get-tuple-element.53, f32[512]{0:T(512)S(1)} %get-tuple-element.52, f32[512]{0:T(512)S(1)} %reduce, bf16[2,2688]{1,0:T(2,128)(2,1)S(1)} %get-tuple-element.47, bf16[1,512,1280]{2,1,0:T(8,128)(2,1)S(1)} %copy-done), kind=kOutput, calls=%fused_computation.3 | convolution fusion | flops 7208960 | bytes 5254144 | tf_op jit(solution)/shard_map/sn,sd->nd/dot_general | solution.py:356
  41.5 0.0 collective-permute-done.14
  41.5 0.9 %collective-permute-start.17 = (f32[1,2,1280]{2,1,0:T(2,128)S(1)}, f32[1,2,1280]{2,1,0:T(2,128)S(1)}, u32[]{:S(2)}, u32[]{:S(2)}) collective-permute-start(f32[1,2,1280]{2,1,0:T(2,128)S(1)} %add_add_fusion.2.refs_0_), channel_id=1, source_target_pairs={{0,17},{1,16},{2,19},{3,18},{4,21},{5,20},{6,23},{7,22},{8,25},{9,... | collective-permute-start | bytes 30728 | tf_op jit(solution)/shard_map/ppermute | solution.py:25
  42.4 1.5 %collective-permute-start.18 = (f32[1,2,1280]{2,1,0:T(2,128)S(1)}, f32[1,2,1280]{2,1,0:T(2,128)S(1)}, u32[]{:S(2)}, u32[]{:S(2)}) collective-permute-start(f32[1,2,1280]{2,1,0:T(2,128)S(1)} %add_add_fusion.2.refs_0_), channel_id=1, source_target_pairs={{0,25},{1,24},{2,27},{3,26},{4,29},{5,28},{6,31},{7,30},{8,17},{9,... | collective-permute-start | bytes 30728 | tf_op jit(solution)/shard_map/ppermute | solution.py:25
  43.9 0.9 %collective-permute-start.19 = (f32[1,2,1280]{2,1,0:T(2,128)S(1)}, f32[1,2,1280]{2,1,0:T(2,128)S(1)}, u32[]{:S(2)}, u32[]{:S(2)}) collective-permute-start(f32[1,2,1280]{2,1,0:T(2,128)S(1)} %add_add_fusion.2.refs_0_), channel_id=1, source_target_pairs={{0,9},{1,8},{2,11},{3,10},{4,13},{5,12},{6,15},{7,14},{8,1},{9,0},... | collective-permute-start | bytes 30728 | tf_op jit(solution)/shard_map/ppermute | solution.py:25
  44.7 1.6 %fusion.2 = bf16[1,512,1280]{2,1,0:T(8,128)(2,1)} fusion(bf16[2,512]{1,0:T(2,128)(2,1)S(1)} %get-tuple-element.26, bf16[2,2688]{1,0:T(2,128)(2,1)S(1)} %get-tuple-element.47), kind=kOutput, calls=%fused_computation.4 | convolution fusion | flops 3276800 | bytes 1317888 | tf_op jit(solution)/shard_map/sn,sd->nd/dot_general | solution.py:354
  46.4 0.9 %collective-permute-done.18.refs_2_ = f32[1,2,1280]{2,1,0:T(2,128)S(1)} collective-permute-done((f32[1,2,1280]{2,1,0:T(2,128)S(1)}, f32[1,2,1280]{2,1,0:T(2,128)S(1)}, u32[]{:S(2)}, u32[]{:S(2)}) %collective-permute-start.18) | collective-permute-done | bytes 10272 | tf_op jit(solution)/shard_map/ppermute | solution.py:25
  47.3 0.0 collective-permute-done.19.refs_3_
  47.3 0.8 %finish.1 = f32[2,1280]{1,0:T(2,128)} custom-call(bf16[2,1280]{1,0:T(2,128)(2,1)S(1)} %bitcast.41, f32[1,2,1280]{2,1,0:T(2,128)S(1)} %add_add_fusion.2.refs_0_, f32[1,2,1280]{2,1,0:T(2,128)S(1)} %collective-permute-done.17.refs_1_, f32[1,2,1280]{2,1,0:T(2,128)S(1)} %collective-permute-done.18.refs_2_, f32[1,2,1280]{2,1,0:T(2,128)S(1)} %collective-permute-done.19.refs_3_), custom_call_target="tpu_custom_call" | custom-call | tf_op jit(solution)/shard_map/finish/pallas_call | solution.py:341
  (27 shorter events, 0.2 us)
Async XLA Ops:
  0.6 3.9 %copy-start.2 = (bf16[1280,2]{0,1:T(2,128)(2,1)S(1)}, bf16[1280,2]{0,1:T(2,128)(2,1)}, u32[]{:S(2)}) copy-start(bf16[1280,2]{0,1:T(2,128)(2,1)} %param.8) | copy-start | bytes 15364
  4.0 1.4 %collective-permute-start = (f32[2,2688]{1,0:T(2,128)S(1)}, f32[2,2688]{1,0:T(2,128)S(1)}, u32[]{:S(2)}, u32[]{:S(2)}) collective-permute-start(f32[2,2688]{1,0:T(2,128)S(1)} %get-tuple-element.27), channel_id=1, source_target_pairs={{0,1},{1,0},{2,3},{3,2},{4,5},{5,4},{6,7},{7,6},{8,9},{9,8},{10,11... | collective-permute-start | bytes 64520 | tf_op jit(solution)/shard_map/ppermute | solution.py:29
  5.5 5.3 %collective-permute-start.2 = (f32[1,2,2688]{2,1,0:T(2,128)S(1)}, f32[1,2,2688]{2,1,0:T(2,128)S(1)}, u32[]{:S(2)}, u32[]{:S(2)}) collective-permute-start(f32[1,2,2688]{2,1,0:T(2,128)S(1)} %get-tuple-element.51), channel_id=1, source_target_pairs={{0,17},{1,16},{2,19},{3,18},{4,21},{5,20},{6,23},{7,22},{8,25},{9,... | collective-permute-start | bytes 64520 | tf_op jit(solution)/shard_map/ppermute | solution.py:25
  9.3 5.1 %collective-permute-start.3 = (f32[1,2,2688]{2,1,0:T(2,128)S(1)}, f32[1,2,2688]{2,1,0:T(2,128)S(1)}, u32[]{:S(2)}, u32[]{:S(2)}) collective-permute-start(f32[1,2,2688]{2,1,0:T(2,128)S(1)} %get-tuple-element.50), channel_id=1, source_target_pairs={{0,25},{1,24},{2,27},{3,26},{4,29},{5,28},{6,31},{7,30},{8,17},{9,... | collective-permute-start | bytes 64520 | tf_op jit(solution)/shard_map/ppermute | solution.py:25
  10.6 3.8 %collective-permute-start.1 = (f32[1,2,2688]{2,1,0:T(2,128)S(1)}, f32[1,2,2688]{2,1,0:T(2,128)S(1)}, u32[]{:S(2)}, u32[]{:S(2)}) collective-permute-start(f32[1,2,2688]{2,1,0:T(2,128)S(1)} %get-tuple-element.49), channel_id=1, source_target_pairs={{0,9},{1,8},{2,11},{3,10},{4,13},{5,12},{6,15},{7,14},{8,1},{9,0},... | collective-permute-start | bytes 64520 | tf_op jit(solution)/shard_map/ppermute | solution.py:25
  14.4 5.4 %collective-permute-start.5 = (f32[1,2,2688]{2,1,0:T(2,128)S(1)}, f32[1,2,2688]{2,1,0:T(2,128)S(1)}, u32[]{:S(2)}, u32[]{:S(2)}) collective-permute-start(f32[1,2,2688]{2,1,0:T(2,128)S(1)} %add_add_fusion.1), channel_id=1, source_target_pairs={{0,5},{1,4},{2,7},{3,6},{4,1},{5,0},{6,3},{7,2},{8,13},{9,12},{10,... | collective-permute-start | bytes 64520 | tf_op jit(solution)/shard_map/ppermute | solution.py:25
  16.0 4.1 %collective-permute-start.6 = (f32[1,2,2688]{2,1,0:T(2,128)S(1)}, f32[1,2,2688]{2,1,0:T(2,128)S(1)}, u32[]{:S(2)}, u32[]{:S(2)}) collective-permute-start(f32[1,2,2688]{2,1,0:T(2,128)S(1)} %add_add_fusion.1), channel_id=1, source_target_pairs={{0,7},{1,6},{2,5},{3,4},{4,3},{5,2},{6,1},{7,0},{8,15},{9,14},{10,... | collective-permute-start | bytes 64520 | tf_op jit(solution)/shard_map/ppermute | solution.py:25
  17.1 3.2 %collective-permute-start.4 = (f32[1,2,2688]{2,1,0:T(2,128)S(1)}, f32[1,2,2688]{2,1,0:T(2,128)S(1)}, u32[]{:S(2)}, u32[]{:S(2)}) collective-permute-start(f32[1,2,2688]{2,1,0:T(2,128)S(1)} %add_add_fusion.1), channel_id=1, source_target_pairs={{0,3},{1,2},{2,1},{3,0},{4,7},{5,6},{6,5},{7,4},{8,11},{9,10},{10,... | collective-permute-start | bytes 64520 | tf_op jit(solution)/shard_map/ppermute | solution.py:25
  21.9 12.3 %copy-start = (bf16[1,512,1280]{2,1,0:T(8,128)(2,1)S(1)}, bf16[1,512,1280]{2,1,0:T(8,128)(2,1)}, u32[]{:S(2)}) copy-start(bf16[1,512,1280]{2,1,0:T(8,128)(2,1)} %param.6) | copy-start | bytes 3932164
  21.9 12.3 %copy-start.1 = (bf16[1,512,1280]{2,1,0:T(8,128)(2,1)S(1)}, bf16[1,512,1280]{2,1,0:T(8,128)(2,1)}, u32[]{:S(2)}) copy-start(bf16[1,512,1280]{2,1,0:T(8,128)(2,1)} %param.7) | copy-start | bytes 3932164
  21.9 4.9 %collective-permute-start.8 = (f32[1,2,2688]{2,1,0:T(2,128)S(1)}, f32[1,2,2688]{2,1,0:T(2,128)S(1)}, u32[]{:S(2)}, u32[]{:S(2)}) collective-permute-start(f32[1,2,2688]{2,1,0:T(2,128)S(1)} %bitcast.42), channel_id=1, source_target_pairs={{0,5},{1,4},{2,7},{3,6},{4,1},{5,0},{6,3},{7,2},{8,13},{9,12},{10,... | collective-permute-start | bytes 64520 | tf_op jit(solution)/shard_map/ppermute | solution.py:25
  23.5 4.1 %collective-permute-start.9 = (f32[1,2,2688]{2,1,0:T(2,128)S(1)}, f32[1,2,2688]{2,1,0:T(2,128)S(1)}, u32[]{:S(2)}, u32[]{:S(2)}) collective-permute-start(f32[1,2,2688]{2,1,0:T(2,128)S(1)} %bitcast.43), channel_id=1, source_target_pairs={{0,7},{1,6},{2,5},{3,4},{4,3},{5,2},{6,1},{7,0},{8,15},{9,14},{10,... | collective-permute-start | bytes 64520 | tf_op jit(solution)/shard_map/ppermute | solution.py:25
  24.4 3.2 %collective-permute-start.7 = (f32[1,2,2688]{2,1,0:T(2,128)S(1)}, f32[1,2,2688]{2,1,0:T(2,128)S(1)}, u32[]{:S(2)}, u32[]{:S(2)}) collective-permute-start(f32[1,2,2688]{2,1,0:T(2,128)S(1)} %bitcast.44), channel_id=1, source_target_pairs={{0,3},{1,2},{2,1},{3,0},{4,7},{5,6},{6,5},{7,4},{8,11},{9,10},{10,... | collective-permute-start | bytes 64520 | tf_op jit(solution)/shard_map/ppermute | solution.py:25
  27.6 4.7 %collective-permute-start.11 = (f32[1,2,2688]{2,1,0:T(2,128)S(1)}, f32[1,2,2688]{2,1,0:T(2,128)S(1)}, u32[]{:S(2)}, u32[]{:S(2)}) collective-permute-start(f32[1,2,2688]{2,1,0:T(2,128)S(1)} %add_add_fusion), channel_id=1, source_target_pairs={{0,17},{1,16},{2,19},{3,18},{4,21},{5,20},{6,23},{7,22},{8,25},{9,... | collective-permute-start | bytes 64520 | tf_op jit(solution)/shard_map/ppermute | solution.py:25
  28.9 5.1 %collective-permute-start.12 = (f32[1,2,2688]{2,1,0:T(2,128)S(1)}, f32[1,2,2688]{2,1,0:T(2,128)S(1)}, u32[]{:S(2)}, u32[]{:S(2)}) collective-permute-start(f32[1,2,2688]{2,1,0:T(2,128)S(1)} %add_add_fusion), channel_id=1, source_target_pairs={{0,25},{1,24},{2,27},{3,26},{4,29},{5,28},{6,31},{7,30},{8,17},{9,... | collective-permute-start | bytes 64520 | tf_op jit(solution)/shard_map/ppermute | solution.py:25
  29.7 4.3 %collective-permute-start.10 = (f32[1,2,2688]{2,1,0:T(2,128)S(1)}, f32[1,2,2688]{2,1,0:T(2,128)S(1)}, u32[]{:S(2)}, u32[]{:S(2)}) collective-permute-start(f32[1,2,2688]{2,1,0:T(2,128)S(1)} %add_add_fusion), channel_id=1, source_target_pairs={{0,9},{1,8},{2,11},{3,10},{4,13},{5,12},{6,15},{7,14},{8,1},{9,0},... | collective-permute-start | bytes 64520 | tf_op jit(solution)/shard_map/ppermute | solution.py:25
  35.3 1.2 %collective-permute-start.13 = (f32[2,1280]{1,0:T(2,128)S(1)}, f32[2,1280]{1,0:T(2,128)S(1)}, u32[]{:S(2)}, u32[]{:S(2)}) collective-permute-start(f32[2,1280]{1,0:T(2,128)S(1)} %get-tuple-element.46), channel_id=1, source_target_pairs={{0,1},{1,0},{2,3},{3,2},{4,5},{5,4},{6,7},{7,6},{8,9},{9,8},{10,11... | collective-permute-start | bytes 30728 | tf_op jit(solution)/shard_map/ppermute | solution.py:29
  36.5 5.0 %collective-permute-start.15 = (f32[1,2,1280]{2,1,0:T(2,128)S(1)}, f32[1,2,1280]{2,1,0:T(2,128)S(1)}, u32[]{:S(2)}, u32[]{:S(2)}) collective-permute-start(f32[1,2,1280]{2,1,0:T(2,128)S(1)} %add_bitcast_fusion.3), channel_id=1, source_target_pairs={{0,5},{1,4},{2,7},{3,6},{4,1},{5,0},{6,3},{7,2},{8,13},{9,12},{10,... | collective-permute-start | bytes 30728 | tf_op jit(solution)/shard_map/ppermute | solution.py:25
  37.4 4.1 %collective-permute-start.16 = (f32[1,2,1280]{2,1,0:T(2,128)S(1)}, f32[1,2,1280]{2,1,0:T(2,128)S(1)}, u32[]{:S(2)}, u32[]{:S(2)}) collective-permute-start(f32[1,2,1280]{2,1,0:T(2,128)S(1)} %add_bitcast_fusion.3), channel_id=1, source_target_pairs={{0,7},{1,6},{2,5},{3,4},{4,3},{5,2},{6,1},{7,0},{8,15},{9,14},{10,... | collective-permute-start | bytes 30728 | tf_op jit(solution)/shard_map/ppermute | solution.py:25
  38.4 3.1 %collective-permute-start.14 = (f32[1,2,1280]{2,1,0:T(2,128)S(1)}, f32[1,2,1280]{2,1,0:T(2,128)S(1)}, u32[]{:S(2)}, u32[]{:S(2)}) collective-permute-start(f32[1,2,1280]{2,1,0:T(2,128)S(1)} %add_bitcast_fusion.3), channel_id=1, source_target_pairs={{0,3},{1,2},{2,1},{3,0},{4,7},{5,6},{6,5},{7,4},{8,11},{9,10},{10,... | collective-permute-start | bytes 30728 | tf_op jit(solution)/shard_map/ppermute | solution.py:25
  41.5 4.9 %collective-permute-start.17 = (f32[1,2,1280]{2,1,0:T(2,128)S(1)}, f32[1,2,1280]{2,1,0:T(2,128)S(1)}, u32[]{:S(2)}, u32[]{:S(2)}) collective-permute-start(f32[1,2,1280]{2,1,0:T(2,128)S(1)} %add_add_fusion.2.refs_0_), channel_id=1, source_target_pairs={{0,17},{1,16},{2,19},{3,18},{4,21},{5,20},{6,23},{7,22},{8,25},{9,... | collective-permute-start | bytes 30728 | tf_op jit(solution)/shard_map/ppermute | solution.py:25
  42.4 4.9 %collective-permute-start.18 = (f32[1,2,1280]{2,1,0:T(2,128)S(1)}, f32[1,2,1280]{2,1,0:T(2,128)S(1)}, u32[]{:S(2)}, u32[]{:S(2)}) collective-permute-start(f32[1,2,1280]{2,1,0:T(2,128)S(1)} %add_add_fusion.2.refs_0_), channel_id=1, source_target_pairs={{0,25},{1,24},{2,27},{3,26},{4,29},{5,28},{6,31},{7,30},{8,17},{9,... | collective-permute-start | bytes 30728 | tf_op jit(solution)/shard_map/ppermute | solution.py:25
  43.9 3.4 %collective-permute-start.19 = (f32[1,2,1280]{2,1,0:T(2,128)S(1)}, f32[1,2,1280]{2,1,0:T(2,128)S(1)}, u32[]{:S(2)}, u32[]{:S(2)}) collective-permute-start(f32[1,2,1280]{2,1,0:T(2,128)S(1)} %add_add_fusion.2.refs_0_), channel_id=1, source_target_pairs={{0,9},{1,8},{2,11},{3,10},{4,13},{5,12},{6,15},{7,14},{8,1},{9,0},... | collective-permute-start | bytes 30728 | tf_op jit(solution)/shard_map/ppermute | solution.py:25

commit v19 on v18

--- a/solution.py
+++ b/solution.py
@@ -51,7 +51,9 @@
     if len(masks) == 1:
         return terms[0] + terms[masks[0]]
     low, high = masks
-    return (terms[0] + terms[low]) + (terms[high] + terms[low | high])
+    others = [terms[low | high], terms[high]]
+    first, second = others if low == 1 else others[::-1]
+    return (terms[0] + terms[low]) + (first + second)
 
 
 def sum_to_owner(value, group):

time: 48.3 us -> 48.1 us (level)
  transfers between devices with their start and end apart: 20 -> 20, of which waited for: 8 -> 11; matrix products, arithmetic and copies ran while one was open for 16% -> 16% of each run, Pallas kernels for 4% -> 4%
where the time goes in v19:
time: 48.1 us; the launch traced here: 47.9 us
  starting transfers between devices  22.1 us (46%)
  waiting for transfers between devices  8.13 us (17%)
  Pallas kernels  8.05 us (17%)
  matrix products  7.52 us (16%)
  between operations  1.46 us (3%)
  other arithmetic  0.56 us (1%)
    ppermute x18, starting transfers between devices, exchange(): return lax.ppermute(value, AXES, pairs)  21.3 us
    ppermute x18, waiting for transfers between devices, exchange(): return lax.ppermute(value, AXES, pairs)  7.29 us
    pallas_call x1, Pallas kernels, per_device(): pl.pallas_call(token_sums, in_specs=[scalar, in_hbm, in_hbm, in_hbm], out...  2.71 us
    dot_general x1, matrix products, per_device(): jnp.einsum('sn,sd->nd', dispatch, slot_dx, preferred_element_type=f32)  1.98 us
    pallas_call x1, Pallas kernels, per_device(): pl.pallas_call(fetch, in_specs=[in_hbm] * 2, out_specs=[in_vmem] * 2, out...  1.94 us
    dot_general x1, matrix products, per_device(): jnp.einsum('sn,sd->nd', combine, slot_y, preferred_element_type=f32)  1.61 us
    dot_general x1, matrix products, per_device(): jnp.einsum('od,oh->dh', mine_x, pre_grad, preferred_element_type=f32)  1.59 us
    dot_general x1, matrix products, per_device(): jnp.einsum('oh,od->hd', hidden, mine_cot, preferred_element_type=f32)  1.59 us
  transfers between devices with their start and end apart: 20, of which 11 were waited for; matrix products, arithmetic and copies ran while one was open for 16% of the time, Pallas kernels for 4%

profile of v19, /device:TPU:0, one launch (start us, length us, event | category | flops | bytes accessed | tf_op | source)
XLA Modules:
  0.0 47.9 jit_solution(9424515808149226690)
XLA Ops:
  1.3 2.7 %token_sums.1 = (f32[2,2688]{1,0:T(2,128)S(1)}, f32[2,512]{1,0:T(2,128)S(1)}, bf16[2,512]{1,0:T(2,128)(2,1)S(1)}, f32[512,1]{1,0:T(8,128)S(1)}, bf16[512,1280]{1,0:T(8,128)(2,1)S(1)}) custom-call(f32[1]{0:T(128)S(6)} %copy.11.scale_ref, bf16[2,1280]{1,0:T(2,128)(2,1)} %bitcast.40, bf16[512,1280]{1,0:T(8,128)(2,1)} %bitcast.36, bf16[512,1280]{1,0:T(8,128)(2,1)} %bitcast.38), custom_call_target="tpu_custom_call" | custom-call | tf_op jit(solution)/shard_map/token_sums/pallas_call | solution.py:264
  4.0 0.5 %collective-permute-start = (f32[2,2688]{1,0:T(2,128)S(1)}, f32[2,2688]{1,0:T(2,128)S(1)}, u32[]{:S(2)}, u32[]{:S(2)}) collective-permute-start(f32[2,2688]{1,0:T(2,128)S(1)} %get-tuple-element.27), channel_id=1, source_target_pairs={{0,1},{1,0},{2,3},{3,2},{4,5},{5,4},{6,7},{7,6},{8,9},{9,8},{10,11... | collective-permute-start | bytes 64520 | tf_op jit(solution)/shard_map/ppermute | solution.py:29
  4.5 0.1 fusion.3
  4.7 0.7 %collective-permute-done = f32[2,2688]{1,0:T(2,128)S(1)} collective-permute-done((f32[2,2688]{1,0:T(2,128)S(1)}, f32[2,2688]{1,0:T(2,128)S(1)}, u32[]{:S(2)}, u32[]{:S(2)}) %collective-permute-start) | collective-permute-done | bytes 21536 | tf_op jit(solution)/shard_map/ppermute | solution.py:29
  5.4 0.1 broadcast_select_fusion
  5.5 3.8 %collective-permute-start.2 = (f32[1,2,2688]{2,1,0:T(2,128)S(1)}, f32[1,2,2688]{2,1,0:T(2,128)S(1)}, u32[]{:S(2)}, u32[]{:S(2)}) collective-permute-start(f32[1,2,2688]{2,1,0:T(2,128)S(1)} %get-tuple-element.51), channel_id=1, source_target_pairs={{0,17},{1,16},{2,19},{3,18},{4,21},{5,20},{6,23},{7,22},{8,25},{9,... | collective-permute-start | bytes 64520 | tf_op jit(solution)/shard_map/ppermute | solution.py:25
  9.3 1.3 %collective-permute-start.3 = (f32[1,2,2688]{2,1,0:T(2,128)S(1)}, f32[1,2,2688]{2,1,0:T(2,128)S(1)}, u32[]{:S(2)}, u32[]{:S(2)}) collective-permute-start(f32[1,2,2688]{2,1,0:T(2,128)S(1)} %get-tuple-element.50), channel_id=1, source_target_pairs={{0,25},{1,24},{2,27},{3,26},{4,29},{5,28},{6,31},{7,30},{8,17},{9,... | collective-permute-start | bytes 64520 | tf_op jit(solution)/shard_map/ppermute | solution.py:25
  10.6 0.2 collective-permute-start.1
  10.8 0.0 collective-permute-done.2
  10.8 3.6 %collective-permute-done.3 = f32[1,2,2688]{2,1,0:T(2,128)S(1)} collective-permute-done((f32[1,2,2688]{2,1,0:T(2,128)S(1)}, f32[1,2,2688]{2,1,0:T(2,128)S(1)}, u32[]{:S(2)}, u32[]{:S(2)}) %collective-permute-start.3) | collective-permute-done | bytes 21536 | tf_op jit(solution)/shard_map/ppermute | solution.py:25
  14.4 0.0 collective-permute-done.1
  14.4 2.5 %collective-permute-start.5 = (f32[1,2,2688]{2,1,0:T(2,128)S(1)}, f32[1,2,2688]{2,1,0:T(2,128)S(1)}, u32[]{:S(2)}, u32[]{:S(2)}) collective-permute-start(f32[1,2,2688]{2,1,0:T(2,128)S(1)} %add_add_fusion.1), channel_id=1, source_target_pairs={{0,7},{1,6},{2,5},{3,4},{4,3},{5,2},{6,1},{7,0},{8,15},{9,14},{10,... | collective-permute-start | bytes 64520 | tf_op jit(solution)/shard_map/ppermute | solution.py:25
  16.9 0.2 collective-permute-start.6
  17.1 0.6 %collective-permute-start.4 = (f32[1,2,2688]{2,1,0:T(2,128)S(1)}, f32[1,2,2688]{2,1,0:T(2,128)S(1)}, u32[]{:S(2)}, u32[]{:S(2)}) collective-permute-start(f32[1,2,2688]{2,1,0:T(2,128)S(1)} %add_add_fusion.1), channel_id=1, source_target_pairs={{0,3},{1,2},{2,1},{3,0},{4,7},{5,6},{6,5},{7,4},{8,11},{9,10},{10,... | collective-permute-start | bytes 64520 | tf_op jit(solution)/shard_map/ppermute | solution.py:25
  17.7 0.1 reduce
  17.9 1.9 %fetch_weights.1 = (bf16[1280,640]{1,0:T(8,128)(2,1)S(1)}, bf16[640,1280]{1,0:T(8,128)(2,1)S(1)}) custom-call(bf16[1280,640]{1,0:T(8,128)(2,1)} %in_ref, bf16[640,1280]{1,0:T(8,128)(2,1)} %out_ref), custom_call_target="tpu_custom_call" | custom-call | bytes 6553600 | tf_op jit(solution)/shard_map/fetch_weights/pallas_call | solution.py:286
  19.8 0.0 collective-permute-done.5
  19.8 0.3 collective-permute-done.6
  20.1 0.2 collective-permute-done.4
  20.4 1.5 %expert_rows.1 = (f32[2,2688]{1,0:T(2,128)S(1)}, bf16[2,1280]{1,0:T(2,128)(2,1)S(1)}, bf16[2,1280]{1,0:T(2,128)(2,1)S(1)}, bf16[2,640]{1,0:T(2,128)(2,1)S(1)}, bf16[2,640]{1,0:T(2,128)(2,1)S(1)}) custom-call(s32[1]{0:T(128)} %bitcast.3.owned_ref, f32[2,2688]{1,0:T(2,128)S(1)} %add_bitcast_fusion.2.sums_ref, bf16[1280,640]{1,0:T(8,128)(2,1)S(1)} %get-tuple-element.31.in_ref, ...), custom_call_target="tpu_custom_call" | custom-call | tf_op jit(solution)/shard_map/expert_rows/pallas_call | solution.py:303
  21.9 1.6 %collective-permute-start.8 = (f32[1,2,2688]{2,1,0:T(2,128)S(1)}, f32[1,2,2688]{2,1,0:T(2,128)S(1)}, u32[]{:S(2)}, u32[]{:S(2)}) collective-permute-start(f32[1,2,2688]{2,1,0:T(2,128)S(1)} %bitcast.42), channel_id=1, source_target_pairs={{0,7},{1,6},{2,5},{3,4},{4,3},{5,2},{6,1},{7,0},{8,15},{9,14},{10,... | collective-permute-start | bytes 64520 | tf_op jit(solution)/shard_map/ppermute | solution.py:25
  23.5 0.6 %collective-permute-start.9 = (f32[1,2,2688]{2,1,0:T(2,128)S(1)}, f32[1,2,2688]{2,1,0:T(2,128)S(1)}, u32[]{:S(2)}, u32[]{:S(2)}) collective-permute-start(f32[1,2,2688]{2,1,0:T(2,128)S(1)} %bitcast.43), channel_id=1, source_target_pairs={{0,5},{1,4},{2,7},{3,6},{4,1},{5,0},{6,3},{7,2},{8,13},{9,12},{10,... | collective-permute-start | bytes 64520 | tf_op jit(solution)/shard_map/ppermute | solution.py:25
  24.1 1.1 %collective-permute-start.7 = (f32[1,2,2688]{2,1,0:T(2,128)S(1)}, f32[1,2,2688]{2,1,0:T(2,128)S(1)}, u32[]{:S(2)}, u32[]{:S(2)}) collective-permute-start(f32[1,2,2688]{2,1,0:T(2,128)S(1)} %bitcast.44), channel_id=1, source_target_pairs={{0,3},{1,2},{2,1},{3,0},{4,7},{5,6},{6,5},{7,4},{8,11},{9,10},{10,... | collective-permute-start | bytes 64520 | tf_op jit(solution)/shard_map/ppermute | solution.py:25
  25.2 1.6 %fusion.11 = f32[640,640]{1,0:T(8,128)} fusion(bf16[2,640]{1,0:T(2,128)(2,1)S(1)} %get-tuple-element.43, bf16[2,1280]{1,0:T(2,128)(2,1)S(1)} %get-tuple-element.42, s32[]{:T(128)S(6)} %select_n.63), kind=kOutput, calls=%fused_computation.25 | convolution fusion | flops 1638400 | bytes 1643524 | tf_op jit(solution)/shard_map/od,oh->dh/dot_general | solution.py:322
  26.8 0.1 collective-permute-done.9
  26.9 0.4 collective-permute-done.7
  27.3 1.0 %collective-permute-start.11 = (f32[1,2,2688]{2,1,0:T(2,128)S(1)}, f32[1,2,2688]{2,1,0:T(2,128)S(1)}, u32[]{:S(2)}, u32[]{:S(2)}) collective-permute-start(f32[1,2,2688]{2,1,0:T(2,128)S(1)} %add_add_fusion), channel_id=1, source_target_pairs={{0,17},{1,16},{2,19},{3,18},{4,21},{5,20},{6,23},{7,22},{8,25},{9,... | collective-permute-start | bytes 64520 | tf_op jit(solution)/shard_map/ppermute | solution.py:25
  28.4 0.9 %collective-permute-start.12 = (f32[1,2,2688]{2,1,0:T(2,128)S(1)}, f32[1,2,2688]{2,1,0:T(2,128)S(1)}, u32[]{:S(2)}, u32[]{:S(2)}) collective-permute-start(f32[1,2,2688]{2,1,0:T(2,128)S(1)} %add_add_fusion), channel_id=1, source_target_pairs={{0,25},{1,24},{2,27},{3,26},{4,29},{5,28},{6,31},{7,30},{8,17},{9,... | collective-permute-start | bytes 64520 | tf_op jit(solution)/shard_map/ppermute | solution.py:25
  29.2 1.1 %collective-permute-start.10 = (f32[1,2,2688]{2,1,0:T(2,128)S(1)}, f32[1,2,2688]{2,1,0:T(2,128)S(1)}, u32[]{:S(2)}, u32[]{:S(2)}) collective-permute-start(f32[1,2,2688]{2,1,0:T(2,128)S(1)} %add_add_fusion), channel_id=1, source_target_pairs={{0,9},{1,8},{2,11},{3,10},{4,13},{5,12},{6,15},{7,14},{8,1},{9,0},... | collective-permute-start | bytes 64520 | tf_op jit(solution)/shard_map/ppermute | solution.py:25
  30.4 1.6 %fusion.9 = f32[640,640]{1,0:T(8,128)} fusion(bf16[2,640]{1,0:T(2,128)(2,1)S(1)} %get-tuple-element.44, bf16[2,1280]{1,0:T(2,128)(2,1)S(1)} %get-tuple-element.45, s32[]{:T(128)S(6)} %select_n.63), kind=kOutput, calls=%fused_computation.23 | convolution fusion | flops 1638400 | bytes 1643524 | tf_op jit(solution)/shard_map/oh,od->hd/dot_general | solution.py:323
  32.0 1.4 %collective-permute-done.12 = f32[1,2,2688]{2,1,0:T(2,128)S(1)} collective-permute-done((f32[1,2,2688]{2,1,0:T(2,128)S(1)}, f32[1,2,2688]{2,1,0:T(2,128)S(1)}, u32[]{:S(2)}, u32[]{:S(2)}) %collective-permute-start.12) | collective-permute-done | bytes 21536 | tf_op jit(solution)/shard_map/ppermute | solution.py:25
  33.5 0.1 fusion.16
  33.6 1.1 %score_grads.1 = (bf16[2,512]{1,0:T(2,128)(2,1)S(1)}, bf16[2,512]{1,0:T(2,128)(2,1)S(1)}, f32[2,1280]{1,0:T(2,128)S(1)}) custom-call(f32[1]{0:T(128)S(6)} %copy.11.scale_ref, f32[2,2688]{1,0:T(2,128)S(1)} %get-tuple-element.48.slots_ref, f32[1,128]{1,0:T(1,128)S(1)} %constant_dynamic-slice_fusion.1.totals_ref, bf16[512,1280]{1,0:T(8,128)(2,1)S(1)} %bitcast.37, ...), custom_call_target="tpu_custom_call" | custom-call | tf_op jit(solution)/shard_map/score_grads/pallas_call | solution.py:324
  34.7 0.3 collective-permute-start.13
  35.0 0.7 %multiply_reduce_fusion = (f32[512]{0:T(512)S(1)}, f32[512,1280]{1,0:T(8,128)S(1)}) fusion(f32[512]{0:T(512)S(1)} %reduce, bf16[1,512,1280]{2,1,0:T(8,128)(2,1)S(1)} %copy-done, bf16[2,512]{1,0:T(2,128)(2,1)S(1)} %get-tuple-element.41, f32[2]{0:T(128)S(1)} %add_rsqrt_fusion, bf16[1280,2]{0,1:T(2,128)(2,1)S(1)} %copy-done.2), kind=kOutput, calls=%fused_computation.5 | convolution fusion | flops 5250048 | bytes 3943432 | tf_op jit(solution)/shard_map/sn,sd->nd/dot_general | solution.py:357
  35.7 0.1 collective-permute-done.13
  35.9 2.3 %collective-permute-start.15 = (f32[1,2,1280]{2,1,0:T(2,128)S(1)}, f32[1,2,1280]{2,1,0:T(2,128)S(1)}, u32[]{:S(2)}, u32[]{:S(2)}) collective-permute-start(f32[1,2,1280]{2,1,0:T(2,128)S(1)} %add_bitcast_fusion.3), channel_id=1, source_target_pairs={{0,7},{1,6},{2,5},{3,4},{4,3},{5,2},{6,1},{7,0},{8,15},{9,14},{10,... | collective-permute-start | bytes 30728 | tf_op jit(solution)/shard_map/ppermute | solution.py:25
  38.1 0.2 collective-permute-start.16
  38.3 0.7 %collective-permute-start.14 = (f32[1,2,1280]{2,1,0:T(2,128)S(1)}, f32[1,2,1280]{2,1,0:T(2,128)S(1)}, u32[]{:S(2)}, u32[]{:S(2)}) collective-permute-start(f32[1,2,1280]{2,1,0:T(2,128)S(1)} %add_bitcast_fusion.3), channel_id=1, source_target_pairs={{0,3},{1,2},{2,1},{3,0},{4,7},{5,6},{6,5},{7,4},{8,11},{9,10},{10,... | collective-permute-start | bytes 30728 | tf_op jit(solution)/shard_map/ppermute | solution.py:25
  39.0 2.0 %fusion.1 = bf16[1,512,1280]{2,1,0:T(8,128)(2,1)} fusion(bf16[2,512]{1,0:T(2,128)(2,1)S(1)} %get-tuple-element.39, f32[512,1280]{1,0:T(8,128)S(1)} %get-tuple-element.53, f32[512]{0:T(512)S(1)} %get-tuple-element.52, f32[512]{0:T(512)S(1)} %reduce, bf16[2,2688]{1,0:T(2,128)(2,1)S(1)} %get-tuple-element.47, bf16[1,512,1280]{2,1,0:T(8,128)(2,1)S(1)} %copy-done), kind=kOutput, calls=%fused_computation.3 | convolution fusion | flops 7208960 | bytes 5254144 | tf_op jit(solution)/shard_map/sn,sd->nd/dot_general | solution.py:358
  41.0 0.2 collective-permute-done.16
  41.2 0.2 collective-permute-done.14
  41.4 0.8 %collective-permute-start.17 = (f32[1,2,1280]{2,1,0:T(2,128)S(1)}, f32[1,2,1280]{2,1,0:T(2,128)S(1)}, u32[]{:S(2)}, u32[]{:S(2)}) collective-permute-start(f32[1,2,1280]{2,1,0:T(2,128)S(1)} %add_add_fusion.2.refs_0_), channel_id=1, source_target_pairs={{0,17},{1,16},{2,19},{3,18},{4,21},{5,20},{6,23},{7,22},{8,25},{9,... | collective-permute-start | bytes 30728 | tf_op jit(solution)/shard_map/ppermute | solution.py:25
  42.2 1.7 %collective-permute-start.18 = (f32[1,2,1280]{2,1,0:T(2,128)S(1)}, f32[1,2,1280]{2,1,0:T(2,128)S(1)}, u32[]{:S(2)}, u32[]{:S(2)}) collective-permute-start(f32[1,2,1280]{2,1,0:T(2,128)S(1)} %add_add_fusion.2.refs_0_), channel_id=1, source_target_pairs={{0,25},{1,24},{2,27},{3,26},{4,29},{5,28},{6,31},{7,30},{8,17},{9,... | collective-permute-start | bytes 30728 | tf_op jit(solution)/shard_map/ppermute | solution.py:25
  43.9 0.8 %collective-permute-start.19 = (f32[1,2,1280]{2,1,0:T(2,128)S(1)}, f32[1,2,1280]{2,1,0:T(2,128)S(1)}, u32[]{:S(2)}, u32[]{:S(2)}) collective-permute-start(f32[1,2,1280]{2,1,0:T(2,128)S(1)} %add_add_fusion.2.refs_0_), channel_id=1, source_target_pairs={{0,9},{1,8},{2,11},{3,10},{4,13},{5,12},{6,15},{7,14},{8,1},{9,0},... | collective-permute-start | bytes 30728 | tf_op jit(solution)/shard_map/ppermute | solution.py:25
  44.7 1.6 %fusion.2 = bf16[1,512,1280]{2,1,0:T(8,128)(2,1)} fusion(bf16[2,512]{1,0:T(2,128)(2,1)S(1)} %get-tuple-element.26, bf16[2,2688]{1,0:T(2,128)(2,1)S(1)} %get-tuple-element.47), kind=kOutput, calls=%fused_computation.4 | convolution fusion | flops 3276800 | bytes 1317888 | tf_op jit(solution)/shard_map/sn,sd->nd/dot_general | solution.py:356
  46.3 0.8 %collective-permute-done.18.refs_2_ = f32[1,2,1280]{2,1,0:T(2,128)S(1)} collective-permute-done((f32[1,2,1280]{2,1,0:T(2,128)S(1)}, f32[1,2,1280]{2,1,0:T(2,128)S(1)}, u32[]{:S(2)}, u32[]{:S(2)}) %collective-permute-start.18) | collective-permute-done | bytes 10272 | tf_op jit(solution)/shard_map/ppermute | solution.py:25
  47.1 0.8 %finish.1 = f32[2,1280]{1,0:T(2,128)} custom-call(bf16[2,1280]{1,0:T(2,128)(2,1)S(1)} %bitcast.41, f32[1,2,1280]{2,1,0:T(2,128)S(1)} %add_add_fusion.2.refs_0_, f32[1,2,1280]{2,1,0:T(2,128)S(1)} %collective-permute-done.17.refs_1_, f32[1,2,1280]{2,1,0:T(2,128)S(1)} %collective-permute-done.18.refs_2_, f32[1,2,1280]{2,1,0:T(2,128)S(1)} %collective-permute-done.19.refs_3_), custom_call_target="tpu_custom_call" | custom-call | tf_op jit(solution)/shard_map/finish/pallas_call | solution.py:343
  (27 shorter events, 0.2 us)
Async XLA Ops:
  0.6 3.9 %copy-start.2 = (bf16[1280,2]{0,1:T(2,128)(2,1)S(1)}, bf16[1280,2]{0,1:T(2,128)(2,1)}, u32[]{:S(2)}) copy-start(bf16[1280,2]{0,1:T(2,128)(2,1)} %param.8) | copy-start | bytes 15364
  4.0 1.4 %collective-permute-start = (f32[2,2688]{1,0:T(2,128)S(1)}, f32[2,2688]{1,0:T(2,128)S(1)}, u32[]{:S(2)}, u32[]{:S(2)}) collective-permute-start(f32[2,2688]{1,0:T(2,128)S(1)} %get-tuple-element.27), channel_id=1, source_target_pairs={{0,1},{1,0},{2,3},{3,2},{4,5},{5,4},{6,7},{7,6},{8,9},{9,8},{10,11... | collective-permute-start | bytes 64520 | tf_op jit(solution)/shard_map/ppermute | solution.py:29
  5.5 5.3 %collective-permute-start.2 = (f32[1,2,2688]{2,1,0:T(2,128)S(1)}, f32[1,2,2688]{2,1,0:T(2,128)S(1)}, u32[]{:S(2)}, u32[]{:S(2)}) collective-permute-start(f32[1,2,2688]{2,1,0:T(2,128)S(1)} %get-tuple-element.51), channel_id=1, source_target_pairs={{0,17},{1,16},{2,19},{3,18},{4,21},{5,20},{6,23},{7,22},{8,25},{9,... | collective-permute-start | bytes 64520 | tf_op jit(solution)/shard_map/ppermute | solution.py:25
  9.3 5.1 %collective-permute-start.3 = (f32[1,2,2688]{2,1,0:T(2,128)S(1)}, f32[1,2,2688]{2,1,0:T(2,128)S(1)}, u32[]{:S(2)}, u32[]{:S(2)}) collective-permute-start(f32[1,2,2688]{2,1,0:T(2,128)S(1)} %get-tuple-element.50), channel_id=1, source_target_pairs={{0,25},{1,24},{2,27},{3,26},{4,29},{5,28},{6,31},{7,30},{8,17},{9,... | collective-permute-start | bytes 64520 | tf_op jit(solution)/shard_map/ppermute | solution.py:25
  10.6 3.8 %collective-permute-start.1 = (f32[1,2,2688]{2,1,0:T(2,128)S(1)}, f32[1,2,2688]{2,1,0:T(2,128)S(1)}, u32[]{:S(2)}, u32[]{:S(2)}) collective-permute-start(f32[1,2,2688]{2,1,0:T(2,128)S(1)} %get-tuple-element.49), channel_id=1, source_target_pairs={{0,9},{1,8},{2,11},{3,10},{4,13},{5,12},{6,15},{7,14},{8,1},{9,0},... | collective-permute-start | bytes 64520 | tf_op jit(solution)/shard_map/ppermute | solution.py:25
  14.4 5.4 %collective-permute-start.5 = (f32[1,2,2688]{2,1,0:T(2,128)S(1)}, f32[1,2,2688]{2,1,0:T(2,128)S(1)}, u32[]{:S(2)}, u32[]{:S(2)}) collective-permute-start(f32[1,2,2688]{2,1,0:T(2,128)S(1)} %add_add_fusion.1), channel_id=1, source_target_pairs={{0,7},{1,6},{2,5},{3,4},{4,3},{5,2},{6,1},{7,0},{8,15},{9,14},{10,... | collective-permute-start | bytes 64520 | tf_op jit(solution)/shard_map/ppermute | solution.py:25
  16.9 3.2 %collective-permute-start.6 = (f32[1,2,2688]{2,1,0:T(2,128)S(1)}, f32[1,2,2688]{2,1,0:T(2,128)S(1)}, u32[]{:S(2)}, u32[]{:S(2)}) collective-permute-start(f32[1,2,2688]{2,1,0:T(2,128)S(1)} %add_add_fusion.1), channel_id=1, source_target_pairs={{0,5},{1,4},{2,7},{3,6},{4,1},{5,0},{6,3},{7,2},{8,13},{9,12},{10,... | collective-permute-start | bytes 64520 | tf_op jit(solution)/shard_map/ppermute | solution.py:25
  17.1 3.2 %collective-permute-start.4 = (f32[1,2,2688]{2,1,0:T(2,128)S(1)}, f32[1,2,2688]{2,1,0:T(2,128)S(1)}, u32[]{:S(2)}, u32[]{:S(2)}) collective-permute-start(f32[1,2,2688]{2,1,0:T(2,128)S(1)} %add_add_fusion.1), channel_id=1, source_target_pairs={{0,3},{1,2},{2,1},{3,0},{4,7},{5,6},{6,5},{7,4},{8,11},{9,10},{10,... | collective-permute-start | bytes 64520 | tf_op jit(solution)/shard_map/ppermute | solution.py:25
  21.9 11.7 %copy-start = (bf16[1,512,1280]{2,1,0:T(8,128)(2,1)S(1)}, bf16[1,512,1280]{2,1,0:T(8,128)(2,1)}, u32[]{:S(2)}) copy-start(bf16[1,512,1280]{2,1,0:T(8,128)(2,1)} %param.6) | copy-start | bytes 3932164
  21.9 11.7 %copy-start.1 = (bf16[1,512,1280]{2,1,0:T(8,128)(2,1)S(1)}, bf16[1,512,1280]{2,1,0:T(8,128)(2,1)}, u32[]{:S(2)}) copy-start(bf16[1,512,1280]{2,1,0:T(8,128)(2,1)} %param.7) | copy-start | bytes 3932164
  21.9 4.9 %collective-permute-start.8 = (f32[1,2,2688]{2,1,0:T(2,128)S(1)}, f32[1,2,2688]{2,1,0:T(2,128)S(1)}, u32[]{:S(2)}, u32[]{:S(2)}) collective-permute-start(f32[1,2,2688]{2,1,0:T(2,128)S(1)} %bitcast.42), channel_id=1, source_target_pairs={{0,7},{1,6},{2,5},{3,4},{4,3},{5,2},{6,1},{7,0},{8,15},{9,14},{10,... | collective-permute-start | bytes 64520 | tf_op jit(solution)/shard_map/ppermute | solution.py:25
  23.5 3.4 %collective-permute-start.9 = (f32[1,2,2688]{2,1,0:T(2,128)S(1)}, f32[1,2,2688]{2,1,0:T(2,128)S(1)}, u32[]{:S(2)}, u32[]{:S(2)}) collective-permute-start(f32[1,2,2688]{2,1,0:T(2,128)S(1)} %bitcast.43), channel_id=1, source_target_pairs={{0,5},{1,4},{2,7},{3,6},{4,1},{5,0},{6,3},{7,2},{8,13},{9,12},{10,... | collective-permute-start | bytes 64520 | tf_op jit(solution)/shard_map/ppermute | solution.py:25
  24.1 3.2 %collective-permute-start.7 = (f32[1,2,2688]{2,1,0:T(2,128)S(1)}, f32[1,2,2688]{2,1,0:T(2,128)S(1)}, u32[]{:S(2)}, u32[]{:S(2)}) collective-permute-start(f32[1,2,2688]{2,1,0:T(2,128)S(1)} %bitcast.44), channel_id=1, source_target_pairs={{0,3},{1,2},{2,1},{3,0},{4,7},{5,6},{6,5},{7,4},{8,11},{9,10},{10,... | collective-permute-start | bytes 64520 | tf_op jit(solution)/shard_map/ppermute | solution.py:25
  27.3 4.6 %collective-permute-start.11 = (f32[1,2,2688]{2,1,0:T(2,128)S(1)}, f32[1,2,2688]{2,1,0:T(2,128)S(1)}, u32[]{:S(2)}, u32[]{:S(2)}) collective-permute-start(f32[1,2,2688]{2,1,0:T(2,128)S(1)} %add_add_fusion), channel_id=1, source_target_pairs={{0,17},{1,16},{2,19},{3,18},{4,21},{5,20},{6,23},{7,22},{8,25},{9,... | collective-permute-start | bytes 64520 | tf_op jit(solution)/shard_map/ppermute | solution.py:25
  28.4 5.0 %collective-permute-start.12 = (f32[1,2,2688]{2,1,0:T(2,128)S(1)}, f32[1,2,2688]{2,1,0:T(2,128)S(1)}, u32[]{:S(2)}, u32[]{:S(2)}) collective-permute-start(f32[1,2,2688]{2,1,0:T(2,128)S(1)} %add_add_fusion), channel_id=1, source_target_pairs={{0,25},{1,24},{2,27},{3,26},{4,29},{5,28},{6,31},{7,30},{8,17},{9,... | collective-permute-start | bytes 64520 | tf_op jit(solution)/shard_map/ppermute | solution.py:25
  29.2 4.2 %collective-permute-start.10 = (f32[1,2,2688]{2,1,0:T(2,128)S(1)}, f32[1,2,2688]{2,1,0:T(2,128)S(1)}, u32[]{:S(2)}, u32[]{:S(2)}) collective-permute-start(f32[1,2,2688]{2,1,0:T(2,128)S(1)} %add_add_fusion), channel_id=1, source_target_pairs={{0,9},{1,8},{2,11},{3,10},{4,13},{5,12},{6,15},{7,14},{8,1},{9,0},... | collective-permute-start | bytes 64520 | tf_op jit(solution)/shard_map/ppermute | solution.py:25
  34.7 1.2 %collective-permute-start.13 = (f32[2,1280]{1,0:T(2,128)S(1)}, f32[2,1280]{1,0:T(2,128)S(1)}, u32[]{:S(2)}, u32[]{:S(2)}) collective-permute-start(f32[2,1280]{1,0:T(2,128)S(1)} %get-tuple-element.46), channel_id=1, source_target_pairs={{0,1},{1,0},{2,3},{3,2},{4,5},{5,4},{6,7},{7,6},{8,9},{9,8},{10,11... | collective-permute-start | bytes 30728 | tf_op jit(solution)/shard_map/ppermute | solution.py:29
  35.9 5.1 %collective-permute-start.15 = (f32[1,2,1280]{2,1,0:T(2,128)S(1)}, f32[1,2,1280]{2,1,0:T(2,128)S(1)}, u32[]{:S(2)}, u32[]{:S(2)}) collective-permute-start(f32[1,2,1280]{2,1,0:T(2,128)S(1)} %add_bitcast_fusion.3), channel_id=1, source_target_pairs={{0,7},{1,6},{2,5},{3,4},{4,3},{5,2},{6,1},{7,0},{8,15},{9,14},{10,... | collective-permute-start | bytes 30728 | tf_op jit(solution)/shard_map/ppermute | solution.py:25
  38.1 3.1 %collective-permute-start.16 = (f32[1,2,1280]{2,1,0:T(2,128)S(1)}, f32[1,2,1280]{2,1,0:T(2,128)S(1)}, u32[]{:S(2)}, u32[]{:S(2)}) collective-permute-start(f32[1,2,1280]{2,1,0:T(2,128)S(1)} %add_bitcast_fusion.3), channel_id=1, source_target_pairs={{0,5},{1,4},{2,7},{3,6},{4,1},{5,0},{6,3},{7,2},{8,13},{9,12},{10,... | collective-permute-start | bytes 30728 | tf_op jit(solution)/shard_map/ppermute | solution.py:25
  38.3 3.1 %collective-permute-start.14 = (f32[1,2,1280]{2,1,0:T(2,128)S(1)}, f32[1,2,1280]{2,1,0:T(2,128)S(1)}, u32[]{:S(2)}, u32[]{:S(2)}) collective-permute-start(f32[1,2,1280]{2,1,0:T(2,128)S(1)} %add_bitcast_fusion.3), channel_id=1, source_target_pairs={{0,3},{1,2},{2,1},{3,0},{4,7},{5,6},{6,5},{7,4},{8,11},{9,10},{10,... | collective-permute-start | bytes 30728 | tf_op jit(solution)/shard_map/ppermute | solution.py:25
  41.4 4.8 %collective-permute-start.17 = (f32[1,2,1280]{2,1,0:T(2,128)S(1)}, f32[1,2,1280]{2,1,0:T(2,128)S(1)}, u32[]{:S(2)}, u32[]{:S(2)}) collective-permute-start(f32[1,2,1280]{2,1,0:T(2,128)S(1)} %add_add_fusion.2.refs_0_), channel_id=1, source_target_pairs={{0,17},{1,16},{2,19},{3,18},{4,21},{5,20},{6,23},{7,22},{8,25},{9,... | collective-permute-start | bytes 30728 | tf_op jit(solution)/shard_map/ppermute | solution.py:25
  42.2 4.9 %collective-permute-start.18 = (f32[1,2,1280]{2,1,0:T(2,128)S(1)}, f32[1,2,1280]{2,1,0:T(2,128)S(1)}, u32[]{:S(2)}, u32[]{:S(2)}) collective-permute-start(f32[1,2,1280]{2,1,0:T(2,128)S(1)} %add_add_fusion.2.refs_0_), channel_id=1, source_target_pairs={{0,25},{1,24},{2,27},{3,26},{4,29},{5,28},{6,31},{7,30},{8,17},{9,... | collective-permute-start | bytes 30728 | tf_op jit(solution)/shard_map/ppermute | solution.py:25
  43.9 3.2 %collective-permute-start.19 = (f32[1,2,1280]{2,1,0:T(2,128)S(1)}, f32[1,2,1280]{2,1,0:T(2,128)S(1)}, u32[]{:S(2)}, u32[]{:S(2)}) collective-permute-start(f32[1,2,1280]{2,1,0:T(2,128)S(1)} %add_add_fusion.2.refs_0_), channel_id=1, source_target_pairs={{0,9},{1,8},{2,11},{3,10},{4,13},{5,12},{6,15},{7,14},{8,1},{9,0},... | collective-permute-start | bytes 30728 | tf_op jit(solution)/shard_map/ppermute | solution.py:25

commit v20 on v19

--- a/solution.py
+++ b/solution.py
@@ -208,12 +208,21 @@
     return jnp.sum(jnp.where(same, row, 0.0), axis=1, keepdims=True)
 
 
-def score_grads(scale_ref, slots_ref, totals_ref, tok_ref, cot_ref, norm_ref, exp_ref, grad_ref, dispatch_ref, phi_ref):
+def score_grads(clip_ref, scale_ref, message_ref, totals_ref, tok_ref, cot_ref, norm_ref, exp_ref, grad_ref, dispatch_ref, phi_ref, slot_y_ref, slot_dx_ref):
     width = tok_ref.shape[1]
-    slot_y = slots_ref[:, :width].astype(bf16)
-    slot_dx = slots_ref[:, width : 2 * width].astype(bf16)
-    column_stat = slots_ref[:, 2 * width : 2 * width + 1]
-    totals = as_column(totals_ref[...], slot_y.shape[0])
+    experts = message_ref.shape[0]
+
+    def of_clip(values):
+        mine = lax.broadcasted_iota(jnp.int32, values.shape, 0) == clip_ref[0]
+        return jnp.sum(jnp.where(mine, values, 0.0), axis=0, keepdims=True)
+
+    slots = jnp.concatenate([of_clip(message_ref[slot]) for slot in range(experts)], axis=0)
+    slot_y = slots[:, :width].astype(bf16)
+    slot_dx = slots[:, width : 2 * width].astype(bf16)
+    slot_y_ref[...] = slot_y
+    slot_dx_ref[...] = slot_dx
+    column_stat = slots[:, 2 * width : 2 * width + 1]
+    totals = as_column(of_clip(totals_ref[...]), experts)
     exp_scores = exp_ref[...]
     combine_f = exp_scores / jnp.sum(exp_scores, axis=0, keepdims=True)
     comb_dot = lax.dot_general(slot_y, cot_ref[...], ROWS, preferred_element_type=f32)
@@ -314,24 +323,24 @@
         name="expert_rows",
     )(owned[None], message, expert_in, expert_out)
     message, hidden, row_cot = sum_to_all(message[None], group, (hidden, row_cot))
-    slots = lax.dynamic_index_in_dim(message, clip, 1, keepdims=False)
-    totals = lax.dynamic_index_in_dim(totals, clip, 0, keepdims=True)
     share = width // clips
     mine_x = lax.dynamic_slice_in_dim(row_x, clip * share, share, 1)
     mine_cot = lax.dynamic_slice_in_dim(row_cot, clip * share, share, 1)
     grad_expert_in = jnp.einsum("od,oh->dh", mine_x, pre_grad, preferred_element_type=f32)
     grad_expert_out = jnp.einsum("oh,od->hd", hidden, mine_cot, preferred_element_type=f32)
-    score_grad, dispatch, phi_part = pl.pallas_call(
+    score_grad, dispatch, phi_part, slot_y, slot_dx = pl.pallas_call(
         score_grads,
-        in_specs=[scalar] + [in_vmem] * 6,
+        in_specs=[scalar, scalar] + [in_vmem] * 6,
         out_shape=[
             jax.ShapeDtypeStruct((experts, count), bf16),
             jax.ShapeDtypeStruct((experts, count), bf16),
             jax.ShapeDtypeStruct((experts, width), f32),
+            jax.ShapeDtypeStruct((experts, width), bf16),
+            jax.ShapeDtypeStruct((experts, width), bf16),
         ],
         compiler_params=params,
         name="score_grads",
-    )(logit_scale, slots, totals, tok_in, tok_cot, tok_norm, exp_scores)
+    )(clip[None], logit_scale, message, totals, tok_in, tok_cot, tok_norm, exp_scores)
     phi_sum = phi_part
     for step in range(1, clips):
         phi_sum = phi_sum + hop(phi_part, step)
@@ -351,8 +360,6 @@
     phi_scale = lax.rsqrt(jnp.sum(phi_f32 * phi_f32, axis=1, keepdims=True) + epsilon)
     phi_unit = phi_f32 * phi_scale
     phi_norm = phi_unit.astype(bf16)
-    slot_y = slots[:, :width].astype(bf16)
-    slot_dx = slots[:, width : 2 * width].astype(bf16)
     mixed = jnp.einsum("sn,sd->nd", combine, slot_y, preferred_element_type=f32).astype(bf16)
     norm_grad = jnp.einsum("sn,sd->nd", score_grad, phi_norm, preferred_element_type=f32)
     through = jnp.einsum("sn,sd->nd", dispatch, slot_dx, preferred_element_type=f32)

time: 48.1 us -> 48.1 us (level)
  transfers between devices with their start and end apart: 20 -> 20, of which waited for: 11 -> 12; matrix products, arithmetic and copies ran while one was open for 16% -> 16% of each run, Pallas kernels for 4% -> 4%
where the time goes in v20:
time: 48.1 us; the launch traced here: 47.9 us
  starting transfers between devices  22.1 us (46%)
  waiting for transfers between devices  8.21 us (17%)
  Pallas kernels  8.05 us (17%)
  matrix products  7.52 us (16%)
  between operations  1.44 us (3%)
  other arithmetic  0.56 us (1%)
    ppermute x18, starting transfers between devices, exchange(): return lax.ppermute(value, AXES, pairs)  21.3 us
    ppermute x18, waiting for transfers between devices, exchange(): return lax.ppermute(value, AXES, pairs)  7.38 us
    pallas_call x1, Pallas kernels, per_device(): pl.pallas_call(token_sums, in_specs=[scalar, in_hbm, in_hbm, in_hbm], out...  2.71 us
    dot_general x1, matrix products, per_device(): jnp.einsum('sn,sd->nd', dispatch, slot_dx, preferred_element_type=f32)  1.98 us
    pallas_call x1, Pallas kernels, per_device(): pl.pallas_call(fetch, in_specs=[in_hbm] * 2, out_specs=[in_vmem] * 2, out...  1.94 us
    dot_general x1, matrix products, per_device(): jnp.einsum('sn,sd->nd', combine, slot_y, preferred_element_type=f32)  1.61 us
    dot_general x1, matrix products, per_device(): jnp.einsum('od,oh->dh', mine_x, pre_grad, preferred_element_type=f32)  1.59 us
    dot_general x1, matrix products, per_device(): jnp.einsum('oh,od->hd', hidden, mine_cot, preferred_element_type=f32)  1.59 us
  transfers between devices with their start and end apart: 20, of which 12 were waited for; matrix products, arithmetic and copies ran while one was open for 16% of the time, Pallas kernels for 4%

profile of v20, /device:TPU:0, one launch (start us, length us, event | category | flops | bytes accessed | tf_op | source)
XLA Modules:
  0.0 47.9 jit_solution(15673421667529912045)
XLA Ops:
  1.3 2.7 %token_sums.1 = (f32[2,2688]{1,0:T(2,128)S(1)}, f32[2,512]{1,0:T(2,128)S(1)}, bf16[2,512]{1,0:T(2,128)(2,1)S(1)}, f32[512,1]{1,0:T(8,128)S(1)}, bf16[512,1280]{1,0:T(8,128)(2,1)S(1)}) custom-call(f32[1]{0:T(128)S(6)} %copy.11.scale_ref, bf16[2,1280]{1,0:T(2,128)(2,1)} %bitcast.40, bf16[512,1280]{1,0:T(8,128)(2,1)} %bitcast.36, bf16[512,1280]{1,0:T(8,128)(2,1)} %bitcast.38), custom_call_target="tpu_custom_call" | custom-call | tf_op jit(solution)/shard_map/token_sums/pallas_call | solution.py:273
  4.0 0.5 %collective-permute-start = (f32[2,2688]{1,0:T(2,128)S(1)}, f32[2,2688]{1,0:T(2,128)S(1)}, u32[]{:S(2)}, u32[]{:S(2)}) collective-permute-start(f32[2,2688]{1,0:T(2,128)S(1)} %get-tuple-element.29), channel_id=1, source_target_pairs={{0,1},{1,0},{2,3},{3,2},{4,5},{5,4},{6,7},{7,6},{8,9},{9,8},{10,11... | collective-permute-start | bytes 64520 | tf_op jit(solution)/shard_map/ppermute | solution.py:29
  4.5 0.1 fusion.3
  4.7 0.7 %collective-permute-done = f32[2,2688]{1,0:T(2,128)S(1)} collective-permute-done((f32[2,2688]{1,0:T(2,128)S(1)}, f32[2,2688]{1,0:T(2,128)S(1)}, u32[]{:S(2)}, u32[]{:S(2)}) %collective-permute-start) | collective-permute-done | bytes 21536 | tf_op jit(solution)/shard_map/ppermute | solution.py:29
  5.4 0.1 broadcast_select_fusion
  5.5 3.8 %collective-permute-start.2 = (f32[1,2,2688]{2,1,0:T(2,128)S(1)}, f32[1,2,2688]{2,1,0:T(2,128)S(1)}, u32[]{:S(2)}, u32[]{:S(2)}) collective-permute-start(f32[1,2,2688]{2,1,0:T(2,128)S(1)} %get-tuple-element.53), channel_id=1, source_target_pairs={{0,17},{1,16},{2,19},{3,18},{4,21},{5,20},{6,23},{7,22},{8,25},{9,... | collective-permute-start | bytes 64520 | tf_op jit(solution)/shard_map/ppermute | solution.py:25
  9.3 1.3 %collective-permute-start.3 = (f32[1,2,2688]{2,1,0:T(2,128)S(1)}, f32[1,2,2688]{2,1,0:T(2,128)S(1)}, u32[]{:S(2)}, u32[]{:S(2)}) collective-permute-start(f32[1,2,2688]{2,1,0:T(2,128)S(1)} %get-tuple-element.52), channel_id=1, source_target_pairs={{0,25},{1,24},{2,27},{3,26},{4,29},{5,28},{6,31},{7,30},{8,17},{9,... | collective-permute-start | bytes 64520 | tf_op jit(solution)/shard_map/ppermute | solution.py:25
  10.6 0.2 collective-permute-start.1
  10.8 0.0 collective-permute-done.2
  10.8 3.6 %collective-permute-done.3 = f32[1,2,2688]{2,1,0:T(2,128)S(1)} collective-permute-done((f32[1,2,2688]{2,1,0:T(2,128)S(1)}, f32[1,2,2688]{2,1,0:T(2,128)S(1)}, u32[]{:S(2)}, u32[]{:S(2)}) %collective-permute-start.3) | collective-permute-done | bytes 21536 | tf_op jit(solution)/shard_map/ppermute | solution.py:25
  14.4 0.0 collective-permute-done.1
  14.4 2.5 %collective-permute-start.5 = (f32[1,2,2688]{2,1,0:T(2,128)S(1)}, f32[1,2,2688]{2,1,0:T(2,128)S(1)}, u32[]{:S(2)}, u32[]{:S(2)}) collective-permute-start(f32[1,2,2688]{2,1,0:T(2,128)S(1)} %add_add_fusion.1), channel_id=1, source_target_pairs={{0,7},{1,6},{2,5},{3,4},{4,3},{5,2},{6,1},{7,0},{8,15},{9,14},{10,... | collective-permute-start | bytes 64520 | tf_op jit(solution)/shard_map/ppermute | solution.py:25
  16.9 0.2 collective-permute-start.6
  17.1 0.6 %collective-permute-start.4 = (f32[1,2,2688]{2,1,0:T(2,128)S(1)}, f32[1,2,2688]{2,1,0:T(2,128)S(1)}, u32[]{:S(2)}, u32[]{:S(2)}) collective-permute-start(f32[1,2,2688]{2,1,0:T(2,128)S(1)} %add_add_fusion.1), channel_id=1, source_target_pairs={{0,3},{1,2},{2,1},{3,0},{4,7},{5,6},{6,5},{7,4},{8,11},{9,10},{10,... | collective-permute-start | bytes 64520 | tf_op jit(solution)/shard_map/ppermute | solution.py:25
  17.7 0.1 reduce
  17.9 1.9 %fetch_weights.1 = (bf16[1280,640]{1,0:T(8,128)(2,1)S(1)}, bf16[640,1280]{1,0:T(8,128)(2,1)S(1)}) custom-call(bf16[1280,640]{1,0:T(8,128)(2,1)} %in_ref, bf16[640,1280]{1,0:T(8,128)(2,1)} %out_ref), custom_call_target="tpu_custom_call" | custom-call | bytes 6553600 | tf_op jit(solution)/shard_map/fetch_weights/pallas_call | solution.py:295
  19.8 0.3 collective-permute-done.6
  20.1 0.2 collective-permute-done.4
  20.4 1.5 %expert_rows.1 = (f32[2,2688]{1,0:T(2,128)S(1)}, bf16[2,1280]{1,0:T(2,128)(2,1)S(1)}, bf16[2,1280]{1,0:T(2,128)(2,1)S(1)}, bf16[2,640]{1,0:T(2,128)(2,1)S(1)}, bf16[2,640]{1,0:T(2,128)(2,1)S(1)}) custom-call(s32[1]{0:T(128)} %bitcast.4.owned_ref, f32[2,2688]{1,0:T(2,128)S(1)} %add_bitcast_fusion.2.sums_ref, bf16[1280,640]{1,0:T(8,128)(2,1)S(1)} %get-tuple-element.33.in_ref, ...), custom_call_target="tpu_custom_call" | custom-call | tf_op jit(solution)/shard_map/expert_rows/pallas_call | solution.py:312
  21.9 1.6 %collective-permute-start.8 = (f32[1,2,2688]{2,1,0:T(2,128)S(1)}, f32[1,2,2688]{2,1,0:T(2,128)S(1)}, u32[]{:S(2)}, u32[]{:S(2)}) collective-permute-start(f32[1,2,2688]{2,1,0:T(2,128)S(1)} %bitcast.42), channel_id=1, source_target_pairs={{0,7},{1,6},{2,5},{3,4},{4,3},{5,2},{6,1},{7,0},{8,15},{9,14},{10,... | collective-permute-start | bytes 64520 | tf_op jit(solution)/shard_map/ppermute | solution.py:25
  23.5 0.6 %collective-permute-start.9 = (f32[1,2,2688]{2,1,0:T(2,128)S(1)}, f32[1,2,2688]{2,1,0:T(2,128)S(1)}, u32[]{:S(2)}, u32[]{:S(2)}) collective-permute-start(f32[1,2,2688]{2,1,0:T(2,128)S(1)} %bitcast.43), channel_id=1, source_target_pairs={{0,5},{1,4},{2,7},{3,6},{4,1},{5,0},{6,3},{7,2},{8,13},{9,12},{10,... | collective-permute-start | bytes 64520 | tf_op jit(solution)/shard_map/ppermute | solution.py:25
  24.1 1.1 %collective-permute-start.7 = (f32[1,2,2688]{2,1,0:T(2,128)S(1)}, f32[1,2,2688]{2,1,0:T(2,128)S(1)}, u32[]{:S(2)}, u32[]{:S(2)}) collective-permute-start(f32[1,2,2688]{2,1,0:T(2,128)S(1)} %bitcast.44), channel_id=1, source_target_pairs={{0,3},{1,2},{2,1},{3,0},{4,7},{5,6},{6,5},{7,4},{8,11},{9,10},{10,... | collective-permute-start | bytes 64520 | tf_op jit(solution)/shard_map/ppermute | solution.py:25
  25.2 1.6 %fusion.9 = f32[640,640]{1,0:T(8,128)} fusion(bf16[2,640]{1,0:T(2,128)(2,1)S(1)} %get-tuple-element.47, bf16[2,1280]{1,0:T(2,128)(2,1)S(1)} %get-tuple-element.46, s32[]{:T(128)S(6)} %select_n.51), kind=kOutput, calls=%fused_computation.23 | convolution fusion | flops 1638400 | bytes 1643524 | tf_op jit(solution)/shard_map/od,oh->dh/dot_general | solution.py:329
  26.8 0.1 collective-permute-done.9
  26.9 0.4 collective-permute-done.7
  27.3 1.0 %collective-permute-start.11 = (f32[1,2,2688]{2,1,0:T(2,128)S(1)}, f32[1,2,2688]{2,1,0:T(2,128)S(1)}, u32[]{:S(2)}, u32[]{:S(2)}) collective-permute-start(f32[1,2,2688]{2,1,0:T(2,128)S(1)} %add_add_fusion), channel_id=1, source_target_pairs={{0,17},{1,16},{2,19},{3,18},{4,21},{5,20},{6,23},{7,22},{8,25},{9,... | collective-permute-start | bytes 64520 | tf_op jit(solution)/shard_map/ppermute | solution.py:25
  28.4 0.9 %collective-permute-start.12 = (f32[1,2,2688]{2,1,0:T(2,128)S(1)}, f32[1,2,2688]{2,1,0:T(2,128)S(1)}, u32[]{:S(2)}, u32[]{:S(2)}) collective-permute-start(f32[1,2,2688]{2,1,0:T(2,128)S(1)} %add_add_fusion), channel_id=1, source_target_pairs={{0,25},{1,24},{2,27},{3,26},{4,29},{5,28},{6,31},{7,30},{8,17},{9,... | collective-permute-start | bytes 64520 | tf_op jit(solution)/shard_map/ppermute | solution.py:25
  29.2 1.1 %collective-permute-start.10 = (f32[1,2,2688]{2,1,0:T(2,128)S(1)}, f32[1,2,2688]{2,1,0:T(2,128)S(1)}, u32[]{:S(2)}, u32[]{:S(2)}) collective-permute-start(f32[1,2,2688]{2,1,0:T(2,128)S(1)} %add_add_fusion), channel_id=1, source_target_pairs={{0,9},{1,8},{2,11},{3,10},{4,13},{5,12},{6,15},{7,14},{8,1},{9,0},... | collective-permute-start | bytes 64520 | tf_op jit(solution)/shard_map/ppermute | solution.py:25
  30.4 1.6 %fusion.7 = f32[640,640]{1,0:T(8,128)} fusion(bf16[2,640]{1,0:T(2,128)(2,1)S(1)} %get-tuple-element.48, bf16[2,1280]{1,0:T(2,128)(2,1)S(1)} %get-tuple-element.49, s32[]{:T(128)S(6)} %select_n.51), kind=kOutput, calls=%fused_computation.21 | convolution fusion | flops 1638400 | bytes 1643524 | tf_op jit(solution)/shard_map/oh,od->hd/dot_general | solution.py:330
  32.0 0.5 %collective-permute-done.10 = f32[1,2,2688]{2,1,0:T(2,128)S(1)} collective-permute-done((f32[1,2,2688]{2,1,0:T(2,128)S(1)}, f32[1,2,2688]{2,1,0:T(2,128)S(1)}, u32[]{:S(2)}, u32[]{:S(2)}) %collective-permute-start.10) | collective-permute-done | bytes 21536 | tf_op jit(solution)/shard_map/ppermute | solution.py:25
  32.5 0.9 %collective-permute-done.12 = f32[1,2,2688]{2,1,0:T(2,128)S(1)} collective-permute-done((f32[1,2,2688]{2,1,0:T(2,128)S(1)}, f32[1,2,2688]{2,1,0:T(2,128)S(1)}, u32[]{:S(2)}, u32[]{:S(2)}) %collective-permute-start.12) | collective-permute-done | bytes 21536 | tf_op jit(solution)/shard_map/ppermute | solution.py:25
  33.4 0.1 broadcast_select_fusion.1.message_ref
  33.5 1.1 %score_grads.1 = (bf16[2,512]{1,0:T(2,128)(2,1)S(1)}, bf16[2,512]{1,0:T(2,128)(2,1)S(1)}, f32[2,1280]{1,0:T(2,128)S(1)}, bf16[2,1280]{1,0:T(2,128)(2,1)S(1)}, bf16[2,1280]{1,0:T(2,128)(2,1)S(1)}) custom-call(s32[1]{0:T(128)} %bitcast.3.clip_ref, f32[1]{0:T(128)S(6)} %copy.11.scale_ref, f32[2,2,2688]{2,1,0:T(2,128)S(1)} %broadcast_select_fusion.1.message_ref, ...), custom_call_target="tpu_custom_call" | custom-call | tf_op jit(solution)/shard_map/score_grads/pallas_call | solution.py:331
  34.6 0.3 collective-permute-start.13
  34.9 0.7 %multiply_reduce_fusion = (f32[512]{0:T(512)S(1)}, f32[512,1280]{1,0:T(8,128)S(1)}) fusion(f32[512]{0:T(512)S(1)} %reduce, bf16[1,512,1280]{2,1,0:T(8,128)(2,1)S(1)} %copy-done, bf16[2,512]{1,0:T(2,128)(2,1)S(1)} %get-tuple-element.45, f32[2]{0:T(128)S(1)} %add_rsqrt_fusion, bf16[1280,2]{0,1:T(2,128)(2,1)S(1)} %copy-done.2), kind=kOutput, calls=%fused_computation.5 | convolution fusion | flops 5250048 | bytes 3943432 | tf_op jit(solution)/shard_map/sn,sd->nd/dot_general | solution.py:364
  35.6 0.1 collective-permute-done.13
  35.8 2.3 %collective-permute-start.15 = (f32[1,2,1280]{2,1,0:T(2,128)S(1)}, f32[1,2,1280]{2,1,0:T(2,128)S(1)}, u32[]{:S(2)}, u32[]{:S(2)}) collective-permute-start(f32[1,2,1280]{2,1,0:T(2,128)S(1)} %add_bitcast_fusion.3), channel_id=1, source_target_pairs={{0,7},{1,6},{2,5},{3,4},{4,3},{5,2},{6,1},{7,0},{8,15},{9,14},{10,... | collective-permute-start | bytes 30728 | tf_op jit(solution)/shard_map/ppermute | solution.py:25
  38.0 0.2 collective-permute-start.16
  38.2 0.7 %collective-permute-start.14 = (f32[1,2,1280]{2,1,0:T(2,128)S(1)}, f32[1,2,1280]{2,1,0:T(2,128)S(1)}, u32[]{:S(2)}, u32[]{:S(2)}) collective-permute-start(f32[1,2,1280]{2,1,0:T(2,128)S(1)} %add_bitcast_fusion.3), channel_id=1, source_target_pairs={{0,3},{1,2},{2,1},{3,0},{4,7},{5,6},{6,5},{7,4},{8,11},{9,10},{10,... | collective-permute-start | bytes 30728 | tf_op jit(solution)/shard_map/ppermute | solution.py:25
  38.9 2.0 %fusion.1 = bf16[1,512,1280]{2,1,0:T(8,128)(2,1)} fusion(bf16[2,512]{1,0:T(2,128)(2,1)S(1)} %get-tuple-element.42, bf16[2,1280]{1,0:T(2,128)(2,1)S(1)} %get-tuple-element.43, f32[512,1280]{1,0:T(8,128)S(1)} %get-tuple-element.55, f32[512]{0:T(512)S(1)} %get-tuple-element.54, f32[512]{0:T(512)S(1)} %reduce, bf16[1,512,1280]{2,1,0:T(8,128)(2,1)S(1)} %copy-done), kind=kOutput, calls=%fused_computation.3 | convolution fusion | flops 7208960 | bytes 5254144 | tf_op jit(solution)/shard_map/sn,sd->nd/dot_general | solution.py:365
  40.9 0.2 collective-permute-done.16
  41.1 0.2 collective-permute-done.14
  41.4 0.9 %collective-permute-start.17 = (f32[1,2,1280]{2,1,0:T(2,128)S(1)}, f32[1,2,1280]{2,1,0:T(2,128)S(1)}, u32[]{:S(2)}, u32[]{:S(2)}) collective-permute-start(f32[1,2,1280]{2,1,0:T(2,128)S(1)} %add_add_fusion.2.refs_0_), channel_id=1, source_target_pairs={{0,17},{1,16},{2,19},{3,18},{4,21},{5,20},{6,23},{7,22},{8,25},{9,... | collective-permute-start | bytes 30728 | tf_op jit(solution)/shard_map/ppermute | solution.py:25
  42.2 1.7 %collective-permute-start.18 = (f32[1,2,1280]{2,1,0:T(2,128)S(1)}, f32[1,2,1280]{2,1,0:T(2,128)S(1)}, u32[]{:S(2)}, u32[]{:S(2)}) collective-permute-start(f32[1,2,1280]{2,1,0:T(2,128)S(1)} %add_add_fusion.2.refs_0_), channel_id=1, source_target_pairs={{0,25},{1,24},{2,27},{3,26},{4,29},{5,28},{6,31},{7,30},{8,17},{9,... | collective-permute-start | bytes 30728 | tf_op jit(solution)/shard_map/ppermute | solution.py:25
  43.9 0.7 %collective-permute-start.19 = (f32[1,2,1280]{2,1,0:T(2,128)S(1)}, f32[1,2,1280]{2,1,0:T(2,128)S(1)}, u32[]{:S(2)}, u32[]{:S(2)}) collective-permute-start(f32[1,2,1280]{2,1,0:T(2,128)S(1)} %add_add_fusion.2.refs_0_), channel_id=1, source_target_pairs={{0,9},{1,8},{2,11},{3,10},{4,13},{5,12},{6,15},{7,14},{8,1},{9,0},... | collective-permute-start | bytes 30728 | tf_op jit(solution)/shard_map/ppermute | solution.py:25
  44.6 1.6 %fusion.2 = bf16[1,512,1280]{2,1,0:T(8,128)(2,1)} fusion(bf16[2,512]{1,0:T(2,128)(2,1)S(1)} %get-tuple-element.28, bf16[2,1280]{1,0:T(2,128)(2,1)S(1)} %get-tuple-element.41), kind=kOutput, calls=%fused_computation.4 | convolution fusion | flops 3276800 | bytes 1317888 | tf_op jit(solution)/shard_map/sn,sd->nd/dot_general | solution.py:363
  46.2 0.9 %collective-permute-done.18.refs_2_ = f32[1,2,1280]{2,1,0:T(2,128)S(1)} collective-permute-done((f32[1,2,1280]{2,1,0:T(2,128)S(1)}, f32[1,2,1280]{2,1,0:T(2,128)S(1)}, u32[]{:S(2)}, u32[]{:S(2)}) %collective-permute-start.18) | collective-permute-done | bytes 10272 | tf_op jit(solution)/shard_map/ppermute | solution.py:25
  47.1 0.8 %finish.1 = f32[2,1280]{1,0:T(2,128)} custom-call(bf16[2,1280]{1,0:T(2,128)(2,1)S(1)} %bitcast.41, f32[1,2,1280]{2,1,0:T(2,128)S(1)} %add_add_fusion.2.refs_0_, f32[1,2,1280]{2,1,0:T(2,128)S(1)} %collective-permute-done.17.refs_1_, f32[1,2,1280]{2,1,0:T(2,128)S(1)} %collective-permute-done.18.refs_2_, f32[1,2,1280]{2,1,0:T(2,128)S(1)} %collective-permute-done.19.refs_3_), custom_call_target="tpu_custom_call" | custom-call | tf_op jit(solution)/shard_map/finish/pallas_call | solution.py:352
  (24 shorter events, 0.2 us)
Async XLA Ops:
  0.6 3.9 %copy-start.2 = (bf16[1280,2]{0,1:T(2,128)(2,1)S(1)}, bf16[1280,2]{0,1:T(2,128)(2,1)}, u32[]{:S(2)}) copy-start(bf16[1280,2]{0,1:T(2,128)(2,1)} %param.8) | copy-start | bytes 15364
  4.0 1.4 %collective-permute-start = (f32[2,2688]{1,0:T(2,128)S(1)}, f32[2,2688]{1,0:T(2,128)S(1)}, u32[]{:S(2)}, u32[]{:S(2)}) collective-permute-start(f32[2,2688]{1,0:T(2,128)S(1)} %get-tuple-element.29), channel_id=1, source_target_pairs={{0,1},{1,0},{2,3},{3,2},{4,5},{5,4},{6,7},{7,6},{8,9},{9,8},{10,11... | collective-permute-start | bytes 64520 | tf_op jit(solution)/shard_map/ppermute | solution.py:29
  5.5 5.3 %collective-permute-start.2 = (f32[1,2,2688]{2,1,0:T(2,128)S(1)}, f32[1,2,2688]{2,1,0:T(2,128)S(1)}, u32[]{:S(2)}, u32[]{:S(2)}) collective-permute-start(f32[1,2,2688]{2,1,0:T(2,128)S(1)} %get-tuple-element.53), channel_id=1, source_target_pairs={{0,17},{1,16},{2,19},{3,18},{4,21},{5,20},{6,23},{7,22},{8,25},{9,... | collective-permute-start | bytes 64520 | tf_op jit(solution)/shard_map/ppermute | solution.py:25
  9.3 5.1 %collective-permute-start.3 = (f32[1,2,2688]{2,1,0:T(2,128)S(1)}, f32[1,2,2688]{2,1,0:T(2,128)S(1)}, u32[]{:S(2)}, u32[]{:S(2)}) collective-permute-start(f32[1,2,2688]{2,1,0:T(2,128)S(1)} %get-tuple-element.52), channel_id=1, source_target_pairs={{0,25},{1,24},{2,27},{3,26},{4,29},{5,28},{6,31},{7,30},{8,17},{9,... | collective-permute-start | bytes 64520 | tf_op jit(solution)/shard_map/ppermute | solution.py:25
  10.6 3.8 %collective-permute-start.1 = (f32[1,2,2688]{2,1,0:T(2,128)S(1)}, f32[1,2,2688]{2,1,0:T(2,128)S(1)}, u32[]{:S(2)}, u32[]{:S(2)}) collective-permute-start(f32[1,2,2688]{2,1,0:T(2,128)S(1)} %get-tuple-element.51), channel_id=1, source_target_pairs={{0,9},{1,8},{2,11},{3,10},{4,13},{5,12},{6,15},{7,14},{8,1},{9,0},... | collective-permute-start | bytes 64520 | tf_op jit(solution)/shard_map/ppermute | solution.py:25
  14.4 5.4 %collective-permute-start.5 = (f32[1,2,2688]{2,1,0:T(2,128)S(1)}, f32[1,2,2688]{2,1,0:T(2,128)S(1)}, u32[]{:S(2)}, u32[]{:S(2)}) collective-permute-start(f32[1,2,2688]{2,1,0:T(2,128)S(1)} %add_add_fusion.1), channel_id=1, source_target_pairs={{0,7},{1,6},{2,5},{3,4},{4,3},{5,2},{6,1},{7,0},{8,15},{9,14},{10,... | collective-permute-start | bytes 64520 | tf_op jit(solution)/shard_map/ppermute | solution.py:25
  16.9 3.2 %collective-permute-start.6 = (f32[1,2,2688]{2,1,0:T(2,128)S(1)}, f32[1,2,2688]{2,1,0:T(2,128)S(1)}, u32[]{:S(2)}, u32[]{:S(2)}) collective-permute-start(f32[1,2,2688]{2,1,0:T(2,128)S(1)} %add_add_fusion.1), channel_id=1, source_target_pairs={{0,5},{1,4},{2,7},{3,6},{4,1},{5,0},{6,3},{7,2},{8,13},{9,12},{10,... | collective-permute-start | bytes 64520 | tf_op jit(solution)/shard_map/ppermute | solution.py:25
  17.1 3.2 %collective-permute-start.4 = (f32[1,2,2688]{2,1,0:T(2,128)S(1)}, f32[1,2,2688]{2,1,0:T(2,128)S(1)}, u32[]{:S(2)}, u32[]{:S(2)}) collective-permute-start(f32[1,2,2688]{2,1,0:T(2,128)S(1)} %add_add_fusion.1), channel_id=1, source_target_pairs={{0,3},{1,2},{2,1},{3,0},{4,7},{5,6},{6,5},{7,4},{8,11},{9,10},{10,... | collective-permute-start | bytes 64520 | tf_op jit(solution)/shard_map/ppermute | solution.py:25
  21.9 11.6 %copy-start = (bf16[1,512,1280]{2,1,0:T(8,128)(2,1)S(1)}, bf16[1,512,1280]{2,1,0:T(8,128)(2,1)}, u32[]{:S(2)}) copy-start(bf16[1,512,1280]{2,1,0:T(8,128)(2,1)} %param.6) | copy-start | bytes 3932164
  21.9 11.6 %copy-start.1 = (bf16[1,512,1280]{2,1,0:T(8,128)(2,1)S(1)}, bf16[1,512,1280]{2,1,0:T(8,128)(2,1)}, u32[]{:S(2)}) copy-start(bf16[1,512,1280]{2,1,0:T(8,128)(2,1)} %param.7) | copy-start | bytes 3932164
  21.9 4.9 %collective-permute-start.8 = (f32[1,2,2688]{2,1,0:T(2,128)S(1)}, f32[1,2,2688]{2,1,0:T(2,128)S(1)}, u32[]{:S(2)}, u32[]{:S(2)}) collective-permute-start(f32[1,2,2688]{2,1,0:T(2,128)S(1)} %bitcast.42), channel_id=1, source_target_pairs={{0,7},{1,6},{2,5},{3,4},{4,3},{5,2},{6,1},{7,0},{8,15},{9,14},{10,... | collective-permute-start | bytes 64520 | tf_op jit(solution)/shard_map/ppermute | solution.py:25
  23.5 3.4 %collective-permute-start.9 = (f32[1,2,2688]{2,1,0:T(2,128)S(1)}, f32[1,2,2688]{2,1,0:T(2,128)S(1)}, u32[]{:S(2)}, u32[]{:S(2)}) collective-permute-start(f32[1,2,2688]{2,1,0:T(2,128)S(1)} %bitcast.43), channel_id=1, source_target_pairs={{0,5},{1,4},{2,7},{3,6},{4,1},{5,0},{6,3},{7,2},{8,13},{9,12},{10,... | collective-permute-start | bytes 64520 | tf_op jit(solution)/shard_map/ppermute | solution.py:25
  24.1 3.2 %collective-permute-start.7 = (f32[1,2,2688]{2,1,0:T(2,128)S(1)}, f32[1,2,2688]{2,1,0:T(2,128)S(1)}, u32[]{:S(2)}, u32[]{:S(2)}) collective-permute-start(f32[1,2,2688]{2,1,0:T(2,128)S(1)} %bitcast.44), channel_id=1, source_target_pairs={{0,3},{1,2},{2,1},{3,0},{4,7},{5,6},{6,5},{7,4},{8,11},{9,10},{10,... | collective-permute-start | bytes 64520 | tf_op jit(solution)/shard_map/ppermute | solution.py:25
  27.3 5.1 %collective-permute-start.11 = (f32[1,2,2688]{2,1,0:T(2,128)S(1)}, f32[1,2,2688]{2,1,0:T(2,128)S(1)}, u32[]{:S(2)}, u32[]{:S(2)}) collective-permute-start(f32[1,2,2688]{2,1,0:T(2,128)S(1)} %add_add_fusion), channel_id=1, source_target_pairs={{0,17},{1,16},{2,19},{3,18},{4,21},{5,20},{6,23},{7,22},{8,25},{9,... | collective-permute-start | bytes 64520 | tf_op jit(solution)/shard_map/ppermute | solution.py:25
  28.4 5.0 %collective-permute-start.12 = (f32[1,2,2688]{2,1,0:T(2,128)S(1)}, f32[1,2,2688]{2,1,0:T(2,128)S(1)}, u32[]{:S(2)}, u32[]{:S(2)}) collective-permute-start(f32[1,2,2688]{2,1,0:T(2,128)S(1)} %add_add_fusion), channel_id=1, source_target_pairs={{0,25},{1,24},{2,27},{3,26},{4,29},{5,28},{6,31},{7,30},{8,17},{9,... | collective-permute-start | bytes 64520 | tf_op jit(solution)/shard_map/ppermute | solution.py:25
  29.2 3.2 %collective-permute-start.10 = (f32[1,2,2688]{2,1,0:T(2,128)S(1)}, f32[1,2,2688]{2,1,0:T(2,128)S(1)}, u32[]{:S(2)}, u32[]{:S(2)}) collective-permute-start(f32[1,2,2688]{2,1,0:T(2,128)S(1)} %add_add_fusion), channel_id=1, source_target_pairs={{0,9},{1,8},{2,11},{3,10},{4,13},{5,12},{6,15},{7,14},{8,1},{9,0},... | collective-permute-start | bytes 64520 | tf_op jit(solution)/shard_map/ppermute | solution.py:25
  34.6 1.2 %collective-permute-start.13 = (f32[2,1280]{1,0:T(2,128)S(1)}, f32[2,1280]{1,0:T(2,128)S(1)}, u32[]{:S(2)}, u32[]{:S(2)}) collective-permute-start(f32[2,1280]{1,0:T(2,128)S(1)} %get-tuple-element.50), channel_id=1, source_target_pairs={{0,1},{1,0},{2,3},{3,2},{4,5},{5,4},{6,7},{7,6},{8,9},{9,8},{10,11... | collective-permute-start | bytes 30728 | tf_op jit(solution)/shard_map/ppermute | solution.py:29
  35.8 5.1 %collective-permute-start.15 = (f32[1,2,1280]{2,1,0:T(2,128)S(1)}, f32[1,2,1280]{2,1,0:T(2,128)S(1)}, u32[]{:S(2)}, u32[]{:S(2)}) collective-permute-start(f32[1,2,1280]{2,1,0:T(2,128)S(1)} %add_bitcast_fusion.3), channel_id=1, source_target_pairs={{0,7},{1,6},{2,5},{3,4},{4,3},{5,2},{6,1},{7,0},{8,15},{9,14},{10,... | collective-permute-start | bytes 30728 | tf_op jit(solution)/shard_map/ppermute | solution.py:25
  38.0 3.1 %collective-permute-start.16 = (f32[1,2,1280]{2,1,0:T(2,128)S(1)}, f32[1,2,1280]{2,1,0:T(2,128)S(1)}, u32[]{:S(2)}, u32[]{:S(2)}) collective-permute-start(f32[1,2,1280]{2,1,0:T(2,128)S(1)} %add_bitcast_fusion.3), channel_id=1, source_target_pairs={{0,5},{1,4},{2,7},{3,6},{4,1},{5,0},{6,3},{7,2},{8,13},{9,12},{10,... | collective-permute-start | bytes 30728 | tf_op jit(solution)/shard_map/ppermute | solution.py:25
  38.2 3.1 %collective-permute-start.14 = (f32[1,2,1280]{2,1,0:T(2,128)S(1)}, f32[1,2,1280]{2,1,0:T(2,128)S(1)}, u32[]{:S(2)}, u32[]{:S(2)}) collective-permute-start(f32[1,2,1280]{2,1,0:T(2,128)S(1)} %add_bitcast_fusion.3), channel_id=1, source_target_pairs={{0,3},{1,2},{2,1},{3,0},{4,7},{5,6},{6,5},{7,4},{8,11},{9,10},{10,... | collective-permute-start | bytes 30728 | tf_op jit(solution)/shard_map/ppermute | solution.py:25
  41.4 4.8 %collective-permute-start.17 = (f32[1,2,1280]{2,1,0:T(2,128)S(1)}, f32[1,2,1280]{2,1,0:T(2,128)S(1)}, u32[]{:S(2)}, u32[]{:S(2)}) collective-permute-start(f32[1,2,1280]{2,1,0:T(2,128)S(1)} %add_add_fusion.2.refs_0_), channel_id=1, source_target_pairs={{0,17},{1,16},{2,19},{3,18},{4,21},{5,20},{6,23},{7,22},{8,25},{9,... | collective-permute-start | bytes 30728 | tf_op jit(solution)/shard_map/ppermute | solution.py:25
  42.2 4.9 %collective-permute-start.18 = (f32[1,2,1280]{2,1,0:T(2,128)S(1)}, f32[1,2,1280]{2,1,0:T(2,128)S(1)}, u32[]{:S(2)}, u32[]{:S(2)}) collective-permute-start(f32[1,2,1280]{2,1,0:T(2,128)S(1)} %add_add_fusion.2.refs_0_), channel_id=1, source_target_pairs={{0,25},{1,24},{2,27},{3,26},{4,29},{5,28},{6,31},{7,30},{8,17},{9,... | collective-permute-start | bytes 30728 | tf_op jit(solution)/shard_map/ppermute | solution.py:25
  43.9 3.2 %collective-permute-start.19 = (f32[1,2,1280]{2,1,0:T(2,128)S(1)}, f32[1,2,1280]{2,1,0:T(2,128)S(1)}, u32[]{:S(2)}, u32[]{:S(2)}) collective-permute-start(f32[1,2,1280]{2,1,0:T(2,128)S(1)} %add_add_fusion.2.refs_0_), channel_id=1, source_target_pairs={{0,9},{1,8},{2,11},{3,10},{4,13},{5,12},{6,15},{7,14},{8,1},{9,0},... | collective-permute-start | bytes 30728 | tf_op jit(solution)/shard_map/ppermute | solution.py:25

commit v21 on v19

--- a/solution.py
+++ b/solution.py
@@ -126,19 +126,23 @@
     ]
     for copy in tok_copies + [phi_copy] + cot_copies:
         copy.start()
+    cosines = []
     for index in range(0, blocks, 2):
         for copy in tok_copies[index : index + 2]:
             copy.wait()
         piece = pl.ds(index * rows, 2 * rows)
         tok_f32 = tok_buf[piece, :].astype(f32)
         tok_scale = lax.rsqrt(jnp.sum(tok_f32 * tok_f32, axis=1, keepdims=True) + epsilon)
-        norm_ref[piece, :] = (tok_f32 * tok_scale).astype(bf16)
+        tok_norm = (tok_f32 * tok_scale).astype(bf16)
+        norm_ref[piece, :] = tok_norm
         tok_scale_ref[piece, :] = tok_scale
-    phi_copy.wait()
-    phi = phi_buf[...].astype(f32)
-    phi_scale = lax.rsqrt(jnp.sum(phi * phi, axis=1, keepdims=True) + epsilon)
-    phi_norm = (phi * phi_scale).astype(bf16)
-    logits = scale_ref[0] * lax.dot_general(phi_norm, norm_ref[...], ROWS, preferred_element_type=f32)
+        if not index:
+            phi_copy.wait()
+            phi = phi_buf[...].astype(f32)
+            phi_scale = lax.rsqrt(jnp.sum(phi * phi, axis=1, keepdims=True) + epsilon)
+            phi_norm = (phi * phi_scale).astype(bf16)
+        cosines.append(lax.dot_general(phi_norm, tok_norm, ROWS, preferred_element_type=f32))
+    logits = scale_ref[0] * jnp.concatenate(cosines, axis=1)
     exp_scores = jnp.exp(logits)
     combine = (exp_scores / jnp.sum(exp_scores, axis=0, keepdims=True)).astype(bf16)
     exp_high = exp_scores.astype(bf16).astype(f32)

time: 48.1 us -> 48.7 us (1.012)
  Pallas kernels: 8.05 us -> 8.63 us
    pallas_call x1, Pallas kernels: 2.71 us -> 3.29 us  [per_device(): pl.pallas_call(token_sums, in_specs=[scalar, in_hbm, in_hbm, in_hbm], out...]
where the time goes in v21:
time: 48.7 us; the launch traced here: 48.5 us
  starting transfers between devices  22.1 us (45%)
  Pallas kernels  8.63 us (18%)
  waiting for transfers between devices  8.13 us (17%)
  matrix products  7.52 us (15%)
  between operations  1.46 us (3%)
  other arithmetic  0.56 us (1%)
    ppermute x18, starting transfers between devices, exchange(): return lax.ppermute(value, AXES, pairs)  21.3 us
    ppermute x18, waiting for transfers between devices, exchange(): return lax.ppermute(value, AXES, pairs)  7.29 us
    pallas_call x1, Pallas kernels, per_device(): pl.pallas_call(token_sums, in_specs=[scalar, in_hbm, in_hbm, in_hbm], out...  3.29 us
    dot_general x1, matrix products, per_device(): jnp.einsum('sn,sd->nd', dispatch, slot_dx, preferred_element_type=f32)  1.99 us
    pallas_call x1, Pallas kernels, per_device(): pl.pallas_call(fetch, in_specs=[in_hbm] * 2, out_specs=[in_vmem] * 2, out...  1.94 us
    dot_general x1, matrix products, per_device(): jnp.einsum('sn,sd->nd', combine, slot_y, preferred_element_type=f32)  1.61 us
    dot_general x1, matrix products, per_device(): jnp.einsum('od,oh->dh', mine_x, pre_grad, preferred_element_type=f32)  1.59 us
    dot_general x1, matrix products, per_device(): jnp.einsum('oh,od->hd', hidden, mine_cot, preferred_element_type=f32)  1.59 us
  transfers between devices with their start and end apart: 20, of which 11 were waited for; matrix products, arithmetic and copies ran while one was open for 16% of the time, Pallas kernels for 4%

profile of v21, /device:TPU:0, one launch (start us, length us, event | category | flops | bytes accessed | tf_op | source)
XLA Modules:
  0.0 48.5 jit_solution(11080722816138724208)
XLA Ops:
  1.3 3.3 %token_sums.1 = (f32[2,2688]{1,0:T(2,128)S(1)}, f32[2,512]{1,0:T(2,128)S(1)}, bf16[2,512]{1,0:T(2,128)(2,1)S(1)}, f32[512,1]{1,0:T(8,128)S(1)}, bf16[512,1280]{1,0:T(8,128)(2,1)S(1)}) custom-call(f32[1]{0:T(128)S(6)} %copy.11.scale_ref, bf16[2,1280]{1,0:T(2,128)(2,1)} %bitcast.40, bf16[512,1280]{1,0:T(8,128)(2,1)} %bitcast.36, bf16[512,1280]{1,0:T(8,128)(2,1)} %bitcast.38), custom_call_target="tpu_custom_call" | custom-call | tf_op jit(solution)/shard_map/token_sums/pallas_call | solution.py:268
  4.6 0.5 %collective-permute-start = (f32[2,2688]{1,0:T(2,128)S(1)}, f32[2,2688]{1,0:T(2,128)S(1)}, u32[]{:S(2)}, u32[]{:S(2)}) collective-permute-start(f32[2,2688]{1,0:T(2,128)S(1)} %get-tuple-element.27), channel_id=1, source_target_pairs={{0,1},{1,0},{2,3},{3,2},{4,5},{5,4},{6,7},{7,6},{8,9},{9,8},{10,11... | collective-permute-start | bytes 64520 | tf_op jit(solution)/shard_map/ppermute | solution.py:29
  5.1 0.1 fusion.3
  5.3 0.7 %collective-permute-done = f32[2,2688]{1,0:T(2,128)S(1)} collective-permute-done((f32[2,2688]{1,0:T(2,128)S(1)}, f32[2,2688]{1,0:T(2,128)S(1)}, u32[]{:S(2)}, u32[]{:S(2)}) %collective-permute-start) | collective-permute-done | bytes 21536 | tf_op jit(solution)/shard_map/ppermute | solution.py:29
  6.0 0.1 broadcast_select_fusion
  6.1 3.8 %collective-permute-start.2 = (f32[1,2,2688]{2,1,0:T(2,128)S(1)}, f32[1,2,2688]{2,1,0:T(2,128)S(1)}, u32[]{:S(2)}, u32[]{:S(2)}) collective-permute-start(f32[1,2,2688]{2,1,0:T(2,128)S(1)} %get-tuple-element.51), channel_id=1, source_target_pairs={{0,17},{1,16},{2,19},{3,18},{4,21},{5,20},{6,23},{7,22},{8,25},{9,... | collective-permute-start | bytes 64520 | tf_op jit(solution)/shard_map/ppermute | solution.py:25
  9.8 1.3 %collective-permute-start.3 = (f32[1,2,2688]{2,1,0:T(2,128)S(1)}, f32[1,2,2688]{2,1,0:T(2,128)S(1)}, u32[]{:S(2)}, u32[]{:S(2)}) collective-permute-start(f32[1,2,2688]{2,1,0:T(2,128)S(1)} %get-tuple-element.50), channel_id=1, source_target_pairs={{0,25},{1,24},{2,27},{3,26},{4,29},{5,28},{6,31},{7,30},{8,17},{9,... | collective-permute-start | bytes 64520 | tf_op jit(solution)/shard_map/ppermute | solution.py:25
  11.1 0.2 collective-permute-start.1
  11.4 0.0 collective-permute-done.2
  11.4 3.6 %collective-permute-done.3 = f32[1,2,2688]{2,1,0:T(2,128)S(1)} collective-permute-done((f32[1,2,2688]{2,1,0:T(2,128)S(1)}, f32[1,2,2688]{2,1,0:T(2,128)S(1)}, u32[]{:S(2)}, u32[]{:S(2)}) %collective-permute-start.3) | collective-permute-done | bytes 21536 | tf_op jit(solution)/shard_map/ppermute | solution.py:25
  14.9 0.0 collective-permute-done.1
  15.0 2.5 %collective-permute-start.5 = (f32[1,2,2688]{2,1,0:T(2,128)S(1)}, f32[1,2,2688]{2,1,0:T(2,128)S(1)}, u32[]{:S(2)}, u32[]{:S(2)}) collective-permute-start(f32[1,2,2688]{2,1,0:T(2,128)S(1)} %add_add_fusion.1), channel_id=1, source_target_pairs={{0,7},{1,6},{2,5},{3,4},{4,3},{5,2},{6,1},{7,0},{8,15},{9,14},{10,... | collective-permute-start | bytes 64520 | tf_op jit(solution)/shard_map/ppermute | solution.py:25
  17.5 0.2 collective-permute-start.6
  17.7 0.6 %collective-permute-start.4 = (f32[1,2,2688]{2,1,0:T(2,128)S(1)}, f32[1,2,2688]{2,1,0:T(2,128)S(1)}, u32[]{:S(2)}, u32[]{:S(2)}) collective-permute-start(f32[1,2,2688]{2,1,0:T(2,128)S(1)} %add_add_fusion.1), channel_id=1, source_target_pairs={{0,3},{1,2},{2,1},{3,0},{4,7},{5,6},{6,5},{7,4},{8,11},{9,10},{10,... | collective-permute-start | bytes 64520 | tf_op jit(solution)/shard_map/ppermute | solution.py:25
  18.3 0.1 reduce
  18.4 1.9 %fetch_weights.1 = (bf16[1280,640]{1,0:T(8,128)(2,1)S(1)}, bf16[640,1280]{1,0:T(8,128)(2,1)S(1)}) custom-call(bf16[1280,640]{1,0:T(8,128)(2,1)} %in_ref, bf16[640,1280]{1,0:T(8,128)(2,1)} %out_ref), custom_call_target="tpu_custom_call" | custom-call | bytes 6553600 | tf_op jit(solution)/shard_map/fetch_weights/pallas_call | solution.py:290
  20.4 0.0 collective-permute-done.5
  20.4 0.3 collective-permute-done.6
  20.7 0.2 collective-permute-done.4
  20.9 1.5 %expert_rows.1 = (f32[2,2688]{1,0:T(2,128)S(1)}, bf16[2,1280]{1,0:T(2,128)(2,1)S(1)}, bf16[2,1280]{1,0:T(2,128)(2,1)S(1)}, bf16[2,640]{1,0:T(2,128)(2,1)S(1)}, bf16[2,640]{1,0:T(2,128)(2,1)S(1)}) custom-call(s32[1]{0:T(128)} %bitcast.3.owned_ref, f32[2,2688]{1,0:T(2,128)S(1)} %add_bitcast_fusion.2.sums_ref, bf16[1280,640]{1,0:T(8,128)(2,1)S(1)} %get-tuple-element.31.in_ref, ...), custom_call_target="tpu_custom_call" | custom-call | tf_op jit(solution)/shard_map/expert_rows/pallas_call | solution.py:307
  22.5 1.6 %collective-permute-start.8 = (f32[1,2,2688]{2,1,0:T(2,128)S(1)}, f32[1,2,2688]{2,1,0:T(2,128)S(1)}, u32[]{:S(2)}, u32[]{:S(2)}) collective-permute-start(f32[1,2,2688]{2,1,0:T(2,128)S(1)} %bitcast.42), channel_id=1, source_target_pairs={{0,7},{1,6},{2,5},{3,4},{4,3},{5,2},{6,1},{7,0},{8,15},{9,14},{10,... | collective-permute-start | bytes 64520 | tf_op jit(solution)/shard_map/ppermute | solution.py:25
  24.1 0.6 %collective-permute-start.9 = (f32[1,2,2688]{2,1,0:T(2,128)S(1)}, f32[1,2,2688]{2,1,0:T(2,128)S(1)}, u32[]{:S(2)}, u32[]{:S(2)}) collective-permute-start(f32[1,2,2688]{2,1,0:T(2,128)S(1)} %bitcast.43), channel_id=1, source_target_pairs={{0,5},{1,4},{2,7},{3,6},{4,1},{5,0},{6,3},{7,2},{8,13},{9,12},{10,... | collective-permute-start | bytes 64520 | tf_op jit(solution)/shard_map/ppermute | solution.py:25
  24.7 1.1 %collective-permute-start.7 = (f32[1,2,2688]{2,1,0:T(2,128)S(1)}, f32[1,2,2688]{2,1,0:T(2,128)S(1)}, u32[]{:S(2)}, u32[]{:S(2)}) collective-permute-start(f32[1,2,2688]{2,1,0:T(2,128)S(1)} %bitcast.44), channel_id=1, source_target_pairs={{0,3},{1,2},{2,1},{3,0},{4,7},{5,6},{6,5},{7,4},{8,11},{9,10},{10,... | collective-permute-start | bytes 64520 | tf_op jit(solution)/shard_map/ppermute | solution.py:25
  25.8 1.6 %fusion.11 = f32[640,640]{1,0:T(8,128)} fusion(bf16[2,640]{1,0:T(2,128)(2,1)S(1)} %get-tuple-element.43, bf16[2,1280]{1,0:T(2,128)(2,1)S(1)} %get-tuple-element.42, s32[]{:T(128)S(6)} %select_n.63), kind=kOutput, calls=%fused_computation.25 | convolution fusion | flops 1638400 | bytes 1643524 | tf_op jit(solution)/shard_map/od,oh->dh/dot_general | solution.py:326
  27.4 0.1 collective-permute-done.9
  27.5 0.4 collective-permute-done.7
  27.9 1.0 %collective-permute-start.11 = (f32[1,2,2688]{2,1,0:T(2,128)S(1)}, f32[1,2,2688]{2,1,0:T(2,128)S(1)}, u32[]{:S(2)}, u32[]{:S(2)}) collective-permute-start(f32[1,2,2688]{2,1,0:T(2,128)S(1)} %add_add_fusion), channel_id=1, source_target_pairs={{0,17},{1,16},{2,19},{3,18},{4,21},{5,20},{6,23},{7,22},{8,25},{9,... | collective-permute-start | bytes 64520 | tf_op jit(solution)/shard_map/ppermute | solution.py:25
  29.0 0.9 %collective-permute-start.12 = (f32[1,2,2688]{2,1,0:T(2,128)S(1)}, f32[1,2,2688]{2,1,0:T(2,128)S(1)}, u32[]{:S(2)}, u32[]{:S(2)}) collective-permute-start(f32[1,2,2688]{2,1,0:T(2,128)S(1)} %add_add_fusion), channel_id=1, source_target_pairs={{0,25},{1,24},{2,27},{3,26},{4,29},{5,28},{6,31},{7,30},{8,17},{9,... | collective-permute-start | bytes 64520 | tf_op jit(solution)/shard_map/ppermute | solution.py:25
  29.8 1.1 %collective-permute-start.10 = (f32[1,2,2688]{2,1,0:T(2,128)S(1)}, f32[1,2,2688]{2,1,0:T(2,128)S(1)}, u32[]{:S(2)}, u32[]{:S(2)}) collective-permute-start(f32[1,2,2688]{2,1,0:T(2,128)S(1)} %add_add_fusion), channel_id=1, source_target_pairs={{0,9},{1,8},{2,11},{3,10},{4,13},{5,12},{6,15},{7,14},{8,1},{9,0},... | collective-permute-start | bytes 64520 | tf_op jit(solution)/shard_map/ppermute | solution.py:25
  30.9 1.6 %fusion.9 = f32[640,640]{1,0:T(8,128)} fusion(bf16[2,640]{1,0:T(2,128)(2,1)S(1)} %get-tuple-element.44, bf16[2,1280]{1,0:T(2,128)(2,1)S(1)} %get-tuple-element.45, s32[]{:T(128)S(6)} %select_n.63), kind=kOutput, calls=%fused_computation.23 | convolution fusion | flops 1638400 | bytes 1643524 | tf_op jit(solution)/shard_map/oh,od->hd/dot_general | solution.py:327
  32.5 1.4 %collective-permute-done.12 = f32[1,2,2688]{2,1,0:T(2,128)S(1)} collective-permute-done((f32[1,2,2688]{2,1,0:T(2,128)S(1)}, f32[1,2,2688]{2,1,0:T(2,128)S(1)}, u32[]{:S(2)}, u32[]{:S(2)}) %collective-permute-start.12) | collective-permute-done | bytes 21536 | tf_op jit(solution)/shard_map/ppermute | solution.py:25
  34.1 0.1 fusion.16
  34.2 1.1 %score_grads.1 = (bf16[2,512]{1,0:T(2,128)(2,1)S(1)}, bf16[2,512]{1,0:T(2,128)(2,1)S(1)}, f32[2,1280]{1,0:T(2,128)S(1)}) custom-call(f32[1]{0:T(128)S(6)} %copy.11.scale_ref, f32[2,2688]{1,0:T(2,128)S(1)} %get-tuple-element.48.slots_ref, f32[1,128]{1,0:T(1,128)S(1)} %constant_dynamic-slice_fusion.1.totals_ref, bf16[512,1280]{1,0:T(8,128)(2,1)S(1)} %bitcast.37, ...), custom_call_target="tpu_custom_call" | custom-call | tf_op jit(solution)/shard_map/score_grads/pallas_call | solution.py:328
  35.2 0.3 collective-permute-start.13
  35.5 0.7 %multiply_reduce_fusion = (f32[512]{0:T(512)S(1)}, f32[512,1280]{1,0:T(8,128)S(1)}) fusion(f32[512]{0:T(512)S(1)} %reduce, bf16[1,512,1280]{2,1,0:T(8,128)(2,1)S(1)} %copy-done, bf16[2,512]{1,0:T(2,128)(2,1)S(1)} %get-tuple-element.41, f32[2]{0:T(128)S(1)} %add_rsqrt_fusion, bf16[1280,2]{0,1:T(2,128)(2,1)S(1)} %copy-done.2), kind=kOutput, calls=%fused_computation.5 | convolution fusion | flops 5250048 | bytes 3943432 | tf_op jit(solution)/shard_map/sn,sd->nd/dot_general | solution.py:361
  36.3 0.1 collective-permute-done.13
  36.4 2.3 %collective-permute-start.15 = (f32[1,2,1280]{2,1,0:T(2,128)S(1)}, f32[1,2,1280]{2,1,0:T(2,128)S(1)}, u32[]{:S(2)}, u32[]{:S(2)}) collective-permute-start(f32[1,2,1280]{2,1,0:T(2,128)S(1)} %add_bitcast_fusion.3), channel_id=1, source_target_pairs={{0,7},{1,6},{2,5},{3,4},{4,3},{5,2},{6,1},{7,0},{8,15},{9,14},{10,... | collective-permute-start | bytes 30728 | tf_op jit(solution)/shard_map/ppermute | solution.py:25
  38.7 0.2 collective-permute-start.16
  38.9 0.7 %collective-permute-start.14 = (f32[1,2,1280]{2,1,0:T(2,128)S(1)}, f32[1,2,1280]{2,1,0:T(2,128)S(1)}, u32[]{:S(2)}, u32[]{:S(2)}) collective-permute-start(f32[1,2,1280]{2,1,0:T(2,128)S(1)} %add_bitcast_fusion.3), channel_id=1, source_target_pairs={{0,3},{1,2},{2,1},{3,0},{4,7},{5,6},{6,5},{7,4},{8,11},{9,10},{10,... | collective-permute-start | bytes 30728 | tf_op jit(solution)/shard_map/ppermute | solution.py:25
  39.6 2.0 %fusion.1 = bf16[1,512,1280]{2,1,0:T(8,128)(2,1)} fusion(bf16[2,512]{1,0:T(2,128)(2,1)S(1)} %get-tuple-element.39, f32[512,1280]{1,0:T(8,128)S(1)} %get-tuple-element.53, f32[512]{0:T(512)S(1)} %get-tuple-element.52, f32[512]{0:T(512)S(1)} %reduce, bf16[2,2688]{1,0:T(2,128)(2,1)S(1)} %get-tuple-element.47, bf16[1,512,1280]{2,1,0:T(8,128)(2,1)S(1)} %copy-done), kind=kOutput, calls=%fused_computation.3 | convolution fusion | flops 7208960 | bytes 5254144 | tf_op jit(solution)/shard_map/sn,sd->nd/dot_general | solution.py:362
  41.6 0.2 collective-permute-done.16
  41.8 0.2 collective-permute-done.14
  42.0 0.8 %collective-permute-start.17 = (f32[1,2,1280]{2,1,0:T(2,128)S(1)}, f32[1,2,1280]{2,1,0:T(2,128)S(1)}, u32[]{:S(2)}, u32[]{:S(2)}) collective-permute-start(f32[1,2,1280]{2,1,0:T(2,128)S(1)} %add_add_fusion.2.refs_0_), channel_id=1, source_target_pairs={{0,17},{1,16},{2,19},{3,18},{4,21},{5,20},{6,23},{7,22},{8,25},{9,... | collective-permute-start | bytes 30728 | tf_op jit(solution)/shard_map/ppermute | solution.py:25
  42.8 1.7 %collective-permute-start.18 = (f32[1,2,1280]{2,1,0:T(2,128)S(1)}, f32[1,2,1280]{2,1,0:T(2,128)S(1)}, u32[]{:S(2)}, u32[]{:S(2)}) collective-permute-start(f32[1,2,1280]{2,1,0:T(2,128)S(1)} %add_add_fusion.2.refs_0_), channel_id=1, source_target_pairs={{0,25},{1,24},{2,27},{3,26},{4,29},{5,28},{6,31},{7,30},{8,17},{9,... | collective-permute-start | bytes 30728 | tf_op jit(solution)/shard_map/ppermute | solution.py:25
  44.5 0.8 %collective-permute-start.19 = (f32[1,2,1280]{2,1,0:T(2,128)S(1)}, f32[1,2,1280]{2,1,0:T(2,128)S(1)}, u32[]{:S(2)}, u32[]{:S(2)}) collective-permute-start(f32[1,2,1280]{2,1,0:T(2,128)S(1)} %add_add_fusion.2.refs_0_), channel_id=1, source_target_pairs={{0,9},{1,8},{2,11},{3,10},{4,13},{5,12},{6,15},{7,14},{8,1},{9,0},... | collective-permute-start | bytes 30728 | tf_op jit(solution)/shard_map/ppermute | solution.py:25
  45.2 1.6 %fusion.2 = bf16[1,512,1280]{2,1,0:T(8,128)(2,1)} fusion(bf16[2,512]{1,0:T(2,128)(2,1)S(1)} %get-tuple-element.26, bf16[2,2688]{1,0:T(2,128)(2,1)S(1)} %get-tuple-element.47), kind=kOutput, calls=%fused_computation.4 | convolution fusion | flops 3276800 | bytes 1317888 | tf_op jit(solution)/shard_map/sn,sd->nd/dot_general | solution.py:360
  46.9 0.8 %collective-permute-done.18.refs_2_ = f32[1,2,1280]{2,1,0:T(2,128)S(1)} collective-permute-done((f32[1,2,1280]{2,1,0:T(2,128)S(1)}, f32[1,2,1280]{2,1,0:T(2,128)S(1)}, u32[]{:S(2)}, u32[]{:S(2)}) %collective-permute-start.18) | collective-permute-done | bytes 10272 | tf_op jit(solution)/shard_map/ppermute | solution.py:25
  47.7 0.8 %finish.1 = f32[2,1280]{1,0:T(2,128)} custom-call(bf16[2,1280]{1,0:T(2,128)(2,1)S(1)} %bitcast.41, f32[1,2,1280]{2,1,0:T(2,128)S(1)} %add_add_fusion.2.refs_0_, f32[1,2,1280]{2,1,0:T(2,128)S(1)} %collective-permute-done.17.refs_1_, f32[1,2,1280]{2,1,0:T(2,128)S(1)} %collective-permute-done.18.refs_2_, f32[1,2,1280]{2,1,0:T(2,128)S(1)} %collective-permute-done.19.refs_3_), custom_call_target="tpu_custom_call" | custom-call | tf_op jit(solution)/shard_map/finish/pallas_call | solution.py:347
  (27 shorter events, 0.2 us)
Async XLA Ops:
  0.6 4.5 %copy-start.2 = (bf16[1280,2]{0,1:T(2,128)(2,1)S(1)}, bf16[1280,2]{0,1:T(2,128)(2,1)}, u32[]{:S(2)}) copy-start(bf16[1280,2]{0,1:T(2,128)(2,1)} %param.8) | copy-start | bytes 15364
  4.6 1.4 %collective-permute-start = (f32[2,2688]{1,0:T(2,128)S(1)}, f32[2,2688]{1,0:T(2,128)S(1)}, u32[]{:S(2)}, u32[]{:S(2)}) collective-permute-start(f32[2,2688]{1,0:T(2,128)S(1)} %get-tuple-element.27), channel_id=1, source_target_pairs={{0,1},{1,0},{2,3},{3,2},{4,5},{5,4},{6,7},{7,6},{8,9},{9,8},{10,11... | collective-permute-start | bytes 64520 | tf_op jit(solution)/shard_map/ppermute | solution.py:29
  6.1 5.3 %collective-permute-start.2 = (f32[1,2,2688]{2,1,0:T(2,128)S(1)}, f32[1,2,2688]{2,1,0:T(2,128)S(1)}, u32[]{:S(2)}, u32[]{:S(2)}) collective-permute-start(f32[1,2,2688]{2,1,0:T(2,128)S(1)} %get-tuple-element.51), channel_id=1, source_target_pairs={{0,17},{1,16},{2,19},{3,18},{4,21},{5,20},{6,23},{7,22},{8,25},{9,... | collective-permute-start | bytes 64520 | tf_op jit(solution)/shard_map/ppermute | solution.py:25
  9.8 5.1 %collective-permute-start.3 = (f32[1,2,2688]{2,1,0:T(2,128)S(1)}, f32[1,2,2688]{2,1,0:T(2,128)S(1)}, u32[]{:S(2)}, u32[]{:S(2)}) collective-permute-start(f32[1,2,2688]{2,1,0:T(2,128)S(1)} %get-tuple-element.50), channel_id=1, source_target_pairs={{0,25},{1,24},{2,27},{3,26},{4,29},{5,28},{6,31},{7,30},{8,17},{9,... | collective-permute-start | bytes 64520 | tf_op jit(solution)/shard_map/ppermute | solution.py:25
  11.1 3.8 %collective-permute-start.1 = (f32[1,2,2688]{2,1,0:T(2,128)S(1)}, f32[1,2,2688]{2,1,0:T(2,128)S(1)}, u32[]{:S(2)}, u32[]{:S(2)}) collective-permute-start(f32[1,2,2688]{2,1,0:T(2,128)S(1)} %get-tuple-element.49), channel_id=1, source_target_pairs={{0,9},{1,8},{2,11},{3,10},{4,13},{5,12},{6,15},{7,14},{8,1},{9,0},... | collective-permute-start | bytes 64520 | tf_op jit(solution)/shard_map/ppermute | solution.py:25
  15.0 5.4 %collective-permute-start.5 = (f32[1,2,2688]{2,1,0:T(2,128)S(1)}, f32[1,2,2688]{2,1,0:T(2,128)S(1)}, u32[]{:S(2)}, u32[]{:S(2)}) collective-permute-start(f32[1,2,2688]{2,1,0:T(2,128)S(1)} %add_add_fusion.1), channel_id=1, source_target_pairs={{0,7},{1,6},{2,5},{3,4},{4,3},{5,2},{6,1},{7,0},{8,15},{9,14},{10,... | collective-permute-start | bytes 64520 | tf_op jit(solution)/shard_map/ppermute | solution.py:25
  17.5 3.2 %collective-permute-start.6 = (f32[1,2,2688]{2,1,0:T(2,128)S(1)}, f32[1,2,2688]{2,1,0:T(2,128)S(1)}, u32[]{:S(2)}, u32[]{:S(2)}) collective-permute-start(f32[1,2,2688]{2,1,0:T(2,128)S(1)} %add_add_fusion.1), channel_id=1, source_target_pairs={{0,5},{1,4},{2,7},{3,6},{4,1},{5,0},{6,3},{7,2},{8,13},{9,12},{10,... | collective-permute-start | bytes 64520 | tf_op jit(solution)/shard_map/ppermute | solution.py:25
  17.7 3.2 %collective-permute-start.4 = (f32[1,2,2688]{2,1,0:T(2,128)S(1)}, f32[1,2,2688]{2,1,0:T(2,128)S(1)}, u32[]{:S(2)}, u32[]{:S(2)}) collective-permute-start(f32[1,2,2688]{2,1,0:T(2,128)S(1)} %add_add_fusion.1), channel_id=1, source_target_pairs={{0,3},{1,2},{2,1},{3,0},{4,7},{5,6},{6,5},{7,4},{8,11},{9,10},{10,... | collective-permute-start | bytes 64520 | tf_op jit(solution)/shard_map/ppermute | solution.py:25
  22.5 11.7 %copy-start = (bf16[1,512,1280]{2,1,0:T(8,128)(2,1)S(1)}, bf16[1,512,1280]{2,1,0:T(8,128)(2,1)}, u32[]{:S(2)}) copy-start(bf16[1,512,1280]{2,1,0:T(8,128)(2,1)} %param.6) | copy-start | bytes 3932164
  22.5 11.7 %copy-start.1 = (bf16[1,512,1280]{2,1,0:T(8,128)(2,1)S(1)}, bf16[1,512,1280]{2,1,0:T(8,128)(2,1)}, u32[]{:S(2)}) copy-start(bf16[1,512,1280]{2,1,0:T(8,128)(2,1)} %param.7) | copy-start | bytes 3932164
  22.5 4.9 %collective-permute-start.8 = (f32[1,2,2688]{2,1,0:T(2,128)S(1)}, f32[1,2,2688]{2,1,0:T(2,128)S(1)}, u32[]{:S(2)}, u32[]{:S(2)}) collective-permute-start(f32[1,2,2688]{2,1,0:T(2,128)S(1)} %bitcast.42), channel_id=1, source_target_pairs={{0,7},{1,6},{2,5},{3,4},{4,3},{5,2},{6,1},{7,0},{8,15},{9,14},{10,... | collective-permute-start | bytes 64520 | tf_op jit(solution)/shard_map/ppermute | solution.py:25
  24.1 3.4 %collective-permute-start.9 = (f32[1,2,2688]{2,1,0:T(2,128)S(1)}, f32[1,2,2688]{2,1,0:T(2,128)S(1)}, u32[]{:S(2)}, u32[]{:S(2)}) collective-permute-start(f32[1,2,2688]{2,1,0:T(2,128)S(1)} %bitcast.43), channel_id=1, source_target_pairs={{0,5},{1,4},{2,7},{3,6},{4,1},{5,0},{6,3},{7,2},{8,13},{9,12},{10,... | collective-permute-start | bytes 64520 | tf_op jit(solution)/shard_map/ppermute | solution.py:25
  24.7 3.2 %collective-permute-start.7 = (f32[1,2,2688]{2,1,0:T(2,128)S(1)}, f32[1,2,2688]{2,1,0:T(2,128)S(1)}, u32[]{:S(2)}, u32[]{:S(2)}) collective-permute-start(f32[1,2,2688]{2,1,0:T(2,128)S(1)} %bitcast.44), channel_id=1, source_target_pairs={{0,3},{1,2},{2,1},{3,0},{4,7},{5,6},{6,5},{7,4},{8,11},{9,10},{10,... | collective-permute-start | bytes 64520 | tf_op jit(solution)/shard_map/ppermute | solution.py:25
  27.9 4.6 %collective-permute-start.11 = (f32[1,2,2688]{2,1,0:T(2,128)S(1)}, f32[1,2,2688]{2,1,0:T(2,128)S(1)}, u32[]{:S(2)}, u32[]{:S(2)}) collective-permute-start(f32[1,2,2688]{2,1,0:T(2,128)S(1)} %add_add_fusion), channel_id=1, source_target_pairs={{0,17},{1,16},{2,19},{3,18},{4,21},{5,20},{6,23},{7,22},{8,25},{9,... | collective-permute-start | bytes 64520 | tf_op jit(solution)/shard_map/ppermute | solution.py:25
  29.0 5.0 %collective-permute-start.12 = (f32[1,2,2688]{2,1,0:T(2,128)S(1)}, f32[1,2,2688]{2,1,0:T(2,128)S(1)}, u32[]{:S(2)}, u32[]{:S(2)}) collective-permute-start(f32[1,2,2688]{2,1,0:T(2,128)S(1)} %add_add_fusion), channel_id=1, source_target_pairs={{0,25},{1,24},{2,27},{3,26},{4,29},{5,28},{6,31},{7,30},{8,17},{9,... | collective-permute-start | bytes 64520 | tf_op jit(solution)/shard_map/ppermute | solution.py:25
  29.8 4.2 %collective-permute-start.10 = (f32[1,2,2688]{2,1,0:T(2,128)S(1)}, f32[1,2,2688]{2,1,0:T(2,128)S(1)}, u32[]{:S(2)}, u32[]{:S(2)}) collective-permute-start(f32[1,2,2688]{2,1,0:T(2,128)S(1)} %add_add_fusion), channel_id=1, source_target_pairs={{0,9},{1,8},{2,11},{3,10},{4,13},{5,12},{6,15},{7,14},{8,1},{9,0},... | collective-permute-start | bytes 64520 | tf_op jit(solution)/shard_map/ppermute | solution.py:25
  35.2 1.2 %collective-permute-start.13 = (f32[2,1280]{1,0:T(2,128)S(1)}, f32[2,1280]{1,0:T(2,128)S(1)}, u32[]{:S(2)}, u32[]{:S(2)}) collective-permute-start(f32[2,1280]{1,0:T(2,128)S(1)} %get-tuple-element.46), channel_id=1, source_target_pairs={{0,1},{1,0},{2,3},{3,2},{4,5},{5,4},{6,7},{7,6},{8,9},{9,8},{10,11... | collective-permute-start | bytes 30728 | tf_op jit(solution)/shard_map/ppermute | solution.py:29
  36.4 5.1 %collective-permute-start.15 = (f32[1,2,1280]{2,1,0:T(2,128)S(1)}, f32[1,2,1280]{2,1,0:T(2,128)S(1)}, u32[]{:S(2)}, u32[]{:S(2)}) collective-permute-start(f32[1,2,1280]{2,1,0:T(2,128)S(1)} %add_bitcast_fusion.3), channel_id=1, source_target_pairs={{0,7},{1,6},{2,5},{3,4},{4,3},{5,2},{6,1},{7,0},{8,15},{9,14},{10,... | collective-permute-start | bytes 30728 | tf_op jit(solution)/shard_map/ppermute | solution.py:25
  38.7 3.1 %collective-permute-start.16 = (f32[1,2,1280]{2,1,0:T(2,128)S(1)}, f32[1,2,1280]{2,1,0:T(2,128)S(1)}, u32[]{:S(2)}, u32[]{:S(2)}) collective-permute-start(f32[1,2,1280]{2,1,0:T(2,128)S(1)} %add_bitcast_fusion.3), channel_id=1, source_target_pairs={{0,5},{1,4},{2,7},{3,6},{4,1},{5,0},{6,3},{7,2},{8,13},{9,12},{10,... | collective-permute-start | bytes 30728 | tf_op jit(solution)/shard_map/ppermute | solution.py:25
  38.9 3.1 %collective-permute-start.14 = (f32[1,2,1280]{2,1,0:T(2,128)S(1)}, f32[1,2,1280]{2,1,0:T(2,128)S(1)}, u32[]{:S(2)}, u32[]{:S(2)}) collective-permute-start(f32[1,2,1280]{2,1,0:T(2,128)S(1)} %add_bitcast_fusion.3), channel_id=1, source_target_pairs={{0,3},{1,2},{2,1},{3,0},{4,7},{5,6},{6,5},{7,4},{8,11},{9,10},{10,... | collective-permute-start | bytes 30728 | tf_op jit(solution)/shard_map/ppermute | solution.py:25
  42.0 4.8 %collective-permute-start.17 = (f32[1,2,1280]{2,1,0:T(2,128)S(1)}, f32[1,2,1280]{2,1,0:T(2,128)S(1)}, u32[]{:S(2)}, u32[]{:S(2)}) collective-permute-start(f32[1,2,1280]{2,1,0:T(2,128)S(1)} %add_add_fusion.2.refs_0_), channel_id=1, source_target_pairs={{0,17},{1,16},{2,19},{3,18},{4,21},{5,20},{6,23},{7,22},{8,25},{9,... | collective-permute-start | bytes 30728 | tf_op jit(solution)/shard_map/ppermute | solution.py:25
  42.8 4.9 %collective-permute-start.18 = (f32[1,2,1280]{2,1,0:T(2,128)S(1)}, f32[1,2,1280]{2,1,0:T(2,128)S(1)}, u32[]{:S(2)}, u32[]{:S(2)}) collective-permute-start(f32[1,2,1280]{2,1,0:T(2,128)S(1)} %add_add_fusion.2.refs_0_), channel_id=1, source_target_pairs={{0,25},{1,24},{2,27},{3,26},{4,29},{5,28},{6,31},{7,30},{8,17},{9,... | collective-permute-start | bytes 30728 | tf_op jit(solution)/shard_map/ppermute | solution.py:25
  44.5 3.2 %collective-permute-start.19 = (f32[1,2,1280]{2,1,0:T(2,128)S(1)}, f32[1,2,1280]{2,1,0:T(2,128)S(1)}, u32[]{:S(2)}, u32[]{:S(2)}) collective-permute-start(f32[1,2,1280]{2,1,0:T(2,128)S(1)} %add_add_fusion.2.refs_0_), channel_id=1, source_target_pairs={{0,9},{1,8},{2,11},{3,10},{4,13},{5,12},{6,15},{7,14},{8,1},{9,0},... | collective-permute-start | bytes 30728 | tf_op jit(solution)/shard_map/ppermute | solution.py:25
